TPU v7x, 32 devices: a whole 2x2x4 slice. The times are simulated.
32 devices in a mesh: job: 2 (over y), rollout: 4 (over z), tensor: 4 (over x, core).
Axes of the slice: x: 2, y: 2, z: 4, core: 2. Of those that a mesh axis runs over, the one named last changes fastest.
Arguments:
- normed_tokens: bfloat16 [4, 64, 5120], P(None, ('job', 'rollout'), 'tensor'), parts along dimension 1, may hold values from -6 to 6
- key_value_weight: bfloat16 [5120, 2048], P('tensor'), may hold values from -0.078125 to 0.078125
- adapter_down: bfloat16 [10240, 64], P(('job', 'rollout', 'tensor')), parts along dimension 0, may hold values from -0.078125 to 0.078125
- adapter_up: bfloat16 [64, 4096], P(None, ('job', 'rollout')), parts along dimension 1, may hold values from -0.47851562 to 0.47851562
- key_gain: float32 [128], replicated, may hold values from 0.25 to 1.75
- queries: bfloat16 [4, 64, 8192], P(None, ('job', 'rollout'), 'tensor'), parts along dimension 1, may hold values from -100 to 100
- cache_keys: bfloat16 [64, 512, 1024], P(('job', 'rollout'), None, 'tensor'), parts along dimension 0, may hold values from -6 to 6
- stored_values: bfloat16 [64, 512, 1024], P(('job', 'rollout'), None, 'tensor'), parts along dimension 0, may hold values from -6 to 6
- lengths: int32 [64], P(('job', 'rollout')), parts along dimension 0, may hold values from 1 to 512, 6553 in all
- owners: int32 [8], P('job'), parts along dimension 0, may hold values from 0 to 3, each once
Outputs:
- attention: bfloat16 [4, 64, 8192], P(None, ('job', 'rollout'), 'tensor'), parts along dimension 1
- incoming_keys: bfloat16 [4, 64, 1024], P(None, ('job', 'rollout'), 'tensor'), parts along dimension 1
- incoming_values: bfloat16 [4, 64, 1024], P(None, ('job', 'rollout'), 'tensor'), parts along dimension 1
There are 2 independent parts, one for each index of `job`. A program takes and returns all parts, laid end to end along the dimension named above; an argument that names none is the same for every part. Nothing has to cross between parts.
All inputs are finite; a program needn't handle non-finite values. No bound on the sum of `lengths` on one device may be relied on, other than what follows from the above.
Results may differ from a plain program's by a relative error of at most 0.0055.
Values may be sent and summed in bfloat16 or wider, within the bound.
No kernel may reach another device: no remote copies, remote signals or barrier semaphores. Data moves between devices by JAX's collectives and lax.ppermute only.
A program may use at most 64 MiB of HBM per device.

v0:
```python
import jax
import jax.numpy as jnp
from jax import lax
from jax.sharding import PartitionSpec as P

norm_eps = 1e-06
rope_base = 1000000.0
adapter_scale = 2.0
masked_score = -1e30


def rotate(vectors, positions):
    middle = vectors.shape[-1] // 2
    spacing = jnp.arange(middle, dtype=jnp.float32) * (-2.0 / vectors.shape[-1])
    inverse = jnp.power(jnp.float32(rope_base), spacing)
    angles = positions.astype(jnp.float32)[..., None, None] * inverse
    cosine = jnp.cos(angles)
    sine_part = jnp.sin(angles)
    leading = vectors[..., :middle]
    trailing = vectors[..., middle:]
    return jnp.concatenate(
        [leading * cosine - trailing * sine_part, trailing * cosine + leading * sine_part], axis=-1
    )


def key_norm(raw_keys, key_gain):
    mean_square = jnp.mean(raw_keys * raw_keys, axis=-1, keepdims=True)
    return raw_keys * lax.rsqrt(mean_square + norm_eps) * key_gain


def per_device(
    normed_tokens,
    key_value_weight,
    adapter_down,
    adapter_up,
    key_gain,
    queries,
    cache_keys,
    stored_values,
    lengths,
    owners,
):
    rollout_count = lax.axis_size("rollout")
    rank_size = adapter_down.shape[1]
    down_stored = lax.all_gather(adapter_down, "rollout", axis=0, tiled=True)
    down_matrix = jnp.take(
        down_stored.reshape(rollout_count, -1, rank_size), owners, axis=0
    ).reshape(-1, rank_size)
    up_stored = lax.all_gather(adapter_up, "rollout", axis=1, tiled=True)
    up_matrix = jnp.take(up_stored.reshape(rank_size, rollout_count, -1), owners, axis=1).reshape(
        rank_size, -1
    )
    merged_weight = (
        key_value_weight.astype(jnp.float32)
        + adapter_scale * jnp.dot(down_matrix, up_matrix, preferred_element_type=jnp.float32)
    ).astype(jnp.bfloat16)
    step_count = normed_tokens.shape[0]
    row_count = normed_tokens.shape[1]
    head_size = key_gain.shape[0]
    joined_matrix = jnp.stack(
        [
            lax.psum_scatter(
                jnp.dot(
                    normed_tokens[decode_step_index],
                    merged_weight,
                    preferred_element_type=jnp.float32,
                ),
                "tensor",
                scatter_dimension=1,
                tiled=True,
            )
            for decode_step_index in range(step_count)
        ]
    )
    joined_matrix = joined_matrix.reshape(step_count, row_count, -1, 2, head_size)
    incoming_values = joined_matrix[:, :, :, 1].astype(jnp.bfloat16)
    positions = lengths[None, :] + jnp.arange(step_count, dtype=jnp.int32)[:, None]
    incoming_keys = rotate(key_norm(joined_matrix[:, :, :, 0], key_gain), positions).astype(
        jnp.bfloat16
    )
    head_count = incoming_keys.shape[2]
    query_heads = queries.reshape(step_count, row_count, head_count, -1, head_size)
    keys_local = cache_keys.reshape(row_count, -1, head_count, head_size)
    values_local = stored_values.reshape(row_count, -1, head_count, head_size)
    scale_factor = head_size ** (-0.5)
    cached = (
        jnp.einsum("tbhge,bphe->tbhgp", query_heads, keys_local, preferred_element_type=jnp.float32)
        * scale_factor
    )
    live_mask = jnp.arange(keys_local.shape[1])[None, :] < lengths[:, None]
    cached = jnp.where(live_mask[None, :, None, None, :], cached, masked_score)
    recent = (
        jnp.einsum(
            "tbhge,sbhe->tbhgs", query_heads, incoming_keys, preferred_element_type=jnp.float32
        )
        * scale_factor
    )
    causal = jnp.arange(step_count)[None, :] <= jnp.arange(step_count)[:, None]
    recent = jnp.where(causal[:, None, None, None, :], recent, masked_score)
    row_peak = jnp.maximum(
        jnp.max(cached, axis=-1, keepdims=True), jnp.max(recent, axis=-1, keepdims=True)
    )
    raised_cached = jnp.exp(cached - row_peak)
    raised_recent = jnp.exp(recent - row_peak)
    denominator = jnp.sum(raised_cached, axis=-1, keepdims=True) + jnp.sum(
        raised_recent, axis=-1, keepdims=True
    )
    weights_cached = (raised_cached / denominator).astype(jnp.bfloat16)
    weights_recent = (raised_recent / denominator).astype(jnp.bfloat16)
    combined = jnp.einsum(
        "tbhgp,bphe->tbhge", weights_cached, values_local, preferred_element_type=jnp.float32
    )
    combined = combined + jnp.einsum(
        "tbhgs,sbhe->tbhge", weights_recent, incoming_values, preferred_element_type=jnp.float32
    )
    attention = combined.reshape(step_count, row_count, -1).astype(jnp.bfloat16)
    return (
        attention,
        incoming_keys.reshape(step_count, row_count, -1),
        incoming_values.reshape(step_count, row_count, -1),
    )


def solution(mesh):
    placed = (
        P(None, ("job", "rollout"), "tensor"),
        P("tensor", None),
        P(("job", "rollout", "tensor"), None),
        P(None, ("job", "rollout")),
        P(),
        P(None, ("job", "rollout"), "tensor"),
        P(("job", "rollout"), None, "tensor"),
        P(("job", "rollout"), None, "tensor"),
        P(("job", "rollout")),
        P("job"),
    )
    return jax.shard_map(
        per_device,
        mesh=mesh,
        in_specs=placed,
        out_specs=(
            P(None, ("job", "rollout"), "tensor"),
            P(None, ("job", "rollout"), "tensor"),
            P(None, ("job", "rollout"), "tensor"),
        ),
        check_vma=False,
    )
```

profile of v0, /device:TPU:0, one launch (start us, length us, event | category | flops | bytes accessed | tf_op | source)
XLA Modules:
  0.0 148.7 jit_solution(3551775698042899782)
XLA Ops:
  7.2 0.0 copy-start
  7.2 0.0 reduce-scatter.5.cloned.1.call-start
  7.2 0.7 compare_select_fusion
  7.9 0.7 compare_and_fusion
  8.6 15.8 %all_gather.7 = bf16[64,2048]{1,0:T(8,128)(2,1)S(1)} all-gather(bf16[64,512]{1,0:T(8,128)(2,1)} %param.13), channel_id=1, replica_groups=mesh['job'=2,'rollout'=4,'tensor'=4] {'rollout'}, dimensions={1}, use_global_device_ids=true | all-gather | bytes 327680 | tf_op jit(solution)/shard_map/all_gather | solution.py:49
  24.4 0.6 gather_fusion.1
  25.0 0.1 select_bitcast_fusion
  25.1 14.4 %all-gather = bf16[4,320,64]{1,2,0:T(8,128)(2,1)S(1)} all-gather(bf16[1,320,64]{1,2,0:T(8,128)(2,1)} %bitcast.92), channel_id=1, replica_groups=mesh['job'=2,'rollout'=4,'tensor'=4] {'rollout'}, dimensions={0}, use_global_device_ids=true | all-gather | bytes 204800 | tf_op jit(solution)/shard_map/all_gather | solution.py:45
  39.5 0.6 gather_fusion
  40.1 0.1 broadcast_select_fusion
  40.2 0.2 copy.49
  40.4 0.2 select_n.50
  40.6 0.0 copy-start.4
  40.6 4.1 %add_convert_fusion = bf16[1280,2048]{1,0:T(8,128)(2,1)S(1)} fusion(bf16[1280,2048]{1,0:T(8,128)(2,1)} %param.11, bf16[1280,64]{0,1:T(8,128)(2,1)S(1)} %select_n.50, bf16[64,2048]{1,0:T(8,128)(2,1)S(1)} %bitcast.89), kind=kOutput, calls=%fused_computation.2 | convolution fusion | flops 346030080 | bytes 10911744 | tf_op jit(solution)/shard_map/dot_general | solution.py:55
  44.7 0.0 copy-start.1
  44.7 2.3 %copy-done.1 = bf16[1280,2048]{1,0:T(8,128)(2,1)} copy-done((bf16[1280,2048]{1,0:T(8,128)(2,1)}, bf16[1280,2048]{1,0:T(8,128)(2,1)S(1)}, u32[]{:S(2)}) %copy-start.1) | copy-done | bytes 5242904
  47.0 0.0 copy-done.4
  47.0 1.4 convolution_bitcast_fusion.3
  48.4 0.0 reduce-scatter.5.cloned.1.call-update
  48.4 0.0 reduce-scatter.7.cloned.1.call-start
  48.5 3.9 %convolution_bitcast_fusion.2 = f32[8,2048]{1,0:T(8,128)} fusion(bf16[1280,2048]{1,0:T(8,128)(2,1)} %copy-done.1, bf16[4,8,1280]{2,1,0:T(8,128)(2,1)S(1)} %copy-done.4), kind=kOutput, calls=%fused_computation.5 | convolution fusion | flops 41943040 | bytes 5328896 | tf_op jit(solution)/shard_map/dot_general | solution.py:63
  52.3 0.0 reduce-scatter.7.cloned.1.call-update
  52.4 0.0 copy-start.5
  52.4 0.0 copy-start.2
  52.4 0.0 reduce-scatter.9.cloned.1.call-start
  52.4 4.0 %convolution_bitcast_fusion.1 = f32[8,2048]{1,0:T(8,128)} fusion(bf16[1280,2048]{1,0:T(8,128)(2,1)} %copy-done.1, bf16[4,8,1280]{2,1,0:T(8,128)(2,1)S(1)} %copy-done.4), kind=kOutput, calls=%fused_computation.4 | convolution fusion | flops 41943040 | bytes 5328896 | tf_op jit(solution)/shard_map/dot_general | solution.py:63
  56.5 0.0 reduce-scatter.9.cloned.1.call-update
  56.5 0.0 reduce-scatter.11.cloned.1.call-start
  56.6 3.9 %convolution_bitcast_fusion = f32[8,2048]{1,0:T(8,128)} fusion(bf16[1280,2048]{1,0:T(8,128)(2,1)} %copy-done.1, bf16[4,8,1280]{2,1,0:T(8,128)(2,1)S(1)} %copy-done.4), kind=kOutput, calls=%fused_computation.3 | convolution fusion | flops 41943040 | bytes 5328896 | tf_op jit(solution)/shard_map/dot_general | solution.py:63
  60.5 0.0 reduce-scatter.11.cloned.1.call-update
  60.5 0.0 copy-done.5
  60.5 0.1 add_convert_fusion.1
  60.6 0.1 iota_compare_fusion
  60.7 0.0 copy-done.2
  60.7 2.1 %reshape.194 = bf16[8,512,2,128]{3,2,1,0:T(2,128)(2,1)} reshape(bf16[8,512,256]{2,1,0:T(8,128)(2,1)S(1)} %copy-done.2) | data formatting | bytes 4194304 | tf_op jit(solution)/shard_map/reshape | solution.py:83
  62.8 0.0 copy-done
  62.8 0.0 copy-start.3
  62.8 0.0 copy-start.6
  62.8 2.6 %fusion.42 = (f32[4,8,2,8]{3,0,2,1:T(4,128)S(1)}, f32[4,8,2,8,512]{4,3,0,2,1:T(8,128)S(1)}) fusion(bf16[4,8,2,8,128]{4,1,3,2,0:T(8,128)(2,1)S(1)} %bitcast.85, bf16[8,512,2,128,1]{3,2,1,0,4:T(2,128)(2,1)} %bitcast.88, pred[8,512]{1,0:T(8,128)(4,1)S(1)} %iota_compare_fusion), kind=kOutput, calls=%fused_computation.66 | convolution fusion | flops 67894784 | bytes 3282944 | tf_op jit(solution)/shard_map/tbhge,bphe->tbhgp/dot_general | solution.py:87
  65.4 0.2 multiply_cosine_fusion
  65.6 0.0 copy-done.3
  65.6 2.1 %reshape.198 = bf16[8,512,2,128]{3,2,1,0:T(2,128)(2,1)} reshape(bf16[8,512,256]{2,1,0:T(8,128)(2,1)S(1)} %copy-done.3) | data formatting | bytes 4194304 | tf_op jit(solution)/shard_map/reshape | solution.py:84
  67.7 1.3 reduce-scatter.5.cloned.1.call-done
  69.0 0.7 copy.52
  69.7 21.3 %reduce-scatter.7.cloned.1.call-done = f32[8,512]{1,0:T(8,128)} async-done(((f32[8,2048]{1,0:T(8,128)}), f32[8,512]{1,0:T(8,128)}) %reduce-scatter.7.cloned.1.call-update) | async-done | bytes 16400 | tf_op jit(solution)/shard_map/reduce_scatter | solution.py:62
  91.0 0.7 copy.53
  91.7 21.2 %reduce-scatter.9.cloned.1.call-done = f32[8,512]{1,0:T(8,128)} async-done(((f32[8,2048]{1,0:T(8,128)}), f32[8,512]{1,0:T(8,128)}) %reduce-scatter.9.cloned.1.call-update) | async-done | bytes 16400 | tf_op jit(solution)/shard_map/reduce_scatter | solution.py:62
  112.9 0.7 copy.54
  113.6 21.7 %reduce-scatter.11.cloned.1.call-done = f32[8,512]{1,0:T(8,128)} async-done(((f32[8,2048]{1,0:T(8,128)}), f32[8,512]{1,0:T(8,128)}) %reduce-scatter.11.cloned.1.call-update) | async-done | bytes 16400 | tf_op jit(solution)/shard_map/reduce_scatter | solution.py:62
  135.3 0.7 copy.55
  136.1 0.1 pad_maximum_fusion
  136.1 0.1 multiply_reduce_fusion
  136.3 0.0 copy-done.6
  136.3 0.1 multiply_multiply_fusion
  136.4 0.1 multiply_subtract_fusion
  136.5 0.1 maximum_convert_fusion
  136.6 0.6 copy.102
  137.2 0.7 fusion.43
  137.9 0.1 fusion.29
  138.0 0.4 fusion.24
  138.4 0.3 convolution_bitcast_fusion.4
  138.7 2.1 %fusion.19 = bf16[4,8,2,8,128]{4,3,0,2,1:T(8,128)(2,1)S(1)} fusion(f32[4,8,2,8,128]{4,3,0,2,1:T(8,128)S(1)} %convolution_bitcast_fusion.4, bf16[8,512,2,128,1]{3,2,1,0,4:T(2,128)(2,1)} %bitcast.87, f32[4,8,2,8,512]{4,3,0,2,1:T(8,128)S(1)} %get-tuple-element.8, f32[4,8,2,8]{3,0,2,1:T(4,128)S(1)} %add.67, f32[4,8,2,8]{3,0,2,1:T(4,128)S(1)} %max.8), kind=kOutput, calls=%fused_computation.17 | convolution fusion | flops 68026368 | bytes 3543040 | tf_op jit(solution)/shard_map/tbhgp,bphe->tbhge/dot_general | solution.py:110
  140.9 0.7 convert_element_type.51
  141.6 0.6 copy.101
  (10 shorter events, 0.1 us)
Async XLA Ops:
  7.2 55.6 %copy-start = (bf16[4,8,2048]{2,1,0:T(8,128)(2,1)S(1)}, bf16[4,8,2048]{2,1,0:T(8,128)(2,1)}, u32[]{:S(2)}) copy-start(bf16[4,8,2048]{2,1,0:T(8,128)(2,1)} %param.15) | copy-start | bytes 393220
  7.2 61.8 %reduce-scatter.5.cloned.1.call-start = ((), (), s32[]{:S(2)}) async-start(), calls=%async_computation.4 | async-start | bytes 81920 | tf_op jit(solution)/shard_map/reduce_scatter | solution.py:62
  40.6 6.4 %copy-start.4 = (bf16[4,8,1280]{2,1,0:T(8,128)(2,1)S(1)}, bf16[4,8,1280]{2,1,0:T(8,128)(2,1)}, u32[]{:S(2)}) copy-start(bf16[4,8,1280]{2,1,0:T(8,128)(2,1)} %param.10) | copy-start | bytes 245764
  44.7 2.3 %copy-start.1 = (bf16[1280,2048]{1,0:T(8,128)(2,1)}, bf16[1280,2048]{1,0:T(8,128)(2,1)S(1)}, u32[]{:S(2)}) copy-start(bf16[1280,2048]{1,0:T(8,128)(2,1)S(1)} %add_convert_fusion) | copy-start | bytes 15728644
  48.4 42.6 %reduce-scatter.7.cloned.1.call-start = ((), (), s32[]{:S(2)}) async-start(), calls=%async_computation.5 | async-start | bytes 81920 | tf_op jit(solution)/shard_map/reduce_scatter | solution.py:62
  52.4 8.2 %copy-start.5 = (s32[8]{0:T(128)S(1)}, s32[8]{0:T(128)}, u32[]{:S(2)}) copy-start(s32[8]{0:T(128)} %param.18) | copy-start | bytes 100
  52.4 8.3 %copy-start.2 = (bf16[8,512,256]{2,1,0:T(8,128)(2,1)S(1)}, bf16[8,512,256]{2,1,0:T(8,128)(2,1)}, u32[]{:S(2)}) copy-start(bf16[8,512,256]{2,1,0:T(8,128)(2,1)} %param.16) | copy-start | bytes 6291460
  52.4 60.5 %reduce-scatter.9.cloned.1.call-start = ((), (), s32[]{:S(2)}) async-start(), calls=%async_computation.6 | async-start | bytes 81920 | tf_op jit(solution)/shard_map/reduce_scatter | solution.py:62
  56.5 78.8 %reduce-scatter.11.cloned.1.call-start = ((), (), s32[]{:S(2)}) async-start(), calls=%async_computation.7 | async-start | bytes 81920 | tf_op jit(solution)/shard_map/reduce_scatter | solution.py:62
  62.8 2.8 %copy-start.3 = (bf16[8,512,256]{2,1,0:T(8,128)(2,1)S(1)}, bf16[8,512,256]{2,1,0:T(8,128)(2,1)}, u32[]{:S(2)}) copy-start(bf16[8,512,256]{2,1,0:T(8,128)(2,1)} %param.17) | copy-start | bytes 6291460
  62.8 73.5 %copy-start.6 = (f32[128]{0:T(128)S(1)}, f32[128]{0:T(128)}, u32[]{:S(2)}) copy-start(f32[128]{0:T(128)} %param.14) | copy-start | bytes 1540
Sparse Core Ops, SparseCore 0:
  48.5 20.4 reduce-scatter.4
  71.5 19.4 reduce-scatter.6
  93.4 19.4 reduce-scatter.8
  115.9 19.4 reduce-scatter.10
where the time goes:
time: 149 us
  waiting for transfers between devices  65.5 us (44%)
  blocking collectives  30.2 us (20%)
  matrix products  23.1 us (16%)
  between operations  14 us (9%)
  local copies, waits for them, and re-layouts  12.9 us (9%)
  other arithmetic  2.88 us (2%)
    reduce_scatter x4, waiting for transfers between devices, per_device(): lax.psum_scatter(jnp.dot(normed_tokens[decode_step_index], merged_weight,...  65.4 us
    all_gather x1, blocking collectives, per_device(): up_stored = lax.all_gather(adapter_up, 'rollout', axis=1, tiled=True)  15.8 us
    all_gather x1, blocking collectives, per_device(): down_stored = lax.all_gather(adapter_down, 'rollout', axis=0, tiled=True)  14.4 us
    dot_general x4, matrix products, per_device(): jnp.dot(normed_tokens[decode_step_index], merged_weight, preferred_elemen...  13.3 us
    dot_general x1, matrix products, per_device(): jnp.dot(down_matrix, up_matrix, preferred_element_type=jnp.float32)  4.07 us
  transfers between devices with their start and end apart: 4, of which 4 were waited for; matrix products, arithmetic and copies ran while one was open for 14% of the time, Pallas kernels for 0%

commit v1 on v0

--- a/solution.py
+++ b/solution.py
@@ -28,6 +28,19 @@
     return raw_keys * lax.rsqrt(mean_square + norm_eps) * key_gain
 
 
+def swap(block, axis, offset):
+    count = lax.axis_size(axis)
+    return lax.ppermute(block, axis, [(s, s ^ offset) for s in range(count)])
+
+
+def gather_by_offset(block, axis):
+    count = lax.axis_size(axis)
+    if count <= 8:
+        return jnp.stack([block] + [swap(block, axis, i) for i in range(1, count)])
+    whole = lax.all_gather(block, axis, axis=0, tiled=False)
+    return jnp.take(whole, jnp.arange(count) ^ lax.axis_index(axis), axis=0, mode="clip")
+
+
 def per_device(
     normed_tokens,
     key_value_weight,
@@ -40,39 +53,71 @@
     lengths,
     owners,
 ):
-    rollout_count = lax.axis_size("rollout")
-    rank_size = adapter_down.shape[1]
-    down_stored = lax.all_gather(adapter_down, "rollout", axis=0, tiled=True)
-    down_matrix = jnp.take(
-        down_stored.reshape(rollout_count, -1, rank_size), owners, axis=0
+    replicas = lax.axis_size("rollout")
+    shards = lax.axis_size("tensor")
+    replica = lax.axis_index("rollout")
+    shard = lax.axis_index("tensor")
+    down_rows, rank_size = adapter_down.shape
+    up_columns = adapter_up.shape[1]
+    step_count, row_count, depth = normed_tokens.shape
+    head_size = key_gain.shape[0]
+    columns = key_value_weight.shape[1]
+    own_columns = columns // shards
+
+    rank_part = rank_size // shards
+    up_part = lax.dynamic_slice_in_dim(adapter_up, shard * rank_part, rank_part, axis=0)
+    half = down_rows // 2
+    down_packed = jnp.concatenate([adapter_down[:half], adapter_down[half:]], axis=1)
+    packed = jnp.concatenate([down_packed, up_part.reshape(-1, 2 * rank_size)], axis=0)
+    pieces = gather_by_offset(packed, "rollout")
+
+    tokens = normed_tokens.reshape(step_count * row_count, depth)
+    base = jnp.dot(tokens, key_value_weight, preferred_element_type=jnp.float32)
+    joined = lax.dynamic_slice_in_dim(base, shard * own_columns, own_columns, axis=1)
+    for i in range(1, shards):
+        block = lax.dynamic_slice_in_dim(base, (shard ^ i) * own_columns, own_columns, axis=1)
+        joined = joined + swap(block, "tensor", i)
+
+    ordered = jnp.take(pieces, owners ^ replica, axis=0, mode="clip")
+    down_ordered = ordered[:, :half]
+    down_matrix = jnp.concatenate(
+        [down_ordered[:, :, :rank_size], down_ordered[:, :, rank_size:]], axis=1
     ).reshape(-1, rank_size)
-    up_stored = lax.all_gather(adapter_up, "rollout", axis=1, tiled=True)
-    up_matrix = jnp.take(up_stored.reshape(rank_size, rollout_count, -1), owners, axis=1).reshape(
-        rank_size, -1
+    up_matrix = (
+        ordered[:, half:]
+        .reshape(replicas, rank_part, up_columns)
+        .transpose(1, 0, 2)
+        .reshape(rank_part, columns)
     )
-    merged_weight = (
-        key_value_weight.astype(jnp.float32)
-        + adapter_scale * jnp.dot(down_matrix, up_matrix, preferred_element_type=jnp.float32)
-    ).astype(jnp.bfloat16)
-    step_count = normed_tokens.shape[0]
-    row_count = normed_tokens.shape[1]
-    head_size = key_gain.shape[0]
-    joined_matrix = jnp.stack(
-        [
-            lax.psum_scatter(
-                jnp.dot(
-                    normed_tokens[decode_step_index],
-                    merged_weight,
-                    preferred_element_type=jnp.float32,
-                ),
-                "tensor",
-                scatter_dimension=1,
-                tiled=True,
-            )
-            for decode_step_index in range(step_count)
-        ]
+    lowered = jnp.dot(tokens, down_matrix, preferred_element_type=jnp.float32)
+    high = lowered.astype(jnp.bfloat16)
+    low = (lowered - high.astype(jnp.float32)).astype(jnp.bfloat16)
+    lowered_packed = jnp.concatenate([high, low], axis=1)
+
+    sums = []
+    ups = []
+    for i in range(shards):
+        up_block = lax.dynamic_slice_in_dim(
+            up_matrix, (shard ^ i) * own_columns, own_columns, axis=1
+        )
+        block = jnp.concatenate([lowered_packed, up_block.reshape(-1, 2 * rank_size)], axis=0)
+        if i:
+            block = swap(block, "tensor", i)
+        sums.append(block[: step_count * row_count])
+        ups.append(block[step_count * row_count :].reshape(rank_part, own_columns))
+    total = sum(s.astype(jnp.float32) for s in sums)
+    total = total[:, :rank_size] + total[:, rank_size:]
+    total_high = total.astype(jnp.bfloat16)
+    total_low = (total - total_high.astype(jnp.float32)).astype(jnp.bfloat16)
+    up_own = jnp.take(jnp.stack(ups), jnp.arange(shards) ^ shard, axis=0, mode="clip").reshape(
+        rank_size, own_columns
     )
-    joined_matrix = joined_matrix.reshape(step_count, row_count, -1, 2, head_size)
+    raised_up = jnp.dot(total_high, up_own, preferred_element_type=jnp.float32) + jnp.dot(
+        total_low, up_own, preferred_element_type=jnp.float32
+    )
+    joined = joined + adapter_scale * raised_up
+
+    joined_matrix = joined.reshape(step_count, row_count, -1, 2, head_size)
     incoming_values = joined_matrix[:, :, :, 1].astype(jnp.bfloat16)
     positions = lengths[None, :] + jnp.arange(step_count, dtype=jnp.int32)[:, None]
     incoming_keys = rotate(key_norm(joined_matrix[:, :, :, 0], key_gain), positions).astype(

time: 149 us -> 38.5 us (0.26)
  waiting for transfers between devices: 65.5 us -> 2.9 us
  blocking collectives: 30.2 us -> 0 us
  matrix products: 23.1 us -> 9.69 us
  between operations: 14 us -> 1.06 us
  starting transfers between devices: 0.16 us -> 9.84 us
  local copies, waits for them, and re-layouts: 12.9 us -> 10.1 us
  other arithmetic: 2.88 us -> 4.58 us
    reduce_scatter x4 -> x0, waiting for transfers between devices: 65.4 us -> none  [per_device(): lax.psum_scatter(jnp.dot(normed_tokens[decode_step_index], merged_weight,...]
    all_gather x2 -> x0, blocking collectives: 30.2 us -> none  [the longest x1 15.8 us: per_device(): up_stored = lax.all_gather(adapter_up, 'rollout', axis=1, tiled=True)]
    dot_general x5 -> x4, matrix products: 17.3 us -> 4.16 us  [the longest x1 3.68 us: per_device(): base = jnp.dot(tokens, key_value_weight, preferred_element_type=jnp.float32)]
    ppermute x0 -> x9, starting transfers between devices: none -> 9.84 us  [swap(): return lax.ppermute(block, axis, [(s, s ^ offset) for s in range(count)])]
    ppermute x0 -> x9, waiting for transfers between devices: none -> 2.9 us  [swap(): return lax.ppermute(block, axis, [(s, s ^ offset) for s in range(count)])]
    another operation x4, local copies, waits for them, and re-layouts: 2.94 us -> 0.09 us  [per_device(): jnp.stack(ups)]
    unnamed x14 -> x25, local copies, waits for them, and re-layouts: 2.34 us -> 0.06 us
    dot_general x1, matrix products: 2.13 us -> 0.58 us  [per_device(): jnp.einsum('tbhgp,bphe->tbhge', weights_cached, values_local, preferred_e...]
  transfers between devices with their start and end apart: 4 -> 9, of which waited for: 4 -> 1; matrix products, arithmetic and copies ran while one was open for 14% -> 47% of each run, Pallas kernels for 0% -> 0%
where the time goes in v1:
time: 38.5 us; the launch traced here: 38.2 us
  local copies, waits for them, and re-layouts  10.1 us (26%)
  starting transfers between devices  9.84 us (26%)
  matrix products  9.69 us (25%)
  other arithmetic  4.58 us (12%)
  waiting for transfers between devices  2.9 us (8%)
  between operations  1.06 us (3%)
    ppermute x9, starting transfers between devices, swap(): return lax.ppermute(block, axis, [(s, s ^ offset) for s in range(count)])  9.84 us
    dot_general x1, matrix products, per_device(): jnp.einsum('tbhge,bphe->tbhgp', query_heads, keys_local, preferred_elemen...  3.98 us
    dot_general x1, matrix products, per_device(): base = jnp.dot(tokens, key_value_weight, preferred_element_type=jnp.float32)  3.68 us
    ppermute x9, waiting for transfers between devices, swap(): return lax.ppermute(block, axis, [(s, s ^ offset) for s in range(count)])  2.9 us
    reshape x1, local copies, waits for them, and re-layouts, per_device(): values_local = stored_values.reshape(row_count, -1, head_count, head_size)  2.07 us
    reshape x1, local copies, waits for them, and re-layouts, per_device(): keys_local = cache_keys.reshape(row_count, -1, head_count, head_size)  2.05 us
    another operation x2, other arithmetic, gather_by_offset(): return jnp.stack([block] + [swap(block, axis, i) for i in range(1, count)])  1.04 us
    slice x1, local copies, waits for them, and re-layouts, per_device(): adapter_down[:half]  0.92 us
  transfers between devices with their start and end apart: 9, of which 1 were waited for; matrix products, arithmetic and copies ran while one was open for 47% of the time, Pallas kernels for 0%

profile of v1, /device:TPU:0, one launch (start us, length us, event | category | flops | bytes accessed | tf_op | source)
XLA Modules:
  0.0 38.2 jit_solution(5342456697694153207)
XLA Ops:
  0.6 0.0 copy-start
  0.7 0.8 %constant_dynamic-slice_fusion.3 = bf16[16,512]{1,0:T(8,128)(2,1)S(1)} fusion(bf16[64,512]{1,0:T(8,128)(2,1)} %param.13, s32[]{:T(128)S(6)} %select_n.36), kind=kLoop, calls=%fused_computation.70 | loop fusion | bytes 32772 | tf_op jit(solution)/shard_map/dynamic_slice | solution.py:68
  1.4 0.1 copy.33
  1.6 0.9 %fusion.41 = (bf16[160,64]{0,1:T(8,128)(2,1)S(1)}, bf16[160,64]{0,1:T(8,128)(2,1)S(1)}) fusion(bf16[320,64]{0,1:T(8,128)(2,1)} %param.12), kind=kLoop, calls=%fused_computation.80 | loop fusion | bytes 81920 | tf_op jit(solution)/shard_map/slice | solution.py:70
  2.5 0.1 pad_maximum_fusion.2
  2.6 4.1 %collective-permute-start.4 = (bf16[224,128]{0,1:T(8,128)(2,1)S(1)}, bf16[224,128]{0,1:T(8,128)(2,1)S(1)}, u32[]{:S(2)}, u32[]{:S(2)}) collective-permute-start(bf16[224,128]{0,1:T(8,128)(2,1)S(1)} %pad_maximum_fusion.2), channel_id=1, source_target_pairs={{0,8},{4,12},{8,0},{12,4},{1,9},{5,13},{9,1},{13,5},{2,10},{6,14},... | collective-permute-start | bytes 172040 | tf_op jit(solution)/shard_map/ppermute | solution.py:33
  6.7 1.6 %collective-permute-start.3 = (bf16[224,128]{0,1:T(8,128)(2,1)S(1)}, bf16[224,128]{0,1:T(8,128)(2,1)S(1)}, u32[]{:S(2)}, u32[]{:S(2)}) collective-permute-start(bf16[224,128]{0,1:T(8,128)(2,1)S(1)} %pad_maximum_fusion.2), channel_id=1, source_target_pairs={{0,4},{4,0},{8,12},{12,8},{1,5},{5,1},{9,13},{13,9},{2,6},{6,2},{1... | collective-permute-start | bytes 172040 | tf_op jit(solution)/shard_map/ppermute | solution.py:33
  8.2 0.0 collective-permute-start.5
  8.3 3.7 %fusion.32 = f32[32,2048]{1,0:T(8,128)S(1)} fusion(bf16[1280,2048]{1,0:T(8,128)(2,1)} %param.11, bf16[4,8,1280]{2,1,0:T(8,128)(2,1)} %param.10), kind=kOutput, calls=%fused_computation.32 | convolution fusion | flops 167772160 | bytes 5586944 | tf_op jit(solution)/shard_map/dot_general | solution.py:75
  12.0 0.1 collective-permute-start
  12.0 1.8 %collective-permute-start.2 = (f32[32,512]{1,0:T(8,128)S(1)}, f32[32,512]{1,0:T(8,128)S(1)}, u32[]{:S(2)}, u32[]{:S(2)}) collective-permute-start(f32[32,512]{1,0:T(8,128)S(1)} %get-tuple-element.6), channel_id=1, source_target_pairs={{0,3},{1,2},{2,1},{3,0},{4,7},{5,6},{6,5},{7,4},{8,11},{9,10},{10,... | collective-permute-start | bytes 196616 | tf_op jit(solution)/shard_map/ppermute | solution.py:33
  13.9 0.0 copy-done.9
  13.9 0.1 add_convert_fusion
  14.0 0.1 iota_compare_fusion
  14.0 0.1 fusion.51
  14.1 0.0 copy-done.11
  14.2 0.6 %pad_clamp_fusion.1 = s32[1024]{0:T(1024)} fusion(s32[4]{0:T(128)S(1)} %broadcast_xor_fusion), kind=kLoop, calls=%fused_computation.65 | loop fusion | flops 1024 | bytes 4112 | tf_op jit(solution)/shard_map/jit(_take)/gather | solution.py:81
  14.8 2.1 %reshape.145 = bf16[8,512,2,128]{3,2,1,0:T(2,128)(2,1)} reshape(bf16[8,512,256]{2,1,0:T(8,128)(2,1)S(1)} %copy-done.1) | data formatting | bytes 4194304 | tf_op jit(solution)/shard_map/reshape | solution.py:128
  16.8 0.8 %multiply_cosine_fusion = (f32[4,8,64]{2,0,1:T(4,128)}, f32[4,8,64]{2,0,1:T(4,128)}) fusion(f32[64]{0:T(128)S(1)} %multiply_power_fusion, f32[4,8]{0,1:T(8,128)S(1)} %add_convert_fusion), kind=kLoop, calls=%fused_computation.51 | loop fusion | flops 2048 | bytes 16768 | tf_op jit(solution)/shard_map/cos | solution.py:17
  17.6 4.0 %fusion.43 = (f32[4,8,2,8]{3,0,2,1:T(4,128)}, f32[4,8,2,8,512]{4,3,0,2,1:T(8,128)}) fusion(bf16[4,8,2,8,128]{4,1,3,2,0:T(8,128)(2,1)S(1)} %bitcast.74, bf16[8,512,2,128,1]{3,2,1,0,4:T(2,128)(2,1)} %bitcast.77, pred[8,512]{1,0:T(8,128)(4,1)S(1)} %iota_compare_fusion), kind=kOutput, calls=%fused_computation.82 | convolution fusion | flops 67894784 | bytes 3282944 | tf_op jit(solution)/shard_map/tbhge,bphe->tbhgp/dot_general | solution.py:132
  21.6 0.6 %pad_clamp_fusion = s32[1024]{0:T(1024)} fusion(s32[4]{0:T(128)S(1)} %xor_bitcast_fusion), kind=kLoop, calls=%fused_computation.64 | loop fusion | flops 1024 | bytes 4112 | tf_op jit(solution)/shard_map/jit(_take)/gather | solution.py:112
  22.2 0.0 collective-permute-done.4
  22.2 0.0 collective-permute-done.3
  22.2 0.0 collective-permute-done.5
  22.2 1.0 %pad_maximum_fusion = bf16[4,224,128]{1,2,0:T(8,128)(2,1)S(1)} fusion(bf16[1,224,128]{1,2,0:T(8,128)(2,1)} %bitcast.7, bf16[1,224,128]{1,2,0:T(8,128)(2,1)S(1)} %bitcast.84, bf16[1,224,128]{1,2,0:T(8,128)(2,1)S(1)} %bitcast.85, bf16[1,224,128]{1,2,0:T(8,128)(2,1)S(1)} %fusion.51), kind=kLoop, calls=%fused_computation.24 | loop fusion | flops 344064 | bytes 458752 | tf_op jit(solution)/shard_map/stack | solution.py:39
  23.2 0.7 %gather_fusion = bf16[4,224,128]{1,2,0:T(8,128)(2,1)S(1)} fusion(bf16[4,224,128]{1,2,0:T(8,128)(2,1)S(1)} %pad_maximum_fusion, s32[1024]{0:T(1024)} %pad_clamp_fusion.1), kind=kCustom, calls=%fused_computation | custom fusion | bytes 458768 | tf_op jit(solution)/shard_map/jit(_take)/gather | solution.py:81
  23.9 0.1 slice.77
  24.0 0.1 copy.35
  24.1 0.1 reshape.150
  24.2 0.1 pad_maximum_fusion.1
  24.3 0.2 copy.34
  24.5 0.2 reshape.149
  24.6 0.2 fusion.42
  24.9 0.1 pad_maximum_fusion.4
  25.0 0.1 collective-permute-start.6
  25.1 0.3 collective-permute-start.7
  25.4 1.5 %collective-permute-start.8 = (bf16[96,128]{1,0:T(8,128)(2,1)S(1)}, bf16[96,128]{1,0:T(8,128)(2,1)S(1)}, u32[]{:S(2)}, u32[]{:S(2)}) collective-permute-start(bf16[96,128]{1,0:T(8,128)(2,1)S(1)} %get-tuple-element.18), channel_id=1, source_target_pairs={{0,3},{1,2},{2,1},{3,0},{4,7},{5,6},{6,5},{7,4},{8,11},{9,10},{10,... | collective-permute-start | bytes 73736 | tf_op jit(solution)/shard_map/ppermute | solution.py:33
  26.9 0.0 copy-start.6
  26.9 0.0 copy-start.7
  26.9 2.1 %reshape.157 = bf16[8,512,2,128]{3,2,1,0:T(2,128)(2,1)} reshape(bf16[8,512,256]{2,1,0:T(8,128)(2,1)S(1)} %copy-done.2) | data formatting | bytes 4194304 | tf_op jit(solution)/shard_map/reshape | solution.py:129
  29.0 0.0 collective-permute-done.6
  29.0 0.4 %collective-permute-start.1 = (f32[32,512]{1,0:T(8,128)S(1)}, f32[32,512]{1,0:T(8,128)S(1)}, u32[]{:S(2)}, u32[]{:S(2)}) collective-permute-start(f32[32,512]{1,0:T(8,128)S(1)} %get-tuple-element.7), channel_id=1, source_target_pairs={{0,2},{1,3},{2,0},{3,1},{4,6},{5,7},{6,4},{7,5},{8,10},{9,11},{10,... | collective-permute-start | bytes 196616 | tf_op jit(solution)/shard_map/ppermute | solution.py:33
  29.4 0.0 collective-permute-done.7
  29.5 0.0 collective-permute-done.8
  29.5 0.1 convert_add_fusion
  29.6 0.1 fusion.38
  29.7 0.7 %gather_fusion.1 = bf16[4,16,512]{2,1,0:T(8,128)(2,1)S(1)} fusion(bf16[4,16,512]{2,1,0:T(8,128)(2,1)S(1)} %pad_maximum_fusion.3, s32[1024]{0:T(1024)} %pad_clamp_fusion), kind=kCustom, calls=%fused_computation.1 | custom fusion | bytes 131088 | tf_op jit(solution)/shard_map/jit(_take)/gather | solution.py:112
  30.4 0.1 fusion.45
  30.5 0.0 collective-permute-done
  30.5 0.0 collective-permute-done.2
  30.5 2.9 %collective-permute-done.1 = f32[32,512]{1,0:T(8,128)S(1)} collective-permute-done((f32[32,512]{1,0:T(8,128)S(1)}, f32[32,512]{1,0:T(8,128)S(1)}, u32[]{:S(2)}, u32[]{:S(2)}) %collective-permute-start.1) | collective-permute-done | bytes 65568 | tf_op jit(solution)/shard_map/ppermute | solution.py:33
  33.4 0.2 add_add_fusion
  33.6 0.1 multiply_reduce_fusion
  33.8 0.1 multiply_multiply_fusion
  33.9 0.1 multiply_subtract_fusion
  34.0 0.1 maximum_convert_fusion
  34.1 0.6 %copy.94 = bf16[4,8,2,128]{3,1,2,0:T(8,128)(2,1)} copy(bf16[4,8,2,128]{3,0,2,1:T(4,128)(2,1)S(1)} %maximum_convert_fusion) | data formatting | bytes 32768 | tf_op jit(solution)/shard_map/convert_element_type | solution.py:123
  34.7 0.6 %copy.93 = bf16[4,8,2,1,128]{4,1,3,2,0:T(8,128)(2,1)} copy(bf16[4,8,2,1,128]{4,0,2,1,3:T(4,128)(2,1)S(1)} %copy.55) | data formatting | bytes 32768 | tf_op jit(solution)/shard_map/convert_element_type | solution.py:121
  35.3 0.7 %fusion.44 = (f32[4,8,2,8]{3,0,2,1:T(4,128)S(1)}, f32[4,8,2,8,4]{3,4,0,2,1:T(4,128)S(1)}) fusion(bf16[4,8,2,8,128]{4,1,3,2,0:T(8,128)(2,1)S(1)} %bitcast.75, bf16[4,8,2,128]{3,0,2,1:T(4,128)(2,1)S(1)} %maximum_convert_fusion, pred[4,4]{1,0:T(4,128)(4,1)S(1)} %iota_compare_fusion.1), kind=kOutput, calls=%fused_computation.83 | convolution fusion | flops 529920 | bytes 157712 | tf_op jit(solution)/shard_map/tbhge,sbhe->tbhgs/dot_general | solution.py:138
  36.0 0.1 fusion.30
  36.2 0.4 fusion.25
  36.6 0.3 convolution_bitcast_fusion
  36.9 0.6 %fusion.19 = bf16[4,8,2,8,128]{4,3,0,2,1:T(8,128)(2,1)S(1)} fusion(f32[4,8,2,8,128]{4,3,0,2,1:T(8,128)S(1)} %convolution_bitcast_fusion, bf16[8,512,2,128,1]{3,2,1,0,4:T(2,128)(2,1)S(1)} %bitcast.76, f32[4,8,2,8,512]{4,3,0,2,1:T(8,128)S(1)} %copy-done.4, f32[4,8,2,8]{3,0,2,1:T(4,128)S(1)} %add.108, f32[4,8,2,8]{3,0,2,1:T(4,128)S(1)} %max.8), kind=kOutput, calls=%fused_computation.12 | convolution fusion | flops 68026368 | bytes 3543040 | tf_op jit(solution)/shard_map/tbhgp,bphe->tbhge/dot_general | solution.py:155
  37.5 0.7 %convert_element_type.83 = bf16[4,8,2048]{2,1,0:T(8,128)(2,1)} reshape(bf16[4,8,2,8,128]{4,3,2,1,0:T(8,128)(2,1)S(1)} %copy.41) | data formatting | bytes 262144 | tf_op jit(solution)/shard_map/convert_element_type | solution.py:161
  (45 shorter events, 0.4 us)
Async XLA Ops:
  0.6 17.0 %copy-start = (bf16[4,8,2048]{2,1,0:T(8,128)(2,1)S(1)}, bf16[4,8,2048]{2,1,0:T(8,128)(2,1)}, u32[]{:S(2)}) copy-start(bf16[4,8,2048]{2,1,0:T(8,128)(2,1)} %param.15) | copy-start | bytes 393220
  2.6 19.6 %collective-permute-start.4 = (bf16[224,128]{0,1:T(8,128)(2,1)S(1)}, bf16[224,128]{0,1:T(8,128)(2,1)S(1)}, u32[]{:S(2)}, u32[]{:S(2)}) collective-permute-start(bf16[224,128]{0,1:T(8,128)(2,1)S(1)} %pad_maximum_fusion.2), channel_id=1, source_target_pairs={{0,8},{4,12},{8,0},{12,4},{1,9},{5,13},{9,1},{13,5},{2,10},{6,14},... | collective-permute-start | bytes 172040 | tf_op jit(solution)/shard_map/ppermute | solution.py:33
  6.7 15.5 %collective-permute-start.3 = (bf16[224,128]{0,1:T(8,128)(2,1)S(1)}, bf16[224,128]{0,1:T(8,128)(2,1)S(1)}, u32[]{:S(2)}, u32[]{:S(2)}) collective-permute-start(bf16[224,128]{0,1:T(8,128)(2,1)S(1)} %pad_maximum_fusion.2), channel_id=1, source_target_pairs={{0,4},{4,0},{8,12},{12,8},{1,5},{5,1},{9,13},{13,9},{2,6},{6,2},{1... | collective-permute-start | bytes 172040 | tf_op jit(solution)/shard_map/ppermute | solution.py:33
  8.2 14.0 %collective-permute-start.5 = (bf16[224,128]{0,1:T(8,128)(2,1)S(1)}, bf16[224,128]{0,1:T(8,128)(2,1)}, u32[]{:S(2)}, u32[]{:S(2)}) collective-permute-start(bf16[224,128]{0,1:T(8,128)(2,1)S(1)} %pad_maximum_fusion.2), channel_id=1, source_target_pairs={{0,12},{4,8},{8,4},{12,0},{1,13},{5,9},{9,5},{13,1},{2,14},{6,10},... | collective-permute-start | bytes 172040 | tf_op jit(solution)/shard_map/ppermute | solution.py:33
  8.2 5.6 %copy-start.9 = (s32[8]{0:T(128)S(1)}, s32[8]{0:T(128)}, u32[]{:S(2)}) copy-start(s32[8]{0:T(128)} %param.18) | copy-start | bytes 100
  8.2 5.9 %copy-start.11 = (s32[4]{0:T(128)S(1)}, s32[4]{0:T(128)}, u32[]{:S(2)}) copy-start(s32[4]{0:T(128)} %param.19) | copy-start | bytes 52
  8.3 6.5 %copy-start.1 = (bf16[8,512,256]{2,1,0:T(8,128)(2,1)S(1)}, bf16[8,512,256]{2,1,0:T(8,128)(2,1)}, u32[]{:S(2)}) copy-start(bf16[8,512,256]{2,1,0:T(8,128)(2,1)} %param.16) | copy-start | bytes 6291460
  12.0 18.6 %collective-permute-start = (f32[32,512]{1,0:T(8,128)S(1)}, f32[32,512]{1,0:T(8,128)S(1)}, u32[]{:S(2)}, u32[]{:S(2)}) collective-permute-start(f32[32,512]{1,0:T(8,128)S(1)} %get-tuple-element.5), channel_id=1, source_target_pairs={{0,1},{1,0},{2,3},{3,2},{4,5},{5,4},{6,7},{7,6},{8,9},{9,8},{10,11... | collective-permute-start | bytes 196616 | tf_op jit(solution)/shard_map/ppermute | solution.py:33
  12.0 18.5 %collective-permute-start.2 = (f32[32,512]{1,0:T(8,128)S(1)}, f32[32,512]{1,0:T(8,128)S(1)}, u32[]{:S(2)}, u32[]{:S(2)}) collective-permute-start(f32[32,512]{1,0:T(8,128)S(1)} %get-tuple-element.6), channel_id=1, source_target_pairs={{0,3},{1,2},{2,1},{3,0},{4,7},{5,6},{6,5},{7,4},{8,11},{9,10},{10,... | collective-permute-start | bytes 196616 | tf_op jit(solution)/shard_map/ppermute | solution.py:33
  21.6 3.0 %copy-start.5 = (bf16[4,8,1280]{2,1,0:T(8,128)(2,1)S(1)}, bf16[4,8,1280]{2,1,0:T(8,128)(2,1)}, u32[]{:S(2)}) copy-start(bf16[4,8,1280]{2,1,0:T(8,128)(2,1)} %param.10) | copy-start | bytes 245764
  21.6 5.3 %copy-start.2 = (bf16[8,512,256]{2,1,0:T(8,128)(2,1)S(1)}, bf16[8,512,256]{2,1,0:T(8,128)(2,1)}, u32[]{:S(2)}) copy-start(bf16[8,512,256]{2,1,0:T(8,128)(2,1)} %param.17) | copy-start | bytes 6291460
  25.0 4.0 %collective-permute-start.6 = (bf16[96,128]{1,0:T(8,128)(2,1)S(1)}, bf16[96,128]{1,0:T(8,128)(2,1)S(1)}, u32[]{:S(2)}, u32[]{:S(2)}) collective-permute-start(bf16[96,128]{1,0:T(8,128)(2,1)S(1)} %get-tuple-element.16), channel_id=1, source_target_pairs={{0,1},{1,0},{2,3},{3,2},{4,5},{5,4},{6,7},{7,6},{8,9},{9,8},{10,11... | collective-permute-start | bytes 73736 | tf_op jit(solution)/shard_map/ppermute | solution.py:33
  25.1 4.3 %collective-permute-start.7 = (bf16[96,128]{1,0:T(8,128)(2,1)S(1)}, bf16[96,128]{1,0:T(8,128)(2,1)S(1)}, u32[]{:S(2)}, u32[]{:S(2)}) collective-permute-start(bf16[96,128]{1,0:T(8,128)(2,1)S(1)} %get-tuple-element.17), channel_id=1, source_target_pairs={{0,2},{1,3},{2,0},{3,1},{4,6},{5,7},{6,4},{7,5},{8,10},{9,11},{10,... | collective-permute-start | bytes 73736 | tf_op jit(solution)/shard_map/ppermute | solution.py:33
  25.4 4.1 %collective-permute-start.8 = (bf16[96,128]{1,0:T(8,128)(2,1)S(1)}, bf16[96,128]{1,0:T(8,128)(2,1)S(1)}, u32[]{:S(2)}, u32[]{:S(2)}) collective-permute-start(bf16[96,128]{1,0:T(8,128)(2,1)S(1)} %get-tuple-element.18), channel_id=1, source_target_pairs={{0,3},{1,2},{2,1},{3,0},{4,7},{5,6},{6,5},{7,4},{8,11},{9,10},{10,... | collective-permute-start | bytes 73736 | tf_op jit(solution)/shard_map/ppermute | solution.py:33
  26.9 6.9 %copy-start.10 = (f32[128]{0:T(128)S(1)}, f32[128]{0:T(128)}, u32[]{:S(2)}) copy-start(f32[128]{0:T(128)} %param.14) | copy-start | bytes 1540
  26.9 7.0 %copy-start.6 = (f32[4,8,64]{2,0,1:T(4,128)S(1)}, f32[4,8,64]{2,0,1:T(4,128)}, u32[]{:S(2)}) copy-start(f32[4,8,64]{2,0,1:T(4,128)} %get-tuple-element.21) | copy-start | bytes 24580
  26.9 7.0 %copy-start.7 = (f32[4,8,64]{2,0,1:T(4,128)S(1)}, f32[4,8,64]{2,0,1:T(4,128)}, u32[]{:S(2)}) copy-start(f32[4,8,64]{2,0,1:T(4,128)} %get-tuple-element.22) | copy-start | bytes 24580
  29.0 7.0 %copy-start.8 = (f32[4,8,2,8]{3,0,2,1:T(4,128)S(1)}, f32[4,8,2,8]{3,0,2,1:T(4,128)}, u32[]{:S(2)}) copy-start(f32[4,8,2,8]{3,0,2,1:T(4,128)} %get-tuple-element.23) | copy-start | bytes 6148
  29.0 7.2 %copy-start.4 = (f32[4,8,2,8,512]{4,3,0,2,1:T(8,128)S(1)}, f32[4,8,2,8,512]{4,3,0,2,1:T(8,128)}, u32[]{:S(2)}) copy-start(f32[4,8,2,8,512]{4,3,0,2,1:T(8,128)} %get-tuple-element.24) | copy-start | bytes 3145732
  29.0 4.4 %collective-permute-start.1 = (f32[32,512]{1,0:T(8,128)S(1)}, f32[32,512]{1,0:T(8,128)S(1)}, u32[]{:S(2)}, u32[]{:S(2)}) collective-permute-start(f32[32,512]{1,0:T(8,128)S(1)} %get-tuple-element.7), channel_id=1, source_target_pairs={{0,2},{1,3},{2,0},{3,1},{4,6},{5,7},{6,4},{7,5},{8,10},{9,11},{10,... | collective-permute-start | bytes 196616 | tf_op jit(solution)/shard_map/ppermute | solution.py:33
  30.4 6.5 %copy-start.3 = (bf16[8,512,2,128]{3,2,1,0:T(2,128)(2,1)S(1)}, bf16[8,512,2,128]{3,2,1,0:T(2,128)(2,1)}, u32[]{:S(2)}) copy-start(bf16[8,512,2,128]{3,2,1,0:T(2,128)(2,1)} %reshape.157) | copy-start | bytes 6291460

commit v2 on v1

--- a/solution.py
+++ b/solution.py
@@ -28,17 +28,8 @@
     return raw_keys * lax.rsqrt(mean_square + norm_eps) * key_gain
 
 
-def swap(block, axis, offset):
-    count = lax.axis_size(axis)
-    return lax.ppermute(block, axis, [(s, s ^ offset) for s in range(count)])
-
-
-def gather_by_offset(block, axis):
-    count = lax.axis_size(axis)
-    if count <= 8:
-        return jnp.stack([block] + [swap(block, axis, i) for i in range(1, count)])
-    whole = lax.all_gather(block, axis, axis=0, tiled=False)
-    return jnp.take(whole, jnp.arange(count) ^ lax.axis_index(axis), axis=0, mode="clip")
+def exchange(blocks, axis):
+    return lax.all_to_all(blocks, axis, split_axis=0, concat_axis=0)
 
 
 def per_device(
@@ -55,7 +46,6 @@
 ):
     replicas = lax.axis_size("rollout")
     shards = lax.axis_size("tensor")
-    replica = lax.axis_index("rollout")
     shard = lax.axis_index("tensor")
     down_rows, rank_size = adapter_down.shape
     up_columns = adapter_up.shape[1]
@@ -69,16 +59,14 @@
     half = down_rows // 2
     down_packed = jnp.concatenate([adapter_down[:half], adapter_down[half:]], axis=1)
     packed = jnp.concatenate([down_packed, up_part.reshape(-1, 2 * rank_size)], axis=0)
-    pieces = gather_by_offset(packed, "rollout")
+    pieces = exchange(jnp.broadcast_to(packed, (replicas,) + packed.shape), "rollout")
 
     tokens = normed_tokens.reshape(step_count * row_count, depth)
     base = jnp.dot(tokens, key_value_weight, preferred_element_type=jnp.float32)
-    joined = lax.dynamic_slice_in_dim(base, shard * own_columns, own_columns, axis=1)
-    for i in range(1, shards):
-        block = lax.dynamic_slice_in_dim(base, (shard ^ i) * own_columns, own_columns, axis=1)
-        joined = joined + swap(block, "tensor", i)
+    blocks = base.reshape(-1, shards, own_columns).transpose(1, 0, 2)
+    joined = jnp.sum(exchange(blocks, "tensor"), axis=0)
 
-    ordered = jnp.take(pieces, owners ^ replica, axis=0, mode="clip")
+    ordered = jnp.take(pieces, owners, axis=0, mode="clip")
     down_ordered = ordered[:, :half]
     down_matrix = jnp.concatenate(
         [down_ordered[:, :, :rank_size], down_ordered[:, :, rank_size:]], axis=1
@@ -94,24 +82,18 @@
     low = (lowered - high.astype(jnp.float32)).astype(jnp.bfloat16)
     lowered_packed = jnp.concatenate([high, low], axis=1)
 
-    sums = []
-    ups = []
-    for i in range(shards):
-        up_block = lax.dynamic_slice_in_dim(
-            up_matrix, (shard ^ i) * own_columns, own_columns, axis=1
-        )
-        block = jnp.concatenate([lowered_packed, up_block.reshape(-1, 2 * rank_size)], axis=0)
-        if i:
-            block = swap(block, "tensor", i)
-        sums.append(block[: step_count * row_count])
-        ups.append(block[step_count * row_count :].reshape(rank_part, own_columns))
-    total = sum(s.astype(jnp.float32) for s in sums)
+    row_total = step_count * row_count
+    up_blocks = up_matrix.reshape(rank_part, shards, own_columns).transpose(1, 0, 2)
+    up_blocks = up_blocks.reshape(shards, -1, 2 * rank_size)
+    blocks = jnp.concatenate(
+        [jnp.broadcast_to(lowered_packed, (shards,) + lowered_packed.shape), up_blocks], axis=1
+    )
+    blocks = exchange(blocks, "tensor")
+    total = jnp.sum(blocks[:, :row_total].astype(jnp.float32), axis=0)
     total = total[:, :rank_size] + total[:, rank_size:]
     total_high = total.astype(jnp.bfloat16)
     total_low = (total - total_high.astype(jnp.float32)).astype(jnp.bfloat16)
-    up_own = jnp.take(jnp.stack(ups), jnp.arange(shards) ^ shard, axis=0, mode="clip").reshape(
-        rank_size, own_columns
-    )
+    up_own = blocks[:, row_total:].reshape(rank_size, own_columns)
     raised_up = jnp.dot(total_high, up_own, preferred_element_type=jnp.float32) + jnp.dot(
         total_low, up_own, preferred_element_type=jnp.float32
     )

time: 38.5 us -> 59.1 us (1.54)
  local copies, waits for them, and re-layouts: 10.1 us -> 18.1 us
  waiting for transfers between devices: 2.9 us -> 8.47 us
  starting transfers between devices: 9.84 us -> 13 us
  other arithmetic: 4.58 us -> 6.86 us
  matrix products: 9.69 us -> 10.8 us
    all_to_all x0 -> x3, starting transfers between devices: none -> 13 us  [exchange(): return lax.all_to_all(blocks, axis, split_axis=0, concat_axis=0)]
    ppermute x9 -> x0, starting transfers between devices: 9.84 us -> none  [swap(): return lax.ppermute(block, axis, [(s, s ^ offset) for s in range(count)])]
    all_to_all x0 -> x3, waiting for transfers between devices: none -> 8.47 us  [exchange(): return lax.all_to_all(blocks, axis, split_axis=0, concat_axis=0)]
    dot_general x0 -> x1, local copies, waits for them, and re-layouts: none -> 8.04 us  [per_device(): base = jnp.dot(tokens, key_value_weight, preferred_element_type=jnp.float32)]
    ppermute x9 -> x0, waiting for transfers between devices: 2.9 us -> none  [swap(): return lax.ppermute(block, axis, [(s, s ^ offset) for s in range(count)])]
    gather x2 -> x1, other arithmetic: 1.2 us -> 0.01 us  [per_device(): ordered = jnp.take(pieces, owners, axis=0, mode='clip')]
    reduce_sum x1, other arithmetic: 0.38 us -> 1.56 us  [per_device(): jnp.sum(raised_cached, axis=-1, keepdims=True)]
    dot_general x1, matrix products: 3.68 us -> 4.82 us  [per_device(): base = jnp.dot(tokens, key_value_weight, preferred_element_type=jnp.float32)]
  transfers between devices with their start and end apart: 9 -> 3, of which waited for: 1 -> 2; matrix products, arithmetic and copies ran while one was open for 47% -> 44% of each run, Pallas kernels for 0% -> 0%
where the time goes in v2:
time: 59.1 us; the launch traced here: 58.2 us
  local copies, waits for them, and re-layouts  18.1 us (31%)
  starting transfers between devices  13 us (22%)
  matrix products  10.8 us (18%)
  waiting for transfers between devices  8.47 us (14%)
  other arithmetic  6.86 us (12%)
  between operations  0.89 us (2%)
    all_to_all x3, starting transfers between devices, exchange(): return lax.all_to_all(blocks, axis, split_axis=0, concat_axis=0)  13 us
    all_to_all x3, waiting for transfers between devices, exchange(): return lax.all_to_all(blocks, axis, split_axis=0, concat_axis=0)  8.47 us
    dot_general x1, local copies, waits for them, and re-layouts, per_device(): base = jnp.dot(tokens, key_value_weight, preferred_element_type=jnp.float32)  8.04 us
    dot_general x1, matrix products, per_device(): base = jnp.dot(tokens, key_value_weight, preferred_element_type=jnp.float32)  4.82 us
    dot_general x1, matrix products, per_device(): jnp.einsum('tbhge,bphe->tbhgp', query_heads, keys_local, preferred_elemen...  3.98 us
    reshape x1, local copies, waits for them, and re-layouts, per_device(): values_local = stored_values.reshape(row_count, -1, head_count, head_size)  2.54 us
    reshape x1, local copies, waits for them, and re-layouts, per_device(): keys_local = cache_keys.reshape(row_count, -1, head_count, head_size)  2.1 us
    reduce_sum x1, other arithmetic, per_device(): jnp.sum(raised_cached, axis=-1, keepdims=True)  1.56 us
  transfers between devices with their start and end apart: 3, of which 2 were waited for; matrix products, arithmetic and copies ran while one was open for 44% of the time, Pallas kernels for 0%

profile of v2, /device:TPU:0, one launch (start us, length us, event | category | flops | bytes accessed | tf_op | source)
XLA Modules:
  0.0 58.2 jit_solution(1172657526410247960)
XLA Ops:
  0.6 0.0 copy-start
  0.6 0.8 %constant_dynamic-slice_fusion = bf16[16,512]{1,0:T(8,128)(2,1)S(1)} fusion(bf16[64,512]{1,0:T(8,128)(2,1)} %param.13, s32[]{:T(128)S(6)} %select_n.16), kind=kLoop, calls=%fused_computation.62 | loop fusion | bytes 32772 | tf_op jit(solution)/shard_map/dynamic_slice | solution.py:58
  1.4 0.1 copy.36
  1.6 0.9 %fusion.41 = (bf16[160,64]{0,1:T(8,128)(2,1)S(1)}, bf16[160,64]{0,1:T(8,128)(2,1)S(1)}) fusion(bf16[320,64]{0,1:T(8,128)(2,1)} %param.12), kind=kLoop, calls=%fused_computation.65 | loop fusion | bytes 81920 | tf_op jit(solution)/shard_map/slice | solution.py:60
  2.5 0.1 pad_maximum_fusion.2
  2.6 0.1 copy.37
  2.7 0.7 %broadcast_in_dim.35 = bf16[4,224,128]{2,1,0:T(8,128)(2,1)} broadcast(bf16[224,128]{1,0:T(8,128)(2,1)S(1)} %copy.37), dimensions={1,2} | broadcast | bytes 286720 | tf_op jit(solution)/shard_map/broadcast_in_dim | solution.py:62
  3.4 6.3 %all-to-all-start.1 = ((bf16[4,224,128]{2,1,0:T(8,128)(2,1)}), bf16[4,224,128]{2,1,0:T(8,128)(2,1)S(1)}, u32[]{:S(2)}, u32[]{:S(2)}) async-start(bf16[4,224,128]{2,1,0:T(8,128)(2,1)} %broadcast_in_dim.35), calls=%async_computation.1 | async-start | bytes 458752 | tf_op jit(solution)/shard_map/all_to_all | solution.py:32
  9.7 0.7 %add_convert_fusion = f32[4,8]{0,1:T(8,128)S(1)} fusion(s32[8]{0:T(128)} %param.18), kind=kLoop, calls=%fused_computation.59 | loop fusion | flops 64 | bytes 160 | tf_op jit(solution)/shard_map/convert_element_type | solution.py:16
  10.5 0.7 %iota_compare_fusion = pred[8,512]{1,0:T(8,128)(4,1)S(1)} fusion(s32[8]{0:T(128)} %param.18), kind=kLoop, calls=%fused_computation.54 | loop fusion | flops 4096 | bytes 4128 | tf_op jit(solution)/shard_map/lt | solution.py:117
  11.2 0.0 copy-start.5
  11.2 0.0 copy-start.1
  11.2 8.0 %copy.51 = bf16[2048,1280]{1,0:T(8,128)(2,1)} copy(bf16[2048,1280]{0,1:T(8,128)(2,1)} %bitcast.69) | data formatting | bytes 10485760 | tf_op jit(solution)/shard_map/dot_general | solution.py:65
  19.2 0.0 copy-done.5
  19.2 0.0 copy-done.1
  19.3 2.1 %reshape.125 = bf16[8,512,2,128]{3,2,1,0:T(2,128)(2,1)} reshape(bf16[8,512,256]{2,1,0:T(8,128)(2,1)S(1)} %copy-done.1) | data formatting | bytes 4194304 | tf_op jit(solution)/shard_map/reshape | solution.py:110
  21.4 2.5 %reshape.132 = bf16[8,512,2,128]{3,2,1,0:T(2,128)(2,1)S(1)} reshape(bf16[8,512,256]{2,1,0:T(8,128)(2,1)} %param.17) | data formatting | bytes 4194304 | tf_op jit(solution)/shard_map/reshape | solution.py:111
  23.9 0.0 copy-start.3
  23.9 0.8 %multiply_cosine_fusion = (f32[4,8,64]{2,0,1:T(4,128)S(1)}, f32[4,8,64]{2,0,1:T(4,128)}) fusion(f32[64]{0:T(128)S(1)} %multiply_power_fusion, f32[4,8]{0,1:T(8,128)S(1)} %add_convert_fusion), kind=kLoop, calls=%fused_computation.46 | loop fusion | flops 2048 | bytes 16768 | tf_op jit(solution)/shard_map/cos | solution.py:17
  24.7 0.0 copy-done
  24.7 4.0 %fusion.42 = (f32[4,8,2,8]{3,0,2,1:T(4,128)}, f32[4,8,2,8,512]{4,3,0,2,1:T(8,128)}) fusion(bf16[4,8,2,8,128]{4,1,3,2,0:T(8,128)(2,1)S(1)} %bitcast.66, bf16[8,512,2,128,1]{3,2,1,0,4:T(2,128)(2,1)} %bitcast.71, pred[8,512]{1,0:T(8,128)(4,1)S(1)} %iota_compare_fusion), kind=kOutput, calls=%fused_computation.66 | convolution fusion | flops 67894784 | bytes 3282944 | tf_op jit(solution)/shard_map/tbhge,bphe->tbhgp/dot_general | solution.py:114
  28.7 0.0 copy-done.3
  28.7 4.8 %convolution_bitcast_fusion = f32[4,32,512]{2,1,0:T(8,128)} fusion(bf16[4,512,1280]{2,1,0:T(8,128)(2,1)} %bitcast.68, bf16[4,8,1280]{2,1,0:T(8,128)(2,1)S(1)} %copy-done.3), kind=kOutput, calls=%fused_computation.10 | convolution fusion | flops 167772160 | bytes 5586944 | tf_op jit(solution)/shard_map/dot_general | solution.py:65
  33.5 0.0 all-to-all-done.1
  33.5 3.4 %all-to-all-start = ((f32[4,32,512]{2,1,0:T(8,128)}), f32[4,32,512]{2,1,0:T(8,128)S(1)}, u32[]{:S(2)}, u32[]{:S(2)}) async-start(f32[4,32,512]{2,1,0:T(8,128)} %convolution_bitcast_fusion), calls=%async_computation | async-start | bytes 524288 | tf_op jit(solution)/shard_map/all_to_all | solution.py:32
  37.0 0.0 copy-start.4
  37.0 0.6 %gather_fusion = bf16[4,224,128]{2,1,0:T(8,128)(2,1)S(1)} fusion(bf16[4,224,128]{2,1,0:T(8,128)(2,1)S(1)} %all-to-all-done.1, s32[1024]{0:T(1024)S(1)} %pad_clamp_fusion), kind=kCustom, calls=%fused_computation | custom fusion | bytes 458768 | tf_op jit(solution)/shard_map/jit(_take)/gather | solution.py:69
  37.6 0.1 fusion.40
  37.7 0.1 pad_maximum_fusion
  37.8 0.2 subtract_convert_fusion.1
  38.0 0.1 pad_maximum_fusion.3
  38.1 0.7 %pad_maximum_fusion.1 = bf16[4,96,128]{2,1,0:T(8,128)(2,1)} fusion(bf16[4,64,128]{2,1,0:T(8,128)(2,1)S(1)} %slice.59, bf16[4,32,128]{2,1,0:T(8,128)(2,1)S(1)} %broadcast_in_dim.55), kind=kLoop, calls=%fused_computation.31 | loop fusion | flops 196608 | bytes 196608 | tf_op jit(solution)/shard_map/concatenate | solution.py:88
  38.7 4.2 %all-to-all-done = f32[4,32,512]{2,1,0:T(8,128)S(1)} async-done(((f32[4,32,512]{2,1,0:T(8,128)}), f32[4,32,512]{2,1,0:T(8,128)S(1)}, u32[]{:S(2)}, u32[]{:S(2)}) %all-to-all-start) | async-done | bytes 262176 | tf_op jit(solution)/shard_map/all_to_all | solution.py:32
  43.0 3.3 %all-to-all-start.2 = ((bf16[4,96,128]{2,1,0:T(8,128)(2,1)}), bf16[4,96,128]{2,1,0:T(8,128)(2,1)S(1)}, u32[]{:S(2)}, u32[]{:S(2)}) async-start(bf16[4,96,128]{2,1,0:T(8,128)(2,1)} %pad_maximum_fusion.1), calls=%async_computation.2 | async-start | bytes 196608 | tf_op jit(solution)/shard_map/all_to_all | solution.py:32
  46.3 4.2 %all-to-all-done.2 = bf16[4,96,128]{2,1,0:T(8,128)(2,1)S(1)} async-done(((bf16[4,96,128]{2,1,0:T(8,128)(2,1)}), bf16[4,96,128]{2,1,0:T(8,128)(2,1)S(1)}, u32[]{:S(2)}, u32[]{:S(2)}) %all-to-all-start.2) | async-done | bytes 98336 | tf_op jit(solution)/shard_map/all_to_all | solution.py:32
  50.5 0.1 fusion.38
  50.6 0.0 copy-start.2
  50.6 0.1 reshape.130
  50.7 0.1 fusion.44
  50.8 0.2 fusion.25
  51.0 0.1 multiply_reduce_fusion
  51.2 0.0 copy-done.4
  51.2 0.1 multiply_multiply_fusion
  51.3 0.8 %multiply_subtract_fusion = (bf16[4,8,2,64]{3,0,2,1:T(4,128)(2,1)S(1)}, bf16[4,8,2,64]{3,0,2,1:T(4,128)(2,1)S(1)}) fusion(f32[4,8,2,128]{3,0,2,1:T(4,128)S(1)} %multiply_multiply_fusion, f32[4,8,64]{2,0,1:T(4,128)} %get-tuple-element.12, f32[4,8,64]{2,0,1:T(4,128)S(1)} %get-tuple-element.11), kind=kLoop, calls=%fused_computation.42 | loop fusion | flops 32768 | bytes 65536 | tf_op jit(solution)/shard_map/sub | solution.py:22
  52.1 0.1 maximum_convert_fusion
  52.2 0.6 %copy.95 = bf16[4,8,2,128]{3,1,2,0:T(8,128)(2,1)} copy(bf16[4,8,2,128]{3,0,2,1:T(4,128)(2,1)S(1)} %maximum_convert_fusion) | data formatting | bytes 32768 | tf_op jit(solution)/shard_map/convert_element_type | solution.py:105
  52.8 0.7 %fusion.43 = (f32[4,8,2,8]{3,0,2,1:T(4,128)S(1)}, f32[4,8,2,8,4]{3,4,0,2,1:T(4,128)S(1)}) fusion(bf16[4,8,2,8,128]{4,1,3,2,0:T(8,128)(2,1)S(1)} %bitcast.67, bf16[4,8,2,128]{3,0,2,1:T(4,128)(2,1)S(1)} %maximum_convert_fusion, pred[4,4]{1,0:T(4,128)(4,1)S(1)} %iota_compare_fusion.1), kind=kOutput, calls=%fused_computation.67 | convolution fusion | flops 529920 | bytes 157712 | tf_op jit(solution)/shard_map/tbhge,sbhe->tbhgs/dot_general | solution.py:120
  53.5 0.8 %max.8 = f32[4,8,2,8]{3,0,2,1:T(4,128)S(1)} maximum(f32[4,8,2,8]{3,0,2,1:T(4,128)} %get-tuple-element.13, f32[4,8,2,8]{3,0,2,1:T(4,128)S(1)} %get-tuple-element.15) | non-fusion elementwise | flops 512 | bytes 6144 | tf_op jit(solution)/shard_map/max | solution.py:127
  54.3 1.6 %fusion.26 = f32[4,8,2,8]{3,0,2,1:T(4,128)S(1)} fusion(f32[4,8,2,8,512]{4,3,0,2,1:T(8,128)} %get-tuple-element.14, f32[4,8,2,8]{3,0,2,1:T(4,128)S(1)} %max.8), kind=kLoop, calls=%fused_computation.22 | loop fusion | flops 523776 | bytes 1052672 | tf_op jit(solution)/shard_map/reduce_sum | solution.py:132
  55.8 0.1 fusion.31
  56.0 0.3 convolution_bitcast_fusion.1
  56.3 0.0 copy-done.2
  56.3 0.6 fusion.19
  56.9 0.7 %convert_element_type.71 = bf16[4,8,2048]{2,1,0:T(8,128)(2,1)} reshape(bf16[4,8,2,8,128]{4,3,2,1,0:T(8,128)(2,1)S(1)} %copy.42) | data formatting | bytes 262144 | tf_op jit(solution)/shard_map/convert_element_type | solution.py:143
  57.6 0.6 %copy.94 = bf16[4,8,2,1,128]{4,1,3,2,0:T(8,128)(2,1)} copy(bf16[4,8,2,1,128]{4,0,2,1,3:T(4,128)(2,1)S(1)} %copy.56) | data formatting | bytes 32768 | tf_op jit(solution)/shard_map/convert_element_type | solution.py:103
  (15 shorter events, 0.2 us)
Async XLA Ops:
  0.6 24.1 %copy-start = (bf16[4,8,2048]{2,1,0:T(8,128)(2,1)S(1)}, bf16[4,8,2048]{2,1,0:T(8,128)(2,1)}, u32[]{:S(2)}) copy-start(bf16[4,8,2048]{2,1,0:T(8,128)(2,1)} %param.15) | copy-start | bytes 393220
  3.4 30.1 %all-to-all-start.1 = ((bf16[4,224,128]{2,1,0:T(8,128)(2,1)}), bf16[4,224,128]{2,1,0:T(8,128)(2,1)S(1)}, u32[]{:S(2)}, u32[]{:S(2)}) async-start(bf16[4,224,128]{2,1,0:T(8,128)(2,1)} %broadcast_in_dim.35), calls=%async_computation.1 | async-start | bytes 458752 | tf_op jit(solution)/shard_map/all_to_all | solution.py:32
  11.2 8.0 %copy-start.5 = (s32[4]{0:T(128)S(1)}, s32[4]{0:T(128)}, u32[]{:S(2)}) copy-start(s32[4]{0:T(128)} %param.19) | copy-start | bytes 52
  11.2 8.1 %copy-start.1 = (bf16[8,512,256]{2,1,0:T(8,128)(2,1)S(1)}, bf16[8,512,256]{2,1,0:T(8,128)(2,1)}, u32[]{:S(2)}) copy-start(bf16[8,512,256]{2,1,0:T(8,128)(2,1)} %param.16) | copy-start | bytes 6291460
  23.9 4.8 %copy-start.3 = (bf16[4,8,1280]{2,1,0:T(8,128)(2,1)S(1)}, bf16[4,8,1280]{2,1,0:T(8,128)(2,1)}, u32[]{:S(2)}) copy-start(bf16[4,8,1280]{2,1,0:T(8,128)(2,1)} %param.10) | copy-start | bytes 245764
  33.5 9.4 %all-to-all-start = ((f32[4,32,512]{2,1,0:T(8,128)}), f32[4,32,512]{2,1,0:T(8,128)S(1)}, u32[]{:S(2)}, u32[]{:S(2)}) async-start(f32[4,32,512]{2,1,0:T(8,128)} %convolution_bitcast_fusion), calls=%async_computation | async-start | bytes 524288 | tf_op jit(solution)/shard_map/all_to_all | solution.py:32
  37.0 14.2 %copy-start.4 = (f32[128]{0:T(128)S(1)}, f32[128]{0:T(128)}, u32[]{:S(2)}) copy-start(f32[128]{0:T(128)} %param.14) | copy-start | bytes 1540
  43.0 7.6 %all-to-all-start.2 = ((bf16[4,96,128]{2,1,0:T(8,128)(2,1)}), bf16[4,96,128]{2,1,0:T(8,128)(2,1)S(1)}, u32[]{:S(2)}, u32[]{:S(2)}) async-start(bf16[4,96,128]{2,1,0:T(8,128)(2,1)} %pad_maximum_fusion.1), calls=%async_computation.2 | async-start | bytes 196608 | tf_op jit(solution)/shard_map/all_to_all | solution.py:32
  50.6 5.7 %copy-start.2 = (f32[4,8,2,8,512]{4,3,0,2,1:T(8,128)S(1)}, f32[4,8,2,8,512]{4,3,0,2,1:T(8,128)}, u32[]{:S(2)}) copy-start(f32[4,8,2,8,512]{4,3,0,2,1:T(8,128)} %get-tuple-element.14) | copy-start | bytes 3145732

commit v3 on v0

v3 whole, which is shorter than its diff:
```python
import functools
import math

import jax
import jax.numpy as jnp
from jax import lax
from jax.experimental import pallas as pl
from jax.experimental.pallas import tpu as pltpu
from jax.sharding import PartitionSpec as P

norm_eps = 1e-06
rope_base = 1000000.0
adapter_scale = 2.0
masked_score = -1e30
lanes = 128
f32 = jnp.float32
bf16 = jnp.bfloat16

whole_in_vmem = pl.BlockSpec(memory_space=pltpu.VMEM)
whole_in_smem = pl.BlockSpec(memory_space=pltpu.SMEM)
left_in_place = pl.BlockSpec(memory_space=pl.ANY)


def swap(block, axis, offset):
    count = lax.axis_size(axis)
    return lax.ppermute(block, axis, [(s, s ^ offset) for s in range(count)])


def side_by_side(rows_of_blocks):
    r, c = rows_of_blocks.shape
    return rows_of_blocks.reshape(r, c // lanes, lanes).transpose(1, 0, 2).reshape(-1, lanes)


def split_halves(total):
    high = total.astype(bf16)
    return high, (total - high.astype(f32)).astype(bf16)


def pack_kernel(down_ref, up_ref, out_ref):
    half = down_ref.shape[0] // 2
    rank_part = (out_ref.shape[0] - half) * lanes // up_ref.shape[1]
    out_ref[:half, :] = jnp.concatenate([down_ref[:half, :], down_ref[half:, :]], axis=1)
    first = pl.multiple_of(lax.axis_index("tensor") * rank_part, rank_part)
    for c in range(up_ref.shape[1] // lanes):
        out_ref[half + c * rank_part : half + (c + 1) * rank_part, :] = up_ref[
            pl.ds(first, rank_part), c * lanes : (c + 1) * lanes
        ]


def pack(down, up, rank_part):
    rows = down.shape[0] // 2 + rank_part * up.shape[1] // lanes
    return pl.pallas_call(
        pack_kernel,
        out_shape=jax.ShapeDtypeStruct((rows, lanes), bf16),
        in_specs=[whole_in_vmem] * 2,
        out_specs=whole_in_vmem,
        name="pack",
        cost_estimate=pl.CostEstimate(flops=0, bytes_accessed=200000, transcendentals=0),
    )(down, up)


def front_kernel(
    step_count,
    row_count,
    head_count,
    shards,
    lengths_ref,
    tokens_ref,
    queries_ref,
    weight_ref,
    keys_ref,
    values_ref,
    base_ref,
    grouped_ref,
    total_ref,
    peak_ref,
    sum_ref,
    cosine_ref,
    sine_ref,
    weight_buf,
    keys_buf,
    values_buf,
    regroup,
    scores,
    raised,
    key_sems,
    value_sems,
    weight_sems,
):
    shard = lax.axis_index("tensor")
    own = base_ref.shape[2]
    slots = keys_buf.shape[1]
    group = queries_ref.shape[1] // (head_count * lanes)
    seen = step_count * group
    scale = lanes**-0.5

    key_copies = [
        pltpu.make_async_copy(keys_ref.at[b], keys_buf.at[b], key_sems.at[b])
        for b in range(row_count)
    ]
    value_copies = [
        pltpu.make_async_copy(values_ref.at[b], values_buf.at[b], value_sems.at[b])
        for b in range(row_count)
    ]
    weight_copies = [
        pltpu.make_async_copy(
            weight_ref.at[:, pl.ds(pl.multiple_of((shard ^ i) * own, lanes), own)],
            weight_buf.at[i],
            weight_sems.at[i],
        )
        for i in range(shards)
    ]
    for copy in key_copies + value_copies + weight_copies:
        copy.start()

    for pair in range(step_count // 2):
        for q in range(head_count * group):
            h, g = q // group, q % group
            both = queries_ref[
                pair * 2 * row_count : (pair + 1) * 2 * row_count, q * lanes : (q + 1) * lanes
            ].astype(f32)
            for side in range(2):
                first = h * row_count * seen + (pair * 2 + side) * group + g
                regroup[pl.ds(first, row_count, stride=seen), :] = both[
                    side * row_count : (side + 1) * row_count, :
                ]
    grouped_ref[...] = regroup[...].astype(bf16)

    rows = step_count * row_count
    row = lax.broadcasted_iota(jnp.int32, (rows, lanes), 0)
    lane = lax.broadcasted_iota(jnp.int32, (rows, lanes), 1)
    position = row // row_count
    for b in range(row_count):
        position = position + jnp.where(row % row_count == b, lengths_ref[b], 0)
    middle = lanes // 2
    spacing = (lane % middle).astype(f32) * (-2.0 / lanes * math.log(rope_base))
    angles = position.astype(f32) * jnp.exp(spacing)
    cosine_ref[...] = jnp.cos(angles)
    sine = jnp.sin(angles)
    sine_ref[...] = jnp.where(lane < middle, -sine, sine)

    for b in range(row_count):
        key_copies[b].wait()
        for h in range(head_count):
            at = (h * row_count + b) * seen
            scores[at : at + seen, :] = lax.dot_general(
                grouped_ref[at : at + seen, :],
                keys_buf[b, :, h * lanes : (h + 1) * lanes],
                (((1,), (1,)), ((), ())),
                preferred_element_type=f32,
            )
    slot = lax.broadcasted_iota(jnp.int32, (seen, slots), 1)
    for b in range(row_count):
        live = slot < lengths_ref[b]
        for h in range(head_count):
            at = (h * row_count + b) * seen
            score = jnp.where(live, scores[at : at + seen, :] * scale, masked_score)
            peak = jnp.max(score, axis=1, keepdims=True)
            lifted = jnp.exp(score - peak)
            raised[at : at + seen, :] = lifted.astype(bf16)
            peak_ref[at : at + seen, :] = jnp.broadcast_to(peak, (seen, lanes))
            sum_ref[at : at + seen, :] = jnp.broadcast_to(
                jnp.sum(lifted, axis=1, keepdims=True), (seen, lanes)
            )
    for b in range(row_count):
        value_copies[b].wait()
        for h in range(head_count):
            at = (h * row_count + b) * seen
            total_ref[at : at + seen, :] = jnp.dot(
                raised[at : at + seen, :],
                values_buf[b, :, h * lanes : (h + 1) * lanes],
                preferred_element_type=f32,
            )
    for i in range(shards):
        weight_copies[i].wait()
        base_ref[i] = jnp.dot(tokens_ref[...], weight_buf[i], preferred_element_type=f32)


def front(lengths, tokens, queries, weight, keys, values, step_count, shards):
    row_count, slots, width = keys.shape
    head_count = width // lanes
    depth, columns = weight.shape
    own = columns // shards
    rows = step_count * row_count
    seen_rows = rows * queries.shape[1] // lanes
    table = jax.ShapeDtypeStruct((rows, lanes), f32)
    seen_table = jax.ShapeDtypeStruct((seen_rows, lanes), f32)
    return pl.pallas_call(
        functools.partial(front_kernel, step_count, row_count, head_count, shards),
        out_shape=(
            jax.ShapeDtypeStruct((shards, rows, own), f32),
            jax.ShapeDtypeStruct((seen_rows, lanes), bf16),
            seen_table,
            seen_table,
            seen_table,
            table,
            table,
        ),
        in_specs=[whole_in_smem, whole_in_vmem, whole_in_vmem] + [left_in_place] * 3,
        out_specs=(whole_in_vmem,) * 7,
        scratch_shapes=[
            pltpu.VMEM((shards, depth, own), bf16),
            pltpu.VMEM(keys.shape, bf16),
            pltpu.VMEM(values.shape, bf16),
            pltpu.VMEM((seen_rows, lanes), f32),
            pltpu.VMEM((seen_rows, slots), f32),
            pltpu.VMEM((seen_rows, slots), bf16),
            pltpu.SemaphoreType.DMA((row_count,)),
            pltpu.SemaphoreType.DMA((row_count,)),
            pltpu.SemaphoreType.DMA((shards,)),
        ],
        compiler_params=pltpu.CompilerParams(vmem_limit_bytes=32 * 2**20),
        name="front",
        cost_estimate=pl.CostEstimate(
            flops=2 * rows * depth * columns + 4 * seen_rows * slots * lanes,
            bytes_accessed=2 * (weight.size + keys.size + values.size),
            transcendentals=seen_rows * slots,
        ),
    )(lengths, tokens, queries, weight, keys, values)


def route_kernel(replicas, shards, *refs):
    owners_ref, tokens_ref, base_ref = refs[:3]
    piece_refs = refs[3 : 3 + replicas]
    out_refs = refs[3 + replicas : 3 + replicas + shards]
    down_buf, up_buf = refs[3 + replicas + shards :]
    replica = lax.axis_index("rollout")
    shard = lax.axis_index("tensor")
    down_rows = down_buf.shape[0] // replicas
    rank = down_buf.shape[1]
    half = down_rows // 2
    for i in range(replicas):
        source = replica ^ i
        place = jnp.int32(0)
        for k in range(1, replicas):
            place = place + jnp.where(owners_ref[k] == source, k, 0)
        first = pl.multiple_of(place * down_rows, half)
        down_buf[pl.ds(first, half), :] = piece_refs[i][:half, :rank]
        second = pl.multiple_of(place * down_rows + half, half)
        down_buf[pl.ds(second, half), :] = piece_refs[i][:half, rank:]
        up_buf[i] = piece_refs[i][half:, :]
    lowered = jnp.dot(tokens_ref[...], down_buf[...], preferred_element_type=f32)
    both = jnp.concatenate(split_halves(lowered), axis=1)
    rows = tokens_ref.shape[0]
    for i in range(shards):
        first = 0
        if i:
            for c in range(base_ref.shape[2] // lanes):
                out_refs[i][first : first + rows, :] = base_ref[
                    i, :, c * lanes : (c + 1) * lanes
                ].astype(bf16)
                first += rows
        out_refs[i][first : first + rows, :] = both
        out_refs[i][first + rows :, :] = up_buf[owners_ref[shard ^ i] ^ replica]


def route(owners, tokens, base, pieces, down_rows, rank):
    shards, rows, own = base.shape
    replicas = len(pieces)
    up_rows = pieces[0].shape[0] - down_rows // 2
    sent = rows * own // lanes
    return pl.pallas_call(
        functools.partial(route_kernel, replicas, shards),
        out_shape=[
            jax.ShapeDtypeStruct(((sent if i else 0) + rows + up_rows, lanes), bf16)
            for i in range(shards)
        ],
        in_specs=[whole_in_smem] + [whole_in_vmem] * (2 + replicas),
        out_specs=[whole_in_vmem] * shards,
        scratch_shapes=[
            pltpu.VMEM((replicas * down_rows, rank), bf16),
            pltpu.VMEM((replicas, up_rows, lanes), bf16),
        ],
        name="route",
        cost_estimate=pl.CostEstimate(flops=0, bytes_accessed=800000, transcendentals=0),
    )(owners, tokens, base, *pieces)


def route_plain(owners, tokens, base, down, up, rank_part):
    shards, rows, own = base.shape
    rank = down.shape[1]
    shard = lax.axis_index("tensor")
    first = shard * rank_part
    up_part = lax.dynamic_slice_in_dim(up, first, rank_part, axis=0)
    downs = lax.all_gather(down, "rollout", axis=0, tiled=False)
    ups = lax.all_gather(up_part, "rollout", axis=0, tiled=False)
    down_matrix = jnp.take(downs, owners, axis=0, mode="clip").reshape(-1, rank)
    up_matrix = jnp.take(ups, owners, axis=0, mode="clip").transpose(1, 0, 2)
    up_matrix = up_matrix.reshape(rank_part, -1)
    lowered = jnp.dot(tokens, down_matrix, preferred_element_type=f32)
    both = jnp.concatenate(split_halves(lowered), axis=1)
    packets = []
    for i in range(shards):
        up_block = lax.dynamic_slice_in_dim(up_matrix, (shard ^ i) * own, own, axis=1)
        parts = [both, side_by_side(up_block)]
        if i:
            parts = [side_by_side(base[i].astype(bf16))] + parts
        packets.append(jnp.concatenate(parts, axis=0))
    return packets


def finish_kernel(step_count, row_count, head_count, shards, *refs):
    base_ref, gain_ref, grouped_ref, total_ref, peak_ref, sum_ref, cosine_ref, sine_ref = refs[:8]
    packet_refs = refs[8 : 8 + shards]
    attention_ref, keys_ref, values_ref = refs[8 + shards : 11 + shards]
    up_buf, ordered = refs[11 + shards :]
    shard = lax.axis_index("tensor")
    rows = step_count * row_count
    own = base_ref.shape[2]
    blocks = own // lanes
    rank = up_buf.shape[0]
    rank_part = rank // shards
    group = grouped_ref.shape[0] // (head_count * rows)
    seen = step_count * group
    scale = lanes**-0.5

    lowered = jnp.zeros((rows, lanes), f32)
    for i in range(shards):
        first = rows * blocks if i else 0
        lowered = lowered + packet_refs[i][first : first + rows, :].astype(f32)
        ups = packet_refs[i][first + rows :, :].astype(f32)
        at = pl.multiple_of((shard ^ i) * rank_part, rank_part)
        for c in range(blocks):
            up_buf[pl.ds(at, rank_part), c * lanes : (c + 1) * lanes] = ups[
                c * rank_part : (c + 1) * rank_part, :
            ]
    lane = lax.broadcasted_iota(jnp.int32, (rows, lanes), 1)
    lowered = lowered + pltpu.roll(lowered, rank, 1)
    high, low = split_halves(lowered)
    left = jnp.where(lane < rank, high.astype(f32), low.astype(f32)).astype(bf16)
    up = up_buf[...].astype(bf16)
    raised_up = jnp.dot(left, jnp.concatenate([up, up], axis=0), preferred_element_type=f32)
    joined = []
    for c in range(blocks):
        block = base_ref[0, :, c * lanes : (c + 1) * lanes]
        for i in range(1, shards):
            block = block + packet_refs[i][c * rows : (c + 1) * rows, :].astype(f32)
        joined.append(block + adapter_scale * raised_up[:, c * lanes : (c + 1) * lanes])

    all_rows = row_count * seen
    seen_by = lax.broadcasted_iota(jnp.int32, (all_rows, rows), 0)
    made_by = lax.broadcasted_iota(jnp.int32, (all_rows, rows), 1)
    visible = (seen_by // seen == made_by % row_count) & (
        made_by // row_count <= seen_by % seen // group
    )
    for h in range(head_count):
        raw_key = joined[2 * h]
        mean_square = jnp.mean(raw_key * raw_key, axis=1, keepdims=True)
        normed = raw_key * lax.rsqrt(mean_square + norm_eps) * gain_ref[...]
        key = normed * cosine_ref[...] + pltpu.roll(normed, lanes // 2, 1) * sine_ref[...]
        key = key.astype(bf16)
        value = joined[2 * h + 1].astype(bf16)
        keys_ref[:, h * lanes : (h + 1) * lanes] = key
        values_ref[:, h * lanes : (h + 1) * lanes] = value
        mine = slice(h * all_rows, (h + 1) * all_rows)
        score = lax.dot_general(
            grouped_ref[mine, :], key, (((1,), (1,)), ((), ())), preferred_element_type=f32
        )
        score = jnp.where(visible, score * scale, masked_score)
        old_peak = peak_ref[mine, :]
        peak = jnp.maximum(old_peak, jnp.max(score, axis=1, keepdims=True))
        fade = jnp.exp(old_peak - peak)
        lifted = jnp.exp(score - peak[:, :rows])
        denominator = fade * sum_ref[mine, :] + jnp.sum(lifted, axis=1, keepdims=True)
        total = fade * total_ref[mine, :] + jnp.dot(
            lifted.astype(bf16), value, preferred_element_type=f32
        )
        ordered[mine, :] = total / denominator
    for pair in range(step_count // 2):
        for q in range(head_count * group):
            h, g = q // group, q % group
            both = [
                ordered[
                    pl.ds(
                        h * all_rows + (pair * 2 + side) * group + g, row_count, stride=seen
                    ),
                    :,
                ]
                for side in range(2)
            ]
            attention_ref[
                pair * 2 * row_count : (pair + 1) * 2 * row_count, q * lanes : (q + 1) * lanes
            ] = jnp.concatenate(both, axis=0).astype(bf16)


def finish(partials, gain, packets, rank, step_count, row_count, query_width):
    base, grouped, total, peak, denominator, cosine, sine = partials
    shards, rows, own = base.shape
    head_count = own // (2 * lanes)
    return pl.pallas_call(
        functools.partial(finish_kernel, step_count, row_count, head_count, shards),
        out_shape=(
            jax.ShapeDtypeStruct((rows, query_width), bf16),
            jax.ShapeDtypeStruct((rows, head_count * lanes), bf16),
            jax.ShapeDtypeStruct((rows, head_count * lanes), bf16),
        ),
        in_specs=[whole_in_vmem] * (8 + shards),
        out_specs=(whole_in_vmem,) * 3,
        scratch_shapes=[
            pltpu.VMEM((rank, own), f32),
            pltpu.VMEM(total.shape, f32),
        ],
        name="finish",
        cost_estimate=pl.CostEstimate(flops=0, bytes_accessed=1000000, transcendentals=0),
    )(base, gain, grouped, total, peak, denominator, cosine, sine, *packets)


def per_device(
    normed_tokens,
    key_value_weight,
    adapter_down,
    adapter_up,
    key_gain,
    queries,
    cache_keys,
    stored_values,
    lengths,
    owners,
):
    replicas = lax.axis_size("rollout")
    shards = lax.axis_size("tensor")
    down_rows, rank = adapter_down.shape
    step_count, row_count, depth = normed_tokens.shape
    own = key_value_weight.shape[1] // shards
    rank_part = rank // shards
    rows = step_count * row_count
    tokens = normed_tokens.reshape(rows, depth)
    query_rows = queries.reshape(rows, -1)

    fits = (
        replicas <= 4 and adapter_up.shape[1] == own and down_rows % 32 == 0 and rank_part % 16 == 0
    )
    if fits:
        packed = pack(adapter_down, adapter_up, rank_part)
        pieces = [packed] + [swap(packed, "rollout", i) for i in range(1, replicas)]
    partials = front(
        lengths, tokens, query_rows, key_value_weight, cache_keys, stored_values, step_count, shards
    )
    base = partials[0]
    if fits:
        packets = route(owners, tokens, base, pieces, down_rows, rank)
    else:
        packets = route_plain(owners, tokens, base, adapter_down, adapter_up, rank_part)
    packets = [packets[0]] + [swap(packets[i], "tensor", i) for i in range(1, shards)]
    attention, keys, values = finish(
        partials, key_gain.reshape(1, -1), packets, rank, step_count, row_count, query_rows.shape[1]
    )
    return tuple(a.reshape(step_count, row_count, -1) for a in (attention, keys, values))


def solution(mesh):
    placed = (
        P(None, ("job", "rollout"), "tensor"),
        P("tensor", None),
        P(("job", "rollout", "tensor"), None),
        P(None, ("job", "rollout")),
        P(),
        P(None, ("job", "rollout"), "tensor"),
        P(("job", "rollout"), None, "tensor"),
        P(("job", "rollout"), None, "tensor"),
        P(("job", "rollout")),
        P("job"),
    )
    return jax.shard_map(
        per_device,
        mesh=mesh,
        in_specs=placed,
        out_specs=(
            P(None, ("job", "rollout"), "tensor"),
            P(None, ("job", "rollout"), "tensor"),
            P(None, ("job", "rollout"), "tensor"),
        ),
        check_vma=False,
    )
```

time: 149 us -> 41.4 us (0.28)
  waiting for transfers between devices: 65.5 us -> 4.05 us
  blocking collectives: 30.2 us -> 0 us
  matrix products: 23.1 us -> 0 us
  between operations: 14 us -> 0.7 us
  Pallas kernels: 0 us -> 13.2 us
  starting transfers between devices: 0.16 us -> 7.49 us
  other arithmetic: 2.88 us -> 0 us
  local copies, waits for them, and re-layouts: 12.9 us -> 15.5 us
    reduce_scatter x4 -> x0, waiting for transfers between devices: 65.4 us -> none  [per_device(): lax.psum_scatter(jnp.dot(normed_tokens[decode_step_index], merged_weight,...]
    all_gather x2 -> x0, blocking collectives: 30.2 us -> none  [the longest x1 15.8 us: per_device(): up_stored = lax.all_gather(adapter_up, 'rollout', axis=1, tiled=True)]
    dot_general x9 -> x0, matrix products: 23.1 us -> none  [the longest x4 13.3 us: per_device(): jnp.dot(normed_tokens[decode_step_index], merged_weight, preferred_elemen...]
    unnamed x14 -> x39, local copies, waits for them, and re-layouts: 2.34 us -> 15.5 us
    pallas_call x0 -> x4, Pallas kernels: none -> 13.2 us  [the longest x1 6.6 us: front(): pl.pallas_call(functools.partial(front_kernel, step_count, row_count, hea...]
    ppermute x0 -> x6, starting transfers between devices: none -> 7.49 us  [swap(): return lax.ppermute(block, axis, [(s, s ^ offset) for s in range(count)])]
    reshape x3 -> x0, local copies, waits for them, and re-layouts: 4.18 us -> none  [the longest x1 2.09 us: per_device(): values_local = stored_values.reshape(row_count, -1, head_count, head_size)]
    ppermute x0 -> x6, waiting for transfers between devices: none -> 4.05 us  [swap(): return lax.ppermute(block, axis, [(s, s ^ offset) for s in range(count)])]
  transfers between devices with their start and end apart: 4 -> 6, of which waited for: 4 -> 2; matrix products, arithmetic and copies ran while one was open for 14% -> 0% of each run, Pallas kernels for 0% -> 16%
where the time goes in v3:
time: 41.4 us; the launch traced here: 40.9 us
  local copies, waits for them, and re-layouts  15.5 us (37%)
  Pallas kernels  13.2 us (32%)
  starting transfers between devices  7.49 us (18%)
  waiting for transfers between devices  4.05 us (10%)
  between operations  0.7 us (2%)
    unnamed x39, local copies, waits for them, and re-layouts  15.5 us
    ppermute x6, starting transfers between devices, swap(): return lax.ppermute(block, axis, [(s, s ^ offset) for s in range(count)])  7.49 us
    pallas_call x1, Pallas kernels, front(): pl.pallas_call(functools.partial(front_kernel, step_count, row_count, hea...  6.6 us
    ppermute x6, waiting for transfers between devices, swap(): return lax.ppermute(block, axis, [(s, s ^ offset) for s in range(count)])  4.05 us
    pallas_call x1, Pallas kernels, finish(): pl.pallas_call(functools.partial(finish_kernel, step_count, row_count, he...  2.87 us
    pallas_call x1, Pallas kernels, route(): pl.pallas_call(functools.partial(route_kernel, replicas, shards), out_sha...  2.12 us
    pallas_call x1, Pallas kernels, pack(): pl.pallas_call(pack_kernel, out_shape=jax.ShapeDtypeStruct((rows, lanes),...  1.58 us
  transfers between devices with their start and end apart: 6, of which 2 were waited for; matrix products, arithmetic and copies ran while one was open for 0% of the time, Pallas kernels for 16%

profile of v3, /device:TPU:0, one launch (start us, length us, event | category | flops | bytes accessed | tf_op | source)
XLA Modules:
  0.0 40.9 jit_solution(6408753423353812682)
XLA Ops:
  0.6 1.5 %copy.13.down_ref = bf16[320,64]{1,0:T(8,128)(2,1)} copy(bf16[320,64]{0,1:T(8,128)(2,1)} %param.12) | data formatting | bytes 81920 | tf_op args[2]
  2.2 1.6 %pack.1.refs_3_ = bf16[224,128]{1,0:T(8,128)(2,1)} custom-call(bf16[320,64]{1,0:T(8,128)(2,1)} %copy.13.down_ref, bf16[64,512]{1,0:T(8,128)(2,1)} %up_ref.1), custom_call_target="tpu_custom_call" | custom-call | bytes 200000 | tf_op jit(solution)/shard_map/pack/pallas_call | solution.py:52
  3.7 3.0 %collective-permute-start = (bf16[224,128]{1,0:T(8,128)(2,1)}, bf16[224,128]{1,0:T(8,128)(2,1)S(1)}, u32[]{:S(2)}, u32[]{:S(2)}) collective-permute-start(bf16[224,128]{1,0:T(8,128)(2,1)} %pack.1.refs_3_), channel_id=1, source_target_pairs={{0,4},{4,0},{8,12},{12,8},{1,5},{5,1},{9,13},{13,9},{2,6},{6,2},{1... | collective-permute-start | bytes 172040 | tf_op jit(solution)/shard_map/ppermute | solution.py:26
  6.8 2.6 %collective-permute-start.1 = (bf16[224,128]{1,0:T(8,128)(2,1)}, bf16[224,128]{1,0:T(8,128)(2,1)S(1)}, u32[]{:S(2)}, u32[]{:S(2)}) collective-permute-start(bf16[224,128]{1,0:T(8,128)(2,1)} %pack.1.refs_3_), channel_id=1, source_target_pairs={{0,8},{4,12},{8,0},{12,4},{1,9},{5,13},{9,1},{13,5},{2,10},{6,14},... | collective-permute-start | bytes 172040 | tf_op jit(solution)/shard_map/ppermute | solution.py:26
  9.4 0.0 collective-permute-start.2
  9.4 0.0 copy-start
  9.4 2.5 %copy-done = bf16[1280,2048]{1,0:T(8,128)(2,1)S(1)} copy-done((bf16[1280,2048]{1,0:T(8,128)(2,1)S(1)}, bf16[1280,2048]{1,0:T(8,128)(2,1)}, u32[]{:S(2)}) %copy-start) | copy-done | bytes 5242904
  11.9 0.0 copy-start.1
  11.9 1.6 %copy-done.1 = bf16[8,512,256]{2,1,0:T(8,128)(2,1)S(1)} copy-done((bf16[8,512,256]{2,1,0:T(8,128)(2,1)S(1)}, bf16[8,512,256]{2,1,0:T(8,128)(2,1)}, u32[]{:S(2)}) %copy-start.1) | copy-done | bytes 2097176
  13.4 0.0 copy-start.2
  13.4 1.6 %copy-done.2 = bf16[8,512,256]{2,1,0:T(8,128)(2,1)S(1)} copy-done((bf16[8,512,256]{2,1,0:T(8,128)(2,1)S(1)}, bf16[8,512,256]{2,1,0:T(8,128)(2,1)}, u32[]{:S(2)}) %copy-start.2) | copy-done | bytes 2097176
  15.0 0.0 copy-start.4
  15.0 0.9 %copy-done.4 = bf16[4,8,1280]{2,1,0:T(8,128)(2,1)S(1)} copy-done((bf16[4,8,1280]{2,1,0:T(8,128)(2,1)S(1)}, bf16[4,8,1280]{2,1,0:T(8,128)(2,1)}, u32[]{:S(2)}) %copy-start.4) | copy-done | bytes 81944
  15.9 0.0 copy-start.8
  15.9 0.9 %copy-done.8 = bf16[4,8,2048]{2,1,0:T(8,128)(2,1)S(1)} copy-done((bf16[4,8,2048]{2,1,0:T(8,128)(2,1)S(1)}, bf16[4,8,2048]{2,1,0:T(8,128)(2,1)}, u32[]{:S(2)}) %copy-start.8) | copy-done | bytes 131096
  16.8 0.0 copy-start.12
  16.8 0.7 %copy-done.12 = s32[8]{0:T(128)S(1)} copy-done((s32[8]{0:T(128)S(1)}, s32[8]{0:T(128)}, u32[]{:S(2)}) %copy-start.12) | copy-done | bytes 56
  17.5 6.6 %front.1 = (f32[4,32,512]{2,1,0:T(8,128)S(1)}, bf16[512,128]{1,0:T(8,128)(2,1)S(1)}, f32[512,128]{1,0:T(8,128)S(1)}, f32[512,128]{1,0:T(8,128)S(1)}, f32[512,128...) custom-call(s32[8]{0:T(128)S(1)} %copy-done.12, bf16[32,1280]{1,0:T(8,128)(2,1)S(1)} %bitcast.7, ...), custom_call_target="tpu_custom_call" | custom-call | flops 301989888 | bytes 9437184 | tf_op jit(solution)/shard_map/front/pallas_call | solution.py:188
  24.1 0.0 copy-start.3
  24.1 0.7 %copy-done.3 = f32[4,32,512]{2,1,0:T(8,128)} copy-done((f32[4,32,512]{2,1,0:T(8,128)}, f32[4,32,512]{2,1,0:T(8,128)S(1)}, u32[]{:S(2)}) %copy-start.3) | copy-done | bytes 262168
  24.8 0.0 copy-start.5
  24.8 0.7 %copy-done.5 = f32[512,128]{1,0:T(8,128)} copy-done((f32[512,128]{1,0:T(8,128)}, f32[512,128]{1,0:T(8,128)S(1)}, u32[]{:S(2)}) %copy-start.5) | copy-done | bytes 262168
  25.5 0.0 copy-start.6
  25.5 0.7 %copy-done.6 = f32[512,128]{1,0:T(8,128)} copy-done((f32[512,128]{1,0:T(8,128)}, f32[512,128]{1,0:T(8,128)S(1)}, u32[]{:S(2)}) %copy-start.6) | copy-done | bytes 262168
  26.2 0.0 copy-start.7
  26.2 0.7 %copy-done.7 = f32[512,128]{1,0:T(8,128)} copy-done((f32[512,128]{1,0:T(8,128)}, f32[512,128]{1,0:T(8,128)S(1)}, u32[]{:S(2)}) %copy-start.7) | copy-done | bytes 262168
  26.9 0.0 copy-start.9
  26.9 0.6 %copy-done.9 = bf16[512,128]{1,0:T(8,128)(2,1)} copy-done((bf16[512,128]{1,0:T(8,128)(2,1)}, bf16[512,128]{1,0:T(8,128)(2,1)S(1)}, u32[]{:S(2)}) %copy-start.9) | copy-done | bytes 131096
  27.5 0.0 copy-start.10
  27.5 0.6 %copy-done.10 = f32[32,128]{1,0:T(8,128)} copy-done((f32[32,128]{1,0:T(8,128)}, f32[32,128]{1,0:T(8,128)S(1)}, u32[]{:S(2)}) %copy-start.10) | copy-done | bytes 16408
  28.1 0.0 copy-start.11
  28.1 0.6 %copy-done.11 = f32[32,128]{1,0:T(8,128)} copy-done((f32[32,128]{1,0:T(8,128)}, f32[32,128]{1,0:T(8,128)S(1)}, u32[]{:S(2)}) %copy-start.11) | copy-done | bytes 16408
  28.7 0.0 collective-permute-done.refs_4_
  28.7 0.0 copy-start.14
  28.7 0.0 collective-permute-done.1.refs_5_
  28.8 0.0 copy-start.16
  28.8 0.0 collective-permute-done.2.refs_6_
  28.8 0.0 copy-start.18
  28.8 0.6 %copy-done.14 = bf16[224,128]{1,0:T(8,128)(2,1)} copy-done((bf16[224,128]{1,0:T(8,128)(2,1)}, bf16[224,128]{1,0:T(8,128)(2,1)S(1)}, u32[]{:S(2)}) %copy-start.14) | copy-done | bytes 57368
  29.4 0.0 copy-done.16
  29.4 0.0 copy-done.18
  29.4 2.1 %route.1 = (bf16[96,128]{1,0:T(8,128)(2,1)}, bf16[224,128]{1,0:T(8,128)(2,1)}, bf16[224,128]{1,0:T(8,128)(2,1)}, bf16[224,128]{1,0:T(8,128)(2,1)}) custom-call(s32[4]{0:T(128)} %refs_0_.1, bf16[32,1280]{1,0:T(8,128)(2,1)} %bitcast.6, f32[4,32,512]{2,1,0:T(8,128)} %copy-done.3, bf16[224,128]{1,0:T(8,128)(2,1)} %pack.1.refs_3_, bf16[224,128]{1,0:T(8,128)(2,1)} %copy-done.14, ...), custom_call_target="tpu_custom_call" | custom-call | bytes 800000 | tf_op jit(solution)/shard_map/route/pallas_call | solution.py:262
  31.5 0.0 collective-permute-start.3
  31.5 1.8 %collective-permute-start.4 = (bf16[224,128]{1,0:T(8,128)(2,1)}, bf16[224,128]{1,0:T(8,128)(2,1)S(1)}, u32[]{:S(2)}, u32[]{:S(2)}) collective-permute-start(bf16[224,128]{1,0:T(8,128)(2,1)} %get-tuple-element.26), channel_id=1, source_target_pairs={{0,2},{1,3},{2,0},{3,1},{4,6},{5,7},{6,4},{7,5},{8,10},{9,11},{10,... | collective-permute-start | bytes 172040 | tf_op jit(solution)/shard_map/ppermute | solution.py:26
  33.3 0.1 collective-permute-start.5
  33.4 0.0 collective-permute-done.3.refs_9_
  33.4 0.0 copy-start.13
  33.4 2.7 %collective-permute-done.4.refs_10_ = bf16[224,128]{1,0:T(8,128)(2,1)S(1)} collective-permute-done((bf16[224,128]{1,0:T(8,128)(2,1)}, bf16[224,128]{1,0:T(8,128)(2,1)S(1)}, u32[]{:S(2)}, u32[]{:S(2)}) %collective-permute-start.4) | collective-permute-done | bytes 57376 | tf_op jit(solution)/shard_map/ppermute | solution.py:26
  36.1 0.0 copy-start.15
  36.1 1.4 %collective-permute-done.5.refs_11_ = bf16[224,128]{1,0:T(8,128)(2,1)S(1)} collective-permute-done((bf16[224,128]{1,0:T(8,128)(2,1)}, bf16[224,128]{1,0:T(8,128)(2,1)S(1)}, u32[]{:S(2)}, u32[]{:S(2)}) %collective-permute-start.5) | collective-permute-done | bytes 57376 | tf_op jit(solution)/shard_map/ppermute | solution.py:26
  37.4 0.0 copy-start.17
  37.4 0.0 copy-done.13
  37.5 0.0 copy-done.15
  37.5 0.6 %copy-done.17 = bf16[224,128]{1,0:T(8,128)(2,1)} copy-done((bf16[224,128]{1,0:T(8,128)(2,1)}, bf16[224,128]{1,0:T(8,128)(2,1)S(1)}, u32[]{:S(2)}) %copy-start.17) | copy-done | bytes 57368
  38.1 2.9 %finish.1 = (bf16[32,2048]{1,0:T(8,128)(2,1)}, bf16[32,256]{1,0:T(8,128)(2,1)}, bf16[32,256]{1,0:T(8,128)(2,1)}) custom-call(f32[4,32,512]{2,1,0:T(8,128)} %copy-done.3, f32[1,128]{1,0:T(1,128)} %bitcast.9, bf16[512,128]{1,0:T(8,128)(2,1)} %copy-done.9, f32[512,128]{1,0:T(8,128)} %copy-done.5, f32[512,128]{1,0:T(8,128)} %copy-done.6, f32[512,128]{1,0:T(8,128)} %copy-done.7, ...), custom_call_target="tpu_custom_call" | custom-call | bytes 1000000 | tf_op jit(solution)/shard_map/finish/pallas_call | solution.py:390
Async XLA Ops:
  3.7 25.0 %collective-permute-start = (bf16[224,128]{1,0:T(8,128)(2,1)}, bf16[224,128]{1,0:T(8,128)(2,1)S(1)}, u32[]{:S(2)}, u32[]{:S(2)}) collective-permute-start(bf16[224,128]{1,0:T(8,128)(2,1)} %pack.1.refs_3_), channel_id=1, source_target_pairs={{0,4},{4,0},{8,12},{12,8},{1,5},{5,1},{9,13},{13,9},{2,6},{6,2},{1... | collective-permute-start | bytes 172040 | tf_op jit(solution)/shard_map/ppermute | solution.py:26
  6.8 22.0 %collective-permute-start.1 = (bf16[224,128]{1,0:T(8,128)(2,1)}, bf16[224,128]{1,0:T(8,128)(2,1)S(1)}, u32[]{:S(2)}, u32[]{:S(2)}) collective-permute-start(bf16[224,128]{1,0:T(8,128)(2,1)} %pack.1.refs_3_), channel_id=1, source_target_pairs={{0,8},{4,12},{8,0},{12,4},{1,9},{5,13},{9,1},{13,5},{2,10},{6,14},... | collective-permute-start | bytes 172040 | tf_op jit(solution)/shard_map/ppermute | solution.py:26
  9.4 19.4 %collective-permute-start.2 = (bf16[224,128]{1,0:T(8,128)(2,1)}, bf16[224,128]{1,0:T(8,128)(2,1)S(1)}, u32[]{:S(2)}, u32[]{:S(2)}) collective-permute-start(bf16[224,128]{1,0:T(8,128)(2,1)} %pack.1.refs_3_), channel_id=1, source_target_pairs={{0,12},{4,8},{8,4},{12,0},{1,13},{5,9},{9,5},{13,1},{2,14},{6,10},... | collective-permute-start | bytes 172040 | tf_op jit(solution)/shard_map/ppermute | solution.py:26
  9.4 2.5 %copy-start = (bf16[1280,2048]{1,0:T(8,128)(2,1)S(1)}, bf16[1280,2048]{1,0:T(8,128)(2,1)}, u32[]{:S(2)}) copy-start(bf16[1280,2048]{1,0:T(8,128)(2,1)} %weight_ref.1) | copy-start | bytes 15728644
  11.9 1.6 %copy-start.1 = (bf16[8,512,256]{2,1,0:T(8,128)(2,1)S(1)}, bf16[8,512,256]{2,1,0:T(8,128)(2,1)}, u32[]{:S(2)}) copy-start(bf16[8,512,256]{2,1,0:T(8,128)(2,1)} %keys_ref.1) | copy-start | bytes 6291460
  13.4 1.6 %copy-start.2 = (bf16[8,512,256]{2,1,0:T(8,128)(2,1)S(1)}, bf16[8,512,256]{2,1,0:T(8,128)(2,1)}, u32[]{:S(2)}) copy-start(bf16[8,512,256]{2,1,0:T(8,128)(2,1)} %values_ref.1) | copy-start | bytes 6291460
  15.0 0.9 %copy-start.4 = (bf16[4,8,1280]{2,1,0:T(8,128)(2,1)S(1)}, bf16[4,8,1280]{2,1,0:T(8,128)(2,1)}, u32[]{:S(2)}) copy-start(bf16[4,8,1280]{2,1,0:T(8,128)(2,1)} %param.10) | copy-start | bytes 245764
  15.9 0.9 %copy-start.8 = (bf16[4,8,2048]{2,1,0:T(8,128)(2,1)S(1)}, bf16[4,8,2048]{2,1,0:T(8,128)(2,1)}, u32[]{:S(2)}) copy-start(bf16[4,8,2048]{2,1,0:T(8,128)(2,1)} %param.15) | copy-start | bytes 393220
  16.8 0.7 %copy-start.12 = (s32[8]{0:T(128)S(1)}, s32[8]{0:T(128)}, u32[]{:S(2)}) copy-start(s32[8]{0:T(128)} %lengths_ref.1) | copy-start | bytes 100
  24.1 0.7 %copy-start.3 = (f32[4,32,512]{2,1,0:T(8,128)}, f32[4,32,512]{2,1,0:T(8,128)S(1)}, u32[]{:S(2)}) copy-start(f32[4,32,512]{2,1,0:T(8,128)S(1)} %get-tuple-element.17.refs_2_.refs_0_) | copy-start | bytes 786436
  24.8 0.7 %copy-start.5 = (f32[512,128]{1,0:T(8,128)}, f32[512,128]{1,0:T(8,128)S(1)}, u32[]{:S(2)}) copy-start(f32[512,128]{1,0:T(8,128)S(1)} %get-tuple-element.19.refs_3_) | copy-start | bytes 786436
  25.5 0.7 %copy-start.6 = (f32[512,128]{1,0:T(8,128)}, f32[512,128]{1,0:T(8,128)S(1)}, u32[]{:S(2)}) copy-start(f32[512,128]{1,0:T(8,128)S(1)} %get-tuple-element.20.refs_4_) | copy-start | bytes 786436
  26.2 0.7 %copy-start.7 = (f32[512,128]{1,0:T(8,128)}, f32[512,128]{1,0:T(8,128)S(1)}, u32[]{:S(2)}) copy-start(f32[512,128]{1,0:T(8,128)S(1)} %get-tuple-element.21.refs_5_) | copy-start | bytes 786436
  26.9 0.6 %copy-start.9 = (bf16[512,128]{1,0:T(8,128)(2,1)}, bf16[512,128]{1,0:T(8,128)(2,1)S(1)}, u32[]{:S(2)}) copy-start(bf16[512,128]{1,0:T(8,128)(2,1)S(1)} %get-tuple-element.18.refs_2_) | copy-start | bytes 393220
  27.5 0.6 %copy-start.10 = (f32[32,128]{1,0:T(8,128)}, f32[32,128]{1,0:T(8,128)S(1)}, u32[]{:S(2)}) copy-start(f32[32,128]{1,0:T(8,128)S(1)} %get-tuple-element.22.refs_6_) | copy-start | bytes 49156
  28.1 0.6 %copy-start.11 = (f32[32,128]{1,0:T(8,128)}, f32[32,128]{1,0:T(8,128)S(1)}, u32[]{:S(2)}) copy-start(f32[32,128]{1,0:T(8,128)S(1)} %get-tuple-element.23.refs_7_) | copy-start | bytes 49156
  28.7 0.6 %copy-start.14 = (bf16[224,128]{1,0:T(8,128)(2,1)}, bf16[224,128]{1,0:T(8,128)(2,1)S(1)}, u32[]{:S(2)}) copy-start(bf16[224,128]{1,0:T(8,128)(2,1)S(1)} %collective-permute-done.refs_4_) | copy-start | bytes 172036
  28.8 0.6 %copy-start.16 = (bf16[224,128]{1,0:T(8,128)(2,1)}, bf16[224,128]{1,0:T(8,128)(2,1)S(1)}, u32[]{:S(2)}) copy-start(bf16[224,128]{1,0:T(8,128)(2,1)S(1)} %collective-permute-done.1.refs_5_) | copy-start | bytes 172036
  28.8 0.6 %copy-start.18 = (bf16[224,128]{1,0:T(8,128)(2,1)}, bf16[224,128]{1,0:T(8,128)(2,1)S(1)}, u32[]{:S(2)}) copy-start(bf16[224,128]{1,0:T(8,128)(2,1)S(1)} %collective-permute-done.2.refs_6_) | copy-start | bytes 172036
  31.5 1.9 %collective-permute-start.3 = (bf16[224,128]{1,0:T(8,128)(2,1)}, bf16[224,128]{1,0:T(8,128)(2,1)S(1)}, u32[]{:S(2)}, u32[]{:S(2)}) collective-permute-start(bf16[224,128]{1,0:T(8,128)(2,1)} %get-tuple-element.25), channel_id=1, source_target_pairs={{0,1},{1,0},{2,3},{3,2},{4,5},{5,4},{6,7},{7,6},{8,9},{9,8},{10,11... | collective-permute-start | bytes 172040 | tf_op jit(solution)/shard_map/ppermute | solution.py:26
  31.5 4.5 %collective-permute-start.4 = (bf16[224,128]{1,0:T(8,128)(2,1)}, bf16[224,128]{1,0:T(8,128)(2,1)S(1)}, u32[]{:S(2)}, u32[]{:S(2)}) collective-permute-start(bf16[224,128]{1,0:T(8,128)(2,1)} %get-tuple-element.26), channel_id=1, source_target_pairs={{0,2},{1,3},{2,0},{3,1},{4,6},{5,7},{6,4},{7,5},{8,10},{9,11},{10,... | collective-permute-start | bytes 172040 | tf_op jit(solution)/shard_map/ppermute | solution.py:26
  33.3 4.2 %collective-permute-start.5 = (bf16[224,128]{1,0:T(8,128)(2,1)}, bf16[224,128]{1,0:T(8,128)(2,1)S(1)}, u32[]{:S(2)}, u32[]{:S(2)}) collective-permute-start(bf16[224,128]{1,0:T(8,128)(2,1)} %get-tuple-element.27), channel_id=1, source_target_pairs={{0,3},{1,2},{2,1},{3,0},{4,7},{5,6},{6,5},{7,4},{8,11},{9,10},{10,... | collective-permute-start | bytes 172040 | tf_op jit(solution)/shard_map/ppermute | solution.py:26
  33.4 4.0 %copy-start.13 = (bf16[224,128]{1,0:T(8,128)(2,1)}, bf16[224,128]{1,0:T(8,128)(2,1)S(1)}, u32[]{:S(2)}) copy-start(bf16[224,128]{1,0:T(8,128)(2,1)S(1)} %collective-permute-done.3.refs_9_) | copy-start | bytes 172036
  36.1 1.4 %copy-start.15 = (bf16[224,128]{1,0:T(8,128)(2,1)}, bf16[224,128]{1,0:T(8,128)(2,1)S(1)}, u32[]{:S(2)}) copy-start(bf16[224,128]{1,0:T(8,128)(2,1)S(1)} %collective-permute-done.4.refs_10_) | copy-start | bytes 172036
  37.4 0.6 %copy-start.17 = (bf16[224,128]{1,0:T(8,128)(2,1)}, bf16[224,128]{1,0:T(8,128)(2,1)S(1)}, u32[]{:S(2)}) copy-start(bf16[224,128]{1,0:T(8,128)(2,1)S(1)} %collective-permute-done.5.refs_11_) | copy-start | bytes 172036

commit v4 on v3

v4 whole, which is shorter than its diff:
```python
import functools
import math

import jax
import jax.numpy as jnp
from jax import lax
from jax.experimental import pallas as pl
from jax.experimental.pallas import tpu as pltpu
from jax.sharding import PartitionSpec as P

norm_eps = 1e-06
rope_base = 1000000.0
adapter_scale = 2.0
masked_score = -1e30
lanes = 128
f32 = jnp.float32
bf16 = jnp.bfloat16

whole_in_vmem = pl.BlockSpec(memory_space=pltpu.VMEM)
whole_in_smem = pl.BlockSpec(memory_space=pltpu.SMEM)
stays_in_hbm = pl.BlockSpec(memory_space=pltpu.HBM)


def swap(block, axis, offset):
    count = lax.axis_size(axis)
    return lax.ppermute(block, axis, [(s, s ^ offset) for s in range(count)])


def in_hbm(*arrays):
    return tuple(pltpu.with_memory_space_constraint(a, pltpu.HBM) for a in arrays)


def side_by_side(rows_of_blocks):
    r, c = rows_of_blocks.shape
    return rows_of_blocks.reshape(r, c // lanes, lanes).transpose(1, 0, 2).reshape(-1, lanes)


def split_halves(total):
    high = total.astype(bf16)
    return high, (total - high.astype(f32)).astype(bf16)


def pack_kernel(down_hbm, up_hbm, out_ref, down_ref, up_ref, sems):
    rank, down_rows = down_ref.shape
    rank_part = up_ref.shape[0]
    start = pl.multiple_of(lax.axis_index("tensor") * rank_part, rank_part)
    copies = [
        pltpu.make_async_copy(down_hbm, down_ref, sems.at[0]),
        pltpu.make_async_copy(up_hbm.at[pl.ds(start, rank_part), :], up_ref, sems.at[1]),
    ]
    for copy in copies:
        copy.start()
    for copy in copies:
        copy.wait()
    first = 0
    for c in range(down_rows // lanes):
        out_ref[first : first + rank, :] = down_ref[:, c * lanes : (c + 1) * lanes]
        first += rank
    rest = down_rows % lanes
    if rest:
        half = rank // 2
        tail = down_ref[:, down_rows - rest :]
        out_ref[first : first + half, :] = jnp.concatenate([tail[:half], tail[half:]], axis=1)
        first += half
    for c in range(up_ref.shape[1] // lanes):
        out_ref[first : first + rank_part, :] = up_ref[:, c * lanes : (c + 1) * lanes]
        first += rank_part


def pack(down, up, rank_part):
    rows = (down.size + rank_part * up.shape[1]) // lanes
    return pl.pallas_call(
        pack_kernel,
        out_shape=jax.ShapeDtypeStruct((rows, lanes), bf16),
        in_specs=[stays_in_hbm] * 2,
        out_specs=whole_in_vmem,
        scratch_shapes=[
            pltpu.VMEM(down.shape, bf16),
            pltpu.VMEM((rank_part, up.shape[1]), bf16),
            pltpu.SemaphoreType.DMA((2,)),
        ],
        compiler_params=pltpu.CompilerParams(vmem_limit_bytes=2 * 2**20),
        name="pack",
        cost_estimate=pl.CostEstimate(flops=0, bytes_accessed=200000, transcendentals=0),
    )(*in_hbm(down, up))


def project_kernel(
    step_count,
    row_count,
    head_count,
    shards,
    lengths_hbm,
    tokens_hbm,
    queries_hbm,
    weight_hbm,
    own_ref,
    base_ref,
    grouped_ref,
    cosine_ref,
    sine_ref,
    lengths_ref,
    tokens_ref,
    queries_ref,
    weight_ref,
    regroup,
    sems,
    weight_sems,
):
    shard = lax.axis_index("tensor")
    rows, own = own_ref.shape
    group = queries_ref.shape[1] // (head_count * lanes)
    seen = step_count * group
    lengths_copy = pltpu.make_async_copy(lengths_hbm, lengths_ref, sems.at[0])
    queries_copy = pltpu.make_async_copy(queries_hbm, queries_ref, sems.at[1])
    tokens_copy = pltpu.make_async_copy(tokens_hbm, tokens_ref, sems.at[2])
    weight_copies = [
        pltpu.make_async_copy(
            weight_hbm.at[:, pl.ds(pl.multiple_of((shard ^ i) * own, lanes), own)],
            weight_ref.at[i],
            weight_sems.at[i],
        )
        for i in range(shards)
    ]
    for copy in [lengths_copy, queries_copy, tokens_copy] + weight_copies:
        copy.start()

    lengths_copy.wait()
    row = lax.broadcasted_iota(jnp.int32, (rows, lanes), 0)
    lane = lax.broadcasted_iota(jnp.int32, (rows, lanes), 1)
    position = row // row_count
    for b in range(row_count):
        position = position + jnp.where(row % row_count == b, lengths_ref[b], 0)
    middle = lanes // 2
    spacing = (lane % middle).astype(f32) * (-2.0 / lanes * math.log(rope_base))
    angles = position.astype(f32) * jnp.exp(spacing)
    cosine_ref[...] = jnp.cos(angles)
    sine = jnp.sin(angles)
    sine_ref[...] = jnp.where(lane < middle, -sine, sine)

    queries_copy.wait()
    for pair in range(step_count // 2):
        for q in range(head_count * group):
            h, g = q // group, q % group
            both = queries_ref[
                pair * 2 * row_count : (pair + 1) * 2 * row_count, q * lanes : (q + 1) * lanes
            ].astype(f32)
            for side in range(2):
                first = h * row_count * seen + (pair * 2 + side) * group + g
                regroup[pl.ds(first, row_count, stride=seen), :] = both[
                    side * row_count : (side + 1) * row_count, :
                ]
    grouped_ref[...] = regroup[...].astype(bf16)

    tokens_copy.wait()
    for i in range(shards):
        weight_copies[i].wait()
        block = jnp.dot(tokens_ref[...], weight_ref[i], preferred_element_type=f32)
        if i == 0:
            own_ref[...] = block
            continue
        for c in range(own // lanes):
            base_ref[i - 1, c * rows : (c + 1) * rows, :] = block[
                :, c * lanes : (c + 1) * lanes
            ].astype(bf16)


def project(lengths, tokens, queries, weight, step_count, head_count, shards):
    rows, depth = tokens.shape
    columns = weight.shape[1]
    own = columns // shards
    seen_rows = rows * queries.shape[1] // lanes
    table = jax.ShapeDtypeStruct((rows, lanes), f32)
    return pl.pallas_call(
        functools.partial(project_kernel, step_count, rows // step_count, head_count, shards),
        out_shape=(
            jax.ShapeDtypeStruct((rows, own), f32),
            jax.ShapeDtypeStruct((shards - 1, rows * own // lanes, lanes), bf16),
            jax.ShapeDtypeStruct((seen_rows, lanes), bf16),
            table,
            table,
        ),
        in_specs=[stays_in_hbm] * 4,
        out_specs=(whole_in_vmem,) * 5,
        scratch_shapes=[
            pltpu.SMEM(lengths.shape, jnp.int32),
            pltpu.VMEM(tokens.shape, bf16),
            pltpu.VMEM(queries.shape, bf16),
            pltpu.VMEM((shards, depth, own), bf16),
            pltpu.VMEM((seen_rows, lanes), f32),
            pltpu.SemaphoreType.DMA((3,)),
            pltpu.SemaphoreType.DMA((shards,)),
        ],
        compiler_params=pltpu.CompilerParams(vmem_limit_bytes=12 * 2**20),
        name="project",
        cost_estimate=pl.CostEstimate(
            flops=2 * rows * weight.size, bytes_accessed=2 * weight.size, transcendentals=0
        ),
    )(*in_hbm(lengths, tokens, queries, weight))


def attend_kernel(
    head_count,
    lengths_hbm,
    grouped_ref,
    keys_hbm,
    values_hbm,
    total_ref,
    peak_ref,
    sum_ref,
    lengths_ref,
    keys_ref,
    values_ref,
    scores,
    raised,
    length_sem,
    key_sems,
    value_sems,
):
    row_count, slots, _ = keys_ref.shape
    seen = grouped_ref.shape[0] // (head_count * row_count)
    scale = lanes**-0.5
    lengths_copy = pltpu.make_async_copy(lengths_hbm, lengths_ref, length_sem)
    key_copies = [
        pltpu.make_async_copy(keys_hbm.at[b], keys_ref.at[b], key_sems.at[b])
        for b in range(row_count)
    ]
    value_copies = [
        pltpu.make_async_copy(values_hbm.at[b], values_ref.at[b], value_sems.at[b])
        for b in range(row_count)
    ]
    for copy in [lengths_copy] + key_copies + value_copies:
        copy.start()
    lengths_copy.wait()

    def place(h, b):
        at = (h * row_count + b) * seen
        return slice(at, at + seen)

    for b in range(row_count):
        key_copies[b].wait()
        for h in range(head_count):
            scores[place(h, b), :] = lax.dot_general(
                grouped_ref[place(h, b), :],
                keys_ref[b, :, h * lanes : (h + 1) * lanes],
                (((1,), (1,)), ((), ())),
                preferred_element_type=f32,
            )
    for copy in value_copies:
        copy.wait()
    slot = lax.broadcasted_iota(jnp.int32, (seen, slots), 1)
    for b in range(row_count):
        live = slot < lengths_ref[b]
        for h in range(head_count):
            score = jnp.where(live, scores[place(h, b), :] * scale, masked_score)
            peak = jnp.max(score, axis=1, keepdims=True)
            lifted = jnp.exp(score - peak)
            raised[place(h, b), :] = lifted.astype(bf16)
            peak_ref[place(h, b), :] = jnp.broadcast_to(peak, (seen, lanes))
            sum_ref[place(h, b), :] = jnp.broadcast_to(
                jnp.sum(lifted, axis=1, keepdims=True), (seen, lanes)
            )
    for b in range(row_count):
        for h in range(head_count):
            total_ref[place(h, b), :] = jnp.dot(
                raised[place(h, b), :],
                values_ref[b, :, h * lanes : (h + 1) * lanes],
                preferred_element_type=f32,
            )


def attend(lengths, grouped, keys, values):
    row_count, slots, width = keys.shape
    seen_rows = grouped.shape[0]
    seen_table = jax.ShapeDtypeStruct((seen_rows, lanes), f32)
    lengths, keys, values = in_hbm(lengths, keys, values)
    return pl.pallas_call(
        functools.partial(attend_kernel, width // lanes),
        out_shape=(seen_table,) * 3,
        in_specs=[stays_in_hbm, whole_in_vmem, stays_in_hbm, stays_in_hbm],
        out_specs=(whole_in_vmem,) * 3,
        scratch_shapes=[
            pltpu.SMEM(lengths.shape, jnp.int32),
            pltpu.VMEM(keys.shape, bf16),
            pltpu.VMEM(values.shape, bf16),
            pltpu.VMEM((seen_rows, slots), f32),
            pltpu.VMEM((seen_rows, slots), bf16),
            pltpu.SemaphoreType.DMA,
            pltpu.SemaphoreType.DMA((row_count,)),
            pltpu.SemaphoreType.DMA((row_count,)),
        ],
        compiler_params=pltpu.CompilerParams(vmem_limit_bytes=12 * 2**20),
        name="attend",
        cost_estimate=pl.CostEstimate(
            flops=4 * seen_rows * slots * lanes,
            bytes_accessed=2 * (keys.size + values.size),
            transcendentals=seen_rows * slots,
        ),
    )(lengths, grouped, keys, values)


def route_kernel(replicas, shards, *refs):
    owners_ref, tokens_ref, base_ref = refs[:3]
    piece_refs = refs[3 : 3 + replicas]
    out_refs = refs[3 + replicas : 3 + replicas + shards]
    token_buf, left, right, up_buf = refs[3 + replicas + shards :]
    replica = lax.axis_index("rollout")
    shard = lax.axis_index("tensor")
    rows, depth = tokens_ref.shape
    rank = right.shape[0]
    down_rows = depth // replicas
    width = token_buf.shape[2]
    rest = down_rows % lanes
    for k in range(replicas):
        token_buf[k, :, :down_rows] = tokens_ref[:, k * down_rows : (k + 1) * down_rows]
        if rest:
            token_buf[k, :, down_rows:] = jnp.zeros((rows, width - down_rows), bf16)
    for i in range(replicas):
        source = replica ^ i
        place = jnp.int32(0)
        for k in range(1, replicas):
            place = place + jnp.where(owners_ref[k] == source, k, 0)
        left[:, i * width : (i + 1) * width] = token_buf[place]
        first = 0
        for c in range(down_rows // lanes):
            right[:, i * width + c * lanes : i * width + (c + 1) * lanes] = piece_refs[i][
                first : first + rank, :
            ]
            first += rank
        if rest:
            both = piece_refs[i][first : first + rank // 2, :]
            tail = jnp.concatenate([both[:, :rest], both[:, rest:]], axis=0)
            right[:, (i + 1) * width - lanes : (i + 1) * width] = jnp.concatenate(
                [tail, jnp.zeros((rank, lanes - rest), bf16)], axis=1
            )
            first += rank // 2
        up_buf[i] = piece_refs[i][first:, :]
    lowered = lax.dot_general(
        left[...], right[...], (((1,), (1,)), ((), ())), preferred_element_type=f32
    )
    both = jnp.concatenate(split_halves(lowered), axis=1)
    for i in range(shards):
        first = 0
        if i:
            first = base_ref.shape[1]
            out_refs[i][:first, :] = base_ref[i - 1]
        out_refs[i][first : first + rows, :] = both
        out_refs[i][first + rows :, :] = up_buf[owners_ref[shard ^ i] ^ replica]


def route(owners, tokens, base, pieces, rank, up_rows):
    rows, depth = tokens.shape
    shards = base.shape[0] + 1
    replicas = len(pieces)
    sent = base.shape[1]
    width = -(-depth // replicas // lanes) * lanes
    return pl.pallas_call(
        functools.partial(route_kernel, replicas, shards),
        out_shape=[
            jax.ShapeDtypeStruct(((sent if i else 0) + rows + up_rows, lanes), bf16)
            for i in range(shards)
        ],
        in_specs=[whole_in_smem] + [whole_in_vmem] * (2 + replicas),
        out_specs=[whole_in_vmem] * shards,
        scratch_shapes=[
            pltpu.VMEM((replicas, rows, width), bf16),
            pltpu.VMEM((rows, replicas * width), bf16),
            pltpu.VMEM((rank, replicas * width), bf16),
            pltpu.VMEM((replicas, up_rows, lanes), bf16),
        ],
        compiler_params=pltpu.CompilerParams(vmem_limit_bytes=4 * 2**20),
        name="route",
        cost_estimate=pl.CostEstimate(flops=0, bytes_accessed=800000, transcendentals=0),
    )(owners, tokens, base, *pieces)


def route_plain(owners, tokens, base, down, up, rank_part, own):
    shards = base.shape[0] + 1
    rank = down.shape[1]
    shard = lax.axis_index("tensor")
    first = shard * rank_part
    up_part = lax.dynamic_slice_in_dim(up, first, rank_part, axis=0)
    downs = lax.all_gather(down, "rollout", axis=0, tiled=False)
    ups = lax.all_gather(up_part, "rollout", axis=0, tiled=False)
    down_matrix = jnp.take(downs, owners, axis=0, mode="clip").reshape(-1, rank)
    up_matrix = jnp.take(ups, owners, axis=0, mode="clip").transpose(1, 0, 2)
    up_matrix = up_matrix.reshape(rank_part, -1)
    lowered = jnp.dot(tokens, down_matrix, preferred_element_type=f32)
    both = jnp.concatenate(split_halves(lowered), axis=1)
    packets = []
    for i in range(shards):
        up_block = lax.dynamic_slice_in_dim(up_matrix, (shard ^ i) * own, own, axis=1)
        parts = [both, side_by_side(up_block)]
        if i:
            parts = [base[i - 1]] + parts
        packets.append(jnp.concatenate(parts, axis=0))
    return packets


def finish_kernel(step_count, row_count, head_count, shards, *refs):
    own_ref, gain_ref, grouped_ref, total_ref, peak_ref, sum_ref, cosine_ref, sine_ref = refs[:8]
    packet_refs = refs[8 : 8 + shards]
    attention_ref, keys_ref, values_ref = refs[8 + shards : 11 + shards]
    up_buf, ordered = refs[11 + shards :]
    shard = lax.axis_index("tensor")
    rows = step_count * row_count
    own = own_ref.shape[1]
    blocks = own // lanes
    rank = up_buf.shape[0]
    rank_part = rank // shards
    group = grouped_ref.shape[0] // (head_count * rows)
    seen = step_count * group
    scale = lanes**-0.5

    lowered = jnp.zeros((rows, lanes), f32)
    for i in range(shards):
        first = rows * blocks if i else 0
        lowered = lowered + packet_refs[i][first : first + rows, :].astype(f32)
        ups = packet_refs[i][first + rows :, :].astype(f32)
        at = pl.multiple_of((shard ^ i) * rank_part, rank_part)
        for c in range(blocks):
            up_buf[pl.ds(at, rank_part), c * lanes : (c + 1) * lanes] = ups[
                c * rank_part : (c + 1) * rank_part, :
            ]
    lane = lax.broadcasted_iota(jnp.int32, (rows, lanes), 1)
    lowered = lowered + pltpu.roll(lowered, rank, 1)
    high, low = split_halves(lowered)
    left = jnp.where(lane < rank, high.astype(f32), low.astype(f32)).astype(bf16)
    up = up_buf[...].astype(bf16)
    raised_up = jnp.dot(left, jnp.concatenate([up, up], axis=0), preferred_element_type=f32)
    joined = []
    for c in range(blocks):
        block = own_ref[:, c * lanes : (c + 1) * lanes]
        for i in range(1, shards):
            block = block + packet_refs[i][c * rows : (c + 1) * rows, :].astype(f32)
        joined.append(block + adapter_scale * raised_up[:, c * lanes : (c + 1) * lanes])

    all_rows = row_count * seen
    seen_by = lax.broadcasted_iota(jnp.int32, (all_rows, rows), 0)
    made_by = lax.broadcasted_iota(jnp.int32, (all_rows, rows), 1)
    visible = (seen_by // seen == made_by % row_count) & (
        made_by // row_count <= seen_by % seen // group
    )
    for h in range(head_count):
        raw_key = joined[2 * h]
        mean_square = jnp.mean(raw_key * raw_key, axis=1, keepdims=True)
        normed = raw_key * lax.rsqrt(mean_square + norm_eps) * gain_ref[...]
        key = normed * cosine_ref[...] + pltpu.roll(normed, lanes // 2, 1) * sine_ref[...]
        key = key.astype(bf16)
        value = joined[2 * h + 1].astype(bf16)
        keys_ref[:, h * lanes : (h + 1) * lanes] = key
        values_ref[:, h * lanes : (h + 1) * lanes] = value
        mine = slice(h * all_rows, (h + 1) * all_rows)
        score = lax.dot_general(
            grouped_ref[mine, :], key, (((1,), (1,)), ((), ())), preferred_element_type=f32
        )
        score = jnp.where(visible, score * scale, masked_score)
        old_peak = peak_ref[mine, :]
        peak = jnp.maximum(old_peak, jnp.max(score, axis=1, keepdims=True))
        fade = jnp.exp(old_peak - peak)
        lifted = jnp.exp(score - peak[:, :rows])
        denominator = fade * sum_ref[mine, :] + jnp.sum(lifted, axis=1, keepdims=True)
        total = fade * total_ref[mine, :] + jnp.dot(
            lifted.astype(bf16), value, preferred_element_type=f32
        )
        ordered[mine, :] = total / denominator
    for pair in range(step_count // 2):
        for q in range(head_count * group):
            h, g = q // group, q % group
            both = [
                ordered[
                    pl.ds(
                        h * all_rows + (pair * 2 + side) * group + g, row_count, stride=seen
                    ),
                    :,
                ]
                for side in range(2)
            ]
            attention_ref[
                pair * 2 * row_count : (pair + 1) * 2 * row_count, q * lanes : (q + 1) * lanes
            ] = jnp.concatenate(both, axis=0).astype(bf16)


def finish(partials, gain, packets, rank, step_count, row_count, query_width):
    mine, grouped, total, peak, denominator, cosine, sine = partials
    rows, own = mine.shape
    shards = len(packets)
    head_count = own // (2 * lanes)
    return pl.pallas_call(
        functools.partial(finish_kernel, step_count, row_count, head_count, shards),
        out_shape=(
            jax.ShapeDtypeStruct((rows, query_width), bf16),
            jax.ShapeDtypeStruct((rows, head_count * lanes), bf16),
            jax.ShapeDtypeStruct((rows, head_count * lanes), bf16),
        ),
        in_specs=[whole_in_vmem] * (8 + shards),
        out_specs=(whole_in_vmem,) * 3,
        scratch_shapes=[
            pltpu.VMEM((rank, own), f32),
            pltpu.VMEM(total.shape, f32),
        ],
        compiler_params=pltpu.CompilerParams(vmem_limit_bytes=6 * 2**20),
        name="finish",
        cost_estimate=pl.CostEstimate(flops=0, bytes_accessed=1000000, transcendentals=0),
    )(mine, gain, grouped, total, peak, denominator, cosine, sine, *packets)


def per_device(
    normed_tokens,
    key_value_weight,
    adapter_down,
    adapter_up,
    key_gain,
    queries,
    cache_keys,
    stored_values,
    lengths,
    owners,
):
    replicas = lax.axis_size("rollout")
    shards = lax.axis_size("tensor")
    down_rows, rank = adapter_down.shape
    step_count, row_count, depth = normed_tokens.shape
    own = key_value_weight.shape[1] // shards
    rank_part = rank // shards
    rows = step_count * row_count
    tokens = normed_tokens.reshape(rows, depth)
    query_rows = queries.reshape(rows, -1)

    fits = (
        replicas <= 4
        and adapter_up.shape[1] == own
        and down_rows % lanes in (0, lanes // 2)
        and rank == lanes // 2
        and rank_part % 16 == 0
    )
    if fits:
        packed = pack(adapter_down.T, adapter_up, rank_part)
        arrived = {i: swap(packed, "rollout", i) for i in reversed(range(1, replicas))}
        pieces = [packed] + [arrived[i] for i in range(1, replicas)]
    head_count = cache_keys.shape[2] // lanes
    mine, base, grouped, cosine, sine = project(
        lengths, tokens, query_rows, key_value_weight, step_count, head_count, shards
    )
    if fits:
        packets = route(owners, tokens, base, pieces, rank, rank_part * own // lanes)
    else:
        packets = route_plain(owners, tokens, base, adapter_down, adapter_up, rank_part, own)
    arrived = {i: swap(packets[i], "tensor", i) for i in reversed(range(1, shards))}
    packets = [packets[0]] + [arrived[i] for i in range(1, shards)]
    total, peak, denominator = attend(lengths, grouped, cache_keys, stored_values)
    attention, keys, values = finish(
        (mine, grouped, total, peak, denominator, cosine, sine),
        key_gain.reshape(1, -1),
        packets,
        rank,
        step_count,
        row_count,
        query_rows.shape[1],
    )
    return tuple(a.reshape(step_count, row_count, -1) for a in (attention, keys, values))


def solution(mesh):
    placed = (
        P(None, ("job", "rollout"), "tensor"),
        P("tensor", None),
        P(("job", "rollout", "tensor"), None),
        P(None, ("job", "rollout")),
        P(),
        P(None, ("job", "rollout"), "tensor"),
        P(("job", "rollout"), None, "tensor"),
        P(("job", "rollout"), None, "tensor"),
        P(("job", "rollout")),
        P("job"),
    )
    return jax.shard_map(
        per_device,
        mesh=mesh,
        in_specs=placed,
        out_specs=(
            P(None, ("job", "rollout"), "tensor"),
            P(None, ("job", "rollout"), "tensor"),
            P(None, ("job", "rollout"), "tensor"),
        ),
        check_vma=False,
    )
```

time: 41.4 us -> 19.9 us (0.48)
  local copies, waits for them, and re-layouts: 15.5 us -> 0.01 us
  waiting for transfers between devices: 4.05 us -> 0.85 us
  Pallas kernels: 13.2 us -> 10.5 us
    unnamed x39 -> x6, local copies, waits for them, and re-layouts: 15.5 us -> 0.01 us
    ppermute x6, waiting for transfers between devices: 4.05 us -> 0.85 us  [swap(): return lax.ppermute(block, axis, [(s, s ^ offset) for s in range(count)])]
    pallas_call x1, Pallas kernels: 2.87 us -> 1.58 us  [finish(): pl.pallas_call(functools.partial(finish_kernel, step_count, row_count, he...]
    pallas_call x1, Pallas kernels: 2.12 us -> 0.88 us  [route(): pl.pallas_call(functools.partial(route_kernel, replicas, shards), out_sha...]
    pallas_call x1, Pallas kernels: 1.58 us -> 0.9 us  [pack(): pl.pallas_call(pack_kernel, out_shape=jax.ShapeDtypeStruct((rows, lanes),...]
    pallas_call x1 -> x2, Pallas kernels: 6.6 us -> 7.13 us  [the longest x1 3.77 us: project(): pl.pallas_call(functools.partial(project_kernel, step_count, rows // step...]
  transfers between devices with their start and end apart: 6 -> 6, of which waited for: 2 -> 2; matrix products, arithmetic and copies ran while one was open for 0% -> 0% of each run, Pallas kernels for 16% -> 36%
where the time goes in v4:
time: 19.9 us; the launch traced here: 19.7 us
  Pallas kernels  10.5 us (53%)
  starting transfers between devices  7.65 us (38%)
  waiting for transfers between devices  0.85 us (4%)
  between operations  0.7 us (4%)
    ppermute x6, starting transfers between devices, swap(): return lax.ppermute(block, axis, [(s, s ^ offset) for s in range(count)])  7.65 us
    pallas_call x1, Pallas kernels, project(): pl.pallas_call(functools.partial(project_kernel, step_count, rows // step...  3.77 us
    pallas_call x1, Pallas kernels, attend(): pl.pallas_call(functools.partial(attend_kernel, width // lanes), out_shap...  3.37 us
    pallas_call x1, Pallas kernels, finish(): pl.pallas_call(functools.partial(finish_kernel, step_count, row_count, he...  1.58 us
    pallas_call x1, Pallas kernels, pack(): pl.pallas_call(pack_kernel, out_shape=jax.ShapeDtypeStruct((rows, lanes),...  0.9 us
    pallas_call x1, Pallas kernels, route(): pl.pallas_call(functools.partial(route_kernel, replicas, shards), out_sha...  0.88 us
    ppermute x6, waiting for transfers between devices, swap(): return lax.ppermute(block, axis, [(s, s ^ offset) for s in range(count)])  0.85 us
  transfers between devices with their start and end apart: 6, of which 2 were waited for; matrix products, arithmetic and copies ran while one was open for 0% of the time, Pallas kernels for 36%

profile of v4, /device:TPU:0, one launch (start us, length us, event | category | flops | bytes accessed | tf_op | source)
XLA Modules:
  0.0 19.7 jit_solution(7679629221910694077)
XLA Ops:
  0.6 0.9 %pack.1.refs_3_ = bf16[224,128]{1,0:T(8,128)(2,1)S(1)} custom-call(bf16[64,320]{1,0:T(8,128)(2,1)} %bitcast.11, bf16[64,512]{1,0:T(8,128)(2,1)} %up_hbm.1), custom_call_target="tpu_custom_call" | custom-call | bytes 200000 | tf_op jit(solution)/shard_map/pack/pallas_call | solution.py:72
  1.5 5.1 %collective-permute-start.2 = (bf16[224,128]{1,0:T(8,128)(2,1)S(1)}, bf16[224,128]{1,0:T(8,128)(2,1)S(1)}, u32[]{:S(2)}, u32[]{:S(2)}) collective-permute-start(bf16[224,128]{1,0:T(8,128)(2,1)S(1)} %pack.1.refs_3_), channel_id=1, source_target_pairs={{0,12},{4,8},{8,4},{12,0},{1,13},{5,9},{9,5},{13,1},{2,14},{6,10},... | collective-permute-start | bytes 172040 | tf_op jit(solution)/shard_map/ppermute | solution.py:26
  6.7 0.0 collective-permute-start.1
  6.7 0.6 %collective-permute-start = (bf16[224,128]{1,0:T(8,128)(2,1)S(1)}, bf16[224,128]{1,0:T(8,128)(2,1)S(1)}, u32[]{:S(2)}, u32[]{:S(2)}) collective-permute-start(bf16[224,128]{1,0:T(8,128)(2,1)S(1)} %pack.1.refs_3_), channel_id=1, source_target_pairs={{0,4},{4,0},{8,12},{12,8},{1,5},{5,1},{9,13},{13,9},{2,6},{6,2},{1... | collective-permute-start | bytes 172040 | tf_op jit(solution)/shard_map/ppermute | solution.py:26
  7.3 0.0 copy-start
  7.3 0.0 copy-start.1
  7.3 3.8 %project.1 = (f32[32,512]{1,0:T(8,128)S(1)}, bf16[3,128,128]{2,1,0:T(8,128)(2,1)S(1)}, bf16[512,128]{1,0:T(8,128)(2,1)S(1)}, f32[32,128]{1,0:T(8,128)S(1)}, f32[32,128]{1,0:T(8,128)S(1)}) custom-call(s32[8]{0:T(128)} %lengths_hbm.3, bf16[32,1280]{1,0:T(8,128)(2,1)} %bitcast.7, bf16[32,2048]{1,0:T(8,128)(2,1)} %bitcast.10, bf16[1280,2048]{1,0:T(8,128)(2,1)} %weight_hbm.1), custom_call_target="tpu_custom_call" | custom-call | flops 167772160 | bytes 5242880 | tf_op jit(solution)/shard_map/project/pallas_call | solution.py:174
  11.1 0.0 collective-permute-done.2.refs_6_
  11.1 0.6 %collective-permute-done.1.refs_5_ = bf16[224,128]{1,0:T(8,128)(2,1)S(1)} collective-permute-done((bf16[224,128]{1,0:T(8,128)(2,1)S(1)}, bf16[224,128]{1,0:T(8,128)(2,1)S(1)}, u32[]{:S(2)}, u32[]{:S(2)}) %collective-permute-start.1) | collective-permute-done | bytes 57376 | tf_op jit(solution)/shard_map/ppermute | solution.py:26
  11.7 0.0 collective-permute-done.refs_4_
  11.7 0.0 copy-done
  11.7 0.0 copy-done.1
  11.7 0.9 %route.1 = (bf16[96,128]{1,0:T(8,128)(2,1)S(1)}, bf16[224,128]{1,0:T(8,128)(2,1)S(1)}, bf16[224,128]{1,0:T(8,128)(2,1)S(1)}, bf16[224,128]{1,0:T(8,128)(2,1)S(1)}) custom-call(s32[4]{0:T(128)S(1)} %copy-done.1, bf16[32,1280]{1,0:T(8,128)(2,1)S(1)} %bitcast.8, bf16[3,128,128]{2,1,0:T(8,128)(2,1)S(1)} %get-tuple-element.25.refs_2_, ...), custom_call_target="tpu_custom_call" | custom-call | bytes 800000 | tf_op jit(solution)/shard_map/route/pallas_call | solution.py:357
  12.6 0.0 collective-permute-start.3
  12.7 1.6 %collective-permute-start.4 = (bf16[224,128]{1,0:T(8,128)(2,1)S(1)}, bf16[224,128]{1,0:T(8,128)(2,1)S(1)}, u32[]{:S(2)}, u32[]{:S(2)}) collective-permute-start(bf16[224,128]{1,0:T(8,128)(2,1)S(1)} %get-tuple-element.28), channel_id=1, source_target_pairs={{0,2},{1,3},{2,0},{3,1},{4,6},{5,7},{6,4},{7,5},{8,10},{9,11},{10,... | collective-permute-start | bytes 172040 | tf_op jit(solution)/shard_map/ppermute | solution.py:26
  14.2 0.3 %collective-permute-start.5 = (bf16[224,128]{1,0:T(8,128)(2,1)S(1)}, bf16[224,128]{1,0:T(8,128)(2,1)S(1)}, u32[]{:S(2)}, u32[]{:S(2)}) collective-permute-start(bf16[224,128]{1,0:T(8,128)(2,1)S(1)} %get-tuple-element.29), channel_id=1, source_target_pairs={{0,3},{1,2},{2,1},{3,0},{4,7},{5,6},{6,5},{7,4},{8,11},{9,10},{10,... | collective-permute-start | bytes 172040 | tf_op jit(solution)/shard_map/ppermute | solution.py:26
  14.5 0.0 copy-start.2
  14.5 3.4 %attend.1 = (f32[512,128]{1,0:T(8,128)S(1)}, f32[512,128]{1,0:T(8,128)S(1)}, f32[512,128]{1,0:T(8,128)S(1)}) custom-call(s32[8]{0:T(128)} %lengths_hbm.3, bf16[512,128]{1,0:T(8,128)(2,1)S(1)} %get-tuple-element.19.grouped_ref.refs_2_, bf16[8,512,256]{2,1,0:T(8,128)(2,1)} %keys_hbm.1, bf16[8,512,256]{2,1,0:T(8,128)(2,1)} %values_hbm.1), custom_call_target="tpu_custom_call" | custom-call | flops 134217728 | bytes 4194304 | tf_op jit(solution)/shard_map/attend/pallas_call | solution.py:277
  17.9 0.0 collective-permute-done.3.refs_9_
  17.9 0.0 collective-permute-done.4.refs_10_
  17.9 0.2 collective-permute-done.5.refs_11_
  18.1 0.0 copy-done.2
  18.1 1.6 %finish.1 = (bf16[32,2048]{1,0:T(8,128)(2,1)}, bf16[32,256]{1,0:T(8,128)(2,1)}, bf16[32,256]{1,0:T(8,128)(2,1)}) custom-call(f32[32,512]{1,0:T(8,128)S(1)} %get-tuple-element.18.refs_0_, f32[1,128]{1,0:T(1,128)S(1)} %bitcast.9, bf16[512,128]{1,0:T(8,128)(2,1)S(1)} %get-tuple-element.19.grouped_ref.refs_2_, f32[512,128]{1,0:T(8,128)S(1)} %get-tuple-element.20.refs_3_, ...), custom_call_target="tpu_custom_call" | custom-call | bytes 1000000 | tf_op jit(solution)/shard_map/finish/pallas_call | solution.py:489
Async XLA Ops:
  1.5 9.5 %collective-permute-start.2 = (bf16[224,128]{1,0:T(8,128)(2,1)S(1)}, bf16[224,128]{1,0:T(8,128)(2,1)S(1)}, u32[]{:S(2)}, u32[]{:S(2)}) collective-permute-start(bf16[224,128]{1,0:T(8,128)(2,1)S(1)} %pack.1.refs_3_), channel_id=1, source_target_pairs={{0,12},{4,8},{8,4},{12,0},{1,13},{5,9},{9,5},{13,1},{2,14},{6,10},... | collective-permute-start | bytes 172040 | tf_op jit(solution)/shard_map/ppermute | solution.py:26
  6.7 5.1 %collective-permute-start.1 = (bf16[224,128]{1,0:T(8,128)(2,1)S(1)}, bf16[224,128]{1,0:T(8,128)(2,1)S(1)}, u32[]{:S(2)}, u32[]{:S(2)}) collective-permute-start(bf16[224,128]{1,0:T(8,128)(2,1)S(1)} %pack.1.refs_3_), channel_id=1, source_target_pairs={{0,8},{4,12},{8,0},{12,4},{1,9},{5,13},{9,1},{13,5},{2,10},{6,14},... | collective-permute-start | bytes 172040 | tf_op jit(solution)/shard_map/ppermute | solution.py:26
  6.7 5.1 %collective-permute-start = (bf16[224,128]{1,0:T(8,128)(2,1)S(1)}, bf16[224,128]{1,0:T(8,128)(2,1)S(1)}, u32[]{:S(2)}, u32[]{:S(2)}) collective-permute-start(bf16[224,128]{1,0:T(8,128)(2,1)S(1)} %pack.1.refs_3_), channel_id=1, source_target_pairs={{0,4},{4,0},{8,12},{12,8},{1,5},{5,1},{9,13},{13,9},{2,6},{6,2},{1... | collective-permute-start | bytes 172040 | tf_op jit(solution)/shard_map/ppermute | solution.py:26
  7.3 4.4 %copy-start = (bf16[4,8,1280]{2,1,0:T(8,128)(2,1)S(1)}, bf16[4,8,1280]{2,1,0:T(8,128)(2,1)}, u32[]{:S(2)}) copy-start(bf16[4,8,1280]{2,1,0:T(8,128)(2,1)} %param.10) | copy-start | bytes 245764
  7.3 4.4 %copy-start.1 = (s32[4]{0:T(128)S(1)}, s32[4]{0:T(128)}, u32[]{:S(2)}) copy-start(s32[4]{0:T(128)} %refs_0_.1) | copy-start | bytes 52
  12.6 5.3 %collective-permute-start.3 = (bf16[224,128]{1,0:T(8,128)(2,1)S(1)}, bf16[224,128]{1,0:T(8,128)(2,1)S(1)}, u32[]{:S(2)}, u32[]{:S(2)}) collective-permute-start(bf16[224,128]{1,0:T(8,128)(2,1)S(1)} %get-tuple-element.27), channel_id=1, source_target_pairs={{0,1},{1,0},{2,3},{3,2},{4,5},{5,4},{6,7},{7,6},{8,9},{9,8},{10,11... | collective-permute-start | bytes 172040 | tf_op jit(solution)/shard_map/ppermute | solution.py:26
  12.7 5.3 %collective-permute-start.4 = (bf16[224,128]{1,0:T(8,128)(2,1)S(1)}, bf16[224,128]{1,0:T(8,128)(2,1)S(1)}, u32[]{:S(2)}, u32[]{:S(2)}) collective-permute-start(bf16[224,128]{1,0:T(8,128)(2,1)S(1)} %get-tuple-element.28), channel_id=1, source_target_pairs={{0,2},{1,3},{2,0},{3,1},{4,6},{5,7},{6,4},{7,5},{8,10},{9,11},{10,... | collective-permute-start | bytes 172040 | tf_op jit(solution)/shard_map/ppermute | solution.py:26
  14.2 3.9 %collective-permute-start.5 = (bf16[224,128]{1,0:T(8,128)(2,1)S(1)}, bf16[224,128]{1,0:T(8,128)(2,1)S(1)}, u32[]{:S(2)}, u32[]{:S(2)}) collective-permute-start(bf16[224,128]{1,0:T(8,128)(2,1)S(1)} %get-tuple-element.29), channel_id=1, source_target_pairs={{0,3},{1,2},{2,1},{3,0},{4,7},{5,6},{6,5},{7,4},{8,11},{9,10},{10,... | collective-permute-start | bytes 172040 | tf_op jit(solution)/shard_map/ppermute | solution.py:26
  14.5 3.6 %copy-start.2 = (f32[128]{0:T(128)S(1)}, f32[128]{0:T(128)}, u32[]{:S(2)}) copy-start(f32[128]{0:T(128)} %param.14) | copy-start | bytes 1540

commit v5 on v4

--- a/solution.py
+++ b/solution.py
@@ -67,7 +67,7 @@
         first += rank_part
 
 
-def pack(down, up, rank_part):
+def pack(down, up, rank_part, beside):
     rows = (down.size + rank_part * up.shape[1]) // lanes
     return pl.pallas_call(
         pack_kernel,
@@ -81,64 +81,57 @@
         ],
         compiler_params=pltpu.CompilerParams(vmem_limit_bytes=2 * 2**20),
         name="pack",
-        cost_estimate=pl.CostEstimate(flops=0, bytes_accessed=200000, transcendentals=0),
+        cost_estimate=beside,
     )(*in_hbm(down, up))
 
 
-def project_kernel(
+def front_kernel(
     step_count,
     row_count,
     head_count,
     shards,
     lengths_hbm,
-    tokens_hbm,
-    queries_hbm,
-    weight_hbm,
+    tokens_ref,
+    queries_ref,
+    weight_ref,
+    keys_ref,
+    values_ref,
     own_ref,
     base_ref,
     grouped_ref,
+    total_ref,
+    peak_ref,
+    sum_ref,
     cosine_ref,
     sine_ref,
     lengths_ref,
-    tokens_ref,
-    queries_ref,
-    weight_ref,
     regroup,
-    sems,
-    weight_sems,
+    scores,
+    raised,
+    length_sem,
 ):
+    lengths_copy = pltpu.make_async_copy(lengths_hbm, lengths_ref, length_sem)
+    lengths_copy.start()
     shard = lax.axis_index("tensor")
     rows, own = own_ref.shape
+    slots = keys_ref.shape[1]
     group = queries_ref.shape[1] // (head_count * lanes)
     seen = step_count * group
-    lengths_copy = pltpu.make_async_copy(lengths_hbm, lengths_ref, sems.at[0])
-    queries_copy = pltpu.make_async_copy(queries_hbm, queries_ref, sems.at[1])
-    tokens_copy = pltpu.make_async_copy(tokens_hbm, tokens_ref, sems.at[2])
-    weight_copies = [
-        pltpu.make_async_copy(
-            weight_hbm.at[:, pl.ds(pl.multiple_of((shard ^ i) * own, lanes), own)],
-            weight_ref.at[i],
-            weight_sems.at[i],
+    scale = lanes**-0.5
+
+    def product(i):
+        first = pl.multiple_of((shard ^ i) * own, lanes)
+        block = jnp.dot(
+            tokens_ref[...], weight_ref[:, pl.ds(first, own)], preferred_element_type=f32
         )
-        for i in range(shards)
-    ]
-    for copy in [lengths_copy, queries_copy, tokens_copy] + weight_copies:
-        copy.start()
-
-    lengths_copy.wait()
-    row = lax.broadcasted_iota(jnp.int32, (rows, lanes), 0)
-    lane = lax.broadcasted_iota(jnp.int32, (rows, lanes), 1)
-    position = row // row_count
-    for b in range(row_count):
-        position = position + jnp.where(row % row_count == b, lengths_ref[b], 0)
-    middle = lanes // 2
-    spacing = (lane % middle).astype(f32) * (-2.0 / lanes * math.log(rope_base))
-    angles = position.astype(f32) * jnp.exp(spacing)
-    cosine_ref[...] = jnp.cos(angles)
-    sine = jnp.sin(angles)
-    sine_ref[...] = jnp.where(lane < middle, -sine, sine)
-
-    queries_copy.wait()
+        if i == 0:
+            own_ref[...] = block
+            return
+        for c in range(own // lanes):
+            base_ref[i - 1, c * rows : (c + 1) * rows, :] = block[
+                :, c * lanes : (c + 1) * lanes
+            ].astype(bf16)
+
     for pair in range(step_count // 2):
         for q in range(head_count * group):
             h, g = q // group, q % group
@@ -152,93 +145,11 @@
                 ]
     grouped_ref[...] = regroup[...].astype(bf16)
 
-    tokens_copy.wait()
-    for i in range(shards):
-        weight_copies[i].wait()
-        block = jnp.dot(tokens_ref[...], weight_ref[i], preferred_element_type=f32)
-        if i == 0:
-            own_ref[...] = block
-            continue
-        for c in range(own // lanes):
-            base_ref[i - 1, c * rows : (c + 1) * rows, :] = block[
-                :, c * lanes : (c + 1) * lanes
-            ].astype(bf16)
-
-
-def project(lengths, tokens, queries, weight, step_count, head_count, shards):
-    rows, depth = tokens.shape
-    columns = weight.shape[1]
-    own = columns // shards
-    seen_rows = rows * queries.shape[1] // lanes
-    table = jax.ShapeDtypeStruct((rows, lanes), f32)
-    return pl.pallas_call(
-        functools.partial(project_kernel, step_count, rows // step_count, head_count, shards),
-        out_shape=(
-            jax.ShapeDtypeStruct((rows, own), f32),
-            jax.ShapeDtypeStruct((shards - 1, rows * own // lanes, lanes), bf16),
-            jax.ShapeDtypeStruct((seen_rows, lanes), bf16),
-            table,
-            table,
-        ),
-        in_specs=[stays_in_hbm] * 4,
-        out_specs=(whole_in_vmem,) * 5,
-        scratch_shapes=[
-            pltpu.SMEM(lengths.shape, jnp.int32),
-            pltpu.VMEM(tokens.shape, bf16),
-            pltpu.VMEM(queries.shape, bf16),
-            pltpu.VMEM((shards, depth, own), bf16),
-            pltpu.VMEM((seen_rows, lanes), f32),
-            pltpu.SemaphoreType.DMA((3,)),
-            pltpu.SemaphoreType.DMA((shards,)),
-        ],
-        compiler_params=pltpu.CompilerParams(vmem_limit_bytes=12 * 2**20),
-        name="project",
-        cost_estimate=pl.CostEstimate(
-            flops=2 * rows * weight.size, bytes_accessed=2 * weight.size, transcendentals=0
-        ),
-    )(*in_hbm(lengths, tokens, queries, weight))
-
-
-def attend_kernel(
-    head_count,
-    lengths_hbm,
-    grouped_ref,
-    keys_hbm,
-    values_hbm,
-    total_ref,
-    peak_ref,
-    sum_ref,
-    lengths_ref,
-    keys_ref,
-    values_ref,
-    scores,
-    raised,
-    length_sem,
-    key_sems,
-    value_sems,
-):
-    row_count, slots, _ = keys_ref.shape
-    seen = grouped_ref.shape[0] // (head_count * row_count)
-    scale = lanes**-0.5
-    lengths_copy = pltpu.make_async_copy(lengths_hbm, lengths_ref, length_sem)
-    key_copies = [
-        pltpu.make_async_copy(keys_hbm.at[b], keys_ref.at[b], key_sems.at[b])
-        for b in range(row_count)
-    ]
-    value_copies = [
-        pltpu.make_async_copy(values_hbm.at[b], values_ref.at[b], value_sems.at[b])
-        for b in range(row_count)
-    ]
-    for copy in [lengths_copy] + key_copies + value_copies:
-        copy.start()
-    lengths_copy.wait()
-
     def place(h, b):
         at = (h * row_count + b) * seen
         return slice(at, at + seen)
 
-    for b in range(row_count):
-        key_copies[b].wait()
+    def score_row(b):
         for h in range(head_count):
             scores[place(h, b), :] = lax.dot_general(
                 grouped_ref[place(h, b), :],
@@ -246,10 +157,10 @@
                 (((1,), (1,)), ((), ())),
                 preferred_element_type=f32,
             )
-    for copy in value_copies:
-        copy.wait()
+
     slot = lax.broadcasted_iota(jnp.int32, (seen, slots), 1)
-    for b in range(row_count):
+
+    def lift_row(b):
         live = slot < lengths_ref[b]
         for h in range(head_count):
             score = jnp.where(live, scores[place(h, b), :] * scale, masked_score)
@@ -260,7 +171,8 @@
             sum_ref[place(h, b), :] = jnp.broadcast_to(
                 jnp.sum(lifted, axis=1, keepdims=True), (seen, lanes)
             )
-    for b in range(row_count):
+
+    def weigh_row(b):
         for h in range(head_count):
             total_ref[place(h, b), :] = jnp.dot(
                 raised[place(h, b), :],
@@ -268,40 +180,73 @@
                 preferred_element_type=f32,
             )
 
-
-def attend(lengths, grouped, keys, values):
+    for b in range(row_count):
+        score_row(b)
+    lengths_copy.wait()
+    for b in range(row_count):
+        lift_row(b)
+        if b < shards:
+            product(b)
+    for i in range(row_count, shards):
+        product(i)
+    for b in range(row_count):
+        weigh_row(b)
+
+    row = lax.broadcasted_iota(jnp.int32, (rows, lanes), 0)
+    lane = lax.broadcasted_iota(jnp.int32, (rows, lanes), 1)
+    position = row // row_count
+    for b in range(row_count):
+        position = position + jnp.where(row % row_count == b, lengths_ref[b], 0)
+    middle = lanes // 2
+    spacing = (lane % middle).astype(f32) * (-2.0 / lanes * math.log(rope_base))
+    angles = position.astype(f32) * jnp.exp(spacing)
+    cosine_ref[...] = jnp.cos(angles)
+    sine = jnp.sin(angles)
+    sine_ref[...] = jnp.where(lane < middle, -sine, sine)
+
+def front(lengths, tokens, queries, weight, keys, values, step_count, shards):
     row_count, slots, width = keys.shape
-    seen_rows = grouped.shape[0]
+    head_count = width // lanes
+    depth, columns = weight.shape
+    own = columns // shards
+    rows = step_count * row_count
+    seen_rows = rows * queries.shape[1] // lanes
+    table = jax.ShapeDtypeStruct((rows, lanes), f32)
     seen_table = jax.ShapeDtypeStruct((seen_rows, lanes), f32)
-    lengths, keys, values = in_hbm(lengths, keys, values)
     return pl.pallas_call(
-        functools.partial(attend_kernel, width // lanes),
-        out_shape=(seen_table,) * 3,
-        in_specs=[stays_in_hbm, whole_in_vmem, stays_in_hbm, stays_in_hbm],
-        out_specs=(whole_in_vmem,) * 3,
+        functools.partial(front_kernel, step_count, row_count, head_count, shards),
+        out_shape=(
+            jax.ShapeDtypeStruct((rows, own), f32),
+            jax.ShapeDtypeStruct((shards - 1, rows * own // lanes, lanes), bf16),
+            jax.ShapeDtypeStruct((seen_rows, lanes), bf16),
+            seen_table,
+            seen_table,
+            seen_table,
+            table,
+            table,
+        ),
+        in_specs=[stays_in_hbm] + [whole_in_vmem] * 5,
+        out_specs=(whole_in_vmem,) * 8,
         scratch_shapes=[
             pltpu.SMEM(lengths.shape, jnp.int32),
-            pltpu.VMEM(keys.shape, bf16),
-            pltpu.VMEM(values.shape, bf16),
+            pltpu.VMEM((seen_rows, lanes), f32),
             pltpu.VMEM((seen_rows, slots), f32),
             pltpu.VMEM((seen_rows, slots), bf16),
             pltpu.SemaphoreType.DMA,
-            pltpu.SemaphoreType.DMA((row_count,)),
-            pltpu.SemaphoreType.DMA((row_count,)),
         ],
-        compiler_params=pltpu.CompilerParams(vmem_limit_bytes=12 * 2**20),
-        name="attend",
+        compiler_params=pltpu.CompilerParams(vmem_limit_bytes=8 * 2**20),
+        name="front",
         cost_estimate=pl.CostEstimate(
-            flops=4 * seen_rows * slots * lanes,
-            bytes_accessed=2 * (keys.size + values.size),
+            flops=2 * rows * depth * columns + 4 * seen_rows * slots * lanes,
+            bytes_accessed=2 * (weight.size + keys.size + values.size),
             transcendentals=seen_rows * slots,
         ),
-    )(lengths, grouped, keys, values)
+    )(*in_hbm(lengths), tokens, queries, weight, keys, values)
 
 
 def route_kernel(replicas, shards, *refs):
     owners_ref, tokens_ref, base_ref = refs[:3]
-    piece_refs = refs[3 : 3 + replicas]
+    piece_refs = refs[3 : 3 + replicas][::-1]
     out_refs = refs[3 + replicas : 3 + replicas + shards]
     token_buf, left, right, up_buf = refs[3 + replicas + shards :]
     replica = lax.axis_index("rollout")
@@ -371,7 +316,7 @@
         compiler_params=pltpu.CompilerParams(vmem_limit_bytes=4 * 2**20),
         name="route",
         cost_estimate=pl.CostEstimate(flops=0, bytes_accessed=800000, transcendentals=0),
-    )(owners, tokens, base, *pieces)
+    )(owners, tokens, base, *pieces[::-1])
 
 
 def route_plain(owners, tokens, base, down, up, rank_part, own):
@@ -399,7 +344,7 @@
 
 def finish_kernel(step_count, row_count, head_count, shards, *refs):
     own_ref, gain_ref, grouped_ref, total_ref, peak_ref, sum_ref, cosine_ref, sine_ref = refs[:8]
-    packet_refs = refs[8 : 8 + shards]
+    packet_refs = refs[8 : 8 + shards][::-1]
     attention_ref, keys_ref, values_ref = refs[8 + shards : 11 + shards]
     up_buf, ordered = refs[11 + shards :]
     shard = lax.axis_index("tensor")
@@ -502,7 +447,7 @@
         compiler_params=pltpu.CompilerParams(vmem_limit_bytes=6 * 2**20),
         name="finish",
         cost_estimate=pl.CostEstimate(flops=0, bytes_accessed=1000000, transcendentals=0),
-    )(mine, gain, grouped, total, peak, denominator, cosine, sine, *packets)
+    )(mine, gain, grouped, total, peak, denominator, cosine, sine, *packets[::-1])
 
 
 def per_device(
@@ -535,12 +480,13 @@
         and rank_part % 16 == 0
     )
     if fits:
-        packed = pack(adapter_down.T, adapter_up, rank_part)
+        fetched = 2 * (key_value_weight.size + cache_keys.size + stored_values.size)
+        beside = pl.CostEstimate(flops=1000 * fetched, bytes_accessed=fetched, transcendentals=0)
+        packed = pack(adapter_down.T, adapter_up, rank_part, beside)
         arrived = {i: swap(packed, "rollout", i) for i in reversed(range(1, replicas))}
         pieces = [packed] + [arrived[i] for i in range(1, replicas)]
-    head_count = cache_keys.shape[2] // lanes
-    mine, base, grouped, cosine, sine = project(
-        lengths, tokens, query_rows, key_value_weight, step_count, head_count, shards
+    mine, base, *partials = front(
+        lengths, tokens, query_rows, key_value_weight, cache_keys, stored_values, step_count, shards
     )
     if fits:
         packets = route(owners, tokens, base, pieces, rank, rank_part * own // lanes)
@@ -548,9 +494,8 @@
         packets = route_plain(owners, tokens, base, adapter_down, adapter_up, rank_part, own)
     arrived = {i: swap(packets[i], "tensor", i) for i in reversed(range(1, shards))}
     packets = [packets[0]] + [arrived[i] for i in range(1, shards)]
-    total, peak, denominator = attend(lengths, grouped, cache_keys, stored_values)
     attention, keys, values = finish(
-        (mine, grouped, total, peak, denominator, cosine, sine),
+        [mine] + partials,
         key_gain.reshape(1, -1),
         packets,
         rank,

time: 19.9 us -> 20.1 us (1.010)
  waiting for transfers between devices: 0.85 us -> 5.07 us
  Pallas kernels: 10.5 us -> 6.35 us
    pallas_call x2 -> x1, Pallas kernels: 7.13 us -> 2.84 us  [front(): pl.pallas_call(functools.partial(front_kernel, step_count, row_count, hea...]
    ppermute x6, waiting for transfers between devices: 0.85 us -> 5.07 us  [swap(): return lax.ppermute(block, axis, [(s, s ^ offset) for s in range(count)])]
  transfers between devices with their start and end apart: 6 -> 6, of which waited for: 2 -> 3; matrix products, arithmetic and copies ran while one was open for 0% -> 0% of each run, Pallas kernels for 36% -> 14%
where the time goes in v5:
time: 20.1 us; the launch traced here: 19.9 us
  starting transfers between devices  7.64 us (38%)
  Pallas kernels  6.35 us (32%)
  waiting for transfers between devices  5.07 us (25%)
  between operations  0.76 us (4%)
    ppermute x6, starting transfers between devices, swap(): return lax.ppermute(block, axis, [(s, s ^ offset) for s in range(count)])  7.64 us
    ppermute x6, waiting for transfers between devices, swap(): return lax.ppermute(block, axis, [(s, s ^ offset) for s in range(count)])  5.07 us
    pallas_call x1, Pallas kernels, front(): pl.pallas_call(functools.partial(front_kernel, step_count, row_count, hea...  2.84 us
    pallas_call x1, Pallas kernels, finish(): pl.pallas_call(functools.partial(finish_kernel, step_count, row_count, he...  1.59 us
    pallas_call x1, Pallas kernels, pack(): pl.pallas_call(pack_kernel, out_shape=jax.ShapeDtypeStruct((rows, lanes),...  1.05 us
    pallas_call x1, Pallas kernels, route(): pl.pallas_call(functools.partial(route_kernel, replicas, shards), out_sha...  0.88 us
  transfers between devices with their start and end apart: 6, of which 3 were waited for; matrix products, arithmetic and copies ran while one was open for 0% of the time, Pallas kernels for 14%

profile of v5, /device:TPU:0, one launch (start us, length us, event | category | flops | bytes accessed | tf_op | source)
XLA Modules:
  0.0 19.9 jit_solution(14827420906716274694)
XLA Ops:
  0.6 0.0 slice-start
  0.6 0.0 slice-start.1
  0.7 0.0 copy-start
  0.7 0.0 copy-start.1
  0.7 0.0 copy-start.2
  0.7 0.0 copy-start.3
  0.7 1.0 %pack.1.refs_6_ = bf16[224,128]{1,0:T(8,128)(2,1)S(1)} custom-call(bf16[64,320]{1,0:T(8,128)(2,1)} %bitcast.14, bf16[64,512]{1,0:T(8,128)(2,1)} %up_hbm.1), custom_call_target="tpu_custom_call" | custom-call | flops 9437184000 | bytes 9437184 | tf_op jit(solution)/shard_map/pack/pallas_call | solution.py:72
  1.7 5.1 %collective-permute-start = (bf16[224,128]{1,0:T(8,128)(2,1)S(1)}, bf16[224,128]{1,0:T(8,128)(2,1)S(1)}, u32[]{:S(2)}, u32[]{:S(2)}) collective-permute-start(bf16[224,128]{1,0:T(8,128)(2,1)S(1)} %pack.1.refs_6_), channel_id=1, source_target_pairs={{0,12},{4,8},{8,4},{12,0},{1,13},{5,9},{9,5},{13,1},{2,14},{6,10},... | collective-permute-start | bytes 172040 | tf_op jit(solution)/shard_map/ppermute | solution.py:26
  6.9 0.0 collective-permute-start.1
  6.9 0.6 %collective-permute-start.2 = (bf16[224,128]{1,0:T(8,128)(2,1)S(1)}, bf16[224,128]{1,0:T(8,128)(2,1)S(1)}, u32[]{:S(2)}, u32[]{:S(2)}) collective-permute-start(bf16[224,128]{1,0:T(8,128)(2,1)S(1)} %pack.1.refs_6_), channel_id=1, source_target_pairs={{0,4},{4,0},{8,12},{12,8},{1,5},{5,1},{9,13},{13,9},{2,6},{6,2},{1... | collective-permute-start | bytes 172040 | tf_op jit(solution)/shard_map/ppermute | solution.py:26
  7.5 0.0 slice-done
  7.5 0.0 slice-done.1
  7.5 0.0 copy-done
  7.5 0.0 copy-done.1
  7.5 0.0 copy-done.2
  7.5 0.0 copy-done.3
  7.5 0.0 copy-start.4
  7.6 0.0 copy-start.5
  7.6 2.8 %front.1 = (f32[32,512]{1,0:T(8,128)S(1)}, bf16[3,128,128]{2,1,0:T(8,128)(2,1)S(1)}, bf16[512,128]{1,0:T(8,128)(2,1)S(1)}, f32[512,128]{1,0:T(8,128)S(1)}, f32[5...) custom-call(s32[8]{0:T(128)} %lengths_hbm.1, ...), custom_call_target="tpu_custom_call" | custom-call | flops 301989888 | bytes 9437184 | tf_op jit(solution)/shard_map/front/pallas_call | solution.py:216
  10.4 0.0 collective-permute-done.refs_3_
  10.4 1.5 %collective-permute-done.1.refs_4_ = bf16[224,128]{1,0:T(8,128)(2,1)S(1)} collective-permute-done((bf16[224,128]{1,0:T(8,128)(2,1)S(1)}, bf16[224,128]{1,0:T(8,128)(2,1)S(1)}, u32[]{:S(2)}, u32[]{:S(2)}) %collective-permute-start.1) | collective-permute-done | bytes 57376 | tf_op jit(solution)/shard_map/ppermute | solution.py:26
  11.9 0.0 collective-permute-done.2.refs_5_
  11.9 0.0 copy-done.4
  11.9 0.9 %route.1 = (bf16[96,128]{1,0:T(8,128)(2,1)S(1)}, bf16[224,128]{1,0:T(8,128)(2,1)S(1)}, bf16[224,128]{1,0:T(8,128)(2,1)S(1)}, bf16[224,128]{1,0:T(8,128)(2,1)S(1)}) custom-call(s32[4]{0:T(128)S(1)} %copy-done.4, bf16[32,1280]{1,0:T(8,128)(2,1)S(1)} %bitcast.10, bf16[3,128,128]{2,1,0:T(8,128)(2,1)S(1)} %get-tuple-element.25.refs_2_, ...), custom_call_target="tpu_custom_call" | custom-call | bytes 800000 | tf_op jit(solution)/shard_map/route/pallas_call | solution.py:302
  12.8 0.3 %collective-permute-start.3 = (bf16[224,128]{1,0:T(8,128)(2,1)S(1)}, bf16[224,128]{1,0:T(8,128)(2,1)S(1)}, u32[]{:S(2)}, u32[]{:S(2)}) collective-permute-start(bf16[224,128]{1,0:T(8,128)(2,1)S(1)} %get-tuple-element.26), channel_id=1, source_target_pairs={{0,3},{1,2},{2,1},{3,0},{4,7},{5,6},{6,5},{7,4},{8,11},{9,10},{10,... | collective-permute-start | bytes 172040 | tf_op jit(solution)/shard_map/ppermute | solution.py:26
  13.2 1.3 %collective-permute-start.4 = (bf16[224,128]{1,0:T(8,128)(2,1)S(1)}, bf16[224,128]{1,0:T(8,128)(2,1)S(1)}, u32[]{:S(2)}, u32[]{:S(2)}) collective-permute-start(bf16[224,128]{1,0:T(8,128)(2,1)S(1)} %get-tuple-element.27), channel_id=1, source_target_pairs={{0,2},{1,3},{2,0},{3,1},{4,6},{5,7},{6,4},{7,5},{8,10},{9,11},{10,... | collective-permute-start | bytes 172040 | tf_op jit(solution)/shard_map/ppermute | solution.py:26
  14.4 0.3 %collective-permute-start.5 = (bf16[224,128]{1,0:T(8,128)(2,1)S(1)}, bf16[224,128]{1,0:T(8,128)(2,1)S(1)}, u32[]{:S(2)}, u32[]{:S(2)}) collective-permute-start(bf16[224,128]{1,0:T(8,128)(2,1)S(1)} %get-tuple-element.28), channel_id=1, source_target_pairs={{0,1},{1,0},{2,3},{3,2},{4,5},{5,4},{6,7},{7,6},{8,9},{9,8},{10,11... | collective-permute-start | bytes 172040 | tf_op jit(solution)/shard_map/ppermute | solution.py:26
  14.7 2.3 %collective-permute-done.3.refs_8_ = bf16[224,128]{1,0:T(8,128)(2,1)S(1)} collective-permute-done((bf16[224,128]{1,0:T(8,128)(2,1)S(1)}, bf16[224,128]{1,0:T(8,128)(2,1)S(1)}, u32[]{:S(2)}, u32[]{:S(2)}) %collective-permute-start.3) | collective-permute-done | bytes 57376 | tf_op jit(solution)/shard_map/ppermute | solution.py:26
  17.0 1.3 %collective-permute-done.4.refs_9_ = bf16[224,128]{1,0:T(8,128)(2,1)S(1)} collective-permute-done((bf16[224,128]{1,0:T(8,128)(2,1)S(1)}, bf16[224,128]{1,0:T(8,128)(2,1)S(1)}, u32[]{:S(2)}, u32[]{:S(2)}) %collective-permute-start.4) | collective-permute-done | bytes 57376 | tf_op jit(solution)/shard_map/ppermute | solution.py:26
  18.3 0.0 collective-permute-done.5.refs_10_
  18.3 0.0 copy-done.5
  18.3 1.6 %finish.1 = (bf16[32,2048]{1,0:T(8,128)(2,1)}, bf16[32,256]{1,0:T(8,128)(2,1)}, bf16[32,256]{1,0:T(8,128)(2,1)}) custom-call(f32[32,512]{1,0:T(8,128)S(1)} %get-tuple-element.18.refs_0_, f32[1,128]{1,0:T(1,128)S(1)} %bitcast.12, bf16[512,128]{1,0:T(8,128)(2,1)S(1)} %get-tuple-element.19.refs_2_, f32[512,128]{1,0:T(8,128)S(1)} %get-tuple-element.20.refs_3_, ...), custom_call_target="tpu_custom_call" | custom-call | bytes 1000000 | tf_op jit(solution)/shard_map/finish/pallas_call | solution.py:434
  (1 shorter events, 0.0 us)
Async XLA Ops:
  0.6 6.9 %slice-start = ((s8[5242880]{0:T(1024)(128)(4,1)}), s8[4194304]{0:T(1024)(128)(4,1)S(1)}, s32[]{:S(2)}) async-start(s8[5242880]{0:T(1024)(128)(4,1)} %bitcast.7), calls=%async_computation | async-start | bytes 8388608
  0.6 6.9 %slice-start.1 = ((s8[5242880]{0:T(1024)(128)(4,1)}), s8[1048576]{0:T(1024)(128)(4,1)S(1)}, s32[]{:S(2)}) async-start(s8[5242880]{0:T(1024)(128)(4,1)} %bitcast.7), calls=%async_computation.1 | async-start | bytes 2097152
  0.7 6.9 %copy-start = (bf16[8,512,256]{2,1,0:T(8,128)(2,1)S(1)}, bf16[8,512,256]{2,1,0:T(8,128)(2,1)}, u32[]{:S(2)}) copy-start(bf16[8,512,256]{2,1,0:T(8,128)(2,1)} %keys_ref.1) | copy-start | bytes 6291460
  0.7 6.9 %copy-start.1 = (bf16[8,512,256]{2,1,0:T(8,128)(2,1)S(1)}, bf16[8,512,256]{2,1,0:T(8,128)(2,1)}, u32[]{:S(2)}) copy-start(bf16[8,512,256]{2,1,0:T(8,128)(2,1)} %values_ref.1) | copy-start | bytes 6291460
  0.7 6.8 %copy-start.2 = (bf16[4,8,1280]{2,1,0:T(8,128)(2,1)S(1)}, bf16[4,8,1280]{2,1,0:T(8,128)(2,1)}, u32[]{:S(2)}) copy-start(bf16[4,8,1280]{2,1,0:T(8,128)(2,1)} %param.10) | copy-start | bytes 245764
  0.7 6.8 %copy-start.3 = (bf16[4,8,2048]{2,1,0:T(8,128)(2,1)S(1)}, bf16[4,8,2048]{2,1,0:T(8,128)(2,1)}, u32[]{:S(2)}) copy-start(bf16[4,8,2048]{2,1,0:T(8,128)(2,1)} %param.15) | copy-start | bytes 393220
  1.7 8.7 %collective-permute-start = (bf16[224,128]{1,0:T(8,128)(2,1)S(1)}, bf16[224,128]{1,0:T(8,128)(2,1)S(1)}, u32[]{:S(2)}, u32[]{:S(2)}) collective-permute-start(bf16[224,128]{1,0:T(8,128)(2,1)S(1)} %pack.1.refs_6_), channel_id=1, source_target_pairs={{0,12},{4,8},{8,4},{12,0},{1,13},{5,9},{9,5},{13,1},{2,14},{6,10},... | collective-permute-start | bytes 172040 | tf_op jit(solution)/shard_map/ppermute | solution.py:26
  6.9 5.1 %collective-permute-start.1 = (bf16[224,128]{1,0:T(8,128)(2,1)S(1)}, bf16[224,128]{1,0:T(8,128)(2,1)S(1)}, u32[]{:S(2)}, u32[]{:S(2)}) collective-permute-start(bf16[224,128]{1,0:T(8,128)(2,1)S(1)} %pack.1.refs_6_), channel_id=1, source_target_pairs={{0,8},{4,12},{8,0},{12,4},{1,9},{5,13},{9,1},{13,5},{2,10},{6,14},... | collective-permute-start | bytes 172040 | tf_op jit(solution)/shard_map/ppermute | solution.py:26
  6.9 5.1 %collective-permute-start.2 = (bf16[224,128]{1,0:T(8,128)(2,1)S(1)}, bf16[224,128]{1,0:T(8,128)(2,1)S(1)}, u32[]{:S(2)}, u32[]{:S(2)}) collective-permute-start(bf16[224,128]{1,0:T(8,128)(2,1)S(1)} %pack.1.refs_6_), channel_id=1, source_target_pairs={{0,4},{4,0},{8,12},{12,8},{1,5},{5,1},{9,13},{13,9},{2,6},{6,2},{1... | collective-permute-start | bytes 172040 | tf_op jit(solution)/shard_map/ppermute | solution.py:26
  7.5 4.4 %copy-start.4 = (s32[4]{0:T(128)S(1)}, s32[4]{0:T(128)}, u32[]{:S(2)}) copy-start(s32[4]{0:T(128)} %refs_0_.1) | copy-start | bytes 52
  7.6 10.7 %copy-start.5 = (f32[128]{0:T(128)S(1)}, f32[128]{0:T(128)}, u32[]{:S(2)}) copy-start(f32[128]{0:T(128)} %param.14) | copy-start | bytes 1540
  12.8 4.2 %collective-permute-start.3 = (bf16[224,128]{1,0:T(8,128)(2,1)S(1)}, bf16[224,128]{1,0:T(8,128)(2,1)S(1)}, u32[]{:S(2)}, u32[]{:S(2)}) collective-permute-start(bf16[224,128]{1,0:T(8,128)(2,1)S(1)} %get-tuple-element.26), channel_id=1, source_target_pairs={{0,3},{1,2},{2,1},{3,0},{4,7},{5,6},{6,5},{7,4},{8,11},{9,10},{10,... | collective-permute-start | bytes 172040 | tf_op jit(solution)/shard_map/ppermute | solution.py:26
  13.2 5.1 %collective-permute-start.4 = (bf16[224,128]{1,0:T(8,128)(2,1)S(1)}, bf16[224,128]{1,0:T(8,128)(2,1)S(1)}, u32[]{:S(2)}, u32[]{:S(2)}) collective-permute-start(bf16[224,128]{1,0:T(8,128)(2,1)S(1)} %get-tuple-element.27), channel_id=1, source_target_pairs={{0,2},{1,3},{2,0},{3,1},{4,6},{5,7},{6,4},{7,5},{8,10},{9,11},{10,... | collective-permute-start | bytes 172040 | tf_op jit(solution)/shard_map/ppermute | solution.py:26
  14.4 3.8 %collective-permute-start.5 = (bf16[224,128]{1,0:T(8,128)(2,1)S(1)}, bf16[224,128]{1,0:T(8,128)(2,1)S(1)}, u32[]{:S(2)}, u32[]{:S(2)}) collective-permute-start(bf16[224,128]{1,0:T(8,128)(2,1)S(1)} %get-tuple-element.28), channel_id=1, source_target_pairs={{0,1},{1,0},{2,3},{3,2},{4,5},{5,4},{6,7},{7,6},{8,9},{9,8},{10,11... | collective-permute-start | bytes 172040 | tf_op jit(solution)/shard_map/ppermute | solution.py:26

commit v6 on v5

--- a/solution.py
+++ b/solution.py
@@ -85,19 +85,49 @@
     )(*in_hbm(down, up))
 
 
-def front_kernel(
+def project_kernel(tokens_ref, weight_ref, own_ref, *base_refs):
+    shard = lax.axis_index("tensor")
+    rows, own = own_ref.shape
+    for i in reversed(range(1 + len(base_refs))):
+        first = pl.multiple_of((shard ^ i) * own, lanes)
+        block = jnp.dot(
+            tokens_ref[...], weight_ref[:, pl.ds(first, own)], preferred_element_type=f32
+        )
+        if i == 0:
+            own_ref[...] = block
+            continue
+        for c in range(own // lanes):
+            base_refs[i - 1][c * rows : (c + 1) * rows, :] = block[
+                :, c * lanes : (c + 1) * lanes
+            ].astype(bf16)
+
+
+def project(tokens, weight, shards):
+    rows, depth = tokens.shape
+    own = weight.shape[1] // shards
+    mine, *base = pl.pallas_call(
+        project_kernel,
+        out_shape=[jax.ShapeDtypeStruct((rows, own), f32)]
+        + [jax.ShapeDtypeStruct((rows * own // lanes, lanes), bf16)] * (shards - 1),
+        in_specs=[whole_in_vmem] * 2,
+        out_specs=[whole_in_vmem] * shards,
+        compiler_params=pltpu.CompilerParams(vmem_limit_bytes=4 * 2**20),
+        name="project",
+        cost_estimate=pl.CostEstimate(
+            flops=2 * rows * weight.size, bytes_accessed=2 * weight.size, transcendentals=0
+        ),
+    )(tokens, weight)
+    return mine, base
+
+
+def attend_kernel(
     step_count,
-    row_count,
     head_count,
-    shards,
     lengths_hbm,
-    tokens_ref,
     queries_ref,
-    weight_ref,
     keys_ref,
     values_ref,
-    own_ref,
-    base_ref,
+    _,
     grouped_ref,
     total_ref,
     peak_ref,
@@ -112,25 +142,11 @@
 ):
     lengths_copy = pltpu.make_async_copy(lengths_hbm, lengths_ref, length_sem)
     lengths_copy.start()
-    shard = lax.axis_index("tensor")
-    rows, own = own_ref.shape
-    slots = keys_ref.shape[1]
+    row_count, slots, _ = keys_ref.shape
+    rows = step_count * row_count
     group = queries_ref.shape[1] // (head_count * lanes)
     seen = step_count * group
     scale = lanes**-0.5
-
-    def product(i):
-        first = pl.multiple_of((shard ^ i) * own, lanes)
-        block = jnp.dot(
-            tokens_ref[...], weight_ref[:, pl.ds(first, own)], preferred_element_type=f32
-        )
-        if i == 0:
-            own_ref[...] = block
-            return
-        for c in range(own // lanes):
-            base_ref[i - 1, c * rows : (c + 1) * rows, :] = block[
-                :, c * lanes : (c + 1) * lanes
-            ].astype(bf16)
 
     for pair in range(step_count // 2):
         for q in range(head_count * group):
@@ -149,7 +165,7 @@
         at = (h * row_count + b) * seen
         return slice(at, at + seen)
 
-    def score_row(b):
+    for b in range(row_count):
         for h in range(head_count):
             scores[place(h, b), :] = lax.dot_general(
                 grouped_ref[place(h, b), :],
@@ -157,10 +173,9 @@
                 (((1,), (1,)), ((), ())),
                 preferred_element_type=f32,
             )
-
+    lengths_copy.wait()
     slot = lax.broadcasted_iota(jnp.int32, (seen, slots), 1)
-
-    def lift_row(b):
+    for b in range(row_count):
         live = slot < lengths_ref[b]
         for h in range(head_count):
             score = jnp.where(live, scores[place(h, b), :] * scale, masked_score)
@@ -171,26 +186,13 @@
             sum_ref[place(h, b), :] = jnp.broadcast_to(
                 jnp.sum(lifted, axis=1, keepdims=True), (seen, lanes)
             )
-
-    def weigh_row(b):
+    for b in range(row_count):
         for h in range(head_count):
             total_ref[place(h, b), :] = jnp.dot(
                 raised[place(h, b), :],
                 values_ref[b, :, h * lanes : (h + 1) * lanes],
                 preferred_element_type=f32,
             )
-
-    for b in range(row_count):
-        score_row(b)
-    lengths_copy.wait()
-    for b in range(row_count):
-        lift_row(b)
-        if b < shards:
-            product(b)
-    for i in range(row_count, shards):
-        product(i)
-    for b in range(row_count):
-        weigh_row(b)
 
     row = lax.broadcasted_iota(jnp.int32, (rows, lanes), 0)
     lane = lax.broadcasted_iota(jnp.int32, (rows, lanes), 1)
@@ -204,20 +206,16 @@
     sine = jnp.sin(angles)
     sine_ref[...] = jnp.where(lane < middle, -sine, sine)
 
-def front(lengths, tokens, queries, weight, keys, values, step_count, shards):
+
+def attend(lengths, queries, keys, values, after, step_count):
     row_count, slots, width = keys.shape
-    head_count = width // lanes
-    depth, columns = weight.shape
-    own = columns // shards
     rows = step_count * row_count
     seen_rows = rows * queries.shape[1] // lanes
     table = jax.ShapeDtypeStruct((rows, lanes), f32)
     seen_table = jax.ShapeDtypeStruct((seen_rows, lanes), f32)
     return pl.pallas_call(
-        functools.partial(front_kernel, step_count, row_count, head_count, shards),
+        functools.partial(attend_kernel, step_count, width // lanes),
         out_shape=(
-            jax.ShapeDtypeStruct((rows, own), f32),
-            jax.ShapeDtypeStruct((shards - 1, rows * own // lanes, lanes), bf16),
             jax.ShapeDtypeStruct((seen_rows, lanes), bf16),
             seen_table,
             seen_table,
@@ -225,8 +223,8 @@
             table,
             table,
         ),
-        in_specs=[stays_in_hbm] + [whole_in_vmem] * 5,
-        out_specs=(whole_in_vmem,) * 8,
+        in_specs=[stays_in_hbm] + [whole_in_vmem] * 4,
+        out_specs=(whole_in_vmem,) * 6,
         scratch_shapes=[
             pltpu.SMEM(lengths.shape, jnp.int32),
             pltpu.VMEM((seen_rows, lanes), f32),
@@ -235,20 +233,34 @@
             pltpu.SemaphoreType.DMA,
         ],
         compiler_params=pltpu.CompilerParams(vmem_limit_bytes=8 * 2**20),
-        name="front",
+        name="attend",
         cost_estimate=pl.CostEstimate(
-            flops=2 * rows * depth * columns + 4 * seen_rows * slots * lanes,
-            bytes_accessed=2 * (weight.size + keys.size + values.size),
+            flops=4 * seen_rows * slots * lanes,
+            bytes_accessed=2 * (keys.size + values.size),
             transcendentals=seen_rows * slots,
         ),
-    )(*in_hbm(lengths), tokens, queries, weight, keys, values)
+    )(*in_hbm(lengths), queries, keys, values, after)
+
+
+def add_far(mine, far):
+    rows = mine.shape[0]
+    blocks = []
+    for c in range(mine.shape[1] // lanes):
+        block = mine[:, c * lanes : (c + 1) * lanes]
+        for sent in far:
+            block = block + sent[c * rows : (c + 1) * rows, :].astype(f32)
+        blocks.append(block)
+    return jnp.concatenate(blocks, axis=1)
 
 
 def route_kernel(replicas, shards, *refs):
-    owners_ref, tokens_ref, base_ref = refs[:3]
-    piece_refs = refs[3 : 3 + replicas][::-1]
-    out_refs = refs[3 + replicas : 3 + replicas + shards]
-    token_buf, left, right, up_buf = refs[3 + replicas + shards :]
+    owners_ref, tokens_ref, mine_ref, base_ref = refs[:4]
+    piece_refs = refs[4 : 4 + replicas]
+    far_refs = refs[4 + replicas : 2 + replicas + shards][::-1]
+    sum_ref = refs[2 + replicas + shards]
+    out_refs = refs[3 + replicas + shards : 3 + replicas + 2 * shards]
+    token_buf, left, right, up_buf = refs[3 + replicas + 2 * shards :]
+    sum_ref[...] = add_far(mine_ref[...], far_refs)
     replica = lax.axis_index("rollout")
     shard = lax.axis_index("tensor")
     rows, depth = tokens_ref.shape
@@ -286,27 +298,27 @@
     both = jnp.concatenate(split_halves(lowered), axis=1)
     for i in range(shards):
         first = 0
-        if i:
-            first = base_ref.shape[1]
-            out_refs[i][:first, :] = base_ref[i - 1]
+        if i == 1:
+            first = base_ref.shape[0]
+            out_refs[i][:first, :] = base_ref[...]
         out_refs[i][first : first + rows, :] = both
         out_refs[i][first + rows :, :] = up_buf[owners_ref[shard ^ i] ^ replica]
 
 
-def route(owners, tokens, base, pieces, rank, up_rows):
+def route(owners, tokens, mine, near, far, pieces, rank, up_rows, shards):
     rows, depth = tokens.shape
-    shards = base.shape[0] + 1
     replicas = len(pieces)
-    sent = base.shape[1]
+    sent = near.shape[0]
     width = -(-depth // replicas // lanes) * lanes
-    return pl.pallas_call(
+    mine, *packets = pl.pallas_call(
         functools.partial(route_kernel, replicas, shards),
-        out_shape=[
-            jax.ShapeDtypeStruct(((sent if i else 0) + rows + up_rows, lanes), bf16)
+        out_shape=[jax.ShapeDtypeStruct(mine.shape, f32)]
+        + [
+            jax.ShapeDtypeStruct(((sent if i == 1 else 0) + rows + up_rows, lanes), bf16)
             for i in range(shards)
         ],
-        in_specs=[whole_in_smem] + [whole_in_vmem] * (2 + replicas),
-        out_specs=[whole_in_vmem] * shards,
+        in_specs=[whole_in_smem] + [whole_in_vmem] * (1 + replicas + shards),
+        out_specs=[whole_in_vmem] * (1 + shards),
         scratch_shapes=[
             pltpu.VMEM((replicas, rows, width), bf16),
             pltpu.VMEM((rows, replicas * width), bf16),
@@ -316,11 +328,11 @@
         compiler_params=pltpu.CompilerParams(vmem_limit_bytes=4 * 2**20),
         name="route",
         cost_estimate=pl.CostEstimate(flops=0, bytes_accessed=800000, transcendentals=0),
-    )(owners, tokens, base, *pieces[::-1])
-
-
-def route_plain(owners, tokens, base, down, up, rank_part, own):
-    shards = base.shape[0] + 1
+    )(owners, tokens, mine, near, *pieces, *far[::-1])
+    return mine, packets
+
+
+def route_plain(owners, tokens, near, down, up, rank_part, own, shards):
     rank = down.shape[1]
     shard = lax.axis_index("tensor")
     first = shard * rank_part
@@ -336,8 +348,8 @@
     for i in range(shards):
         up_block = lax.dynamic_slice_in_dim(up_matrix, (shard ^ i) * own, own, axis=1)
         parts = [both, side_by_side(up_block)]
-        if i:
-            parts = [base[i - 1]] + parts
+        if i == 1:
+            parts = [near] + parts
         packets.append(jnp.concatenate(parts, axis=0))
     return packets
 
@@ -359,7 +371,7 @@
 
     lowered = jnp.zeros((rows, lanes), f32)
     for i in range(shards):
-        first = rows * blocks if i else 0
+        first = rows * blocks if i == 1 else 0
         lowered = lowered + packet_refs[i][first : first + rows, :].astype(f32)
         ups = packet_refs[i][first + rows :, :].astype(f32)
         at = pl.multiple_of((shard ^ i) * rank_part, rank_part)
@@ -376,8 +388,7 @@
     joined = []
     for c in range(blocks):
         block = own_ref[:, c * lanes : (c + 1) * lanes]
-        for i in range(1, shards):
-            block = block + packet_refs[i][c * rows : (c + 1) * rows, :].astype(f32)
+        block = block + packet_refs[1][c * rows : (c + 1) * rows, :].astype(f32)
         joined.append(block + adapter_scale * raised_up[:, c * lanes : (c + 1) * lanes])
 
     all_rows = row_count * seen
@@ -485,17 +496,21 @@
         packed = pack(adapter_down.T, adapter_up, rank_part, beside)
         arrived = {i: swap(packed, "rollout", i) for i in reversed(range(1, replicas))}
         pieces = [packed] + [arrived[i] for i in range(1, replicas)]
-    mine, base, *partials = front(
-        lengths, tokens, query_rows, key_value_weight, cache_keys, stored_values, step_count, shards
-    )
+    mine, base = project(tokens, key_value_weight, shards)
+    far = [swap(base[i - 1], "tensor", i) for i in range(2, shards)]
     if fits:
-        packets = route(owners, tokens, base, pieces, rank, rank_part * own // lanes)
+        mine, packets = route(
+            owners, tokens, mine, base[0], far, pieces, rank, rank_part * own // lanes, shards
+        )
     else:
-        packets = route_plain(owners, tokens, base, adapter_down, adapter_up, rank_part, own)
-    arrived = {i: swap(packets[i], "tensor", i) for i in reversed(range(1, shards))}
-    packets = [packets[0]] + [arrived[i] for i in range(1, shards)]
+        packets = route_plain(
+            owners, tokens, base[0], adapter_down, adapter_up, rank_part, own, shards
+        )
+        mine = add_far(mine, far)
+    partials = attend(lengths, query_rows, cache_keys, stored_values, packets[0], step_count)
+    packets = [packets[0]] + [swap(packets[i], "tensor", i) for i in range(1, shards)]
     attention, keys, values = finish(
-        [mine] + partials,
+        [mine] + list(partials),
         key_gain.reshape(1, -1),
         packets,
         rank,

time: 20.1 us -> 20.9 us (1.040)
  starting transfers between devices: 7.64 us -> 9.62 us
  waiting for transfers between devices: 5.07 us -> 3.64 us
  Pallas kernels: 6.35 us -> 6.67 us
    ppermute x6 -> x8, starting transfers between devices: 7.64 us -> 9.62 us  [swap(): return lax.ppermute(block, axis, [(s, s ^ offset) for s in range(count)])]
    ppermute x6 -> x8, waiting for transfers between devices: 5.07 us -> 3.64 us  [swap(): return lax.ppermute(block, axis, [(s, s ^ offset) for s in range(count)])]
    pallas_call x1 -> x2, Pallas kernels: 2.84 us -> 3.15 us  [the longest x1 2.15 us: attend(): pl.pallas_call(functools.partial(attend_kernel, step_count, width // lane...]
  transfers between devices with their start and end apart: 6 -> 8, of which waited for: 3 -> 3; matrix products, arithmetic and copies ran while one was open for 0% -> 0% of each run, Pallas kernels for 14% -> 15%
where the time goes in v6:
time: 20.9 us; the launch traced here: 20.7 us
  starting transfers between devices  9.62 us (46%)
  Pallas kernels  6.67 us (32%)
  waiting for transfers between devices  3.64 us (17%)
  between operations  0.74 us (4%)
    ppermute x8, starting transfers between devices, swap(): return lax.ppermute(block, axis, [(s, s ^ offset) for s in range(count)])  9.62 us
    ppermute x8, waiting for transfers between devices, swap(): return lax.ppermute(block, axis, [(s, s ^ offset) for s in range(count)])  3.64 us
    pallas_call x1, Pallas kernels, attend(): pl.pallas_call(functools.partial(attend_kernel, step_count, width // lane...  2.15 us
    pallas_call x1, Pallas kernels, finish(): pl.pallas_call(functools.partial(finish_kernel, step_count, row_count, he...  1.59 us
    pallas_call x1, Pallas kernels, pack(): pl.pallas_call(pack_kernel, out_shape=jax.ShapeDtypeStruct((rows, lanes),...  1.05 us
    pallas_call x1, Pallas kernels, project(): pl.pallas_call(project_kernel, out_shape=[jax.ShapeDtypeStruct((rows, own...  1 us
    pallas_call x1, Pallas kernels, route(): pl.pallas_call(functools.partial(route_kernel, replicas, shards), out_sha...  0.88 us
  transfers between devices with their start and end apart: 8, of which 3 were waited for; matrix products, arithmetic and copies ran while one was open for 0% of the time, Pallas kernels for 15%

profile of v6, /device:TPU:0, one launch (start us, length us, event | category | flops | bytes accessed | tf_op | source)
XLA Modules:
  0.0 20.7 jit_solution(15503775558763227345)
XLA Ops:
  0.6 0.0 slice-start
  0.6 0.0 slice-start.1
  0.7 0.0 copy-start.2
  0.7 1.0 %pack.1.refs_4_ = bf16[224,128]{1,0:T(8,128)(2,1)S(1)} custom-call(bf16[64,320]{1,0:T(8,128)(2,1)} %bitcast.14, bf16[64,512]{1,0:T(8,128)(2,1)} %up_hbm.1), custom_call_target="tpu_custom_call" | custom-call | flops 9437184000 | bytes 9437184 | tf_op jit(solution)/shard_map/pack/pallas_call | solution.py:72
  1.7 5.1 %collective-permute-start.2 = (bf16[224,128]{1,0:T(8,128)(2,1)S(1)}, bf16[224,128]{1,0:T(8,128)(2,1)S(1)}, u32[]{:S(2)}, u32[]{:S(2)}) collective-permute-start(bf16[224,128]{1,0:T(8,128)(2,1)S(1)} %pack.1.refs_4_), channel_id=1, source_target_pairs={{0,12},{4,8},{8,4},{12,0},{1,13},{5,9},{9,5},{13,1},{2,14},{6,10},... | collective-permute-start | bytes 172040 | tf_op jit(solution)/shard_map/ppermute | solution.py:26
  6.8 0.0 collective-permute-start.1
  6.8 0.6 %collective-permute-start = (bf16[224,128]{1,0:T(8,128)(2,1)S(1)}, bf16[224,128]{1,0:T(8,128)(2,1)S(1)}, u32[]{:S(2)}, u32[]{:S(2)}) collective-permute-start(bf16[224,128]{1,0:T(8,128)(2,1)S(1)} %pack.1.refs_4_), channel_id=1, source_target_pairs={{0,4},{4,0},{8,12},{12,8},{1,5},{5,1},{9,13},{13,9},{2,6},{6,2},{1... | collective-permute-start | bytes 172040 | tf_op jit(solution)/shard_map/ppermute | solution.py:26
  7.5 0.0 slice-done
  7.5 0.0 slice-done.1
  7.5 0.0 copy-done.2
  7.5 0.0 copy-start.4
  7.5 0.0 copy-start
  7.5 0.0 copy-start.1
  7.5 0.0 copy-start.3
  7.5 1.0 %project.1 = (f32[32,512]{1,0:T(8,128)S(1)}, bf16[128,128]{1,0:T(8,128)(2,1)S(1)}, bf16[128,128]{1,0:T(8,128)(2,1)S(1)}, bf16[128,128]{1,0:T(8,128)(2,1)S(1)}) custom-call(bf16[32,1280]{1,0:T(8,128)(2,1)S(1)} %bitcast.9, bf16[1280,2048]{1,0:T(8,128)(2,1)S(1)} %bitcast.8), custom_call_target="tpu_custom_call" | custom-call | flops 167772160 | bytes 5242880 | tf_op jit(solution)/shard_map/project/pallas_call | solution.py:108
  8.5 0.4 %collective-permute-start.3 = (bf16[128,128]{1,0:T(8,128)(2,1)S(1)}, bf16[128,128]{1,0:T(8,128)(2,1)S(1)}, u32[]{:S(2)}, u32[]{:S(2)}) collective-permute-start(bf16[128,128]{1,0:T(8,128)(2,1)S(1)} %get-tuple-element.23), channel_id=1, source_target_pairs={{0,3},{1,2},{2,1},{3,0},{4,7},{5,6},{6,5},{7,4},{8,11},{9,10},{10,... | collective-permute-start | bytes 98312 | tf_op jit(solution)/shard_map/ppermute | solution.py:26
  8.9 1.3 %collective-permute-start.4 = (bf16[128,128]{1,0:T(8,128)(2,1)S(1)}, bf16[128,128]{1,0:T(8,128)(2,1)S(1)}, u32[]{:S(2)}, u32[]{:S(2)}) collective-permute-start(bf16[128,128]{1,0:T(8,128)(2,1)S(1)} %get-tuple-element.24), channel_id=1, source_target_pairs={{0,2},{1,3},{2,0},{3,1},{4,6},{5,7},{6,4},{7,5},{8,10},{9,11},{10,... | collective-permute-start | bytes 98312 | tf_op jit(solution)/shard_map/ppermute | solution.py:26
  10.2 1.8 %collective-permute-done.3.refs_8_ = bf16[128,128]{1,0:T(8,128)(2,1)S(1)} collective-permute-done((bf16[128,128]{1,0:T(8,128)(2,1)S(1)}, bf16[128,128]{1,0:T(8,128)(2,1)S(1)}, u32[]{:S(2)}, u32[]{:S(2)}) %collective-permute-start.3) | collective-permute-done | bytes 32800 | tf_op jit(solution)/shard_map/ppermute | solution.py:26
  12.1 0.8 %collective-permute-done.4.refs_9_ = bf16[128,128]{1,0:T(8,128)(2,1)S(1)} collective-permute-done((bf16[128,128]{1,0:T(8,128)(2,1)S(1)}, bf16[128,128]{1,0:T(8,128)(2,1)S(1)}, u32[]{:S(2)}, u32[]{:S(2)}) %collective-permute-start.4) | collective-permute-done | bytes 32800 | tf_op jit(solution)/shard_map/ppermute | solution.py:26
  12.8 0.0 collective-permute-done.2.refs_7_
  12.8 0.0 collective-permute-done.1.refs_6_
  12.9 0.0 collective-permute-done.refs_5_
  12.9 0.0 copy-done.4
  12.9 0.9 %route.1 = (f32[32,512]{1,0:T(8,128)S(1)}, bf16[96,128]{1,0:T(8,128)(2,1)S(1)}, bf16[224,128]{1,0:T(8,128)(2,1)S(1)}, bf16[96,128]{1,0:T(8,128)(2,1)S(1)}, bf16[96,128]{1,0:T(8,128)(2,1)S(1)}) custom-call(s32[4]{0:T(128)S(1)} %copy-done.4, bf16[32,1280]{1,0:T(8,128)(2,1)S(1)} %bitcast.10, f32[32,512]{1,0:T(8,128)S(1)} %get-tuple-element.21.refs_2_, ...), custom_call_target="tpu_custom_call" | custom-call | bytes 800000 | tf_op jit(solution)/shard_map/route/pallas_call | solution.py:313
  13.7 0.3 %collective-permute-start.7 = (bf16[224,128]{1,0:T(8,128)(2,1)S(1)}, bf16[224,128]{1,0:T(8,128)(2,1)S(1)}, u32[]{:S(2)}, u32[]{:S(2)}) collective-permute-start(bf16[224,128]{1,0:T(8,128)(2,1)S(1)} %get-tuple-element.35), channel_id=1, source_target_pairs={{0,1},{1,0},{2,3},{3,2},{4,5},{5,4},{6,7},{7,6},{8,9},{9,8},{10,11... | collective-permute-start | bytes 172040 | tf_op jit(solution)/shard_map/ppermute | solution.py:26
  14.0 1.3 %collective-permute-start.5 = (bf16[96,128]{1,0:T(8,128)(2,1)S(1)}, bf16[96,128]{1,0:T(8,128)(2,1)S(1)}, u32[]{:S(2)}, u32[]{:S(2)}) collective-permute-start(bf16[96,128]{1,0:T(8,128)(2,1)S(1)} %get-tuple-element.33), channel_id=1, source_target_pairs={{0,3},{1,2},{2,1},{3,0},{4,7},{5,6},{6,5},{7,4},{8,11},{9,10},{10,... | collective-permute-start | bytes 73736 | tf_op jit(solution)/shard_map/ppermute | solution.py:26
  15.3 0.6 %collective-permute-start.6 = (bf16[96,128]{1,0:T(8,128)(2,1)S(1)}, bf16[96,128]{1,0:T(8,128)(2,1)S(1)}, u32[]{:S(2)}, u32[]{:S(2)}) collective-permute-start(bf16[96,128]{1,0:T(8,128)(2,1)S(1)} %get-tuple-element.34), channel_id=1, source_target_pairs={{0,2},{1,3},{2,0},{3,1},{4,6},{5,7},{6,4},{7,5},{8,10},{9,11},{10,... | collective-permute-start | bytes 73736 | tf_op jit(solution)/shard_map/ppermute | solution.py:26
  15.9 0.0 copy-done
  15.9 0.0 copy-done.1
  15.9 0.0 copy-done.3
  15.9 0.0 copy-start.5
  15.9 2.1 %attend.1 = (bf16[512,128]{1,0:T(8,128)(2,1)S(1)}, f32[512,128]{1,0:T(8,128)S(1)}, f32[512,128]{1,0:T(8,128)S(1)}, f32[512,128]{1,0:T(8,128)S(1)}, f32[32,128]{1,0:T(8,128)S(1)}, /*index=5*/f32[32,128]{1,0:T(8,128)S(1)}) custom-call(s32[8]{0:T(128)} %lengths_hbm.1, bf16[32,2048]{1,0:T(8,128)(2,1)S(1)} %bitcast.11, bf16[8,512,256]{2,1,0:T(8,128)(2,1)S(1)} %copy-done, ...), custom_call_target="tpu_custom_call" | custom-call | flops 134217728 | bytes 4194304 | tf_op jit(solution)/shard_map/attend/pallas_call | solution.py:216
  18.1 0.0 collective-permute-done.5.refs_8_
  18.1 1.0 %collective-permute-done.6.refs_9_ = bf16[96,128]{1,0:T(8,128)(2,1)S(1)} collective-permute-done((bf16[96,128]{1,0:T(8,128)(2,1)S(1)}, bf16[96,128]{1,0:T(8,128)(2,1)S(1)}, u32[]{:S(2)}, u32[]{:S(2)}) %collective-permute-start.6) | collective-permute-done | bytes 24608 | tf_op jit(solution)/shard_map/ppermute | solution.py:26
  19.1 0.0 collective-permute-done.7.refs_10_
  19.1 0.0 copy-done.5
  19.1 1.6 %finish.1 = (bf16[32,2048]{1,0:T(8,128)(2,1)}, bf16[32,256]{1,0:T(8,128)(2,1)}, bf16[32,256]{1,0:T(8,128)(2,1)}) custom-call(f32[32,512]{1,0:T(8,128)S(1)} %get-tuple-element.25.refs_0_, f32[1,128]{1,0:T(1,128)S(1)} %bitcast.12, bf16[512,128]{1,0:T(8,128)(2,1)S(1)} %get-tuple-element.27.refs_2_, f32[512,128]{1,0:T(8,128)S(1)} %get-tuple-element.28.refs_3_, ...), custom_call_target="tpu_custom_call" | custom-call | bytes 1000000 | tf_op jit(solution)/shard_map/finish/pallas_call | solution.py:445
  (1 shorter events, 0.0 us)
Async XLA Ops:
  0.6 6.8 %slice-start = ((s8[5242880]{0:T(1024)(128)(4,1)}), s8[4194304]{0:T(1024)(128)(4,1)S(1)}, s32[]{:S(2)}) async-start(s8[5242880]{0:T(1024)(128)(4,1)} %bitcast.7), calls=%async_computation | async-start | bytes 8388608
  0.6 6.8 %slice-start.1 = ((s8[5242880]{0:T(1024)(128)(4,1)}), s8[1048576]{0:T(1024)(128)(4,1)S(1)}, s32[]{:S(2)}) async-start(s8[5242880]{0:T(1024)(128)(4,1)} %bitcast.7), calls=%async_computation.1 | async-start | bytes 2097152
  0.7 6.8 %copy-start.2 = (bf16[4,8,1280]{2,1,0:T(8,128)(2,1)S(1)}, bf16[4,8,1280]{2,1,0:T(8,128)(2,1)}, u32[]{:S(2)}) copy-start(bf16[4,8,1280]{2,1,0:T(8,128)(2,1)} %param.10) | copy-start | bytes 245764
  1.7 11.1 %collective-permute-start.2 = (bf16[224,128]{1,0:T(8,128)(2,1)S(1)}, bf16[224,128]{1,0:T(8,128)(2,1)S(1)}, u32[]{:S(2)}, u32[]{:S(2)}) collective-permute-start(bf16[224,128]{1,0:T(8,128)(2,1)S(1)} %pack.1.refs_4_), channel_id=1, source_target_pairs={{0,12},{4,8},{8,4},{12,0},{1,13},{5,9},{9,5},{13,1},{2,14},{6,10},... | collective-permute-start | bytes 172040 | tf_op jit(solution)/shard_map/ppermute | solution.py:26
  6.8 6.0 %collective-permute-start.1 = (bf16[224,128]{1,0:T(8,128)(2,1)S(1)}, bf16[224,128]{1,0:T(8,128)(2,1)S(1)}, u32[]{:S(2)}, u32[]{:S(2)}) collective-permute-start(bf16[224,128]{1,0:T(8,128)(2,1)S(1)} %pack.1.refs_4_), channel_id=1, source_target_pairs={{0,8},{4,12},{8,0},{12,4},{1,9},{5,13},{9,1},{13,5},{2,10},{6,14},... | collective-permute-start | bytes 172040 | tf_op jit(solution)/shard_map/ppermute | solution.py:26
  6.8 6.0 %collective-permute-start = (bf16[224,128]{1,0:T(8,128)(2,1)S(1)}, bf16[224,128]{1,0:T(8,128)(2,1)S(1)}, u32[]{:S(2)}, u32[]{:S(2)}) collective-permute-start(bf16[224,128]{1,0:T(8,128)(2,1)S(1)} %pack.1.refs_4_), channel_id=1, source_target_pairs={{0,4},{4,0},{8,12},{12,8},{1,5},{5,1},{9,13},{13,9},{2,6},{6,2},{1... | collective-permute-start | bytes 172040 | tf_op jit(solution)/shard_map/ppermute | solution.py:26
  7.5 5.4 %copy-start.4 = (s32[4]{0:T(128)S(1)}, s32[4]{0:T(128)}, u32[]{:S(2)}) copy-start(s32[4]{0:T(128)} %refs_0_.1) | copy-start | bytes 52
  7.5 8.4 %copy-start = (bf16[8,512,256]{2,1,0:T(8,128)(2,1)S(1)}, bf16[8,512,256]{2,1,0:T(8,128)(2,1)}, u32[]{:S(2)}) copy-start(bf16[8,512,256]{2,1,0:T(8,128)(2,1)} %keys_ref.1) | copy-start | bytes 6291460
  7.5 8.4 %copy-start.1 = (bf16[8,512,256]{2,1,0:T(8,128)(2,1)S(1)}, bf16[8,512,256]{2,1,0:T(8,128)(2,1)}, u32[]{:S(2)}) copy-start(bf16[8,512,256]{2,1,0:T(8,128)(2,1)} %values_ref.1) | copy-start | bytes 6291460
  7.5 8.4 %copy-start.3 = (bf16[4,8,2048]{2,1,0:T(8,128)(2,1)S(1)}, bf16[4,8,2048]{2,1,0:T(8,128)(2,1)}, u32[]{:S(2)}) copy-start(bf16[4,8,2048]{2,1,0:T(8,128)(2,1)} %param.15) | copy-start | bytes 393220
  8.5 3.5 %collective-permute-start.3 = (bf16[128,128]{1,0:T(8,128)(2,1)S(1)}, bf16[128,128]{1,0:T(8,128)(2,1)S(1)}, u32[]{:S(2)}, u32[]{:S(2)}) collective-permute-start(bf16[128,128]{1,0:T(8,128)(2,1)S(1)} %get-tuple-element.23), channel_id=1, source_target_pairs={{0,3},{1,2},{2,1},{3,0},{4,7},{5,6},{6,5},{7,4},{8,11},{9,10},{10,... | collective-permute-start | bytes 98312 | tf_op jit(solution)/shard_map/ppermute | solution.py:26
  8.9 3.9 %collective-permute-start.4 = (bf16[128,128]{1,0:T(8,128)(2,1)S(1)}, bf16[128,128]{1,0:T(8,128)(2,1)S(1)}, u32[]{:S(2)}, u32[]{:S(2)}) collective-permute-start(bf16[128,128]{1,0:T(8,128)(2,1)S(1)} %get-tuple-element.24), channel_id=1, source_target_pairs={{0,2},{1,3},{2,0},{3,1},{4,6},{5,7},{6,4},{7,5},{8,10},{9,11},{10,... | collective-permute-start | bytes 98312 | tf_op jit(solution)/shard_map/ppermute | solution.py:26
  13.7 5.4 %collective-permute-start.7 = (bf16[224,128]{1,0:T(8,128)(2,1)S(1)}, bf16[224,128]{1,0:T(8,128)(2,1)S(1)}, u32[]{:S(2)}, u32[]{:S(2)}) collective-permute-start(bf16[224,128]{1,0:T(8,128)(2,1)S(1)} %get-tuple-element.35), channel_id=1, source_target_pairs={{0,1},{1,0},{2,3},{3,2},{4,5},{5,4},{6,7},{7,6},{8,9},{9,8},{10,11... | collective-permute-start | bytes 172040 | tf_op jit(solution)/shard_map/ppermute | solution.py:26
  14.0 4.1 %collective-permute-start.5 = (bf16[96,128]{1,0:T(8,128)(2,1)S(1)}, bf16[96,128]{1,0:T(8,128)(2,1)S(1)}, u32[]{:S(2)}, u32[]{:S(2)}) collective-permute-start(bf16[96,128]{1,0:T(8,128)(2,1)S(1)} %get-tuple-element.33), channel_id=1, source_target_pairs={{0,3},{1,2},{2,1},{3,0},{4,7},{5,6},{6,5},{7,4},{8,11},{9,10},{10,... | collective-permute-start | bytes 73736 | tf_op jit(solution)/shard_map/ppermute | solution.py:26
  15.3 3.8 %collective-permute-start.6 = (bf16[96,128]{1,0:T(8,128)(2,1)S(1)}, bf16[96,128]{1,0:T(8,128)(2,1)S(1)}, u32[]{:S(2)}, u32[]{:S(2)}) collective-permute-start(bf16[96,128]{1,0:T(8,128)(2,1)S(1)} %get-tuple-element.34), channel_id=1, source_target_pairs={{0,2},{1,3},{2,0},{3,1},{4,6},{5,7},{6,4},{7,5},{8,10},{9,11},{10,... | collective-permute-start | bytes 73736 | tf_op jit(solution)/shard_map/ppermute | solution.py:26
  15.9 3.2 %copy-start.5 = (f32[128]{0:T(128)S(1)}, f32[128]{0:T(128)}, u32[]{:S(2)}) copy-start(f32[128]{0:T(128)} %param.14) | copy-start | bytes 1540

commit v7 on v6

--- a/solution.py
+++ b/solution.py
@@ -85,39 +85,48 @@
     )(*in_hbm(down, up))
 
 
-def project_kernel(tokens_ref, weight_ref, own_ref, *base_refs):
+def project_kernel(tokens_ref, weight_ref, _, own_ref, first_ref, near_ref, kept_ref):
     shard = lax.axis_index("tensor")
-    rows, own = own_ref.shape
-    for i in reversed(range(1 + len(base_refs))):
+    pairs, rows, own = kept_ref.shape
+
+    def product(i):
         first = pl.multiple_of((shard ^ i) * own, lanes)
-        block = jnp.dot(
+        return jnp.dot(
             tokens_ref[...], weight_ref[:, pl.ds(first, own)], preferred_element_type=f32
         )
-        if i == 0:
-            own_ref[...] = block
-            continue
+
+    def put(block, ref):
         for c in range(own // lanes):
-            base_refs[i - 1][c * rows : (c + 1) * rows, :] = block[
-                :, c * lanes : (c + 1) * lanes
-            ].astype(bf16)
-
-
-def project(tokens, weight, shards):
+            ref[c * rows : (c + 1) * rows, :] = block[:, c * lanes : (c + 1) * lanes].astype(bf16)
+
+    for m in range(pairs):
+        put(product(2 * m + 3), near_ref.at[m])
+        kept_ref[m] = product(2 * m + 2)
+    put(product(1), first_ref)
+    own_ref[...] = product(0)
+
+
+def project(tokens, weight, after, shards):
     rows, depth = tokens.shape
     own = weight.shape[1] // shards
-    mine, *base = pl.pallas_call(
+    pairs = shards // 2 - 1
+    sent = rows * own // lanes
+    return pl.pallas_call(
         project_kernel,
-        out_shape=[jax.ShapeDtypeStruct((rows, own), f32)]
-        + [jax.ShapeDtypeStruct((rows * own // lanes, lanes), bf16)] * (shards - 1),
-        in_specs=[whole_in_vmem] * 2,
-        out_specs=[whole_in_vmem] * shards,
+        out_shape=(
+            jax.ShapeDtypeStruct((rows, own), f32),
+            jax.ShapeDtypeStruct((sent, lanes), bf16),
+            jax.ShapeDtypeStruct((pairs, sent, lanes), bf16),
+            jax.ShapeDtypeStruct((pairs, rows, own), f32),
+        ),
+        in_specs=[whole_in_vmem] * 3,
+        out_specs=(whole_in_vmem,) * 4,
         compiler_params=pltpu.CompilerParams(vmem_limit_bytes=4 * 2**20),
         name="project",
         cost_estimate=pl.CostEstimate(
             flops=2 * rows * weight.size, bytes_accessed=2 * weight.size, transcendentals=0
         ),
-    )(tokens, weight)
-    return mine, base
+    )(tokens, weight, after)
 
 
 def attend_kernel(
@@ -242,25 +251,24 @@
     )(*in_hbm(lengths), queries, keys, values, after)
 
 
-def add_far(mine, far):
-    rows = mine.shape[0]
-    blocks = []
-    for c in range(mine.shape[1] // lanes):
-        block = mine[:, c * lanes : (c + 1) * lanes]
-        for sent in far:
-            block = block + sent[c * rows : (c + 1) * rows, :].astype(f32)
-        blocks.append(block)
-    return jnp.concatenate(blocks, axis=1)
+def add_near(kept, near):
+    rows, own = kept.shape
+    return [
+        kept[:, c * lanes : (c + 1) * lanes] + near[c * rows : (c + 1) * rows, :].astype(f32)
+        for c in range(own // lanes)
+    ]
+
+
+def carries_sums(i):
+    return i == 1 or (i > 0 and i % 2 == 0)
 
 
 def route_kernel(replicas, shards, *refs):
-    owners_ref, tokens_ref, mine_ref, base_ref = refs[:4]
+    owners_ref, tokens_ref, first_ref, kept_ref = refs[:4]
     piece_refs = refs[4 : 4 + replicas]
-    far_refs = refs[4 + replicas : 2 + replicas + shards][::-1]
-    sum_ref = refs[2 + replicas + shards]
-    out_refs = refs[3 + replicas + shards : 3 + replicas + 2 * shards]
-    token_buf, left, right, up_buf = refs[3 + replicas + 2 * shards :]
-    sum_ref[...] = add_far(mine_ref[...], far_refs)
+    near_ref = refs[4 + replicas]
+    out_refs = refs[5 + replicas : 5 + replicas + shards]
+    token_buf, left, right, up_buf = refs[5 + replicas + shards :]
     replica = lax.axis_index("rollout")
     shard = lax.axis_index("tensor")
     rows, depth = tokens_ref.shape
@@ -299,26 +307,30 @@
     for i in range(shards):
         first = 0
         if i == 1:
-            first = base_ref.shape[0]
-            out_refs[i][:first, :] = base_ref[...]
+            first = first_ref.shape[0]
+            out_refs[i][:first, :] = first_ref[...]
+        elif carries_sums(i):
+            for block in add_near(kept_ref[i // 2 - 1], near_ref[i // 2 - 1]):
+                out_refs[i][first : first + rows, :] = block.astype(bf16)
+                first += rows
         out_refs[i][first : first + rows, :] = both
         out_refs[i][first + rows :, :] = up_buf[owners_ref[shard ^ i] ^ replica]
 
 
-def route(owners, tokens, mine, near, far, pieces, rank, up_rows, shards):
+def route(owners, tokens, sums, pieces, rank, up_rows, shards):
     rows, depth = tokens.shape
     replicas = len(pieces)
-    sent = near.shape[0]
+    first, kept, near = sums
+    sent = first.shape[0]
     width = -(-depth // replicas // lanes) * lanes
-    mine, *packets = pl.pallas_call(
+    return pl.pallas_call(
         functools.partial(route_kernel, replicas, shards),
-        out_shape=[jax.ShapeDtypeStruct(mine.shape, f32)]
-        + [
-            jax.ShapeDtypeStruct(((sent if i == 1 else 0) + rows + up_rows, lanes), bf16)
+        out_shape=[
+            jax.ShapeDtypeStruct(((sent if carries_sums(i) else 0) + rows + up_rows, lanes), bf16)
             for i in range(shards)
         ],
-        in_specs=[whole_in_smem] + [whole_in_vmem] * (1 + replicas + shards),
-        out_specs=[whole_in_vmem] * (1 + shards),
+        in_specs=[whole_in_smem] + [whole_in_vmem] * (4 + replicas),
+        out_specs=[whole_in_vmem] * shards,
         scratch_shapes=[
             pltpu.VMEM((replicas, rows, width), bf16),
             pltpu.VMEM((rows, replicas * width), bf16),
@@ -328,11 +340,11 @@
         compiler_params=pltpu.CompilerParams(vmem_limit_bytes=4 * 2**20),
         name="route",
         cost_estimate=pl.CostEstimate(flops=0, bytes_accessed=800000, transcendentals=0),
-    )(owners, tokens, mine, near, *pieces, *far[::-1])
-    return mine, packets
-
-
-def route_plain(owners, tokens, near, down, up, rank_part, own, shards):
+    )(owners, tokens, first, kept, *pieces, near)
+
+
+def route_plain(owners, tokens, sums, down, up, rank_part, own, shards):
+    first_sent, kept, near = sums
     rank = down.shape[1]
     shard = lax.axis_index("tensor")
     first = shard * rank_part
@@ -349,7 +361,10 @@
         up_block = lax.dynamic_slice_in_dim(up_matrix, (shard ^ i) * own, own, axis=1)
         parts = [both, side_by_side(up_block)]
         if i == 1:
-            parts = [near] + parts
+            parts = [first_sent] + parts
+        elif carries_sums(i):
+            sums = add_near(kept[i // 2 - 1], near[i // 2 - 1])
+            parts = [jnp.concatenate(sums, axis=0).astype(bf16)] + parts
         packets.append(jnp.concatenate(parts, axis=0))
     return packets
 
@@ -371,7 +386,7 @@
 
     lowered = jnp.zeros((rows, lanes), f32)
     for i in range(shards):
-        first = rows * blocks if i == 1 else 0
+        first = rows * blocks if carries_sums(i) else 0
         lowered = lowered + packet_refs[i][first : first + rows, :].astype(f32)
         ups = packet_refs[i][first + rows :, :].astype(f32)
         at = pl.multiple_of((shard ^ i) * rank_part, rank_part)
@@ -388,7 +403,8 @@
     joined = []
     for c in range(blocks):
         block = own_ref[:, c * lanes : (c + 1) * lanes]
-        block = block + packet_refs[1][c * rows : (c + 1) * rows, :].astype(f32)
+        for i in filter(carries_sums, range(shards)):
+            block = block + packet_refs[i][c * rows : (c + 1) * rows, :].astype(f32)
         joined.append(block + adapter_scale * raised_up[:, c * lanes : (c + 1) * lanes])
 
     all_rows = row_count * seen
@@ -496,17 +512,16 @@
         packed = pack(adapter_down.T, adapter_up, rank_part, beside)
         arrived = {i: swap(packed, "rollout", i) for i in reversed(range(1, replicas))}
         pieces = [packed] + [arrived[i] for i in range(1, replicas)]
-    mine, base = project(tokens, key_value_weight, shards)
-    far = [swap(base[i - 1], "tensor", i) for i in range(2, shards)]
+    mine, first, near, kept = project(
+        tokens, key_value_weight, packed if fits else adapter_up, shards
+    )
+    sums = (first, kept, swap(near, "tensor", 1))
     if fits:
-        mine, packets = route(
-            owners, tokens, mine, base[0], far, pieces, rank, rank_part * own // lanes, shards
-        )
+        packets = route(owners, tokens, sums, pieces, rank, rank_part * own // lanes, shards)
     else:
         packets = route_plain(
-            owners, tokens, base[0], adapter_down, adapter_up, rank_part, own, shards
+            owners, tokens, sums, adapter_down, adapter_up, rank_part, own, shards
         )
-        mine = add_far(mine, far)
     partials = attend(lengths, query_rows, cache_keys, stored_values, packets[0], step_count)
     packets = [packets[0]] + [swap(packets[i], "tensor", i) for i in range(1, shards)]
     attention, keys, values = finish(

time: 20.9 us -> 19.5 us (0.933)
  starting transfers between devices: 9.62 us -> 7.92 us
    ppermute x8 -> x7, starting transfers between devices: 9.62 us -> 7.92 us  [swap(): return lax.ppermute(block, axis, [(s, s ^ offset) for s in range(count)])]
    ppermute x8 -> x7, waiting for transfers between devices: 3.64 us -> 3.75 us  [swap(): return lax.ppermute(block, axis, [(s, s ^ offset) for s in range(count)])]
  transfers between devices with their start and end apart: 8 -> 7, of which waited for: 3 -> 3; matrix products, arithmetic and copies ran while one was open for 0% -> 0% of each run, Pallas kernels for 15% -> 17%
where the time goes in v7:
time: 19.5 us; the launch traced here: 19.2 us
  starting transfers between devices  7.92 us (41%)
  Pallas kernels  6.75 us (35%)
  waiting for transfers between devices  3.75 us (19%)
  between operations  0.73 us (4%)
    ppermute x7, starting transfers between devices, swap(): return lax.ppermute(block, axis, [(s, s ^ offset) for s in range(count)])  7.92 us
    ppermute x7, waiting for transfers between devices, swap(): return lax.ppermute(block, axis, [(s, s ^ offset) for s in range(count)])  3.75 us
    pallas_call x1, Pallas kernels, attend(): pl.pallas_call(functools.partial(attend_kernel, step_count, width // lane...  2.23 us
    pallas_call x1, Pallas kernels, finish(): pl.pallas_call(functools.partial(finish_kernel, step_count, row_count, he...  1.59 us
    pallas_call x1, Pallas kernels, pack(): pl.pallas_call(pack_kernel, out_shape=jax.ShapeDtypeStruct((rows, lanes),...  1.05 us
    pallas_call x1, Pallas kernels, project(): pl.pallas_call(project_kernel, out_shape=(jax.ShapeDtypeStruct((rows, own...  1 us
    pallas_call x1, Pallas kernels, route(): pl.pallas_call(functools.partial(route_kernel, replicas, shards), out_sha...  0.88 us
  transfers between devices with their start and end apart: 7, of which 3 were waited for; matrix products, arithmetic and copies ran while one was open for 0% of the time, Pallas kernels for 17%

profile of v7, /device:TPU:0, one launch (start us, length us, event | category | flops | bytes accessed | tf_op | source)
XLA Modules:
  0.0 19.2 jit_solution(2798126787273979372)
XLA Ops:
  0.6 0.0 slice-start
  0.6 0.0 slice-start.1
  0.7 0.0 copy-start.2
  0.7 1.0 %pack.1._.refs_4_ = bf16[224,128]{1,0:T(8,128)(2,1)S(1)} custom-call(bf16[64,320]{1,0:T(8,128)(2,1)} %bitcast.14, bf16[64,512]{1,0:T(8,128)(2,1)} %up_hbm.1), custom_call_target="tpu_custom_call" | custom-call | flops 9437184000 | bytes 9437184 | tf_op jit(solution)/shard_map/pack/pallas_call | solution.py:72
  1.7 5.1 %collective-permute-start.2 = (bf16[224,128]{1,0:T(8,128)(2,1)S(1)}, bf16[224,128]{1,0:T(8,128)(2,1)S(1)}, u32[]{:S(2)}, u32[]{:S(2)}) collective-permute-start(bf16[224,128]{1,0:T(8,128)(2,1)S(1)} %pack.1._.refs_4_), channel_id=1, source_target_pairs={{0,12},{4,8},{8,4},{12,0},{1,13},{5,9},{9,5},{13,1},{2,14},{6,10},... | collective-permute-start | bytes 172040 | tf_op jit(solution)/shard_map/ppermute | solution.py:26
  6.8 0.0 collective-permute-start.1
  6.8 0.6 %collective-permute-start = (bf16[224,128]{1,0:T(8,128)(2,1)S(1)}, bf16[224,128]{1,0:T(8,128)(2,1)S(1)}, u32[]{:S(2)}, u32[]{:S(2)}) collective-permute-start(bf16[224,128]{1,0:T(8,128)(2,1)S(1)} %pack.1._.refs_4_), channel_id=1, source_target_pairs={{0,4},{4,0},{8,12},{12,8},{1,5},{5,1},{9,13},{13,9},{2,6},{6,2},{1... | collective-permute-start | bytes 172040 | tf_op jit(solution)/shard_map/ppermute | solution.py:26
  7.5 0.0 slice-done
  7.5 0.0 slice-done.1
  7.5 0.0 copy-done.2
  7.5 0.0 copy-start.5
  7.5 0.0 copy-start
  7.5 0.0 copy-start.1
  7.5 0.0 copy-start.3
  7.5 1.0 %project.1 = (f32[32,512]{1,0:T(8,128)S(1)}, bf16[128,128]{1,0:T(8,128)(2,1)S(1)}, bf16[1,128,128]{2,1,0:T(8,128)(2,1)S(1)}, f32[1,32,512]{2,1,0:T(8,128)S(1)}) custom-call(bf16[32,1280]{1,0:T(8,128)(2,1)S(1)} %bitcast.9, bf16[1280,2048]{1,0:T(8,128)(2,1)S(1)} %bitcast.8, bf16[224,128]{1,0:T(8,128)(2,1)S(1)} %pack.1._.refs_4_), custom_call_target="tpu_custom_call" | custom-call | flops 167772160 | bytes 5242880 | tf_op jit(solution)/shard_map/project/pallas_call | solution.py:114
  8.5 0.0 collective-permute-start.3
  8.5 1.2 %collective-permute-done.3.refs_8_ = bf16[1,128,128]{2,1,0:T(8,128)(2,1)S(1)} collective-permute-done((bf16[1,128,128]{2,1,0:T(8,128)(2,1)S(1)}, bf16[1,128,128]{2,1,0:T(8,128)(2,1)S(1)}, u32[]{:S(2)}, u32[]{:S(2)}) %collective-permute-start.3) | collective-permute-done | bytes 32800 | tf_op jit(solution)/shard_map/ppermute | solution.py:26
  9.8 0.0 collective-permute-done.2.refs_7_
  9.8 2.1 %collective-permute-done.1.refs_6_ = bf16[224,128]{1,0:T(8,128)(2,1)S(1)} collective-permute-done((bf16[224,128]{1,0:T(8,128)(2,1)S(1)}, bf16[224,128]{1,0:T(8,128)(2,1)S(1)}, u32[]{:S(2)}, u32[]{:S(2)}) %collective-permute-start.1) | collective-permute-done | bytes 57376 | tf_op jit(solution)/shard_map/ppermute | solution.py:26
  11.9 0.0 collective-permute-done.refs_5_
  11.9 0.0 copy-done.5
  11.9 0.9 %route.1 = (bf16[96,128]{1,0:T(8,128)(2,1)S(1)}, bf16[224,128]{1,0:T(8,128)(2,1)S(1)}, bf16[224,128]{1,0:T(8,128)(2,1)S(1)}, bf16[96,128]{1,0:T(8,128)(2,1)S(1)}) custom-call(s32[4]{0:T(128)S(1)} %copy-done.5, bf16[32,1280]{1,0:T(8,128)(2,1)S(1)} %bitcast.10, bf16[128,128]{1,0:T(8,128)(2,1)S(1)} %get-tuple-element.21.refs_2_, ...), custom_call_target="tpu_custom_call" | custom-call | bytes 800000 | tf_op jit(solution)/shard_map/route/pallas_call | solution.py:326
  12.8 1.5 %collective-permute-start.5 = (bf16[224,128]{1,0:T(8,128)(2,1)S(1)}, bf16[224,128]{1,0:T(8,128)(2,1)S(1)}, u32[]{:S(2)}, u32[]{:S(2)}) collective-permute-start(bf16[224,128]{1,0:T(8,128)(2,1)S(1)} %get-tuple-element.32), channel_id=1, source_target_pairs={{0,2},{1,3},{2,0},{3,1},{4,6},{5,7},{6,4},{7,5},{8,10},{9,11},{10,... | collective-permute-start | bytes 172040 | tf_op jit(solution)/shard_map/ppermute | solution.py:26
  14.3 0.0 collective-permute-start.6
  14.3 0.6 %collective-permute-start.4 = (bf16[96,128]{1,0:T(8,128)(2,1)S(1)}, bf16[96,128]{1,0:T(8,128)(2,1)S(1)}, u32[]{:S(2)}, u32[]{:S(2)}) collective-permute-start(bf16[96,128]{1,0:T(8,128)(2,1)S(1)} %get-tuple-element.31), channel_id=1, source_target_pairs={{0,3},{1,2},{2,1},{3,0},{4,7},{5,6},{6,5},{7,4},{8,11},{9,10},{10,... | collective-permute-start | bytes 73736 | tf_op jit(solution)/shard_map/ppermute | solution.py:26
  15.0 0.0 copy-done
  15.0 0.0 copy-done.1
  15.0 0.0 copy-done.3
  15.0 0.0 copy-start.4
  15.0 2.2 %attend.1 = (bf16[512,128]{1,0:T(8,128)(2,1)S(1)}, f32[512,128]{1,0:T(8,128)S(1)}, f32[512,128]{1,0:T(8,128)S(1)}, f32[512,128]{1,0:T(8,128)S(1)}, f32[32,128]{1,0:T(8,128)S(1)}, /*index=5*/f32[32,128]{1,0:T(8,128)S(1)}) custom-call(s32[8]{0:T(128)} %lengths_hbm.1, bf16[32,2048]{1,0:T(8,128)(2,1)S(1)} %bitcast.11, bf16[8,512,256]{2,1,0:T(8,128)(2,1)S(1)} %copy-done, ...), custom_call_target="tpu_custom_call" | custom-call | flops 134217728 | bytes 4194304 | tf_op jit(solution)/shard_map/attend/pallas_call | solution.py:225
  17.2 0.4 %collective-permute-done.4.refs_8_ = bf16[96,128]{1,0:T(8,128)(2,1)S(1)} collective-permute-done((bf16[96,128]{1,0:T(8,128)(2,1)S(1)}, bf16[96,128]{1,0:T(8,128)(2,1)S(1)}, u32[]{:S(2)}, u32[]{:S(2)}) %collective-permute-start.4) | collective-permute-done | bytes 24608 | tf_op jit(solution)/shard_map/ppermute | solution.py:26
  17.6 0.0 collective-permute-done.5.refs_9_
  17.6 0.0 collective-permute-done.6.refs_10_
  17.6 0.0 copy-done.4
  17.6 1.6 %finish.1 = (bf16[32,2048]{1,0:T(8,128)(2,1)}, bf16[32,256]{1,0:T(8,128)(2,1)}, bf16[32,256]{1,0:T(8,128)(2,1)}) custom-call(f32[32,512]{1,0:T(8,128)S(1)} %get-tuple-element.20.refs_0_, f32[1,128]{1,0:T(1,128)S(1)} %bitcast.12, bf16[512,128]{1,0:T(8,128)(2,1)S(1)} %get-tuple-element.25.refs_2_, f32[512,128]{1,0:T(8,128)S(1)} %get-tuple-element.26.refs_3_, ...), custom_call_target="tpu_custom_call" | custom-call | bytes 1000000 | tf_op jit(solution)/shard_map/finish/pallas_call | solution.py:461
  (1 shorter events, 0.0 us)
Async XLA Ops:
  0.6 6.8 %slice-start = ((s8[5242880]{0:T(1024)(128)(4,1)}), s8[4194304]{0:T(1024)(128)(4,1)S(1)}, s32[]{:S(2)}) async-start(s8[5242880]{0:T(1024)(128)(4,1)} %bitcast.7), calls=%async_computation | async-start | bytes 8388608
  0.6 6.8 %slice-start.1 = ((s8[5242880]{0:T(1024)(128)(4,1)}), s8[1048576]{0:T(1024)(128)(4,1)S(1)}, s32[]{:S(2)}) async-start(s8[5242880]{0:T(1024)(128)(4,1)} %bitcast.7), calls=%async_computation.1 | async-start | bytes 2097152
  0.7 6.8 %copy-start.2 = (bf16[4,8,1280]{2,1,0:T(8,128)(2,1)S(1)}, bf16[4,8,1280]{2,1,0:T(8,128)(2,1)}, u32[]{:S(2)}) copy-start(bf16[4,8,1280]{2,1,0:T(8,128)(2,1)} %param.10) | copy-start | bytes 245764
  1.7 8.0 %collective-permute-start.2 = (bf16[224,128]{1,0:T(8,128)(2,1)S(1)}, bf16[224,128]{1,0:T(8,128)(2,1)S(1)}, u32[]{:S(2)}, u32[]{:S(2)}) collective-permute-start(bf16[224,128]{1,0:T(8,128)(2,1)S(1)} %pack.1._.refs_4_), channel_id=1, source_target_pairs={{0,12},{4,8},{8,4},{12,0},{1,13},{5,9},{9,5},{13,1},{2,14},{6,10},... | collective-permute-start | bytes 172040 | tf_op jit(solution)/shard_map/ppermute | solution.py:26
  6.8 5.1 %collective-permute-start.1 = (bf16[224,128]{1,0:T(8,128)(2,1)S(1)}, bf16[224,128]{1,0:T(8,128)(2,1)S(1)}, u32[]{:S(2)}, u32[]{:S(2)}) collective-permute-start(bf16[224,128]{1,0:T(8,128)(2,1)S(1)} %pack.1._.refs_4_), channel_id=1, source_target_pairs={{0,8},{4,12},{8,0},{12,4},{1,9},{5,13},{9,1},{13,5},{2,10},{6,14},... | collective-permute-start | bytes 172040 | tf_op jit(solution)/shard_map/ppermute | solution.py:26
  6.8 5.1 %collective-permute-start = (bf16[224,128]{1,0:T(8,128)(2,1)S(1)}, bf16[224,128]{1,0:T(8,128)(2,1)S(1)}, u32[]{:S(2)}, u32[]{:S(2)}) collective-permute-start(bf16[224,128]{1,0:T(8,128)(2,1)S(1)} %pack.1._.refs_4_), channel_id=1, source_target_pairs={{0,4},{4,0},{8,12},{12,8},{1,5},{5,1},{9,13},{13,9},{2,6},{6,2},{1... | collective-permute-start | bytes 172040 | tf_op jit(solution)/shard_map/ppermute | solution.py:26
  7.5 4.4 %copy-start.5 = (s32[4]{0:T(128)S(1)}, s32[4]{0:T(128)}, u32[]{:S(2)}) copy-start(s32[4]{0:T(128)} %refs_0_.1) | copy-start | bytes 52
  7.5 7.5 %copy-start = (bf16[8,512,256]{2,1,0:T(8,128)(2,1)S(1)}, bf16[8,512,256]{2,1,0:T(8,128)(2,1)}, u32[]{:S(2)}) copy-start(bf16[8,512,256]{2,1,0:T(8,128)(2,1)} %keys_ref.1) | copy-start | bytes 6291460
  7.5 7.5 %copy-start.1 = (bf16[8,512,256]{2,1,0:T(8,128)(2,1)S(1)}, bf16[8,512,256]{2,1,0:T(8,128)(2,1)}, u32[]{:S(2)}) copy-start(bf16[8,512,256]{2,1,0:T(8,128)(2,1)} %values_ref.1) | copy-start | bytes 6291460
  7.5 7.4 %copy-start.3 = (bf16[4,8,2048]{2,1,0:T(8,128)(2,1)S(1)}, bf16[4,8,2048]{2,1,0:T(8,128)(2,1)}, u32[]{:S(2)}) copy-start(bf16[4,8,2048]{2,1,0:T(8,128)(2,1)} %param.15) | copy-start | bytes 393220
  8.5 1.2 %collective-permute-start.3 = (bf16[1,128,128]{2,1,0:T(8,128)(2,1)S(1)}, bf16[1,128,128]{2,1,0:T(8,128)(2,1)S(1)}, u32[]{:S(2)}, u32[]{:S(2)}) collective-permute-start(bf16[1,128,128]{2,1,0:T(8,128)(2,1)S(1)} %get-tuple-element.23), channel_id=1, source_target_pairs={{0,1},{1,0},{2,3},{3,2},{4,5},{5,4},{6,7},{7,6},{8,9},{9,8},{10,11... | collective-permute-start | bytes 98312 | tf_op jit(solution)/shard_map/ppermute | solution.py:26
  12.8 4.8 %collective-permute-start.5 = (bf16[224,128]{1,0:T(8,128)(2,1)S(1)}, bf16[224,128]{1,0:T(8,128)(2,1)S(1)}, u32[]{:S(2)}, u32[]{:S(2)}) collective-permute-start(bf16[224,128]{1,0:T(8,128)(2,1)S(1)} %get-tuple-element.32), channel_id=1, source_target_pairs={{0,2},{1,3},{2,0},{3,1},{4,6},{5,7},{6,4},{7,5},{8,10},{9,11},{10,... | collective-permute-start | bytes 172040 | tf_op jit(solution)/shard_map/ppermute | solution.py:26
  14.3 3.3 %collective-permute-start.6 = (bf16[224,128]{1,0:T(8,128)(2,1)S(1)}, bf16[224,128]{1,0:T(8,128)(2,1)S(1)}, u32[]{:S(2)}, u32[]{:S(2)}) collective-permute-start(bf16[224,128]{1,0:T(8,128)(2,1)S(1)} %get-tuple-element.33), channel_id=1, source_target_pairs={{0,1},{1,0},{2,3},{3,2},{4,5},{5,4},{6,7},{7,6},{8,9},{9,8},{10,11... | collective-permute-start | bytes 172040 | tf_op jit(solution)/shard_map/ppermute | solution.py:26
  14.3 3.3 %collective-permute-start.4 = (bf16[96,128]{1,0:T(8,128)(2,1)S(1)}, bf16[96,128]{1,0:T(8,128)(2,1)S(1)}, u32[]{:S(2)}, u32[]{:S(2)}) collective-permute-start(bf16[96,128]{1,0:T(8,128)(2,1)S(1)} %get-tuple-element.31), channel_id=1, source_target_pairs={{0,3},{1,2},{2,1},{3,0},{4,7},{5,6},{6,5},{7,4},{8,11},{9,10},{10,... | collective-permute-start | bytes 73736 | tf_op jit(solution)/shard_map/ppermute | solution.py:26
  15.0 2.6 %copy-start.4 = (f32[128]{0:T(128)S(1)}, f32[128]{0:T(128)}, u32[]{:S(2)}) copy-start(f32[128]{0:T(128)} %param.14) | copy-start | bytes 1540

commit v8 on v7

--- a/solution.py
+++ b/solution.py
@@ -13,6 +13,7 @@
 adapter_scale = 2.0
 masked_score = -1e30
 lanes = 128
+exponent_scale = lanes**-0.5 / math.log(2.0)
 f32 = jnp.float32
 bf16 = jnp.bfloat16
 
@@ -85,78 +86,18 @@
     )(*in_hbm(down, up))
 
 
-def project_kernel(tokens_ref, weight_ref, _, own_ref, first_ref, near_ref, kept_ref):
-    shard = lax.axis_index("tensor")
-    pairs, rows, own = kept_ref.shape
-
-    def product(i):
-        first = pl.multiple_of((shard ^ i) * own, lanes)
-        return jnp.dot(
-            tokens_ref[...], weight_ref[:, pl.ds(first, own)], preferred_element_type=f32
-        )
-
-    def put(block, ref):
-        for c in range(own // lanes):
-            ref[c * rows : (c + 1) * rows, :] = block[:, c * lanes : (c + 1) * lanes].astype(bf16)
-
-    for m in range(pairs):
-        put(product(2 * m + 3), near_ref.at[m])
-        kept_ref[m] = product(2 * m + 2)
-    put(product(1), first_ref)
-    own_ref[...] = product(0)
-
-
-def project(tokens, weight, after, shards):
-    rows, depth = tokens.shape
-    own = weight.shape[1] // shards
-    pairs = shards // 2 - 1
-    sent = rows * own // lanes
-    return pl.pallas_call(
-        project_kernel,
-        out_shape=(
-            jax.ShapeDtypeStruct((rows, own), f32),
-            jax.ShapeDtypeStruct((sent, lanes), bf16),
-            jax.ShapeDtypeStruct((pairs, sent, lanes), bf16),
-            jax.ShapeDtypeStruct((pairs, rows, own), f32),
-        ),
-        in_specs=[whole_in_vmem] * 3,
-        out_specs=(whole_in_vmem,) * 4,
-        compiler_params=pltpu.CompilerParams(vmem_limit_bytes=4 * 2**20),
-        name="project",
-        cost_estimate=pl.CostEstimate(
-            flops=2 * rows * weight.size, bytes_accessed=2 * weight.size, transcendentals=0
-        ),
-    )(tokens, weight, after)
-
-
-def attend_kernel(
-    step_count,
-    head_count,
-    lengths_hbm,
-    queries_ref,
-    keys_ref,
-    values_ref,
-    _,
-    grouped_ref,
-    total_ref,
-    peak_ref,
-    sum_ref,
-    cosine_ref,
-    sine_ref,
-    lengths_ref,
-    regroup,
-    scores,
-    raised,
-    length_sem,
-):
+def project_kernel(step_count, head_count, shards, *refs):
+    lengths_hbm, tokens_ref, weight_ref, queries_ref, keys_ref, _ = refs[:6]
+    pairs = shards // 2
+    near_refs = refs[6 : 6 + pairs]
+    kept_ref, grouped_ref, scores_ref, cosine_ref, sine_ref = refs[6 + pairs : 11 + pairs]
+    lengths_ref, regroup, length_sem = refs[11 + pairs :]
     lengths_copy = pltpu.make_async_copy(lengths_hbm, lengths_ref, length_sem)
     lengths_copy.start()
-    row_count, slots, _ = keys_ref.shape
-    rows = step_count * row_count
+
+    row_count = keys_ref.shape[0]
     group = queries_ref.shape[1] // (head_count * lanes)
     seen = step_count * group
-    scale = lanes**-0.5
-
     for pair in range(step_count // 2):
         for q in range(head_count * group):
             h, g = q // group, q % group
@@ -170,39 +111,32 @@
                 ]
     grouped_ref[...] = regroup[...].astype(bf16)
 
-    def place(h, b):
-        at = (h * row_count + b) * seen
-        return slice(at, at + seen)
+    shard = lax.axis_index("tensor")
+    _, rows, own = kept_ref.shape
+    for i in range(shards):
+        first = pl.multiple_of((shard ^ i) * own, lanes)
+        block = jnp.dot(
+            tokens_ref[...], weight_ref[:, pl.ds(first, own)], preferred_element_type=f32
+        )
+        if i % 2 == 0:
+            kept_ref[i // 2] = block
+            continue
+        for c in range(own // lanes):
+            near_refs[i // 2][c * rows : (c + 1) * rows, :] = block[
+                :, c * lanes : (c + 1) * lanes
+            ].astype(bf16)
 
     for b in range(row_count):
         for h in range(head_count):
-            scores[place(h, b), :] = lax.dot_general(
-                grouped_ref[place(h, b), :],
+            at = (h * row_count + b) * seen
+            scores_ref[at : at + seen, :] = lax.dot_general(
+                grouped_ref[at : at + seen, :],
                 keys_ref[b, :, h * lanes : (h + 1) * lanes],
                 (((1,), (1,)), ((), ())),
                 preferred_element_type=f32,
             )
+
     lengths_copy.wait()
-    slot = lax.broadcasted_iota(jnp.int32, (seen, slots), 1)
-    for b in range(row_count):
-        live = slot < lengths_ref[b]
-        for h in range(head_count):
-            score = jnp.where(live, scores[place(h, b), :] * scale, masked_score)
-            peak = jnp.max(score, axis=1, keepdims=True)
-            lifted = jnp.exp(score - peak)
-            raised[place(h, b), :] = lifted.astype(bf16)
-            peak_ref[place(h, b), :] = jnp.broadcast_to(peak, (seen, lanes))
-            sum_ref[place(h, b), :] = jnp.broadcast_to(
-                jnp.sum(lifted, axis=1, keepdims=True), (seen, lanes)
-            )
-    for b in range(row_count):
-        for h in range(head_count):
-            total_ref[place(h, b), :] = jnp.dot(
-                raised[place(h, b), :],
-                values_ref[b, :, h * lanes : (h + 1) * lanes],
-                preferred_element_type=f32,
-            )
-
     row = lax.broadcasted_iota(jnp.int32, (rows, lanes), 0)
     lane = lax.broadcasted_iota(jnp.int32, (rows, lanes), 1)
     position = row // row_count
@@ -216,39 +150,104 @@
     sine_ref[...] = jnp.where(lane < middle, -sine, sine)
 
 
-def attend(lengths, queries, keys, values, after, step_count):
+def project(lengths, tokens, weight, queries, keys, after, step_count, shards):
+    rows, depth = tokens.shape
+    own = weight.shape[1] // shards
+    pairs = shards // 2
     row_count, slots, width = keys.shape
-    rows = step_count * row_count
     seen_rows = rows * queries.shape[1] // lanes
     table = jax.ShapeDtypeStruct((rows, lanes), f32)
-    seen_table = jax.ShapeDtypeStruct((seen_rows, lanes), f32)
-    return pl.pallas_call(
-        functools.partial(attend_kernel, step_count, width // lanes),
-        out_shape=(
+    outs = pl.pallas_call(
+        functools.partial(project_kernel, step_count, width // lanes, shards),
+        out_shape=[jax.ShapeDtypeStruct((rows * own // lanes, lanes), bf16)] * pairs
+        + [
+            jax.ShapeDtypeStruct((pairs, rows, own), f32),
             jax.ShapeDtypeStruct((seen_rows, lanes), bf16),
-            seen_table,
-            seen_table,
-            seen_table,
+            jax.ShapeDtypeStruct((seen_rows, slots), f32),
             table,
             table,
-        ),
-        in_specs=[stays_in_hbm] + [whole_in_vmem] * 4,
-        out_specs=(whole_in_vmem,) * 6,
+        ],
+        in_specs=[stays_in_hbm] + [whole_in_vmem] * 5,
+        out_specs=[whole_in_vmem] * (pairs + 5),
         scratch_shapes=[
             pltpu.SMEM(lengths.shape, jnp.int32),
             pltpu.VMEM((seen_rows, lanes), f32),
-            pltpu.VMEM((seen_rows, slots), f32),
+            pltpu.SemaphoreType.DMA,
+        ],
+        compiler_params=pltpu.CompilerParams(vmem_limit_bytes=6 * 2**20),
+        name="project",
+        cost_estimate=pl.CostEstimate(
+            flops=2 * rows * weight.size + 2 * seen_rows * slots * lanes,
+            bytes_accessed=2 * (weight.size + keys.size),
+            transcendentals=0,
+        ),
+    )(*in_hbm(lengths), tokens, weight, queries, keys, after)
+    return outs[:pairs], *outs[pairs:]
+
+
+def attend_kernel(
+    head_count,
+    lengths_hbm,
+    scores_ref,
+    values_ref,
+    _,
+    total_ref,
+    peak_ref,
+    sum_ref,
+    lengths_ref,
+    raised,
+    length_sem,
+):
+    lengths_copy = pltpu.make_async_copy(lengths_hbm, lengths_ref, length_sem)
+    lengths_copy.start()
+    row_count, slots, _ = values_ref.shape
+    seen = scores_ref.shape[0] // (head_count * row_count)
+    places = [
+        (b, h, slice((h * row_count + b) * seen, (h * row_count + b + 1) * seen))
+        for b in range(row_count)
+        for h in range(head_count)
+    ]
+    lengths_copy.wait()
+    slot = lax.broadcasted_iota(jnp.int32, (seen, slots), 1)
+    for b, h, place in places:
+        score = jnp.where(slot < lengths_ref[b], scores_ref[place, :], masked_score)
+        peak = jnp.max(score, axis=1, keepdims=True)
+        lifted = jnp.exp2((score - peak) * exponent_scale)
+        raised[place, :] = lifted.astype(bf16)
+        peak_ref[place, :] = jnp.broadcast_to(peak, (seen, lanes))
+        sum_ref[place, :] = jnp.broadcast_to(
+            jnp.sum(lifted, axis=1, keepdims=True), (seen, lanes)
+        )
+    for b, h, place in places:
+        total_ref[place, :] = jnp.dot(
+            raised[place, :],
+            values_ref[b, :, h * lanes : (h + 1) * lanes],
+            preferred_element_type=f32,
+        )
+
+
+def attend(lengths, scores, values, after):
+    row_count, slots, width = values.shape
+    seen_rows = scores.shape[0]
+    seen_table = jax.ShapeDtypeStruct((seen_rows, lanes), f32)
+    return pl.pallas_call(
+        functools.partial(attend_kernel, width // lanes),
+        out_shape=(seen_table,) * 3,
+        in_specs=[stays_in_hbm] + [whole_in_vmem] * 3,
+        out_specs=(whole_in_vmem,) * 3,
+        scratch_shapes=[
+            pltpu.SMEM(lengths.shape, jnp.int32),
             pltpu.VMEM((seen_rows, slots), bf16),
             pltpu.SemaphoreType.DMA,
         ],
-        compiler_params=pltpu.CompilerParams(vmem_limit_bytes=8 * 2**20),
+        compiler_params=pltpu.CompilerParams(vmem_limit_bytes=6 * 2**20),
         name="attend",
         cost_estimate=pl.CostEstimate(
-            flops=4 * seen_rows * slots * lanes,
-            bytes_accessed=2 * (keys.size + values.size),
+            flops=2 * seen_rows * slots * lanes,
+            bytes_accessed=2 * values.size,
             transcendentals=seen_rows * slots,
         ),
-    )(*in_hbm(lengths), queries, keys, values, after)
+    )(*in_hbm(lengths), scores, values, after)
 
 
 def add_near(kept, near):
@@ -260,15 +259,15 @@
 
 
 def carries_sums(i):
-    return i == 1 or (i > 0 and i % 2 == 0)
+    return i > 0 and i % 2 == 0
 
 
 def route_kernel(replicas, shards, *refs):
-    owners_ref, tokens_ref, first_ref, kept_ref = refs[:4]
-    piece_refs = refs[4 : 4 + replicas]
-    near_ref = refs[4 + replicas]
-    out_refs = refs[5 + replicas : 5 + replicas + shards]
-    token_buf, left, right, up_buf = refs[5 + replicas + shards :]
+    owners_ref, tokens_ref, kept_ref = refs[:3]
+    piece_refs = refs[3 : 3 + replicas]
+    near_refs = refs[3 + replicas : 3 + replicas + shards // 2]
+    out_refs = refs[3 + replicas + shards // 2 : 3 + replicas + shards // 2 + shards]
+    token_buf, left, right, up_buf = refs[3 + replicas + shards // 2 + shards :]
     replica = lax.axis_index("rollout")
     shard = lax.axis_index("tensor")
     rows, depth = tokens_ref.shape
@@ -306,11 +305,8 @@
     both = jnp.concatenate(split_halves(lowered), axis=1)
     for i in range(shards):
         first = 0
-        if i == 1:
-            first = first_ref.shape[0]
-            out_refs[i][:first, :] = first_ref[...]
-        elif carries_sums(i):
-            for block in add_near(kept_ref[i // 2 - 1], near_ref[i // 2 - 1]):
+        if carries_sums(i):
+            for block in add_near(kept_ref[i // 2], near_refs[i // 2]):
                 out_refs[i][first : first + rows, :] = block.astype(bf16)
                 first += rows
         out_refs[i][first : first + rows, :] = both
@@ -320,8 +316,8 @@
 def route(owners, tokens, sums, pieces, rank, up_rows, shards):
     rows, depth = tokens.shape
     replicas = len(pieces)
-    first, kept, near = sums
-    sent = first.shape[0]
+    kept, near = sums
+    sent = near[0].shape[0]
     width = -(-depth // replicas // lanes) * lanes
     return pl.pallas_call(
         functools.partial(route_kernel, replicas, shards),
@@ -329,7 +325,7 @@
             jax.ShapeDtypeStruct(((sent if carries_sums(i) else 0) + rows + up_rows, lanes), bf16)
             for i in range(shards)
         ],
-        in_specs=[whole_in_smem] + [whole_in_vmem] * (4 + replicas),
+        in_specs=[whole_in_smem] + [whole_in_vmem] * (2 + replicas + len(near)),
         out_specs=[whole_in_vmem] * shards,
         scratch_shapes=[
             pltpu.VMEM((replicas, rows, width), bf16),
@@ -340,11 +336,11 @@
         compiler_params=pltpu.CompilerParams(vmem_limit_bytes=4 * 2**20),
         name="route",
         cost_estimate=pl.CostEstimate(flops=0, bytes_accessed=800000, transcendentals=0),
-    )(owners, tokens, first, kept, *pieces, near)
+    )(owners, tokens, kept, *pieces, *near)
 
 
 def route_plain(owners, tokens, sums, down, up, rank_part, own, shards):
-    first_sent, kept, near = sums
+    kept, near = sums
     rank = down.shape[1]
     shard = lax.axis_index("tensor")
     first = shard * rank_part
@@ -360,29 +356,27 @@
     for i in range(shards):
         up_block = lax.dynamic_slice_in_dim(up_matrix, (shard ^ i) * own, own, axis=1)
         parts = [both, side_by_side(up_block)]
-        if i == 1:
-            parts = [first_sent] + parts
-        elif carries_sums(i):
-            sums = add_near(kept[i // 2 - 1], near[i // 2 - 1])
+        if carries_sums(i):
+            sums = add_near(kept[i // 2], near[i // 2])
             parts = [jnp.concatenate(sums, axis=0).astype(bf16)] + parts
         packets.append(jnp.concatenate(parts, axis=0))
     return packets
 
 
 def finish_kernel(step_count, row_count, head_count, shards, *refs):
-    own_ref, gain_ref, grouped_ref, total_ref, peak_ref, sum_ref, cosine_ref, sine_ref = refs[:8]
-    packet_refs = refs[8 : 8 + shards][::-1]
-    attention_ref, keys_ref, values_ref = refs[8 + shards : 11 + shards]
-    up_buf, ordered = refs[11 + shards :]
+    kept_ref, near_ref, gain_ref, grouped_ref, total_ref, peak_ref, sum_ref = refs[:7]
+    cosine_ref, sine_ref = refs[7:9]
+    packet_refs = refs[9 : 9 + shards][::-1]
+    attention_ref, keys_ref, values_ref = refs[9 + shards : 12 + shards]
+    up_buf, ordered = refs[12 + shards :]
     shard = lax.axis_index("tensor")
     rows = step_count * row_count
-    own = own_ref.shape[1]
+    own = kept_ref.shape[2]
     blocks = own // lanes
     rank = up_buf.shape[0]
     rank_part = rank // shards
     group = grouped_ref.shape[0] // (head_count * rows)
     seen = step_count * group
-    scale = lanes**-0.5
 
     lowered = jnp.zeros((rows, lanes), f32)
     for i in range(shards):
@@ -401,8 +395,7 @@
     up = up_buf[...].astype(bf16)
     raised_up = jnp.dot(left, jnp.concatenate([up, up], axis=0), preferred_element_type=f32)
     joined = []
-    for c in range(blocks):
-        block = own_ref[:, c * lanes : (c + 1) * lanes]
+    for c, block in enumerate(add_near(kept_ref[0], near_ref)):
         for i in filter(carries_sums, range(shards)):
             block = block + packet_refs[i][c * rows : (c + 1) * rows, :].astype(f32)
         joined.append(block + adapter_scale * raised_up[:, c * lanes : (c + 1) * lanes])
@@ -426,11 +419,11 @@
         score = lax.dot_general(
             grouped_ref[mine, :], key, (((1,), (1,)), ((), ())), preferred_element_type=f32
         )
-        score = jnp.where(visible, score * scale, masked_score)
+        score = jnp.where(visible, score, masked_score)
         old_peak = peak_ref[mine, :]
         peak = jnp.maximum(old_peak, jnp.max(score, axis=1, keepdims=True))
-        fade = jnp.exp(old_peak - peak)
-        lifted = jnp.exp(score - peak[:, :rows])
+        fade = jnp.exp2((old_peak - peak) * exponent_scale)
+        lifted = jnp.exp2((score - peak[:, :rows]) * exponent_scale)
         denominator = fade * sum_ref[mine, :] + jnp.sum(lifted, axis=1, keepdims=True)
         total = fade * total_ref[mine, :] + jnp.dot(
             lifted.astype(bf16), value, preferred_element_type=f32
@@ -453,9 +446,9 @@
             ] = jnp.concatenate(both, axis=0).astype(bf16)
 
 
-def finish(partials, gain, packets, rank, step_count, row_count, query_width):
-    mine, grouped, total, peak, denominator, cosine, sine = partials
-    rows, own = mine.shape
+def finish(kept, near, partials, gain, packets, rank, step_count, row_count, query_width):
+    grouped, total, peak, denominator, cosine, sine = partials
+    _, rows, own = kept.shape
     shards = len(packets)
     head_count = own // (2 * lanes)
     return pl.pallas_call(
@@ -465,7 +458,7 @@
             jax.ShapeDtypeStruct((rows, head_count * lanes), bf16),
             jax.ShapeDtypeStruct((rows, head_count * lanes), bf16),
         ),
-        in_specs=[whole_in_vmem] * (8 + shards),
+        in_specs=[whole_in_vmem] * (9 + shards),
         out_specs=(whole_in_vmem,) * 3,
         scratch_shapes=[
             pltpu.VMEM((rank, own), f32),
@@ -474,7 +467,7 @@
         compiler_params=pltpu.CompilerParams(vmem_limit_bytes=6 * 2**20),
         name="finish",
         cost_estimate=pl.CostEstimate(flops=0, bytes_accessed=1000000, transcendentals=0),
-    )(mine, gain, grouped, total, peak, denominator, cosine, sine, *packets[::-1])
+    )(kept, near, gain, grouped, total, peak, denominator, cosine, sine, *packets[::-1])
 
 
 def per_device(
@@ -512,20 +505,31 @@
         packed = pack(adapter_down.T, adapter_up, rank_part, beside)
         arrived = {i: swap(packed, "rollout", i) for i in reversed(range(1, replicas))}
         pieces = [packed] + [arrived[i] for i in range(1, replicas)]
-    mine, first, near, kept = project(
-        tokens, key_value_weight, packed if fits else adapter_up, shards
-    )
-    sums = (first, kept, swap(near, "tensor", 1))
+    near, kept, grouped, scores, cosine, sine = project(
+        lengths,
+        tokens,
+        key_value_weight,
+        query_rows,
+        cache_keys,
+        packed if fits else adapter_up,
+        step_count,
+        shards,
+    )
+    near = [swap(block, "tensor", 1) for block in near]
     if fits:
-        packets = route(owners, tokens, sums, pieces, rank, rank_part * own // lanes, shards)
+        packets = route(
+            owners, tokens, (kept, near), pieces, rank, rank_part * own // lanes, shards
+        )
     else:
         packets = route_plain(
-            owners, tokens, sums, adapter_down, adapter_up, rank_part, own, shards
-        )
-    partials = attend(lengths, query_rows, cache_keys, stored_values, packets[0], step_count)
+            owners, tokens, (kept, near), adapter_down, adapter_up, rank_part, own, shards
+        )
+    total, peak, denominator = attend(lengths, scores, stored_values, packets[0])
     packets = [packets[0]] + [swap(packets[i], "tensor", i) for i in range(1, shards)]
     attention, keys, values = finish(
-        [mine] + list(partials),
+        kept,
+        near[0],
+        (grouped, total, peak, denominator, cosine, sine),
         key_gain.reshape(1, -1),
         packets,
         rank,

time: 19.5 us -> 19.4 us (level)
  waiting for transfers between devices: 3.75 us -> 3.11 us
  starting transfers between devices: 7.92 us -> 8.49 us
    ppermute x7 -> x8, waiting for transfers between devices: 3.75 us -> 3.11 us  [swap(): return lax.ppermute(block, axis, [(s, s ^ offset) for s in range(count)])]
    ppermute x7 -> x8, starting transfers between devices: 7.92 us -> 8.49 us  [swap(): return lax.ppermute(block, axis, [(s, s ^ offset) for s in range(count)])]
  transfers between devices with their start and end apart: 7 -> 8, of which waited for: 3 -> 4; matrix products, arithmetic and copies ran while one was open for 0% -> 0% of each run, Pallas kernels for 17% -> 17%
where the time goes in v8:
time: 19.4 us; the launch traced here: 19.2 us
  starting transfers between devices  8.49 us (44%)
  Pallas kernels  6.82 us (35%)
  waiting for transfers between devices  3.11 us (16%)
  between operations  0.76 us (4%)
    ppermute x8, starting transfers between devices, swap(): return lax.ppermute(block, axis, [(s, s ^ offset) for s in range(count)])  8.49 us
    ppermute x8, waiting for transfers between devices, swap(): return lax.ppermute(block, axis, [(s, s ^ offset) for s in range(count)])  3.11 us
    pallas_call x1, Pallas kernels, project(): pl.pallas_call(functools.partial(project_kernel, step_count, width // lan...  1.93 us
    pallas_call x1, Pallas kernels, finish(): pl.pallas_call(functools.partial(finish_kernel, step_count, row_count, he...  1.6 us
    pallas_call x1, Pallas kernels, attend(): pl.pallas_call(functools.partial(attend_kernel, width // lanes), out_shap...  1.36 us
    pallas_call x1, Pallas kernels, pack(): pl.pallas_call(pack_kernel, out_shape=jax.ShapeDtypeStruct((rows, lanes),...  1.05 us
    pallas_call x1, Pallas kernels, route(): pl.pallas_call(functools.partial(route_kernel, replicas, shards), out_sha...  0.88 us
  transfers between devices with their start and end apart: 8, of which 4 were waited for; matrix products, arithmetic and copies ran while one was open for 0% of the time, Pallas kernels for 17%

profile of v8, /device:TPU:0, one launch (start us, length us, event | category | flops | bytes accessed | tf_op | source)
XLA Modules:
  0.0 19.2 jit_solution(3958926310735221739)
XLA Ops:
  0.6 0.0 slice-start
  0.6 0.0 slice-start.1
  0.7 0.0 copy-start
  0.7 0.0 copy-start.2
  0.7 0.0 copy-start.3
  0.7 1.0 %pack.1.refs_5_.refs_3_ = bf16[224,128]{1,0:T(8,128)(2,1)S(1)} custom-call(bf16[64,320]{1,0:T(8,128)(2,1)} %bitcast.14, bf16[64,512]{1,0:T(8,128)(2,1)} %up_hbm.1), custom_call_target="tpu_custom_call" | custom-call | flops 9437184000 | bytes 9437184 | tf_op jit(solution)/shard_map/pack/pallas_call | solution.py:73
  1.7 5.1 %collective-permute-start.3 = (bf16[224,128]{1,0:T(8,128)(2,1)S(1)}, bf16[224,128]{1,0:T(8,128)(2,1)S(1)}, u32[]{:S(2)}, u32[]{:S(2)}) collective-permute-start(bf16[224,128]{1,0:T(8,128)(2,1)S(1)} %pack.1.refs_5_.refs_3_), channel_id=1, source_target_pairs={{0,12},{4,8},{8,4},{12,0},{1,13},{5,9},{9,5},{13,1},{2,14},{6,10},... | collective-permute-start | bytes 172040 | tf_op jit(solution)/shard_map/ppermute | solution.py:27
  6.9 0.0 collective-permute-start.2
  6.9 0.6 %collective-permute-start.1 = (bf16[224,128]{1,0:T(8,128)(2,1)S(1)}, bf16[224,128]{1,0:T(8,128)(2,1)S(1)}, u32[]{:S(2)}, u32[]{:S(2)}) collective-permute-start(bf16[224,128]{1,0:T(8,128)(2,1)S(1)} %pack.1.refs_5_.refs_3_), channel_id=1, source_target_pairs={{0,4},{4,0},{8,12},{12,8},{1,5},{5,1},{9,13},{13,9},{2,6},{6,2},{1... | collective-permute-start | bytes 172040 | tf_op jit(solution)/shard_map/ppermute | solution.py:27
  7.5 0.0 slice-done
  7.5 0.0 slice-done.1
  7.5 0.0 copy-done
  7.5 0.0 copy-done.2
  7.5 0.0 copy-done.3
  7.5 0.0 copy-start.4
  7.5 0.0 copy-start.1
  7.6 1.9 %project.1 = (bf16[128,128]{1,0:T(8,128)(2,1)S(1)}, bf16[128,128]{1,0:T(8,128)(2,1)S(1)}, f32[2,32,512]{2,1,0:T(8,128)S(1)}, bf16[512,128]{1,0:T(8,128)(2,1)S(1)...) custom-call(s32[8]{0:T(128)} %lengths_hbm.1, bf16[32,1280]{1,0:T(8,128)(2,1)S(1)} %bitcast.9, ...), custom_call_target="tpu_custom_call" | custom-call | flops 234881024 | bytes 7340032 | tf_op jit(solution)/shard_map/project/pallas_call | solution.py:160
  9.5 0.0 copy-start.5
  9.5 0.1 collective-permute-start
  9.6 0.5 %collective-permute-start.4 = (bf16[128,128]{1,0:T(8,128)(2,1)S(1)}, bf16[128,128]{1,0:T(8,128)(2,1)S(1)}, u32[]{:S(2)}, u32[]{:S(2)}) collective-permute-start(bf16[128,128]{1,0:T(8,128)(2,1)S(1)} %get-tuple-element.24), channel_id=1, source_target_pairs={{0,1},{1,0},{2,3},{3,2},{4,5},{5,4},{6,7},{7,6},{8,9},{9,8},{10,11... | collective-permute-start | bytes 98312 | tf_op jit(solution)/shard_map/ppermute | solution.py:27
  10.1 0.7 %collective-permute-done.refs_7_.refs_1_ = bf16[128,128]{1,0:T(8,128)(2,1)S(1)} collective-permute-done((bf16[128,128]{1,0:T(8,128)(2,1)S(1)}, bf16[128,128]{1,0:T(8,128)(2,1)S(1)}, u32[]{:S(2)}, u32[]{:S(2)}) %collective-permute-start) | collective-permute-done | bytes 32800 | tf_op jit(solution)/shard_map/ppermute | solution.py:27
  10.8 0.2 collective-permute-done.4.refs_8_
  10.9 0.0 collective-permute-done.3.refs_6_
  10.9 1.0 %collective-permute-done.2.refs_5_ = bf16[224,128]{1,0:T(8,128)(2,1)S(1)} collective-permute-done((bf16[224,128]{1,0:T(8,128)(2,1)S(1)}, bf16[224,128]{1,0:T(8,128)(2,1)S(1)}, u32[]{:S(2)}, u32[]{:S(2)}) %collective-permute-start.2) | collective-permute-done | bytes 57376 | tf_op jit(solution)/shard_map/ppermute | solution.py:27
  11.9 0.0 collective-permute-done.1.refs_4_
  11.9 0.0 copy-done.4
  11.9 0.9 %route.1 = (bf16[96,128]{1,0:T(8,128)(2,1)S(1)}, bf16[96,128]{1,0:T(8,128)(2,1)S(1)}, bf16[224,128]{1,0:T(8,128)(2,1)S(1)}, bf16[96,128]{1,0:T(8,128)(2,1)S(1)}) custom-call(s32[4]{0:T(128)S(1)} %copy-done.4, bf16[32,1280]{1,0:T(8,128)(2,1)S(1)} %bitcast.10, f32[2,32,512]{2,1,0:T(8,128)S(1)} %get-tuple-element.20.refs_2_.refs_0_, ...), custom_call_target="tpu_custom_call" | custom-call | bytes 800000 | tf_op jit(solution)/shard_map/route/pallas_call | solution.py:322
  12.8 1.5 %collective-permute-start.6 = (bf16[224,128]{1,0:T(8,128)(2,1)S(1)}, bf16[224,128]{1,0:T(8,128)(2,1)S(1)}, u32[]{:S(2)}, u32[]{:S(2)}) collective-permute-start(bf16[224,128]{1,0:T(8,128)(2,1)S(1)} %get-tuple-element.32), channel_id=1, source_target_pairs={{0,2},{1,3},{2,0},{3,1},{4,6},{5,7},{6,4},{7,5},{8,10},{9,11},{10,... | collective-permute-start | bytes 172040 | tf_op jit(solution)/shard_map/ppermute | solution.py:27
  14.4 0.0 collective-permute-start.5
  14.4 0.6 %collective-permute-start.7 = (bf16[96,128]{1,0:T(8,128)(2,1)S(1)}, bf16[96,128]{1,0:T(8,128)(2,1)S(1)}, u32[]{:S(2)}, u32[]{:S(2)}) collective-permute-start(bf16[96,128]{1,0:T(8,128)(2,1)S(1)} %get-tuple-element.33), channel_id=1, source_target_pairs={{0,1},{1,0},{2,3},{3,2},{4,5},{5,4},{6,7},{7,6},{8,9},{9,8},{10,11... | collective-permute-start | bytes 73736 | tf_op jit(solution)/shard_map/ppermute | solution.py:27
  15.0 0.0 copy-done.1
  15.0 1.4 %attend.1 = (f32[512,128]{1,0:T(8,128)S(1)}, f32[512,128]{1,0:T(8,128)S(1)}, f32[512,128]{1,0:T(8,128)S(1)}) custom-call(s32[8]{0:T(128)} %lengths_hbm.1, f32[512,512]{1,0:T(8,128)S(1)} %get-tuple-element.23.scores_ref, bf16[8,512,256]{2,1,0:T(8,128)(2,1)S(1)} %copy-done.1, bf16[96,128]{1,0:T(8,128)(2,1)S(1)} %get-tuple-element.25._.refs_12_), custom_call_target="tpu_custom_call" | custom-call | flops 67108864 | bytes 2097152 | tf_op jit(solution)/shard_map/attend/pallas_call | solution.py:233
  16.4 1.3 %collective-permute-done.5.refs_9_ = bf16[96,128]{1,0:T(8,128)(2,1)S(1)} collective-permute-done((bf16[96,128]{1,0:T(8,128)(2,1)S(1)}, bf16[96,128]{1,0:T(8,128)(2,1)S(1)}, u32[]{:S(2)}, u32[]{:S(2)}) %collective-permute-start.5) | collective-permute-done | bytes 24608 | tf_op jit(solution)/shard_map/ppermute | solution.py:27
  17.6 0.0 collective-permute-done.7.refs_11_
  17.6 0.0 collective-permute-done.6.refs_10_
  17.6 0.0 copy-done.5
  17.6 1.6 %finish.1 = (bf16[32,2048]{1,0:T(8,128)(2,1)}, bf16[32,256]{1,0:T(8,128)(2,1)}, bf16[32,256]{1,0:T(8,128)(2,1)}) custom-call(f32[2,32,512]{2,1,0:T(8,128)S(1)} %get-tuple-element.20.refs_2_.refs_0_, bf16[128,128]{1,0:T(8,128)(2,1)S(1)} %collective-permute-done.refs_7_.refs_1_, f32[1,128]{1,0:T(1,128)S(1)} %bitcast.12, ...), custom_call_target="tpu_custom_call" | custom-call | bytes 1000000 | tf_op jit(solution)/shard_map/finish/pallas_call | solution.py:454
  (1 shorter events, 0.0 us)
Async XLA Ops:
  0.6 6.9 %slice-start = ((s8[5242880]{0:T(1024)(128)(4,1)}), s8[4194304]{0:T(1024)(128)(4,1)S(1)}, s32[]{:S(2)}) async-start(s8[5242880]{0:T(1024)(128)(4,1)} %bitcast.7), calls=%async_computation | async-start | bytes 8388608
  0.6 6.9 %slice-start.1 = ((s8[5242880]{0:T(1024)(128)(4,1)}), s8[1048576]{0:T(1024)(128)(4,1)S(1)}, s32[]{:S(2)}) async-start(s8[5242880]{0:T(1024)(128)(4,1)} %bitcast.7), calls=%async_computation.1 | async-start | bytes 2097152
  0.7 6.9 %copy-start = (bf16[8,512,256]{2,1,0:T(8,128)(2,1)S(1)}, bf16[8,512,256]{2,1,0:T(8,128)(2,1)}, u32[]{:S(2)}) copy-start(bf16[8,512,256]{2,1,0:T(8,128)(2,1)} %refs_4_.1) | copy-start | bytes 6291460
  0.7 6.8 %copy-start.2 = (bf16[4,8,1280]{2,1,0:T(8,128)(2,1)S(1)}, bf16[4,8,1280]{2,1,0:T(8,128)(2,1)}, u32[]{:S(2)}) copy-start(bf16[4,8,1280]{2,1,0:T(8,128)(2,1)} %param.10) | copy-start | bytes 245764
  0.7 6.8 %copy-start.3 = (bf16[4,8,2048]{2,1,0:T(8,128)(2,1)S(1)}, bf16[4,8,2048]{2,1,0:T(8,128)(2,1)}, u32[]{:S(2)}) copy-start(bf16[4,8,2048]{2,1,0:T(8,128)(2,1)} %param.15) | copy-start | bytes 393220
  1.7 9.2 %collective-permute-start.3 = (bf16[224,128]{1,0:T(8,128)(2,1)S(1)}, bf16[224,128]{1,0:T(8,128)(2,1)S(1)}, u32[]{:S(2)}, u32[]{:S(2)}) collective-permute-start(bf16[224,128]{1,0:T(8,128)(2,1)S(1)} %pack.1.refs_5_.refs_3_), channel_id=1, source_target_pairs={{0,12},{4,8},{8,4},{12,0},{1,13},{5,9},{9,5},{13,1},{2,14},{6,10},... | collective-permute-start | bytes 172040 | tf_op jit(solution)/shard_map/ppermute | solution.py:27
  6.9 5.1 %collective-permute-start.2 = (bf16[224,128]{1,0:T(8,128)(2,1)S(1)}, bf16[224,128]{1,0:T(8,128)(2,1)S(1)}, u32[]{:S(2)}, u32[]{:S(2)}) collective-permute-start(bf16[224,128]{1,0:T(8,128)(2,1)S(1)} %pack.1.refs_5_.refs_3_), channel_id=1, source_target_pairs={{0,8},{4,12},{8,0},{12,4},{1,9},{5,13},{9,1},{13,5},{2,10},{6,14},... | collective-permute-start | bytes 172040 | tf_op jit(solution)/shard_map/ppermute | solution.py:27
  6.9 5.1 %collective-permute-start.1 = (bf16[224,128]{1,0:T(8,128)(2,1)S(1)}, bf16[224,128]{1,0:T(8,128)(2,1)S(1)}, u32[]{:S(2)}, u32[]{:S(2)}) collective-permute-start(bf16[224,128]{1,0:T(8,128)(2,1)S(1)} %pack.1.refs_5_.refs_3_), channel_id=1, source_target_pairs={{0,4},{4,0},{8,12},{12,8},{1,5},{5,1},{9,13},{13,9},{2,6},{6,2},{1... | collective-permute-start | bytes 172040 | tf_op jit(solution)/shard_map/ppermute | solution.py:27
  7.5 4.4 %copy-start.4 = (s32[4]{0:T(128)S(1)}, s32[4]{0:T(128)}, u32[]{:S(2)}) copy-start(s32[4]{0:T(128)} %refs_0_.3) | copy-start | bytes 52
  7.5 7.4 %copy-start.1 = (bf16[8,512,256]{2,1,0:T(8,128)(2,1)S(1)}, bf16[8,512,256]{2,1,0:T(8,128)(2,1)}, u32[]{:S(2)}) copy-start(bf16[8,512,256]{2,1,0:T(8,128)(2,1)} %values_ref.1) | copy-start | bytes 6291460
  9.5 8.1 %copy-start.5 = (f32[128]{0:T(128)S(1)}, f32[128]{0:T(128)}, u32[]{:S(2)}) copy-start(f32[128]{0:T(128)} %param.14) | copy-start | bytes 1540
  9.5 1.3 %collective-permute-start = (bf16[128,128]{1,0:T(8,128)(2,1)S(1)}, bf16[128,128]{1,0:T(8,128)(2,1)S(1)}, u32[]{:S(2)}, u32[]{:S(2)}) collective-permute-start(bf16[128,128]{1,0:T(8,128)(2,1)S(1)} %get-tuple-element.21), channel_id=1, source_target_pairs={{0,1},{1,0},{2,3},{3,2},{4,5},{5,4},{6,7},{7,6},{8,9},{9,8},{10,11... | collective-permute-start | bytes 98312 | tf_op jit(solution)/shard_map/ppermute | solution.py:27
  9.6 1.4 %collective-permute-start.4 = (bf16[128,128]{1,0:T(8,128)(2,1)S(1)}, bf16[128,128]{1,0:T(8,128)(2,1)S(1)}, u32[]{:S(2)}, u32[]{:S(2)}) collective-permute-start(bf16[128,128]{1,0:T(8,128)(2,1)S(1)} %get-tuple-element.24), channel_id=1, source_target_pairs={{0,1},{1,0},{2,3},{3,2},{4,5},{5,4},{6,7},{7,6},{8,9},{9,8},{10,11... | collective-permute-start | bytes 98312 | tf_op jit(solution)/shard_map/ppermute | solution.py:27
  12.8 4.8 %collective-permute-start.6 = (bf16[224,128]{1,0:T(8,128)(2,1)S(1)}, bf16[224,128]{1,0:T(8,128)(2,1)S(1)}, u32[]{:S(2)}, u32[]{:S(2)}) collective-permute-start(bf16[224,128]{1,0:T(8,128)(2,1)S(1)} %get-tuple-element.32), channel_id=1, source_target_pairs={{0,2},{1,3},{2,0},{3,1},{4,6},{5,7},{6,4},{7,5},{8,10},{9,11},{10,... | collective-permute-start | bytes 172040 | tf_op jit(solution)/shard_map/ppermute | solution.py:27
  14.4 3.3 %collective-permute-start.5 = (bf16[96,128]{1,0:T(8,128)(2,1)S(1)}, bf16[96,128]{1,0:T(8,128)(2,1)S(1)}, u32[]{:S(2)}, u32[]{:S(2)}) collective-permute-start(bf16[96,128]{1,0:T(8,128)(2,1)S(1)} %get-tuple-element.31), channel_id=1, source_target_pairs={{0,3},{1,2},{2,1},{3,0},{4,7},{5,6},{6,5},{7,4},{8,11},{9,10},{10,... | collective-permute-start | bytes 73736 | tf_op jit(solution)/shard_map/ppermute | solution.py:27
  14.4 3.3 %collective-permute-start.7 = (bf16[96,128]{1,0:T(8,128)(2,1)S(1)}, bf16[96,128]{1,0:T(8,128)(2,1)S(1)}, u32[]{:S(2)}, u32[]{:S(2)}) collective-permute-start(bf16[96,128]{1,0:T(8,128)(2,1)S(1)} %get-tuple-element.33), channel_id=1, source_target_pairs={{0,1},{1,0},{2,3},{3,2},{4,5},{5,4},{6,7},{7,6},{8,9},{9,8},{10,11... | collective-permute-start | bytes 73736 | tf_op jit(solution)/shard_map/ppermute | solution.py:27

commit v9 on v8

--- a/solution.py
+++ b/solution.py
@@ -25,6 +25,11 @@
 def swap(block, axis, offset):
     count = lax.axis_size(axis)
     return lax.ppermute(block, axis, [(s, s ^ offset) for s in range(count)])
+
+
+def shift(block, axis, offset):
+    count = lax.axis_size(axis)
+    return lax.ppermute(block, axis, [((s + offset) % count, s) for s in range(count)])
 
 
 def in_hbm(*arrays):
@@ -86,14 +91,16 @@
     )(*in_hbm(down, up))
 
 
-def project_kernel(step_count, head_count, shards, *refs):
-    lengths_hbm, tokens_ref, weight_ref, queries_ref, keys_ref, _ = refs[:6]
+def project_kernel(step_count, head_count, shards, replicas, *refs):
+    lengths_hbm, owners_hbm, tokens_ref, weight_ref, queries_ref, keys_ref, _ = refs[:7]
     pairs = shards // 2
-    near_refs = refs[6 : 6 + pairs]
-    kept_ref, grouped_ref, scores_ref, cosine_ref, sine_ref = refs[6 + pairs : 11 + pairs]
-    lengths_ref, regroup, length_sem = refs[11 + pairs :]
-    lengths_copy = pltpu.make_async_copy(lengths_hbm, lengths_ref, length_sem)
+    near_refs = refs[7 : 7 + pairs]
+    kept_ref, grouped_ref, scores_ref, cosine_ref, sine_ref, left_ref = refs[7 + pairs : 13 + pairs]
+    lengths_ref, owners_ref, regroup, token_buf, sems = refs[13 + pairs :]
+    lengths_copy = pltpu.make_async_copy(lengths_hbm, lengths_ref, sems.at[0])
+    owners_copy = pltpu.make_async_copy(owners_hbm, owners_ref, sems.at[1])
     lengths_copy.start()
+    owners_copy.start()
 
     row_count = keys_ref.shape[0]
     group = queries_ref.shape[1] // (head_count * lanes)
@@ -109,7 +116,14 @@
                 regroup[pl.ds(first, row_count, stride=seen), :] = both[
                     side * row_count : (side + 1) * row_count, :
                 ]
-    grouped_ref[...] = regroup[...].astype(bf16)
+            if g % 2:
+                for side in range(2):
+                    half = slice(side * row_count, (side + 1) * row_count)
+                    last = (h * seen + (pair * 2 + side) * group + g + 1) * row_count
+                    grouped_ref[last - 2 * row_count : last, :] = jnp.concatenate(
+                        [before[half], both[half]], axis=0
+                    ).astype(bf16)
+            before = both
 
     shard = lax.axis_index("tensor")
     _, rows, own = kept_ref.shape
@@ -130,7 +144,7 @@
         for h in range(head_count):
             at = (h * row_count + b) * seen
             scores_ref[at : at + seen, :] = lax.dot_general(
-                grouped_ref[at : at + seen, :],
+                regroup[at : at + seen, :].astype(bf16),
                 keys_ref[b, :, h * lanes : (h + 1) * lanes],
                 (((1,), (1,)), ((), ())),
                 preferred_element_type=f32,
@@ -149,16 +163,33 @@
     sine = jnp.sin(angles)
     sine_ref[...] = jnp.where(lane < middle, -sine, sine)
 
-
-def project(lengths, tokens, weight, queries, keys, after, step_count, shards):
+    owners_copy.wait()
+    width = token_buf.shape[2]
+    down_rows = tokens_ref.shape[1] // replicas
+    for k in range(replicas):
+        token_buf[k, :, :down_rows] = tokens_ref[:, k * down_rows : (k + 1) * down_rows]
+        if down_rows < width:
+            token_buf[k, :, down_rows:] = jnp.zeros((rows, width - down_rows), bf16)
+    for i in range(replicas):
+        source = lax.rem(lax.axis_index("rollout") + i, replicas)
+        place = jnp.int32(0)
+        for k in range(1, replicas):
+            place = place + jnp.where(owners_ref[k] == source, k, 0)
+        left_ref[:, i * width : (i + 1) * width] = token_buf[place]
+
+
+def project(
+    lengths, owners, tokens, weight, queries, keys, after, step_count, shards, replicas
+):
     rows, depth = tokens.shape
     own = weight.shape[1] // shards
     pairs = shards // 2
     row_count, slots, width = keys.shape
     seen_rows = rows * queries.shape[1] // lanes
     table = jax.ShapeDtypeStruct((rows, lanes), f32)
+    piece_width = -(-depth // replicas // lanes) * lanes
     outs = pl.pallas_call(
-        functools.partial(project_kernel, step_count, width // lanes, shards),
+        functools.partial(project_kernel, step_count, width // lanes, shards, replicas),
         out_shape=[jax.ShapeDtypeStruct((rows * own // lanes, lanes), bf16)] * pairs
         + [
             jax.ShapeDtypeStruct((pairs, rows, own), f32),
@@ -166,13 +197,16 @@
             jax.ShapeDtypeStruct((seen_rows, slots), f32),
             table,
             table,
-        ],
-        in_specs=[stays_in_hbm] + [whole_in_vmem] * 5,
-        out_specs=[whole_in_vmem] * (pairs + 5),
+            jax.ShapeDtypeStruct((rows, replicas * piece_width), bf16),
+        ],
+        in_specs=[stays_in_hbm] * 2 + [whole_in_vmem] * 5,
+        out_specs=[whole_in_vmem] * (pairs + 6),
         scratch_shapes=[
             pltpu.SMEM(lengths.shape, jnp.int32),
+            pltpu.SMEM(owners.shape, jnp.int32),
             pltpu.VMEM((seen_rows, lanes), f32),
-            pltpu.SemaphoreType.DMA,
+            pltpu.VMEM((replicas, rows, piece_width), bf16),
+            pltpu.SemaphoreType.DMA((2,)),
         ],
         compiler_params=pltpu.CompilerParams(vmem_limit_bytes=6 * 2**20),
         name="project",
@@ -181,7 +215,7 @@
             bytes_accessed=2 * (weight.size + keys.size),
             transcendentals=0,
         ),
-    )(*in_hbm(lengths), tokens, weight, queries, keys, after)
+    )(*in_hbm(lengths, owners), tokens, weight, queries, keys, after)
     return outs[:pairs], *outs[pairs:]
 
 
@@ -203,23 +237,28 @@
     row_count, slots, _ = values_ref.shape
     seen = scores_ref.shape[0] // (head_count * row_count)
     places = [
-        (b, h, slice((h * row_count + b) * seen, (h * row_count + b + 1) * seen))
+        (
+            b,
+            h,
+            slice((h * row_count + b) * seen, (h * row_count + b + 1) * seen),
+            pl.ds(h * row_count * seen + b, seen, stride=row_count),
+        )
         for b in range(row_count)
         for h in range(head_count)
     ]
     lengths_copy.wait()
     slot = lax.broadcasted_iota(jnp.int32, (seen, slots), 1)
-    for b, h, place in places:
+    for b, h, place, out in places:
         score = jnp.where(slot < lengths_ref[b], scores_ref[place, :], masked_score)
         peak = jnp.max(score, axis=1, keepdims=True)
         lifted = jnp.exp2((score - peak) * exponent_scale)
         raised[place, :] = lifted.astype(bf16)
-        peak_ref[place, :] = jnp.broadcast_to(peak, (seen, lanes))
-        sum_ref[place, :] = jnp.broadcast_to(
+        peak_ref[out, :] = jnp.broadcast_to(peak, (seen, lanes))
+        sum_ref[out, :] = jnp.broadcast_to(
             jnp.sum(lifted, axis=1, keepdims=True), (seen, lanes)
         )
-    for b, h, place in places:
-        total_ref[place, :] = jnp.dot(
+    for b, h, place, out in places:
+        total_ref[out, :] = jnp.dot(
             raised[place, :],
             values_ref[b, :, h * lanes : (h + 1) * lanes],
             preferred_element_type=f32,
@@ -263,46 +302,40 @@
 
 
 def route_kernel(replicas, shards, *refs):
-    owners_ref, tokens_ref, kept_ref = refs[:3]
+    owners_hbm, left_ref, kept_ref = refs[:3]
     piece_refs = refs[3 : 3 + replicas]
     near_refs = refs[3 + replicas : 3 + replicas + shards // 2]
     out_refs = refs[3 + replicas + shards // 2 : 3 + replicas + shards // 2 + shards]
-    token_buf, left, right, up_buf = refs[3 + replicas + shards // 2 + shards :]
-    replica = lax.axis_index("rollout")
-    shard = lax.axis_index("tensor")
-    rows, depth = tokens_ref.shape
+    owners_ref, right, up_buf, owner_sem = refs[3 + replicas + shards // 2 + shards :]
+    owners_copy = pltpu.make_async_copy(owners_hbm, owners_ref, owner_sem)
+    owners_copy.start()
+    rows = left_ref.shape[0]
     rank = right.shape[0]
-    down_rows = depth // replicas
-    width = token_buf.shape[2]
-    rest = down_rows % lanes
-    for k in range(replicas):
-        token_buf[k, :, :down_rows] = tokens_ref[:, k * down_rows : (k + 1) * down_rows]
-        if rest:
-            token_buf[k, :, down_rows:] = jnp.zeros((rows, width - down_rows), bf16)
+    width = right.shape[1] // replicas
+    half = rank // 2
+    rest = (piece_refs[0].shape[0] - up_buf.shape[1]) % rank
     for i in range(replicas):
-        source = replica ^ i
-        place = jnp.int32(0)
-        for k in range(1, replicas):
-            place = place + jnp.where(owners_ref[k] == source, k, 0)
-        left[:, i * width : (i + 1) * width] = token_buf[place]
         first = 0
-        for c in range(down_rows // lanes):
+        for c in range(width // lanes - (1 if rest else 0)):
             right[:, i * width + c * lanes : i * width + (c + 1) * lanes] = piece_refs[i][
                 first : first + rank, :
             ]
             first += rank
         if rest:
-            both = piece_refs[i][first : first + rank // 2, :]
-            tail = jnp.concatenate([both[:, :rest], both[:, rest:]], axis=0)
+            both = piece_refs[i][first : first + half, :]
+            tail = jnp.concatenate([both[:, : lanes // 2], both[:, lanes // 2 :]], axis=0)
             right[:, (i + 1) * width - lanes : (i + 1) * width] = jnp.concatenate(
-                [tail, jnp.zeros((rank, lanes - rest), bf16)], axis=1
+                [tail, jnp.zeros((rank, lanes // 2), bf16)], axis=1
             )
-            first += rank // 2
+            first += half
         up_buf[i] = piece_refs[i][first:, :]
     lowered = lax.dot_general(
-        left[...], right[...], (((1,), (1,)), ((), ())), preferred_element_type=f32
+        left_ref[...], right[...], (((1,), (1,)), ((), ())), preferred_element_type=f32
     )
     both = jnp.concatenate(split_halves(lowered), axis=1)
+    replica = lax.axis_index("rollout")
+    shard = lax.axis_index("tensor")
+    owners_copy.wait()
     for i in range(shards):
         first = 0
         if carries_sums(i):
@@ -310,33 +343,33 @@
                 out_refs[i][first : first + rows, :] = block.astype(bf16)
                 first += rows
         out_refs[i][first : first + rows, :] = both
-        out_refs[i][first + rows :, :] = up_buf[owners_ref[shard ^ i] ^ replica]
-
-
-def route(owners, tokens, sums, pieces, rank, up_rows, shards):
-    rows, depth = tokens.shape
+        slot = lax.rem(owners_ref[shard ^ i] + replicas - replica, replicas)
+        out_refs[i][first + rows :, :] = up_buf[slot]
+
+
+def route(owners, left, sums, pieces, rank, up_rows, shards):
+    rows, depth = left.shape
     replicas = len(pieces)
     kept, near = sums
     sent = near[0].shape[0]
-    width = -(-depth // replicas // lanes) * lanes
     return pl.pallas_call(
         functools.partial(route_kernel, replicas, shards),
         out_shape=[
             jax.ShapeDtypeStruct(((sent if carries_sums(i) else 0) + rows + up_rows, lanes), bf16)
             for i in range(shards)
         ],
-        in_specs=[whole_in_smem] + [whole_in_vmem] * (2 + replicas + len(near)),
+        in_specs=[stays_in_hbm] + [whole_in_vmem] * (2 + replicas + len(near)),
         out_specs=[whole_in_vmem] * shards,
         scratch_shapes=[
-            pltpu.VMEM((replicas, rows, width), bf16),
-            pltpu.VMEM((rows, replicas * width), bf16),
-            pltpu.VMEM((rank, replicas * width), bf16),
+            pltpu.SMEM(owners.shape, jnp.int32),
+            pltpu.VMEM((rank, depth), bf16),
             pltpu.VMEM((replicas, up_rows, lanes), bf16),
+            pltpu.SemaphoreType.DMA,
         ],
         compiler_params=pltpu.CompilerParams(vmem_limit_bytes=4 * 2**20),
         name="route",
         cost_estimate=pl.CostEstimate(flops=0, bytes_accessed=800000, transcendentals=0),
-    )(owners, tokens, kept, *pieces, *near)
+    )(*in_hbm(owners), left, kept, *pieces, *near)
 
 
 def route_plain(owners, tokens, sums, down, up, rank_part, own, shards):
@@ -368,7 +401,7 @@
     cosine_ref, sine_ref = refs[7:9]
     packet_refs = refs[9 : 9 + shards][::-1]
     attention_ref, keys_ref, values_ref = refs[9 + shards : 12 + shards]
-    up_buf, ordered = refs[12 + shards :]
+    (up_buf,) = refs[12 + shards :]
     shard = lax.axis_index("tensor")
     rows = step_count * row_count
     own = kept_ref.shape[2]
@@ -403,44 +436,42 @@
     all_rows = row_count * seen
     seen_by = lax.broadcasted_iota(jnp.int32, (all_rows, rows), 0)
     made_by = lax.broadcasted_iota(jnp.int32, (all_rows, rows), 1)
-    visible = (seen_by // seen == made_by % row_count) & (
-        made_by // row_count <= seen_by % seen // group
-    )
-    for h in range(head_count):
+    visible = (seen_by % row_count == made_by % row_count) & (
+        made_by // row_count <= seen_by // (row_count * group)
+    )
+    heads = [(h, slice(h * all_rows, (h + 1) * all_rows)) for h in range(head_count)]
+    keys, values, scores, results = [], [], [], []
+    for h, _ in heads:
         raw_key = joined[2 * h]
         mean_square = jnp.mean(raw_key * raw_key, axis=1, keepdims=True)
         normed = raw_key * lax.rsqrt(mean_square + norm_eps) * gain_ref[...]
         key = normed * cosine_ref[...] + pltpu.roll(normed, lanes // 2, 1) * sine_ref[...]
-        key = key.astype(bf16)
-        value = joined[2 * h + 1].astype(bf16)
-        keys_ref[:, h * lanes : (h + 1) * lanes] = key
-        values_ref[:, h * lanes : (h + 1) * lanes] = value
-        mine = slice(h * all_rows, (h + 1) * all_rows)
+        keys.append(key.astype(bf16))
+        values.append(joined[2 * h + 1].astype(bf16))
+        keys_ref[:, h * lanes : (h + 1) * lanes] = keys[h]
+        values_ref[:, h * lanes : (h + 1) * lanes] = values[h]
+    for h, mine in heads:
         score = lax.dot_general(
-            grouped_ref[mine, :], key, (((1,), (1,)), ((), ())), preferred_element_type=f32
-        )
-        score = jnp.where(visible, score, masked_score)
+            grouped_ref[mine, :], keys[h], (((1,), (1,)), ((), ())), preferred_element_type=f32
+        )
+        scores.append(jnp.where(visible, score, masked_score))
+    for h, mine in heads:
         old_peak = peak_ref[mine, :]
-        peak = jnp.maximum(old_peak, jnp.max(score, axis=1, keepdims=True))
+        peak = jnp.maximum(old_peak, jnp.max(scores[h], axis=1, keepdims=True))
         fade = jnp.exp2((old_peak - peak) * exponent_scale)
-        lifted = jnp.exp2((score - peak[:, :rows]) * exponent_scale)
+        lifted = jnp.exp2((scores[h] - peak[:, :rows]) * exponent_scale)
         denominator = fade * sum_ref[mine, :] + jnp.sum(lifted, axis=1, keepdims=True)
         total = fade * total_ref[mine, :] + jnp.dot(
-            lifted.astype(bf16), value, preferred_element_type=f32
-        )
-        ordered[mine, :] = total / denominator
+            lifted.astype(bf16), values[h], preferred_element_type=f32
+        )
+        results.append(total / denominator)
     for pair in range(step_count // 2):
         for q in range(head_count * group):
             h, g = q // group, q % group
-            both = [
-                ordered[
-                    pl.ds(
-                        h * all_rows + (pair * 2 + side) * group + g, row_count, stride=seen
-                    ),
-                    :,
-                ]
-                for side in range(2)
-            ]
+            both = []
+            for side in range(2):
+                first = ((pair * 2 + side) * group + g) * row_count
+                both.append(results[h][first : first + row_count])
             attention_ref[
                 pair * 2 * row_count : (pair + 1) * 2 * row_count, q * lanes : (q + 1) * lanes
             ] = jnp.concatenate(both, axis=0).astype(bf16)
@@ -462,7 +493,6 @@
         out_specs=(whole_in_vmem,) * 3,
         scratch_shapes=[
             pltpu.VMEM((rank, own), f32),
-            pltpu.VMEM(total.shape, f32),
         ],
         compiler_params=pltpu.CompilerParams(vmem_limit_bytes=6 * 2**20),
         name="finish",
@@ -503,10 +533,10 @@
         fetched = 2 * (key_value_weight.size + cache_keys.size + stored_values.size)
         beside = pl.CostEstimate(flops=1000 * fetched, bytes_accessed=fetched, transcendentals=0)
         packed = pack(adapter_down.T, adapter_up, rank_part, beside)
-        arrived = {i: swap(packed, "rollout", i) for i in reversed(range(1, replicas))}
-        pieces = [packed] + [arrived[i] for i in range(1, replicas)]
-    near, kept, grouped, scores, cosine, sine = project(
+        pieces = [packed] + [shift(packed, "rollout", i) for i in range(1, replicas)]
+    near, kept, grouped, scores, cosine, sine, left = project(
         lengths,
+        owners,
         tokens,
         key_value_weight,
         query_rows,
@@ -514,11 +544,12 @@
         packed if fits else adapter_up,
         step_count,
         shards,
+        replicas if fits else 1,
     )
     near = [swap(block, "tensor", 1) for block in near]
     if fits:
         packets = route(
-            owners, tokens, (kept, near), pieces, rank, rank_part * own // lanes, shards
+            owners, left, (kept, near), pieces, rank, rank_part * own // lanes, shards
         )
     else:
         packets = route_plain(

time: 19.4 us -> 19.6 us (1.010)
  starting transfers between devices: 8.49 us -> 9.79 us
  waiting for transfers between devices: 3.11 us -> 2.16 us
  Pallas kernels: 6.82 us -> 6.59 us
    ppermute x0 -> x3, starting transfers between devices: none -> 7.01 us  [shift(): lax.ppermute(block, axis, [((s + offset) % count, s) for s in range(count)])]
    ppermute x8 -> x5, starting transfers between devices: 8.49 us -> 2.77 us  [swap(): return lax.ppermute(block, axis, [(s, s ^ offset) for s in range(count)])]
    ppermute x8 -> x5, waiting for transfers between devices: 3.11 us -> 2.15 us  [swap(): return lax.ppermute(block, axis, [(s, s ^ offset) for s in range(count)])]
  transfers between devices with their start and end apart: 8 -> 8, of which waited for: 4 -> 3; matrix products, arithmetic and copies ran while one was open for 0% -> 0% of each run, Pallas kernels for 17% -> 17%
where the time goes in v9:
time: 19.6 us; the launch traced here: 19.3 us
  starting transfers between devices  9.79 us (50%)
  Pallas kernels  6.59 us (34%)
  waiting for transfers between devices  2.16 us (11%)
  between operations  0.76 us (4%)
    ppermute x3, starting transfers between devices, shift(): lax.ppermute(block, axis, [((s + offset) % count, s) for s in range(count)])  7.01 us
    ppermute x5, starting transfers between devices, swap(): return lax.ppermute(block, axis, [(s, s ^ offset) for s in range(count)])  2.77 us
    ppermute x5, waiting for transfers between devices, swap(): return lax.ppermute(block, axis, [(s, s ^ offset) for s in range(count)])  2.15 us
    pallas_call x1, Pallas kernels, project(): pl.pallas_call(functools.partial(project_kernel, step_count, width // lan...  2.05 us
    pallas_call x1, Pallas kernels, finish(): pl.pallas_call(functools.partial(finish_kernel, step_count, row_count, he...  1.44 us
    pallas_call x1, Pallas kernels, attend(): pl.pallas_call(functools.partial(attend_kernel, width // lanes), out_shap...  1.32 us
    pallas_call x1, Pallas kernels, pack(): pl.pallas_call(pack_kernel, out_shape=jax.ShapeDtypeStruct((rows, lanes),...  1.05 us
    pallas_call x1, Pallas kernels, route(): pl.pallas_call(functools.partial(route_kernel, replicas, shards), out_sha...  0.74 us
  transfers between devices with their start and end apart: 8, of which 3 were waited for; matrix products, arithmetic and copies ran while one was open for 0% of the time, Pallas kernels for 17%

profile of v9, /device:TPU:0, one launch (start us, length us, event | category | flops | bytes accessed | tf_op | source)
XLA Modules:
  0.0 19.3 jit_solution(1482129859865156642)
XLA Ops:
  0.6 0.0 slice-start
  0.6 0.0 slice-start.1
  0.7 0.0 copy-start
  0.7 0.0 copy-start.2
  0.7 0.0 copy-start.3
  0.7 1.0 %pack.1.refs_6_.refs_3_ = bf16[224,128]{1,0:T(8,128)(2,1)S(1)} custom-call(bf16[64,320]{1,0:T(8,128)(2,1)} %bitcast.13, bf16[64,512]{1,0:T(8,128)(2,1)} %up_hbm.1), custom_call_target="tpu_custom_call" | custom-call | flops 9437184000 | bytes 9437184 | tf_op jit(solution)/shard_map/pack/pallas_call | solution.py:78
  1.7 3.1 %collective-permute-start.3 = (bf16[224,128]{1,0:T(8,128)(2,1)S(1)}, bf16[224,128]{1,0:T(8,128)(2,1)S(1)}, u32[]{:S(2)}, u32[]{:S(2)}) collective-permute-start(bf16[224,128]{1,0:T(8,128)(2,1)S(1)} %pack.1.refs_6_.refs_3_), channel_id=1, source_target_pairs={{12,0},{0,4},{4,8},{8,12},{13,1},{1,5},{5,9},{9,13},{14,2},{2,6},{... | collective-permute-start | bytes 172040 | tf_op jit(solution)/shard_map/ppermute | solution.py:32
  4.8 2.6 %collective-permute-start.2 = (bf16[224,128]{1,0:T(8,128)(2,1)S(1)}, bf16[224,128]{1,0:T(8,128)(2,1)S(1)}, u32[]{:S(2)}, u32[]{:S(2)}) collective-permute-start(bf16[224,128]{1,0:T(8,128)(2,1)S(1)} %pack.1.refs_6_.refs_3_), channel_id=1, source_target_pairs={{8,0},{12,4},{0,8},{4,12},{9,1},{13,5},{1,9},{5,13},{10,2},{14,6},... | collective-permute-start | bytes 172040 | tf_op jit(solution)/shard_map/ppermute | solution.py:32
  7.4 1.3 %collective-permute-start.1 = (bf16[224,128]{1,0:T(8,128)(2,1)S(1)}, bf16[224,128]{1,0:T(8,128)(2,1)S(1)}, u32[]{:S(2)}, u32[]{:S(2)}) collective-permute-start(bf16[224,128]{1,0:T(8,128)(2,1)S(1)} %pack.1.refs_6_.refs_3_), channel_id=1, source_target_pairs={{4,0},{8,4},{12,8},{0,12},{5,1},{9,5},{13,9},{1,13},{6,2},{10,6},{... | collective-permute-start | bytes 172040 | tf_op jit(solution)/shard_map/ppermute | solution.py:32
  8.8 0.0 slice-done
  8.8 0.0 slice-done.1
  8.8 0.0 copy-done
  8.8 0.0 copy-done.2
  8.8 0.0 copy-done.3
  8.8 0.0 copy-start.1
  8.8 2.1 %project.1 = (bf16[128,128]{1,0:T(8,128)(2,1)S(1)}, bf16[128,128]{1,0:T(8,128)(2,1)S(1)}, f32[2,32,512]{2,1,0:T(8,128)S(1)}, bf16[512,128]{1,0:T(8,128)(2,1)S(1)...) custom-call(s32[8]{0:T(128)} %lengths_hbm.1, ...), custom_call_target="tpu_custom_call" | custom-call | flops 234881024 | bytes 7340032 | tf_op jit(solution)/shard_map/project/pallas_call | solution.py:191
  10.9 0.0 copy-start.4
  10.9 0.1 collective-permute-start
  11.0 0.5 %collective-permute-start.4 = (bf16[128,128]{1,0:T(8,128)(2,1)S(1)}, bf16[128,128]{1,0:T(8,128)(2,1)S(1)}, u32[]{:S(2)}, u32[]{:S(2)}) collective-permute-start(bf16[128,128]{1,0:T(8,128)(2,1)S(1)} %get-tuple-element.26), channel_id=1, source_target_pairs={{0,1},{1,0},{2,3},{3,2},{4,5},{5,4},{6,7},{7,6},{8,9},{9,8},{10,11... | collective-permute-start | bytes 98312 | tf_op jit(solution)/shard_map/ppermute | solution.py:27
  11.4 0.7 %collective-permute-done.refs_7_.refs_1_ = bf16[128,128]{1,0:T(8,128)(2,1)S(1)} collective-permute-done((bf16[128,128]{1,0:T(8,128)(2,1)S(1)}, bf16[128,128]{1,0:T(8,128)(2,1)S(1)}, u32[]{:S(2)}, u32[]{:S(2)}) %collective-permute-start) | collective-permute-done | bytes 32800 | tf_op jit(solution)/shard_map/ppermute | solution.py:27
  12.1 0.2 collective-permute-done.4.refs_8_
  12.3 0.0 collective-permute-done.3.refs_6_
  12.3 0.0 collective-permute-done.2.refs_5_
  12.3 0.0 collective-permute-done.1.refs_4_
  12.3 0.7 %route.1 = (bf16[96,128]{1,0:T(8,128)(2,1)S(1)}, bf16[96,128]{1,0:T(8,128)(2,1)S(1)}, bf16[224,128]{1,0:T(8,128)(2,1)S(1)}, bf16[96,128]{1,0:T(8,128)(2,1)S(1)}) custom-call(s32[4]{0:T(128)} %refs_0_.3, bf16[32,1536]{1,0:T(8,128)(2,1)S(1)} %get-tuple-element.25.refs_1_, f32[2,32,512]{2,1,0:T(8,128)S(1)} %get-tuple-element.21.refs_2_.refs_0_, ...), custom_call_target="tpu_custom_call" | custom-call | bytes 800000 | tf_op jit(solution)/shard_map/route/pallas_call | solution.py:355
  13.1 1.6 %collective-permute-start.6 = (bf16[224,128]{1,0:T(8,128)(2,1)S(1)}, bf16[224,128]{1,0:T(8,128)(2,1)S(1)}, u32[]{:S(2)}, u32[]{:S(2)}) collective-permute-start(bf16[224,128]{1,0:T(8,128)(2,1)S(1)} %get-tuple-element.34), channel_id=1, source_target_pairs={{0,2},{1,3},{2,0},{3,1},{4,6},{5,7},{6,4},{7,5},{8,10},{9,11},{10,... | collective-permute-start | bytes 172040 | tf_op jit(solution)/shard_map/ppermute | solution.py:27
  14.6 0.2 %collective-permute-start.5 = (bf16[96,128]{1,0:T(8,128)(2,1)S(1)}, bf16[96,128]{1,0:T(8,128)(2,1)S(1)}, u32[]{:S(2)}, u32[]{:S(2)}) collective-permute-start(bf16[96,128]{1,0:T(8,128)(2,1)S(1)} %get-tuple-element.33), channel_id=1, source_target_pairs={{0,3},{1,2},{2,1},{3,0},{4,7},{5,6},{6,5},{7,4},{8,11},{9,10},{10,... | collective-permute-start | bytes 73736 | tf_op jit(solution)/shard_map/ppermute | solution.py:27
  14.8 0.4 %collective-permute-start.7 = (bf16[96,128]{1,0:T(8,128)(2,1)S(1)}, bf16[96,128]{1,0:T(8,128)(2,1)S(1)}, u32[]{:S(2)}, u32[]{:S(2)}) collective-permute-start(bf16[96,128]{1,0:T(8,128)(2,1)S(1)} %get-tuple-element.35), channel_id=1, source_target_pairs={{0,1},{1,0},{2,3},{3,2},{4,5},{5,4},{6,7},{7,6},{8,9},{9,8},{10,11... | collective-permute-start | bytes 73736 | tf_op jit(solution)/shard_map/ppermute | solution.py:27
  15.3 0.0 copy-done.1
  15.3 1.3 %attend.1 = (f32[512,128]{1,0:T(8,128)S(1)}, f32[512,128]{1,0:T(8,128)S(1)}, f32[512,128]{1,0:T(8,128)S(1)}) custom-call(s32[8]{0:T(128)} %lengths_hbm.1, f32[512,512]{1,0:T(8,128)S(1)} %get-tuple-element.24.scores_ref, bf16[8,512,256]{2,1,0:T(8,128)(2,1)S(1)} %copy-done.1, bf16[96,128]{1,0:T(8,128)(2,1)S(1)} %get-tuple-element.27._.refs_12_), custom_call_target="tpu_custom_call" | custom-call | flops 67108864 | bytes 2097152 | tf_op jit(solution)/shard_map/attend/pallas_call | solution.py:272
  16.6 1.3 %collective-permute-done.5.refs_9_ = bf16[96,128]{1,0:T(8,128)(2,1)S(1)} collective-permute-done((bf16[96,128]{1,0:T(8,128)(2,1)S(1)}, bf16[96,128]{1,0:T(8,128)(2,1)S(1)}, u32[]{:S(2)}, u32[]{:S(2)}) %collective-permute-start.5) | collective-permute-done | bytes 24608 | tf_op jit(solution)/shard_map/ppermute | solution.py:27
  17.9 0.0 collective-permute-done.7.refs_11_
  17.9 0.0 collective-permute-done.6.refs_10_
  17.9 0.0 copy-done.4
  17.9 1.4 %finish.1 = (bf16[32,2048]{1,0:T(8,128)(2,1)}, bf16[32,256]{1,0:T(8,128)(2,1)}, bf16[32,256]{1,0:T(8,128)(2,1)}) custom-call(f32[2,32,512]{2,1,0:T(8,128)S(1)} %get-tuple-element.21.refs_2_.refs_0_, bf16[128,128]{1,0:T(8,128)(2,1)S(1)} %collective-permute-done.refs_7_.refs_1_, f32[1,128]{1,0:T(1,128)S(1)} %bitcast.11, ...), custom_call_target="tpu_custom_call" | custom-call | bytes 1000000 | tf_op jit(solution)/shard_map/finish/pallas_call | solution.py:485
  (1 shorter events, 0.0 us)
Async XLA Ops:
  0.6 8.1 %slice-start = ((s8[5242880]{0:T(1024)(128)(4,1)}), s8[4194304]{0:T(1024)(128)(4,1)S(1)}, s32[]{:S(2)}) async-start(s8[5242880]{0:T(1024)(128)(4,1)} %bitcast.7), calls=%async_computation | async-start | bytes 8388608
  0.6 8.1 %slice-start.1 = ((s8[5242880]{0:T(1024)(128)(4,1)}), s8[1048576]{0:T(1024)(128)(4,1)S(1)}, s32[]{:S(2)}) async-start(s8[5242880]{0:T(1024)(128)(4,1)} %bitcast.7), calls=%async_computation.1 | async-start | bytes 2097152
  0.7 8.1 %copy-start = (bf16[8,512,256]{2,1,0:T(8,128)(2,1)S(1)}, bf16[8,512,256]{2,1,0:T(8,128)(2,1)}, u32[]{:S(2)}) copy-start(bf16[8,512,256]{2,1,0:T(8,128)(2,1)} %refs_5_.1) | copy-start | bytes 6291460
  0.7 8.1 %copy-start.2 = (bf16[4,8,2048]{2,1,0:T(8,128)(2,1)S(1)}, bf16[4,8,2048]{2,1,0:T(8,128)(2,1)}, u32[]{:S(2)}) copy-start(bf16[4,8,2048]{2,1,0:T(8,128)(2,1)} %param.15) | copy-start | bytes 393220
  0.7 8.1 %copy-start.3 = (bf16[4,8,1280]{2,1,0:T(8,128)(2,1)S(1)}, bf16[4,8,1280]{2,1,0:T(8,128)(2,1)}, u32[]{:S(2)}) copy-start(bf16[4,8,1280]{2,1,0:T(8,128)(2,1)} %param.10) | copy-start | bytes 245764
  1.7 10.6 %collective-permute-start.3 = (bf16[224,128]{1,0:T(8,128)(2,1)S(1)}, bf16[224,128]{1,0:T(8,128)(2,1)S(1)}, u32[]{:S(2)}, u32[]{:S(2)}) collective-permute-start(bf16[224,128]{1,0:T(8,128)(2,1)S(1)} %pack.1.refs_6_.refs_3_), channel_id=1, source_target_pairs={{12,0},{0,4},{4,8},{8,12},{13,1},{1,5},{5,9},{9,13},{14,2},{2,6},{... | collective-permute-start | bytes 172040 | tf_op jit(solution)/shard_map/ppermute | solution.py:32
  4.8 7.5 %collective-permute-start.2 = (bf16[224,128]{1,0:T(8,128)(2,1)S(1)}, bf16[224,128]{1,0:T(8,128)(2,1)S(1)}, u32[]{:S(2)}, u32[]{:S(2)}) collective-permute-start(bf16[224,128]{1,0:T(8,128)(2,1)S(1)} %pack.1.refs_6_.refs_3_), channel_id=1, source_target_pairs={{8,0},{12,4},{0,8},{4,12},{9,1},{13,5},{1,9},{5,13},{10,2},{14,6},... | collective-permute-start | bytes 172040 | tf_op jit(solution)/shard_map/ppermute | solution.py:32
  7.4 4.9 %collective-permute-start.1 = (bf16[224,128]{1,0:T(8,128)(2,1)S(1)}, bf16[224,128]{1,0:T(8,128)(2,1)S(1)}, u32[]{:S(2)}, u32[]{:S(2)}) collective-permute-start(bf16[224,128]{1,0:T(8,128)(2,1)S(1)} %pack.1.refs_6_.refs_3_), channel_id=1, source_target_pairs={{4,0},{8,4},{12,8},{0,12},{5,1},{9,5},{13,9},{1,13},{6,2},{10,6},{... | collective-permute-start | bytes 172040 | tf_op jit(solution)/shard_map/ppermute | solution.py:32
  8.8 6.5 %copy-start.1 = (bf16[8,512,256]{2,1,0:T(8,128)(2,1)S(1)}, bf16[8,512,256]{2,1,0:T(8,128)(2,1)}, u32[]{:S(2)}) copy-start(bf16[8,512,256]{2,1,0:T(8,128)(2,1)} %values_ref.1) | copy-start | bytes 6291460
  10.9 7.0 %copy-start.4 = (f32[128]{0:T(128)S(1)}, f32[128]{0:T(128)}, u32[]{:S(2)}) copy-start(f32[128]{0:T(128)} %param.14) | copy-start | bytes 1540
  10.9 1.3 %collective-permute-start = (bf16[128,128]{1,0:T(8,128)(2,1)S(1)}, bf16[128,128]{1,0:T(8,128)(2,1)S(1)}, u32[]{:S(2)}, u32[]{:S(2)}) collective-permute-start(bf16[128,128]{1,0:T(8,128)(2,1)S(1)} %get-tuple-element.22), channel_id=1, source_target_pairs={{0,1},{1,0},{2,3},{3,2},{4,5},{5,4},{6,7},{7,6},{8,9},{9,8},{10,11... | collective-permute-start | bytes 98312 | tf_op jit(solution)/shard_map/ppermute | solution.py:27
  11.0 1.4 %collective-permute-start.4 = (bf16[128,128]{1,0:T(8,128)(2,1)S(1)}, bf16[128,128]{1,0:T(8,128)(2,1)S(1)}, u32[]{:S(2)}, u32[]{:S(2)}) collective-permute-start(bf16[128,128]{1,0:T(8,128)(2,1)S(1)} %get-tuple-element.26), channel_id=1, source_target_pairs={{0,1},{1,0},{2,3},{3,2},{4,5},{5,4},{6,7},{7,6},{8,9},{9,8},{10,11... | collective-permute-start | bytes 98312 | tf_op jit(solution)/shard_map/ppermute | solution.py:27
  13.1 4.8 %collective-permute-start.6 = (bf16[224,128]{1,0:T(8,128)(2,1)S(1)}, bf16[224,128]{1,0:T(8,128)(2,1)S(1)}, u32[]{:S(2)}, u32[]{:S(2)}) collective-permute-start(bf16[224,128]{1,0:T(8,128)(2,1)S(1)} %get-tuple-element.34), channel_id=1, source_target_pairs={{0,2},{1,3},{2,0},{3,1},{4,6},{5,7},{6,4},{7,5},{8,10},{9,11},{10,... | collective-permute-start | bytes 172040 | tf_op jit(solution)/shard_map/ppermute | solution.py:27
  14.6 3.3 %collective-permute-start.5 = (bf16[96,128]{1,0:T(8,128)(2,1)S(1)}, bf16[96,128]{1,0:T(8,128)(2,1)S(1)}, u32[]{:S(2)}, u32[]{:S(2)}) collective-permute-start(bf16[96,128]{1,0:T(8,128)(2,1)S(1)} %get-tuple-element.33), channel_id=1, source_target_pairs={{0,3},{1,2},{2,1},{3,0},{4,7},{5,6},{6,5},{7,4},{8,11},{9,10},{10,... | collective-permute-start | bytes 73736 | tf_op jit(solution)/shard_map/ppermute | solution.py:27
  14.8 3.1 %collective-permute-start.7 = (bf16[96,128]{1,0:T(8,128)(2,1)S(1)}, bf16[96,128]{1,0:T(8,128)(2,1)S(1)}, u32[]{:S(2)}, u32[]{:S(2)}) collective-permute-start(bf16[96,128]{1,0:T(8,128)(2,1)S(1)} %get-tuple-element.35), channel_id=1, source_target_pairs={{0,1},{1,0},{2,3},{3,2},{4,5},{5,4},{6,7},{7,6},{8,9},{9,8},{10,11... | collective-permute-start | bytes 73736 | tf_op jit(solution)/shard_map/ppermute | solution.py:27

commit v10 on v9

--- a/solution.py
+++ b/solution.py
@@ -91,18 +91,97 @@
     )(*in_hbm(down, up))
 
 
-def project_kernel(step_count, head_count, shards, replicas, *refs):
-    lengths_hbm, owners_hbm, tokens_ref, weight_ref, queries_ref, keys_ref, _ = refs[:7]
+def project_kernel(shards, replicas, *refs):
+    owners_hbm, tokens_ref, weight_ref, _ = refs[:4]
     pairs = shards // 2
-    near_refs = refs[7 : 7 + pairs]
-    kept_ref, grouped_ref, scores_ref, cosine_ref, sine_ref, left_ref = refs[7 + pairs : 13 + pairs]
-    lengths_ref, owners_ref, regroup, token_buf, sems = refs[13 + pairs :]
-    lengths_copy = pltpu.make_async_copy(lengths_hbm, lengths_ref, sems.at[0])
-    owners_copy = pltpu.make_async_copy(owners_hbm, owners_ref, sems.at[1])
+    near_refs = refs[4 : 4 + pairs]
+    kept_ref, left_ref, owners_ref, token_buf, owner_sem = refs[4 + pairs :]
+    owners_copy = pltpu.make_async_copy(owners_hbm, owners_ref, owner_sem)
+    owners_copy.start()
+
+    shard = lax.axis_index("tensor")
+    _, rows, own = kept_ref.shape
+    for i in range(shards):
+        first = pl.multiple_of((shard ^ i) * own, lanes)
+        block = jnp.dot(
+            tokens_ref[...], weight_ref[:, pl.ds(first, own)], preferred_element_type=f32
+        )
+        if i % 2 == 0:
+            kept_ref[i // 2] = block
+            continue
+        for c in range(own // lanes):
+            near_refs[i // 2][c * rows : (c + 1) * rows, :] = block[
+                :, c * lanes : (c + 1) * lanes
+            ].astype(bf16)
+
+    owners_copy.wait()
+    width = token_buf.shape[2]
+    down_rows = tokens_ref.shape[1] // replicas
+    for k in range(replicas):
+        token_buf[k, :, :down_rows] = tokens_ref[:, k * down_rows : (k + 1) * down_rows]
+        if down_rows < width:
+            token_buf[k, :, down_rows:] = jnp.zeros((rows, width - down_rows), bf16)
+    for i in range(replicas):
+        source = lax.rem(lax.axis_index("rollout") + i, replicas)
+        place = jnp.int32(0)
+        for k in range(1, replicas):
+            place = place + jnp.where(owners_ref[k] == source, k, 0)
+        left_ref[:, i * width : (i + 1) * width] = token_buf[place]
+
+
+def project(owners, tokens, weight, after, shards, replicas):
+    rows, depth = tokens.shape
+    own = weight.shape[1] // shards
+    pairs = shards // 2
+    piece_width = -(-depth // replicas // lanes) * lanes
+    outs = pl.pallas_call(
+        functools.partial(project_kernel, shards, replicas),
+        out_shape=[jax.ShapeDtypeStruct((rows * own // lanes, lanes), bf16)] * pairs
+        + [
+            jax.ShapeDtypeStruct((pairs, rows, own), f32),
+            jax.ShapeDtypeStruct((rows, replicas * piece_width), bf16),
+        ],
+        in_specs=[stays_in_hbm] + [whole_in_vmem] * 3,
+        out_specs=[whole_in_vmem] * (pairs + 2),
+        scratch_shapes=[
+            pltpu.SMEM(owners.shape, jnp.int32),
+            pltpu.VMEM((replicas, rows, piece_width), bf16),
+            pltpu.SemaphoreType.DMA,
+        ],
+        compiler_params=pltpu.CompilerParams(vmem_limit_bytes=4 * 2**20),
+        name="project",
+        cost_estimate=pl.CostEstimate(
+            flops=2 * rows * weight.size, bytes_accessed=2 * weight.size, transcendentals=0
+        ),
+    )(*in_hbm(owners), tokens, weight, after)
+    return outs[:pairs], *outs[pairs:]
+
+
+def attend_kernel(
+    step_count,
+    head_count,
+    lengths_hbm,
+    queries_ref,
+    keys_ref,
+    values_ref,
+    _,
+    grouped_ref,
+    total_ref,
+    peak_ref,
+    sum_ref,
+    cosine_ref,
+    sine_ref,
+    lengths_ref,
+    regroup,
+    scores_ref,
+    raised,
+    length_sem,
+):
+    lengths_copy = pltpu.make_async_copy(lengths_hbm, lengths_ref, length_sem)
     lengths_copy.start()
-    owners_copy.start()
-
-    row_count = keys_ref.shape[0]
+    rows = cosine_ref.shape[0]
+
+    row_count, slots, _ = keys_ref.shape
     group = queries_ref.shape[1] // (head_count * lanes)
     seen = step_count * group
     for pair in range(step_count // 2):
@@ -125,21 +204,6 @@
                     ).astype(bf16)
             before = both
 
-    shard = lax.axis_index("tensor")
-    _, rows, own = kept_ref.shape
-    for i in range(shards):
-        first = pl.multiple_of((shard ^ i) * own, lanes)
-        block = jnp.dot(
-            tokens_ref[...], weight_ref[:, pl.ds(first, own)], preferred_element_type=f32
-        )
-        if i % 2 == 0:
-            kept_ref[i // 2] = block
-            continue
-        for c in range(own // lanes):
-            near_refs[i // 2][c * rows : (c + 1) * rows, :] = block[
-                :, c * lanes : (c + 1) * lanes
-            ].astype(bf16)
-
     for b in range(row_count):
         for h in range(head_count):
             at = (h * row_count + b) * seen
@@ -150,92 +214,6 @@
                 preferred_element_type=f32,
             )
 
-    lengths_copy.wait()
-    row = lax.broadcasted_iota(jnp.int32, (rows, lanes), 0)
-    lane = lax.broadcasted_iota(jnp.int32, (rows, lanes), 1)
-    position = row // row_count
-    for b in range(row_count):
-        position = position + jnp.where(row % row_count == b, lengths_ref[b], 0)
-    middle = lanes // 2
-    spacing = (lane % middle).astype(f32) * (-2.0 / lanes * math.log(rope_base))
-    angles = position.astype(f32) * jnp.exp(spacing)
-    cosine_ref[...] = jnp.cos(angles)
-    sine = jnp.sin(angles)
-    sine_ref[...] = jnp.where(lane < middle, -sine, sine)
-
-    owners_copy.wait()
-    width = token_buf.shape[2]
-    down_rows = tokens_ref.shape[1] // replicas
-    for k in range(replicas):
-        token_buf[k, :, :down_rows] = tokens_ref[:, k * down_rows : (k + 1) * down_rows]
-        if down_rows < width:
-            token_buf[k, :, down_rows:] = jnp.zeros((rows, width - down_rows), bf16)
-    for i in range(replicas):
-        source = lax.rem(lax.axis_index("rollout") + i, replicas)
-        place = jnp.int32(0)
-        for k in range(1, replicas):
-            place = place + jnp.where(owners_ref[k] == source, k, 0)
-        left_ref[:, i * width : (i + 1) * width] = token_buf[place]
-
-
-def project(
-    lengths, owners, tokens, weight, queries, keys, after, step_count, shards, replicas
-):
-    rows, depth = tokens.shape
-    own = weight.shape[1] // shards
-    pairs = shards // 2
-    row_count, slots, width = keys.shape
-    seen_rows = rows * queries.shape[1] // lanes
-    table = jax.ShapeDtypeStruct((rows, lanes), f32)
-    piece_width = -(-depth // replicas // lanes) * lanes
-    outs = pl.pallas_call(
-        functools.partial(project_kernel, step_count, width // lanes, shards, replicas),
-        out_shape=[jax.ShapeDtypeStruct((rows * own // lanes, lanes), bf16)] * pairs
-        + [
-            jax.ShapeDtypeStruct((pairs, rows, own), f32),
-            jax.ShapeDtypeStruct((seen_rows, lanes), bf16),
-            jax.ShapeDtypeStruct((seen_rows, slots), f32),
-            table,
-            table,
-            jax.ShapeDtypeStruct((rows, replicas * piece_width), bf16),
-        ],
-        in_specs=[stays_in_hbm] * 2 + [whole_in_vmem] * 5,
-        out_specs=[whole_in_vmem] * (pairs + 6),
-        scratch_shapes=[
-            pltpu.SMEM(lengths.shape, jnp.int32),
-            pltpu.SMEM(owners.shape, jnp.int32),
-            pltpu.VMEM((seen_rows, lanes), f32),
-            pltpu.VMEM((replicas, rows, piece_width), bf16),
-            pltpu.SemaphoreType.DMA((2,)),
-        ],
-        compiler_params=pltpu.CompilerParams(vmem_limit_bytes=6 * 2**20),
-        name="project",
-        cost_estimate=pl.CostEstimate(
-            flops=2 * rows * weight.size + 2 * seen_rows * slots * lanes,
-            bytes_accessed=2 * (weight.size + keys.size),
-            transcendentals=0,
-        ),
-    )(*in_hbm(lengths, owners), tokens, weight, queries, keys, after)
-    return outs[:pairs], *outs[pairs:]
-
-
-def attend_kernel(
-    head_count,
-    lengths_hbm,
-    scores_ref,
-    values_ref,
-    _,
-    total_ref,
-    peak_ref,
-    sum_ref,
-    lengths_ref,
-    raised,
-    length_sem,
-):
-    lengths_copy = pltpu.make_async_copy(lengths_hbm, lengths_ref, length_sem)
-    lengths_copy.start()
-    row_count, slots, _ = values_ref.shape
-    seen = scores_ref.shape[0] // (head_count * row_count)
     places = [
         (
             b,
@@ -264,29 +242,52 @@
             preferred_element_type=f32,
         )
 
-
-def attend(lengths, scores, values, after):
-    row_count, slots, width = values.shape
-    seen_rows = scores.shape[0]
+    row = lax.broadcasted_iota(jnp.int32, (rows, lanes), 0)
+    lane = lax.broadcasted_iota(jnp.int32, (rows, lanes), 1)
+    position = row // row_count
+    for b in range(row_count):
+        position = position + jnp.where(row % row_count == b, lengths_ref[b], 0)
+    middle = lanes // 2
+    spacing = (lane % middle).astype(f32) * (-2.0 / lanes * math.log(rope_base))
+    angles = position.astype(f32) * jnp.exp(spacing)
+    cosine_ref[...] = jnp.cos(angles)
+    sine = jnp.sin(angles)
+    sine_ref[...] = jnp.where(lane < middle, -sine, sine)
+
+
+def attend(lengths, queries, keys, values, after, step_count):
+    row_count, slots, width = keys.shape
+    rows = step_count * row_count
+    seen_rows = rows * queries.shape[1] // lanes
+    table = jax.ShapeDtypeStruct((rows, lanes), f32)
     seen_table = jax.ShapeDtypeStruct((seen_rows, lanes), f32)
     return pl.pallas_call(
-        functools.partial(attend_kernel, width // lanes),
-        out_shape=(seen_table,) * 3,
-        in_specs=[stays_in_hbm] + [whole_in_vmem] * 3,
-        out_specs=(whole_in_vmem,) * 3,
+        functools.partial(attend_kernel, step_count, width // lanes),
+        out_shape=(
+            jax.ShapeDtypeStruct((seen_rows, lanes), bf16),
+            seen_table,
+            seen_table,
+            seen_table,
+            table,
+            table,
+        ),
+        in_specs=[stays_in_hbm] + [whole_in_vmem] * 4,
+        out_specs=(whole_in_vmem,) * 6,
         scratch_shapes=[
             pltpu.SMEM(lengths.shape, jnp.int32),
+            pltpu.VMEM((seen_rows, lanes), f32),
+            pltpu.VMEM((seen_rows, slots), f32),
             pltpu.VMEM((seen_rows, slots), bf16),
             pltpu.SemaphoreType.DMA,
         ],
-        compiler_params=pltpu.CompilerParams(vmem_limit_bytes=6 * 2**20),
+        compiler_params=pltpu.CompilerParams(vmem_limit_bytes=8 * 2**20),
         name="attend",
         cost_estimate=pl.CostEstimate(
-            flops=2 * seen_rows * slots * lanes,
-            bytes_accessed=2 * values.size,
+            flops=4 * seen_rows * slots * lanes,
+            bytes_accessed=2 * (keys.size + values.size),
             transcendentals=seen_rows * slots,
         ),
-    )(*in_hbm(lengths), scores, values, after)
+    )(*in_hbm(lengths), queries, keys, values, after)
 
 
 def add_near(kept, near):
@@ -534,15 +535,11 @@
         beside = pl.CostEstimate(flops=1000 * fetched, bytes_accessed=fetched, transcendentals=0)
         packed = pack(adapter_down.T, adapter_up, rank_part, beside)
         pieces = [packed] + [shift(packed, "rollout", i) for i in range(1, replicas)]
-    near, kept, grouped, scores, cosine, sine, left = project(
-        lengths,
+    near, kept, left = project(
         owners,
         tokens,
         key_value_weight,
-        query_rows,
-        cache_keys,
         packed if fits else adapter_up,
-        step_count,
         shards,
         replicas if fits else 1,
     )
@@ -555,12 +552,12 @@
         packets = route_plain(
             owners, tokens, (kept, near), adapter_down, adapter_up, rank_part, own, shards
         )
-    total, peak, denominator = attend(lengths, scores, stored_values, packets[0])
+    partials = attend(lengths, query_rows, cache_keys, stored_values, packets[0], step_count)
     packets = [packets[0]] + [swap(packets[i], "tensor", i) for i in range(1, shards)]
     attention, keys, values = finish(
         kept,
         near[0],
-        (grouped, total, peak, denominator, cosine, sine),
+        partials,
         key_gain.reshape(1, -1),
         packets,
         rank,

time: 19.6 us -> 19.1 us (0.974)
  waiting for transfers between devices: 2.16 us -> 1.78 us
    ppermute x5, waiting for transfers between devices: 2.15 us -> 1.36 us  [swap(): return lax.ppermute(block, axis, [(s, s ^ offset) for s in range(count)])]
    ppermute x3, waiting for transfers between devices: 0.01 us -> 0.42 us  [shift(): lax.ppermute(block, axis, [((s + offset) % count, s) for s in range(count)])]
  transfers between devices with their start and end apart: 8 -> 8, of which waited for: 3 -> 5; matrix products, arithmetic and copies ran while one was open for 0% -> 0% of each run, Pallas kernels for 17% -> 18%
where the time goes in v10:
time: 19.1 us; the launch traced here: 18.9 us
  starting transfers between devices  9.79 us (51%)
  Pallas kernels  6.55 us (34%)
  waiting for transfers between devices  1.78 us (9%)
  between operations  0.74 us (4%)
    ppermute x3, starting transfers between devices, shift(): lax.ppermute(block, axis, [((s + offset) % count, s) for s in range(count)])  7.01 us
    ppermute x5, starting transfers between devices, swap(): return lax.ppermute(block, axis, [(s, s ^ offset) for s in range(count)])  2.77 us
    pallas_call x1, Pallas kernels, attend(): pl.pallas_call(functools.partial(attend_kernel, step_count, width // lane...  2.19 us
    pallas_call x1, Pallas kernels, finish(): pl.pallas_call(functools.partial(finish_kernel, step_count, row_count, he...  1.44 us
    ppermute x5, waiting for transfers between devices, swap(): return lax.ppermute(block, axis, [(s, s ^ offset) for s in range(count)])  1.36 us
    pallas_call x1, Pallas kernels, project(): pl.pallas_call(functools.partial(project_kernel, shards, replicas), out_s...  1.14 us
    pallas_call x1, Pallas kernels, pack(): pl.pallas_call(pack_kernel, out_shape=jax.ShapeDtypeStruct((rows, lanes),...  1.05 us
    pallas_call x1, Pallas kernels, route(): pl.pallas_call(functools.partial(route_kernel, replicas, shards), out_sha...  0.73 us
  transfers between devices with their start and end apart: 8, of which 5 were waited for; matrix products, arithmetic and copies ran while one was open for 0% of the time, Pallas kernels for 18%

profile of v10, /device:TPU:0, one launch (start us, length us, event | category | flops | bytes accessed | tf_op | source)
XLA Modules:
  0.0 18.9 jit_solution(9111654247256072186)
XLA Ops:
  0.6 0.0 slice-start
  0.6 0.0 slice-start.1
  0.7 0.0 copy-start.3
  0.7 1.0 %pack.1.refs_3_ = bf16[224,128]{1,0:T(8,128)(2,1)S(1)} custom-call(bf16[64,320]{1,0:T(8,128)(2,1)} %bitcast.13, bf16[64,512]{1,0:T(8,128)(2,1)} %up_hbm.1), custom_call_target="tpu_custom_call" | custom-call | flops 9437184000 | bytes 9437184 | tf_op jit(solution)/shard_map/pack/pallas_call | solution.py:78
  1.7 3.1 %collective-permute-start.3 = (bf16[224,128]{1,0:T(8,128)(2,1)S(1)}, bf16[224,128]{1,0:T(8,128)(2,1)S(1)}, u32[]{:S(2)}, u32[]{:S(2)}) collective-permute-start(bf16[224,128]{1,0:T(8,128)(2,1)S(1)} %pack.1.refs_3_), channel_id=1, source_target_pairs={{12,0},{0,4},{4,8},{8,12},{13,1},{1,5},{5,9},{9,13},{14,2},{2,6},{... | collective-permute-start | bytes 172040 | tf_op jit(solution)/shard_map/ppermute | solution.py:32
  4.8 2.6 %collective-permute-start.2 = (bf16[224,128]{1,0:T(8,128)(2,1)S(1)}, bf16[224,128]{1,0:T(8,128)(2,1)S(1)}, u32[]{:S(2)}, u32[]{:S(2)}) collective-permute-start(bf16[224,128]{1,0:T(8,128)(2,1)S(1)} %pack.1.refs_3_), channel_id=1, source_target_pairs={{8,0},{12,4},{0,8},{4,12},{9,1},{13,5},{1,9},{5,13},{10,2},{14,6},... | collective-permute-start | bytes 172040 | tf_op jit(solution)/shard_map/ppermute | solution.py:32
  7.4 1.3 %collective-permute-start.1 = (bf16[224,128]{1,0:T(8,128)(2,1)S(1)}, bf16[224,128]{1,0:T(8,128)(2,1)S(1)}, u32[]{:S(2)}, u32[]{:S(2)}) collective-permute-start(bf16[224,128]{1,0:T(8,128)(2,1)S(1)} %pack.1.refs_3_), channel_id=1, source_target_pairs={{4,0},{8,4},{12,8},{0,12},{5,1},{9,5},{13,9},{1,13},{6,2},{10,6},{... | collective-permute-start | bytes 172040 | tf_op jit(solution)/shard_map/ppermute | solution.py:32
  8.7 0.0 slice-done
  8.7 0.0 slice-done.1
  8.7 0.0 copy-done.3
  8.7 0.0 copy-start
  8.8 0.0 copy-start.1
  8.8 0.0 copy-start.2
  8.8 1.1 %project.1 = (bf16[128,128]{1,0:T(8,128)(2,1)S(1)}, bf16[128,128]{1,0:T(8,128)(2,1)S(1)}, f32[2,32,512]{2,1,0:T(8,128)S(1)}, bf16[32,1536]{1,0:T(8,128)(2,1)S(1)}) custom-call(s32[4]{0:T(128)} %refs_0_.3, bf16[32,1280]{1,0:T(8,128)(2,1)S(1)} %bitcast.10, bf16[1280,2048]{1,0:T(8,128)(2,1)S(1)} %bitcast.8, bf16[224,128]{1,0:T(8,128)(2,1)S(1)} %pack.1.refs_3_), custom_call_target="tpu_custom_call" | custom-call | flops 167772160 | bytes 5242880 | tf_op jit(solution)/shard_map/project/pallas_call | solution.py:137
  9.9 0.1 collective-permute-start
  10.0 0.5 %collective-permute-start.4 = (bf16[128,128]{1,0:T(8,128)(2,1)S(1)}, bf16[128,128]{1,0:T(8,128)(2,1)S(1)}, u32[]{:S(2)}, u32[]{:S(2)}) collective-permute-start(bf16[128,128]{1,0:T(8,128)(2,1)S(1)} %get-tuple-element.23), channel_id=1, source_target_pairs={{0,1},{1,0},{2,3},{3,2},{4,5},{5,4},{6,7},{7,6},{8,9},{9,8},{10,11... | collective-permute-start | bytes 98312 | tf_op jit(solution)/shard_map/ppermute | solution.py:27
  10.5 0.7 %collective-permute-done.refs_7_.refs_1_ = bf16[128,128]{1,0:T(8,128)(2,1)S(1)} collective-permute-done((bf16[128,128]{1,0:T(8,128)(2,1)S(1)}, bf16[128,128]{1,0:T(8,128)(2,1)S(1)}, u32[]{:S(2)}, u32[]{:S(2)}) %collective-permute-start) | collective-permute-done | bytes 32800 | tf_op jit(solution)/shard_map/ppermute | solution.py:27
  11.2 0.2 collective-permute-done.4.refs_8_
  11.4 0.0 collective-permute-done.3.refs_6_
  11.4 0.1 collective-permute-done.2.refs_5_
  11.4 0.4 %collective-permute-done.1.refs_4_ = bf16[224,128]{1,0:T(8,128)(2,1)S(1)} collective-permute-done((bf16[224,128]{1,0:T(8,128)(2,1)S(1)}, bf16[224,128]{1,0:T(8,128)(2,1)S(1)}, u32[]{:S(2)}, u32[]{:S(2)}) %collective-permute-start.1) | collective-permute-done | bytes 57376 | tf_op jit(solution)/shard_map/ppermute | solution.py:32
  11.8 0.7 %route.1 = (bf16[96,128]{1,0:T(8,128)(2,1)S(1)}, bf16[96,128]{1,0:T(8,128)(2,1)S(1)}, bf16[224,128]{1,0:T(8,128)(2,1)S(1)}, bf16[96,128]{1,0:T(8,128)(2,1)S(1)}) custom-call(s32[4]{0:T(128)} %refs_0_.3, bf16[32,1536]{1,0:T(8,128)(2,1)S(1)} %get-tuple-element.22.refs_1_, f32[2,32,512]{2,1,0:T(8,128)S(1)} %get-tuple-element.20.refs_2_.refs_0_, ...), custom_call_target="tpu_custom_call" | custom-call | bytes 800000 | tf_op jit(solution)/shard_map/route/pallas_call | solution.py:356
  12.5 1.6 %collective-permute-start.6 = (bf16[224,128]{1,0:T(8,128)(2,1)S(1)}, bf16[224,128]{1,0:T(8,128)(2,1)S(1)}, u32[]{:S(2)}, u32[]{:S(2)}) collective-permute-start(bf16[224,128]{1,0:T(8,128)(2,1)S(1)} %get-tuple-element.32), channel_id=1, source_target_pairs={{0,2},{1,3},{2,0},{3,1},{4,6},{5,7},{6,4},{7,5},{8,10},{9,11},{10,... | collective-permute-start | bytes 172040 | tf_op jit(solution)/shard_map/ppermute | solution.py:27
  14.1 0.0 collective-permute-start.5
  14.2 0.6 %collective-permute-start.7 = (bf16[96,128]{1,0:T(8,128)(2,1)S(1)}, bf16[96,128]{1,0:T(8,128)(2,1)S(1)}, u32[]{:S(2)}, u32[]{:S(2)}) collective-permute-start(bf16[96,128]{1,0:T(8,128)(2,1)S(1)} %get-tuple-element.33), channel_id=1, source_target_pairs={{0,1},{1,0},{2,3},{3,2},{4,5},{5,4},{6,7},{7,6},{8,9},{9,8},{10,11... | collective-permute-start | bytes 73736 | tf_op jit(solution)/shard_map/ppermute | solution.py:27
  14.7 0.0 copy-done
  14.7 0.0 copy-done.1
  14.7 0.0 copy-done.2
  14.7 0.0 copy-start.4
  14.8 2.2 %attend.1 = (bf16[512,128]{1,0:T(8,128)(2,1)S(1)}, f32[512,128]{1,0:T(8,128)S(1)}, f32[512,128]{1,0:T(8,128)S(1)}, f32[512,128]{1,0:T(8,128)S(1)}, f32[32,128]{1,0:T(8,128)S(1)}, /*index=5*/f32[32,128]{1,0:T(8,128)S(1)}) custom-call(s32[8]{0:T(128)} %lengths_hbm.1, bf16[32,2048]{1,0:T(8,128)(2,1)S(1)} %bitcast.9, bf16[8,512,256]{2,1,0:T(8,128)(2,1)S(1)} %copy-done, ...), custom_call_target="tpu_custom_call" | custom-call | flops 134217728 | bytes 4194304 | tf_op jit(solution)/shard_map/attend/pallas_call | solution.py:264
  16.9 0.5 %collective-permute-done.5.refs_9_ = bf16[96,128]{1,0:T(8,128)(2,1)S(1)} collective-permute-done((bf16[96,128]{1,0:T(8,128)(2,1)S(1)}, bf16[96,128]{1,0:T(8,128)(2,1)S(1)}, u32[]{:S(2)}, u32[]{:S(2)}) %collective-permute-start.5) | collective-permute-done | bytes 24608 | tf_op jit(solution)/shard_map/ppermute | solution.py:27
  17.4 0.0 collective-permute-done.7.refs_11_
  17.4 0.0 collective-permute-done.6.refs_10_
  17.4 0.0 copy-done.4
  17.5 1.4 %finish.1 = (bf16[32,2048]{1,0:T(8,128)(2,1)}, bf16[32,256]{1,0:T(8,128)(2,1)}, bf16[32,256]{1,0:T(8,128)(2,1)}) custom-call(f32[2,32,512]{2,1,0:T(8,128)S(1)} %get-tuple-element.20.refs_2_.refs_0_, bf16[128,128]{1,0:T(8,128)(2,1)S(1)} %collective-permute-done.refs_7_.refs_1_, f32[1,128]{1,0:T(1,128)S(1)} %bitcast.11, ...), custom_call_target="tpu_custom_call" | custom-call | bytes 1000000 | tf_op jit(solution)/shard_map/finish/pallas_call | solution.py:486
  (1 shorter events, 0.0 us)
Async XLA Ops:
  0.6 8.1 %slice-start = ((s8[5242880]{0:T(1024)(128)(4,1)}), s8[4194304]{0:T(1024)(128)(4,1)S(1)}, s32[]{:S(2)}) async-start(s8[5242880]{0:T(1024)(128)(4,1)} %bitcast.7), calls=%async_computation | async-start | bytes 8388608
  0.6 8.1 %slice-start.1 = ((s8[5242880]{0:T(1024)(128)(4,1)}), s8[1048576]{0:T(1024)(128)(4,1)S(1)}, s32[]{:S(2)}) async-start(s8[5242880]{0:T(1024)(128)(4,1)} %bitcast.7), calls=%async_computation.1 | async-start | bytes 2097152
  0.7 8.1 %copy-start.3 = (bf16[4,8,1280]{2,1,0:T(8,128)(2,1)S(1)}, bf16[4,8,1280]{2,1,0:T(8,128)(2,1)}, u32[]{:S(2)}) copy-start(bf16[4,8,1280]{2,1,0:T(8,128)(2,1)} %param.10) | copy-start | bytes 245764
  1.7 9.6 %collective-permute-start.3 = (bf16[224,128]{1,0:T(8,128)(2,1)S(1)}, bf16[224,128]{1,0:T(8,128)(2,1)S(1)}, u32[]{:S(2)}, u32[]{:S(2)}) collective-permute-start(bf16[224,128]{1,0:T(8,128)(2,1)S(1)} %pack.1.refs_3_), channel_id=1, source_target_pairs={{12,0},{0,4},{4,8},{8,12},{13,1},{1,5},{5,9},{9,13},{14,2},{2,6},{... | collective-permute-start | bytes 172040 | tf_op jit(solution)/shard_map/ppermute | solution.py:32
  4.8 6.6 %collective-permute-start.2 = (bf16[224,128]{1,0:T(8,128)(2,1)S(1)}, bf16[224,128]{1,0:T(8,128)(2,1)S(1)}, u32[]{:S(2)}, u32[]{:S(2)}) collective-permute-start(bf16[224,128]{1,0:T(8,128)(2,1)S(1)} %pack.1.refs_3_), channel_id=1, source_target_pairs={{8,0},{12,4},{0,8},{4,12},{9,1},{13,5},{1,9},{5,13},{10,2},{14,6},... | collective-permute-start | bytes 172040 | tf_op jit(solution)/shard_map/ppermute | solution.py:32
  7.4 4.4 %collective-permute-start.1 = (bf16[224,128]{1,0:T(8,128)(2,1)S(1)}, bf16[224,128]{1,0:T(8,128)(2,1)S(1)}, u32[]{:S(2)}, u32[]{:S(2)}) collective-permute-start(bf16[224,128]{1,0:T(8,128)(2,1)S(1)} %pack.1.refs_3_), channel_id=1, source_target_pairs={{4,0},{8,4},{12,8},{0,12},{5,1},{9,5},{13,9},{1,13},{6,2},{10,6},{... | collective-permute-start | bytes 172040 | tf_op jit(solution)/shard_map/ppermute | solution.py:32
  8.7 6.0 %copy-start = (bf16[8,512,256]{2,1,0:T(8,128)(2,1)S(1)}, bf16[8,512,256]{2,1,0:T(8,128)(2,1)}, u32[]{:S(2)}) copy-start(bf16[8,512,256]{2,1,0:T(8,128)(2,1)} %keys_ref.1) | copy-start | bytes 6291460
  8.8 6.0 %copy-start.1 = (bf16[8,512,256]{2,1,0:T(8,128)(2,1)S(1)}, bf16[8,512,256]{2,1,0:T(8,128)(2,1)}, u32[]{:S(2)}) copy-start(bf16[8,512,256]{2,1,0:T(8,128)(2,1)} %values_ref.1) | copy-start | bytes 6291460
  8.8 6.0 %copy-start.2 = (bf16[4,8,2048]{2,1,0:T(8,128)(2,1)S(1)}, bf16[4,8,2048]{2,1,0:T(8,128)(2,1)}, u32[]{:S(2)}) copy-start(bf16[4,8,2048]{2,1,0:T(8,128)(2,1)} %param.15) | copy-start | bytes 393220
  9.9 1.3 %collective-permute-start = (bf16[128,128]{1,0:T(8,128)(2,1)S(1)}, bf16[128,128]{1,0:T(8,128)(2,1)S(1)}, u32[]{:S(2)}, u32[]{:S(2)}) collective-permute-start(bf16[128,128]{1,0:T(8,128)(2,1)S(1)} %get-tuple-element.21), channel_id=1, source_target_pairs={{0,1},{1,0},{2,3},{3,2},{4,5},{5,4},{6,7},{7,6},{8,9},{9,8},{10,11... | collective-permute-start | bytes 98312 | tf_op jit(solution)/shard_map/ppermute | solution.py:27
  10.0 1.4 %collective-permute-start.4 = (bf16[128,128]{1,0:T(8,128)(2,1)S(1)}, bf16[128,128]{1,0:T(8,128)(2,1)S(1)}, u32[]{:S(2)}, u32[]{:S(2)}) collective-permute-start(bf16[128,128]{1,0:T(8,128)(2,1)S(1)} %get-tuple-element.23), channel_id=1, source_target_pairs={{0,1},{1,0},{2,3},{3,2},{4,5},{5,4},{6,7},{7,6},{8,9},{9,8},{10,11... | collective-permute-start | bytes 98312 | tf_op jit(solution)/shard_map/ppermute | solution.py:27
  12.5 4.9 %collective-permute-start.6 = (bf16[224,128]{1,0:T(8,128)(2,1)S(1)}, bf16[224,128]{1,0:T(8,128)(2,1)S(1)}, u32[]{:S(2)}, u32[]{:S(2)}) collective-permute-start(bf16[224,128]{1,0:T(8,128)(2,1)S(1)} %get-tuple-element.32), channel_id=1, source_target_pairs={{0,2},{1,3},{2,0},{3,1},{4,6},{5,7},{6,4},{7,5},{8,10},{9,11},{10,... | collective-permute-start | bytes 172040 | tf_op jit(solution)/shard_map/ppermute | solution.py:27
  14.1 3.3 %collective-permute-start.5 = (bf16[96,128]{1,0:T(8,128)(2,1)S(1)}, bf16[96,128]{1,0:T(8,128)(2,1)S(1)}, u32[]{:S(2)}, u32[]{:S(2)}) collective-permute-start(bf16[96,128]{1,0:T(8,128)(2,1)S(1)} %get-tuple-element.31), channel_id=1, source_target_pairs={{0,3},{1,2},{2,1},{3,0},{4,7},{5,6},{6,5},{7,4},{8,11},{9,10},{10,... | collective-permute-start | bytes 73736 | tf_op jit(solution)/shard_map/ppermute | solution.py:27
  14.2 3.3 %collective-permute-start.7 = (bf16[96,128]{1,0:T(8,128)(2,1)S(1)}, bf16[96,128]{1,0:T(8,128)(2,1)S(1)}, u32[]{:S(2)}, u32[]{:S(2)}) collective-permute-start(bf16[96,128]{1,0:T(8,128)(2,1)S(1)} %get-tuple-element.33), channel_id=1, source_target_pairs={{0,1},{1,0},{2,3},{3,2},{4,5},{5,4},{6,7},{7,6},{8,9},{9,8},{10,11... | collective-permute-start | bytes 73736 | tf_op jit(solution)/shard_map/ppermute | solution.py:27
  14.7 2.7 %copy-start.4 = (f32[128]{0:T(128)S(1)}, f32[128]{0:T(128)}, u32[]{:S(2)}) copy-start(f32[128]{0:T(128)} %param.14) | copy-start | bytes 1540

commit v11 on v10

--- a/solution.py
+++ b/solution.py
@@ -25,11 +25,6 @@
 def swap(block, axis, offset):
     count = lax.axis_size(axis)
     return lax.ppermute(block, axis, [(s, s ^ offset) for s in range(count)])
-
-
-def shift(block, axis, offset):
-    count = lax.axis_size(axis)
-    return lax.ppermute(block, axis, [((s + offset) % count, s) for s in range(count)])
 
 
 def in_hbm(*arrays):
@@ -122,7 +117,7 @@
         if down_rows < width:
             token_buf[k, :, down_rows:] = jnp.zeros((rows, width - down_rows), bf16)
     for i in range(replicas):
-        source = lax.rem(lax.axis_index("rollout") + i, replicas)
+        source = lax.axis_index("rollout") ^ i
         place = jnp.int32(0)
         for k in range(1, replicas):
             place = place + jnp.where(owners_ref[k] == source, k, 0)
@@ -157,6 +152,35 @@
     return outs[:pairs], *outs[pairs:]
 
 
+def chip_sums_kernel(kept_ref, *refs):
+    pairs, rows, own = kept_ref.shape
+    near_refs, own_ref, far_refs = refs[:pairs], refs[pairs], refs[pairs + 1 :]
+    for c in range(own // lanes):
+        for m in range(pairs):
+            block = kept_ref[m, :, c * lanes : (c + 1) * lanes] + near_refs[m][
+                c * rows : (c + 1) * rows, :
+            ].astype(f32)
+            if m == 0:
+                own_ref[:, c * lanes : (c + 1) * lanes] = block
+            else:
+                far_refs[m - 1][c * rows : (c + 1) * rows, :] = block.astype(bf16)
+
+
+def chip_sums(kept, near):
+    pairs, rows, own = kept.shape
+    mine, *far = pl.pallas_call(
+        chip_sums_kernel,
+        out_shape=[jax.ShapeDtypeStruct((rows, own), f32)]
+        + [jax.ShapeDtypeStruct(near[0].shape, bf16)] * (pairs - 1),
+        in_specs=[whole_in_vmem] * (1 + pairs),
+        out_specs=[whole_in_vmem] * pairs,
+        compiler_params=pltpu.CompilerParams(vmem_limit_bytes=2 * 2**20),
+        name="chip_sums",
+        cost_estimate=pl.CostEstimate(flops=0, bytes_accessed=400000, transcendentals=0),
+    )(kept, *near)
+    return mine, far
+
+
 def attend_kernel(
     step_count,
     head_count,
@@ -165,21 +189,20 @@
     keys_ref,
     values_ref,
     _,
-    grouped_ref,
-    total_ref,
-    peak_ref,
-    sum_ref,
-    cosine_ref,
-    sine_ref,
-    lengths_ref,
-    regroup,
-    scores_ref,
-    raised,
-    length_sem,
+    own_ref,
+    *refs,
 ):
+    far_refs = refs[:-12]
+    base_ref, grouped_ref, total_ref, peak_ref, sum_ref, cosine_ref, sine_ref = refs[-12:-5]
+    lengths_ref, regroup, scores_ref, raised, length_sem = refs[-5:]
     lengths_copy = pltpu.make_async_copy(lengths_hbm, lengths_ref, length_sem)
     lengths_copy.start()
-    rows = cosine_ref.shape[0]
+    rows, own = own_ref.shape
+    for c in range(own // lanes):
+        block = own_ref[:, c * lanes : (c + 1) * lanes]
+        for far_ref in far_refs:
+            block = block + far_ref[c * rows : (c + 1) * rows, :].astype(f32)
+        base_ref[:, c * lanes : (c + 1) * lanes] = block
 
     row_count, slots, _ = keys_ref.shape
     group = queries_ref.shape[1] // (head_count * lanes)
@@ -255,7 +278,7 @@
     sine_ref[...] = jnp.where(lane < middle, -sine, sine)
 
 
-def attend(lengths, queries, keys, values, after, step_count):
+def attend(lengths, queries, keys, values, after, mine, far, step_count):
     row_count, slots, width = keys.shape
     rows = step_count * row_count
     seen_rows = rows * queries.shape[1] // lanes
@@ -264,6 +287,7 @@
     return pl.pallas_call(
         functools.partial(attend_kernel, step_count, width // lanes),
         out_shape=(
+            jax.ShapeDtypeStruct(mine.shape, f32),
             jax.ShapeDtypeStruct((seen_rows, lanes), bf16),
             seen_table,
             seen_table,
@@ -271,8 +295,8 @@
             table,
             table,
         ),
-        in_specs=[stays_in_hbm] + [whole_in_vmem] * 4,
-        out_specs=(whole_in_vmem,) * 6,
+        in_specs=[stays_in_hbm] + [whole_in_vmem] * (5 + len(far)),
+        out_specs=(whole_in_vmem,) * 7,
         scratch_shapes=[
             pltpu.SMEM(lengths.shape, jnp.int32),
             pltpu.VMEM((seen_rows, lanes), f32),
@@ -287,27 +311,14 @@
             bytes_accessed=2 * (keys.size + values.size),
             transcendentals=seen_rows * slots,
         ),
-    )(*in_hbm(lengths), queries, keys, values, after)
-
-
-def add_near(kept, near):
-    rows, own = kept.shape
-    return [
-        kept[:, c * lanes : (c + 1) * lanes] + near[c * rows : (c + 1) * rows, :].astype(f32)
-        for c in range(own // lanes)
-    ]
-
-
-def carries_sums(i):
-    return i > 0 and i % 2 == 0
+    )(*in_hbm(lengths), queries, keys, values, after, mine, *far)
 
 
 def route_kernel(replicas, shards, *refs):
-    owners_hbm, left_ref, kept_ref = refs[:3]
-    piece_refs = refs[3 : 3 + replicas]
-    near_refs = refs[3 + replicas : 3 + replicas + shards // 2]
-    out_refs = refs[3 + replicas + shards // 2 : 3 + replicas + shards // 2 + shards]
-    owners_ref, right, up_buf, owner_sem = refs[3 + replicas + shards // 2 + shards :]
+    owners_hbm, left_ref = refs[:2]
+    piece_refs = refs[2 : 2 + replicas]
+    out_refs = refs[3 + replicas : 3 + replicas + shards]
+    owners_ref, right, up_buf, owner_sem = refs[3 + replicas + shards :]
     owners_copy = pltpu.make_async_copy(owners_hbm, owners_ref, owner_sem)
     owners_copy.start()
     rows = left_ref.shape[0]
@@ -338,28 +349,18 @@
     shard = lax.axis_index("tensor")
     owners_copy.wait()
     for i in range(shards):
-        first = 0
-        if carries_sums(i):
-            for block in add_near(kept_ref[i // 2], near_refs[i // 2]):
-                out_refs[i][first : first + rows, :] = block.astype(bf16)
-                first += rows
-        out_refs[i][first : first + rows, :] = both
-        slot = lax.rem(owners_ref[shard ^ i] + replicas - replica, replicas)
-        out_refs[i][first + rows :, :] = up_buf[slot]
-
-
-def route(owners, left, sums, pieces, rank, up_rows, shards):
+        out_refs[i][:rows, :] = both
+        slot = owners_ref[shard ^ i] ^ replica
+        out_refs[i][rows:, :] = up_buf[slot]
+
+
+def route(owners, left, pieces, after, rank, up_rows, shards):
     rows, depth = left.shape
     replicas = len(pieces)
-    kept, near = sums
-    sent = near[0].shape[0]
     return pl.pallas_call(
         functools.partial(route_kernel, replicas, shards),
-        out_shape=[
-            jax.ShapeDtypeStruct(((sent if carries_sums(i) else 0) + rows + up_rows, lanes), bf16)
-            for i in range(shards)
-        ],
-        in_specs=[stays_in_hbm] + [whole_in_vmem] * (2 + replicas + len(near)),
+        out_shape=[jax.ShapeDtypeStruct((rows + up_rows, lanes), bf16)] * shards,
+        in_specs=[stays_in_hbm] + [whole_in_vmem] * (2 + replicas),
         out_specs=[whole_in_vmem] * shards,
         scratch_shapes=[
             pltpu.SMEM(owners.shape, jnp.int32),
@@ -370,11 +371,10 @@
         compiler_params=pltpu.CompilerParams(vmem_limit_bytes=4 * 2**20),
         name="route",
         cost_estimate=pl.CostEstimate(flops=0, bytes_accessed=800000, transcendentals=0),
-    )(*in_hbm(owners), left, kept, *pieces, *near)
-
-
-def route_plain(owners, tokens, sums, down, up, rank_part, own, shards):
-    kept, near = sums
+    )(*in_hbm(owners), left, *pieces, after)
+
+
+def route_plain(owners, tokens, down, up, rank_part, own, shards):
     rank = down.shape[1]
     shard = lax.axis_index("tensor")
     first = shard * rank_part
@@ -390,22 +390,18 @@
     for i in range(shards):
         up_block = lax.dynamic_slice_in_dim(up_matrix, (shard ^ i) * own, own, axis=1)
         parts = [both, side_by_side(up_block)]
-        if carries_sums(i):
-            sums = add_near(kept[i // 2], near[i // 2])
-            parts = [jnp.concatenate(sums, axis=0).astype(bf16)] + parts
         packets.append(jnp.concatenate(parts, axis=0))
     return packets
 
 
 def finish_kernel(step_count, row_count, head_count, shards, *refs):
-    kept_ref, near_ref, gain_ref, grouped_ref, total_ref, peak_ref, sum_ref = refs[:7]
-    cosine_ref, sine_ref = refs[7:9]
-    packet_refs = refs[9 : 9 + shards][::-1]
-    attention_ref, keys_ref, values_ref = refs[9 + shards : 12 + shards]
-    (up_buf,) = refs[12 + shards :]
+    gain_ref, base_ref, grouped_ref, total_ref, peak_ref, sum_ref, cosine_ref, sine_ref = refs[:8]
+    packet_refs = refs[8 : 8 + shards][::-1]
+    attention_ref, keys_ref, values_ref = refs[8 + shards : 11 + shards]
+    (up_buf,) = refs[11 + shards :]
     shard = lax.axis_index("tensor")
     rows = step_count * row_count
-    own = kept_ref.shape[2]
+    own = base_ref.shape[1]
     blocks = own // lanes
     rank = up_buf.shape[0]
     rank_part = rank // shards
@@ -414,9 +410,8 @@
 
     lowered = jnp.zeros((rows, lanes), f32)
     for i in range(shards):
-        first = rows * blocks if carries_sums(i) else 0
-        lowered = lowered + packet_refs[i][first : first + rows, :].astype(f32)
-        ups = packet_refs[i][first + rows :, :].astype(f32)
+        lowered = lowered + packet_refs[i][:rows, :].astype(f32)
+        ups = packet_refs[i][rows:, :].astype(f32)
         at = pl.multiple_of((shard ^ i) * rank_part, rank_part)
         for c in range(blocks):
             up_buf[pl.ds(at, rank_part), c * lanes : (c + 1) * lanes] = ups[
@@ -429,9 +424,8 @@
     up = up_buf[...].astype(bf16)
     raised_up = jnp.dot(left, jnp.concatenate([up, up], axis=0), preferred_element_type=f32)
     joined = []
-    for c, block in enumerate(add_near(kept_ref[0], near_ref)):
-        for i in filter(carries_sums, range(shards)):
-            block = block + packet_refs[i][c * rows : (c + 1) * rows, :].astype(f32)
+    for c in range(blocks):
+        block = base_ref[:, c * lanes : (c + 1) * lanes]
         joined.append(block + adapter_scale * raised_up[:, c * lanes : (c + 1) * lanes])
 
     all_rows = row_count * seen
@@ -478,9 +472,9 @@
             ] = jnp.concatenate(both, axis=0).astype(bf16)
 
 
-def finish(kept, near, partials, gain, packets, rank, step_count, row_count, query_width):
-    grouped, total, peak, denominator, cosine, sine = partials
-    _, rows, own = kept.shape
+def finish(partials, gain, packets, rank, step_count, row_count, query_width):
+    rows, own = partials[0].shape
+    total = partials[2]
     shards = len(packets)
     head_count = own // (2 * lanes)
     return pl.pallas_call(
@@ -490,7 +484,7 @@
             jax.ShapeDtypeStruct((rows, head_count * lanes), bf16),
             jax.ShapeDtypeStruct((rows, head_count * lanes), bf16),
         ),
-        in_specs=[whole_in_vmem] * (9 + shards),
+        in_specs=[whole_in_vmem] * (8 + shards),
         out_specs=(whole_in_vmem,) * 3,
         scratch_shapes=[
             pltpu.VMEM((rank, own), f32),
@@ -498,7 +492,7 @@
         compiler_params=pltpu.CompilerParams(vmem_limit_bytes=6 * 2**20),
         name="finish",
         cost_estimate=pl.CostEstimate(flops=0, bytes_accessed=1000000, transcendentals=0),
-    )(kept, near, gain, grouped, total, peak, denominator, cosine, sine, *packets[::-1])
+    )(gain, *partials, *packets[::-1])
 
 
 def per_device(
@@ -534,7 +528,7 @@
         fetched = 2 * (key_value_weight.size + cache_keys.size + stored_values.size)
         beside = pl.CostEstimate(flops=1000 * fetched, bytes_accessed=fetched, transcendentals=0)
         packed = pack(adapter_down.T, adapter_up, rank_part, beside)
-        pieces = [packed] + [shift(packed, "rollout", i) for i in range(1, replicas)]
+        pieces = [packed] + [swap(packed, "rollout", i) for i in range(1, replicas)]
     near, kept, left = project(
         owners,
         tokens,
@@ -543,20 +537,19 @@
         shards,
         replicas if fits else 1,
     )
-    near = [swap(block, "tensor", 1) for block in near]
+    mine, far = chip_sums(kept, [swap(block, "tensor", 1) for block in near])
+    far = [swap(block, "tensor", 2 * m + 2) for m, block in enumerate(far)]
     if fits:
         packets = route(
-            owners, left, (kept, near), pieces, rank, rank_part * own // lanes, shards
+            owners, left, pieces, mine, rank, rank_part * own // lanes, shards
         )
     else:
-        packets = route_plain(
-            owners, tokens, (kept, near), adapter_down, adapter_up, rank_part, own, shards
-        )
-    partials = attend(lengths, query_rows, cache_keys, stored_values, packets[0], step_count)
+        packets = route_plain(owners, tokens, adapter_down, adapter_up, rank_part, own, shards)
+    partials = attend(
+        lengths, query_rows, cache_keys, stored_values, packets[0], mine, far, step_count
+    )
     packets = [packets[0]] + [swap(packets[i], "tensor", i) for i in range(1, shards)]
     attention, keys, values = finish(
-        kept,
-        near[0],
         partials,
         key_gain.reshape(1, -1),
         packets,

time: 19.1 us -> 18.5 us (0.969)
  Pallas kernels: 6.55 us -> 5.99 us
  waiting for transfers between devices: 1.78 us -> 1.52 us
    ppermute x5 -> x9, starting transfers between devices: 2.77 us -> 9.95 us  [swap(): return lax.ppermute(block, axis, [(s, s ^ offset) for s in range(count)])]
    ppermute x3 -> x0, starting transfers between devices: 7.01 us -> none  [shift(): lax.ppermute(block, axis, [((s + offset) % count, s) for s in range(count)])]
    pallas_call x1, Pallas kernels: 2.19 us -> 1.67 us  [attend(): pl.pallas_call(functools.partial(attend_kernel, step_count, width // lane...]
    ppermute x3 -> x0, waiting for transfers between devices: 0.42 us -> none  [shift(): lax.ppermute(block, axis, [((s + offset) % count, s) for s in range(count)])]
    ppermute x5 -> x9, waiting for transfers between devices: 1.36 us -> 1.52 us  [swap(): return lax.ppermute(block, axis, [(s, s ^ offset) for s in range(count)])]
  transfers between devices with their start and end apart: 8 -> 9, of which waited for: 5 -> 4; matrix products, arithmetic and copies ran while one was open for 0% -> 0% of each run, Pallas kernels for 18% -> 19%
where the time goes in v11:
time: 18.5 us; the launch traced here: 18.3 us
  starting transfers between devices  9.95 us (54%)
  Pallas kernels  5.99 us (32%)
  waiting for transfers between devices  1.52 us (8%)
  between operations  0.76 us (4%)
    ppermute x9, starting transfers between devices, swap(): return lax.ppermute(block, axis, [(s, s ^ offset) for s in range(count)])  9.95 us
    pallas_call x1, Pallas kernels, attend(): pl.pallas_call(functools.partial(attend_kernel, step_count, width // lane...  1.67 us
    ppermute x9, waiting for transfers between devices, swap(): return lax.ppermute(block, axis, [(s, s ^ offset) for s in range(count)])  1.52 us
    pallas_call x1, Pallas kernels, finish(): pl.pallas_call(functools.partial(finish_kernel, step_count, row_count, he...  1.43 us
    pallas_call x1, Pallas kernels, project(): pl.pallas_call(functools.partial(project_kernel, shards, replicas), out_s...  1.14 us
    pallas_call x1, Pallas kernels, pack(): pl.pallas_call(pack_kernel, out_shape=jax.ShapeDtypeStruct((rows, lanes),...  1.05 us
    pallas_call x1, Pallas kernels, route(): pl.pallas_call(functools.partial(route_kernel, replicas, shards), out_sha...  0.68 us
  transfers between devices with their start and end apart: 9, of which 4 were waited for; matrix products, arithmetic and copies ran while one was open for 0% of the time, Pallas kernels for 19%

profile of v11, /device:TPU:0, one launch (start us, length us, event | category | flops | bytes accessed | tf_op | source)
XLA Modules:
  0.0 18.3 jit_solution(11720807257732276679)
XLA Ops:
  0.6 0.0 slice-start
  0.6 0.0 slice-start.1
  0.7 0.0 copy-start.3
  0.7 1.0 %pack.1.refs_3_.refs_2_ = bf16[224,128]{1,0:T(8,128)(2,1)S(1)} custom-call(bf16[64,320]{1,0:T(8,128)(2,1)} %bitcast.13, bf16[64,512]{1,0:T(8,128)(2,1)} %up_hbm.1), custom_call_target="tpu_custom_call" | custom-call | flops 9437184000 | bytes 9437184 | tf_op jit(solution)/shard_map/pack/pallas_call | solution.py:73
  1.7 5.1 %collective-permute-start.2 = (bf16[224,128]{1,0:T(8,128)(2,1)S(1)}, bf16[224,128]{1,0:T(8,128)(2,1)S(1)}, u32[]{:S(2)}, u32[]{:S(2)}) collective-permute-start(bf16[224,128]{1,0:T(8,128)(2,1)S(1)} %pack.1.refs_3_.refs_2_), channel_id=1, source_target_pairs={{0,12},{4,8},{8,4},{12,0},{1,13},{5,9},{9,5},{13,1},{2,14},{6,10},... | collective-permute-start | bytes 172040 | tf_op jit(solution)/shard_map/ppermute | solution.py:27
  6.8 0.0 collective-permute-start.1
  6.8 0.6 %collective-permute-start = (bf16[224,128]{1,0:T(8,128)(2,1)S(1)}, bf16[224,128]{1,0:T(8,128)(2,1)S(1)}, u32[]{:S(2)}, u32[]{:S(2)}) collective-permute-start(bf16[224,128]{1,0:T(8,128)(2,1)S(1)} %pack.1.refs_3_.refs_2_), channel_id=1, source_target_pairs={{0,4},{4,0},{8,12},{12,8},{1,5},{5,1},{9,13},{13,9},{2,6},{6,2},{1... | collective-permute-start | bytes 172040 | tf_op jit(solution)/shard_map/ppermute | solution.py:27
  7.5 0.0 slice-done
  7.5 0.0 slice-done.1
  7.5 0.0 copy-done.3
  7.5 0.0 copy-start
  7.5 0.0 copy-start.1
  7.5 0.0 copy-start.2
  7.5 1.1 %project.1 = (bf16[128,128]{1,0:T(8,128)(2,1)S(1)}, bf16[128,128]{1,0:T(8,128)(2,1)S(1)}, f32[2,32,512]{2,1,0:T(8,128)S(1)}, bf16[32,1536]{1,0:T(8,128)(2,1)S(1)}) custom-call(s32[4]{0:T(128)} %refs_0_.3, bf16[32,1280]{1,0:T(8,128)(2,1)S(1)} %bitcast.10, bf16[1280,2048]{1,0:T(8,128)(2,1)S(1)} %bitcast.8, bf16[224,128]{1,0:T(8,128)(2,1)S(1)} %pack.1.refs_3_.refs_2_), custom_call_target="tpu_custom_call" | custom-call | flops 167772160 | bytes 5242880 | tf_op jit(solution)/shard_map/project/pallas_call | solution.py:132
  8.7 0.1 collective-permute-start.3
  8.8 0.5 %collective-permute-start.4 = (bf16[128,128]{1,0:T(8,128)(2,1)S(1)}, bf16[128,128]{1,0:T(8,128)(2,1)S(1)}, u32[]{:S(2)}, u32[]{:S(2)}) collective-permute-start(bf16[128,128]{1,0:T(8,128)(2,1)S(1)} %get-tuple-element.26), channel_id=1, source_target_pairs={{0,1},{1,0},{2,3},{3,2},{4,5},{5,4},{6,7},{7,6},{8,9},{9,8},{10,11... | collective-permute-start | bytes 98312 | tf_op jit(solution)/shard_map/ppermute | solution.py:27
  9.2 0.7 %collective-permute-done.3.refs_0_ = bf16[128,128]{1,0:T(8,128)(2,1)S(1)} collective-permute-done((bf16[128,128]{1,0:T(8,128)(2,1)S(1)}, bf16[128,128]{1,0:T(8,128)(2,1)S(1)}, u32[]{:S(2)}, u32[]{:S(2)}) %collective-permute-start.3) | collective-permute-done | bytes 32800 | tf_op jit(solution)/shard_map/ppermute | solution.py:27
  9.9 0.2 collective-permute-done.4.refs_1_
  10.1 1.7 %collective-permute-start.5 = (bf16[128,128]{1,0:T(8,128)(2,1)S(1)}, bf16[128,128]{1,0:T(8,128)(2,1)S(1)}, u32[]{:S(2)}, u32[]{:S(2)}) collective-permute-start(bf16[128,128]{1,0:T(8,128)(2,1)S(1)} %get-tuple-element.29), channel_id=1, source_target_pairs={{0,2},{1,3},{2,0},{3,1},{4,6},{5,7},{6,4},{7,5},{8,10},{9,11},{10,... | collective-permute-start | bytes 98312 | tf_op jit(solution)/shard_map/ppermute | solution.py:27
  11.8 0.0 collective-permute-done.2.refs_5_
  11.8 0.1 collective-permute-done.1.refs_4_
  11.9 0.0 collective-permute-done.refs_3_
  11.9 0.7 %route.1 = (bf16[96,128]{1,0:T(8,128)(2,1)S(1)}, bf16[96,128]{1,0:T(8,128)(2,1)S(1)}, bf16[96,128]{1,0:T(8,128)(2,1)S(1)}, bf16[96,128]{1,0:T(8,128)(2,1)S(1)}) custom-call(s32[4]{0:T(128)} %refs_0_.3, bf16[32,1536]{1,0:T(8,128)(2,1)S(1)} %get-tuple-element.23.refs_1_, bf16[224,128]{1,0:T(8,128)(2,1)S(1)} %pack.1.refs_3_.refs_2_, ...), custom_call_target="tpu_custom_call" | custom-call | bytes 800000 | tf_op jit(solution)/shard_map/route/pallas_call | solution.py:360
  12.6 0.4 %collective-permute-start.6 = (bf16[96,128]{1,0:T(8,128)(2,1)S(1)}, bf16[96,128]{1,0:T(8,128)(2,1)S(1)}, u32[]{:S(2)}, u32[]{:S(2)}) collective-permute-start(bf16[96,128]{1,0:T(8,128)(2,1)S(1)} %get-tuple-element.37), channel_id=1, source_target_pairs={{0,3},{1,2},{2,1},{3,0},{4,7},{5,6},{6,5},{7,4},{8,11},{9,10},{10,... | collective-permute-start | bytes 73736 | tf_op jit(solution)/shard_map/ppermute | solution.py:27
  13.0 1.3 %collective-permute-start.7 = (bf16[96,128]{1,0:T(8,128)(2,1)S(1)}, bf16[96,128]{1,0:T(8,128)(2,1)S(1)}, u32[]{:S(2)}, u32[]{:S(2)}) collective-permute-start(bf16[96,128]{1,0:T(8,128)(2,1)S(1)} %get-tuple-element.38), channel_id=1, source_target_pairs={{0,2},{1,3},{2,0},{3,1},{4,6},{5,7},{6,4},{7,5},{8,10},{9,11},{10,... | collective-permute-start | bytes 73736 | tf_op jit(solution)/shard_map/ppermute | solution.py:27
  14.3 0.2 %collective-permute-start.8 = (bf16[96,128]{1,0:T(8,128)(2,1)S(1)}, bf16[96,128]{1,0:T(8,128)(2,1)S(1)}, u32[]{:S(2)}, u32[]{:S(2)}) collective-permute-start(bf16[96,128]{1,0:T(8,128)(2,1)S(1)} %get-tuple-element.39), channel_id=1, source_target_pairs={{0,1},{1,0},{2,3},{3,2},{4,5},{5,4},{6,7},{7,6},{8,9},{9,8},{10,11... | collective-permute-start | bytes 73736 | tf_op jit(solution)/shard_map/ppermute | solution.py:27
  14.5 0.0 collective-permute-done.5.refs_0_
  14.5 0.0 copy-done
  14.5 0.0 copy-done.1
  14.5 0.0 copy-done.2
  14.6 0.0 copy-start.4
  14.6 1.7 %attend.1 = (f32[32,512]{1,0:T(8,128)S(1)}, bf16[512,128]{1,0:T(8,128)(2,1)S(1)}, f32[512,128]{1,0:T(8,128)S(1)}, f32[512,128]{1,0:T(8,128)S(1)}, f32[512,128]{1...) custom-call(s32[8]{0:T(128)} %lengths_hbm.1, bf16[32,2048]{1,0:T(8,128)(2,1)S(1)} %bitcast.9, ...), custom_call_target="tpu_custom_call" | custom-call | flops 134217728 | bytes 4194304 | tf_op jit(solution)/shard_map/attend/pallas_call | solution.py:287
  16.2 0.0 collective-permute-done.6.refs_8_
  16.2 0.6 %collective-permute-done.7.refs_9_ = bf16[96,128]{1,0:T(8,128)(2,1)S(1)} collective-permute-done((bf16[96,128]{1,0:T(8,128)(2,1)S(1)}, bf16[96,128]{1,0:T(8,128)(2,1)S(1)}, u32[]{:S(2)}, u32[]{:S(2)}) %collective-permute-start.7) | collective-permute-done | bytes 24608 | tf_op jit(solution)/shard_map/ppermute | solution.py:27
  16.8 0.0 collective-permute-done.8.refs_10_
  16.8 0.0 copy-done.4
  16.8 1.4 %finish.1 = (bf16[32,2048]{1,0:T(8,128)(2,1)}, bf16[32,256]{1,0:T(8,128)(2,1)}, bf16[32,256]{1,0:T(8,128)(2,1)}) custom-call(f32[1,128]{1,0:T(1,128)S(1)} %bitcast.11, f32[32,512]{1,0:T(8,128)S(1)} %get-tuple-element.30.refs_1_, bf16[512,128]{1,0:T(8,128)(2,1)S(1)} %get-tuple-element.31.refs_2_, f32[512,128]{1,0:T(8,128)S(1)} %get-tuple-element.32.refs_3_, ...), custom_call_target="tpu_custom_call" | custom-call | bytes 1000000 | tf_op jit(solution)/shard_map/finish/pallas_call | solution.py:480
  (2 shorter events, 0.0 us)
Async XLA Ops:
  0.6 6.8 %slice-start = ((s8[5242880]{0:T(1024)(128)(4,1)}), s8[4194304]{0:T(1024)(128)(4,1)S(1)}, s32[]{:S(2)}) async-start(s8[5242880]{0:T(1024)(128)(4,1)} %bitcast.7), calls=%async_computation | async-start | bytes 8388608
  0.6 6.8 %slice-start.1 = ((s8[5242880]{0:T(1024)(128)(4,1)}), s8[1048576]{0:T(1024)(128)(4,1)S(1)}, s32[]{:S(2)}) async-start(s8[5242880]{0:T(1024)(128)(4,1)} %bitcast.7), calls=%async_computation.1 | async-start | bytes 2097152
  0.7 6.8 %copy-start.3 = (bf16[4,8,1280]{2,1,0:T(8,128)(2,1)S(1)}, bf16[4,8,1280]{2,1,0:T(8,128)(2,1)}, u32[]{:S(2)}) copy-start(bf16[4,8,1280]{2,1,0:T(8,128)(2,1)} %param.10) | copy-start | bytes 245764
  1.7 10.1 %collective-permute-start.2 = (bf16[224,128]{1,0:T(8,128)(2,1)S(1)}, bf16[224,128]{1,0:T(8,128)(2,1)S(1)}, u32[]{:S(2)}, u32[]{:S(2)}) collective-permute-start(bf16[224,128]{1,0:T(8,128)(2,1)S(1)} %pack.1.refs_3_.refs_2_), channel_id=1, source_target_pairs={{0,12},{4,8},{8,4},{12,0},{1,13},{5,9},{9,5},{13,1},{2,14},{6,10},... | collective-permute-start | bytes 172040 | tf_op jit(solution)/shard_map/ppermute | solution.py:27
  6.8 5.1 %collective-permute-start.1 = (bf16[224,128]{1,0:T(8,128)(2,1)S(1)}, bf16[224,128]{1,0:T(8,128)(2,1)S(1)}, u32[]{:S(2)}, u32[]{:S(2)}) collective-permute-start(bf16[224,128]{1,0:T(8,128)(2,1)S(1)} %pack.1.refs_3_.refs_2_), channel_id=1, source_target_pairs={{0,8},{4,12},{8,0},{12,4},{1,9},{5,13},{9,1},{13,5},{2,10},{6,14},... | collective-permute-start | bytes 172040 | tf_op jit(solution)/shard_map/ppermute | solution.py:27
  6.8 5.1 %collective-permute-start = (bf16[224,128]{1,0:T(8,128)(2,1)S(1)}, bf16[224,128]{1,0:T(8,128)(2,1)S(1)}, u32[]{:S(2)}, u32[]{:S(2)}) collective-permute-start(bf16[224,128]{1,0:T(8,128)(2,1)S(1)} %pack.1.refs_3_.refs_2_), channel_id=1, source_target_pairs={{0,4},{4,0},{8,12},{12,8},{1,5},{5,1},{9,13},{13,9},{2,6},{6,2},{1... | collective-permute-start | bytes 172040 | tf_op jit(solution)/shard_map/ppermute | solution.py:27
  7.5 7.0 %copy-start = (bf16[8,512,256]{2,1,0:T(8,128)(2,1)S(1)}, bf16[8,512,256]{2,1,0:T(8,128)(2,1)}, u32[]{:S(2)}) copy-start(bf16[8,512,256]{2,1,0:T(8,128)(2,1)} %keys_ref.1) | copy-start | bytes 6291460
  7.5 7.0 %copy-start.1 = (bf16[8,512,256]{2,1,0:T(8,128)(2,1)S(1)}, bf16[8,512,256]{2,1,0:T(8,128)(2,1)}, u32[]{:S(2)}) copy-start(bf16[8,512,256]{2,1,0:T(8,128)(2,1)} %values_ref.1) | copy-start | bytes 6291460
  7.5 7.0 %copy-start.2 = (bf16[4,8,2048]{2,1,0:T(8,128)(2,1)S(1)}, bf16[4,8,2048]{2,1,0:T(8,128)(2,1)}, u32[]{:S(2)}) copy-start(bf16[4,8,2048]{2,1,0:T(8,128)(2,1)} %param.15) | copy-start | bytes 393220
  8.7 1.3 %collective-permute-start.3 = (bf16[128,128]{1,0:T(8,128)(2,1)S(1)}, bf16[128,128]{1,0:T(8,128)(2,1)S(1)}, u32[]{:S(2)}, u32[]{:S(2)}) collective-permute-start(bf16[128,128]{1,0:T(8,128)(2,1)S(1)} %get-tuple-element.25), channel_id=1, source_target_pairs={{0,1},{1,0},{2,3},{3,2},{4,5},{5,4},{6,7},{7,6},{8,9},{9,8},{10,11... | collective-permute-start | bytes 98312 | tf_op jit(solution)/shard_map/ppermute | solution.py:27
  8.8 1.4 %collective-permute-start.4 = (bf16[128,128]{1,0:T(8,128)(2,1)S(1)}, bf16[128,128]{1,0:T(8,128)(2,1)S(1)}, u32[]{:S(2)}, u32[]{:S(2)}) collective-permute-start(bf16[128,128]{1,0:T(8,128)(2,1)S(1)} %get-tuple-element.26), channel_id=1, source_target_pairs={{0,1},{1,0},{2,3},{3,2},{4,5},{5,4},{6,7},{7,6},{8,9},{9,8},{10,11... | collective-permute-start | bytes 98312 | tf_op jit(solution)/shard_map/ppermute | solution.py:27
  10.1 4.4 %collective-permute-start.5 = (bf16[128,128]{1,0:T(8,128)(2,1)S(1)}, bf16[128,128]{1,0:T(8,128)(2,1)S(1)}, u32[]{:S(2)}, u32[]{:S(2)}) collective-permute-start(bf16[128,128]{1,0:T(8,128)(2,1)S(1)} %get-tuple-element.29), channel_id=1, source_target_pairs={{0,2},{1,3},{2,0},{3,1},{4,6},{5,7},{6,4},{7,5},{8,10},{9,11},{10,... | collective-permute-start | bytes 98312 | tf_op jit(solution)/shard_map/ppermute | solution.py:27
  12.6 3.6 %collective-permute-start.6 = (bf16[96,128]{1,0:T(8,128)(2,1)S(1)}, bf16[96,128]{1,0:T(8,128)(2,1)S(1)}, u32[]{:S(2)}, u32[]{:S(2)}) collective-permute-start(bf16[96,128]{1,0:T(8,128)(2,1)S(1)} %get-tuple-element.37), channel_id=1, source_target_pairs={{0,3},{1,2},{2,1},{3,0},{4,7},{5,6},{6,5},{7,4},{8,11},{9,10},{10,... | collective-permute-start | bytes 73736 | tf_op jit(solution)/shard_map/ppermute | solution.py:27
  13.0 3.8 %collective-permute-start.7 = (bf16[96,128]{1,0:T(8,128)(2,1)S(1)}, bf16[96,128]{1,0:T(8,128)(2,1)S(1)}, u32[]{:S(2)}, u32[]{:S(2)}) collective-permute-start(bf16[96,128]{1,0:T(8,128)(2,1)S(1)} %get-tuple-element.38), channel_id=1, source_target_pairs={{0,2},{1,3},{2,0},{3,1},{4,6},{5,7},{6,4},{7,5},{8,10},{9,11},{10,... | collective-permute-start | bytes 73736 | tf_op jit(solution)/shard_map/ppermute | solution.py:27
  14.3 2.5 %collective-permute-start.8 = (bf16[96,128]{1,0:T(8,128)(2,1)S(1)}, bf16[96,128]{1,0:T(8,128)(2,1)S(1)}, u32[]{:S(2)}, u32[]{:S(2)}) collective-permute-start(bf16[96,128]{1,0:T(8,128)(2,1)S(1)} %get-tuple-element.39), channel_id=1, source_target_pairs={{0,1},{1,0},{2,3},{3,2},{4,5},{5,4},{6,7},{7,6},{8,9},{9,8},{10,11... | collective-permute-start | bytes 73736 | tf_op jit(solution)/shard_map/ppermute | solution.py:27
  14.6 2.3 %copy-start.4 = (f32[128]{0:T(128)S(1)}, f32[128]{0:T(128)}, u32[]{:S(2)}) copy-start(f32[128]{0:T(128)} %param.14) | copy-start | bytes 1540

commit v12 on v11

--- a/solution.py
+++ b/solution.py
@@ -50,7 +50,7 @@
         pltpu.make_async_copy(up_hbm.at[pl.ds(start, rank_part), :], up_ref, sems.at[1]),
     ]
     for copy in copies:
-        copy.start()
+        copy.start(priority=1)
     for copy in copies:
         copy.wait()
     first = 0
@@ -314,9 +314,14 @@
     )(*in_hbm(lengths), queries, keys, values, after, mine, *far)
 
 
+def piece_places(replicas):
+    order = [0, 1] + list(range(replicas - 1, 1, -1))
+    return [order.index(i) for i in range(replicas)]
+
+
 def route_kernel(replicas, shards, *refs):
     owners_hbm, left_ref = refs[:2]
-    piece_refs = refs[2 : 2 + replicas]
+    piece_refs = [refs[2 + place] for place in piece_places(replicas)]
     out_refs = refs[3 + replicas : 3 + replicas + shards]
     owners_ref, right, up_buf, owner_sem = refs[3 + replicas + shards :]
     owners_copy = pltpu.make_async_copy(owners_hbm, owners_ref, owner_sem)
@@ -371,7 +376,7 @@
         compiler_params=pltpu.CompilerParams(vmem_limit_bytes=4 * 2**20),
         name="route",
         cost_estimate=pl.CostEstimate(flops=0, bytes_accessed=800000, transcendentals=0),
-    )(*in_hbm(owners), left, *pieces, after)
+    )(*in_hbm(owners), left, *[pieces[i] for i in piece_places(replicas)], after)
 
 
 def route_plain(owners, tokens, down, up, rank_part, own, shards):

time: 18.5 us -> 18.3 us (0.989)
  starting transfers between devices: 9.95 us -> 9.72 us
    ppermute x9, starting transfers between devices: 9.95 us -> 9.72 us  [swap(): return lax.ppermute(block, axis, [(s, s ^ offset) for s in range(count)])]
  transfers between devices with their start and end apart: 9 -> 9, of which waited for: 4 -> 5; matrix products, arithmetic and copies ran while one was open for 0% -> 0% of each run, Pallas kernels for 19% -> 19%
where the time goes in v12:
time: 18.3 us; the launch traced here: 18.1 us
  starting transfers between devices  9.72 us (53%)
  Pallas kernels  5.98 us (33%)
  waiting for transfers between devices  1.55 us (8%)
  between operations  0.77 us (4%)
    ppermute x9, starting transfers between devices, swap(): return lax.ppermute(block, axis, [(s, s ^ offset) for s in range(count)])  9.72 us
    pallas_call x1, Pallas kernels, attend(): pl.pallas_call(functools.partial(attend_kernel, step_count, width // lane...  1.66 us
    ppermute x9, waiting for transfers between devices, swap(): return lax.ppermute(block, axis, [(s, s ^ offset) for s in range(count)])  1.55 us
    pallas_call x1, Pallas kernels, finish(): pl.pallas_call(functools.partial(finish_kernel, step_count, row_count, he...  1.43 us
    pallas_call x1, Pallas kernels, project(): pl.pallas_call(functools.partial(project_kernel, shards, replicas), out_s...  1.14 us
    pallas_call x1, Pallas kernels, pack(): pl.pallas_call(pack_kernel, out_shape=jax.ShapeDtypeStruct((rows, lanes),...  1.05 us
    pallas_call x1, Pallas kernels, route(): pl.pallas_call(functools.partial(route_kernel, replicas, shards), out_sha...  0.68 us
  transfers between devices with their start and end apart: 9, of which 5 were waited for; matrix products, arithmetic and copies ran while one was open for 0% of the time, Pallas kernels for 19%

profile of v12, /device:TPU:0, one launch (start us, length us, event | category | flops | bytes accessed | tf_op | source)
XLA Modules:
  0.0 18.1 jit_solution(5756075481439860245)
XLA Ops:
  0.6 0.0 slice-start
  0.6 0.0 slice-start.1
  0.7 0.0 copy-start.3
  0.7 1.0 %pack.1.refs_3_.refs_2_ = bf16[224,128]{1,0:T(8,128)(2,1)S(1)} custom-call(bf16[64,320]{1,0:T(8,128)(2,1)} %bitcast.13, bf16[64,512]{1,0:T(8,128)(2,1)} %up_hbm.1), custom_call_target="tpu_custom_call" | custom-call | flops 9437184000 | bytes 9437184 | tf_op jit(solution)/shard_map/pack/pallas_call | solution.py:73
  1.7 4.1 %collective-permute-start.2 = (bf16[224,128]{1,0:T(8,128)(2,1)S(1)}, bf16[224,128]{1,0:T(8,128)(2,1)S(1)}, u32[]{:S(2)}, u32[]{:S(2)}) collective-permute-start(bf16[224,128]{1,0:T(8,128)(2,1)S(1)} %pack.1.refs_3_.refs_2_), channel_id=1, source_target_pairs={{0,8},{4,12},{8,0},{12,4},{1,9},{5,13},{9,1},{13,5},{2,10},{6,14},... | collective-permute-start | bytes 172040 | tf_op jit(solution)/shard_map/ppermute | solution.py:27
  5.8 1.3 %collective-permute-start.1 = (bf16[224,128]{1,0:T(8,128)(2,1)S(1)}, bf16[224,128]{1,0:T(8,128)(2,1)S(1)}, u32[]{:S(2)}, u32[]{:S(2)}) collective-permute-start(bf16[224,128]{1,0:T(8,128)(2,1)S(1)} %pack.1.refs_3_.refs_2_), channel_id=1, source_target_pairs={{0,12},{4,8},{8,4},{12,0},{1,13},{5,9},{9,5},{13,1},{2,14},{6,10},... | collective-permute-start | bytes 172040 | tf_op jit(solution)/shard_map/ppermute | solution.py:27
  7.2 0.2 %collective-permute-start = (bf16[224,128]{1,0:T(8,128)(2,1)S(1)}, bf16[224,128]{1,0:T(8,128)(2,1)S(1)}, u32[]{:S(2)}, u32[]{:S(2)}) collective-permute-start(bf16[224,128]{1,0:T(8,128)(2,1)S(1)} %pack.1.refs_3_.refs_2_), channel_id=1, source_target_pairs={{0,4},{4,0},{8,12},{12,8},{1,5},{5,1},{9,13},{13,9},{2,6},{6,2},{1... | collective-permute-start | bytes 172040 | tf_op jit(solution)/shard_map/ppermute | solution.py:27
  7.4 0.0 slice-done
  7.4 0.0 slice-done.1
  7.4 0.0 copy-done.3
  7.4 0.0 copy-start
  7.4 0.0 copy-start.1
  7.4 0.0 copy-start.2
  7.4 1.1 %project.1 = (bf16[128,128]{1,0:T(8,128)(2,1)S(1)}, bf16[128,128]{1,0:T(8,128)(2,1)S(1)}, f32[2,32,512]{2,1,0:T(8,128)S(1)}, bf16[32,1536]{1,0:T(8,128)(2,1)S(1)}) custom-call(s32[4]{0:T(128)} %refs_0_.3, bf16[32,1280]{1,0:T(8,128)(2,1)S(1)} %bitcast.10, bf16[1280,2048]{1,0:T(8,128)(2,1)S(1)} %bitcast.8, bf16[224,128]{1,0:T(8,128)(2,1)S(1)} %pack.1.refs_3_.refs_2_), custom_call_target="tpu_custom_call" | custom-call | flops 167772160 | bytes 5242880 | tf_op jit(solution)/shard_map/project/pallas_call | solution.py:132
  8.6 0.1 collective-permute-start.3
  8.7 0.5 %collective-permute-start.4 = (bf16[128,128]{1,0:T(8,128)(2,1)S(1)}, bf16[128,128]{1,0:T(8,128)(2,1)S(1)}, u32[]{:S(2)}, u32[]{:S(2)}) collective-permute-start(bf16[128,128]{1,0:T(8,128)(2,1)S(1)} %get-tuple-element.26), channel_id=1, source_target_pairs={{0,1},{1,0},{2,3},{3,2},{4,5},{5,4},{6,7},{7,6},{8,9},{9,8},{10,11... | collective-permute-start | bytes 98312 | tf_op jit(solution)/shard_map/ppermute | solution.py:27
  9.2 0.7 %collective-permute-done.3.refs_0_ = bf16[128,128]{1,0:T(8,128)(2,1)S(1)} collective-permute-done((bf16[128,128]{1,0:T(8,128)(2,1)S(1)}, bf16[128,128]{1,0:T(8,128)(2,1)S(1)}, u32[]{:S(2)}, u32[]{:S(2)}) %collective-permute-start.3) | collective-permute-done | bytes 32800 | tf_op jit(solution)/shard_map/ppermute | solution.py:27
  9.9 0.2 collective-permute-done.4.refs_1_
  10.0 1.6 %collective-permute-start.5 = (bf16[128,128]{1,0:T(8,128)(2,1)S(1)}, bf16[128,128]{1,0:T(8,128)(2,1)S(1)}, u32[]{:S(2)}, u32[]{:S(2)}) collective-permute-start(bf16[128,128]{1,0:T(8,128)(2,1)S(1)} %get-tuple-element.29), channel_id=1, source_target_pairs={{0,2},{1,3},{2,0},{3,1},{4,6},{5,7},{6,4},{7,5},{8,10},{9,11},{10,... | collective-permute-start | bytes 98312 | tf_op jit(solution)/shard_map/ppermute | solution.py:27
  11.6 0.0 collective-permute-done.2.refs_5_
  11.6 0.3 %collective-permute-done.1.refs_4_ = bf16[224,128]{1,0:T(8,128)(2,1)S(1)} collective-permute-done((bf16[224,128]{1,0:T(8,128)(2,1)S(1)}, bf16[224,128]{1,0:T(8,128)(2,1)S(1)}, u32[]{:S(2)}, u32[]{:S(2)}) %collective-permute-start.1) | collective-permute-done | bytes 57376 | tf_op jit(solution)/shard_map/ppermute | solution.py:27
  11.9 0.1 collective-permute-done.refs_3_
  12.0 0.7 %route.1 = (bf16[96,128]{1,0:T(8,128)(2,1)S(1)}, bf16[96,128]{1,0:T(8,128)(2,1)S(1)}, bf16[96,128]{1,0:T(8,128)(2,1)S(1)}, bf16[96,128]{1,0:T(8,128)(2,1)S(1)}) custom-call(s32[4]{0:T(128)} %refs_0_.3, bf16[32,1536]{1,0:T(8,128)(2,1)S(1)} %get-tuple-element.23.refs_1_, bf16[224,128]{1,0:T(8,128)(2,1)S(1)} %pack.1.refs_3_.refs_2_, ...), custom_call_target="tpu_custom_call" | custom-call | bytes 800000 | tf_op jit(solution)/shard_map/route/pallas_call | solution.py:365
  12.7 0.1 collective-permute-start.6
  12.7 1.6 %collective-permute-start.7 = (bf16[96,128]{1,0:T(8,128)(2,1)S(1)}, bf16[96,128]{1,0:T(8,128)(2,1)S(1)}, u32[]{:S(2)}, u32[]{:S(2)}) collective-permute-start(bf16[96,128]{1,0:T(8,128)(2,1)S(1)} %get-tuple-element.38), channel_id=1, source_target_pairs={{0,2},{1,3},{2,0},{3,1},{4,6},{5,7},{6,4},{7,5},{8,10},{9,11},{10,... | collective-permute-start | bytes 73736 | tf_op jit(solution)/shard_map/ppermute | solution.py:27
  14.3 0.3 %collective-permute-start.8 = (bf16[96,128]{1,0:T(8,128)(2,1)S(1)}, bf16[96,128]{1,0:T(8,128)(2,1)S(1)}, u32[]{:S(2)}, u32[]{:S(2)}) collective-permute-start(bf16[96,128]{1,0:T(8,128)(2,1)S(1)} %get-tuple-element.39), channel_id=1, source_target_pairs={{0,1},{1,0},{2,3},{3,2},{4,5},{5,4},{6,7},{7,6},{8,9},{9,8},{10,11... | collective-permute-start | bytes 73736 | tf_op jit(solution)/shard_map/ppermute | solution.py:27
  14.6 0.0 collective-permute-done.5.refs_0_
  14.6 0.0 copy-done
  14.6 0.0 copy-done.1
  14.6 0.0 copy-done.2
  14.6 0.0 copy-start.4
  14.6 1.7 %attend.1 = (f32[32,512]{1,0:T(8,128)S(1)}, bf16[512,128]{1,0:T(8,128)(2,1)S(1)}, f32[512,128]{1,0:T(8,128)S(1)}, f32[512,128]{1,0:T(8,128)S(1)}, f32[512,128]{1...) custom-call(s32[8]{0:T(128)} %lengths_hbm.1, bf16[32,2048]{1,0:T(8,128)(2,1)S(1)} %bitcast.9, ...), custom_call_target="tpu_custom_call" | custom-call | flops 134217728 | bytes 4194304 | tf_op jit(solution)/shard_map/attend/pallas_call | solution.py:287
  16.3 0.0 collective-permute-done.6.refs_8_
  16.3 0.3 %collective-permute-done.7.refs_9_ = bf16[96,128]{1,0:T(8,128)(2,1)S(1)} collective-permute-done((bf16[96,128]{1,0:T(8,128)(2,1)S(1)}, bf16[96,128]{1,0:T(8,128)(2,1)S(1)}, u32[]{:S(2)}, u32[]{:S(2)}) %collective-permute-start.7) | collective-permute-done | bytes 24608 | tf_op jit(solution)/shard_map/ppermute | solution.py:27
  16.6 0.0 collective-permute-done.8.refs_10_
  16.6 0.0 copy-done.4
  16.6 1.4 %finish.1 = (bf16[32,2048]{1,0:T(8,128)(2,1)}, bf16[32,256]{1,0:T(8,128)(2,1)}, bf16[32,256]{1,0:T(8,128)(2,1)}) custom-call(f32[1,128]{1,0:T(1,128)S(1)} %bitcast.11, f32[32,512]{1,0:T(8,128)S(1)} %get-tuple-element.30.refs_1_, bf16[512,128]{1,0:T(8,128)(2,1)S(1)} %get-tuple-element.31.refs_2_, f32[512,128]{1,0:T(8,128)S(1)} %get-tuple-element.32.refs_3_, ...), custom_call_target="tpu_custom_call" | custom-call | bytes 1000000 | tf_op jit(solution)/shard_map/finish/pallas_call | solution.py:485
  (2 shorter events, 0.0 us)
Async XLA Ops:
  0.6 6.8 %slice-start = ((s8[5242880]{0:T(1024)(128)(4,1)}), s8[4194304]{0:T(1024)(128)(4,1)S(1)}, s32[]{:S(2)}) async-start(s8[5242880]{0:T(1024)(128)(4,1)} %bitcast.7), calls=%async_computation | async-start | bytes 8388608
  0.6 6.8 %slice-start.1 = ((s8[5242880]{0:T(1024)(128)(4,1)}), s8[1048576]{0:T(1024)(128)(4,1)S(1)}, s32[]{:S(2)}) async-start(s8[5242880]{0:T(1024)(128)(4,1)} %bitcast.7), calls=%async_computation.1 | async-start | bytes 2097152
  0.7 6.8 %copy-start.3 = (bf16[4,8,1280]{2,1,0:T(8,128)(2,1)S(1)}, bf16[4,8,1280]{2,1,0:T(8,128)(2,1)}, u32[]{:S(2)}) copy-start(bf16[4,8,1280]{2,1,0:T(8,128)(2,1)} %param.10) | copy-start | bytes 245764
  1.7 9.9 %collective-permute-start.2 = (bf16[224,128]{1,0:T(8,128)(2,1)S(1)}, bf16[224,128]{1,0:T(8,128)(2,1)S(1)}, u32[]{:S(2)}, u32[]{:S(2)}) collective-permute-start(bf16[224,128]{1,0:T(8,128)(2,1)S(1)} %pack.1.refs_3_.refs_2_), channel_id=1, source_target_pairs={{0,8},{4,12},{8,0},{12,4},{1,9},{5,13},{9,1},{13,5},{2,10},{6,14},... | collective-permute-start | bytes 172040 | tf_op jit(solution)/shard_map/ppermute | solution.py:27
  5.8 6.1 %collective-permute-start.1 = (bf16[224,128]{1,0:T(8,128)(2,1)S(1)}, bf16[224,128]{1,0:T(8,128)(2,1)S(1)}, u32[]{:S(2)}, u32[]{:S(2)}) collective-permute-start(bf16[224,128]{1,0:T(8,128)(2,1)S(1)} %pack.1.refs_3_.refs_2_), channel_id=1, source_target_pairs={{0,12},{4,8},{8,4},{12,0},{1,13},{5,9},{9,5},{13,1},{2,14},{6,10},... | collective-permute-start | bytes 172040 | tf_op jit(solution)/shard_map/ppermute | solution.py:27
  7.2 4.8 %collective-permute-start = (bf16[224,128]{1,0:T(8,128)(2,1)S(1)}, bf16[224,128]{1,0:T(8,128)(2,1)S(1)}, u32[]{:S(2)}, u32[]{:S(2)}) collective-permute-start(bf16[224,128]{1,0:T(8,128)(2,1)S(1)} %pack.1.refs_3_.refs_2_), channel_id=1, source_target_pairs={{0,4},{4,0},{8,12},{12,8},{1,5},{5,1},{9,13},{13,9},{2,6},{6,2},{1... | collective-permute-start | bytes 172040 | tf_op jit(solution)/shard_map/ppermute | solution.py:27
  7.4 7.2 %copy-start = (bf16[8,512,256]{2,1,0:T(8,128)(2,1)S(1)}, bf16[8,512,256]{2,1,0:T(8,128)(2,1)}, u32[]{:S(2)}) copy-start(bf16[8,512,256]{2,1,0:T(8,128)(2,1)} %keys_ref.1) | copy-start | bytes 6291460
  7.4 7.2 %copy-start.1 = (bf16[8,512,256]{2,1,0:T(8,128)(2,1)S(1)}, bf16[8,512,256]{2,1,0:T(8,128)(2,1)}, u32[]{:S(2)}) copy-start(bf16[8,512,256]{2,1,0:T(8,128)(2,1)} %values_ref.1) | copy-start | bytes 6291460
  7.4 7.2 %copy-start.2 = (bf16[4,8,2048]{2,1,0:T(8,128)(2,1)S(1)}, bf16[4,8,2048]{2,1,0:T(8,128)(2,1)}, u32[]{:S(2)}) copy-start(bf16[4,8,2048]{2,1,0:T(8,128)(2,1)} %param.15) | copy-start | bytes 393220
  8.6 1.3 %collective-permute-start.3 = (bf16[128,128]{1,0:T(8,128)(2,1)S(1)}, bf16[128,128]{1,0:T(8,128)(2,1)S(1)}, u32[]{:S(2)}, u32[]{:S(2)}) collective-permute-start(bf16[128,128]{1,0:T(8,128)(2,1)S(1)} %get-tuple-element.25), channel_id=1, source_target_pairs={{0,1},{1,0},{2,3},{3,2},{4,5},{5,4},{6,7},{7,6},{8,9},{9,8},{10,11... | collective-permute-start | bytes 98312 | tf_op jit(solution)/shard_map/ppermute | solution.py:27
  8.7 1.4 %collective-permute-start.4 = (bf16[128,128]{1,0:T(8,128)(2,1)S(1)}, bf16[128,128]{1,0:T(8,128)(2,1)S(1)}, u32[]{:S(2)}, u32[]{:S(2)}) collective-permute-start(bf16[128,128]{1,0:T(8,128)(2,1)S(1)} %get-tuple-element.26), channel_id=1, source_target_pairs={{0,1},{1,0},{2,3},{3,2},{4,5},{5,4},{6,7},{7,6},{8,9},{9,8},{10,11... | collective-permute-start | bytes 98312 | tf_op jit(solution)/shard_map/ppermute | solution.py:27
  10.0 4.5 %collective-permute-start.5 = (bf16[128,128]{1,0:T(8,128)(2,1)S(1)}, bf16[128,128]{1,0:T(8,128)(2,1)S(1)}, u32[]{:S(2)}, u32[]{:S(2)}) collective-permute-start(bf16[128,128]{1,0:T(8,128)(2,1)S(1)} %get-tuple-element.29), channel_id=1, source_target_pairs={{0,2},{1,3},{2,0},{3,1},{4,6},{5,7},{6,4},{7,5},{8,10},{9,11},{10,... | collective-permute-start | bytes 98312 | tf_op jit(solution)/shard_map/ppermute | solution.py:27
  12.7 3.6 %collective-permute-start.6 = (bf16[96,128]{1,0:T(8,128)(2,1)S(1)}, bf16[96,128]{1,0:T(8,128)(2,1)S(1)}, u32[]{:S(2)}, u32[]{:S(2)}) collective-permute-start(bf16[96,128]{1,0:T(8,128)(2,1)S(1)} %get-tuple-element.37), channel_id=1, source_target_pairs={{0,3},{1,2},{2,1},{3,0},{4,7},{5,6},{6,5},{7,4},{8,11},{9,10},{10,... | collective-permute-start | bytes 73736 | tf_op jit(solution)/shard_map/ppermute | solution.py:27
  12.7 3.9 %collective-permute-start.7 = (bf16[96,128]{1,0:T(8,128)(2,1)S(1)}, bf16[96,128]{1,0:T(8,128)(2,1)S(1)}, u32[]{:S(2)}, u32[]{:S(2)}) collective-permute-start(bf16[96,128]{1,0:T(8,128)(2,1)S(1)} %get-tuple-element.38), channel_id=1, source_target_pairs={{0,2},{1,3},{2,0},{3,1},{4,6},{5,7},{6,4},{7,5},{8,10},{9,11},{10,... | collective-permute-start | bytes 73736 | tf_op jit(solution)/shard_map/ppermute | solution.py:27
  14.3 2.3 %collective-permute-start.8 = (bf16[96,128]{1,0:T(8,128)(2,1)S(1)}, bf16[96,128]{1,0:T(8,128)(2,1)S(1)}, u32[]{:S(2)}, u32[]{:S(2)}) collective-permute-start(bf16[96,128]{1,0:T(8,128)(2,1)S(1)} %get-tuple-element.39), channel_id=1, source_target_pairs={{0,1},{1,0},{2,3},{3,2},{4,5},{5,4},{6,7},{7,6},{8,9},{9,8},{10,11... | collective-permute-start | bytes 73736 | tf_op jit(solution)/shard_map/ppermute | solution.py:27
  14.6 2.0 %copy-start.4 = (f32[128]{0:T(128)S(1)}, f32[128]{0:T(128)}, u32[]{:S(2)}) copy-start(f32[128]{0:T(128)} %param.14) | copy-start | bytes 1540

commit v13 on v10

--- a/solution.py
+++ b/solution.py
@@ -25,11 +25,6 @@
 def swap(block, axis, offset):
     count = lax.axis_size(axis)
     return lax.ppermute(block, axis, [(s, s ^ offset) for s in range(count)])
-
-
-def shift(block, axis, offset):
-    count = lax.axis_size(axis)
-    return lax.ppermute(block, axis, [((s + offset) % count, s) for s in range(count)])
 
 
 def in_hbm(*arrays):
@@ -55,7 +50,7 @@
         pltpu.make_async_copy(up_hbm.at[pl.ds(start, rank_part), :], up_ref, sems.at[1]),
     ]
     for copy in copies:
-        copy.start()
+        copy.start(priority=1)
     for copy in copies:
         copy.wait()
     first = 0
@@ -93,28 +88,31 @@
 
 def project_kernel(shards, replicas, *refs):
     owners_hbm, tokens_ref, weight_ref, _ = refs[:4]
-    pairs = shards // 2
-    near_refs = refs[4 : 4 + pairs]
-    kept_ref, left_ref, owners_ref, token_buf, owner_sem = refs[4 + pairs :]
+    own_ref, near_ref = refs[4:6]
+    far_refs = refs[6 : 4 + shards]
+    left_ref, pick_ref, owners_ref, token_buf, owner_sem = refs[4 + shards :]
     owners_copy = pltpu.make_async_copy(owners_hbm, owners_ref, owner_sem)
     owners_copy.start()
 
     shard = lax.axis_index("tensor")
-    _, rows, own = kept_ref.shape
+    rows, own = own_ref.shape
     for i in range(shards):
         first = pl.multiple_of((shard ^ i) * own, lanes)
         block = jnp.dot(
             tokens_ref[...], weight_ref[:, pl.ds(first, own)], preferred_element_type=f32
         )
-        if i % 2 == 0:
-            kept_ref[i // 2] = block
-            continue
-        for c in range(own // lanes):
-            near_refs[i // 2][c * rows : (c + 1) * rows, :] = block[
-                :, c * lanes : (c + 1) * lanes
-            ].astype(bf16)
+        if i == 0:
+            own_ref[...] = block
+        elif i > 1:
+            far_refs[i - 2][...] = block
+        else:
+            for c in range(own // lanes):
+                near_ref[c * rows : (c + 1) * rows, :] = block[
+                    :, c * lanes : (c + 1) * lanes
+                ].astype(bf16)
 
     owners_copy.wait()
+    replica = lax.axis_index("rollout")
     width = token_buf.shape[2]
     down_rows = tokens_ref.shape[1] // replicas
     for k in range(replicas):
@@ -122,27 +120,35 @@
         if down_rows < width:
             token_buf[k, :, down_rows:] = jnp.zeros((rows, width - down_rows), bf16)
     for i in range(replicas):
-        source = lax.rem(lax.axis_index("rollout") + i, replicas)
         place = jnp.int32(0)
         for k in range(1, replicas):
-            place = place + jnp.where(owners_ref[k] == source, k, 0)
+            place = place + jnp.where(owners_ref[k] == replica ^ i, k, 0)
         left_ref[:, i * width : (i + 1) * width] = token_buf[place]
+    if replicas > 1:
+        for i in range(shards):
+            for k in range(replicas):
+                picked = jnp.where(owners_ref[shard ^ i] == replica ^ k, 1.0, 0.0)
+                row = i * replicas + k
+                pick_ref[row : row + 1, :] = jnp.full((1, lanes), picked, f32)
 
 
 def project(owners, tokens, weight, after, shards, replicas):
     rows, depth = tokens.shape
     own = weight.shape[1] // shards
-    pairs = shards // 2
     piece_width = -(-depth // replicas // lanes) * lanes
-    outs = pl.pallas_call(
+    mine, near, *rest = pl.pallas_call(
         functools.partial(project_kernel, shards, replicas),
-        out_shape=[jax.ShapeDtypeStruct((rows * own // lanes, lanes), bf16)] * pairs
+        out_shape=[
+            jax.ShapeDtypeStruct((rows, own), f32),
+            jax.ShapeDtypeStruct((rows * own // lanes, lanes), bf16),
+        ]
+        + [jax.ShapeDtypeStruct((rows, own), f32)] * (shards - 2)
         + [
-            jax.ShapeDtypeStruct((pairs, rows, own), f32),
             jax.ShapeDtypeStruct((rows, replicas * piece_width), bf16),
+            jax.ShapeDtypeStruct((shards * replicas, lanes), f32),
         ],
         in_specs=[stays_in_hbm] + [whole_in_vmem] * 3,
-        out_specs=[whole_in_vmem] * (pairs + 2),
+        out_specs=[whole_in_vmem] * (shards + 2),
         scratch_shapes=[
             pltpu.SMEM(owners.shape, jnp.int32),
             pltpu.VMEM((replicas, rows, piece_width), bf16),
@@ -154,7 +160,7 @@
             flops=2 * rows * weight.size, bytes_accessed=2 * weight.size, transcendentals=0
         ),
     )(*in_hbm(owners), tokens, weight, after)
-    return outs[:pairs], *outs[pairs:]
+    return mine, near, rest[:-2], *rest[-2:]
 
 
 def attend_kernel(
@@ -290,31 +296,22 @@
     )(*in_hbm(lengths), queries, keys, values, after)
 
 
-def add_near(kept, near):
-    rows, own = kept.shape
-    return [
-        kept[:, c * lanes : (c + 1) * lanes] + near[c * rows : (c + 1) * rows, :].astype(f32)
-        for c in range(own // lanes)
-    ]
-
-
-def carries_sums(i):
-    return i > 0 and i % 2 == 0
+def piece_places(replicas):
+    order = [0, 1] + list(range(replicas - 1, 1, -1))
+    return [order.index(i) for i in range(replicas)]
 
 
 def route_kernel(replicas, shards, *refs):
-    owners_hbm, left_ref, kept_ref = refs[:3]
-    piece_refs = refs[3 : 3 + replicas]
-    near_refs = refs[3 + replicas : 3 + replicas + shards // 2]
-    out_refs = refs[3 + replicas + shards // 2 : 3 + replicas + shards // 2 + shards]
-    owners_ref, right, up_buf, owner_sem = refs[3 + replicas + shards // 2 + shards :]
-    owners_copy = pltpu.make_async_copy(owners_hbm, owners_ref, owner_sem)
-    owners_copy.start()
+    left_ref, pick_ref, near_ref = refs[:3]
+    piece_refs = [refs[3 + place] for place in piece_places(replicas)]
+    out_refs = refs[3 + replicas : 3 + replicas + shards]
+    (right,) = refs[3 + replicas + shards :]
+    up_rows = out_refs[0].shape[0] - left_ref.shape[0]
     rows = left_ref.shape[0]
     rank = right.shape[0]
     width = right.shape[1] // replicas
     half = rank // 2
-    rest = (piece_refs[0].shape[0] - up_buf.shape[1]) % rank
+    rest = (piece_refs[0].shape[0] - up_rows) % rank
     for i in range(replicas):
         first = 0
         for c in range(width // lanes - (1 if rest else 0)):
@@ -329,52 +326,41 @@
                 [tail, jnp.zeros((rank, lanes // 2), bf16)], axis=1
             )
             first += half
-        up_buf[i] = piece_refs[i][first:, :]
     lowered = lax.dot_general(
         left_ref[...], right[...], (((1,), (1,)), ((), ())), preferred_element_type=f32
     )
     both = jnp.concatenate(split_halves(lowered), axis=1)
-    replica = lax.axis_index("rollout")
-    shard = lax.axis_index("tensor")
-    owners_copy.wait()
+    ups = [piece[piece.shape[0] - up_rows :, :].astype(f32) for piece in piece_refs]
     for i in range(shards):
         first = 0
-        if carries_sums(i):
-            for block in add_near(kept_ref[i // 2], near_refs[i // 2]):
-                out_refs[i][first : first + rows, :] = block.astype(bf16)
-                first += rows
+        if i == 1:
+            first = near_ref.shape[0]
+            out_refs[i][:first, :] = near_ref[...]
         out_refs[i][first : first + rows, :] = both
-        slot = lax.rem(owners_ref[shard ^ i] + replicas - replica, replicas)
-        out_refs[i][first + rows :, :] = up_buf[slot]
-
-
-def route(owners, left, sums, pieces, rank, up_rows, shards):
+        picked = sum(up * pick_ref[i * replicas + k, :][None, :] for k, up in enumerate(ups))
+        out_refs[i][first + rows :, :] = picked.astype(bf16)
+
+
+def route(left, pick, near, pieces, rank, up_rows, shards):
     rows, depth = left.shape
     replicas = len(pieces)
-    kept, near = sums
-    sent = near[0].shape[0]
+    sent = near.shape[0]
     return pl.pallas_call(
         functools.partial(route_kernel, replicas, shards),
         out_shape=[
-            jax.ShapeDtypeStruct(((sent if carries_sums(i) else 0) + rows + up_rows, lanes), bf16)
+            jax.ShapeDtypeStruct(((sent if i == 1 else 0) + rows + up_rows, lanes), bf16)
             for i in range(shards)
         ],
-        in_specs=[stays_in_hbm] + [whole_in_vmem] * (2 + replicas + len(near)),
+        in_specs=[whole_in_vmem] * (3 + replicas),
         out_specs=[whole_in_vmem] * shards,
-        scratch_shapes=[
-            pltpu.SMEM(owners.shape, jnp.int32),
-            pltpu.VMEM((rank, depth), bf16),
-            pltpu.VMEM((replicas, up_rows, lanes), bf16),
-            pltpu.SemaphoreType.DMA,
-        ],
+        scratch_shapes=[pltpu.VMEM((rank, depth), bf16)],
         compiler_params=pltpu.CompilerParams(vmem_limit_bytes=4 * 2**20),
         name="route",
         cost_estimate=pl.CostEstimate(flops=0, bytes_accessed=800000, transcendentals=0),
-    )(*in_hbm(owners), left, kept, *pieces, *near)
-
-
-def route_plain(owners, tokens, sums, down, up, rank_part, own, shards):
-    kept, near = sums
+    )(left, pick, near, *[pieces[i] for i in piece_places(replicas)])
+
+
+def route_plain(owners, tokens, near, down, up, rank_part, own, shards):
     rank = down.shape[1]
     shard = lax.axis_index("tensor")
     first = shard * rank_part
@@ -390,22 +376,21 @@
     for i in range(shards):
         up_block = lax.dynamic_slice_in_dim(up_matrix, (shard ^ i) * own, own, axis=1)
         parts = [both, side_by_side(up_block)]
-        if carries_sums(i):
-            sums = add_near(kept[i // 2], near[i // 2])
-            parts = [jnp.concatenate(sums, axis=0).astype(bf16)] + parts
+        if i == 1:
+            parts = [near] + parts
         packets.append(jnp.concatenate(parts, axis=0))
     return packets
 
 
 def finish_kernel(step_count, row_count, head_count, shards, *refs):
-    kept_ref, near_ref, gain_ref, grouped_ref, total_ref, peak_ref, sum_ref = refs[:7]
-    cosine_ref, sine_ref = refs[7:9]
-    packet_refs = refs[9 : 9 + shards][::-1]
-    attention_ref, keys_ref, values_ref = refs[9 + shards : 12 + shards]
-    (up_buf,) = refs[12 + shards :]
+    gain_ref, base_ref, grouped_ref, total_ref, peak_ref, sum_ref, cosine_ref, sine_ref = refs[:8]
+    packet_refs = refs[8 : 8 + shards][::-1]
+    far_refs = refs[8 + shards : 6 + 2 * shards]
+    attention_ref, keys_ref, values_ref = refs[6 + 2 * shards : 9 + 2 * shards]
+    (up_buf,) = refs[9 + 2 * shards :]
     shard = lax.axis_index("tensor")
     rows = step_count * row_count
-    own = kept_ref.shape[2]
+    own = base_ref.shape[1]
     blocks = own // lanes
     rank = up_buf.shape[0]
     rank_part = rank // shards
@@ -414,7 +399,7 @@
 
     lowered = jnp.zeros((rows, lanes), f32)
     for i in range(shards):
-        first = rows * blocks if carries_sums(i) else 0
+        first = rows * blocks if i == 1 else 0
         lowered = lowered + packet_refs[i][first : first + rows, :].astype(f32)
         ups = packet_refs[i][first + rows :, :].astype(f32)
         at = pl.multiple_of((shard ^ i) * rank_part, rank_part)
@@ -429,9 +414,11 @@
     up = up_buf[...].astype(bf16)
     raised_up = jnp.dot(left, jnp.concatenate([up, up], axis=0), preferred_element_type=f32)
     joined = []
-    for c, block in enumerate(add_near(kept_ref[0], near_ref)):
-        for i in filter(carries_sums, range(shards)):
-            block = block + packet_refs[i][c * rows : (c + 1) * rows, :].astype(f32)
+    for c in range(blocks):
+        block = base_ref[:, c * lanes : (c + 1) * lanes]
+        for far_ref in far_refs:
+            block = block + far_ref[:, c * lanes : (c + 1) * lanes]
+        block = block + packet_refs[1][c * rows : (c + 1) * rows, :].astype(f32)
         joined.append(block + adapter_scale * raised_up[:, c * lanes : (c + 1) * lanes])
 
     all_rows = row_count * seen
@@ -478,9 +465,8 @@
             ] = jnp.concatenate(both, axis=0).astype(bf16)
 
 
-def finish(kept, near, partials, gain, packets, rank, step_count, row_count, query_width):
-    grouped, total, peak, denominator, cosine, sine = partials
-    _, rows, own = kept.shape
+def finish(mine, far, partials, gain, packets, rank, step_count, row_count, query_width):
+    rows, own = mine.shape
     shards = len(packets)
     head_count = own // (2 * lanes)
     return pl.pallas_call(
@@ -490,7 +476,7 @@
             jax.ShapeDtypeStruct((rows, head_count * lanes), bf16),
             jax.ShapeDtypeStruct((rows, head_count * lanes), bf16),
         ),
-        in_specs=[whole_in_vmem] * (9 + shards),
+        in_specs=[whole_in_vmem] * (6 + 2 * shards),
         out_specs=(whole_in_vmem,) * 3,
         scratch_shapes=[
             pltpu.VMEM((rank, own), f32),
@@ -498,7 +484,7 @@
         compiler_params=pltpu.CompilerParams(vmem_limit_bytes=6 * 2**20),
         name="finish",
         cost_estimate=pl.CostEstimate(flops=0, bytes_accessed=1000000, transcendentals=0),
-    )(kept, near, gain, grouped, total, peak, denominator, cosine, sine, *packets[::-1])
+    )(gain, mine, *partials, *packets[::-1], *far)
 
 
 def per_device(
@@ -534,8 +520,8 @@
         fetched = 2 * (key_value_weight.size + cache_keys.size + stored_values.size)
         beside = pl.CostEstimate(flops=1000 * fetched, bytes_accessed=fetched, transcendentals=0)
         packed = pack(adapter_down.T, adapter_up, rank_part, beside)
-        pieces = [packed] + [shift(packed, "rollout", i) for i in range(1, replicas)]
-    near, kept, left = project(
+        pieces = [packed] + [swap(packed, "rollout", i) for i in range(1, replicas)]
+    mine, near, far, left, pick = project(
         owners,
         tokens,
         key_value_weight,
@@ -543,20 +529,18 @@
         shards,
         replicas if fits else 1,
     )
-    near = [swap(block, "tensor", 1) for block in near]
+    far = [swap(block, "tensor", i + 2) for i, block in enumerate(far)]
     if fits:
-        packets = route(
-            owners, left, (kept, near), pieces, rank, rank_part * own // lanes, shards
-        )
+        packets = route(left, pick, near, pieces, rank, rank_part * own // lanes, shards)
     else:
         packets = route_plain(
-            owners, tokens, (kept, near), adapter_down, adapter_up, rank_part, own, shards
+            owners, tokens, near, adapter_down, adapter_up, rank_part, own, shards
         )
     partials = attend(lengths, query_rows, cache_keys, stored_values, packets[0], step_count)
     packets = [packets[0]] + [swap(packets[i], "tensor", i) for i in range(1, shards)]
     attention, keys, values = finish(
-        kept,
-        near[0],
+        mine,
+        far,
         partials,
         key_gain.reshape(1, -1),
         packets,

time: 19.1 us -> 19.4 us (1.016)
  waiting for transfers between devices: 1.78 us -> 2.93 us
  Pallas kernels: 6.55 us -> 6.05 us
  starting transfers between devices: 9.79 us -> 9.4 us
    ppermute x3 -> x0, starting transfers between devices: 7.01 us -> none  [shift(): lax.ppermute(block, axis, [((s + offset) % count, s) for s in range(count)])]
    ppermute x5 -> x8, starting transfers between devices: 2.77 us -> 9.4 us  [swap(): return lax.ppermute(block, axis, [(s, s ^ offset) for s in range(count)])]
    ppermute x5 -> x8, waiting for transfers between devices: 1.36 us -> 2.93 us  [swap(): return lax.ppermute(block, axis, [(s, s ^ offset) for s in range(count)])]
    pallas_call x1, Pallas kernels: 0.73 us -> 0.3 us  [route(): pl.pallas_call(functools.partial(route_kernel, replicas, shards), out_sha...]
    ppermute x3 -> x0, waiting for transfers between devices: 0.42 us -> none  [shift(): lax.ppermute(block, axis, [((s + offset) % count, s) for s in range(count)])]
  transfers between devices with their start and end apart: 8 -> 8, of which waited for: 5 -> 3; matrix products, arithmetic and copies ran while one was open for 0% -> 0% of each run, Pallas kernels for 18% -> 19%
where the time goes in v13:
time: 19.4 us; the launch traced here: 19.2 us
  starting transfers between devices  9.4 us (48%)
  Pallas kernels  6.05 us (31%)
  waiting for transfers between devices  2.93 us (15%)
  between operations  0.75 us (4%)
    ppermute x8, starting transfers between devices, swap(): return lax.ppermute(block, axis, [(s, s ^ offset) for s in range(count)])  9.4 us
    ppermute x8, waiting for transfers between devices, swap(): return lax.ppermute(block, axis, [(s, s ^ offset) for s in range(count)])  2.93 us
    pallas_call x1, Pallas kernels, attend(): pl.pallas_call(functools.partial(attend_kernel, step_count, width // lane...  2.13 us
    pallas_call x1, Pallas kernels, finish(): pl.pallas_call(functools.partial(finish_kernel, step_count, row_count, he...  1.43 us
    pallas_call x1, Pallas kernels, project(): pl.pallas_call(functools.partial(project_kernel, shards, replicas), out_s...  1.14 us
    pallas_call x1, Pallas kernels, pack(): pl.pallas_call(pack_kernel, out_shape=jax.ShapeDtypeStruct((rows, lanes),...  1.05 us
  transfers between devices with their start and end apart: 8, of which 3 were waited for; matrix products, arithmetic and copies ran while one was open for 0% of the time, Pallas kernels for 19%

profile of v13, /device:TPU:0, one launch (start us, length us, event | category | flops | bytes accessed | tf_op | source)
XLA Modules:
  0.0 19.2 jit_solution(12998329558783602582)
XLA Ops:
  0.6 0.0 slice-start
  0.6 0.0 slice-start.1
  0.7 0.0 copy-start.3
  0.7 1.0 %pack.1.refs_3_ = bf16[224,128]{1,0:T(8,128)(2,1)S(1)} custom-call(bf16[64,320]{1,0:T(8,128)(2,1)} %bitcast.13, bf16[64,512]{1,0:T(8,128)(2,1)} %up_hbm.1), custom_call_target="tpu_custom_call" | custom-call | flops 9437184000 | bytes 9437184 | tf_op jit(solution)/shard_map/pack/pallas_call | solution.py:73
  1.7 4.1 %collective-permute-start.2 = (bf16[224,128]{1,0:T(8,128)(2,1)S(1)}, bf16[224,128]{1,0:T(8,128)(2,1)S(1)}, u32[]{:S(2)}, u32[]{:S(2)}) collective-permute-start(bf16[224,128]{1,0:T(8,128)(2,1)S(1)} %pack.1.refs_3_), channel_id=1, source_target_pairs={{0,8},{4,12},{8,0},{12,4},{1,9},{5,13},{9,1},{13,5},{2,10},{6,14},... | collective-permute-start | bytes 172040 | tf_op jit(solution)/shard_map/ppermute | solution.py:27
  5.8 1.3 %collective-permute-start.1 = (bf16[224,128]{1,0:T(8,128)(2,1)S(1)}, bf16[224,128]{1,0:T(8,128)(2,1)S(1)}, u32[]{:S(2)}, u32[]{:S(2)}) collective-permute-start(bf16[224,128]{1,0:T(8,128)(2,1)S(1)} %pack.1.refs_3_), channel_id=1, source_target_pairs={{0,12},{4,8},{8,4},{12,0},{1,13},{5,9},{9,5},{13,1},{2,14},{6,10},... | collective-permute-start | bytes 172040 | tf_op jit(solution)/shard_map/ppermute | solution.py:27
  7.2 0.2 %collective-permute-start = (bf16[224,128]{1,0:T(8,128)(2,1)S(1)}, bf16[224,128]{1,0:T(8,128)(2,1)S(1)}, u32[]{:S(2)}, u32[]{:S(2)}) collective-permute-start(bf16[224,128]{1,0:T(8,128)(2,1)S(1)} %pack.1.refs_3_), channel_id=1, source_target_pairs={{0,4},{4,0},{8,12},{12,8},{1,5},{5,1},{9,13},{13,9},{2,6},{6,2},{1... | collective-permute-start | bytes 172040 | tf_op jit(solution)/shard_map/ppermute | solution.py:27
  7.4 0.0 slice-done
  7.4 0.0 slice-done.1
  7.4 0.0 copy-done.3
  7.4 0.0 copy-start
  7.4 0.0 copy-start.1
  7.4 0.0 copy-start.2
  7.4 1.1 %project.1 = (f32[32,512]{1,0:T(8,128)S(1)}, bf16[128,128]{1,0:T(8,128)(2,1)S(1)}, f32[32,512]{1,0:T(8,128)S(1)}, f32[32,512]{1,0:T(8,128)S(1)}, bf16[32,1536]{1,0:T(8,128)(2,1)S(1)}, /*index=5*/f32[16,128]{1,0:T(8,128)S(1)}) custom-call(s32[4]{0:T(128)} %refs_0_.1, bf16[32,1280]{1,0:T(8,128)(2,1)S(1)} %bitcast.10, bf16[1280,2048]{1,0:T(8,128)(2,1)S(1)} %bitcast.8, ...), custom_call_target="tpu_custom_call" | custom-call | flops 167772160 | bytes 5242880 | tf_op jit(solution)/shard_map/project/pallas_call | solution.py:139
  8.6 1.6 %collective-permute-start.6 = (f32[32,512]{1,0:T(8,128)S(1)}, f32[32,512]{1,0:T(8,128)S(1)}, u32[]{:S(2)}, u32[]{:S(2)}) collective-permute-start(f32[32,512]{1,0:T(8,128)S(1)} %get-tuple-element.36), channel_id=1, source_target_pairs={{0,2},{1,3},{2,0},{3,1},{4,6},{5,7},{6,4},{7,5},{8,10},{9,11},{10,... | collective-permute-start | bytes 196616 | tf_op jit(solution)/shard_map/ppermute | solution.py:27
  10.2 0.0 collective-permute-start.7
  10.2 0.0 collective-permute-done.2.refs_6_
  10.2 1.7 %collective-permute-done.1.refs_5_ = bf16[224,128]{1,0:T(8,128)(2,1)S(1)} collective-permute-done((bf16[224,128]{1,0:T(8,128)(2,1)S(1)}, bf16[224,128]{1,0:T(8,128)(2,1)S(1)}, u32[]{:S(2)}, u32[]{:S(2)}) %collective-permute-start.1) | collective-permute-done | bytes 57376 | tf_op jit(solution)/shard_map/ppermute | solution.py:27
  11.9 0.1 collective-permute-done.refs_4_
  12.0 0.3 %route.1 = (bf16[96,128]{1,0:T(8,128)(2,1)S(1)}, bf16[224,128]{1,0:T(8,128)(2,1)S(1)}, bf16[96,128]{1,0:T(8,128)(2,1)S(1)}, bf16[96,128]{1,0:T(8,128)(2,1)S(1)}) custom-call(bf16[32,1536]{1,0:T(8,128)(2,1)S(1)} %get-tuple-element.23.refs_0_, f32[16,128]{1,0:T(8,128)S(1)} %get-tuple-element.24.refs_1_, bf16[128,128]{1,0:T(8,128)(2,1)S(1)} %get-tuple-element.25.refs_2_, ...), custom_call_target="tpu_custom_call" | custom-call | bytes 800000 | tf_op jit(solution)/shard_map/route/pallas_call | solution.py:348
  12.3 0.0 collective-permute-start.5
  12.3 1.6 %collective-permute-start.3 = (bf16[96,128]{1,0:T(8,128)(2,1)S(1)}, bf16[96,128]{1,0:T(8,128)(2,1)S(1)}, u32[]{:S(2)}, u32[]{:S(2)}) collective-permute-start(bf16[96,128]{1,0:T(8,128)(2,1)S(1)} %get-tuple-element.33), channel_id=1, source_target_pairs={{0,3},{1,2},{2,1},{3,0},{4,7},{5,6},{6,5},{7,4},{8,11},{9,10},{10,... | collective-permute-start | bytes 73736 | tf_op jit(solution)/shard_map/ppermute | solution.py:27
  13.9 0.5 %collective-permute-start.4 = (bf16[96,128]{1,0:T(8,128)(2,1)S(1)}, bf16[96,128]{1,0:T(8,128)(2,1)S(1)}, u32[]{:S(2)}, u32[]{:S(2)}) collective-permute-start(bf16[96,128]{1,0:T(8,128)(2,1)S(1)} %get-tuple-element.34), channel_id=1, source_target_pairs={{0,2},{1,3},{2,0},{3,1},{4,6},{5,7},{6,4},{7,5},{8,10},{9,11},{10,... | collective-permute-start | bytes 73736 | tf_op jit(solution)/shard_map/ppermute | solution.py:27
  14.4 0.0 copy-done
  14.4 0.0 copy-done.1
  14.4 0.0 copy-done.2
  14.4 0.0 copy-start.4
  14.4 2.1 %attend.1 = (bf16[512,128]{1,0:T(8,128)(2,1)S(1)}, f32[512,128]{1,0:T(8,128)S(1)}, f32[512,128]{1,0:T(8,128)S(1)}, f32[512,128]{1,0:T(8,128)S(1)}, f32[32,128]{1,0:T(8,128)S(1)}, /*index=5*/f32[32,128]{1,0:T(8,128)S(1)}) custom-call(s32[8]{0:T(128)} %lengths_hbm.1, bf16[32,2048]{1,0:T(8,128)(2,1)S(1)} %bitcast.9, bf16[8,512,256]{2,1,0:T(8,128)(2,1)S(1)} %copy-done, ...), custom_call_target="tpu_custom_call" | custom-call | flops 134217728 | bytes 4194304 | tf_op jit(solution)/shard_map/attend/pallas_call | solution.py:270
  16.6 0.0 collective-permute-done.6.refs_12_
  16.6 0.0 collective-permute-done.7.refs_13_
  16.6 0.0 collective-permute-done.3.refs_8_
  16.6 1.1 %collective-permute-done.4.refs_9_ = bf16[96,128]{1,0:T(8,128)(2,1)S(1)} collective-permute-done((bf16[96,128]{1,0:T(8,128)(2,1)S(1)}, bf16[96,128]{1,0:T(8,128)(2,1)S(1)}, u32[]{:S(2)}, u32[]{:S(2)}) %collective-permute-start.4) | collective-permute-done | bytes 24608 | tf_op jit(solution)/shard_map/ppermute | solution.py:27
  17.7 0.0 collective-permute-done.5.refs_10_
  17.7 0.0 copy-done.4
  17.7 1.4 %finish.1 = (bf16[32,2048]{1,0:T(8,128)(2,1)}, bf16[32,256]{1,0:T(8,128)(2,1)}, bf16[32,256]{1,0:T(8,128)(2,1)}) custom-call(f32[1,128]{1,0:T(1,128)S(1)} %bitcast.11, f32[32,512]{1,0:T(8,128)S(1)} %get-tuple-element.22.refs_1_, bf16[512,128]{1,0:T(8,128)(2,1)S(1)} %get-tuple-element.27.refs_2_, f32[512,128]{1,0:T(8,128)S(1)} %get-tuple-element.28.refs_3_, ...), custom_call_target="tpu_custom_call" | custom-call | bytes 1000000 | tf_op jit(solution)/shard_map/finish/pallas_call | solution.py:472
  (1 shorter events, 0.0 us)
Async XLA Ops:
  0.6 6.8 %slice-start = ((s8[5242880]{0:T(1024)(128)(4,1)}), s8[4194304]{0:T(1024)(128)(4,1)S(1)}, s32[]{:S(2)}) async-start(s8[5242880]{0:T(1024)(128)(4,1)} %bitcast.7), calls=%async_computation | async-start | bytes 8388608
  0.6 6.8 %slice-start.1 = ((s8[5242880]{0:T(1024)(128)(4,1)}), s8[1048576]{0:T(1024)(128)(4,1)S(1)}, s32[]{:S(2)}) async-start(s8[5242880]{0:T(1024)(128)(4,1)} %bitcast.7), calls=%async_computation.1 | async-start | bytes 2097152
  0.7 6.8 %copy-start.3 = (bf16[4,8,1280]{2,1,0:T(8,128)(2,1)S(1)}, bf16[4,8,1280]{2,1,0:T(8,128)(2,1)}, u32[]{:S(2)}) copy-start(bf16[4,8,1280]{2,1,0:T(8,128)(2,1)} %param.10) | copy-start | bytes 245764
  1.7 8.4 %collective-permute-start.2 = (bf16[224,128]{1,0:T(8,128)(2,1)S(1)}, bf16[224,128]{1,0:T(8,128)(2,1)S(1)}, u32[]{:S(2)}, u32[]{:S(2)}) collective-permute-start(bf16[224,128]{1,0:T(8,128)(2,1)S(1)} %pack.1.refs_3_), channel_id=1, source_target_pairs={{0,8},{4,12},{8,0},{12,4},{1,9},{5,13},{9,1},{13,5},{2,10},{6,14},... | collective-permute-start | bytes 172040 | tf_op jit(solution)/shard_map/ppermute | solution.py:27
  5.8 6.1 %collective-permute-start.1 = (bf16[224,128]{1,0:T(8,128)(2,1)S(1)}, bf16[224,128]{1,0:T(8,128)(2,1)S(1)}, u32[]{:S(2)}, u32[]{:S(2)}) collective-permute-start(bf16[224,128]{1,0:T(8,128)(2,1)S(1)} %pack.1.refs_3_), channel_id=1, source_target_pairs={{0,12},{4,8},{8,4},{12,0},{1,13},{5,9},{9,5},{13,1},{2,14},{6,10},... | collective-permute-start | bytes 172040 | tf_op jit(solution)/shard_map/ppermute | solution.py:27
  7.2 4.8 %collective-permute-start = (bf16[224,128]{1,0:T(8,128)(2,1)S(1)}, bf16[224,128]{1,0:T(8,128)(2,1)S(1)}, u32[]{:S(2)}, u32[]{:S(2)}) collective-permute-start(bf16[224,128]{1,0:T(8,128)(2,1)S(1)} %pack.1.refs_3_), channel_id=1, source_target_pairs={{0,4},{4,0},{8,12},{12,8},{1,5},{5,1},{9,13},{13,9},{2,6},{6,2},{1... | collective-permute-start | bytes 172040 | tf_op jit(solution)/shard_map/ppermute | solution.py:27
  7.4 7.0 %copy-start = (bf16[8,512,256]{2,1,0:T(8,128)(2,1)S(1)}, bf16[8,512,256]{2,1,0:T(8,128)(2,1)}, u32[]{:S(2)}) copy-start(bf16[8,512,256]{2,1,0:T(8,128)(2,1)} %keys_ref.1) | copy-start | bytes 6291460
  7.4 7.0 %copy-start.1 = (bf16[8,512,256]{2,1,0:T(8,128)(2,1)S(1)}, bf16[8,512,256]{2,1,0:T(8,128)(2,1)}, u32[]{:S(2)}) copy-start(bf16[8,512,256]{2,1,0:T(8,128)(2,1)} %values_ref.1) | copy-start | bytes 6291460
  7.4 7.0 %copy-start.2 = (bf16[4,8,2048]{2,1,0:T(8,128)(2,1)S(1)}, bf16[4,8,2048]{2,1,0:T(8,128)(2,1)}, u32[]{:S(2)}) copy-start(bf16[4,8,2048]{2,1,0:T(8,128)(2,1)} %param.15) | copy-start | bytes 393220
  8.6 8.0 %collective-permute-start.6 = (f32[32,512]{1,0:T(8,128)S(1)}, f32[32,512]{1,0:T(8,128)S(1)}, u32[]{:S(2)}, u32[]{:S(2)}) collective-permute-start(f32[32,512]{1,0:T(8,128)S(1)} %get-tuple-element.36), channel_id=1, source_target_pairs={{0,2},{1,3},{2,0},{3,1},{4,6},{5,7},{6,4},{7,5},{8,10},{9,11},{10,... | collective-permute-start | bytes 196616 | tf_op jit(solution)/shard_map/ppermute | solution.py:27
  10.2 6.4 %collective-permute-start.7 = (f32[32,512]{1,0:T(8,128)S(1)}, f32[32,512]{1,0:T(8,128)S(1)}, u32[]{:S(2)}, u32[]{:S(2)}) collective-permute-start(f32[32,512]{1,0:T(8,128)S(1)} %get-tuple-element.37), channel_id=1, source_target_pairs={{0,3},{1,2},{2,1},{3,0},{4,7},{5,6},{6,5},{7,4},{8,11},{9,10},{10,... | collective-permute-start | bytes 196616 | tf_op jit(solution)/shard_map/ppermute | solution.py:27
  12.3 5.5 %collective-permute-start.5 = (bf16[224,128]{1,0:T(8,128)(2,1)S(1)}, bf16[224,128]{1,0:T(8,128)(2,1)S(1)}, u32[]{:S(2)}, u32[]{:S(2)}) collective-permute-start(bf16[224,128]{1,0:T(8,128)(2,1)S(1)} %get-tuple-element.35), channel_id=1, source_target_pairs={{0,1},{1,0},{2,3},{3,2},{4,5},{5,4},{6,7},{7,6},{8,9},{9,8},{10,11... | collective-permute-start | bytes 172040 | tf_op jit(solution)/shard_map/ppermute | solution.py:27
  12.3 4.3 %collective-permute-start.3 = (bf16[96,128]{1,0:T(8,128)(2,1)S(1)}, bf16[96,128]{1,0:T(8,128)(2,1)S(1)}, u32[]{:S(2)}, u32[]{:S(2)}) collective-permute-start(bf16[96,128]{1,0:T(8,128)(2,1)S(1)} %get-tuple-element.33), channel_id=1, source_target_pairs={{0,3},{1,2},{2,1},{3,0},{4,7},{5,6},{6,5},{7,4},{8,11},{9,10},{10,... | collective-permute-start | bytes 73736 | tf_op jit(solution)/shard_map/ppermute | solution.py:27
  13.9 3.8 %collective-permute-start.4 = (bf16[96,128]{1,0:T(8,128)(2,1)S(1)}, bf16[96,128]{1,0:T(8,128)(2,1)S(1)}, u32[]{:S(2)}, u32[]{:S(2)}) collective-permute-start(bf16[96,128]{1,0:T(8,128)(2,1)S(1)} %get-tuple-element.34), channel_id=1, source_target_pairs={{0,2},{1,3},{2,0},{3,1},{4,6},{5,7},{6,4},{7,5},{8,10},{9,11},{10,... | collective-permute-start | bytes 73736 | tf_op jit(solution)/shard_map/ppermute | solution.py:27
  14.4 3.3 %copy-start.4 = (f32[128]{0:T(128)S(1)}, f32[128]{0:T(128)}, u32[]{:S(2)}) copy-start(f32[128]{0:T(128)} %param.14) | copy-start | bytes 1540

commit v14 on v13

--- a/solution.py
+++ b/solution.py
@@ -88,8 +88,8 @@
 
 def project_kernel(shards, replicas, *refs):
     owners_hbm, tokens_ref, weight_ref, _ = refs[:4]
-    own_ref, near_ref = refs[4:6]
-    far_refs = refs[6 : 4 + shards]
+    own_ref = refs[4]
+    block_refs = refs[5 : 4 + shards]
     left_ref, pick_ref, owners_ref, token_buf, owner_sem = refs[4 + shards :]
     owners_copy = pltpu.make_async_copy(owners_hbm, owners_ref, owner_sem)
     owners_copy.start()
@@ -103,13 +103,8 @@
         )
         if i == 0:
             own_ref[...] = block
-        elif i > 1:
-            far_refs[i - 2][...] = block
         else:
-            for c in range(own // lanes):
-                near_ref[c * rows : (c + 1) * rows, :] = block[
-                    :, c * lanes : (c + 1) * lanes
-                ].astype(bf16)
+            block_refs[i - 1][...] = block.astype(bf16)
 
     owners_copy.wait()
     replica = lax.axis_index("rollout")
@@ -136,13 +131,10 @@
     rows, depth = tokens.shape
     own = weight.shape[1] // shards
     piece_width = -(-depth // replicas // lanes) * lanes
-    mine, near, *rest = pl.pallas_call(
+    mine, *rest = pl.pallas_call(
         functools.partial(project_kernel, shards, replicas),
-        out_shape=[
-            jax.ShapeDtypeStruct((rows, own), f32),
-            jax.ShapeDtypeStruct((rows * own // lanes, lanes), bf16),
-        ]
-        + [jax.ShapeDtypeStruct((rows, own), f32)] * (shards - 2)
+        out_shape=[jax.ShapeDtypeStruct((rows, own), f32)]
+        + [jax.ShapeDtypeStruct((rows, own), bf16)] * (shards - 1)
         + [
             jax.ShapeDtypeStruct((rows, replicas * piece_width), bf16),
             jax.ShapeDtypeStruct((shards * replicas, lanes), f32),
@@ -160,7 +152,7 @@
             flops=2 * rows * weight.size, bytes_accessed=2 * weight.size, transcendentals=0
         ),
     )(*in_hbm(owners), tokens, weight, after)
-    return mine, near, rest[:-2], *rest[-2:]
+    return mine, rest[:-2], *rest[-2:]
 
 
 def attend_kernel(
@@ -302,10 +294,10 @@
 
 
 def route_kernel(replicas, shards, *refs):
-    left_ref, pick_ref, near_ref = refs[:3]
-    piece_refs = [refs[3 + place] for place in piece_places(replicas)]
-    out_refs = refs[3 + replicas : 3 + replicas + shards]
-    (right,) = refs[3 + replicas + shards :]
+    left_ref, pick_ref = refs[:2]
+    piece_refs = [refs[2 + place] for place in piece_places(replicas)]
+    out_refs = refs[2 + replicas : 2 + replicas + shards]
+    (right,) = refs[2 + replicas + shards :]
     up_rows = out_refs[0].shape[0] - left_ref.shape[0]
     rows = left_ref.shape[0]
     rank = right.shape[0]
@@ -332,35 +324,27 @@
     both = jnp.concatenate(split_halves(lowered), axis=1)
     ups = [piece[piece.shape[0] - up_rows :, :].astype(f32) for piece in piece_refs]
     for i in range(shards):
-        first = 0
-        if i == 1:
-            first = near_ref.shape[0]
-            out_refs[i][:first, :] = near_ref[...]
-        out_refs[i][first : first + rows, :] = both
+        out_refs[i][:rows, :] = both
         picked = sum(up * pick_ref[i * replicas + k, :][None, :] for k, up in enumerate(ups))
-        out_refs[i][first + rows :, :] = picked.astype(bf16)
-
-
-def route(left, pick, near, pieces, rank, up_rows, shards):
+        out_refs[i][rows:, :] = picked.astype(bf16)
+
+
+def route(left, pick, pieces, rank, up_rows, shards):
     rows, depth = left.shape
     replicas = len(pieces)
-    sent = near.shape[0]
     return pl.pallas_call(
         functools.partial(route_kernel, replicas, shards),
-        out_shape=[
-            jax.ShapeDtypeStruct(((sent if i == 1 else 0) + rows + up_rows, lanes), bf16)
-            for i in range(shards)
-        ],
-        in_specs=[whole_in_vmem] * (3 + replicas),
+        out_shape=[jax.ShapeDtypeStruct((rows + up_rows, lanes), bf16)] * shards,
+        in_specs=[whole_in_vmem] * (2 + replicas),
         out_specs=[whole_in_vmem] * shards,
         scratch_shapes=[pltpu.VMEM((rank, depth), bf16)],
         compiler_params=pltpu.CompilerParams(vmem_limit_bytes=4 * 2**20),
         name="route",
         cost_estimate=pl.CostEstimate(flops=0, bytes_accessed=800000, transcendentals=0),
-    )(left, pick, near, *[pieces[i] for i in piece_places(replicas)])
-
-
-def route_plain(owners, tokens, near, down, up, rank_part, own, shards):
+    )(left, pick, *[pieces[i] for i in piece_places(replicas)])
+
+
+def route_plain(owners, tokens, down, up, rank_part, own, shards):
     rank = down.shape[1]
     shard = lax.axis_index("tensor")
     first = shard * rank_part
@@ -376,8 +360,6 @@
     for i in range(shards):
         up_block = lax.dynamic_slice_in_dim(up_matrix, (shard ^ i) * own, own, axis=1)
         parts = [both, side_by_side(up_block)]
-        if i == 1:
-            parts = [near] + parts
         packets.append(jnp.concatenate(parts, axis=0))
     return packets
 
@@ -385,9 +367,9 @@
 def finish_kernel(step_count, row_count, head_count, shards, *refs):
     gain_ref, base_ref, grouped_ref, total_ref, peak_ref, sum_ref, cosine_ref, sine_ref = refs[:8]
     packet_refs = refs[8 : 8 + shards][::-1]
-    far_refs = refs[8 + shards : 6 + 2 * shards]
-    attention_ref, keys_ref, values_ref = refs[6 + 2 * shards : 9 + 2 * shards]
-    (up_buf,) = refs[9 + 2 * shards :]
+    sum_refs = refs[8 + shards : 7 + 2 * shards]
+    attention_ref, keys_ref, values_ref = refs[7 + 2 * shards : 10 + 2 * shards]
+    (up_buf,) = refs[10 + 2 * shards :]
     shard = lax.axis_index("tensor")
     rows = step_count * row_count
     own = base_ref.shape[1]
@@ -399,9 +381,8 @@
 
     lowered = jnp.zeros((rows, lanes), f32)
     for i in range(shards):
-        first = rows * blocks if i == 1 else 0
-        lowered = lowered + packet_refs[i][first : first + rows, :].astype(f32)
-        ups = packet_refs[i][first + rows :, :].astype(f32)
+        lowered = lowered + packet_refs[i][:rows, :].astype(f32)
+        ups = packet_refs[i][rows:, :].astype(f32)
         at = pl.multiple_of((shard ^ i) * rank_part, rank_part)
         for c in range(blocks):
             up_buf[pl.ds(at, rank_part), c * lanes : (c + 1) * lanes] = ups[
@@ -416,9 +397,8 @@
     joined = []
     for c in range(blocks):
         block = base_ref[:, c * lanes : (c + 1) * lanes]
-        for far_ref in far_refs:
-            block = block + far_ref[:, c * lanes : (c + 1) * lanes]
-        block = block + packet_refs[1][c * rows : (c + 1) * rows, :].astype(f32)
+        for partial_ref in sum_refs:
+            block = block + partial_ref[:, c * lanes : (c + 1) * lanes].astype(f32)
         joined.append(block + adapter_scale * raised_up[:, c * lanes : (c + 1) * lanes])
 
     all_rows = row_count * seen
@@ -465,7 +445,7 @@
             ] = jnp.concatenate(both, axis=0).astype(bf16)
 
 
-def finish(mine, far, partials, gain, packets, rank, step_count, row_count, query_width):
+def finish(mine, others, partials, gain, packets, rank, step_count, row_count, query_width):
     rows, own = mine.shape
     shards = len(packets)
     head_count = own // (2 * lanes)
@@ -476,7 +456,7 @@
             jax.ShapeDtypeStruct((rows, head_count * lanes), bf16),
             jax.ShapeDtypeStruct((rows, head_count * lanes), bf16),
         ),
-        in_specs=[whole_in_vmem] * (6 + 2 * shards),
+        in_specs=[whole_in_vmem] * (7 + 2 * shards),
         out_specs=(whole_in_vmem,) * 3,
         scratch_shapes=[
             pltpu.VMEM((rank, own), f32),
@@ -484,7 +464,7 @@
         compiler_params=pltpu.CompilerParams(vmem_limit_bytes=6 * 2**20),
         name="finish",
         cost_estimate=pl.CostEstimate(flops=0, bytes_accessed=1000000, transcendentals=0),
-    )(gain, mine, *partials, *packets[::-1], *far)
+    )(gain, mine, *partials, *packets[::-1], *others)
 
 
 def per_device(
@@ -521,7 +501,7 @@
         beside = pl.CostEstimate(flops=1000 * fetched, bytes_accessed=fetched, transcendentals=0)
         packed = pack(adapter_down.T, adapter_up, rank_part, beside)
         pieces = [packed] + [swap(packed, "rollout", i) for i in range(1, replicas)]
-    mine, near, far, left, pick = project(
+    mine, blocks, left, pick = project(
         owners,
         tokens,
         key_value_weight,
@@ -529,18 +509,18 @@
         shards,
         replicas if fits else 1,
     )
-    far = [swap(block, "tensor", i + 2) for i, block in enumerate(far)]
+    others = [swap(block, "tensor", i + 1) for i, block in enumerate(blocks)]
     if fits:
-        packets = route(left, pick, near, pieces, rank, rank_part * own // lanes, shards)
+        packets = route(left, pick, pieces, rank, rank_part * own // lanes, shards)
     else:
         packets = route_plain(
-            owners, tokens, near, adapter_down, adapter_up, rank_part, own, shards
+            owners, tokens, adapter_down, adapter_up, rank_part, own, shards
         )
     partials = attend(lengths, query_rows, cache_keys, stored_values, packets[0], step_count)
     packets = [packets[0]] + [swap(packets[i], "tensor", i) for i in range(1, shards)]
     attention, keys, values = finish(
         mine,
-        far,
+        others,
         partials,
         key_gain.reshape(1, -1),
         packets,

time: 19.4 us -> 18 us (0.928)
  waiting for transfers between devices: 2.93 us -> 1.44 us
    ppermute x8 -> x9, waiting for transfers between devices: 2.93 us -> 1.44 us  [swap(): return lax.ppermute(block, axis, [(s, s ^ offset) for s in range(count)])]
    ppermute x8 -> x9, starting transfers between devices: 9.4 us -> 9.49 us  [swap(): return lax.ppermute(block, axis, [(s, s ^ offset) for s in range(count)])]
  transfers between devices with their start and end apart: 8 -> 9, of which waited for: 3 -> 2; matrix products, arithmetic and copies ran while one was open for 0% -> 0% of each run, Pallas kernels for 19% -> 20%
where the time goes in v14:
time: 18 us; the launch traced here: 17.8 us
  starting transfers between devices  9.49 us (53%)
  Pallas kernels  6.06 us (34%)
  waiting for transfers between devices  1.44 us (8%)
  between operations  0.78 us (4%)
    ppermute x9, starting transfers between devices, swap(): return lax.ppermute(block, axis, [(s, s ^ offset) for s in range(count)])  9.49 us
    pallas_call x1, Pallas kernels, attend(): pl.pallas_call(functools.partial(attend_kernel, step_count, width // lane...  2.13 us
    ppermute x9, waiting for transfers between devices, swap(): return lax.ppermute(block, axis, [(s, s ^ offset) for s in range(count)])  1.44 us
    pallas_call x1, Pallas kernels, finish(): pl.pallas_call(functools.partial(finish_kernel, step_count, row_count, he...  1.44 us
    pallas_call x1, Pallas kernels, project(): pl.pallas_call(functools.partial(project_kernel, shards, replicas), out_s...  1.14 us
    pallas_call x1, Pallas kernels, pack(): pl.pallas_call(pack_kernel, out_shape=jax.ShapeDtypeStruct((rows, lanes),...  1.05 us
  transfers between devices with their start and end apart: 9, of which 2 were waited for; matrix products, arithmetic and copies ran while one was open for 0% of the time, Pallas kernels for 20%

profile of v14, /device:TPU:0, one launch (start us, length us, event | category | flops | bytes accessed | tf_op | source)
XLA Modules:
  0.0 17.8 jit_solution(2105020482477553632)
XLA Ops:
  0.6 0.0 slice-start
  0.6 0.0 slice-start.1
  0.7 0.0 copy-start.3
  0.7 1.0 %pack.1.refs_3_.refs_2_ = bf16[224,128]{1,0:T(8,128)(2,1)S(1)} custom-call(bf16[64,320]{1,0:T(8,128)(2,1)} %bitcast.13, bf16[64,512]{1,0:T(8,128)(2,1)} %up_hbm.1), custom_call_target="tpu_custom_call" | custom-call | flops 9437184000 | bytes 9437184 | tf_op jit(solution)/shard_map/pack/pallas_call | solution.py:73
  1.7 4.1 %collective-permute-start.2 = (bf16[224,128]{1,0:T(8,128)(2,1)S(1)}, bf16[224,128]{1,0:T(8,128)(2,1)S(1)}, u32[]{:S(2)}, u32[]{:S(2)}) collective-permute-start(bf16[224,128]{1,0:T(8,128)(2,1)S(1)} %pack.1.refs_3_.refs_2_), channel_id=1, source_target_pairs={{0,8},{4,12},{8,0},{12,4},{1,9},{5,13},{9,1},{13,5},{2,10},{6,14},... | collective-permute-start | bytes 172040 | tf_op jit(solution)/shard_map/ppermute | solution.py:27
  5.8 1.3 %collective-permute-start.1 = (bf16[224,128]{1,0:T(8,128)(2,1)S(1)}, bf16[224,128]{1,0:T(8,128)(2,1)S(1)}, u32[]{:S(2)}, u32[]{:S(2)}) collective-permute-start(bf16[224,128]{1,0:T(8,128)(2,1)S(1)} %pack.1.refs_3_.refs_2_), channel_id=1, source_target_pairs={{0,12},{4,8},{8,4},{12,0},{1,13},{5,9},{9,5},{13,1},{2,14},{6,10},... | collective-permute-start | bytes 172040 | tf_op jit(solution)/shard_map/ppermute | solution.py:27
  7.2 0.2 %collective-permute-start = (bf16[224,128]{1,0:T(8,128)(2,1)S(1)}, bf16[224,128]{1,0:T(8,128)(2,1)S(1)}, u32[]{:S(2)}, u32[]{:S(2)}) collective-permute-start(bf16[224,128]{1,0:T(8,128)(2,1)S(1)} %pack.1.refs_3_.refs_2_), channel_id=1, source_target_pairs={{0,4},{4,0},{8,12},{12,8},{1,5},{5,1},{9,13},{13,9},{2,6},{6,2},{1... | collective-permute-start | bytes 172040 | tf_op jit(solution)/shard_map/ppermute | solution.py:27
  7.4 0.0 slice-done
  7.4 0.0 slice-done.1
  7.4 0.0 copy-done.3
  7.4 0.0 copy-start
  7.4 0.0 copy-start.1
  7.4 0.0 copy-start.2
  7.4 1.1 %project.1 = (f32[32,512]{1,0:T(8,128)S(1)}, bf16[32,512]{1,0:T(8,128)(2,1)S(1)}, bf16[32,512]{1,0:T(8,128)(2,1)S(1)}, bf16[32,512]{1,0:T(8,128)(2,1)S(1)}, bf16...) custom-call(s32[4]{0:T(128)} %refs_0_.1, bf16[32,1280]{1,0:T(8,128)(2,1)S(1)} %bitcast.10, ...), custom_call_target="tpu_custom_call" | custom-call | flops 167772160 | bytes 5242880 | tf_op jit(solution)/shard_map/project/pallas_call | solution.py:134
  8.6 0.1 collective-permute-start.6
  8.7 1.6 %collective-permute-start.7 = (bf16[32,512]{1,0:T(8,128)(2,1)S(1)}, bf16[32,512]{1,0:T(8,128)(2,1)S(1)}, u32[]{:S(2)}, u32[]{:S(2)}) collective-permute-start(bf16[32,512]{1,0:T(8,128)(2,1)S(1)} %get-tuple-element.36), channel_id=1, source_target_pairs={{0,2},{1,3},{2,0},{3,1},{4,6},{5,7},{6,4},{7,5},{8,10},{9,11},{10,... | collective-permute-start | bytes 98312 | tf_op jit(solution)/shard_map/ppermute | solution.py:27
  10.2 0.0 collective-permute-done.2.refs_5_
  10.2 0.3 %collective-permute-start.8 = (bf16[32,512]{1,0:T(8,128)(2,1)S(1)}, bf16[32,512]{1,0:T(8,128)(2,1)S(1)}, u32[]{:S(2)}, u32[]{:S(2)}) collective-permute-start(bf16[32,512]{1,0:T(8,128)(2,1)S(1)} %get-tuple-element.37), channel_id=1, source_target_pairs={{0,3},{1,2},{2,1},{3,0},{4,7},{5,6},{6,5},{7,4},{8,11},{9,10},{10,... | collective-permute-start | bytes 98312 | tf_op jit(solution)/shard_map/ppermute | solution.py:27
  10.5 1.4 %collective-permute-done.1.refs_4_ = bf16[224,128]{1,0:T(8,128)(2,1)S(1)} collective-permute-done((bf16[224,128]{1,0:T(8,128)(2,1)S(1)}, bf16[224,128]{1,0:T(8,128)(2,1)S(1)}, u32[]{:S(2)}, u32[]{:S(2)}) %collective-permute-start.1) | collective-permute-done | bytes 57376 | tf_op jit(solution)/shard_map/ppermute | solution.py:27
  11.9 0.1 collective-permute-done.refs_3_
  12.0 0.3 %route.1 = (bf16[96,128]{1,0:T(8,128)(2,1)S(1)}, bf16[96,128]{1,0:T(8,128)(2,1)S(1)}, bf16[96,128]{1,0:T(8,128)(2,1)S(1)}, bf16[96,128]{1,0:T(8,128)(2,1)S(1)}) custom-call(bf16[32,1536]{1,0:T(8,128)(2,1)S(1)} %get-tuple-element.23.refs_0_, f32[16,128]{1,0:T(8,128)S(1)} %get-tuple-element.24.refs_1_, bf16[224,128]{1,0:T(8,128)(2,1)S(1)} %pack.1.refs_3_.refs_2_, ...), custom_call_target="tpu_custom_call" | custom-call | bytes 800000 | tf_op jit(solution)/shard_map/route/pallas_call | solution.py:335
  12.3 0.0 collective-permute-start.3
  12.3 1.5 %collective-permute-start.4 = (bf16[96,128]{1,0:T(8,128)(2,1)S(1)}, bf16[96,128]{1,0:T(8,128)(2,1)S(1)}, u32[]{:S(2)}, u32[]{:S(2)}) collective-permute-start(bf16[96,128]{1,0:T(8,128)(2,1)S(1)} %get-tuple-element.33), channel_id=1, source_target_pairs={{0,2},{1,3},{2,0},{3,1},{4,6},{5,7},{6,4},{7,5},{8,10},{9,11},{10,... | collective-permute-start | bytes 73736 | tf_op jit(solution)/shard_map/ppermute | solution.py:27
  13.8 0.0 collective-permute-done.6.refs_12_
  13.8 0.3 %collective-permute-start.5 = (bf16[96,128]{1,0:T(8,128)(2,1)S(1)}, bf16[96,128]{1,0:T(8,128)(2,1)S(1)}, u32[]{:S(2)}, u32[]{:S(2)}) collective-permute-start(bf16[96,128]{1,0:T(8,128)(2,1)S(1)} %get-tuple-element.34), channel_id=1, source_target_pairs={{0,1},{1,0},{2,3},{3,2},{4,5},{5,4},{6,7},{7,6},{8,9},{9,8},{10,11... | collective-permute-start | bytes 73736 | tf_op jit(solution)/shard_map/ppermute | solution.py:27
  14.1 0.0 copy-done
  14.1 0.0 copy-done.1
  14.1 0.0 copy-done.2
  14.1 0.0 copy-start.4
  14.2 2.1 %attend.1 = (bf16[512,128]{1,0:T(8,128)(2,1)S(1)}, f32[512,128]{1,0:T(8,128)S(1)}, f32[512,128]{1,0:T(8,128)S(1)}, f32[512,128]{1,0:T(8,128)S(1)}, f32[32,128]{1,0:T(8,128)S(1)}, /*index=5*/f32[32,128]{1,0:T(8,128)S(1)}) custom-call(s32[8]{0:T(128)} %lengths_hbm.1, bf16[32,2048]{1,0:T(8,128)(2,1)S(1)} %bitcast.9, bf16[8,512,256]{2,1,0:T(8,128)(2,1)S(1)} %copy-done, ...), custom_call_target="tpu_custom_call" | custom-call | flops 134217728 | bytes 4194304 | tf_op jit(solution)/shard_map/attend/pallas_call | solution.py:262
  16.3 0.0 collective-permute-done.7.refs_13_
  16.3 0.0 collective-permute-done.8.refs_14_
  16.3 0.0 collective-permute-done.3.refs_8_
  16.3 0.0 collective-permute-done.4.refs_9_
  16.3 0.0 collective-permute-done.5.refs_10_
  16.3 0.0 copy-done.4
  16.4 1.4 %finish.1 = (bf16[32,2048]{1,0:T(8,128)(2,1)}, bf16[32,256]{1,0:T(8,128)(2,1)}, bf16[32,256]{1,0:T(8,128)(2,1)}) custom-call(f32[1,128]{1,0:T(1,128)S(1)} %bitcast.11, f32[32,512]{1,0:T(8,128)S(1)} %get-tuple-element.22.refs_1_, bf16[512,128]{1,0:T(8,128)(2,1)S(1)} %get-tuple-element.26.refs_2_, f32[512,128]{1,0:T(8,128)S(1)} %get-tuple-element.27.refs_3_, ...), custom_call_target="tpu_custom_call" | custom-call | bytes 1000000 | tf_op jit(solution)/shard_map/finish/pallas_call | solution.py:452
  (1 shorter events, 0.0 us)
Async XLA Ops:
  0.6 6.8 %slice-start = ((s8[5242880]{0:T(1024)(128)(4,1)}), s8[4194304]{0:T(1024)(128)(4,1)S(1)}, s32[]{:S(2)}) async-start(s8[5242880]{0:T(1024)(128)(4,1)} %bitcast.7), calls=%async_computation | async-start | bytes 8388608
  0.6 6.8 %slice-start.1 = ((s8[5242880]{0:T(1024)(128)(4,1)}), s8[1048576]{0:T(1024)(128)(4,1)S(1)}, s32[]{:S(2)}) async-start(s8[5242880]{0:T(1024)(128)(4,1)} %bitcast.7), calls=%async_computation.1 | async-start | bytes 2097152
  0.7 6.8 %copy-start.3 = (bf16[4,8,1280]{2,1,0:T(8,128)(2,1)S(1)}, bf16[4,8,1280]{2,1,0:T(8,128)(2,1)}, u32[]{:S(2)}) copy-start(bf16[4,8,1280]{2,1,0:T(8,128)(2,1)} %param.10) | copy-start | bytes 245764
  1.7 8.5 %collective-permute-start.2 = (bf16[224,128]{1,0:T(8,128)(2,1)S(1)}, bf16[224,128]{1,0:T(8,128)(2,1)S(1)}, u32[]{:S(2)}, u32[]{:S(2)}) collective-permute-start(bf16[224,128]{1,0:T(8,128)(2,1)S(1)} %pack.1.refs_3_.refs_2_), channel_id=1, source_target_pairs={{0,8},{4,12},{8,0},{12,4},{1,9},{5,13},{9,1},{13,5},{2,10},{6,14},... | collective-permute-start | bytes 172040 | tf_op jit(solution)/shard_map/ppermute | solution.py:27
  5.8 6.1 %collective-permute-start.1 = (bf16[224,128]{1,0:T(8,128)(2,1)S(1)}, bf16[224,128]{1,0:T(8,128)(2,1)S(1)}, u32[]{:S(2)}, u32[]{:S(2)}) collective-permute-start(bf16[224,128]{1,0:T(8,128)(2,1)S(1)} %pack.1.refs_3_.refs_2_), channel_id=1, source_target_pairs={{0,12},{4,8},{8,4},{12,0},{1,13},{5,9},{9,5},{13,1},{2,14},{6,10},... | collective-permute-start | bytes 172040 | tf_op jit(solution)/shard_map/ppermute | solution.py:27
  7.2 4.8 %collective-permute-start = (bf16[224,128]{1,0:T(8,128)(2,1)S(1)}, bf16[224,128]{1,0:T(8,128)(2,1)S(1)}, u32[]{:S(2)}, u32[]{:S(2)}) collective-permute-start(bf16[224,128]{1,0:T(8,128)(2,1)S(1)} %pack.1.refs_3_.refs_2_), channel_id=1, source_target_pairs={{0,4},{4,0},{8,12},{12,8},{1,5},{5,1},{9,13},{13,9},{2,6},{6,2},{1... | collective-permute-start | bytes 172040 | tf_op jit(solution)/shard_map/ppermute | solution.py:27
  7.4 6.7 %copy-start = (bf16[8,512,256]{2,1,0:T(8,128)(2,1)S(1)}, bf16[8,512,256]{2,1,0:T(8,128)(2,1)}, u32[]{:S(2)}) copy-start(bf16[8,512,256]{2,1,0:T(8,128)(2,1)} %keys_ref.1) | copy-start | bytes 6291460
  7.4 6.7 %copy-start.1 = (bf16[8,512,256]{2,1,0:T(8,128)(2,1)S(1)}, bf16[8,512,256]{2,1,0:T(8,128)(2,1)}, u32[]{:S(2)}) copy-start(bf16[8,512,256]{2,1,0:T(8,128)(2,1)} %values_ref.1) | copy-start | bytes 6291460
  7.4 6.7 %copy-start.2 = (bf16[4,8,2048]{2,1,0:T(8,128)(2,1)S(1)}, bf16[4,8,2048]{2,1,0:T(8,128)(2,1)}, u32[]{:S(2)}) copy-start(bf16[4,8,2048]{2,1,0:T(8,128)(2,1)} %param.15) | copy-start | bytes 393220
  8.6 5.3 %collective-permute-start.6 = (bf16[32,512]{1,0:T(8,128)(2,1)S(1)}, bf16[32,512]{1,0:T(8,128)(2,1)S(1)}, u32[]{:S(2)}, u32[]{:S(2)}) collective-permute-start(bf16[32,512]{1,0:T(8,128)(2,1)S(1)} %get-tuple-element.35), channel_id=1, source_target_pairs={{0,1},{1,0},{2,3},{3,2},{4,5},{5,4},{6,7},{7,6},{8,9},{9,8},{10,11... | collective-permute-start | bytes 98312 | tf_op jit(solution)/shard_map/ppermute | solution.py:27
  8.7 7.6 %collective-permute-start.7 = (bf16[32,512]{1,0:T(8,128)(2,1)S(1)}, bf16[32,512]{1,0:T(8,128)(2,1)S(1)}, u32[]{:S(2)}, u32[]{:S(2)}) collective-permute-start(bf16[32,512]{1,0:T(8,128)(2,1)S(1)} %get-tuple-element.36), channel_id=1, source_target_pairs={{0,2},{1,3},{2,0},{3,1},{4,6},{5,7},{6,4},{7,5},{8,10},{9,11},{10,... | collective-permute-start | bytes 98312 | tf_op jit(solution)/shard_map/ppermute | solution.py:27
  10.2 6.1 %collective-permute-start.8 = (bf16[32,512]{1,0:T(8,128)(2,1)S(1)}, bf16[32,512]{1,0:T(8,128)(2,1)S(1)}, u32[]{:S(2)}, u32[]{:S(2)}) collective-permute-start(bf16[32,512]{1,0:T(8,128)(2,1)S(1)} %get-tuple-element.37), channel_id=1, source_target_pairs={{0,3},{1,2},{2,1},{3,0},{4,7},{5,6},{6,5},{7,4},{8,11},{9,10},{10,... | collective-permute-start | bytes 98312 | tf_op jit(solution)/shard_map/ppermute | solution.py:27
  12.3 4.1 %collective-permute-start.3 = (bf16[96,128]{1,0:T(8,128)(2,1)S(1)}, bf16[96,128]{1,0:T(8,128)(2,1)S(1)}, u32[]{:S(2)}, u32[]{:S(2)}) collective-permute-start(bf16[96,128]{1,0:T(8,128)(2,1)S(1)} %get-tuple-element.32), channel_id=1, source_target_pairs={{0,3},{1,2},{2,1},{3,0},{4,7},{5,6},{6,5},{7,4},{8,11},{9,10},{10,... | collective-permute-start | bytes 73736 | tf_op jit(solution)/shard_map/ppermute | solution.py:27
  12.3 4.0 %collective-permute-start.4 = (bf16[96,128]{1,0:T(8,128)(2,1)S(1)}, bf16[96,128]{1,0:T(8,128)(2,1)S(1)}, u32[]{:S(2)}, u32[]{:S(2)}) collective-permute-start(bf16[96,128]{1,0:T(8,128)(2,1)S(1)} %get-tuple-element.33), channel_id=1, source_target_pairs={{0,2},{1,3},{2,0},{3,1},{4,6},{5,7},{6,4},{7,5},{8,10},{9,11},{10,... | collective-permute-start | bytes 73736 | tf_op jit(solution)/shard_map/ppermute | solution.py:27
  13.8 2.5 %collective-permute-start.5 = (bf16[96,128]{1,0:T(8,128)(2,1)S(1)}, bf16[96,128]{1,0:T(8,128)(2,1)S(1)}, u32[]{:S(2)}, u32[]{:S(2)}) collective-permute-start(bf16[96,128]{1,0:T(8,128)(2,1)S(1)} %get-tuple-element.34), channel_id=1, source_target_pairs={{0,1},{1,0},{2,3},{3,2},{4,5},{5,4},{6,7},{7,6},{8,9},{9,8},{10,11... | collective-permute-start | bytes 73736 | tf_op jit(solution)/shard_map/ppermute | solution.py:27
  14.1 2.2 %copy-start.4 = (f32[128]{0:T(128)S(1)}, f32[128]{0:T(128)}, u32[]{:S(2)}) copy-start(f32[128]{0:T(128)} %param.14) | copy-start | bytes 1540

commit v15 on v14

--- a/solution.py
+++ b/solution.py
@@ -25,6 +25,11 @@
 def swap(block, axis, offset):
     count = lax.axis_size(axis)
     return lax.ppermute(block, axis, [(s, s ^ offset) for s in range(count)])
+
+
+def shift(block, axis, offset):
+    count = lax.axis_size(axis)
+    return lax.ppermute(block, axis, [((s + offset) % count, s) for s in range(count)])
 
 
 def in_hbm(*arrays):
@@ -117,12 +122,13 @@
     for i in range(replicas):
         place = jnp.int32(0)
         for k in range(1, replicas):
-            place = place + jnp.where(owners_ref[k] == replica ^ i, k, 0)
+            place = place + jnp.where(owners_ref[k] == lax.rem(replica + i, replicas), k, 0)
         left_ref[:, i * width : (i + 1) * width] = token_buf[place]
     if replicas > 1:
         for i in range(shards):
             for k in range(replicas):
-                picked = jnp.where(owners_ref[shard ^ i] == replica ^ k, 1.0, 0.0)
+                source = lax.rem(replica + k, replicas)
+                picked = jnp.where(owners_ref[shard ^ i] == source, 1.0, 0.0)
                 row = i * replicas + k
                 pick_ref[row : row + 1, :] = jnp.full((1, lanes), picked, f32)
 
@@ -500,7 +506,7 @@
         fetched = 2 * (key_value_weight.size + cache_keys.size + stored_values.size)
         beside = pl.CostEstimate(flops=1000 * fetched, bytes_accessed=fetched, transcendentals=0)
         packed = pack(adapter_down.T, adapter_up, rank_part, beside)
-        pieces = [packed] + [swap(packed, "rollout", i) for i in range(1, replicas)]
+        pieces = [packed] + [shift(packed, "rollout", i) for i in range(1, replicas)]
     mine, blocks, left, pick = project(
         owners,
         tokens,

time: 18 us -> 20 us (1.11)
  starting transfers between devices: 9.49 us -> 11.8 us
  waiting for transfers between devices: 1.44 us -> 1.1 us
    ppermute x0 -> x3, starting transfers between devices: none -> 7.93 us  [shift(): lax.ppermute(block, axis, [((s + offset) % count, s) for s in range(count)])]
    ppermute x9 -> x6, starting transfers between devices: 9.49 us -> 3.92 us  [swap(): return lax.ppermute(block, axis, [(s, s ^ offset) for s in range(count)])]
    ppermute x9 -> x6, waiting for transfers between devices: 1.44 us -> 1.09 us  [swap(): return lax.ppermute(block, axis, [(s, s ^ offset) for s in range(count)])]
  transfers between devices with their start and end apart: 9 -> 9, of which waited for: 2 -> 1; matrix products, arithmetic and copies ran while one was open for 0% -> 0% of each run, Pallas kernels for 20% -> 18%
where the time goes in v15:
time: 20 us; the launch traced here: 19.8 us
  starting transfers between devices  11.8 us (59%)
  Pallas kernels  6.05 us (30%)
  waiting for transfers between devices  1.1 us (6%)
  between operations  0.77 us (4%)
    ppermute x3, starting transfers between devices, shift(): lax.ppermute(block, axis, [((s + offset) % count, s) for s in range(count)])  7.93 us
    ppermute x6, starting transfers between devices, swap(): return lax.ppermute(block, axis, [(s, s ^ offset) for s in range(count)])  3.92 us
    pallas_call x1, Pallas kernels, attend(): pl.pallas_call(functools.partial(attend_kernel, step_count, width // lane...  2.13 us
    pallas_call x1, Pallas kernels, finish(): pl.pallas_call(functools.partial(finish_kernel, step_count, row_count, he...  1.43 us
    pallas_call x1, Pallas kernels, project(): pl.pallas_call(functools.partial(project_kernel, shards, replicas), out_s...  1.14 us
    ppermute x6, waiting for transfers between devices, swap(): return lax.ppermute(block, axis, [(s, s ^ offset) for s in range(count)])  1.09 us
    pallas_call x1, Pallas kernels, pack(): pl.pallas_call(pack_kernel, out_shape=jax.ShapeDtypeStruct((rows, lanes),...  1.05 us
  transfers between devices with their start and end apart: 9, of which 1 were waited for; matrix products, arithmetic and copies ran while one was open for 0% of the time, Pallas kernels for 18%

profile of v15, /device:TPU:0, one launch (start us, length us, event | category | flops | bytes accessed | tf_op | source)
XLA Modules:
  0.0 19.8 jit_solution(6181527169470742555)
XLA Ops:
  0.6 0.0 slice-start
  0.6 0.0 slice-start.1
  0.7 0.0 copy-start.3
  0.7 1.0 %pack.1.refs_3_.refs_2_ = bf16[224,128]{1,0:T(8,128)(2,1)S(1)} custom-call(bf16[64,320]{1,0:T(8,128)(2,1)} %bitcast.13, bf16[64,512]{1,0:T(8,128)(2,1)} %up_hbm.1), custom_call_target="tpu_custom_call" | custom-call | flops 9437184000 | bytes 9437184 | tf_op jit(solution)/shard_map/pack/pallas_call | solution.py:78
  1.7 4.1 %collective-permute-start.2 = (bf16[224,128]{1,0:T(8,128)(2,1)S(1)}, bf16[224,128]{1,0:T(8,128)(2,1)S(1)}, u32[]{:S(2)}, u32[]{:S(2)}) collective-permute-start(bf16[224,128]{1,0:T(8,128)(2,1)S(1)} %pack.1.refs_3_.refs_2_), channel_id=1, source_target_pairs={{8,0},{12,4},{0,8},{4,12},{9,1},{13,5},{1,9},{5,13},{10,2},{14,6},... | collective-permute-start | bytes 172040 | tf_op jit(solution)/shard_map/ppermute | solution.py:32
  5.8 1.6 %collective-permute-start.1 = (bf16[224,128]{1,0:T(8,128)(2,1)S(1)}, bf16[224,128]{1,0:T(8,128)(2,1)S(1)}, u32[]{:S(2)}, u32[]{:S(2)}) collective-permute-start(bf16[224,128]{1,0:T(8,128)(2,1)S(1)} %pack.1.refs_3_.refs_2_), channel_id=1, source_target_pairs={{12,0},{0,4},{4,8},{8,12},{13,1},{1,5},{5,9},{9,13},{14,2},{2,6},{... | collective-permute-start | bytes 172040 | tf_op jit(solution)/shard_map/ppermute | solution.py:32
  7.4 2.2 %collective-permute-start = (bf16[224,128]{1,0:T(8,128)(2,1)S(1)}, bf16[224,128]{1,0:T(8,128)(2,1)S(1)}, u32[]{:S(2)}, u32[]{:S(2)}) collective-permute-start(bf16[224,128]{1,0:T(8,128)(2,1)S(1)} %pack.1.refs_3_.refs_2_), channel_id=1, source_target_pairs={{4,0},{8,4},{12,8},{0,12},{5,1},{9,5},{13,9},{1,13},{6,2},{10,6},{... | collective-permute-start | bytes 172040 | tf_op jit(solution)/shard_map/ppermute | solution.py:32
  9.6 0.0 slice-done
  9.6 0.0 slice-done.1
  9.7 0.0 copy-done.3
  9.7 0.0 copy-start
  9.7 0.0 copy-start.1
  9.7 0.0 copy-start.2
  9.7 1.1 %project.1 = (f32[32,512]{1,0:T(8,128)S(1)}, bf16[32,512]{1,0:T(8,128)(2,1)S(1)}, bf16[32,512]{1,0:T(8,128)(2,1)S(1)}, bf16[32,512]{1,0:T(8,128)(2,1)S(1)}, bf16...) custom-call(s32[4]{0:T(128)} %refs_0_.1, bf16[32,1280]{1,0:T(8,128)(2,1)S(1)} %bitcast.10, ...), custom_call_target="tpu_custom_call" | custom-call | flops 167772160 | bytes 5242880 | tf_op jit(solution)/shard_map/project/pallas_call | solution.py:140
  10.8 0.1 collective-permute-start.6
  10.9 1.6 %collective-permute-start.7 = (bf16[32,512]{1,0:T(8,128)(2,1)S(1)}, bf16[32,512]{1,0:T(8,128)(2,1)S(1)}, u32[]{:S(2)}, u32[]{:S(2)}) collective-permute-start(bf16[32,512]{1,0:T(8,128)(2,1)S(1)} %get-tuple-element.36), channel_id=1, source_target_pairs={{0,2},{1,3},{2,0},{3,1},{4,6},{5,7},{6,4},{7,5},{8,10},{9,11},{10,... | collective-permute-start | bytes 98312 | tf_op jit(solution)/shard_map/ppermute | solution.py:27
  12.5 0.0 collective-permute-done.2.refs_5_
  12.5 0.3 %collective-permute-start.8 = (bf16[32,512]{1,0:T(8,128)(2,1)S(1)}, bf16[32,512]{1,0:T(8,128)(2,1)S(1)}, u32[]{:S(2)}, u32[]{:S(2)}) collective-permute-start(bf16[32,512]{1,0:T(8,128)(2,1)S(1)} %get-tuple-element.37), channel_id=1, source_target_pairs={{0,3},{1,2},{2,1},{3,0},{4,7},{5,6},{6,5},{7,4},{8,11},{9,10},{10,... | collective-permute-start | bytes 98312 | tf_op jit(solution)/shard_map/ppermute | solution.py:27
  12.8 0.0 collective-permute-done.1.refs_4_
  12.8 0.0 collective-permute-done.refs_3_
  12.8 0.3 %route.1 = (bf16[96,128]{1,0:T(8,128)(2,1)S(1)}, bf16[96,128]{1,0:T(8,128)(2,1)S(1)}, bf16[96,128]{1,0:T(8,128)(2,1)S(1)}, bf16[96,128]{1,0:T(8,128)(2,1)S(1)}) custom-call(bf16[32,1536]{1,0:T(8,128)(2,1)S(1)} %get-tuple-element.23.refs_0_, f32[16,128]{1,0:T(8,128)S(1)} %get-tuple-element.24.refs_1_, bf16[224,128]{1,0:T(8,128)(2,1)S(1)} %pack.1.refs_3_.refs_2_, ...), custom_call_target="tpu_custom_call" | custom-call | bytes 800000 | tf_op jit(solution)/shard_map/route/pallas_call | solution.py:341
  13.1 1.5 %collective-permute-start.3 = (bf16[96,128]{1,0:T(8,128)(2,1)S(1)}, bf16[96,128]{1,0:T(8,128)(2,1)S(1)}, u32[]{:S(2)}, u32[]{:S(2)}) collective-permute-start(bf16[96,128]{1,0:T(8,128)(2,1)S(1)} %get-tuple-element.32), channel_id=1, source_target_pairs={{0,3},{1,2},{2,1},{3,0},{4,7},{5,6},{6,5},{7,4},{8,11},{9,10},{10,... | collective-permute-start | bytes 73736 | tf_op jit(solution)/shard_map/ppermute | solution.py:27
  14.5 0.5 %collective-permute-start.4 = (bf16[96,128]{1,0:T(8,128)(2,1)S(1)}, bf16[96,128]{1,0:T(8,128)(2,1)S(1)}, u32[]{:S(2)}, u32[]{:S(2)}) collective-permute-start(bf16[96,128]{1,0:T(8,128)(2,1)S(1)} %get-tuple-element.33), channel_id=1, source_target_pairs={{0,2},{1,3},{2,0},{3,1},{4,6},{5,7},{6,4},{7,5},{8,10},{9,11},{10,... | collective-permute-start | bytes 73736 | tf_op jit(solution)/shard_map/ppermute | solution.py:27
  15.1 0.0 collective-permute-done.6.refs_12_
  15.1 0.0 collective-permute-start.5
  15.1 0.0 copy-done
  15.1 0.0 copy-done.1
  15.1 0.0 copy-done.2
  15.1 0.0 copy-start.4
  15.1 2.1 %attend.1 = (bf16[512,128]{1,0:T(8,128)(2,1)S(1)}, f32[512,128]{1,0:T(8,128)S(1)}, f32[512,128]{1,0:T(8,128)S(1)}, f32[512,128]{1,0:T(8,128)S(1)}, f32[32,128]{1,0:T(8,128)S(1)}, /*index=5*/f32[32,128]{1,0:T(8,128)S(1)}) custom-call(s32[8]{0:T(128)} %lengths_hbm.1, bf16[32,2048]{1,0:T(8,128)(2,1)S(1)} %bitcast.9, bf16[8,512,256]{2,1,0:T(8,128)(2,1)S(1)} %copy-done, ...), custom_call_target="tpu_custom_call" | custom-call | flops 134217728 | bytes 4194304 | tf_op jit(solution)/shard_map/attend/pallas_call | solution.py:268
  17.3 0.0 collective-permute-done.7.refs_13_
  17.3 0.0 collective-permute-done.8.refs_14_
  17.3 0.0 collective-permute-done.3.refs_8_
  17.3 1.1 %collective-permute-done.4.refs_9_ = bf16[96,128]{1,0:T(8,128)(2,1)S(1)} collective-permute-done((bf16[96,128]{1,0:T(8,128)(2,1)S(1)}, bf16[96,128]{1,0:T(8,128)(2,1)S(1)}, u32[]{:S(2)}, u32[]{:S(2)}) %collective-permute-start.4) | collective-permute-done | bytes 24608 | tf_op jit(solution)/shard_map/ppermute | solution.py:27
  18.4 0.0 collective-permute-done.5.refs_10_
  18.4 0.0 copy-done.4
  18.4 1.4 %finish.1 = (bf16[32,2048]{1,0:T(8,128)(2,1)}, bf16[32,256]{1,0:T(8,128)(2,1)}, bf16[32,256]{1,0:T(8,128)(2,1)}) custom-call(f32[1,128]{1,0:T(1,128)S(1)} %bitcast.11, f32[32,512]{1,0:T(8,128)S(1)} %get-tuple-element.22.refs_1_, bf16[512,128]{1,0:T(8,128)(2,1)S(1)} %get-tuple-element.26.refs_2_, f32[512,128]{1,0:T(8,128)S(1)} %get-tuple-element.27.refs_3_, ...), custom_call_target="tpu_custom_call" | custom-call | bytes 1000000 | tf_op jit(solution)/shard_map/finish/pallas_call | solution.py:458
  (1 shorter events, 0.0 us)
Async XLA Ops:
  0.6 9.0 %slice-start = ((s8[5242880]{0:T(1024)(128)(4,1)}), s8[4194304]{0:T(1024)(128)(4,1)S(1)}, s32[]{:S(2)}) async-start(s8[5242880]{0:T(1024)(128)(4,1)} %bitcast.7), calls=%async_computation | async-start | bytes 8388608
  0.6 9.0 %slice-start.1 = ((s8[5242880]{0:T(1024)(128)(4,1)}), s8[1048576]{0:T(1024)(128)(4,1)S(1)}, s32[]{:S(2)}) async-start(s8[5242880]{0:T(1024)(128)(4,1)} %bitcast.7), calls=%async_computation.1 | async-start | bytes 2097152
  0.7 9.0 %copy-start.3 = (bf16[4,8,1280]{2,1,0:T(8,128)(2,1)S(1)}, bf16[4,8,1280]{2,1,0:T(8,128)(2,1)}, u32[]{:S(2)}) copy-start(bf16[4,8,1280]{2,1,0:T(8,128)(2,1)} %param.10) | copy-start | bytes 245764
  1.7 10.8 %collective-permute-start.2 = (bf16[224,128]{1,0:T(8,128)(2,1)S(1)}, bf16[224,128]{1,0:T(8,128)(2,1)S(1)}, u32[]{:S(2)}, u32[]{:S(2)}) collective-permute-start(bf16[224,128]{1,0:T(8,128)(2,1)S(1)} %pack.1.refs_3_.refs_2_), channel_id=1, source_target_pairs={{8,0},{12,4},{0,8},{4,12},{9,1},{13,5},{1,9},{5,13},{10,2},{14,6},... | collective-permute-start | bytes 172040 | tf_op jit(solution)/shard_map/ppermute | solution.py:32
  5.8 7.0 %collective-permute-start.1 = (bf16[224,128]{1,0:T(8,128)(2,1)S(1)}, bf16[224,128]{1,0:T(8,128)(2,1)S(1)}, u32[]{:S(2)}, u32[]{:S(2)}) collective-permute-start(bf16[224,128]{1,0:T(8,128)(2,1)S(1)} %pack.1.refs_3_.refs_2_), channel_id=1, source_target_pairs={{12,0},{0,4},{4,8},{8,12},{13,1},{1,5},{5,9},{9,13},{14,2},{2,6},{... | collective-permute-start | bytes 172040 | tf_op jit(solution)/shard_map/ppermute | solution.py:32
  7.4 5.4 %collective-permute-start = (bf16[224,128]{1,0:T(8,128)(2,1)S(1)}, bf16[224,128]{1,0:T(8,128)(2,1)S(1)}, u32[]{:S(2)}, u32[]{:S(2)}) collective-permute-start(bf16[224,128]{1,0:T(8,128)(2,1)S(1)} %pack.1.refs_3_.refs_2_), channel_id=1, source_target_pairs={{4,0},{8,4},{12,8},{0,12},{5,1},{9,5},{13,9},{1,13},{6,2},{10,6},{... | collective-permute-start | bytes 172040 | tf_op jit(solution)/shard_map/ppermute | solution.py:32
  9.7 5.4 %copy-start = (bf16[8,512,256]{2,1,0:T(8,128)(2,1)S(1)}, bf16[8,512,256]{2,1,0:T(8,128)(2,1)}, u32[]{:S(2)}) copy-start(bf16[8,512,256]{2,1,0:T(8,128)(2,1)} %keys_ref.1) | copy-start | bytes 6291460
  9.7 5.4 %copy-start.1 = (bf16[8,512,256]{2,1,0:T(8,128)(2,1)S(1)}, bf16[8,512,256]{2,1,0:T(8,128)(2,1)}, u32[]{:S(2)}) copy-start(bf16[8,512,256]{2,1,0:T(8,128)(2,1)} %values_ref.1) | copy-start | bytes 6291460
  9.7 5.4 %copy-start.2 = (bf16[4,8,2048]{2,1,0:T(8,128)(2,1)S(1)}, bf16[4,8,2048]{2,1,0:T(8,128)(2,1)}, u32[]{:S(2)}) copy-start(bf16[4,8,2048]{2,1,0:T(8,128)(2,1)} %param.15) | copy-start | bytes 393220
  10.8 4.2 %collective-permute-start.6 = (bf16[32,512]{1,0:T(8,128)(2,1)S(1)}, bf16[32,512]{1,0:T(8,128)(2,1)S(1)}, u32[]{:S(2)}, u32[]{:S(2)}) collective-permute-start(bf16[32,512]{1,0:T(8,128)(2,1)S(1)} %get-tuple-element.35), channel_id=1, source_target_pairs={{0,1},{1,0},{2,3},{3,2},{4,5},{5,4},{6,7},{7,6},{8,9},{9,8},{10,11... | collective-permute-start | bytes 98312 | tf_op jit(solution)/shard_map/ppermute | solution.py:27
  10.9 6.3 %collective-permute-start.7 = (bf16[32,512]{1,0:T(8,128)(2,1)S(1)}, bf16[32,512]{1,0:T(8,128)(2,1)S(1)}, u32[]{:S(2)}, u32[]{:S(2)}) collective-permute-start(bf16[32,512]{1,0:T(8,128)(2,1)S(1)} %get-tuple-element.36), channel_id=1, source_target_pairs={{0,2},{1,3},{2,0},{3,1},{4,6},{5,7},{6,4},{7,5},{8,10},{9,11},{10,... | collective-permute-start | bytes 98312 | tf_op jit(solution)/shard_map/ppermute | solution.py:27
  12.5 4.8 %collective-permute-start.8 = (bf16[32,512]{1,0:T(8,128)(2,1)S(1)}, bf16[32,512]{1,0:T(8,128)(2,1)S(1)}, u32[]{:S(2)}, u32[]{:S(2)}) collective-permute-start(bf16[32,512]{1,0:T(8,128)(2,1)S(1)} %get-tuple-element.37), channel_id=1, source_target_pairs={{0,3},{1,2},{2,1},{3,0},{4,7},{5,6},{6,5},{7,4},{8,11},{9,10},{10,... | collective-permute-start | bytes 98312 | tf_op jit(solution)/shard_map/ppermute | solution.py:27
  13.1 4.2 %collective-permute-start.3 = (bf16[96,128]{1,0:T(8,128)(2,1)S(1)}, bf16[96,128]{1,0:T(8,128)(2,1)S(1)}, u32[]{:S(2)}, u32[]{:S(2)}) collective-permute-start(bf16[96,128]{1,0:T(8,128)(2,1)S(1)} %get-tuple-element.32), channel_id=1, source_target_pairs={{0,3},{1,2},{2,1},{3,0},{4,7},{5,6},{6,5},{7,4},{8,11},{9,10},{10,... | collective-permute-start | bytes 73736 | tf_op jit(solution)/shard_map/ppermute | solution.py:27
  14.5 3.8 %collective-permute-start.4 = (bf16[96,128]{1,0:T(8,128)(2,1)S(1)}, bf16[96,128]{1,0:T(8,128)(2,1)S(1)}, u32[]{:S(2)}, u32[]{:S(2)}) collective-permute-start(bf16[96,128]{1,0:T(8,128)(2,1)S(1)} %get-tuple-element.33), channel_id=1, source_target_pairs={{0,2},{1,3},{2,0},{3,1},{4,6},{5,7},{6,4},{7,5},{8,10},{9,11},{10,... | collective-permute-start | bytes 73736 | tf_op jit(solution)/shard_map/ppermute | solution.py:27
  15.1 3.3 %collective-permute-start.5 = (bf16[96,128]{1,0:T(8,128)(2,1)S(1)}, bf16[96,128]{1,0:T(8,128)(2,1)S(1)}, u32[]{:S(2)}, u32[]{:S(2)}) collective-permute-start(bf16[96,128]{1,0:T(8,128)(2,1)S(1)} %get-tuple-element.34), channel_id=1, source_target_pairs={{0,1},{1,0},{2,3},{3,2},{4,5},{5,4},{6,7},{7,6},{8,9},{9,8},{10,11... | collective-permute-start | bytes 73736 | tf_op jit(solution)/shard_map/ppermute | solution.py:27
  15.1 3.3 %copy-start.4 = (f32[128]{0:T(128)S(1)}, f32[128]{0:T(128)}, u32[]{:S(2)}) copy-start(f32[128]{0:T(128)} %param.14) | copy-start | bytes 1540

commit v16 on v14

--- a/solution.py
+++ b/solution.py
@@ -41,18 +41,28 @@
     return high, (total - high.astype(f32)).astype(bf16)
 
 
-def pack_kernel(down_hbm, up_hbm, out_ref, down_ref, up_ref, sems):
+def frequencies_kernel(out_ref):
+    lane = lax.broadcasted_iota(jnp.int32, out_ref.shape, 1)
+    spacing = (lane % (lanes // 2)).astype(f32) * (-2.0 / lanes * math.log(rope_base))
+    out_ref[...] = jnp.exp(spacing)
+
+
+def frequencies(beside):
+    return pl.pallas_call(
+        frequencies_kernel,
+        out_shape=jax.ShapeDtypeStruct((8, lanes), f32),
+        out_specs=whole_in_vmem,
+        compiler_params=pltpu.CompilerParams(vmem_limit_bytes=2**20),
+        name="frequencies",
+        cost_estimate=beside,
+    )()
+
+
+def pack_kernel(down_ref, up_all_ref, _, out_ref):
     rank, down_rows = down_ref.shape
-    rank_part = up_ref.shape[0]
+    rank_part = (out_ref.shape[0] * lanes - down_ref.size) // up_all_ref.shape[1]
     start = pl.multiple_of(lax.axis_index("tensor") * rank_part, rank_part)
-    copies = [
-        pltpu.make_async_copy(down_hbm, down_ref, sems.at[0]),
-        pltpu.make_async_copy(up_hbm.at[pl.ds(start, rank_part), :], up_ref, sems.at[1]),
-    ]
-    for copy in copies:
-        copy.start(priority=1)
-    for copy in copies:
-        copy.wait()
+    up_ref = up_all_ref.at[pl.ds(start, rank_part), :]
     first = 0
     for c in range(down_rows // lanes):
         out_ref[first : first + rank, :] = down_ref[:, c * lanes : (c + 1) * lanes]
@@ -68,31 +78,31 @@
         first += rank_part
 
 
-def pack(down, up, rank_part, beside):
+def pack(down, up, rank_part, after):
     rows = (down.size + rank_part * up.shape[1]) // lanes
     return pl.pallas_call(
         pack_kernel,
         out_shape=jax.ShapeDtypeStruct((rows, lanes), bf16),
-        in_specs=[stays_in_hbm] * 2,
+        in_specs=[whole_in_vmem] * 3,
         out_specs=whole_in_vmem,
-        scratch_shapes=[
-            pltpu.VMEM(down.shape, bf16),
-            pltpu.VMEM((rank_part, up.shape[1]), bf16),
-            pltpu.SemaphoreType.DMA((2,)),
-        ],
         compiler_params=pltpu.CompilerParams(vmem_limit_bytes=2 * 2**20),
         name="pack",
-        cost_estimate=beside,
-    )(*in_hbm(down, up))
-
-
-def project_kernel(shards, replicas, *refs):
-    owners_hbm, tokens_ref, weight_ref, _ = refs[:4]
-    own_ref = refs[4]
-    block_refs = refs[5 : 4 + shards]
-    left_ref, pick_ref, owners_ref, token_buf, owner_sem = refs[4 + shards :]
-    owners_copy = pltpu.make_async_copy(owners_hbm, owners_ref, owner_sem)
+        cost_estimate=pl.CostEstimate(flops=0, bytes_accessed=200000, transcendentals=0),
+    )(down, up, after)
+
+
+def project_kernel(step_count, row_count, head_count, shards, replicas, *refs):
+    owners_hbm, lengths_hbm, tokens_ref, weight_ref, queries_ref, turns_ref, _ = refs[:7]
+    own_ref = refs[7]
+    block_refs = refs[8 : 7 + shards]
+    left_ref, pick_ref, asked_ref, grouped_ref, cosine_ref, sine_ref, bias_ref = refs[
+        7 + shards : 14 + shards
+    ]
+    owners_ref, lengths_ref, token_buf, regroup, sems = refs[14 + shards :]
+    owners_copy = pltpu.make_async_copy(owners_hbm, owners_ref, sems.at[0])
+    lengths_copy = pltpu.make_async_copy(lengths_hbm, lengths_ref, sems.at[1])
     owners_copy.start()
+    lengths_copy.start()
 
     shard = lax.axis_index("tensor")
     rows, own = own_ref.shape
@@ -106,80 +116,6 @@
         else:
             block_refs[i - 1][...] = block.astype(bf16)
 
-    owners_copy.wait()
-    replica = lax.axis_index("rollout")
-    width = token_buf.shape[2]
-    down_rows = tokens_ref.shape[1] // replicas
-    for k in range(replicas):
-        token_buf[k, :, :down_rows] = tokens_ref[:, k * down_rows : (k + 1) * down_rows]
-        if down_rows < width:
-            token_buf[k, :, down_rows:] = jnp.zeros((rows, width - down_rows), bf16)
-    for i in range(replicas):
-        place = jnp.int32(0)
-        for k in range(1, replicas):
-            place = place + jnp.where(owners_ref[k] == replica ^ i, k, 0)
-        left_ref[:, i * width : (i + 1) * width] = token_buf[place]
-    if replicas > 1:
-        for i in range(shards):
-            for k in range(replicas):
-                picked = jnp.where(owners_ref[shard ^ i] == replica ^ k, 1.0, 0.0)
-                row = i * replicas + k
-                pick_ref[row : row + 1, :] = jnp.full((1, lanes), picked, f32)
-
-
-def project(owners, tokens, weight, after, shards, replicas):
-    rows, depth = tokens.shape
-    own = weight.shape[1] // shards
-    piece_width = -(-depth // replicas // lanes) * lanes
-    mine, *rest = pl.pallas_call(
-        functools.partial(project_kernel, shards, replicas),
-        out_shape=[jax.ShapeDtypeStruct((rows, own), f32)]
-        + [jax.ShapeDtypeStruct((rows, own), bf16)] * (shards - 1)
-        + [
-            jax.ShapeDtypeStruct((rows, replicas * piece_width), bf16),
-            jax.ShapeDtypeStruct((shards * replicas, lanes), f32),
-        ],
-        in_specs=[stays_in_hbm] + [whole_in_vmem] * 3,
-        out_specs=[whole_in_vmem] * (shards + 2),
-        scratch_shapes=[
-            pltpu.SMEM(owners.shape, jnp.int32),
-            pltpu.VMEM((replicas, rows, piece_width), bf16),
-            pltpu.SemaphoreType.DMA,
-        ],
-        compiler_params=pltpu.CompilerParams(vmem_limit_bytes=4 * 2**20),
-        name="project",
-        cost_estimate=pl.CostEstimate(
-            flops=2 * rows * weight.size, bytes_accessed=2 * weight.size, transcendentals=0
-        ),
-    )(*in_hbm(owners), tokens, weight, after)
-    return mine, rest[:-2], *rest[-2:]
-
-
-def attend_kernel(
-    step_count,
-    head_count,
-    lengths_hbm,
-    queries_ref,
-    keys_ref,
-    values_ref,
-    _,
-    grouped_ref,
-    total_ref,
-    peak_ref,
-    sum_ref,
-    cosine_ref,
-    sine_ref,
-    lengths_ref,
-    regroup,
-    scores_ref,
-    raised,
-    length_sem,
-):
-    lengths_copy = pltpu.make_async_copy(lengths_hbm, lengths_ref, length_sem)
-    lengths_copy.start()
-    rows = cosine_ref.shape[0]
-
-    row_count, slots, _ = keys_ref.shape
     group = queries_ref.shape[1] // (head_count * lanes)
     seen = step_count * group
     for pair in range(step_count // 2):
@@ -201,12 +137,107 @@
                         [before[half], both[half]], axis=0
                     ).astype(bf16)
             before = both
+    asked_ref[...] = regroup[...].astype(bf16)
+
+    owners_copy.wait()
+    replica = lax.axis_index("rollout")
+    width = token_buf.shape[2]
+    down_rows = tokens_ref.shape[1] // replicas
+    for k in range(replicas):
+        token_buf[k, :, :down_rows] = tokens_ref[:, k * down_rows : (k + 1) * down_rows]
+        if down_rows < width:
+            token_buf[k, :, down_rows:] = jnp.zeros((rows, width - down_rows), bf16)
+    for i in range(replicas):
+        place = jnp.int32(0)
+        for k in range(1, replicas):
+            place = place + jnp.where(owners_ref[k] == replica ^ i, k, 0)
+        left_ref[:, i * width : (i + 1) * width] = token_buf[place]
+    if replicas > 1:
+        for i in range(shards):
+            for k in range(replicas):
+                picked = jnp.where(owners_ref[shard ^ i] == replica ^ k, 1.0, 0.0)
+                row = i * replicas + k
+                pick_ref[row : row + 1, :] = jnp.full((1, lanes), picked, f32)
+
+    lengths_copy.wait()
+    row = lax.broadcasted_iota(jnp.int32, (rows, lanes), 0)
+    lane = lax.broadcasted_iota(jnp.int32, (rows, lanes), 1)
+    position = row // row_count
+    for b in range(row_count):
+        position = position + jnp.where(row % row_count == b, lengths_ref[b], 0)
+    angles = position.astype(f32) * turns_ref[:1, :]
+    cosine_ref[...] = jnp.cos(angles)
+    sine = jnp.sin(angles)
+    sine_ref[...] = jnp.where(lane < lanes // 2, -sine, sine)
+    slot = lax.broadcasted_iota(jnp.int32, bias_ref.shape, 1)
+    whose = lax.broadcasted_iota(jnp.int32, bias_ref.shape, 0)
+    length = jnp.zeros(bias_ref.shape, jnp.int32)
+    for b in range(row_count):
+        length = jnp.where(whose == b, lengths_ref[b], length)
+    bias_ref[...] = jnp.where(slot < length, 0.0, masked_score)
+
+
+def project(
+    owners, lengths, tokens, weight, queries, turns, after, step_count, head_count, slots, shards, replicas
+):
+    rows, depth = tokens.shape
+    row_count = rows // step_count
+    own = weight.shape[1] // shards
+    piece_width = -(-depth // replicas // lanes) * lanes
+    seen_rows = rows * queries.shape[1] // lanes
+    table = jax.ShapeDtypeStruct((rows, lanes), f32)
+    mine, *rest = pl.pallas_call(
+        functools.partial(project_kernel, step_count, row_count, head_count, shards, replicas),
+        out_shape=[jax.ShapeDtypeStruct((rows, own), f32)]
+        + [jax.ShapeDtypeStruct((rows, own), bf16)] * (shards - 1)
+        + [
+            jax.ShapeDtypeStruct((rows, replicas * piece_width), bf16),
+            jax.ShapeDtypeStruct((shards * replicas, lanes), f32),
+            jax.ShapeDtypeStruct((seen_rows, lanes), bf16),
+            jax.ShapeDtypeStruct((seen_rows, lanes), bf16),
+            table,
+            table,
+            jax.ShapeDtypeStruct((row_count, slots), f32),
+        ],
+        in_specs=[stays_in_hbm] * 2 + [whole_in_vmem] * 5,
+        out_specs=[whole_in_vmem] * (shards + 7),
+        scratch_shapes=[
+            pltpu.SMEM(owners.shape, jnp.int32),
+            pltpu.SMEM(lengths.shape, jnp.int32),
+            pltpu.VMEM((replicas, rows, piece_width), bf16),
+            pltpu.VMEM((seen_rows, lanes), f32),
+            pltpu.SemaphoreType.DMA((2,)),
+        ],
+        compiler_params=pltpu.CompilerParams(vmem_limit_bytes=6 * 2**20),
+        name="project",
+        cost_estimate=pl.CostEstimate(
+            flops=2 * rows * weight.size, bytes_accessed=2 * weight.size, transcendentals=0
+        ),
+    )(*in_hbm(owners, lengths), tokens, weight, queries, turns, after)
+    return mine, rest[: shards - 1], *rest[shards - 1 :]
+
+
+def attend_kernel(
+    head_count,
+    asked_ref,
+    keys_ref,
+    values_ref,
+    bias_ref,
+    _,
+    total_ref,
+    peak_ref,
+    sum_ref,
+    scores_ref,
+    raised,
+):
+    row_count, slots, _ = keys_ref.shape
+    seen = asked_ref.shape[0] // (head_count * row_count)
 
     for b in range(row_count):
         for h in range(head_count):
             at = (h * row_count + b) * seen
             scores_ref[at : at + seen, :] = lax.dot_general(
-                regroup[at : at + seen, :].astype(bf16),
+                asked_ref[at : at + seen, :],
                 keys_ref[b, :, h * lanes : (h + 1) * lanes],
                 (((1,), (1,)), ((), ())),
                 preferred_element_type=f32,
@@ -222,10 +253,8 @@
         for b in range(row_count)
         for h in range(head_count)
     ]
-    lengths_copy.wait()
-    slot = lax.broadcasted_iota(jnp.int32, (seen, slots), 1)
     for b, h, place, out in places:
-        score = jnp.where(slot < lengths_ref[b], scores_ref[place, :], masked_score)
+        score = scores_ref[place, :] + bias_ref[b : b + 1, :]
         peak = jnp.max(score, axis=1, keepdims=True)
         lifted = jnp.exp2((score - peak) * exponent_scale)
         raised[place, :] = lifted.astype(bf16)
@@ -240,43 +269,19 @@
             preferred_element_type=f32,
         )
 
-    row = lax.broadcasted_iota(jnp.int32, (rows, lanes), 0)
-    lane = lax.broadcasted_iota(jnp.int32, (rows, lanes), 1)
-    position = row // row_count
-    for b in range(row_count):
-        position = position + jnp.where(row % row_count == b, lengths_ref[b], 0)
-    middle = lanes // 2
-    spacing = (lane % middle).astype(f32) * (-2.0 / lanes * math.log(rope_base))
-    angles = position.astype(f32) * jnp.exp(spacing)
-    cosine_ref[...] = jnp.cos(angles)
-    sine = jnp.sin(angles)
-    sine_ref[...] = jnp.where(lane < middle, -sine, sine)
-
-
-def attend(lengths, queries, keys, values, after, step_count):
+
+def attend(asked, keys, values, bias, after):
     row_count, slots, width = keys.shape
-    rows = step_count * row_count
-    seen_rows = rows * queries.shape[1] // lanes
-    table = jax.ShapeDtypeStruct((rows, lanes), f32)
+    seen_rows = asked.shape[0]
     seen_table = jax.ShapeDtypeStruct((seen_rows, lanes), f32)
     return pl.pallas_call(
-        functools.partial(attend_kernel, step_count, width // lanes),
-        out_shape=(
-            jax.ShapeDtypeStruct((seen_rows, lanes), bf16),
-            seen_table,
-            seen_table,
-            seen_table,
-            table,
-            table,
-        ),
-        in_specs=[stays_in_hbm] + [whole_in_vmem] * 4,
-        out_specs=(whole_in_vmem,) * 6,
+        functools.partial(attend_kernel, width // lanes),
+        out_shape=(seen_table,) * 3,
+        in_specs=[whole_in_vmem] * 5,
+        out_specs=(whole_in_vmem,) * 3,
         scratch_shapes=[
-            pltpu.SMEM(lengths.shape, jnp.int32),
-            pltpu.VMEM((seen_rows, lanes), f32),
             pltpu.VMEM((seen_rows, slots), f32),
             pltpu.VMEM((seen_rows, slots), bf16),
-            pltpu.SemaphoreType.DMA,
         ],
         compiler_params=pltpu.CompilerParams(vmem_limit_bytes=8 * 2**20),
         name="attend",
@@ -285,7 +290,7 @@
             bytes_accessed=2 * (keys.size + values.size),
             transcendentals=seen_rows * slots,
         ),
-    )(*in_hbm(lengths), queries, keys, values, after)
+    )(asked, keys, values, bias, after)
 
 
 def piece_places(replicas):
@@ -496,16 +501,24 @@
         and rank == lanes // 2
         and rank_part % 16 == 0
     )
+    fetched = 2 * (key_value_weight.size + cache_keys.size + stored_values.size)
+    turns = frequencies(
+        pl.CostEstimate(flops=1000 * fetched, bytes_accessed=fetched, transcendentals=0)
+    )
     if fits:
-        fetched = 2 * (key_value_weight.size + cache_keys.size + stored_values.size)
-        beside = pl.CostEstimate(flops=1000 * fetched, bytes_accessed=fetched, transcendentals=0)
-        packed = pack(adapter_down.T, adapter_up, rank_part, beside)
+        packed = pack(adapter_down.T, adapter_up, rank_part, turns)
         pieces = [packed] + [swap(packed, "rollout", i) for i in range(1, replicas)]
-    mine, blocks, left, pick = project(
+    mine, blocks, left, pick, asked, grouped, cosine, sine, bias = project(
         owners,
+        lengths,
         tokens,
         key_value_weight,
+        query_rows,
+        turns,
         packed if fits else adapter_up,
+        step_count,
+        cache_keys.shape[2] // lanes,
+        cache_keys.shape[1],
         shards,
         replicas if fits else 1,
     )
@@ -516,12 +529,12 @@
         packets = route_plain(
             owners, tokens, adapter_down, adapter_up, rank_part, own, shards
         )
-    partials = attend(lengths, query_rows, cache_keys, stored_values, packets[0], step_count)
+    total, peak, denominator = attend(asked, cache_keys, stored_values, bias, packets[0])
     packets = [packets[0]] + [swap(packets[i], "tensor", i) for i in range(1, shards)]
     attention, keys, values = finish(
         mine,
         others,
-        partials,
+        (grouped, total, peak, denominator, cosine, sine),
         key_gain.reshape(1, -1),
         packets,
         rank,

time: 18 us -> 18.2 us (1.011)
  Pallas kernels: 6.06 us -> 4.71 us
  waiting for transfers between devices: 1.44 us -> 2.32 us
  local copies, waits for them, and re-layouts: 0.04 us -> 0.81 us
    pallas_call x1, Pallas kernels: 1.05 us -> 0.08 us  [pack(): pl.pallas_call(pack_kernel, out_shape=jax.ShapeDtypeStruct((rows, lanes),...]
    ppermute x9, waiting for transfers between devices: 1.44 us -> 2.32 us  [swap(): return lax.ppermute(block, axis, [(s, s ^ offset) for s in range(count)])]
    unnamed x14 -> x16, local copies, waits for them, and re-layouts: 0.04 us -> 0.81 us
    pallas_call x2 -> x3, Pallas kernels: 3.27 us -> 2.9 us  [the longest x1 1.66 us: project(): pl.pallas_call(functools.partial(project_kernel, step_count, row_count, h...]
  transfers between devices with their start and end apart: 9 -> 9, of which waited for: 2 -> 4; matrix products, arithmetic and copies ran while one was open for 0% -> 0% of each run, Pallas kernels for 20% -> 18%
where the time goes in v16:
time: 18.2 us; the launch traced here: 18 us
  starting transfers between devices  9.43 us (52%)
  Pallas kernels  4.71 us (26%)
  waiting for transfers between devices  2.32 us (13%)
  local copies, waits for them, and re-layouts  0.81 us (4%)
  between operations  0.74 us (4%)
    ppermute x9, starting transfers between devices, swap(): return lax.ppermute(block, axis, [(s, s ^ offset) for s in range(count)])  9.43 us
    ppermute x9, waiting for transfers between devices, swap(): return lax.ppermute(block, axis, [(s, s ^ offset) for s in range(count)])  2.32 us
    pallas_call x1, Pallas kernels, project(): pl.pallas_call(functools.partial(project_kernel, step_count, row_count, h...  1.66 us
    pallas_call x1, Pallas kernels, finish(): pl.pallas_call(functools.partial(finish_kernel, step_count, row_count, he...  1.43 us
    pallas_call x1, Pallas kernels, attend(): pl.pallas_call(functools.partial(attend_kernel, width // lanes), out_shap...  1.23 us
    unnamed x16, local copies, waits for them, and re-layouts  0.81 us
  transfers between devices with their start and end apart: 9, of which 4 were waited for; matrix products, arithmetic and copies ran while one was open for 0% of the time, Pallas kernels for 18%

profile of v16, /device:TPU:0, one launch (start us, length us, event | category | flops | bytes accessed | tf_op | source)
XLA Modules:
  0.0 18.0 jit_solution(7968094723949744711)
XLA Ops:
  0.6 0.0 copy-start.5
  0.6 0.0 copy-start.6
  0.7 0.0 copy-start.3
  0.7 0.0 copy-start.4
  0.7 0.0 copy-start
  0.7 0.8 %copy-done.5 = bf16[64,512]{1,0:T(8,128)(2,1)S(1)} copy-done((bf16[64,512]{1,0:T(8,128)(2,1)S(1)}, bf16[64,512]{1,0:T(8,128)(2,1)}, u32[]{:S(2)}) %copy-start.5) | copy-done | bytes 65560
  1.5 0.0 copy-done.6
  1.5 0.1 pack.1.refs_6_.refs_2_
  1.6 4.0 %collective-permute-start.2 = (bf16[224,128]{1,0:T(8,128)(2,1)S(1)}, bf16[224,128]{1,0:T(8,128)(2,1)S(1)}, u32[]{:S(2)}, u32[]{:S(2)}) collective-permute-start(bf16[224,128]{1,0:T(8,128)(2,1)S(1)} %pack.1.refs_6_.refs_2_), channel_id=1, source_target_pairs={{0,8},{4,12},{8,0},{12,4},{1,9},{5,13},{9,1},{13,5},{2,10},{6,14},... | collective-permute-start | bytes 172040 | tf_op jit(solution)/shard_map/ppermute | solution.py:27
  5.6 1.3 %collective-permute-start.1 = (bf16[224,128]{1,0:T(8,128)(2,1)S(1)}, bf16[224,128]{1,0:T(8,128)(2,1)S(1)}, u32[]{:S(2)}, u32[]{:S(2)}) collective-permute-start(bf16[224,128]{1,0:T(8,128)(2,1)S(1)} %pack.1.refs_6_.refs_2_), channel_id=1, source_target_pairs={{0,12},{4,8},{8,4},{12,0},{1,13},{5,9},{9,5},{13,1},{2,14},{6,10},... | collective-permute-start | bytes 172040 | tf_op jit(solution)/shard_map/ppermute | solution.py:27
  6.9 0.2 %collective-permute-start = (bf16[224,128]{1,0:T(8,128)(2,1)S(1)}, bf16[224,128]{1,0:T(8,128)(2,1)S(1)}, u32[]{:S(2)}, u32[]{:S(2)}) collective-permute-start(bf16[224,128]{1,0:T(8,128)(2,1)S(1)} %pack.1.refs_6_.refs_2_), channel_id=1, source_target_pairs={{0,4},{4,0},{8,12},{12,8},{1,5},{5,1},{9,13},{13,9},{2,6},{6,2},{1... | collective-permute-start | bytes 172040 | tf_op jit(solution)/shard_map/ppermute | solution.py:27
  7.2 0.0 copy-done.3
  7.2 0.0 copy-done.4
  7.2 0.0 copy-done
  7.2 0.0 copy-start.1
  7.2 0.0 copy-start.2
  7.2 1.7 %project.1 = (f32[32,512]{1,0:T(8,128)S(1)}, bf16[32,512]{1,0:T(8,128)(2,1)S(1)}, bf16[32,512]{1,0:T(8,128)(2,1)S(1)}, bf16[32,512]{1,0:T(8,128)(2,1)S(1)}, bf16...) custom-call(s32[4]{0:T(128)} %refs_0_.1, ...), custom_call_target="tpu_custom_call" | custom-call | flops 167772160 | bytes 5242880 | tf_op jit(solution)/shard_map/project/pallas_call | solution.py:189
  8.9 0.1 collective-permute-start.6
  9.0 1.6 %collective-permute-start.7 = (bf16[32,512]{1,0:T(8,128)(2,1)S(1)}, bf16[32,512]{1,0:T(8,128)(2,1)S(1)}, u32[]{:S(2)}, u32[]{:S(2)}) collective-permute-start(bf16[32,512]{1,0:T(8,128)(2,1)S(1)} %get-tuple-element.40), channel_id=1, source_target_pairs={{0,2},{1,3},{2,0},{3,1},{4,6},{5,7},{6,4},{7,5},{8,10},{9,11},{10,... | collective-permute-start | bytes 98312 | tf_op jit(solution)/shard_map/ppermute | solution.py:27
  10.5 0.0 collective-permute-done.2.refs_5_
  10.5 0.3 %collective-permute-start.8 = (bf16[32,512]{1,0:T(8,128)(2,1)S(1)}, bf16[32,512]{1,0:T(8,128)(2,1)S(1)}, u32[]{:S(2)}, u32[]{:S(2)}) collective-permute-start(bf16[32,512]{1,0:T(8,128)(2,1)S(1)} %get-tuple-element.41), channel_id=1, source_target_pairs={{0,3},{1,2},{2,1},{3,0},{4,7},{5,6},{6,5},{7,4},{8,11},{9,10},{10,... | collective-permute-start | bytes 98312 | tf_op jit(solution)/shard_map/ppermute | solution.py:27
  10.8 0.9 %collective-permute-done.1.refs_4_ = bf16[224,128]{1,0:T(8,128)(2,1)S(1)} collective-permute-done((bf16[224,128]{1,0:T(8,128)(2,1)S(1)}, bf16[224,128]{1,0:T(8,128)(2,1)S(1)}, u32[]{:S(2)}, u32[]{:S(2)}) %collective-permute-start.1) | collective-permute-done | bytes 57376 | tf_op jit(solution)/shard_map/ppermute | solution.py:27
  11.7 0.1 collective-permute-done.refs_3_
  11.7 0.3 %route.1 = (bf16[96,128]{1,0:T(8,128)(2,1)S(1)}, bf16[96,128]{1,0:T(8,128)(2,1)S(1)}, bf16[96,128]{1,0:T(8,128)(2,1)S(1)}, bf16[96,128]{1,0:T(8,128)(2,1)S(1)}) custom-call(bf16[32,1536]{1,0:T(8,128)(2,1)S(1)} %get-tuple-element.28.refs_0_, f32[16,128]{1,0:T(8,128)S(1)} %get-tuple-element.29.refs_1_, bf16[224,128]{1,0:T(8,128)(2,1)S(1)} %pack.1.refs_6_.refs_2_, ...), custom_call_target="tpu_custom_call" | custom-call | bytes 800000 | tf_op jit(solution)/shard_map/route/pallas_call | solution.py:340
  12.0 0.5 %collective-permute-start.3 = (bf16[96,128]{1,0:T(8,128)(2,1)S(1)}, bf16[96,128]{1,0:T(8,128)(2,1)S(1)}, u32[]{:S(2)}, u32[]{:S(2)}) collective-permute-start(bf16[96,128]{1,0:T(8,128)(2,1)S(1)} %get-tuple-element.36), channel_id=1, source_target_pairs={{0,3},{1,2},{2,1},{3,0},{4,7},{5,6},{6,5},{7,4},{8,11},{9,10},{10,... | collective-permute-start | bytes 73736 | tf_op jit(solution)/shard_map/ppermute | solution.py:27
  12.6 1.0 %collective-permute-start.4 = (bf16[96,128]{1,0:T(8,128)(2,1)S(1)}, bf16[96,128]{1,0:T(8,128)(2,1)S(1)}, u32[]{:S(2)}, u32[]{:S(2)}) collective-permute-start(bf16[96,128]{1,0:T(8,128)(2,1)S(1)} %get-tuple-element.37), channel_id=1, source_target_pairs={{0,2},{1,3},{2,0},{3,1},{4,6},{5,7},{6,4},{7,5},{8,10},{9,11},{10,... | collective-permute-start | bytes 73736 | tf_op jit(solution)/shard_map/ppermute | solution.py:27
  13.6 0.0 collective-permute-done.6.refs_12_
  13.6 0.3 %collective-permute-start.5 = (bf16[96,128]{1,0:T(8,128)(2,1)S(1)}, bf16[96,128]{1,0:T(8,128)(2,1)S(1)}, u32[]{:S(2)}, u32[]{:S(2)}) collective-permute-start(bf16[96,128]{1,0:T(8,128)(2,1)S(1)} %get-tuple-element.38), channel_id=1, source_target_pairs={{0,1},{1,0},{2,3},{3,2},{4,5},{5,4},{6,7},{7,6},{8,9},{9,8},{10,11... | collective-permute-start | bytes 73736 | tf_op jit(solution)/shard_map/ppermute | solution.py:27
  13.9 0.0 copy-done.1
  13.9 0.0 copy-done.2
  13.9 0.0 copy-start.7
  13.9 1.2 %attend.1 = (f32[512,128]{1,0:T(8,128)S(1)}, f32[512,128]{1,0:T(8,128)S(1)}, f32[512,128]{1,0:T(8,128)S(1)}) custom-call(bf16[512,128]{1,0:T(8,128)(2,1)S(1)} %get-tuple-element.26.asked_ref, bf16[8,512,256]{2,1,0:T(8,128)(2,1)S(1)} %copy-done.1, bf16[8,512,256]{2,1,0:T(8,128)(2,1)S(1)} %copy-done.2, f32[8,512]{1,0:T(8,128)S(1)} %get-tuple-element.27.bias_ref, ...), custom_call_target="tpu_custom_call" | custom-call | flops 134217728 | bytes 4194304 | tf_op jit(solution)/shard_map/attend/pallas_call | solution.py:277
  15.2 0.0 collective-permute-done.7.refs_13_
  15.2 0.0 collective-permute-done.8.refs_14_
  15.2 0.3 %collective-permute-done.3.refs_8_ = bf16[96,128]{1,0:T(8,128)(2,1)S(1)} collective-permute-done((bf16[96,128]{1,0:T(8,128)(2,1)S(1)}, bf16[96,128]{1,0:T(8,128)(2,1)S(1)}, u32[]{:S(2)}, u32[]{:S(2)}) %collective-permute-start.3) | collective-permute-done | bytes 24608 | tf_op jit(solution)/shard_map/ppermute | solution.py:27
  15.5 1.0 %collective-permute-done.4.refs_9_ = bf16[96,128]{1,0:T(8,128)(2,1)S(1)} collective-permute-done((bf16[96,128]{1,0:T(8,128)(2,1)S(1)}, bf16[96,128]{1,0:T(8,128)(2,1)S(1)}, u32[]{:S(2)}, u32[]{:S(2)}) %collective-permute-start.4) | collective-permute-done | bytes 24608 | tf_op jit(solution)/shard_map/ppermute | solution.py:27
  16.6 0.0 collective-permute-done.5.refs_10_
  16.6 0.0 copy-done.7
  16.6 1.4 %finish.1 = (bf16[32,2048]{1,0:T(8,128)(2,1)}, bf16[32,256]{1,0:T(8,128)(2,1)}, bf16[32,256]{1,0:T(8,128)(2,1)}) custom-call(f32[1,128]{1,0:T(1,128)S(1)} %bitcast.10, f32[32,512]{1,0:T(8,128)S(1)} %get-tuple-element.24.refs_1_, bf16[512,128]{1,0:T(8,128)(2,1)S(1)} %get-tuple-element.25.refs_2_, f32[512,128]{1,0:T(8,128)S(1)} %get-tuple-element.31.refs_3_, ...), custom_call_target="tpu_custom_call" | custom-call | bytes 1000000 | tf_op jit(solution)/shard_map/finish/pallas_call | solution.py:457
  (1 shorter events, 0.0 us)
Async XLA Ops:
  0.6 0.8 %copy-start.5 = (bf16[64,512]{1,0:T(8,128)(2,1)S(1)}, bf16[64,512]{1,0:T(8,128)(2,1)}, u32[]{:S(2)}) copy-start(bf16[64,512]{1,0:T(8,128)(2,1)} %up_all_ref.1) | copy-start | bytes 196612
  0.6 0.8 %copy-start.6 = (bf16[320,64]{0,1:T(8,128)(2,1)S(1)}, bf16[320,64]{0,1:T(8,128)(2,1)}, u32[]{:S(2)}) copy-start(bf16[320,64]{0,1:T(8,128)(2,1)} %param.12) | copy-start | bytes 122884
  0.7 6.5 %copy-start.3 = (bf16[4,8,2048]{2,1,0:T(8,128)(2,1)S(1)}, bf16[4,8,2048]{2,1,0:T(8,128)(2,1)}, u32[]{:S(2)}) copy-start(bf16[4,8,2048]{2,1,0:T(8,128)(2,1)} %param.15) | copy-start | bytes 393220
  0.7 6.5 %copy-start.4 = (bf16[4,8,1280]{2,1,0:T(8,128)(2,1)S(1)}, bf16[4,8,1280]{2,1,0:T(8,128)(2,1)}, u32[]{:S(2)}) copy-start(bf16[4,8,1280]{2,1,0:T(8,128)(2,1)} %param.10) | copy-start | bytes 245764
  0.7 6.5 %copy-start = (bf16[1280,2048]{1,0:T(8,128)(2,1)S(1)}, bf16[1280,2048]{1,0:T(8,128)(2,1)}, u32[]{:S(2)}) copy-start(bf16[1280,2048]{1,0:T(8,128)(2,1)} %refs_3_.1) | copy-start | bytes 15728644
  1.6 9.0 %collective-permute-start.2 = (bf16[224,128]{1,0:T(8,128)(2,1)S(1)}, bf16[224,128]{1,0:T(8,128)(2,1)S(1)}, u32[]{:S(2)}, u32[]{:S(2)}) collective-permute-start(bf16[224,128]{1,0:T(8,128)(2,1)S(1)} %pack.1.refs_6_.refs_2_), channel_id=1, source_target_pairs={{0,8},{4,12},{8,0},{12,4},{1,9},{5,13},{9,1},{13,5},{2,10},{6,14},... | collective-permute-start | bytes 172040 | tf_op jit(solution)/shard_map/ppermute | solution.py:27
  5.6 6.1 %collective-permute-start.1 = (bf16[224,128]{1,0:T(8,128)(2,1)S(1)}, bf16[224,128]{1,0:T(8,128)(2,1)S(1)}, u32[]{:S(2)}, u32[]{:S(2)}) collective-permute-start(bf16[224,128]{1,0:T(8,128)(2,1)S(1)} %pack.1.refs_6_.refs_2_), channel_id=1, source_target_pairs={{0,12},{4,8},{8,4},{12,0},{1,13},{5,9},{9,5},{13,1},{2,14},{6,10},... | collective-permute-start | bytes 172040 | tf_op jit(solution)/shard_map/ppermute | solution.py:27
  6.9 4.8 %collective-permute-start = (bf16[224,128]{1,0:T(8,128)(2,1)S(1)}, bf16[224,128]{1,0:T(8,128)(2,1)S(1)}, u32[]{:S(2)}, u32[]{:S(2)}) collective-permute-start(bf16[224,128]{1,0:T(8,128)(2,1)S(1)} %pack.1.refs_6_.refs_2_), channel_id=1, source_target_pairs={{0,4},{4,0},{8,12},{12,8},{1,5},{5,1},{9,13},{13,9},{2,6},{6,2},{1... | collective-permute-start | bytes 172040 | tf_op jit(solution)/shard_map/ppermute | solution.py:27
  7.2 6.7 %copy-start.1 = (bf16[8,512,256]{2,1,0:T(8,128)(2,1)S(1)}, bf16[8,512,256]{2,1,0:T(8,128)(2,1)}, u32[]{:S(2)}) copy-start(bf16[8,512,256]{2,1,0:T(8,128)(2,1)} %keys_ref.1) | copy-start | bytes 6291460
  7.2 6.7 %copy-start.2 = (bf16[8,512,256]{2,1,0:T(8,128)(2,1)S(1)}, bf16[8,512,256]{2,1,0:T(8,128)(2,1)}, u32[]{:S(2)}) copy-start(bf16[8,512,256]{2,1,0:T(8,128)(2,1)} %values_ref.1) | copy-start | bytes 6291460
  8.9 4.8 %collective-permute-start.6 = (bf16[32,512]{1,0:T(8,128)(2,1)S(1)}, bf16[32,512]{1,0:T(8,128)(2,1)S(1)}, u32[]{:S(2)}, u32[]{:S(2)}) collective-permute-start(bf16[32,512]{1,0:T(8,128)(2,1)S(1)} %get-tuple-element.39), channel_id=1, source_target_pairs={{0,1},{1,0},{2,3},{3,2},{4,5},{5,4},{6,7},{7,6},{8,9},{9,8},{10,11... | collective-permute-start | bytes 98312 | tf_op jit(solution)/shard_map/ppermute | solution.py:27
  9.0 6.2 %collective-permute-start.7 = (bf16[32,512]{1,0:T(8,128)(2,1)S(1)}, bf16[32,512]{1,0:T(8,128)(2,1)S(1)}, u32[]{:S(2)}, u32[]{:S(2)}) collective-permute-start(bf16[32,512]{1,0:T(8,128)(2,1)S(1)} %get-tuple-element.40), channel_id=1, source_target_pairs={{0,2},{1,3},{2,0},{3,1},{4,6},{5,7},{6,4},{7,5},{8,10},{9,11},{10,... | collective-permute-start | bytes 98312 | tf_op jit(solution)/shard_map/ppermute | solution.py:27
  10.5 4.7 %collective-permute-start.8 = (bf16[32,512]{1,0:T(8,128)(2,1)S(1)}, bf16[32,512]{1,0:T(8,128)(2,1)S(1)}, u32[]{:S(2)}, u32[]{:S(2)}) collective-permute-start(bf16[32,512]{1,0:T(8,128)(2,1)S(1)} %get-tuple-element.41), channel_id=1, source_target_pairs={{0,3},{1,2},{2,1},{3,0},{4,7},{5,6},{6,5},{7,4},{8,11},{9,10},{10,... | collective-permute-start | bytes 98312 | tf_op jit(solution)/shard_map/ppermute | solution.py:27
  12.0 3.5 %collective-permute-start.3 = (bf16[96,128]{1,0:T(8,128)(2,1)S(1)}, bf16[96,128]{1,0:T(8,128)(2,1)S(1)}, u32[]{:S(2)}, u32[]{:S(2)}) collective-permute-start(bf16[96,128]{1,0:T(8,128)(2,1)S(1)} %get-tuple-element.36), channel_id=1, source_target_pairs={{0,3},{1,2},{2,1},{3,0},{4,7},{5,6},{6,5},{7,4},{8,11},{9,10},{10,... | collective-permute-start | bytes 73736 | tf_op jit(solution)/shard_map/ppermute | solution.py:27
  12.6 4.0 %collective-permute-start.4 = (bf16[96,128]{1,0:T(8,128)(2,1)S(1)}, bf16[96,128]{1,0:T(8,128)(2,1)S(1)}, u32[]{:S(2)}, u32[]{:S(2)}) collective-permute-start(bf16[96,128]{1,0:T(8,128)(2,1)S(1)} %get-tuple-element.37), channel_id=1, source_target_pairs={{0,2},{1,3},{2,0},{3,1},{4,6},{5,7},{6,4},{7,5},{8,10},{9,11},{10,... | collective-permute-start | bytes 73736 | tf_op jit(solution)/shard_map/ppermute | solution.py:27
  13.6 2.9 %collective-permute-start.5 = (bf16[96,128]{1,0:T(8,128)(2,1)S(1)}, bf16[96,128]{1,0:T(8,128)(2,1)S(1)}, u32[]{:S(2)}, u32[]{:S(2)}) collective-permute-start(bf16[96,128]{1,0:T(8,128)(2,1)S(1)} %get-tuple-element.38), channel_id=1, source_target_pairs={{0,1},{1,0},{2,3},{3,2},{4,5},{5,4},{6,7},{7,6},{8,9},{9,8},{10,11... | collective-permute-start | bytes 73736 | tf_op jit(solution)/shard_map/ppermute | solution.py:27
  13.9 2.6 %copy-start.7 = (f32[128]{0:T(128)S(1)}, f32[128]{0:T(128)}, u32[]{:S(2)}) copy-start(f32[128]{0:T(128)} %param.14) | copy-start | bytes 1540

commit v17 on v16

--- a/solution.py
+++ b/solution.py
@@ -95,10 +95,10 @@
     owners_hbm, lengths_hbm, tokens_ref, weight_ref, queries_ref, turns_ref, _ = refs[:7]
     own_ref = refs[7]
     block_refs = refs[8 : 7 + shards]
-    left_ref, pick_ref, asked_ref, grouped_ref, cosine_ref, sine_ref, bias_ref = refs[
-        7 + shards : 14 + shards
+    left_ref, pick_ref, asked_ref, grouped_ref, cosine_ref, sine_ref, bias_ref, visible_ref = refs[
+        7 + shards : 15 + shards
     ]
-    owners_ref, lengths_ref, token_buf, regroup, sems = refs[14 + shards :]
+    owners_ref, lengths_ref, token_buf, regroup, sems = refs[15 + shards :]
     owners_copy = pltpu.make_async_copy(owners_hbm, owners_ref, sems.at[0])
     lengths_copy = pltpu.make_async_copy(lengths_hbm, lengths_ref, sems.at[1])
     owners_copy.start()
@@ -175,6 +175,13 @@
     for b in range(row_count):
         length = jnp.where(whose == b, lengths_ref[b], length)
     bias_ref[...] = jnp.where(slot < length, 0.0, masked_score)
+    all_rows = row_count * seen
+    seen_by = lax.broadcasted_iota(jnp.int32, (all_rows, rows), 0)
+    made_by = lax.broadcasted_iota(jnp.int32, (all_rows, rows), 1)
+    visible = (seen_by % row_count == made_by % row_count) & (
+        made_by // row_count <= seen_by // (row_count * group)
+    )
+    visible_ref[...] = jnp.where(visible, 0.0, masked_score)
 
 
 def project(
@@ -198,9 +205,10 @@
             table,
             table,
             jax.ShapeDtypeStruct((row_count, slots), f32),
+            jax.ShapeDtypeStruct((seen_rows // head_count, rows), f32),
         ],
         in_specs=[stays_in_hbm] * 2 + [whole_in_vmem] * 5,
-        out_specs=[whole_in_vmem] * (shards + 7),
+        out_specs=[whole_in_vmem] * (shards + 8),
         scratch_shapes=[
             pltpu.SMEM(owners.shape, jnp.int32),
             pltpu.SMEM(lengths.shape, jnp.int32),
@@ -224,12 +232,16 @@
     values_ref,
     bias_ref,
     _,
-    total_ref,
-    peak_ref,
-    sum_ref,
-    scores_ref,
-    raised,
+    mine_ref,
+    *refs,
 ):
+    other_refs = refs[:-6]
+    base_ref, total_ref, peak_ref, sum_ref, scores_ref, raised = refs[-6:]
+    base = mine_ref[...]
+    for other_ref in other_refs:
+        base = base + other_ref[...].astype(f32)
+    base_ref[...] = base
+
     row_count, slots, _ = keys_ref.shape
     seen = asked_ref.shape[0] // (head_count * row_count)
 
@@ -270,15 +282,15 @@
         )
 
 
-def attend(asked, keys, values, bias, after):
+def attend(asked, keys, values, bias, after, mine, others):
     row_count, slots, width = keys.shape
     seen_rows = asked.shape[0]
     seen_table = jax.ShapeDtypeStruct((seen_rows, lanes), f32)
     return pl.pallas_call(
         functools.partial(attend_kernel, width // lanes),
-        out_shape=(seen_table,) * 3,
-        in_specs=[whole_in_vmem] * 5,
-        out_specs=(whole_in_vmem,) * 3,
+        out_shape=(jax.ShapeDtypeStruct(mine.shape, f32),) + (seen_table,) * 3,
+        in_specs=[whole_in_vmem] * (6 + len(others)),
+        out_specs=(whole_in_vmem,) * 4,
         scratch_shapes=[
             pltpu.VMEM((seen_rows, slots), f32),
             pltpu.VMEM((seen_rows, slots), bf16),
@@ -290,7 +302,7 @@
             bytes_accessed=2 * (keys.size + values.size),
             transcendentals=seen_rows * slots,
         ),
-    )(asked, keys, values, bias, after)
+    )(asked, keys, values, bias, after, mine, *others)
 
 
 def piece_places(replicas):
@@ -372,9 +384,7 @@
 def finish_kernel(step_count, row_count, head_count, shards, *refs):
     gain_ref, base_ref, grouped_ref, total_ref, peak_ref, sum_ref, cosine_ref, sine_ref = refs[:8]
     packet_refs = refs[8 : 8 + shards][::-1]
-    sum_refs = refs[8 + shards : 7 + 2 * shards]
-    attention_ref, keys_ref, values_ref = refs[7 + 2 * shards : 10 + 2 * shards]
-    (up_buf,) = refs[10 + 2 * shards :]
+    visible_ref, attention_ref, keys_ref, values_ref, up_buf = refs[8 + shards :]
     shard = lax.axis_index("tensor")
     rows = step_count * row_count
     own = base_ref.shape[1]
@@ -387,7 +397,7 @@
     lowered = jnp.zeros((rows, lanes), f32)
     for i in range(shards):
         lowered = lowered + packet_refs[i][:rows, :].astype(f32)
-        ups = packet_refs[i][rows:, :].astype(f32)
+        ups = packet_refs[i][rows:, :].astype(up_buf.dtype)
         at = pl.multiple_of((shard ^ i) * rank_part, rank_part)
         for c in range(blocks):
             up_buf[pl.ds(at, rank_part), c * lanes : (c + 1) * lanes] = ups[
@@ -402,16 +412,9 @@
     joined = []
     for c in range(blocks):
         block = base_ref[:, c * lanes : (c + 1) * lanes]
-        for partial_ref in sum_refs:
-            block = block + partial_ref[:, c * lanes : (c + 1) * lanes].astype(f32)
         joined.append(block + adapter_scale * raised_up[:, c * lanes : (c + 1) * lanes])
 
     all_rows = row_count * seen
-    seen_by = lax.broadcasted_iota(jnp.int32, (all_rows, rows), 0)
-    made_by = lax.broadcasted_iota(jnp.int32, (all_rows, rows), 1)
-    visible = (seen_by % row_count == made_by % row_count) & (
-        made_by // row_count <= seen_by // (row_count * group)
-    )
     heads = [(h, slice(h * all_rows, (h + 1) * all_rows)) for h in range(head_count)]
     keys, values, scores, results = [], [], [], []
     for h, _ in heads:
@@ -427,7 +430,7 @@
         score = lax.dot_general(
             grouped_ref[mine, :], keys[h], (((1,), (1,)), ((), ())), preferred_element_type=f32
         )
-        scores.append(jnp.where(visible, score, masked_score))
+        scores.append(score + visible_ref[...])
     for h, mine in heads:
         old_peak = peak_ref[mine, :]
         peak = jnp.maximum(old_peak, jnp.max(scores[h], axis=1, keepdims=True))
@@ -450,8 +453,8 @@
             ] = jnp.concatenate(both, axis=0).astype(bf16)
 
 
-def finish(mine, others, partials, gain, packets, rank, step_count, row_count, query_width):
-    rows, own = mine.shape
+def finish(base, visible, partials, gain, packets, rank, step_count, row_count, query_width):
+    rows, own = base.shape
     shards = len(packets)
     head_count = own // (2 * lanes)
     return pl.pallas_call(
@@ -461,15 +464,15 @@
             jax.ShapeDtypeStruct((rows, head_count * lanes), bf16),
             jax.ShapeDtypeStruct((rows, head_count * lanes), bf16),
         ),
-        in_specs=[whole_in_vmem] * (7 + 2 * shards),
+        in_specs=[whole_in_vmem] * (9 + shards),
         out_specs=(whole_in_vmem,) * 3,
         scratch_shapes=[
-            pltpu.VMEM((rank, own), f32),
+            pltpu.VMEM((rank, own), bf16 if rank // shards % 16 == 0 else f32),
         ],
         compiler_params=pltpu.CompilerParams(vmem_limit_bytes=6 * 2**20),
         name="finish",
         cost_estimate=pl.CostEstimate(flops=0, bytes_accessed=1000000, transcendentals=0),
-    )(gain, mine, *partials, *packets[::-1], *others)
+    )(gain, base, *partials, *packets[::-1], visible)
 
 
 def per_device(
@@ -508,7 +511,7 @@
     if fits:
         packed = pack(adapter_down.T, adapter_up, rank_part, turns)
         pieces = [packed] + [swap(packed, "rollout", i) for i in range(1, replicas)]
-    mine, blocks, left, pick, asked, grouped, cosine, sine, bias = project(
+    mine, blocks, left, pick, asked, grouped, cosine, sine, bias, visible = project(
         owners,
         lengths,
         tokens,
@@ -529,11 +532,13 @@
         packets = route_plain(
             owners, tokens, adapter_down, adapter_up, rank_part, own, shards
         )
-    total, peak, denominator = attend(asked, cache_keys, stored_values, bias, packets[0])
+    base, total, peak, denominator = attend(
+        asked, cache_keys, stored_values, bias, packets[0], mine, others
+    )
     packets = [packets[0]] + [swap(packets[i], "tensor", i) for i in range(1, shards)]
     attention, keys, values = finish(
-        mine,
-        others,
+        base,
+        visible,
         (grouped, total, peak, denominator, cosine, sine),
         key_gain.reshape(1, -1),
         packets,

time: 18.2 us -> 18.4 us (1.011)
  no operation moved by 1% of the time
where the time goes in v17:
time: 18.4 us; the launch traced here: 18.2 us
  starting transfers between devices  9.43 us (51%)
  Pallas kernels  4.81 us (26%)
  waiting for transfers between devices  2.44 us (13%)
  local copies, waits for them, and re-layouts  0.81 us (4%)
  between operations  0.72 us (4%)
    ppermute x9, starting transfers between devices, swap(): return lax.ppermute(block, axis, [(s, s ^ offset) for s in range(count)])  9.43 us
    ppermute x9, waiting for transfers between devices, swap(): return lax.ppermute(block, axis, [(s, s ^ offset) for s in range(count)])  2.44 us
    pallas_call x1, Pallas kernels, project(): pl.pallas_call(functools.partial(project_kernel, step_count, row_count, h...  1.77 us
    pallas_call x1, Pallas kernels, finish(): pl.pallas_call(functools.partial(finish_kernel, step_count, row_count, he...  1.43 us
    pallas_call x1, Pallas kernels, attend(): pl.pallas_call(functools.partial(attend_kernel, width // lanes), out_shap...  1.22 us
    unnamed x16, local copies, waits for them, and re-layouts  0.81 us
  transfers between devices with their start and end apart: 9, of which 4 were waited for; matrix products, arithmetic and copies ran while one was open for 0% of the time, Pallas kernels for 18%

profile of v17, /device:TPU:0, one launch (start us, length us, event | category | flops | bytes accessed | tf_op | source)
XLA Modules:
  0.0 18.2 jit_solution(14678159436542064817)
XLA Ops:
  0.6 0.0 copy-start.5
  0.6 0.0 copy-start.6
  0.7 0.0 copy-start.3
  0.7 0.0 copy-start.4
  0.7 0.0 copy-start
  0.7 0.8 %copy-done.5 = bf16[64,512]{1,0:T(8,128)(2,1)S(1)} copy-done((bf16[64,512]{1,0:T(8,128)(2,1)S(1)}, bf16[64,512]{1,0:T(8,128)(2,1)}, u32[]{:S(2)}) %copy-start.5) | copy-done | bytes 65560
  1.5 0.0 copy-done.6
  1.5 0.1 pack.1.refs_6_.refs_2_
  1.6 4.0 %collective-permute-start.2 = (bf16[224,128]{1,0:T(8,128)(2,1)S(1)}, bf16[224,128]{1,0:T(8,128)(2,1)S(1)}, u32[]{:S(2)}, u32[]{:S(2)}) collective-permute-start(bf16[224,128]{1,0:T(8,128)(2,1)S(1)} %pack.1.refs_6_.refs_2_), channel_id=1, source_target_pairs={{0,8},{4,12},{8,0},{12,4},{1,9},{5,13},{9,1},{13,5},{2,10},{6,14},... | collective-permute-start | bytes 172040 | tf_op jit(solution)/shard_map/ppermute | solution.py:27
  5.6 1.3 %collective-permute-start.1 = (bf16[224,128]{1,0:T(8,128)(2,1)S(1)}, bf16[224,128]{1,0:T(8,128)(2,1)S(1)}, u32[]{:S(2)}, u32[]{:S(2)}) collective-permute-start(bf16[224,128]{1,0:T(8,128)(2,1)S(1)} %pack.1.refs_6_.refs_2_), channel_id=1, source_target_pairs={{0,12},{4,8},{8,4},{12,0},{1,13},{5,9},{9,5},{13,1},{2,14},{6,10},... | collective-permute-start | bytes 172040 | tf_op jit(solution)/shard_map/ppermute | solution.py:27
  6.9 0.2 %collective-permute-start = (bf16[224,128]{1,0:T(8,128)(2,1)S(1)}, bf16[224,128]{1,0:T(8,128)(2,1)S(1)}, u32[]{:S(2)}, u32[]{:S(2)}) collective-permute-start(bf16[224,128]{1,0:T(8,128)(2,1)S(1)} %pack.1.refs_6_.refs_2_), channel_id=1, source_target_pairs={{0,4},{4,0},{8,12},{12,8},{1,5},{5,1},{9,13},{13,9},{2,6},{6,2},{1... | collective-permute-start | bytes 172040 | tf_op jit(solution)/shard_map/ppermute | solution.py:27
  7.2 0.0 copy-done.3
  7.2 0.0 copy-done.4
  7.2 0.0 copy-done
  7.2 0.0 copy-start.1
  7.2 0.0 copy-start.2
  7.2 1.8 %project.1 = (f32[32,512]{1,0:T(8,128)S(1)}, bf16[32,512]{1,0:T(8,128)(2,1)S(1)}, bf16[32,512]{1,0:T(8,128)(2,1)S(1)}, bf16[32,512]{1,0:T(8,128)(2,1)S(1)}, bf16...) custom-call(s32[4]{0:T(128)} %refs_0_.1, ...), custom_call_target="tpu_custom_call" | custom-call | flops 167772160 | bytes 5242880 | tf_op jit(solution)/shard_map/project/pallas_call | solution.py:196
  9.0 0.1 collective-permute-start.3
  9.1 1.6 %collective-permute-start.4 = (bf16[32,512]{1,0:T(8,128)(2,1)S(1)}, bf16[32,512]{1,0:T(8,128)(2,1)S(1)}, u32[]{:S(2)}, u32[]{:S(2)}) collective-permute-start(bf16[32,512]{1,0:T(8,128)(2,1)S(1)} %get-tuple-element.33), channel_id=1, source_target_pairs={{0,2},{1,3},{2,0},{3,1},{4,6},{5,7},{6,4},{7,5},{8,10},{9,11},{10,... | collective-permute-start | bytes 98312 | tf_op jit(solution)/shard_map/ppermute | solution.py:27
  10.6 0.0 collective-permute-done.2.refs_5_
  10.6 0.3 %collective-permute-start.5 = (bf16[32,512]{1,0:T(8,128)(2,1)S(1)}, bf16[32,512]{1,0:T(8,128)(2,1)S(1)}, u32[]{:S(2)}, u32[]{:S(2)}) collective-permute-start(bf16[32,512]{1,0:T(8,128)(2,1)S(1)} %get-tuple-element.34), channel_id=1, source_target_pairs={{0,3},{1,2},{2,1},{3,0},{4,7},{5,6},{6,5},{7,4},{8,11},{9,10},{10,... | collective-permute-start | bytes 98312 | tf_op jit(solution)/shard_map/ppermute | solution.py:27
  10.9 0.8 %collective-permute-done.1.refs_4_ = bf16[224,128]{1,0:T(8,128)(2,1)S(1)} collective-permute-done((bf16[224,128]{1,0:T(8,128)(2,1)S(1)}, bf16[224,128]{1,0:T(8,128)(2,1)S(1)}, u32[]{:S(2)}, u32[]{:S(2)}) %collective-permute-start.1) | collective-permute-done | bytes 57376 | tf_op jit(solution)/shard_map/ppermute | solution.py:27
  11.7 0.1 collective-permute-done.refs_3_
  11.7 0.3 %route.1 = (bf16[96,128]{1,0:T(8,128)(2,1)S(1)}, bf16[96,128]{1,0:T(8,128)(2,1)S(1)}, bf16[96,128]{1,0:T(8,128)(2,1)S(1)}, bf16[96,128]{1,0:T(8,128)(2,1)S(1)}) custom-call(bf16[32,1536]{1,0:T(8,128)(2,1)S(1)} %get-tuple-element.28.refs_0_, f32[16,128]{1,0:T(8,128)S(1)} %get-tuple-element.29.refs_1_, bf16[224,128]{1,0:T(8,128)(2,1)S(1)} %pack.1.refs_6_.refs_2_, ...), custom_call_target="tpu_custom_call" | custom-call | bytes 800000 | tf_op jit(solution)/shard_map/route/pallas_call | solution.py:352
  12.0 0.6 %collective-permute-start.6 = (bf16[96,128]{1,0:T(8,128)(2,1)S(1)}, bf16[96,128]{1,0:T(8,128)(2,1)S(1)}, u32[]{:S(2)}, u32[]{:S(2)}) collective-permute-start(bf16[96,128]{1,0:T(8,128)(2,1)S(1)} %get-tuple-element.42), channel_id=1, source_target_pairs={{0,3},{1,2},{2,1},{3,0},{4,7},{5,6},{6,5},{7,4},{8,11},{9,10},{10,... | collective-permute-start | bytes 73736 | tf_op jit(solution)/shard_map/ppermute | solution.py:27
  12.7 0.9 %collective-permute-start.7 = (bf16[96,128]{1,0:T(8,128)(2,1)S(1)}, bf16[96,128]{1,0:T(8,128)(2,1)S(1)}, u32[]{:S(2)}, u32[]{:S(2)}) collective-permute-start(bf16[96,128]{1,0:T(8,128)(2,1)S(1)} %get-tuple-element.43), channel_id=1, source_target_pairs={{0,2},{1,3},{2,0},{3,1},{4,6},{5,7},{6,4},{7,5},{8,10},{9,11},{10,... | collective-permute-start | bytes 73736 | tf_op jit(solution)/shard_map/ppermute | solution.py:27
  13.6 0.0 collective-permute-done.3.refs_0_
  13.6 0.3 %collective-permute-start.8 = (bf16[96,128]{1,0:T(8,128)(2,1)S(1)}, bf16[96,128]{1,0:T(8,128)(2,1)S(1)}, u32[]{:S(2)}, u32[]{:S(2)}) collective-permute-start(bf16[96,128]{1,0:T(8,128)(2,1)S(1)} %get-tuple-element.44), channel_id=1, source_target_pairs={{0,1},{1,0},{2,3},{3,2},{4,5},{5,4},{6,7},{7,6},{8,9},{9,8},{10,11... | collective-permute-start | bytes 73736 | tf_op jit(solution)/shard_map/ppermute | solution.py:27
  13.9 0.0 collective-permute-done.4.refs_1_
  13.9 0.0 collective-permute-done.5.refs_2_
  14.0 0.0 copy-done.1
  14.0 0.0 copy-done.2
  14.0 0.0 copy-start.7
  14.0 1.2 %attend.1 = (f32[32,512]{1,0:T(8,128)S(1)}, f32[512,128]{1,0:T(8,128)S(1)}, f32[512,128]{1,0:T(8,128)S(1)}, f32[512,128]{1,0:T(8,128)S(1)}) custom-call(bf16[512,128]{1,0:T(8,128)(2,1)S(1)} %get-tuple-element.26.asked_ref, bf16[8,512,256]{2,1,0:T(8,128)(2,1)S(1)} %copy-done.1, bf16[8,512,256]{2,1,0:T(8,128)(2,1)S(1)} %copy-done.2, ...), custom_call_target="tpu_custom_call" | custom-call | flops 134217728 | bytes 4194304 | tf_op jit(solution)/shard_map/attend/pallas_call | solution.py:289
  15.2 0.3 %collective-permute-done.6.refs_8_ = bf16[96,128]{1,0:T(8,128)(2,1)S(1)} collective-permute-done((bf16[96,128]{1,0:T(8,128)(2,1)S(1)}, bf16[96,128]{1,0:T(8,128)(2,1)S(1)}, u32[]{:S(2)}, u32[]{:S(2)}) %collective-permute-start.6) | collective-permute-done | bytes 24608 | tf_op jit(solution)/shard_map/ppermute | solution.py:27
  15.5 1.3 %collective-permute-done.7.refs_9_ = bf16[96,128]{1,0:T(8,128)(2,1)S(1)} collective-permute-done((bf16[96,128]{1,0:T(8,128)(2,1)S(1)}, bf16[96,128]{1,0:T(8,128)(2,1)S(1)}, u32[]{:S(2)}, u32[]{:S(2)}) %collective-permute-start.7) | collective-permute-done | bytes 24608 | tf_op jit(solution)/shard_map/ppermute | solution.py:27
  16.8 0.0 collective-permute-done.8.refs_10_
  16.8 0.0 copy-done.7
  16.8 1.4 %finish.1 = (bf16[32,2048]{1,0:T(8,128)(2,1)}, bf16[32,256]{1,0:T(8,128)(2,1)}, bf16[32,256]{1,0:T(8,128)(2,1)}) custom-call(f32[1,128]{1,0:T(1,128)S(1)} %bitcast.10, f32[32,512]{1,0:T(8,128)S(1)} %get-tuple-element.35.refs_1_, bf16[512,128]{1,0:T(8,128)(2,1)S(1)} %get-tuple-element.36.refs_2_, f32[512,128]{1,0:T(8,128)S(1)} %get-tuple-element.37.refs_3_, ...), custom_call_target="tpu_custom_call" | custom-call | bytes 1000000 | tf_op jit(solution)/shard_map/finish/pallas_call | solution.py:460
  (1 shorter events, 0.0 us)
Async XLA Ops:
  0.6 0.8 %copy-start.5 = (bf16[64,512]{1,0:T(8,128)(2,1)S(1)}, bf16[64,512]{1,0:T(8,128)(2,1)}, u32[]{:S(2)}) copy-start(bf16[64,512]{1,0:T(8,128)(2,1)} %up_all_ref.1) | copy-start | bytes 196612
  0.6 0.8 %copy-start.6 = (bf16[320,64]{0,1:T(8,128)(2,1)S(1)}, bf16[320,64]{0,1:T(8,128)(2,1)}, u32[]{:S(2)}) copy-start(bf16[320,64]{0,1:T(8,128)(2,1)} %param.12) | copy-start | bytes 122884
  0.7 6.5 %copy-start.3 = (bf16[4,8,2048]{2,1,0:T(8,128)(2,1)S(1)}, bf16[4,8,2048]{2,1,0:T(8,128)(2,1)}, u32[]{:S(2)}) copy-start(bf16[4,8,2048]{2,1,0:T(8,128)(2,1)} %param.15) | copy-start | bytes 393220
  0.7 6.5 %copy-start.4 = (bf16[4,8,1280]{2,1,0:T(8,128)(2,1)S(1)}, bf16[4,8,1280]{2,1,0:T(8,128)(2,1)}, u32[]{:S(2)}) copy-start(bf16[4,8,1280]{2,1,0:T(8,128)(2,1)} %param.10) | copy-start | bytes 245764
  0.7 6.5 %copy-start = (bf16[1280,2048]{1,0:T(8,128)(2,1)S(1)}, bf16[1280,2048]{1,0:T(8,128)(2,1)}, u32[]{:S(2)}) copy-start(bf16[1280,2048]{1,0:T(8,128)(2,1)} %refs_3_.1) | copy-start | bytes 15728644
  1.6 9.1 %collective-permute-start.2 = (bf16[224,128]{1,0:T(8,128)(2,1)S(1)}, bf16[224,128]{1,0:T(8,128)(2,1)S(1)}, u32[]{:S(2)}, u32[]{:S(2)}) collective-permute-start(bf16[224,128]{1,0:T(8,128)(2,1)S(1)} %pack.1.refs_6_.refs_2_), channel_id=1, source_target_pairs={{0,8},{4,12},{8,0},{12,4},{1,9},{5,13},{9,1},{13,5},{2,10},{6,14},... | collective-permute-start | bytes 172040 | tf_op jit(solution)/shard_map/ppermute | solution.py:27
  5.6 6.1 %collective-permute-start.1 = (bf16[224,128]{1,0:T(8,128)(2,1)S(1)}, bf16[224,128]{1,0:T(8,128)(2,1)S(1)}, u32[]{:S(2)}, u32[]{:S(2)}) collective-permute-start(bf16[224,128]{1,0:T(8,128)(2,1)S(1)} %pack.1.refs_6_.refs_2_), channel_id=1, source_target_pairs={{0,12},{4,8},{8,4},{12,0},{1,13},{5,9},{9,5},{13,1},{2,14},{6,10},... | collective-permute-start | bytes 172040 | tf_op jit(solution)/shard_map/ppermute | solution.py:27
  6.9 4.8 %collective-permute-start = (bf16[224,128]{1,0:T(8,128)(2,1)S(1)}, bf16[224,128]{1,0:T(8,128)(2,1)S(1)}, u32[]{:S(2)}, u32[]{:S(2)}) collective-permute-start(bf16[224,128]{1,0:T(8,128)(2,1)S(1)} %pack.1.refs_6_.refs_2_), channel_id=1, source_target_pairs={{0,4},{4,0},{8,12},{12,8},{1,5},{5,1},{9,13},{13,9},{2,6},{6,2},{1... | collective-permute-start | bytes 172040 | tf_op jit(solution)/shard_map/ppermute | solution.py:27
  7.2 6.8 %copy-start.1 = (bf16[8,512,256]{2,1,0:T(8,128)(2,1)S(1)}, bf16[8,512,256]{2,1,0:T(8,128)(2,1)}, u32[]{:S(2)}) copy-start(bf16[8,512,256]{2,1,0:T(8,128)(2,1)} %keys_ref.1) | copy-start | bytes 6291460
  7.2 6.8 %copy-start.2 = (bf16[8,512,256]{2,1,0:T(8,128)(2,1)S(1)}, bf16[8,512,256]{2,1,0:T(8,128)(2,1)}, u32[]{:S(2)}) copy-start(bf16[8,512,256]{2,1,0:T(8,128)(2,1)} %values_ref.1) | copy-start | bytes 6291460
  9.0 4.6 %collective-permute-start.3 = (bf16[32,512]{1,0:T(8,128)(2,1)S(1)}, bf16[32,512]{1,0:T(8,128)(2,1)S(1)}, u32[]{:S(2)}, u32[]{:S(2)}) collective-permute-start(bf16[32,512]{1,0:T(8,128)(2,1)S(1)} %get-tuple-element.32), channel_id=1, source_target_pairs={{0,1},{1,0},{2,3},{3,2},{4,5},{5,4},{6,7},{7,6},{8,9},{9,8},{10,11... | collective-permute-start | bytes 98312 | tf_op jit(solution)/shard_map/ppermute | solution.py:27
  9.1 4.9 %collective-permute-start.4 = (bf16[32,512]{1,0:T(8,128)(2,1)S(1)}, bf16[32,512]{1,0:T(8,128)(2,1)S(1)}, u32[]{:S(2)}, u32[]{:S(2)}) collective-permute-start(bf16[32,512]{1,0:T(8,128)(2,1)S(1)} %get-tuple-element.33), channel_id=1, source_target_pairs={{0,2},{1,3},{2,0},{3,1},{4,6},{5,7},{6,4},{7,5},{8,10},{9,11},{10,... | collective-permute-start | bytes 98312 | tf_op jit(solution)/shard_map/ppermute | solution.py:27
  10.6 3.3 %collective-permute-start.5 = (bf16[32,512]{1,0:T(8,128)(2,1)S(1)}, bf16[32,512]{1,0:T(8,128)(2,1)S(1)}, u32[]{:S(2)}, u32[]{:S(2)}) collective-permute-start(bf16[32,512]{1,0:T(8,128)(2,1)S(1)} %get-tuple-element.34), channel_id=1, source_target_pairs={{0,3},{1,2},{2,1},{3,0},{4,7},{5,6},{6,5},{7,4},{8,11},{9,10},{10,... | collective-permute-start | bytes 98312 | tf_op jit(solution)/shard_map/ppermute | solution.py:27
  12.0 3.5 %collective-permute-start.6 = (bf16[96,128]{1,0:T(8,128)(2,1)S(1)}, bf16[96,128]{1,0:T(8,128)(2,1)S(1)}, u32[]{:S(2)}, u32[]{:S(2)}) collective-permute-start(bf16[96,128]{1,0:T(8,128)(2,1)S(1)} %get-tuple-element.42), channel_id=1, source_target_pairs={{0,3},{1,2},{2,1},{3,0},{4,7},{5,6},{6,5},{7,4},{8,11},{9,10},{10,... | collective-permute-start | bytes 73736 | tf_op jit(solution)/shard_map/ppermute | solution.py:27
  12.7 4.1 %collective-permute-start.7 = (bf16[96,128]{1,0:T(8,128)(2,1)S(1)}, bf16[96,128]{1,0:T(8,128)(2,1)S(1)}, u32[]{:S(2)}, u32[]{:S(2)}) collective-permute-start(bf16[96,128]{1,0:T(8,128)(2,1)S(1)} %get-tuple-element.43), channel_id=1, source_target_pairs={{0,2},{1,3},{2,0},{3,1},{4,6},{5,7},{6,4},{7,5},{8,10},{9,11},{10,... | collective-permute-start | bytes 73736 | tf_op jit(solution)/shard_map/ppermute | solution.py:27
  13.6 3.1 %collective-permute-start.8 = (bf16[96,128]{1,0:T(8,128)(2,1)S(1)}, bf16[96,128]{1,0:T(8,128)(2,1)S(1)}, u32[]{:S(2)}, u32[]{:S(2)}) collective-permute-start(bf16[96,128]{1,0:T(8,128)(2,1)S(1)} %get-tuple-element.44), channel_id=1, source_target_pairs={{0,1},{1,0},{2,3},{3,2},{4,5},{5,4},{6,7},{7,6},{8,9},{9,8},{10,11... | collective-permute-start | bytes 73736 | tf_op jit(solution)/shard_map/ppermute | solution.py:27
  14.0 2.8 %copy-start.7 = (f32[128]{0:T(128)S(1)}, f32[128]{0:T(128)}, u32[]{:S(2)}) copy-start(f32[128]{0:T(128)} %param.14) | copy-start | bytes 1540

commit v18 on v17

--- a/solution.py
+++ b/solution.py
@@ -34,6 +34,11 @@
 def side_by_side(rows_of_blocks):
     r, c = rows_of_blocks.shape
     return rows_of_blocks.reshape(r, c // lanes, lanes).transpose(1, 0, 2).reshape(-1, lanes)
+
+
+def pack_rows(lowered):
+    half = lowered.shape[0] // 2
+    return jnp.concatenate([lowered[:half], lowered[half:]], axis=1)
 
 
 def split_halves(total):
@@ -315,7 +320,7 @@
     piece_refs = [refs[2 + place] for place in piece_places(replicas)]
     out_refs = refs[2 + replicas : 2 + replicas + shards]
     (right,) = refs[2 + replicas + shards :]
-    up_rows = out_refs[0].shape[0] - left_ref.shape[0]
+    up_rows = out_refs[0].shape[0] - left_ref.shape[0] // 2
     rows = left_ref.shape[0]
     rank = right.shape[0]
     width = right.shape[1] // replicas
@@ -338,12 +343,12 @@
     lowered = lax.dot_general(
         left_ref[...], right[...], (((1,), (1,)), ((), ())), preferred_element_type=f32
     )
-    both = jnp.concatenate(split_halves(lowered), axis=1)
+    sent = pack_rows(lowered.astype(bf16))
     ups = [piece[piece.shape[0] - up_rows :, :].astype(f32) for piece in piece_refs]
     for i in range(shards):
-        out_refs[i][:rows, :] = both
+        out_refs[i][: rows // 2, :] = sent
         picked = sum(up * pick_ref[i * replicas + k, :][None, :] for k, up in enumerate(ups))
-        out_refs[i][rows:, :] = picked.astype(bf16)
+        out_refs[i][rows // 2 :, :] = picked.astype(bf16)
 
 
 def route(left, pick, pieces, rank, up_rows, shards):
@@ -351,7 +356,7 @@
     replicas = len(pieces)
     return pl.pallas_call(
         functools.partial(route_kernel, replicas, shards),
-        out_shape=[jax.ShapeDtypeStruct((rows + up_rows, lanes), bf16)] * shards,
+        out_shape=[jax.ShapeDtypeStruct((rows // 2 + up_rows, lanes), bf16)] * shards,
         in_specs=[whole_in_vmem] * (2 + replicas),
         out_specs=[whole_in_vmem] * shards,
         scratch_shapes=[pltpu.VMEM((rank, depth), bf16)],
@@ -372,11 +377,11 @@
     up_matrix = jnp.take(ups, owners, axis=0, mode="clip").transpose(1, 0, 2)
     up_matrix = up_matrix.reshape(rank_part, -1)
     lowered = jnp.dot(tokens, down_matrix, preferred_element_type=f32)
-    both = jnp.concatenate(split_halves(lowered), axis=1)
+    sent = pack_rows(lowered.astype(bf16))
     packets = []
     for i in range(shards):
         up_block = lax.dynamic_slice_in_dim(up_matrix, (shard ^ i) * own, own, axis=1)
-        parts = [both, side_by_side(up_block)]
+        parts = [sent, side_by_side(up_block)]
         packets.append(jnp.concatenate(parts, axis=0))
     return packets
 
@@ -394,17 +399,22 @@
     group = grouped_ref.shape[0] // (head_count * rows)
     seen = step_count * group
 
-    lowered = jnp.zeros((rows, lanes), f32)
+    half = rows // 2
+    packed = jnp.zeros((half, lanes), f32)
     for i in range(shards):
-        lowered = lowered + packet_refs[i][:rows, :].astype(f32)
-        ups = packet_refs[i][rows:, :].astype(up_buf.dtype)
+        packed = packed + packet_refs[i][:half, :].astype(f32)
+        ups = packet_refs[i][half:, :].astype(up_buf.dtype)
         at = pl.multiple_of((shard ^ i) * rank_part, rank_part)
         for c in range(blocks):
             up_buf[pl.ds(at, rank_part), c * lanes : (c + 1) * lanes] = ups[
                 c * rank_part : (c + 1) * rank_part, :
             ]
+    turned = pltpu.roll(packed, rank, 1)
+    first = lax.broadcasted_iota(jnp.int32, (half, lanes), 1) < rank
+    lowered = jnp.concatenate(
+        [jnp.where(first, packed, turned), jnp.where(first, turned, packed)], axis=0
+    )
     lane = lax.broadcasted_iota(jnp.int32, (rows, lanes), 1)
-    lowered = lowered + pltpu.roll(lowered, rank, 1)
     high, low = split_halves(lowered)
     left = jnp.where(lane < rank, high.astype(f32), low.astype(f32)).astype(bf16)
     up = up_buf[...].astype(bf16)
@@ -436,9 +446,15 @@
         peak = jnp.maximum(old_peak, jnp.max(scores[h], axis=1, keepdims=True))
         fade = jnp.exp2((old_peak - peak) * exponent_scale)
         lifted = jnp.exp2((scores[h] - peak[:, :rows]) * exponent_scale)
-        denominator = fade * sum_ref[mine, :] + jnp.sum(lifted, axis=1, keepdims=True)
+        weights, left_over = split_halves(lifted)
+        ones = jnp.ones((rows, lanes), bf16)
+        denominator = (
+            fade * sum_ref[mine, :]
+            + jnp.dot(weights, ones, preferred_element_type=f32)
+            + jnp.dot(left_over, ones, preferred_element_type=f32)
+        )
         total = fade * total_ref[mine, :] + jnp.dot(
-            lifted.astype(bf16), values[h], preferred_element_type=f32
+            weights, values[h], preferred_element_type=f32
         )
         results.append(total / denominator)
     for pair in range(step_count // 2):

time: 18.4 us -> 18.3 us (level)
  no operation moved by 1% of the time
where the time goes in v18:
time: 18.3 us; the launch traced here: 18.2 us
  starting transfers between devices  9.43 us (52%)
  Pallas kernels  4.81 us (26%)
  waiting for transfers between devices  2.39 us (13%)
  local copies, waits for them, and re-layouts  0.81 us (4%)
  between operations  0.72 us (4%)
    ppermute x9, starting transfers between devices, swap(): return lax.ppermute(block, axis, [(s, s ^ offset) for s in range(count)])  9.43 us
    ppermute x9, waiting for transfers between devices, swap(): return lax.ppermute(block, axis, [(s, s ^ offset) for s in range(count)])  2.39 us
    pallas_call x1, Pallas kernels, project(): pl.pallas_call(functools.partial(project_kernel, step_count, row_count, h...  1.77 us
    pallas_call x1, Pallas kernels, finish(): pl.pallas_call(functools.partial(finish_kernel, step_count, row_count, he...  1.48 us
    pallas_call x1, Pallas kernels, attend(): pl.pallas_call(functools.partial(attend_kernel, width // lanes), out_shap...  1.18 us
    unnamed x16, local copies, waits for them, and re-layouts  0.81 us
  transfers between devices with their start and end apart: 9, of which 4 were waited for; matrix products, arithmetic and copies ran while one was open for 0% of the time, Pallas kernels for 18%

profile of v18, /device:TPU:0, one launch (start us, length us, event | category | flops | bytes accessed | tf_op | source)
XLA Modules:
  0.0 18.2 jit_solution(6412956798863213416)
XLA Ops:
  0.6 0.0 copy-start.5
  0.6 0.0 copy-start.6
  0.7 0.0 copy-start.3
  0.7 0.0 copy-start.4
  0.7 0.0 copy-start
  0.7 0.8 %copy-done.5 = bf16[64,512]{1,0:T(8,128)(2,1)S(1)} copy-done((bf16[64,512]{1,0:T(8,128)(2,1)S(1)}, bf16[64,512]{1,0:T(8,128)(2,1)}, u32[]{:S(2)}) %copy-start.5) | copy-done | bytes 65560
  1.5 0.0 copy-done.6
  1.5 0.1 pack.1.refs_6_.refs_2_
  1.6 4.0 %collective-permute-start.2 = (bf16[224,128]{1,0:T(8,128)(2,1)S(1)}, bf16[224,128]{1,0:T(8,128)(2,1)S(1)}, u32[]{:S(2)}, u32[]{:S(2)}) collective-permute-start(bf16[224,128]{1,0:T(8,128)(2,1)S(1)} %pack.1.refs_6_.refs_2_), channel_id=1, source_target_pairs={{0,8},{4,12},{8,0},{12,4},{1,9},{5,13},{9,1},{13,5},{2,10},{6,14},... | collective-permute-start | bytes 172040 | tf_op jit(solution)/shard_map/ppermute | solution.py:27
  5.6 1.3 %collective-permute-start.1 = (bf16[224,128]{1,0:T(8,128)(2,1)S(1)}, bf16[224,128]{1,0:T(8,128)(2,1)S(1)}, u32[]{:S(2)}, u32[]{:S(2)}) collective-permute-start(bf16[224,128]{1,0:T(8,128)(2,1)S(1)} %pack.1.refs_6_.refs_2_), channel_id=1, source_target_pairs={{0,12},{4,8},{8,4},{12,0},{1,13},{5,9},{9,5},{13,1},{2,14},{6,10},... | collective-permute-start | bytes 172040 | tf_op jit(solution)/shard_map/ppermute | solution.py:27
  6.9 0.2 %collective-permute-start = (bf16[224,128]{1,0:T(8,128)(2,1)S(1)}, bf16[224,128]{1,0:T(8,128)(2,1)S(1)}, u32[]{:S(2)}, u32[]{:S(2)}) collective-permute-start(bf16[224,128]{1,0:T(8,128)(2,1)S(1)} %pack.1.refs_6_.refs_2_), channel_id=1, source_target_pairs={{0,4},{4,0},{8,12},{12,8},{1,5},{5,1},{9,13},{13,9},{2,6},{6,2},{1... | collective-permute-start | bytes 172040 | tf_op jit(solution)/shard_map/ppermute | solution.py:27
  7.2 0.0 copy-done.3
  7.2 0.0 copy-done.4
  7.2 0.0 copy-done
  7.2 0.0 copy-start.1
  7.2 0.0 copy-start.2
  7.2 1.8 %project.1 = (f32[32,512]{1,0:T(8,128)S(1)}, bf16[32,512]{1,0:T(8,128)(2,1)S(1)}, bf16[32,512]{1,0:T(8,128)(2,1)S(1)}, bf16[32,512]{1,0:T(8,128)(2,1)S(1)}, bf16...) custom-call(s32[4]{0:T(128)} %refs_0_.1, ...), custom_call_target="tpu_custom_call" | custom-call | flops 167772160 | bytes 5242880 | tf_op jit(solution)/shard_map/project/pallas_call | solution.py:201
  9.0 0.1 collective-permute-start.3
  9.1 1.6 %collective-permute-start.4 = (bf16[32,512]{1,0:T(8,128)(2,1)S(1)}, bf16[32,512]{1,0:T(8,128)(2,1)S(1)}, u32[]{:S(2)}, u32[]{:S(2)}) collective-permute-start(bf16[32,512]{1,0:T(8,128)(2,1)S(1)} %get-tuple-element.33), channel_id=1, source_target_pairs={{0,2},{1,3},{2,0},{3,1},{4,6},{5,7},{6,4},{7,5},{8,10},{9,11},{10,... | collective-permute-start | bytes 98312 | tf_op jit(solution)/shard_map/ppermute | solution.py:27
  10.6 0.0 collective-permute-done.2.refs_5_
  10.6 0.3 %collective-permute-start.5 = (bf16[32,512]{1,0:T(8,128)(2,1)S(1)}, bf16[32,512]{1,0:T(8,128)(2,1)S(1)}, u32[]{:S(2)}, u32[]{:S(2)}) collective-permute-start(bf16[32,512]{1,0:T(8,128)(2,1)S(1)} %get-tuple-element.34), channel_id=1, source_target_pairs={{0,3},{1,2},{2,1},{3,0},{4,7},{5,6},{6,5},{7,4},{8,11},{9,10},{10,... | collective-permute-start | bytes 98312 | tf_op jit(solution)/shard_map/ppermute | solution.py:27
  10.9 0.8 %collective-permute-done.1.refs_4_ = bf16[224,128]{1,0:T(8,128)(2,1)S(1)} collective-permute-done((bf16[224,128]{1,0:T(8,128)(2,1)S(1)}, bf16[224,128]{1,0:T(8,128)(2,1)S(1)}, u32[]{:S(2)}, u32[]{:S(2)}) %collective-permute-start.1) | collective-permute-done | bytes 57376 | tf_op jit(solution)/shard_map/ppermute | solution.py:27
  11.7 0.1 collective-permute-done.refs_3_
  11.7 0.3 %route.1 = (bf16[80,128]{1,0:T(8,128)(2,1)S(1)}, bf16[80,128]{1,0:T(8,128)(2,1)S(1)}, bf16[80,128]{1,0:T(8,128)(2,1)S(1)}, bf16[80,128]{1,0:T(8,128)(2,1)S(1)}) custom-call(bf16[32,1536]{1,0:T(8,128)(2,1)S(1)} %get-tuple-element.28.refs_0_, f32[16,128]{1,0:T(8,128)S(1)} %get-tuple-element.29.refs_1_, bf16[224,128]{1,0:T(8,128)(2,1)S(1)} %pack.1.refs_6_.refs_2_, ...), custom_call_target="tpu_custom_call" | custom-call | bytes 800000 | tf_op jit(solution)/shard_map/route/pallas_call | solution.py:357
  12.0 0.6 %collective-permute-start.6 = (bf16[80,128]{1,0:T(8,128)(2,1)S(1)}, bf16[80,128]{1,0:T(8,128)(2,1)S(1)}, u32[]{:S(2)}, u32[]{:S(2)}) collective-permute-start(bf16[80,128]{1,0:T(8,128)(2,1)S(1)} %get-tuple-element.42), channel_id=1, source_target_pairs={{0,3},{1,2},{2,1},{3,0},{4,7},{5,6},{6,5},{7,4},{8,11},{9,10},{10,... | collective-permute-start | bytes 61448 | tf_op jit(solution)/shard_map/ppermute | solution.py:27
  12.7 0.9 %collective-permute-start.7 = (bf16[80,128]{1,0:T(8,128)(2,1)S(1)}, bf16[80,128]{1,0:T(8,128)(2,1)S(1)}, u32[]{:S(2)}, u32[]{:S(2)}) collective-permute-start(bf16[80,128]{1,0:T(8,128)(2,1)S(1)} %get-tuple-element.43), channel_id=1, source_target_pairs={{0,2},{1,3},{2,0},{3,1},{4,6},{5,7},{6,4},{7,5},{8,10},{9,11},{10,... | collective-permute-start | bytes 61448 | tf_op jit(solution)/shard_map/ppermute | solution.py:27
  13.6 0.0 collective-permute-done.3.refs_0_
  13.6 0.3 %collective-permute-start.8 = (bf16[80,128]{1,0:T(8,128)(2,1)S(1)}, bf16[80,128]{1,0:T(8,128)(2,1)S(1)}, u32[]{:S(2)}, u32[]{:S(2)}) collective-permute-start(bf16[80,128]{1,0:T(8,128)(2,1)S(1)} %get-tuple-element.44), channel_id=1, source_target_pairs={{0,1},{1,0},{2,3},{3,2},{4,5},{5,4},{6,7},{7,6},{8,9},{9,8},{10,11... | collective-permute-start | bytes 61448 | tf_op jit(solution)/shard_map/ppermute | solution.py:27
  13.9 0.0 collective-permute-done.4.refs_1_
  13.9 0.0 collective-permute-done.5.refs_2_
  14.0 0.0 copy-done.1
  14.0 0.0 copy-done.2
  14.0 0.0 copy-start.7
  14.0 1.2 %attend.1 = (f32[32,512]{1,0:T(8,128)S(1)}, f32[512,128]{1,0:T(8,128)S(1)}, f32[512,128]{1,0:T(8,128)S(1)}, f32[512,128]{1,0:T(8,128)S(1)}) custom-call(bf16[512,128]{1,0:T(8,128)(2,1)S(1)} %get-tuple-element.26.asked_ref, bf16[8,512,256]{2,1,0:T(8,128)(2,1)S(1)} %copy-done.1, bf16[8,512,256]{2,1,0:T(8,128)(2,1)S(1)} %copy-done.2, ...), custom_call_target="tpu_custom_call" | custom-call | flops 134217728 | bytes 4194304 | tf_op jit(solution)/shard_map/attend/pallas_call | solution.py:294
  15.2 0.3 %collective-permute-done.6.refs_8_ = bf16[80,128]{1,0:T(8,128)(2,1)S(1)} collective-permute-done((bf16[80,128]{1,0:T(8,128)(2,1)S(1)}, bf16[80,128]{1,0:T(8,128)(2,1)S(1)}, u32[]{:S(2)}, u32[]{:S(2)}) %collective-permute-start.6) | collective-permute-done | bytes 20512 | tf_op jit(solution)/shard_map/ppermute | solution.py:27
  15.4 1.3 %collective-permute-done.7.refs_9_ = bf16[80,128]{1,0:T(8,128)(2,1)S(1)} collective-permute-done((bf16[80,128]{1,0:T(8,128)(2,1)S(1)}, bf16[80,128]{1,0:T(8,128)(2,1)S(1)}, u32[]{:S(2)}, u32[]{:S(2)}) %collective-permute-start.7) | collective-permute-done | bytes 20512 | tf_op jit(solution)/shard_map/ppermute | solution.py:27
  16.7 0.0 collective-permute-done.8.refs_10_
  16.7 0.0 copy-done.7
  16.7 1.5 %finish.1 = (bf16[32,2048]{1,0:T(8,128)(2,1)}, bf16[32,256]{1,0:T(8,128)(2,1)}, bf16[32,256]{1,0:T(8,128)(2,1)}) custom-call(f32[1,128]{1,0:T(1,128)S(1)} %bitcast.10, f32[32,512]{1,0:T(8,128)S(1)} %get-tuple-element.35.refs_1_, bf16[512,128]{1,0:T(8,128)(2,1)S(1)} %get-tuple-element.36.refs_2_, f32[512,128]{1,0:T(8,128)S(1)} %get-tuple-element.37.refs_3_, ...), custom_call_target="tpu_custom_call" | custom-call | bytes 1000000 | tf_op jit(solution)/shard_map/finish/pallas_call | solution.py:476
  (1 shorter events, 0.0 us)
Async XLA Ops:
  0.6 0.8 %copy-start.5 = (bf16[64,512]{1,0:T(8,128)(2,1)S(1)}, bf16[64,512]{1,0:T(8,128)(2,1)}, u32[]{:S(2)}) copy-start(bf16[64,512]{1,0:T(8,128)(2,1)} %up_all_ref.1) | copy-start | bytes 196612
  0.6 0.8 %copy-start.6 = (bf16[320,64]{0,1:T(8,128)(2,1)S(1)}, bf16[320,64]{0,1:T(8,128)(2,1)}, u32[]{:S(2)}) copy-start(bf16[320,64]{0,1:T(8,128)(2,1)} %param.12) | copy-start | bytes 122884
  0.7 6.5 %copy-start.3 = (bf16[4,8,2048]{2,1,0:T(8,128)(2,1)S(1)}, bf16[4,8,2048]{2,1,0:T(8,128)(2,1)}, u32[]{:S(2)}) copy-start(bf16[4,8,2048]{2,1,0:T(8,128)(2,1)} %param.15) | copy-start | bytes 393220
  0.7 6.5 %copy-start.4 = (bf16[4,8,1280]{2,1,0:T(8,128)(2,1)S(1)}, bf16[4,8,1280]{2,1,0:T(8,128)(2,1)}, u32[]{:S(2)}) copy-start(bf16[4,8,1280]{2,1,0:T(8,128)(2,1)} %param.10) | copy-start | bytes 245764
  0.7 6.5 %copy-start = (bf16[1280,2048]{1,0:T(8,128)(2,1)S(1)}, bf16[1280,2048]{1,0:T(8,128)(2,1)}, u32[]{:S(2)}) copy-start(bf16[1280,2048]{1,0:T(8,128)(2,1)} %refs_3_.1) | copy-start | bytes 15728644
  1.6 9.1 %collective-permute-start.2 = (bf16[224,128]{1,0:T(8,128)(2,1)S(1)}, bf16[224,128]{1,0:T(8,128)(2,1)S(1)}, u32[]{:S(2)}, u32[]{:S(2)}) collective-permute-start(bf16[224,128]{1,0:T(8,128)(2,1)S(1)} %pack.1.refs_6_.refs_2_), channel_id=1, source_target_pairs={{0,8},{4,12},{8,0},{12,4},{1,9},{5,13},{9,1},{13,5},{2,10},{6,14},... | collective-permute-start | bytes 172040 | tf_op jit(solution)/shard_map/ppermute | solution.py:27
  5.6 6.1 %collective-permute-start.1 = (bf16[224,128]{1,0:T(8,128)(2,1)S(1)}, bf16[224,128]{1,0:T(8,128)(2,1)S(1)}, u32[]{:S(2)}, u32[]{:S(2)}) collective-permute-start(bf16[224,128]{1,0:T(8,128)(2,1)S(1)} %pack.1.refs_6_.refs_2_), channel_id=1, source_target_pairs={{0,12},{4,8},{8,4},{12,0},{1,13},{5,9},{9,5},{13,1},{2,14},{6,10},... | collective-permute-start | bytes 172040 | tf_op jit(solution)/shard_map/ppermute | solution.py:27
  6.9 4.8 %collective-permute-start = (bf16[224,128]{1,0:T(8,128)(2,1)S(1)}, bf16[224,128]{1,0:T(8,128)(2,1)S(1)}, u32[]{:S(2)}, u32[]{:S(2)}) collective-permute-start(bf16[224,128]{1,0:T(8,128)(2,1)S(1)} %pack.1.refs_6_.refs_2_), channel_id=1, source_target_pairs={{0,4},{4,0},{8,12},{12,8},{1,5},{5,1},{9,13},{13,9},{2,6},{6,2},{1... | collective-permute-start | bytes 172040 | tf_op jit(solution)/shard_map/ppermute | solution.py:27
  7.2 6.8 %copy-start.1 = (bf16[8,512,256]{2,1,0:T(8,128)(2,1)S(1)}, bf16[8,512,256]{2,1,0:T(8,128)(2,1)}, u32[]{:S(2)}) copy-start(bf16[8,512,256]{2,1,0:T(8,128)(2,1)} %keys_ref.1) | copy-start | bytes 6291460
  7.2 6.8 %copy-start.2 = (bf16[8,512,256]{2,1,0:T(8,128)(2,1)S(1)}, bf16[8,512,256]{2,1,0:T(8,128)(2,1)}, u32[]{:S(2)}) copy-start(bf16[8,512,256]{2,1,0:T(8,128)(2,1)} %values_ref.1) | copy-start | bytes 6291460
  9.0 4.6 %collective-permute-start.3 = (bf16[32,512]{1,0:T(8,128)(2,1)S(1)}, bf16[32,512]{1,0:T(8,128)(2,1)S(1)}, u32[]{:S(2)}, u32[]{:S(2)}) collective-permute-start(bf16[32,512]{1,0:T(8,128)(2,1)S(1)} %get-tuple-element.32), channel_id=1, source_target_pairs={{0,1},{1,0},{2,3},{3,2},{4,5},{5,4},{6,7},{7,6},{8,9},{9,8},{10,11... | collective-permute-start | bytes 98312 | tf_op jit(solution)/shard_map/ppermute | solution.py:27
  9.1 4.9 %collective-permute-start.4 = (bf16[32,512]{1,0:T(8,128)(2,1)S(1)}, bf16[32,512]{1,0:T(8,128)(2,1)S(1)}, u32[]{:S(2)}, u32[]{:S(2)}) collective-permute-start(bf16[32,512]{1,0:T(8,128)(2,1)S(1)} %get-tuple-element.33), channel_id=1, source_target_pairs={{0,2},{1,3},{2,0},{3,1},{4,6},{5,7},{6,4},{7,5},{8,10},{9,11},{10,... | collective-permute-start | bytes 98312 | tf_op jit(solution)/shard_map/ppermute | solution.py:27
  10.6 3.3 %collective-permute-start.5 = (bf16[32,512]{1,0:T(8,128)(2,1)S(1)}, bf16[32,512]{1,0:T(8,128)(2,1)S(1)}, u32[]{:S(2)}, u32[]{:S(2)}) collective-permute-start(bf16[32,512]{1,0:T(8,128)(2,1)S(1)} %get-tuple-element.34), channel_id=1, source_target_pairs={{0,3},{1,2},{2,1},{3,0},{4,7},{5,6},{6,5},{7,4},{8,11},{9,10},{10,... | collective-permute-start | bytes 98312 | tf_op jit(solution)/shard_map/ppermute | solution.py:27
  12.0 3.4 %collective-permute-start.6 = (bf16[80,128]{1,0:T(8,128)(2,1)S(1)}, bf16[80,128]{1,0:T(8,128)(2,1)S(1)}, u32[]{:S(2)}, u32[]{:S(2)}) collective-permute-start(bf16[80,128]{1,0:T(8,128)(2,1)S(1)} %get-tuple-element.42), channel_id=1, source_target_pairs={{0,3},{1,2},{2,1},{3,0},{4,7},{5,6},{6,5},{7,4},{8,11},{9,10},{10,... | collective-permute-start | bytes 61448 | tf_op jit(solution)/shard_map/ppermute | solution.py:27
  12.7 4.0 %collective-permute-start.7 = (bf16[80,128]{1,0:T(8,128)(2,1)S(1)}, bf16[80,128]{1,0:T(8,128)(2,1)S(1)}, u32[]{:S(2)}, u32[]{:S(2)}) collective-permute-start(bf16[80,128]{1,0:T(8,128)(2,1)S(1)} %get-tuple-element.43), channel_id=1, source_target_pairs={{0,2},{1,3},{2,0},{3,1},{4,6},{5,7},{6,4},{7,5},{8,10},{9,11},{10,... | collective-permute-start | bytes 61448 | tf_op jit(solution)/shard_map/ppermute | solution.py:27
  13.6 3.1 %collective-permute-start.8 = (bf16[80,128]{1,0:T(8,128)(2,1)S(1)}, bf16[80,128]{1,0:T(8,128)(2,1)S(1)}, u32[]{:S(2)}, u32[]{:S(2)}) collective-permute-start(bf16[80,128]{1,0:T(8,128)(2,1)S(1)} %get-tuple-element.44), channel_id=1, source_target_pairs={{0,1},{1,0},{2,3},{3,2},{4,5},{5,4},{6,7},{7,6},{8,9},{9,8},{10,11... | collective-permute-start | bytes 61448 | tf_op jit(solution)/shard_map/ppermute | solution.py:27
  14.0 2.7 %copy-start.7 = (f32[128]{0:T(128)S(1)}, f32[128]{0:T(128)}, u32[]{:S(2)}) copy-start(f32[128]{0:T(128)} %param.14) | copy-start | bytes 1540

commit v19 on v17

--- a/solution.py
+++ b/solution.py
@@ -25,6 +25,12 @@
 def swap(block, axis, offset):
     count = lax.axis_size(axis)
     return lax.ppermute(block, axis, [(s, s ^ offset) for s in range(count)])
+
+
+def send(block, axis, offset, down):
+    count = lax.axis_size(axis)
+    pairs = [(s, s ^ offset) for s in range(count)]
+    return lax.ppermute(block, axis, [(s, d) for s, d in pairs if (s > d) == down])
 
 
 def in_hbm(*arrays):
@@ -305,17 +311,24 @@
     )(asked, keys, values, bias, after, mine, *others)
 
 
-def piece_places(replicas):
-    order = [0, 1] + list(range(replicas - 1, 1, -1))
-    return [order.index(i) for i in range(replicas)]
+def arrival_order(shards):
+    far = range(2, shards)
+    order = [(i, True) for i in far] + [(i, False) for i in far]
+    return order + [(1, None), (0, None)]
+
+
+def piece_order(replicas):
+    return [0, 1] + list(range(replicas - 1, 1, -1))
 
 
 def route_kernel(replicas, shards, *refs):
     left_ref, pick_ref = refs[:2]
-    piece_refs = [refs[2 + place] for place in piece_places(replicas)]
-    out_refs = refs[2 + replicas : 2 + replicas + shards]
-    (right,) = refs[2 + replicas + shards :]
-    up_rows = out_refs[0].shape[0] - left_ref.shape[0]
+    order = piece_order(replicas)
+    piece_refs = [refs[2 + order.index(i)] for i in range(replicas)]
+    names = arrival_order(shards)
+    out_refs = dict(zip(names, refs[2 + replicas : 2 + replicas + len(names)]))
+    (right,) = refs[2 + replicas + len(names) :]
+    up_rows = out_refs[0, None].shape[0] - left_ref.shape[0]
     rows = left_ref.shape[0]
     rank = right.shape[0]
     width = right.shape[1] // replicas
@@ -341,24 +354,28 @@
     both = jnp.concatenate(split_halves(lowered), axis=1)
     ups = [piece[piece.shape[0] - up_rows :, :].astype(f32) for piece in piece_refs]
     for i in range(shards):
-        out_refs[i][:rows, :] = both
         picked = sum(up * pick_ref[i * replicas + k, :][None, :] for k, up in enumerate(ups))
-        out_refs[i][rows:, :] = picked.astype(bf16)
+        for (offset, _), out_ref in out_refs.items():
+            if offset == i:
+                out_ref[:rows, :] = both
+                out_ref[rows:, :] = picked.astype(bf16)
 
 
 def route(left, pick, pieces, rank, up_rows, shards):
     rows, depth = left.shape
     replicas = len(pieces)
-    return pl.pallas_call(
+    names = arrival_order(shards)
+    packets = pl.pallas_call(
         functools.partial(route_kernel, replicas, shards),
-        out_shape=[jax.ShapeDtypeStruct((rows + up_rows, lanes), bf16)] * shards,
+        out_shape=[jax.ShapeDtypeStruct((rows + up_rows, lanes), bf16)] * len(names),
         in_specs=[whole_in_vmem] * (2 + replicas),
-        out_specs=[whole_in_vmem] * shards,
+        out_specs=[whole_in_vmem] * len(names),
         scratch_shapes=[pltpu.VMEM((rank, depth), bf16)],
         compiler_params=pltpu.CompilerParams(vmem_limit_bytes=4 * 2**20),
         name="route",
         cost_estimate=pl.CostEstimate(flops=0, bytes_accessed=800000, transcendentals=0),
-    )(left, pick, *[pieces[i] for i in piece_places(replicas)])
+    )(left, pick, *[pieces[i] for i in piece_order(replicas)])
+    return dict(zip(names, packets))
 
 
 def route_plain(owners, tokens, down, up, rank_part, own, shards):
@@ -378,13 +395,16 @@
         up_block = lax.dynamic_slice_in_dim(up_matrix, (shard ^ i) * own, own, axis=1)
         parts = [both, side_by_side(up_block)]
         packets.append(jnp.concatenate(parts, axis=0))
-    return packets
+    return {(i, down): packets[i] for i, down in arrival_order(shards)}
 
 
 def finish_kernel(step_count, row_count, head_count, shards, *refs):
     gain_ref, base_ref, grouped_ref, total_ref, peak_ref, sum_ref, cosine_ref, sine_ref = refs[:8]
-    packet_refs = refs[8 : 8 + shards][::-1]
-    visible_ref, attention_ref, keys_ref, values_ref, up_buf = refs[8 + shards :]
+    names = arrival_order(shards)
+    parts = dict(zip(names, refs[8 : 8 + len(names)]))
+    arrivals = [[ref for (i, _), ref in parts.items() if i == offset] for offset in range(shards)]
+    visible_ref = refs[8 + len(names)]
+    attention_ref, keys_ref, values_ref, up_buf = refs[9 + len(names) :]
     shard = lax.axis_index("tensor")
     rows = step_count * row_count
     own = base_ref.shape[1]
@@ -396,8 +416,9 @@
 
     lowered = jnp.zeros((rows, lanes), f32)
     for i in range(shards):
-        lowered = lowered + packet_refs[i][:rows, :].astype(f32)
-        ups = packet_refs[i][rows:, :].astype(up_buf.dtype)
+        packet = sum(part[...].astype(f32) for part in arrivals[i])
+        lowered = lowered + packet[:rows, :]
+        ups = packet[rows:, :].astype(up_buf.dtype)
         at = pl.multiple_of((shard ^ i) * rank_part, rank_part)
         for c in range(blocks):
             up_buf[pl.ds(at, rank_part), c * lanes : (c + 1) * lanes] = ups[
@@ -453,9 +474,8 @@
             ] = jnp.concatenate(both, axis=0).astype(bf16)
 
 
-def finish(base, visible, partials, gain, packets, rank, step_count, row_count, query_width):
+def finish(base, visible, partials, gain, arrived, shards, rank, step_count, row_count, query_width):
     rows, own = base.shape
-    shards = len(packets)
     head_count = own // (2 * lanes)
     return pl.pallas_call(
         functools.partial(finish_kernel, step_count, row_count, head_count, shards),
@@ -464,7 +484,7 @@
             jax.ShapeDtypeStruct((rows, head_count * lanes), bf16),
             jax.ShapeDtypeStruct((rows, head_count * lanes), bf16),
         ),
-        in_specs=[whole_in_vmem] * (9 + shards),
+        in_specs=[whole_in_vmem] * (7 + 2 * shards),
         out_specs=(whole_in_vmem,) * 3,
         scratch_shapes=[
             pltpu.VMEM((rank, own), bf16 if rank // shards % 16 == 0 else f32),
@@ -472,7 +492,7 @@
         compiler_params=pltpu.CompilerParams(vmem_limit_bytes=6 * 2**20),
         name="finish",
         cost_estimate=pl.CostEstimate(flops=0, bytes_accessed=1000000, transcendentals=0),
-    )(gain, base, *partials, *packets[::-1], visible)
+    )(gain, base, *partials, *[arrived[name] for name in arrival_order(shards)], visible)
 
 
 def per_device(
@@ -533,15 +553,21 @@
             owners, tokens, adapter_down, adapter_up, rank_part, own, shards
         )
     base, total, peak, denominator = attend(
-        asked, cache_keys, stored_values, bias, packets[0], mine, others
-    )
-    packets = [packets[0]] + [swap(packets[i], "tensor", i) for i in range(1, shards)]
+        asked, cache_keys, stored_values, bias, packets[0, None], mine, others
+    )
+    arrived = {}
+    for (i, down), packet in packets.items():
+        if i > 1:
+            arrived[i, down] = send(packet, "tensor", i, down)
+        else:
+            arrived[i, down] = swap(packet, "tensor", i) if i else packet
     attention, keys, values = finish(
         base,
         visible,
         (grouped, total, peak, denominator, cosine, sine),
         key_gain.reshape(1, -1),
-        packets,
+        arrived,
+        shards,
         rank,
         step_count,
         row_count,

time: 18.4 us -> 23.7 us (1.29)
  starting transfers between devices: 9.43 us -> 16.2 us
  waiting for transfers between devices: 2.44 us -> 0.88 us
    ppermute x0 -> x4, starting transfers between devices: none -> 8.41 us  [send(): lax.ppermute(block, axis, [(s, d) for s, d in pairs if (s > d) == down])]
    ppermute x9 -> x7, starting transfers between devices: 9.43 us -> 7.74 us  [swap(): return lax.ppermute(block, axis, [(s, s ^ offset) for s in range(count)])]
    ppermute x9 -> x7, waiting for transfers between devices: 2.44 us -> 0.83 us  [swap(): return lax.ppermute(block, axis, [(s, s ^ offset) for s in range(count)])]
  transfers between devices with their start and end apart: 9 -> 11, of which waited for: 4 -> 2; matrix products, arithmetic and copies ran while one was open for 0% -> 0% of each run, Pallas kernels for 18% -> 14%
where the time goes in v19:
time: 23.7 us; the launch traced here: 23.5 us
  starting transfers between devices  16.2 us (68%)
  Pallas kernels  4.81 us (20%)
  waiting for transfers between devices  0.88 us (4%)
  local copies, waits for them, and re-layouts  0.81 us (3%)
  between operations  0.8 us (3%)
    ppermute x4, starting transfers between devices, send(): lax.ppermute(block, axis, [(s, d) for s, d in pairs if (s > d) == down])  8.41 us
    ppermute x7, starting transfers between devices, swap(): return lax.ppermute(block, axis, [(s, s ^ offset) for s in range(count)])  7.74 us
    pallas_call x1, Pallas kernels, project(): pl.pallas_call(functools.partial(project_kernel, step_count, row_count, h...  1.77 us
    pallas_call x1, Pallas kernels, finish(): pl.pallas_call(functools.partial(finish_kernel, step_count, row_count, he...  1.43 us
    pallas_call x1, Pallas kernels, attend(): pl.pallas_call(functools.partial(attend_kernel, width // lanes), out_shap...  1.22 us
    ppermute x7, waiting for transfers between devices, swap(): return lax.ppermute(block, axis, [(s, s ^ offset) for s in range(count)])  0.83 us
    unnamed x16, local copies, waits for them, and re-layouts  0.81 us
  transfers between devices with their start and end apart: 11, of which 2 were waited for; matrix products, arithmetic and copies ran while one was open for 0% of the time, Pallas kernels for 14%

profile of v19, /device:TPU:0, one launch (start us, length us, event | category | flops | bytes accessed | tf_op | source)
XLA Modules:
  0.0 23.5 jit_solution(5988283192304416908)
XLA Ops:
  0.6 0.0 copy-start.5
  0.6 0.0 copy-start.6
  0.7 0.0 copy-start.3
  0.7 0.0 copy-start.4
  0.7 0.0 copy-start
  0.7 0.8 %copy-done.5 = bf16[64,512]{1,0:T(8,128)(2,1)S(1)} copy-done((bf16[64,512]{1,0:T(8,128)(2,1)S(1)}, bf16[64,512]{1,0:T(8,128)(2,1)}, u32[]{:S(2)}) %copy-start.5) | copy-done | bytes 65560
  1.5 0.0 copy-done.6
  1.5 0.1 pack.1.refs_6_.refs_2_
  1.6 4.0 %collective-permute-start.2 = (bf16[224,128]{1,0:T(8,128)(2,1)S(1)}, bf16[224,128]{1,0:T(8,128)(2,1)S(1)}, u32[]{:S(2)}, u32[]{:S(2)}) collective-permute-start(bf16[224,128]{1,0:T(8,128)(2,1)S(1)} %pack.1.refs_6_.refs_2_), channel_id=1, source_target_pairs={{0,8},{4,12},{8,0},{12,4},{1,9},{5,13},{9,1},{13,5},{2,10},{6,14},... | collective-permute-start | bytes 172040 | tf_op jit(solution)/shard_map/ppermute | solution.py:27
  5.6 1.3 %collective-permute-start.1 = (bf16[224,128]{1,0:T(8,128)(2,1)S(1)}, bf16[224,128]{1,0:T(8,128)(2,1)S(1)}, u32[]{:S(2)}, u32[]{:S(2)}) collective-permute-start(bf16[224,128]{1,0:T(8,128)(2,1)S(1)} %pack.1.refs_6_.refs_2_), channel_id=1, source_target_pairs={{0,12},{4,8},{8,4},{12,0},{1,13},{5,9},{9,5},{13,1},{2,14},{6,10},... | collective-permute-start | bytes 172040 | tf_op jit(solution)/shard_map/ppermute | solution.py:27
  6.9 0.2 collective-permute-start
  7.2 0.0 copy-done.3
  7.2 0.0 copy-done.4
  7.2 0.0 copy-done
  7.2 0.0 copy-start.1
  7.2 0.0 copy-start.2
  7.2 1.8 %project.1 = (f32[32,512]{1,0:T(8,128)S(1)}, bf16[32,512]{1,0:T(8,128)(2,1)S(1)}, bf16[32,512]{1,0:T(8,128)(2,1)S(1)}, bf16[32,512]{1,0:T(8,128)(2,1)S(1)}, bf16...) custom-call(s32[4]{0:T(128)} %refs_0_.1, ...), custom_call_target="tpu_custom_call" | custom-call | flops 167772160 | bytes 5242880 | tf_op jit(solution)/shard_map/project/pallas_call | solution.py:202
  9.0 0.1 collective-permute-start.3
  9.1 1.6 %collective-permute-start.4 = (bf16[32,512]{1,0:T(8,128)(2,1)S(1)}, bf16[32,512]{1,0:T(8,128)(2,1)S(1)}, u32[]{:S(2)}, u32[]{:S(2)}) collective-permute-start(bf16[32,512]{1,0:T(8,128)(2,1)S(1)} %get-tuple-element.35), channel_id=1, source_target_pairs={{0,2},{1,3},{2,0},{3,1},{4,6},{5,7},{6,4},{7,5},{8,10},{9,11},{10,... | collective-permute-start | bytes 98312 | tf_op jit(solution)/shard_map/ppermute | solution.py:27
  10.6 0.0 collective-permute-done.2.refs_5_
  10.6 0.3 %collective-permute-start.5 = (bf16[32,512]{1,0:T(8,128)(2,1)S(1)}, bf16[32,512]{1,0:T(8,128)(2,1)S(1)}, u32[]{:S(2)}, u32[]{:S(2)}) collective-permute-start(bf16[32,512]{1,0:T(8,128)(2,1)S(1)} %get-tuple-element.36), channel_id=1, source_target_pairs={{0,3},{1,2},{2,1},{3,0},{4,7},{5,6},{6,5},{7,4},{8,11},{9,10},{10,... | collective-permute-start | bytes 98312 | tf_op jit(solution)/shard_map/ppermute | solution.py:27
  10.9 0.8 %collective-permute-done.1.refs_4_ = bf16[224,128]{1,0:T(8,128)(2,1)S(1)} collective-permute-done((bf16[224,128]{1,0:T(8,128)(2,1)S(1)}, bf16[224,128]{1,0:T(8,128)(2,1)S(1)}, u32[]{:S(2)}, u32[]{:S(2)}) %collective-permute-start.1) | collective-permute-done | bytes 57376 | tf_op jit(solution)/shard_map/ppermute | solution.py:27
  11.7 0.1 collective-permute-done.refs_3_
  11.7 0.3 %route.1 = (bf16[96,128]{1,0:T(8,128)(2,1)S(1)}, bf16[96,128]{1,0:T(8,128)(2,1)S(1)}, bf16[96,128]{1,0:T(8,128)(2,1)S(1)}, bf16[96,128]{1,0:T(8,128)(2,1)S(1)}, ...) custom-call(bf16[32,1536]{1,0:T(8,128)(2,1)S(1)} %get-tuple-element.30.refs_0_, ...), custom_call_target="tpu_custom_call" | custom-call | bytes 800000 | tf_op jit(solution)/shard_map/route/pallas_call | solution.py:368
  12.0 1.3 %collective-permute-start.6 = (bf16[96,128]{1,0:T(8,128)(2,1)S(1)}, bf16[96,128]{1,0:T(8,128)(2,1)S(1)}, u32[]{:S(2)}, u32[]{:S(2)}) collective-permute-start(bf16[96,128]{1,0:T(8,128)(2,1)S(1)} %get-tuple-element.44), channel_id=1, source_target_pairs={{2,0},{3,1},{6,4},{7,5},{10,8},{11,9},{14,12},{15,13},{18,16},{19,... | collective-permute-start | bytes 73736 | tf_op jit(solution)/shard_map/ppermute | solution.py:33
  13.3 1.3 %collective-permute-start.7 = (bf16[96,128]{1,0:T(8,128)(2,1)S(1)}, bf16[96,128]{1,0:T(8,128)(2,1)S(1)}, u32[]{:S(2)}, u32[]{:S(2)}) collective-permute-start(bf16[96,128]{1,0:T(8,128)(2,1)S(1)} %get-tuple-element.45), channel_id=1, source_target_pairs={{2,1},{3,0},{6,5},{7,4},{10,9},{11,8},{14,13},{15,12},{18,17},{19,... | collective-permute-start | bytes 73736 | tf_op jit(solution)/shard_map/ppermute | solution.py:33
  14.6 0.0 collective-permute-done.3.refs_0_
  14.7 4.5 %collective-permute-start.8 = (bf16[96,128]{1,0:T(8,128)(2,1)S(1)}, bf16[96,128]{1,0:T(8,128)(2,1)S(1)}, u32[]{:S(2)}, u32[]{:S(2)}) collective-permute-start(bf16[96,128]{1,0:T(8,128)(2,1)S(1)} %get-tuple-element.46), channel_id=1, source_target_pairs={{0,2},{1,3},{4,6},{5,7},{8,10},{9,11},{12,14},{13,15},{16,18},{17,... | collective-permute-start | bytes 73736 | tf_op jit(solution)/shard_map/ppermute | solution.py:33
  19.2 0.0 collective-permute-done.4.refs_1_
  19.2 1.3 %collective-permute-start.9 = (bf16[96,128]{1,0:T(8,128)(2,1)S(1)}, bf16[96,128]{1,0:T(8,128)(2,1)S(1)}, u32[]{:S(2)}, u32[]{:S(2)}) collective-permute-start(bf16[96,128]{1,0:T(8,128)(2,1)S(1)} %get-tuple-element.47), channel_id=1, source_target_pairs={{0,3},{1,2},{4,7},{5,6},{8,11},{9,10},{12,15},{13,14},{16,19},{17,... | collective-permute-start | bytes 73736 | tf_op jit(solution)/shard_map/ppermute | solution.py:33
  20.5 0.0 collective-permute-done.5.refs_2_
  20.5 0.2 collective-permute-start.10
  20.7 0.0 copy-done.1
  20.7 0.0 copy-done.2
  20.7 0.0 copy-start.7
  20.7 1.2 %attend.1 = (f32[32,512]{1,0:T(8,128)S(1)}, f32[512,128]{1,0:T(8,128)S(1)}, f32[512,128]{1,0:T(8,128)S(1)}, f32[512,128]{1,0:T(8,128)S(1)}) custom-call(bf16[512,128]{1,0:T(8,128)(2,1)S(1)} %get-tuple-element.28.asked_ref, bf16[8,512,256]{2,1,0:T(8,128)(2,1)S(1)} %copy-done.1, bf16[8,512,256]{2,1,0:T(8,128)(2,1)S(1)} %copy-done.2, ...), custom_call_target="tpu_custom_call" | custom-call | flops 134217728 | bytes 4194304 | tf_op jit(solution)/shard_map/attend/pallas_call | solution.py:295
  21.9 0.0 collective-permute-done.6.refs_8_
  21.9 0.0 collective-permute-done.7.refs_9_
  22.0 0.0 collective-permute-done.8.refs_10_
  22.0 0.0 collective-permute-done.9.refs_11_
  22.0 0.0 collective-permute-done.10.refs_12_
  22.0 0.0 copy-done.7
  22.0 1.4 %finish.1 = (bf16[32,2048]{1,0:T(8,128)(2,1)}, bf16[32,256]{1,0:T(8,128)(2,1)}, bf16[32,256]{1,0:T(8,128)(2,1)}) custom-call(f32[1,128]{1,0:T(1,128)S(1)} %bitcast.10, f32[32,512]{1,0:T(8,128)S(1)} %get-tuple-element.37.refs_1_, bf16[512,128]{1,0:T(8,128)(2,1)S(1)} %get-tuple-element.38.refs_2_, f32[512,128]{1,0:T(8,128)S(1)} %get-tuple-element.39.refs_3_, ...), custom_call_target="tpu_custom_call" | custom-call | bytes 1000000 | tf_op jit(solution)/shard_map/finish/pallas_call | solution.py:480
  (1 shorter events, 0.0 us)
Async XLA Ops:
  0.6 0.8 %copy-start.5 = (bf16[64,512]{1,0:T(8,128)(2,1)S(1)}, bf16[64,512]{1,0:T(8,128)(2,1)}, u32[]{:S(2)}) copy-start(bf16[64,512]{1,0:T(8,128)(2,1)} %up_all_ref.1) | copy-start | bytes 196612
  0.6 0.8 %copy-start.6 = (bf16[320,64]{0,1:T(8,128)(2,1)S(1)}, bf16[320,64]{0,1:T(8,128)(2,1)}, u32[]{:S(2)}) copy-start(bf16[320,64]{0,1:T(8,128)(2,1)} %param.12) | copy-start | bytes 122884
  0.7 6.5 %copy-start.3 = (bf16[4,8,2048]{2,1,0:T(8,128)(2,1)S(1)}, bf16[4,8,2048]{2,1,0:T(8,128)(2,1)}, u32[]{:S(2)}) copy-start(bf16[4,8,2048]{2,1,0:T(8,128)(2,1)} %param.15) | copy-start | bytes 393220
  0.7 6.5 %copy-start.4 = (bf16[4,8,1280]{2,1,0:T(8,128)(2,1)S(1)}, bf16[4,8,1280]{2,1,0:T(8,128)(2,1)}, u32[]{:S(2)}) copy-start(bf16[4,8,1280]{2,1,0:T(8,128)(2,1)} %param.10) | copy-start | bytes 245764
  0.7 6.5 %copy-start = (bf16[1280,2048]{1,0:T(8,128)(2,1)S(1)}, bf16[1280,2048]{1,0:T(8,128)(2,1)}, u32[]{:S(2)}) copy-start(bf16[1280,2048]{1,0:T(8,128)(2,1)} %refs_3_.1) | copy-start | bytes 15728644
  1.6 9.1 %collective-permute-start.2 = (bf16[224,128]{1,0:T(8,128)(2,1)S(1)}, bf16[224,128]{1,0:T(8,128)(2,1)S(1)}, u32[]{:S(2)}, u32[]{:S(2)}) collective-permute-start(bf16[224,128]{1,0:T(8,128)(2,1)S(1)} %pack.1.refs_6_.refs_2_), channel_id=1, source_target_pairs={{0,8},{4,12},{8,0},{12,4},{1,9},{5,13},{9,1},{13,5},{2,10},{6,14},... | collective-permute-start | bytes 172040 | tf_op jit(solution)/shard_map/ppermute | solution.py:27
  5.6 6.1 %collective-permute-start.1 = (bf16[224,128]{1,0:T(8,128)(2,1)S(1)}, bf16[224,128]{1,0:T(8,128)(2,1)S(1)}, u32[]{:S(2)}, u32[]{:S(2)}) collective-permute-start(bf16[224,128]{1,0:T(8,128)(2,1)S(1)} %pack.1.refs_6_.refs_2_), channel_id=1, source_target_pairs={{0,12},{4,8},{8,4},{12,0},{1,13},{5,9},{9,5},{13,1},{2,14},{6,10},... | collective-permute-start | bytes 172040 | tf_op jit(solution)/shard_map/ppermute | solution.py:27
  6.9 4.8 %collective-permute-start = (bf16[224,128]{1,0:T(8,128)(2,1)S(1)}, bf16[224,128]{1,0:T(8,128)(2,1)S(1)}, u32[]{:S(2)}, u32[]{:S(2)}) collective-permute-start(bf16[224,128]{1,0:T(8,128)(2,1)S(1)} %pack.1.refs_6_.refs_2_), channel_id=1, source_target_pairs={{0,4},{4,0},{8,12},{12,8},{1,5},{5,1},{9,13},{13,9},{2,6},{6,2},{1... | collective-permute-start | bytes 172040 | tf_op jit(solution)/shard_map/ppermute | solution.py:27
  7.2 13.5 %copy-start.1 = (bf16[8,512,256]{2,1,0:T(8,128)(2,1)S(1)}, bf16[8,512,256]{2,1,0:T(8,128)(2,1)}, u32[]{:S(2)}) copy-start(bf16[8,512,256]{2,1,0:T(8,128)(2,1)} %keys_ref.1) | copy-start | bytes 6291460
  7.2 13.5 %copy-start.2 = (bf16[8,512,256]{2,1,0:T(8,128)(2,1)S(1)}, bf16[8,512,256]{2,1,0:T(8,128)(2,1)}, u32[]{:S(2)}) copy-start(bf16[8,512,256]{2,1,0:T(8,128)(2,1)} %values_ref.1) | copy-start | bytes 6291460
  9.0 5.7 %collective-permute-start.3 = (bf16[32,512]{1,0:T(8,128)(2,1)S(1)}, bf16[32,512]{1,0:T(8,128)(2,1)S(1)}, u32[]{:S(2)}, u32[]{:S(2)}) collective-permute-start(bf16[32,512]{1,0:T(8,128)(2,1)S(1)} %get-tuple-element.34), channel_id=1, source_target_pairs={{0,1},{1,0},{2,3},{3,2},{4,5},{5,4},{6,7},{7,6},{8,9},{9,8},{10,11... | collective-permute-start | bytes 98312 | tf_op jit(solution)/shard_map/ppermute | solution.py:27
  9.1 10.1 %collective-permute-start.4 = (bf16[32,512]{1,0:T(8,128)(2,1)S(1)}, bf16[32,512]{1,0:T(8,128)(2,1)S(1)}, u32[]{:S(2)}, u32[]{:S(2)}) collective-permute-start(bf16[32,512]{1,0:T(8,128)(2,1)S(1)} %get-tuple-element.35), channel_id=1, source_target_pairs={{0,2},{1,3},{2,0},{3,1},{4,6},{5,7},{6,4},{7,5},{8,10},{9,11},{10,... | collective-permute-start | bytes 98312 | tf_op jit(solution)/shard_map/ppermute | solution.py:27
  10.6 9.9 %collective-permute-start.5 = (bf16[32,512]{1,0:T(8,128)(2,1)S(1)}, bf16[32,512]{1,0:T(8,128)(2,1)S(1)}, u32[]{:S(2)}, u32[]{:S(2)}) collective-permute-start(bf16[32,512]{1,0:T(8,128)(2,1)S(1)} %get-tuple-element.36), channel_id=1, source_target_pairs={{0,3},{1,2},{2,1},{3,0},{4,7},{5,6},{6,5},{7,4},{8,11},{9,10},{10,... | collective-permute-start | bytes 98312 | tf_op jit(solution)/shard_map/ppermute | solution.py:27
  12.0 9.9 %collective-permute-start.6 = (bf16[96,128]{1,0:T(8,128)(2,1)S(1)}, bf16[96,128]{1,0:T(8,128)(2,1)S(1)}, u32[]{:S(2)}, u32[]{:S(2)}) collective-permute-start(bf16[96,128]{1,0:T(8,128)(2,1)S(1)} %get-tuple-element.44), channel_id=1, source_target_pairs={{2,0},{3,1},{6,4},{7,5},{10,8},{11,9},{14,12},{15,13},{18,16},{19,... | collective-permute-start | bytes 73736 | tf_op jit(solution)/shard_map/ppermute | solution.py:33
  13.3 8.6 %collective-permute-start.7 = (bf16[96,128]{1,0:T(8,128)(2,1)S(1)}, bf16[96,128]{1,0:T(8,128)(2,1)S(1)}, u32[]{:S(2)}, u32[]{:S(2)}) collective-permute-start(bf16[96,128]{1,0:T(8,128)(2,1)S(1)} %get-tuple-element.45), channel_id=1, source_target_pairs={{2,1},{3,0},{6,5},{7,4},{10,9},{11,8},{14,13},{15,12},{18,17},{19,... | collective-permute-start | bytes 73736 | tf_op jit(solution)/shard_map/ppermute | solution.py:33
  14.7 7.3 %collective-permute-start.8 = (bf16[96,128]{1,0:T(8,128)(2,1)S(1)}, bf16[96,128]{1,0:T(8,128)(2,1)S(1)}, u32[]{:S(2)}, u32[]{:S(2)}) collective-permute-start(bf16[96,128]{1,0:T(8,128)(2,1)S(1)} %get-tuple-element.46), channel_id=1, source_target_pairs={{0,2},{1,3},{4,6},{5,7},{8,10},{9,11},{12,14},{13,15},{16,18},{17,... | collective-permute-start | bytes 73736 | tf_op jit(solution)/shard_map/ppermute | solution.py:33
  19.2 2.8 %collective-permute-start.9 = (bf16[96,128]{1,0:T(8,128)(2,1)S(1)}, bf16[96,128]{1,0:T(8,128)(2,1)S(1)}, u32[]{:S(2)}, u32[]{:S(2)}) collective-permute-start(bf16[96,128]{1,0:T(8,128)(2,1)S(1)} %get-tuple-element.47), channel_id=1, source_target_pairs={{0,3},{1,2},{4,7},{5,6},{8,11},{9,10},{12,15},{13,14},{16,19},{17,... | collective-permute-start | bytes 73736 | tf_op jit(solution)/shard_map/ppermute | solution.py:33
  20.5 1.5 %collective-permute-start.10 = (bf16[96,128]{1,0:T(8,128)(2,1)S(1)}, bf16[96,128]{1,0:T(8,128)(2,1)S(1)}, u32[]{:S(2)}, u32[]{:S(2)}) collective-permute-start(bf16[96,128]{1,0:T(8,128)(2,1)S(1)} %get-tuple-element.48), channel_id=1, source_target_pairs={{0,1},{1,0},{2,3},{3,2},{4,5},{5,4},{6,7},{7,6},{8,9},{9,8},{10,11... | collective-permute-start | bytes 73736 | tf_op jit(solution)/shard_map/ppermute | solution.py:27
  20.7 1.3 %copy-start.7 = (f32[128]{0:T(128)S(1)}, f32[128]{0:T(128)}, u32[]{:S(2)}) copy-start(f32[128]{0:T(128)} %param.14) | copy-start | bytes 1540

commit v20 on v17

--- a/solution.py
+++ b/solution.py
@@ -384,7 +384,12 @@
 def finish_kernel(step_count, row_count, head_count, shards, *refs):
     gain_ref, base_ref, grouped_ref, total_ref, peak_ref, sum_ref, cosine_ref, sine_ref = refs[:8]
     packet_refs = refs[8 : 8 + shards][::-1]
-    visible_ref, attention_ref, keys_ref, values_ref, up_buf = refs[8 + shards :]
+    visible_ref, attention_hbm, keys_hbm, values_hbm = refs[8 + shards : 12 + shards]
+    up_buf, attention_ref, keys_ref, values_ref, new_sems, sems = refs[12 + shards :]
+    written = [
+        pltpu.make_async_copy(keys_ref, keys_hbm, new_sems.at[0]),
+        pltpu.make_async_copy(values_ref, values_hbm, new_sems.at[1]),
+    ]
     shard = lax.axis_index("tensor")
     rows = step_count * row_count
     own = base_ref.shape[1]
@@ -416,7 +421,7 @@
 
     all_rows = row_count * seen
     heads = [(h, slice(h * all_rows, (h + 1) * all_rows)) for h in range(head_count)]
-    keys, values, scores, results = [], [], [], []
+    keys, values, scores = [], [], []
     for h, _ in heads:
         raw_key = joined[2 * h]
         mean_square = jnp.mean(raw_key * raw_key, axis=1, keepdims=True)
@@ -426,6 +431,8 @@
         values.append(joined[2 * h + 1].astype(bf16))
         keys_ref[:, h * lanes : (h + 1) * lanes] = keys[h]
         values_ref[:, h * lanes : (h + 1) * lanes] = values[h]
+    for copy in written:
+        copy.start()
     for h, mine in heads:
         score = lax.dot_general(
             grouped_ref[mine, :], keys[h], (((1,), (1,)), ((), ())), preferred_element_type=f32
@@ -440,17 +447,30 @@
         total = fade * total_ref[mine, :] + jnp.dot(
             lifted.astype(bf16), values[h], preferred_element_type=f32
         )
-        results.append(total / denominator)
-    for pair in range(step_count // 2):
-        for q in range(head_count * group):
-            h, g = q // group, q % group
-            both = []
-            for side in range(2):
-                first = ((pair * 2 + side) * group + g) * row_count
-                both.append(results[h][first : first + row_count])
-            attention_ref[
-                pair * 2 * row_count : (pair + 1) * 2 * row_count, q * lanes : (q + 1) * lanes
-            ] = jnp.concatenate(both, axis=0).astype(bf16)
+        result = total / denominator
+        for pair in range(step_count // 2):
+            window = slice(pair * 2 * row_count, (pair + 1) * 2 * row_count)
+            for g in range(group):
+                both = []
+                for side in range(2):
+                    first = ((pair * 2 + side) * group + g) * row_count
+                    both.append(result[first : first + row_count])
+                q = h * group + g
+                attention_ref[window, q * lanes : (q + 1) * lanes] = jnp.concatenate(
+                    both, axis=0
+                ).astype(bf16)
+            part = attention_ref.shape[1] // (2 * head_count)
+            for half in range(2):
+                columns = slice((2 * h + half) * part, (2 * h + half + 1) * part)
+                copy = pltpu.make_async_copy(
+                    attention_ref.at[window, columns],
+                    attention_hbm.at[window, columns],
+                    sems.at[(h * (step_count // 2) + pair) * 2 + half],
+                )
+                copy.start()
+                written.append(copy)
+    for copy in written:
+        copy.wait()
 
 
 def finish(base, visible, partials, gain, packets, rank, step_count, row_count, query_width):
@@ -465,9 +485,14 @@
             jax.ShapeDtypeStruct((rows, head_count * lanes), bf16),
         ),
         in_specs=[whole_in_vmem] * (9 + shards),
-        out_specs=(whole_in_vmem,) * 3,
+        out_specs=(stays_in_hbm,) * 3,
         scratch_shapes=[
             pltpu.VMEM((rank, own), bf16 if rank // shards % 16 == 0 else f32),
+            pltpu.VMEM((rows, query_width), bf16),
+            pltpu.VMEM((rows, head_count * lanes), bf16),
+            pltpu.VMEM((rows, head_count * lanes), bf16),
+            pltpu.SemaphoreType.DMA((2,)),
+            pltpu.SemaphoreType.DMA((2 * head_count * (step_count // 2),)),
         ],
         compiler_params=pltpu.CompilerParams(vmem_limit_bytes=6 * 2**20),
         name="finish",

time: 18.4 us -> 18.4 us (level)
  no operation moved by 1% of the time
where the time goes in v20:
time: 18.4 us; the launch traced here: 18.3 us
  starting transfers between devices  9.43 us (51%)
  Pallas kernels  4.87 us (26%)
  waiting for transfers between devices  2.44 us (13%)
  local copies, waits for them, and re-layouts  0.81 us (4%)
  between operations  0.72 us (4%)
    ppermute x9, starting transfers between devices, swap(): return lax.ppermute(block, axis, [(s, s ^ offset) for s in range(count)])  9.43 us
    ppermute x9, waiting for transfers between devices, swap(): return lax.ppermute(block, axis, [(s, s ^ offset) for s in range(count)])  2.44 us
    pallas_call x1, Pallas kernels, project(): pl.pallas_call(functools.partial(project_kernel, step_count, row_count, h...  1.77 us
    pallas_call x1, Pallas kernels, finish(): pl.pallas_call(functools.partial(finish_kernel, step_count, row_count, he...  1.49 us
    pallas_call x1, Pallas kernels, attend(): pl.pallas_call(functools.partial(attend_kernel, width // lanes), out_shap...  1.22 us
    unnamed x16, local copies, waits for them, and re-layouts  0.81 us
  transfers between devices with their start and end apart: 9, of which 4 were waited for; matrix products, arithmetic and copies ran while one was open for 0% of the time, Pallas kernels for 18%

profile of v20, /device:TPU:0, one launch (start us, length us, event | category | flops | bytes accessed | tf_op | source)
XLA Modules:
  0.0 18.3 jit_solution(3673582237571700543)
XLA Ops:
  0.6 0.0 copy-start.5
  0.6 0.0 copy-start.6
  0.7 0.0 copy-start.3
  0.7 0.0 copy-start.4
  0.7 0.0 copy-start
  0.7 0.8 %copy-done.5 = bf16[64,512]{1,0:T(8,128)(2,1)S(1)} copy-done((bf16[64,512]{1,0:T(8,128)(2,1)S(1)}, bf16[64,512]{1,0:T(8,128)(2,1)}, u32[]{:S(2)}) %copy-start.5) | copy-done | bytes 65560
  1.5 0.0 copy-done.6
  1.5 0.1 pack.1.refs_6_.refs_2_
  1.6 4.0 %collective-permute-start.2 = (bf16[224,128]{1,0:T(8,128)(2,1)S(1)}, bf16[224,128]{1,0:T(8,128)(2,1)S(1)}, u32[]{:S(2)}, u32[]{:S(2)}) collective-permute-start(bf16[224,128]{1,0:T(8,128)(2,1)S(1)} %pack.1.refs_6_.refs_2_), channel_id=1, source_target_pairs={{0,8},{4,12},{8,0},{12,4},{1,9},{5,13},{9,1},{13,5},{2,10},{6,14},... | collective-permute-start | bytes 172040 | tf_op jit(solution)/shard_map/ppermute | solution.py:27
  5.6 1.3 %collective-permute-start.1 = (bf16[224,128]{1,0:T(8,128)(2,1)S(1)}, bf16[224,128]{1,0:T(8,128)(2,1)S(1)}, u32[]{:S(2)}, u32[]{:S(2)}) collective-permute-start(bf16[224,128]{1,0:T(8,128)(2,1)S(1)} %pack.1.refs_6_.refs_2_), channel_id=1, source_target_pairs={{0,12},{4,8},{8,4},{12,0},{1,13},{5,9},{9,5},{13,1},{2,14},{6,10},... | collective-permute-start | bytes 172040 | tf_op jit(solution)/shard_map/ppermute | solution.py:27
  6.9 0.2 %collective-permute-start = (bf16[224,128]{1,0:T(8,128)(2,1)S(1)}, bf16[224,128]{1,0:T(8,128)(2,1)S(1)}, u32[]{:S(2)}, u32[]{:S(2)}) collective-permute-start(bf16[224,128]{1,0:T(8,128)(2,1)S(1)} %pack.1.refs_6_.refs_2_), channel_id=1, source_target_pairs={{0,4},{4,0},{8,12},{12,8},{1,5},{5,1},{9,13},{13,9},{2,6},{6,2},{1... | collective-permute-start | bytes 172040 | tf_op jit(solution)/shard_map/ppermute | solution.py:27
  7.2 0.0 copy-done.3
  7.2 0.0 copy-done.4
  7.2 0.0 copy-done
  7.2 0.0 copy-start.1
  7.2 0.0 copy-start.2
  7.2 1.8 %project.1 = (f32[32,512]{1,0:T(8,128)S(1)}, bf16[32,512]{1,0:T(8,128)(2,1)S(1)}, bf16[32,512]{1,0:T(8,128)(2,1)S(1)}, bf16[32,512]{1,0:T(8,128)(2,1)S(1)}, bf16...) custom-call(s32[4]{0:T(128)} %refs_0_.1, ...), custom_call_target="tpu_custom_call" | custom-call | flops 167772160 | bytes 5242880 | tf_op jit(solution)/shard_map/project/pallas_call | solution.py:196
  9.0 0.1 collective-permute-start.3
  9.1 1.6 %collective-permute-start.4 = (bf16[32,512]{1,0:T(8,128)(2,1)S(1)}, bf16[32,512]{1,0:T(8,128)(2,1)S(1)}, u32[]{:S(2)}, u32[]{:S(2)}) collective-permute-start(bf16[32,512]{1,0:T(8,128)(2,1)S(1)} %get-tuple-element.33), channel_id=1, source_target_pairs={{0,2},{1,3},{2,0},{3,1},{4,6},{5,7},{6,4},{7,5},{8,10},{9,11},{10,... | collective-permute-start | bytes 98312 | tf_op jit(solution)/shard_map/ppermute | solution.py:27
  10.6 0.0 collective-permute-done.2.refs_5_
  10.6 0.3 %collective-permute-start.5 = (bf16[32,512]{1,0:T(8,128)(2,1)S(1)}, bf16[32,512]{1,0:T(8,128)(2,1)S(1)}, u32[]{:S(2)}, u32[]{:S(2)}) collective-permute-start(bf16[32,512]{1,0:T(8,128)(2,1)S(1)} %get-tuple-element.34), channel_id=1, source_target_pairs={{0,3},{1,2},{2,1},{3,0},{4,7},{5,6},{6,5},{7,4},{8,11},{9,10},{10,... | collective-permute-start | bytes 98312 | tf_op jit(solution)/shard_map/ppermute | solution.py:27
  10.9 0.8 %collective-permute-done.1.refs_4_ = bf16[224,128]{1,0:T(8,128)(2,1)S(1)} collective-permute-done((bf16[224,128]{1,0:T(8,128)(2,1)S(1)}, bf16[224,128]{1,0:T(8,128)(2,1)S(1)}, u32[]{:S(2)}, u32[]{:S(2)}) %collective-permute-start.1) | collective-permute-done | bytes 57376 | tf_op jit(solution)/shard_map/ppermute | solution.py:27
  11.7 0.1 collective-permute-done.refs_3_
  11.7 0.3 %route.1 = (bf16[96,128]{1,0:T(8,128)(2,1)S(1)}, bf16[96,128]{1,0:T(8,128)(2,1)S(1)}, bf16[96,128]{1,0:T(8,128)(2,1)S(1)}, bf16[96,128]{1,0:T(8,128)(2,1)S(1)}) custom-call(bf16[32,1536]{1,0:T(8,128)(2,1)S(1)} %get-tuple-element.28.refs_0_, f32[16,128]{1,0:T(8,128)S(1)} %get-tuple-element.29.refs_1_, bf16[224,128]{1,0:T(8,128)(2,1)S(1)} %pack.1.refs_6_.refs_2_, ...), custom_call_target="tpu_custom_call" | custom-call | bytes 800000 | tf_op jit(solution)/shard_map/route/pallas_call | solution.py:352
  12.0 0.6 %collective-permute-start.6 = (bf16[96,128]{1,0:T(8,128)(2,1)S(1)}, bf16[96,128]{1,0:T(8,128)(2,1)S(1)}, u32[]{:S(2)}, u32[]{:S(2)}) collective-permute-start(bf16[96,128]{1,0:T(8,128)(2,1)S(1)} %get-tuple-element.42), channel_id=1, source_target_pairs={{0,3},{1,2},{2,1},{3,0},{4,7},{5,6},{6,5},{7,4},{8,11},{9,10},{10,... | collective-permute-start | bytes 73736 | tf_op jit(solution)/shard_map/ppermute | solution.py:27
  12.7 0.9 %collective-permute-start.7 = (bf16[96,128]{1,0:T(8,128)(2,1)S(1)}, bf16[96,128]{1,0:T(8,128)(2,1)S(1)}, u32[]{:S(2)}, u32[]{:S(2)}) collective-permute-start(bf16[96,128]{1,0:T(8,128)(2,1)S(1)} %get-tuple-element.43), channel_id=1, source_target_pairs={{0,2},{1,3},{2,0},{3,1},{4,6},{5,7},{6,4},{7,5},{8,10},{9,11},{10,... | collective-permute-start | bytes 73736 | tf_op jit(solution)/shard_map/ppermute | solution.py:27
  13.6 0.0 collective-permute-done.3.refs_0_
  13.6 0.3 %collective-permute-start.8 = (bf16[96,128]{1,0:T(8,128)(2,1)S(1)}, bf16[96,128]{1,0:T(8,128)(2,1)S(1)}, u32[]{:S(2)}, u32[]{:S(2)}) collective-permute-start(bf16[96,128]{1,0:T(8,128)(2,1)S(1)} %get-tuple-element.44), channel_id=1, source_target_pairs={{0,1},{1,0},{2,3},{3,2},{4,5},{5,4},{6,7},{7,6},{8,9},{9,8},{10,11... | collective-permute-start | bytes 73736 | tf_op jit(solution)/shard_map/ppermute | solution.py:27
  13.9 0.0 collective-permute-done.4.refs_1_
  13.9 0.0 collective-permute-done.5.refs_2_
  14.0 0.0 copy-done.1
  14.0 0.0 copy-done.2
  14.0 0.0 copy-start.7
  14.0 1.2 %attend.1 = (f32[32,512]{1,0:T(8,128)S(1)}, f32[512,128]{1,0:T(8,128)S(1)}, f32[512,128]{1,0:T(8,128)S(1)}, f32[512,128]{1,0:T(8,128)S(1)}) custom-call(bf16[512,128]{1,0:T(8,128)(2,1)S(1)} %get-tuple-element.26.asked_ref, bf16[8,512,256]{2,1,0:T(8,128)(2,1)S(1)} %copy-done.1, bf16[8,512,256]{2,1,0:T(8,128)(2,1)S(1)} %copy-done.2, ...), custom_call_target="tpu_custom_call" | custom-call | flops 134217728 | bytes 4194304 | tf_op jit(solution)/shard_map/attend/pallas_call | solution.py:289
  15.2 0.3 %collective-permute-done.6.refs_8_ = bf16[96,128]{1,0:T(8,128)(2,1)S(1)} collective-permute-done((bf16[96,128]{1,0:T(8,128)(2,1)S(1)}, bf16[96,128]{1,0:T(8,128)(2,1)S(1)}, u32[]{:S(2)}, u32[]{:S(2)}) %collective-permute-start.6) | collective-permute-done | bytes 24608 | tf_op jit(solution)/shard_map/ppermute | solution.py:27
  15.5 1.3 %collective-permute-done.7.refs_9_ = bf16[96,128]{1,0:T(8,128)(2,1)S(1)} collective-permute-done((bf16[96,128]{1,0:T(8,128)(2,1)S(1)}, bf16[96,128]{1,0:T(8,128)(2,1)S(1)}, u32[]{:S(2)}, u32[]{:S(2)}) %collective-permute-start.7) | collective-permute-done | bytes 24608 | tf_op jit(solution)/shard_map/ppermute | solution.py:27
  16.8 0.0 collective-permute-done.8.refs_10_
  16.8 0.0 copy-done.7
  16.8 1.5 %finish.1 = (bf16[32,2048]{1,0:T(8,128)(2,1)}, bf16[32,256]{1,0:T(8,128)(2,1)}, bf16[32,256]{1,0:T(8,128)(2,1)}) custom-call(f32[1,128]{1,0:T(1,128)S(1)} %bitcast.10, f32[32,512]{1,0:T(8,128)S(1)} %get-tuple-element.35.refs_1_, bf16[512,128]{1,0:T(8,128)(2,1)S(1)} %get-tuple-element.36.refs_2_, f32[512,128]{1,0:T(8,128)S(1)} %get-tuple-element.37.refs_3_, ...), custom_call_target="tpu_custom_call" | custom-call | bytes 1000000 | tf_op jit(solution)/shard_map/finish/pallas_call | solution.py:480
  (1 shorter events, 0.0 us)
Async XLA Ops:
  0.6 0.8 %copy-start.5 = (bf16[64,512]{1,0:T(8,128)(2,1)S(1)}, bf16[64,512]{1,0:T(8,128)(2,1)}, u32[]{:S(2)}) copy-start(bf16[64,512]{1,0:T(8,128)(2,1)} %up_all_ref.1) | copy-start | bytes 196612
  0.6 0.8 %copy-start.6 = (bf16[320,64]{0,1:T(8,128)(2,1)S(1)}, bf16[320,64]{0,1:T(8,128)(2,1)}, u32[]{:S(2)}) copy-start(bf16[320,64]{0,1:T(8,128)(2,1)} %param.12) | copy-start | bytes 122884
  0.7 6.5 %copy-start.3 = (bf16[4,8,2048]{2,1,0:T(8,128)(2,1)S(1)}, bf16[4,8,2048]{2,1,0:T(8,128)(2,1)}, u32[]{:S(2)}) copy-start(bf16[4,8,2048]{2,1,0:T(8,128)(2,1)} %param.15) | copy-start | bytes 393220
  0.7 6.5 %copy-start.4 = (bf16[4,8,1280]{2,1,0:T(8,128)(2,1)S(1)}, bf16[4,8,1280]{2,1,0:T(8,128)(2,1)}, u32[]{:S(2)}) copy-start(bf16[4,8,1280]{2,1,0:T(8,128)(2,1)} %param.10) | copy-start | bytes 245764
  0.7 6.5 %copy-start = (bf16[1280,2048]{1,0:T(8,128)(2,1)S(1)}, bf16[1280,2048]{1,0:T(8,128)(2,1)}, u32[]{:S(2)}) copy-start(bf16[1280,2048]{1,0:T(8,128)(2,1)} %refs_3_.1) | copy-start | bytes 15728644
  1.6 9.1 %collective-permute-start.2 = (bf16[224,128]{1,0:T(8,128)(2,1)S(1)}, bf16[224,128]{1,0:T(8,128)(2,1)S(1)}, u32[]{:S(2)}, u32[]{:S(2)}) collective-permute-start(bf16[224,128]{1,0:T(8,128)(2,1)S(1)} %pack.1.refs_6_.refs_2_), channel_id=1, source_target_pairs={{0,8},{4,12},{8,0},{12,4},{1,9},{5,13},{9,1},{13,5},{2,10},{6,14},... | collective-permute-start | bytes 172040 | tf_op jit(solution)/shard_map/ppermute | solution.py:27
  5.6 6.1 %collective-permute-start.1 = (bf16[224,128]{1,0:T(8,128)(2,1)S(1)}, bf16[224,128]{1,0:T(8,128)(2,1)S(1)}, u32[]{:S(2)}, u32[]{:S(2)}) collective-permute-start(bf16[224,128]{1,0:T(8,128)(2,1)S(1)} %pack.1.refs_6_.refs_2_), channel_id=1, source_target_pairs={{0,12},{4,8},{8,4},{12,0},{1,13},{5,9},{9,5},{13,1},{2,14},{6,10},... | collective-permute-start | bytes 172040 | tf_op jit(solution)/shard_map/ppermute | solution.py:27
  6.9 4.8 %collective-permute-start = (bf16[224,128]{1,0:T(8,128)(2,1)S(1)}, bf16[224,128]{1,0:T(8,128)(2,1)S(1)}, u32[]{:S(2)}, u32[]{:S(2)}) collective-permute-start(bf16[224,128]{1,0:T(8,128)(2,1)S(1)} %pack.1.refs_6_.refs_2_), channel_id=1, source_target_pairs={{0,4},{4,0},{8,12},{12,8},{1,5},{5,1},{9,13},{13,9},{2,6},{6,2},{1... | collective-permute-start | bytes 172040 | tf_op jit(solution)/shard_map/ppermute | solution.py:27
  7.2 6.8 %copy-start.1 = (bf16[8,512,256]{2,1,0:T(8,128)(2,1)S(1)}, bf16[8,512,256]{2,1,0:T(8,128)(2,1)}, u32[]{:S(2)}) copy-start(bf16[8,512,256]{2,1,0:T(8,128)(2,1)} %keys_ref.1) | copy-start | bytes 6291460
  7.2 6.8 %copy-start.2 = (bf16[8,512,256]{2,1,0:T(8,128)(2,1)S(1)}, bf16[8,512,256]{2,1,0:T(8,128)(2,1)}, u32[]{:S(2)}) copy-start(bf16[8,512,256]{2,1,0:T(8,128)(2,1)} %values_ref.1) | copy-start | bytes 6291460
  9.0 4.6 %collective-permute-start.3 = (bf16[32,512]{1,0:T(8,128)(2,1)S(1)}, bf16[32,512]{1,0:T(8,128)(2,1)S(1)}, u32[]{:S(2)}, u32[]{:S(2)}) collective-permute-start(bf16[32,512]{1,0:T(8,128)(2,1)S(1)} %get-tuple-element.32), channel_id=1, source_target_pairs={{0,1},{1,0},{2,3},{3,2},{4,5},{5,4},{6,7},{7,6},{8,9},{9,8},{10,11... | collective-permute-start | bytes 98312 | tf_op jit(solution)/shard_map/ppermute | solution.py:27
  9.1 4.9 %collective-permute-start.4 = (bf16[32,512]{1,0:T(8,128)(2,1)S(1)}, bf16[32,512]{1,0:T(8,128)(2,1)S(1)}, u32[]{:S(2)}, u32[]{:S(2)}) collective-permute-start(bf16[32,512]{1,0:T(8,128)(2,1)S(1)} %get-tuple-element.33), channel_id=1, source_target_pairs={{0,2},{1,3},{2,0},{3,1},{4,6},{5,7},{6,4},{7,5},{8,10},{9,11},{10,... | collective-permute-start | bytes 98312 | tf_op jit(solution)/shard_map/ppermute | solution.py:27
  10.6 3.3 %collective-permute-start.5 = (bf16[32,512]{1,0:T(8,128)(2,1)S(1)}, bf16[32,512]{1,0:T(8,128)(2,1)S(1)}, u32[]{:S(2)}, u32[]{:S(2)}) collective-permute-start(bf16[32,512]{1,0:T(8,128)(2,1)S(1)} %get-tuple-element.34), channel_id=1, source_target_pairs={{0,3},{1,2},{2,1},{3,0},{4,7},{5,6},{6,5},{7,4},{8,11},{9,10},{10,... | collective-permute-start | bytes 98312 | tf_op jit(solution)/shard_map/ppermute | solution.py:27
  12.0 3.5 %collective-permute-start.6 = (bf16[96,128]{1,0:T(8,128)(2,1)S(1)}, bf16[96,128]{1,0:T(8,128)(2,1)S(1)}, u32[]{:S(2)}, u32[]{:S(2)}) collective-permute-start(bf16[96,128]{1,0:T(8,128)(2,1)S(1)} %get-tuple-element.42), channel_id=1, source_target_pairs={{0,3},{1,2},{2,1},{3,0},{4,7},{5,6},{6,5},{7,4},{8,11},{9,10},{10,... | collective-permute-start | bytes 73736 | tf_op jit(solution)/shard_map/ppermute | solution.py:27
  12.7 4.1 %collective-permute-start.7 = (bf16[96,128]{1,0:T(8,128)(2,1)S(1)}, bf16[96,128]{1,0:T(8,128)(2,1)S(1)}, u32[]{:S(2)}, u32[]{:S(2)}) collective-permute-start(bf16[96,128]{1,0:T(8,128)(2,1)S(1)} %get-tuple-element.43), channel_id=1, source_target_pairs={{0,2},{1,3},{2,0},{3,1},{4,6},{5,7},{6,4},{7,5},{8,10},{9,11},{10,... | collective-permute-start | bytes 73736 | tf_op jit(solution)/shard_map/ppermute | solution.py:27
  13.6 3.1 %collective-permute-start.8 = (bf16[96,128]{1,0:T(8,128)(2,1)S(1)}, bf16[96,128]{1,0:T(8,128)(2,1)S(1)}, u32[]{:S(2)}, u32[]{:S(2)}) collective-permute-start(bf16[96,128]{1,0:T(8,128)(2,1)S(1)} %get-tuple-element.44), channel_id=1, source_target_pairs={{0,1},{1,0},{2,3},{3,2},{4,5},{5,4},{6,7},{7,6},{8,9},{9,8},{10,11... | collective-permute-start | bytes 73736 | tf_op jit(solution)/shard_map/ppermute | solution.py:27
  14.0 2.8 %copy-start.7 = (f32[128]{0:T(128)S(1)}, f32[128]{0:T(128)}, u32[]{:S(2)}) copy-start(f32[128]{0:T(128)} %param.14) | copy-start | bytes 1540

commit v21 on v16

--- a/solution.py
+++ b/solution.py
@@ -91,14 +91,12 @@
     )(down, up, after)
 
 
-def project_kernel(step_count, row_count, head_count, shards, replicas, *refs):
-    owners_hbm, lengths_hbm, tokens_ref, weight_ref, queries_ref, turns_ref, _ = refs[:7]
-    own_ref = refs[7]
-    block_refs = refs[8 : 7 + shards]
-    left_ref, pick_ref, asked_ref, grouped_ref, cosine_ref, sine_ref, bias_ref = refs[
-        7 + shards : 14 + shards
-    ]
-    owners_ref, lengths_ref, token_buf, regroup, sems = refs[14 + shards :]
+def project_kernel(step_count, row_count, shards, replicas, *refs):
+    owners_hbm, lengths_hbm, tokens_ref, weight_ref, turns_ref, _ = refs[:6]
+    own_ref = refs[6]
+    block_refs = refs[7 : 6 + shards]
+    left_ref, pick_ref, cosine_ref, sine_ref, bias_ref = refs[6 + shards : 11 + shards]
+    owners_ref, lengths_ref, token_buf, sems = refs[11 + shards :]
     owners_copy = pltpu.make_async_copy(owners_hbm, owners_ref, sems.at[0])
     lengths_copy = pltpu.make_async_copy(lengths_hbm, lengths_ref, sems.at[1])
     owners_copy.start()
@@ -116,6 +114,97 @@
         else:
             block_refs[i - 1][...] = block.astype(bf16)
 
+    owners_copy.wait()
+    replica = lax.axis_index("rollout")
+    width = token_buf.shape[2]
+    down_rows = tokens_ref.shape[1] // replicas
+    for k in range(replicas):
+        token_buf[k, :, :down_rows] = tokens_ref[:, k * down_rows : (k + 1) * down_rows]
+        if down_rows < width:
+            token_buf[k, :, down_rows:] = jnp.zeros((rows, width - down_rows), bf16)
+    for i in range(replicas):
+        place = jnp.int32(0)
+        for k in range(1, replicas):
+            place = place + jnp.where(owners_ref[k] == replica ^ i, k, 0)
+        left_ref[:, i * width : (i + 1) * width] = token_buf[place]
+    if replicas > 1:
+        for i in range(shards):
+            for k in range(replicas):
+                picked = jnp.where(owners_ref[shard ^ i] == replica ^ k, 1.0, 0.0)
+                row = i * replicas + k
+                pick_ref[row : row + 1, :] = jnp.full((1, lanes), picked, f32)
+
+    lengths_copy.wait()
+    row = lax.broadcasted_iota(jnp.int32, (rows, lanes), 0)
+    lane = lax.broadcasted_iota(jnp.int32, (rows, lanes), 1)
+    position = row // row_count
+    for b in range(row_count):
+        position = position + jnp.where(row % row_count == b, lengths_ref[b], 0)
+    angles = position.astype(f32) * turns_ref[:1, :]
+    cosine_ref[...] = jnp.cos(angles)
+    sine = jnp.sin(angles)
+    sine_ref[...] = jnp.where(lane < lanes // 2, -sine, sine)
+    slot = lax.broadcasted_iota(jnp.int32, bias_ref.shape, 1)
+    whose = lax.broadcasted_iota(jnp.int32, bias_ref.shape, 0)
+    length = jnp.zeros(bias_ref.shape, jnp.int32)
+    for b in range(row_count):
+        length = jnp.where(whose == b, lengths_ref[b], length)
+    bias_ref[...] = jnp.where(slot < length, 0.0, masked_score)
+
+
+def project(
+    owners, lengths, tokens, weight, turns, after, step_count, slots, shards, replicas
+):
+    rows, depth = tokens.shape
+    row_count = rows // step_count
+    own = weight.shape[1] // shards
+    piece_width = -(-depth // replicas // lanes) * lanes
+    table = jax.ShapeDtypeStruct((rows, lanes), f32)
+    mine, *rest = pl.pallas_call(
+        functools.partial(project_kernel, step_count, row_count, shards, replicas),
+        out_shape=[jax.ShapeDtypeStruct((rows, own), f32)]
+        + [jax.ShapeDtypeStruct((rows, own), bf16)] * (shards - 1)
+        + [
+            jax.ShapeDtypeStruct((rows, replicas * piece_width), bf16),
+            jax.ShapeDtypeStruct((shards * replicas, lanes), f32),
+            table,
+            table,
+            jax.ShapeDtypeStruct((row_count, slots), f32),
+        ],
+        in_specs=[stays_in_hbm] * 2 + [whole_in_vmem] * 4,
+        out_specs=[whole_in_vmem] * (shards + 5),
+        scratch_shapes=[
+            pltpu.SMEM(owners.shape, jnp.int32),
+            pltpu.SMEM(lengths.shape, jnp.int32),
+            pltpu.VMEM((replicas, rows, piece_width), bf16),
+            pltpu.SemaphoreType.DMA((2,)),
+        ],
+        compiler_params=pltpu.CompilerParams(vmem_limit_bytes=6 * 2**20),
+        name="project",
+        cost_estimate=pl.CostEstimate(
+            flops=2 * rows * weight.size, bytes_accessed=2 * weight.size, transcendentals=0
+        ),
+    )(*in_hbm(owners, lengths), tokens, weight, turns, after)
+    return mine, rest[: shards - 1], *rest[shards - 1 :]
+
+
+def attend_kernel(
+    step_count,
+    head_count,
+    queries_ref,
+    keys_ref,
+    values_ref,
+    bias_ref,
+    _,
+    grouped_ref,
+    total_ref,
+    peak_ref,
+    sum_ref,
+    regroup,
+    scores_ref,
+    raised,
+):
+    row_count, slots, _ = keys_ref.shape
     group = queries_ref.shape[1] // (head_count * lanes)
     seen = step_count * group
     for pair in range(step_count // 2):
@@ -137,107 +226,12 @@
                         [before[half], both[half]], axis=0
                     ).astype(bf16)
             before = both
-    asked_ref[...] = regroup[...].astype(bf16)
-
-    owners_copy.wait()
-    replica = lax.axis_index("rollout")
-    width = token_buf.shape[2]
-    down_rows = tokens_ref.shape[1] // replicas
-    for k in range(replicas):
-        token_buf[k, :, :down_rows] = tokens_ref[:, k * down_rows : (k + 1) * down_rows]
-        if down_rows < width:
-            token_buf[k, :, down_rows:] = jnp.zeros((rows, width - down_rows), bf16)
-    for i in range(replicas):
-        place = jnp.int32(0)
-        for k in range(1, replicas):
-            place = place + jnp.where(owners_ref[k] == replica ^ i, k, 0)
-        left_ref[:, i * width : (i + 1) * width] = token_buf[place]
-    if replicas > 1:
-        for i in range(shards):
-            for k in range(replicas):
-                picked = jnp.where(owners_ref[shard ^ i] == replica ^ k, 1.0, 0.0)
-                row = i * replicas + k
-                pick_ref[row : row + 1, :] = jnp.full((1, lanes), picked, f32)
-
-    lengths_copy.wait()
-    row = lax.broadcasted_iota(jnp.int32, (rows, lanes), 0)
-    lane = lax.broadcasted_iota(jnp.int32, (rows, lanes), 1)
-    position = row // row_count
-    for b in range(row_count):
-        position = position + jnp.where(row % row_count == b, lengths_ref[b], 0)
-    angles = position.astype(f32) * turns_ref[:1, :]
-    cosine_ref[...] = jnp.cos(angles)
-    sine = jnp.sin(angles)
-    sine_ref[...] = jnp.where(lane < lanes // 2, -sine, sine)
-    slot = lax.broadcasted_iota(jnp.int32, bias_ref.shape, 1)
-    whose = lax.broadcasted_iota(jnp.int32, bias_ref.shape, 0)
-    length = jnp.zeros(bias_ref.shape, jnp.int32)
-    for b in range(row_count):
-        length = jnp.where(whose == b, lengths_ref[b], length)
-    bias_ref[...] = jnp.where(slot < length, 0.0, masked_score)
-
-
-def project(
-    owners, lengths, tokens, weight, queries, turns, after, step_count, head_count, slots, shards, replicas
-):
-    rows, depth = tokens.shape
-    row_count = rows // step_count
-    own = weight.shape[1] // shards
-    piece_width = -(-depth // replicas // lanes) * lanes
-    seen_rows = rows * queries.shape[1] // lanes
-    table = jax.ShapeDtypeStruct((rows, lanes), f32)
-    mine, *rest = pl.pallas_call(
-        functools.partial(project_kernel, step_count, row_count, head_count, shards, replicas),
-        out_shape=[jax.ShapeDtypeStruct((rows, own), f32)]
-        + [jax.ShapeDtypeStruct((rows, own), bf16)] * (shards - 1)
-        + [
-            jax.ShapeDtypeStruct((rows, replicas * piece_width), bf16),
-            jax.ShapeDtypeStruct((shards * replicas, lanes), f32),
-            jax.ShapeDtypeStruct((seen_rows, lanes), bf16),
-            jax.ShapeDtypeStruct((seen_rows, lanes), bf16),
-            table,
-            table,
-            jax.ShapeDtypeStruct((row_count, slots), f32),
-        ],
-        in_specs=[stays_in_hbm] * 2 + [whole_in_vmem] * 5,
-        out_specs=[whole_in_vmem] * (shards + 7),
-        scratch_shapes=[
-            pltpu.SMEM(owners.shape, jnp.int32),
-            pltpu.SMEM(lengths.shape, jnp.int32),
-            pltpu.VMEM((replicas, rows, piece_width), bf16),
-            pltpu.VMEM((seen_rows, lanes), f32),
-            pltpu.SemaphoreType.DMA((2,)),
-        ],
-        compiler_params=pltpu.CompilerParams(vmem_limit_bytes=6 * 2**20),
-        name="project",
-        cost_estimate=pl.CostEstimate(
-            flops=2 * rows * weight.size, bytes_accessed=2 * weight.size, transcendentals=0
-        ),
-    )(*in_hbm(owners, lengths), tokens, weight, queries, turns, after)
-    return mine, rest[: shards - 1], *rest[shards - 1 :]
-
-
-def attend_kernel(
-    head_count,
-    asked_ref,
-    keys_ref,
-    values_ref,
-    bias_ref,
-    _,
-    total_ref,
-    peak_ref,
-    sum_ref,
-    scores_ref,
-    raised,
-):
-    row_count, slots, _ = keys_ref.shape
-    seen = asked_ref.shape[0] // (head_count * row_count)
 
     for b in range(row_count):
         for h in range(head_count):
             at = (h * row_count + b) * seen
             scores_ref[at : at + seen, :] = lax.dot_general(
-                asked_ref[at : at + seen, :],
+                regroup[at : at + seen, :].astype(bf16),
                 keys_ref[b, :, h * lanes : (h + 1) * lanes],
                 (((1,), (1,)), ((), ())),
                 preferred_element_type=f32,
@@ -270,16 +264,17 @@
         )
 
 
-def attend(asked, keys, values, bias, after):
+def attend(queries, keys, values, bias, after, step_count):
     row_count, slots, width = keys.shape
-    seen_rows = asked.shape[0]
+    seen_rows = step_count * row_count * queries.shape[1] // lanes
     seen_table = jax.ShapeDtypeStruct((seen_rows, lanes), f32)
     return pl.pallas_call(
-        functools.partial(attend_kernel, width // lanes),
-        out_shape=(seen_table,) * 3,
+        functools.partial(attend_kernel, step_count, width // lanes),
+        out_shape=(jax.ShapeDtypeStruct((seen_rows, lanes), bf16),) + (seen_table,) * 3,
         in_specs=[whole_in_vmem] * 5,
-        out_specs=(whole_in_vmem,) * 3,
+        out_specs=(whole_in_vmem,) * 4,
         scratch_shapes=[
+            pltpu.VMEM((seen_rows, lanes), f32),
             pltpu.VMEM((seen_rows, slots), f32),
             pltpu.VMEM((seen_rows, slots), bf16),
         ],
@@ -290,7 +285,7 @@
             bytes_accessed=2 * (keys.size + values.size),
             transcendentals=seen_rows * slots,
         ),
-    )(asked, keys, values, bias, after)
+    )(queries, keys, values, bias, after)
 
 
 def piece_places(replicas):
@@ -508,16 +503,14 @@
     if fits:
         packed = pack(adapter_down.T, adapter_up, rank_part, turns)
         pieces = [packed] + [swap(packed, "rollout", i) for i in range(1, replicas)]
-    mine, blocks, left, pick, asked, grouped, cosine, sine, bias = project(
+    mine, blocks, left, pick, cosine, sine, bias = project(
         owners,
         lengths,
         tokens,
         key_value_weight,
-        query_rows,
         turns,
         packed if fits else adapter_up,
         step_count,
-        cache_keys.shape[2] // lanes,
         cache_keys.shape[1],
         shards,
         replicas if fits else 1,
@@ -529,7 +522,9 @@
         packets = route_plain(
             owners, tokens, adapter_down, adapter_up, rank_part, own, shards
         )
-    total, peak, denominator = attend(asked, cache_keys, stored_values, bias, packets[0])
+    grouped, total, peak, denominator = attend(
+        query_rows, cache_keys, stored_values, bias, packets[0], step_count
+    )
     packets = [packets[0]] + [swap(packets[i], "tensor", i) for i in range(1, shards)]
     attention, keys, values = finish(
         mine,

time: 18.2 us -> 17.7 us (0.973)
  waiting for transfers between devices: 2.32 us -> 2.05 us
  Pallas kernels: 4.71 us -> 4.48 us
    ppermute x9, waiting for transfers between devices: 2.32 us -> 2.05 us  [swap(): return lax.ppermute(block, axis, [(s, s ^ offset) for s in range(count)])]
    pallas_call x2, Pallas kernels: 2.89 us -> 2.66 us  [the longest x1 1.33 us: attend(): pl.pallas_call(functools.partial(attend_kernel, step_count, width // lane...]
  transfers between devices with their start and end apart: 9 -> 9, of which waited for: 4 -> 4; matrix products, arithmetic and copies ran while one was open for 0% -> 0% of each run, Pallas kernels for 18% -> 17%
where the time goes in v21:
time: 17.7 us; the launch traced here: 17.5 us
  starting transfers between devices  9.43 us (53%)
  Pallas kernels  4.48 us (25%)
  waiting for transfers between devices  2.05 us (12%)
  local copies, waits for them, and re-layouts  0.82 us (5%)
  between operations  0.74 us (4%)
    ppermute x9, starting transfers between devices, swap(): return lax.ppermute(block, axis, [(s, s ^ offset) for s in range(count)])  9.43 us
    ppermute x9, waiting for transfers between devices, swap(): return lax.ppermute(block, axis, [(s, s ^ offset) for s in range(count)])  2.05 us
    pallas_call x1, Pallas kernels, finish(): pl.pallas_call(functools.partial(finish_kernel, step_count, row_count, he...  1.43 us
    pallas_call x1, Pallas kernels, attend(): pl.pallas_call(functools.partial(attend_kernel, step_count, width // lane...  1.33 us
    pallas_call x1, Pallas kernels, project(): pl.pallas_call(functools.partial(project_kernel, step_count, row_count, s...  1.33 us
    unnamed x16, local copies, waits for them, and re-layouts  0.82 us
  transfers between devices with their start and end apart: 9, of which 4 were waited for; matrix products, arithmetic and copies ran while one was open for 0% of the time, Pallas kernels for 17%

profile of v21, /device:TPU:0, one launch (start us, length us, event | category | flops | bytes accessed | tf_op | source)
XLA Modules:
  0.0 17.5 jit_solution(5561663945770064750)
XLA Ops:
  0.6 0.0 copy-start.5
  0.6 0.0 copy-start.6
  0.7 0.0 copy-start.4
  0.7 0.0 copy-start
  0.7 0.8 %copy-done.5 = bf16[64,512]{1,0:T(8,128)(2,1)S(1)} copy-done((bf16[64,512]{1,0:T(8,128)(2,1)S(1)}, bf16[64,512]{1,0:T(8,128)(2,1)}, u32[]{:S(2)}) %copy-start.5) | copy-done | bytes 65560
  1.5 0.0 copy-done.6
  1.5 0.1 pack.1.refs_5_.refs_2_
  1.6 4.0 %collective-permute-start.2 = (bf16[224,128]{1,0:T(8,128)(2,1)S(1)}, bf16[224,128]{1,0:T(8,128)(2,1)S(1)}, u32[]{:S(2)}, u32[]{:S(2)}) collective-permute-start(bf16[224,128]{1,0:T(8,128)(2,1)S(1)} %pack.1.refs_5_.refs_2_), channel_id=1, source_target_pairs={{0,8},{4,12},{8,0},{12,4},{1,9},{5,13},{9,1},{13,5},{2,10},{6,14},... | collective-permute-start | bytes 172040 | tf_op jit(solution)/shard_map/ppermute | solution.py:27
  5.6 1.3 %collective-permute-start.1 = (bf16[224,128]{1,0:T(8,128)(2,1)S(1)}, bf16[224,128]{1,0:T(8,128)(2,1)S(1)}, u32[]{:S(2)}, u32[]{:S(2)}) collective-permute-start(bf16[224,128]{1,0:T(8,128)(2,1)S(1)} %pack.1.refs_5_.refs_2_), channel_id=1, source_target_pairs={{0,12},{4,8},{8,4},{12,0},{1,13},{5,9},{9,5},{13,1},{2,14},{6,10},... | collective-permute-start | bytes 172040 | tf_op jit(solution)/shard_map/ppermute | solution.py:27
  6.9 0.2 %collective-permute-start = (bf16[224,128]{1,0:T(8,128)(2,1)S(1)}, bf16[224,128]{1,0:T(8,128)(2,1)S(1)}, u32[]{:S(2)}, u32[]{:S(2)}) collective-permute-start(bf16[224,128]{1,0:T(8,128)(2,1)S(1)} %pack.1.refs_5_.refs_2_), channel_id=1, source_target_pairs={{0,4},{4,0},{8,12},{12,8},{1,5},{5,1},{9,13},{13,9},{2,6},{6,2},{1... | collective-permute-start | bytes 172040 | tf_op jit(solution)/shard_map/ppermute | solution.py:27
  7.2 0.0 copy-done.4
  7.2 0.0 copy-done
  7.2 0.0 copy-start.1
  7.2 0.0 copy-start.2
  7.2 0.0 copy-start.3
  7.2 1.3 %project.1 = (f32[32,512]{1,0:T(8,128)S(1)}, bf16[32,512]{1,0:T(8,128)(2,1)S(1)}, bf16[32,512]{1,0:T(8,128)(2,1)S(1)}, bf16[32,512]{1,0:T(8,128)(2,1)S(1)}, bf16...) custom-call(s32[4]{0:T(128)} %refs_0_.1, ...), custom_call_target="tpu_custom_call" | custom-call | flops 167772160 | bytes 5242880 | tf_op jit(solution)/shard_map/project/pallas_call | solution.py:163
  8.5 0.1 collective-permute-start.6
  8.6 1.6 %collective-permute-start.7 = (bf16[32,512]{1,0:T(8,128)(2,1)S(1)}, bf16[32,512]{1,0:T(8,128)(2,1)S(1)}, u32[]{:S(2)}, u32[]{:S(2)}) collective-permute-start(bf16[32,512]{1,0:T(8,128)(2,1)S(1)} %get-tuple-element.38), channel_id=1, source_target_pairs={{0,2},{1,3},{2,0},{3,1},{4,6},{5,7},{6,4},{7,5},{8,10},{9,11},{10,... | collective-permute-start | bytes 98312 | tf_op jit(solution)/shard_map/ppermute | solution.py:27
  10.2 0.0 collective-permute-done.2.refs_5_
  10.2 0.3 %collective-permute-start.8 = (bf16[32,512]{1,0:T(8,128)(2,1)S(1)}, bf16[32,512]{1,0:T(8,128)(2,1)S(1)}, u32[]{:S(2)}, u32[]{:S(2)}) collective-permute-start(bf16[32,512]{1,0:T(8,128)(2,1)S(1)} %get-tuple-element.39), channel_id=1, source_target_pairs={{0,3},{1,2},{2,1},{3,0},{4,7},{5,6},{6,5},{7,4},{8,11},{9,10},{10,... | collective-permute-start | bytes 98312 | tf_op jit(solution)/shard_map/ppermute | solution.py:27
  10.5 1.2 %collective-permute-done.1.refs_4_ = bf16[224,128]{1,0:T(8,128)(2,1)S(1)} collective-permute-done((bf16[224,128]{1,0:T(8,128)(2,1)S(1)}, bf16[224,128]{1,0:T(8,128)(2,1)S(1)}, u32[]{:S(2)}, u32[]{:S(2)}) %collective-permute-start.1) | collective-permute-done | bytes 57376 | tf_op jit(solution)/shard_map/ppermute | solution.py:27
  11.7 0.1 collective-permute-done.refs_3_
  11.7 0.3 %route.1 = (bf16[96,128]{1,0:T(8,128)(2,1)S(1)}, bf16[96,128]{1,0:T(8,128)(2,1)S(1)}, bf16[96,128]{1,0:T(8,128)(2,1)S(1)}, bf16[96,128]{1,0:T(8,128)(2,1)S(1)}) custom-call(bf16[32,1536]{1,0:T(8,128)(2,1)S(1)} %get-tuple-element.25.refs_0_, f32[16,128]{1,0:T(8,128)S(1)} %get-tuple-element.26.refs_1_, bf16[224,128]{1,0:T(8,128)(2,1)S(1)} %pack.1.refs_5_.refs_2_, ...), custom_call_target="tpu_custom_call" | custom-call | bytes 800000 | tf_op jit(solution)/shard_map/route/pallas_call | solution.py:335
  12.0 0.2 %collective-permute-start.3 = (bf16[96,128]{1,0:T(8,128)(2,1)S(1)}, bf16[96,128]{1,0:T(8,128)(2,1)S(1)}, u32[]{:S(2)}, u32[]{:S(2)}) collective-permute-start(bf16[96,128]{1,0:T(8,128)(2,1)S(1)} %get-tuple-element.34), channel_id=1, source_target_pairs={{0,3},{1,2},{2,1},{3,0},{4,7},{5,6},{6,5},{7,4},{8,11},{9,10},{10,... | collective-permute-start | bytes 73736 | tf_op jit(solution)/shard_map/ppermute | solution.py:27
  12.2 1.4 %collective-permute-start.4 = (bf16[96,128]{1,0:T(8,128)(2,1)S(1)}, bf16[96,128]{1,0:T(8,128)(2,1)S(1)}, u32[]{:S(2)}, u32[]{:S(2)}) collective-permute-start(bf16[96,128]{1,0:T(8,128)(2,1)S(1)} %get-tuple-element.35), channel_id=1, source_target_pairs={{0,2},{1,3},{2,0},{3,1},{4,6},{5,7},{6,4},{7,5},{8,10},{9,11},{10,... | collective-permute-start | bytes 73736 | tf_op jit(solution)/shard_map/ppermute | solution.py:27
  13.6 0.0 collective-permute-done.6.refs_12_
  13.6 0.3 %collective-permute-start.5 = (bf16[96,128]{1,0:T(8,128)(2,1)S(1)}, bf16[96,128]{1,0:T(8,128)(2,1)S(1)}, u32[]{:S(2)}, u32[]{:S(2)}) collective-permute-start(bf16[96,128]{1,0:T(8,128)(2,1)S(1)} %get-tuple-element.36), channel_id=1, source_target_pairs={{0,1},{1,0},{2,3},{3,2},{4,5},{5,4},{6,7},{7,6},{8,9},{9,8},{10,11... | collective-permute-start | bytes 73736 | tf_op jit(solution)/shard_map/ppermute | solution.py:27
  13.9 0.0 copy-done.1
  13.9 0.0 copy-done.2
  13.9 0.0 copy-done.3
  13.9 0.0 copy-start.7
  13.9 1.3 %attend.1 = (bf16[512,128]{1,0:T(8,128)(2,1)S(1)}, f32[512,128]{1,0:T(8,128)S(1)}, f32[512,128]{1,0:T(8,128)S(1)}, f32[512,128]{1,0:T(8,128)S(1)}) custom-call(bf16[32,2048]{1,0:T(8,128)(2,1)S(1)} %bitcast.7, bf16[8,512,256]{2,1,0:T(8,128)(2,1)S(1)} %copy-done.1, bf16[8,512,256]{2,1,0:T(8,128)(2,1)S(1)} %copy-done.2, ...), custom_call_target="tpu_custom_call" | custom-call | flops 134217728 | bytes 4194304 | tf_op jit(solution)/shard_map/attend/pallas_call | solution.py:271
  15.3 0.0 collective-permute-done.7.refs_13_
  15.3 0.0 collective-permute-done.8.refs_14_
  15.3 0.2 %collective-permute-done.3.refs_8_ = bf16[96,128]{1,0:T(8,128)(2,1)S(1)} collective-permute-done((bf16[96,128]{1,0:T(8,128)(2,1)S(1)}, bf16[96,128]{1,0:T(8,128)(2,1)S(1)}, u32[]{:S(2)}, u32[]{:S(2)}) %collective-permute-start.3) | collective-permute-done | bytes 24608 | tf_op jit(solution)/shard_map/ppermute | solution.py:27
  15.5 0.6 %collective-permute-done.4.refs_9_ = bf16[96,128]{1,0:T(8,128)(2,1)S(1)} collective-permute-done((bf16[96,128]{1,0:T(8,128)(2,1)S(1)}, bf16[96,128]{1,0:T(8,128)(2,1)S(1)}, u32[]{:S(2)}, u32[]{:S(2)}) %collective-permute-start.4) | collective-permute-done | bytes 24608 | tf_op jit(solution)/shard_map/ppermute | solution.py:27
  16.1 0.0 collective-permute-done.5.refs_10_
  16.1 0.0 copy-done.7
  16.1 1.4 %finish.1 = (bf16[32,2048]{1,0:T(8,128)(2,1)}, bf16[32,256]{1,0:T(8,128)(2,1)}, bf16[32,256]{1,0:T(8,128)(2,1)}) custom-call(f32[1,128]{1,0:T(1,128)S(1)} %bitcast.10, f32[32,512]{1,0:T(8,128)S(1)} %get-tuple-element.23.refs_1_, bf16[512,128]{1,0:T(8,128)(2,1)S(1)} %get-tuple-element.28.refs_2_, f32[512,128]{1,0:T(8,128)S(1)} %get-tuple-element.29.refs_3_, ...), custom_call_target="tpu_custom_call" | custom-call | bytes 1000000 | tf_op jit(solution)/shard_map/finish/pallas_call | solution.py:452
  (1 shorter events, 0.0 us)
Async XLA Ops:
  0.6 0.8 %copy-start.5 = (bf16[64,512]{1,0:T(8,128)(2,1)S(1)}, bf16[64,512]{1,0:T(8,128)(2,1)}, u32[]{:S(2)}) copy-start(bf16[64,512]{1,0:T(8,128)(2,1)} %up_all_ref.1) | copy-start | bytes 196612
  0.6 0.8 %copy-start.6 = (bf16[320,64]{0,1:T(8,128)(2,1)S(1)}, bf16[320,64]{0,1:T(8,128)(2,1)}, u32[]{:S(2)}) copy-start(bf16[320,64]{0,1:T(8,128)(2,1)} %param.12) | copy-start | bytes 122884
  0.7 6.5 %copy-start.4 = (bf16[4,8,1280]{2,1,0:T(8,128)(2,1)S(1)}, bf16[4,8,1280]{2,1,0:T(8,128)(2,1)}, u32[]{:S(2)}) copy-start(bf16[4,8,1280]{2,1,0:T(8,128)(2,1)} %param.10) | copy-start | bytes 245764
  0.7 6.5 %copy-start = (bf16[1280,2048]{1,0:T(8,128)(2,1)S(1)}, bf16[1280,2048]{1,0:T(8,128)(2,1)}, u32[]{:S(2)}) copy-start(bf16[1280,2048]{1,0:T(8,128)(2,1)} %refs_3_.1) | copy-start | bytes 15728644
  1.6 8.6 %collective-permute-start.2 = (bf16[224,128]{1,0:T(8,128)(2,1)S(1)}, bf16[224,128]{1,0:T(8,128)(2,1)S(1)}, u32[]{:S(2)}, u32[]{:S(2)}) collective-permute-start(bf16[224,128]{1,0:T(8,128)(2,1)S(1)} %pack.1.refs_5_.refs_2_), channel_id=1, source_target_pairs={{0,8},{4,12},{8,0},{12,4},{1,9},{5,13},{9,1},{13,5},{2,10},{6,14},... | collective-permute-start | bytes 172040 | tf_op jit(solution)/shard_map/ppermute | solution.py:27
  5.6 6.1 %collective-permute-start.1 = (bf16[224,128]{1,0:T(8,128)(2,1)S(1)}, bf16[224,128]{1,0:T(8,128)(2,1)S(1)}, u32[]{:S(2)}, u32[]{:S(2)}) collective-permute-start(bf16[224,128]{1,0:T(8,128)(2,1)S(1)} %pack.1.refs_5_.refs_2_), channel_id=1, source_target_pairs={{0,12},{4,8},{8,4},{12,0},{1,13},{5,9},{9,5},{13,1},{2,14},{6,10},... | collective-permute-start | bytes 172040 | tf_op jit(solution)/shard_map/ppermute | solution.py:27
  6.9 4.8 %collective-permute-start = (bf16[224,128]{1,0:T(8,128)(2,1)S(1)}, bf16[224,128]{1,0:T(8,128)(2,1)S(1)}, u32[]{:S(2)}, u32[]{:S(2)}) collective-permute-start(bf16[224,128]{1,0:T(8,128)(2,1)S(1)} %pack.1.refs_5_.refs_2_), channel_id=1, source_target_pairs={{0,4},{4,0},{8,12},{12,8},{1,5},{5,1},{9,13},{13,9},{2,6},{6,2},{1... | collective-permute-start | bytes 172040 | tf_op jit(solution)/shard_map/ppermute | solution.py:27
  7.2 6.7 %copy-start.1 = (bf16[8,512,256]{2,1,0:T(8,128)(2,1)S(1)}, bf16[8,512,256]{2,1,0:T(8,128)(2,1)}, u32[]{:S(2)}) copy-start(bf16[8,512,256]{2,1,0:T(8,128)(2,1)} %keys_ref.1) | copy-start | bytes 6291460
  7.2 6.7 %copy-start.2 = (bf16[8,512,256]{2,1,0:T(8,128)(2,1)S(1)}, bf16[8,512,256]{2,1,0:T(8,128)(2,1)}, u32[]{:S(2)}) copy-start(bf16[8,512,256]{2,1,0:T(8,128)(2,1)} %values_ref.1) | copy-start | bytes 6291460
  7.2 6.7 %copy-start.3 = (bf16[4,8,2048]{2,1,0:T(8,128)(2,1)S(1)}, bf16[4,8,2048]{2,1,0:T(8,128)(2,1)}, u32[]{:S(2)}) copy-start(bf16[4,8,2048]{2,1,0:T(8,128)(2,1)} %param.15) | copy-start | bytes 393220
  8.5 5.1 %collective-permute-start.6 = (bf16[32,512]{1,0:T(8,128)(2,1)S(1)}, bf16[32,512]{1,0:T(8,128)(2,1)S(1)}, u32[]{:S(2)}, u32[]{:S(2)}) collective-permute-start(bf16[32,512]{1,0:T(8,128)(2,1)S(1)} %get-tuple-element.37), channel_id=1, source_target_pairs={{0,1},{1,0},{2,3},{3,2},{4,5},{5,4},{6,7},{7,6},{8,9},{9,8},{10,11... | collective-permute-start | bytes 98312 | tf_op jit(solution)/shard_map/ppermute | solution.py:27
  8.6 6.7 %collective-permute-start.7 = (bf16[32,512]{1,0:T(8,128)(2,1)S(1)}, bf16[32,512]{1,0:T(8,128)(2,1)S(1)}, u32[]{:S(2)}, u32[]{:S(2)}) collective-permute-start(bf16[32,512]{1,0:T(8,128)(2,1)S(1)} %get-tuple-element.38), channel_id=1, source_target_pairs={{0,2},{1,3},{2,0},{3,1},{4,6},{5,7},{6,4},{7,5},{8,10},{9,11},{10,... | collective-permute-start | bytes 98312 | tf_op jit(solution)/shard_map/ppermute | solution.py:27
  10.2 5.1 %collective-permute-start.8 = (bf16[32,512]{1,0:T(8,128)(2,1)S(1)}, bf16[32,512]{1,0:T(8,128)(2,1)S(1)}, u32[]{:S(2)}, u32[]{:S(2)}) collective-permute-start(bf16[32,512]{1,0:T(8,128)(2,1)S(1)} %get-tuple-element.39), channel_id=1, source_target_pairs={{0,3},{1,2},{2,1},{3,0},{4,7},{5,6},{6,5},{7,4},{8,11},{9,10},{10,... | collective-permute-start | bytes 98312 | tf_op jit(solution)/shard_map/ppermute | solution.py:27
  12.0 3.5 %collective-permute-start.3 = (bf16[96,128]{1,0:T(8,128)(2,1)S(1)}, bf16[96,128]{1,0:T(8,128)(2,1)S(1)}, u32[]{:S(2)}, u32[]{:S(2)}) collective-permute-start(bf16[96,128]{1,0:T(8,128)(2,1)S(1)} %get-tuple-element.34), channel_id=1, source_target_pairs={{0,3},{1,2},{2,1},{3,0},{4,7},{5,6},{6,5},{7,4},{8,11},{9,10},{10,... | collective-permute-start | bytes 73736 | tf_op jit(solution)/shard_map/ppermute | solution.py:27
  12.2 3.8 %collective-permute-start.4 = (bf16[96,128]{1,0:T(8,128)(2,1)S(1)}, bf16[96,128]{1,0:T(8,128)(2,1)S(1)}, u32[]{:S(2)}, u32[]{:S(2)}) collective-permute-start(bf16[96,128]{1,0:T(8,128)(2,1)S(1)} %get-tuple-element.35), channel_id=1, source_target_pairs={{0,2},{1,3},{2,0},{3,1},{4,6},{5,7},{6,4},{7,5},{8,10},{9,11},{10,... | collective-permute-start | bytes 73736 | tf_op jit(solution)/shard_map/ppermute | solution.py:27
  13.6 2.5 %collective-permute-start.5 = (bf16[96,128]{1,0:T(8,128)(2,1)S(1)}, bf16[96,128]{1,0:T(8,128)(2,1)S(1)}, u32[]{:S(2)}, u32[]{:S(2)}) collective-permute-start(bf16[96,128]{1,0:T(8,128)(2,1)S(1)} %get-tuple-element.36), channel_id=1, source_target_pairs={{0,1},{1,0},{2,3},{3,2},{4,5},{5,4},{6,7},{7,6},{8,9},{9,8},{10,11... | collective-permute-start | bytes 73736 | tf_op jit(solution)/shard_map/ppermute | solution.py:27
  13.9 2.2 %copy-start.7 = (f32[128]{0:T(128)S(1)}, f32[128]{0:T(128)}, u32[]{:S(2)}) copy-start(f32[128]{0:T(128)} %param.14) | copy-start | bytes 1540

commit v22 on v21

--- a/solution.py
+++ b/solution.py
@@ -91,28 +91,25 @@
     )(down, up, after)
 
 
+def product(tokens_ref, weight_ref, owner, own):
+    columns = pl.ds(pl.multiple_of(owner * own, lanes), own)
+    return jnp.dot(tokens_ref[...], weight_ref[:, columns], preferred_element_type=f32)
+
+
 def project_kernel(step_count, row_count, shards, replicas, *refs):
     owners_hbm, lengths_hbm, tokens_ref, weight_ref, turns_ref, _ = refs[:6]
-    own_ref = refs[6]
-    block_refs = refs[7 : 6 + shards]
-    left_ref, pick_ref, cosine_ref, sine_ref, bias_ref = refs[6 + shards : 11 + shards]
-    owners_ref, lengths_ref, token_buf, sems = refs[11 + shards :]
+    block_refs = refs[6 : 5 + shards]
+    left_ref, pick_ref, cosine_ref, sine_ref, bias_ref = refs[5 + shards : 10 + shards]
+    owners_ref, lengths_ref, token_buf, sems = refs[10 + shards :]
     owners_copy = pltpu.make_async_copy(owners_hbm, owners_ref, sems.at[0])
     lengths_copy = pltpu.make_async_copy(lengths_hbm, lengths_ref, sems.at[1])
     owners_copy.start()
     lengths_copy.start()
 
     shard = lax.axis_index("tensor")
-    rows, own = own_ref.shape
-    for i in range(shards):
-        first = pl.multiple_of((shard ^ i) * own, lanes)
-        block = jnp.dot(
-            tokens_ref[...], weight_ref[:, pl.ds(first, own)], preferred_element_type=f32
-        )
-        if i == 0:
-            own_ref[...] = block
-        else:
-            block_refs[i - 1][...] = block.astype(bf16)
+    rows, own = block_refs[0].shape
+    for i in reversed(range(1, shards)):
+        block_refs[i - 1][...] = product(tokens_ref, weight_ref, shard ^ i, own).astype(bf16)
 
     owners_copy.wait()
     replica = lax.axis_index("rollout")
@@ -160,10 +157,9 @@
     own = weight.shape[1] // shards
     piece_width = -(-depth // replicas // lanes) * lanes
     table = jax.ShapeDtypeStruct((rows, lanes), f32)
-    mine, *rest = pl.pallas_call(
+    outs = pl.pallas_call(
         functools.partial(project_kernel, step_count, row_count, shards, replicas),
-        out_shape=[jax.ShapeDtypeStruct((rows, own), f32)]
-        + [jax.ShapeDtypeStruct((rows, own), bf16)] * (shards - 1)
+        out_shape=[jax.ShapeDtypeStruct((rows, own), bf16)] * (shards - 1)
         + [
             jax.ShapeDtypeStruct((rows, replicas * piece_width), bf16),
             jax.ShapeDtypeStruct((shards * replicas, lanes), f32),
@@ -172,7 +168,7 @@
             jax.ShapeDtypeStruct((row_count, slots), f32),
         ],
         in_specs=[stays_in_hbm] * 2 + [whole_in_vmem] * 4,
-        out_specs=[whole_in_vmem] * (shards + 5),
+        out_specs=[whole_in_vmem] * (shards + 4),
         scratch_shapes=[
             pltpu.SMEM(owners.shape, jnp.int32),
             pltpu.SMEM(lengths.shape, jnp.int32),
@@ -185,7 +181,7 @@
             flops=2 * rows * weight.size, bytes_accessed=2 * weight.size, transcendentals=0
         ),
     )(*in_hbm(owners, lengths), tokens, weight, turns, after)
-    return mine, rest[: shards - 1], *rest[shards - 1 :]
+    return outs[: shards - 1], *outs[shards - 1 :]
 
 
 def attend_kernel(
@@ -196,6 +192,9 @@
     values_ref,
     bias_ref,
     _,
+    tokens_ref,
+    weight_ref,
+    own_ref,
     grouped_ref,
     total_ref,
     peak_ref,
@@ -204,6 +203,8 @@
     scores_ref,
     raised,
 ):
+    own_ref[...] = product(tokens_ref, weight_ref, lax.axis_index("tensor"), own_ref.shape[1])
+
     row_count, slots, _ = keys_ref.shape
     group = queries_ref.shape[1] // (head_count * lanes)
     seen = step_count * group
@@ -264,15 +265,21 @@
         )
 
 
-def attend(queries, keys, values, bias, after, step_count):
+def attend(queries, keys, values, bias, after, tokens, weight, own, step_count):
     row_count, slots, width = keys.shape
     seen_rows = step_count * row_count * queries.shape[1] // lanes
     seen_table = jax.ShapeDtypeStruct((seen_rows, lanes), f32)
     return pl.pallas_call(
         functools.partial(attend_kernel, step_count, width // lanes),
-        out_shape=(jax.ShapeDtypeStruct((seen_rows, lanes), bf16),) + (seen_table,) * 3,
-        in_specs=[whole_in_vmem] * 5,
-        out_specs=(whole_in_vmem,) * 4,
+        out_shape=(
+            jax.ShapeDtypeStruct((tokens.shape[0], own), f32),
+            jax.ShapeDtypeStruct((seen_rows, lanes), bf16),
+            seen_table,
+            seen_table,
+            seen_table,
+        ),
+        in_specs=[whole_in_vmem] * 7,
+        out_specs=(whole_in_vmem,) * 5,
         scratch_shapes=[
             pltpu.VMEM((seen_rows, lanes), f32),
             pltpu.VMEM((seen_rows, slots), f32),
@@ -285,7 +292,7 @@
             bytes_accessed=2 * (keys.size + values.size),
             transcendentals=seen_rows * slots,
         ),
-    )(queries, keys, values, bias, after)
+    )(queries, keys, values, bias, after, tokens, weight)
 
 
 def piece_places(replicas):
@@ -464,7 +471,7 @@
         compiler_params=pltpu.CompilerParams(vmem_limit_bytes=6 * 2**20),
         name="finish",
         cost_estimate=pl.CostEstimate(flops=0, bytes_accessed=1000000, transcendentals=0),
-    )(gain, mine, *partials, *packets[::-1], *others)
+    )(gain, mine, *partials, *packets[::-1], *others[::-1])
 
 
 def per_device(
@@ -503,7 +510,7 @@
     if fits:
         packed = pack(adapter_down.T, adapter_up, rank_part, turns)
         pieces = [packed] + [swap(packed, "rollout", i) for i in range(1, replicas)]
-    mine, blocks, left, pick, cosine, sine, bias = project(
+    blocks, left, pick, cosine, sine, bias = project(
         owners,
         lengths,
         tokens,
@@ -522,8 +529,16 @@
         packets = route_plain(
             owners, tokens, adapter_down, adapter_up, rank_part, own, shards
         )
-    grouped, total, peak, denominator = attend(
-        query_rows, cache_keys, stored_values, bias, packets[0], step_count
+    mine, grouped, total, peak, denominator = attend(
+        query_rows,
+        cache_keys,
+        stored_values,
+        bias,
+        packets[0],
+        tokens,
+        key_value_weight,
+        own,
+        step_count,
     )
     packets = [packets[0]] + [swap(packets[i], "tensor", i) for i in range(1, shards)]
     attention, keys, values = finish(

time: 17.7 us -> 17.6 us (level)
    pallas_call x1, Pallas kernels: 1.33 us -> 1.1 us  [project(): pl.pallas_call(functools.partial(project_kernel, step_count, row_count, s...]
    pallas_call x1, Pallas kernels: 1.33 us -> 1.55 us  [attend(): pl.pallas_call(functools.partial(attend_kernel, step_count, width // lane...]
  transfers between devices with their start and end apart: 9 -> 9, of which waited for: 4 -> 3; matrix products, arithmetic and copies ran while one was open for 0% -> 0% of each run, Pallas kernels for 17% -> 17%
where the time goes in v22:
time: 17.6 us; the launch traced here: 17.4 us
  starting transfers between devices  9.42 us (54%)
  Pallas kernels  4.47 us (25%)
  waiting for transfers between devices  1.96 us (11%)
  local copies, waits for them, and re-layouts  0.82 us (5%)
  between operations  0.73 us (4%)
    ppermute x9, starting transfers between devices, swap(): return lax.ppermute(block, axis, [(s, s ^ offset) for s in range(count)])  9.42 us
    ppermute x9, waiting for transfers between devices, swap(): return lax.ppermute(block, axis, [(s, s ^ offset) for s in range(count)])  1.96 us
    pallas_call x1, Pallas kernels, attend(): pl.pallas_call(functools.partial(attend_kernel, step_count, width // lane...  1.55 us
    pallas_call x1, Pallas kernels, finish(): pl.pallas_call(functools.partial(finish_kernel, step_count, row_count, he...  1.43 us
    pallas_call x1, Pallas kernels, project(): pl.pallas_call(functools.partial(project_kernel, step_count, row_count, s...  1.1 us
    unnamed x16, local copies, waits for them, and re-layouts  0.82 us
  transfers between devices with their start and end apart: 9, of which 3 were waited for; matrix products, arithmetic and copies ran while one was open for 0% of the time, Pallas kernels for 17%

profile of v22, /device:TPU:0, one launch (start us, length us, event | category | flops | bytes accessed | tf_op | source)
XLA Modules:
  0.0 17.4 jit_solution(10707531070561716504)
XLA Ops:
  0.6 0.0 copy-start.5
  0.6 0.0 copy-start.6
  0.7 0.0 copy-start.3
  0.7 0.0 copy-start
  0.7 0.8 %copy-done.5 = bf16[64,512]{1,0:T(8,128)(2,1)S(1)} copy-done((bf16[64,512]{1,0:T(8,128)(2,1)S(1)}, bf16[64,512]{1,0:T(8,128)(2,1)}, u32[]{:S(2)}) %copy-start.5) | copy-done | bytes 65560
  1.5 0.0 copy-done.6
  1.5 0.1 pack.1.refs_5_.refs_2_
  1.6 4.0 %collective-permute-start.2 = (bf16[224,128]{1,0:T(8,128)(2,1)S(1)}, bf16[224,128]{1,0:T(8,128)(2,1)S(1)}, u32[]{:S(2)}, u32[]{:S(2)}) collective-permute-start(bf16[224,128]{1,0:T(8,128)(2,1)S(1)} %pack.1.refs_5_.refs_2_), channel_id=1, source_target_pairs={{0,8},{4,12},{8,0},{12,4},{1,9},{5,13},{9,1},{13,5},{2,10},{6,14},... | collective-permute-start | bytes 172040 | tf_op jit(solution)/shard_map/ppermute | solution.py:27
  5.6 1.3 %collective-permute-start.1 = (bf16[224,128]{1,0:T(8,128)(2,1)S(1)}, bf16[224,128]{1,0:T(8,128)(2,1)S(1)}, u32[]{:S(2)}, u32[]{:S(2)}) collective-permute-start(bf16[224,128]{1,0:T(8,128)(2,1)S(1)} %pack.1.refs_5_.refs_2_), channel_id=1, source_target_pairs={{0,12},{4,8},{8,4},{12,0},{1,13},{5,9},{9,5},{13,1},{2,14},{6,10},... | collective-permute-start | bytes 172040 | tf_op jit(solution)/shard_map/ppermute | solution.py:27
  6.9 0.2 %collective-permute-start = (bf16[224,128]{1,0:T(8,128)(2,1)S(1)}, bf16[224,128]{1,0:T(8,128)(2,1)S(1)}, u32[]{:S(2)}, u32[]{:S(2)}) collective-permute-start(bf16[224,128]{1,0:T(8,128)(2,1)S(1)} %pack.1.refs_5_.refs_2_), channel_id=1, source_target_pairs={{0,4},{4,0},{8,12},{12,8},{1,5},{5,1},{9,13},{13,9},{2,6},{6,2},{1... | collective-permute-start | bytes 172040 | tf_op jit(solution)/shard_map/ppermute | solution.py:27
  7.2 0.0 copy-done.3
  7.2 0.0 copy-done
  7.2 0.0 copy-start.1
  7.2 0.0 copy-start.2
  7.2 0.0 copy-start.4
  7.2 1.1 %project.1 = (bf16[32,512]{1,0:T(8,128)(2,1)S(1)}, bf16[32,512]{1,0:T(8,128)(2,1)S(1)}, bf16[32,512]{1,0:T(8,128)(2,1)S(1)}, bf16[32,1536]{1,0:T(8,128)(2,1)S(1)...) custom-call(s32[4]{0:T(128)} %refs_0_.1, s32[8]{0:T(128)} %refs_1_.1, ...), custom_call_target="tpu_custom_call" | custom-call | flops 167772160 | bytes 5242880 | tf_op jit(solution)/shard_map/project/pallas_call | solution.py:160
  8.3 0.4 %collective-permute-start.6 = (bf16[32,512]{1,0:T(8,128)(2,1)S(1)}, bf16[32,512]{1,0:T(8,128)(2,1)S(1)}, u32[]{:S(2)}, u32[]{:S(2)}) collective-permute-start(bf16[32,512]{1,0:T(8,128)(2,1)S(1)} %get-tuple-element.37), channel_id=1, source_target_pairs={{0,3},{1,2},{2,1},{3,0},{4,7},{5,6},{6,5},{7,4},{8,11},{9,10},{10,... | collective-permute-start | bytes 98312 | tf_op jit(solution)/shard_map/ppermute | solution.py:27
  8.8 1.2 %collective-permute-start.7 = (bf16[32,512]{1,0:T(8,128)(2,1)S(1)}, bf16[32,512]{1,0:T(8,128)(2,1)S(1)}, u32[]{:S(2)}, u32[]{:S(2)}) collective-permute-start(bf16[32,512]{1,0:T(8,128)(2,1)S(1)} %get-tuple-element.38), channel_id=1, source_target_pairs={{0,2},{1,3},{2,0},{3,1},{4,6},{5,7},{6,4},{7,5},{8,10},{9,11},{10,... | collective-permute-start | bytes 98312 | tf_op jit(solution)/shard_map/ppermute | solution.py:27
  10.0 0.0 collective-permute-done.2.refs_5_
  10.0 0.3 %collective-permute-start.8 = (bf16[32,512]{1,0:T(8,128)(2,1)S(1)}, bf16[32,512]{1,0:T(8,128)(2,1)S(1)}, u32[]{:S(2)}, u32[]{:S(2)}) collective-permute-start(bf16[32,512]{1,0:T(8,128)(2,1)S(1)} %get-tuple-element.39), channel_id=1, source_target_pairs={{0,1},{1,0},{2,3},{3,2},{4,5},{5,4},{6,7},{7,6},{8,9},{9,8},{10,11... | collective-permute-start | bytes 98312 | tf_op jit(solution)/shard_map/ppermute | solution.py:27
  10.2 1.4 %collective-permute-done.1.refs_4_ = bf16[224,128]{1,0:T(8,128)(2,1)S(1)} collective-permute-done((bf16[224,128]{1,0:T(8,128)(2,1)S(1)}, bf16[224,128]{1,0:T(8,128)(2,1)S(1)}, u32[]{:S(2)}, u32[]{:S(2)}) %collective-permute-start.1) | collective-permute-done | bytes 57376 | tf_op jit(solution)/shard_map/ppermute | solution.py:27
  11.7 0.1 collective-permute-done.refs_3_
  11.7 0.3 %route.1 = (bf16[96,128]{1,0:T(8,128)(2,1)S(1)}, bf16[96,128]{1,0:T(8,128)(2,1)S(1)}, bf16[96,128]{1,0:T(8,128)(2,1)S(1)}, bf16[96,128]{1,0:T(8,128)(2,1)S(1)}) custom-call(bf16[32,1536]{1,0:T(8,128)(2,1)S(1)} %get-tuple-element.24.refs_0_, f32[16,128]{1,0:T(8,128)S(1)} %get-tuple-element.25.refs_1_, bf16[224,128]{1,0:T(8,128)(2,1)S(1)} %pack.1.refs_5_.refs_2_, ...), custom_call_target="tpu_custom_call" | custom-call | bytes 800000 | tf_op jit(solution)/shard_map/route/pallas_call | solution.py:342
  12.0 0.0 collective-permute-start.3
  12.1 1.6 %collective-permute-start.4 = (bf16[96,128]{1,0:T(8,128)(2,1)S(1)}, bf16[96,128]{1,0:T(8,128)(2,1)S(1)}, u32[]{:S(2)}, u32[]{:S(2)}) collective-permute-start(bf16[96,128]{1,0:T(8,128)(2,1)S(1)} %get-tuple-element.35), channel_id=1, source_target_pairs={{0,2},{1,3},{2,0},{3,1},{4,6},{5,7},{6,4},{7,5},{8,10},{9,11},{10,... | collective-permute-start | bytes 73736 | tf_op jit(solution)/shard_map/ppermute | solution.py:27
  13.6 0.0 collective-permute-done.6.refs_12_
  13.6 0.3 %collective-permute-start.5 = (bf16[96,128]{1,0:T(8,128)(2,1)S(1)}, bf16[96,128]{1,0:T(8,128)(2,1)S(1)}, u32[]{:S(2)}, u32[]{:S(2)}) collective-permute-start(bf16[96,128]{1,0:T(8,128)(2,1)S(1)} %get-tuple-element.36), channel_id=1, source_target_pairs={{0,1},{1,0},{2,3},{3,2},{4,5},{5,4},{6,7},{7,6},{8,9},{9,8},{10,11... | collective-permute-start | bytes 73736 | tf_op jit(solution)/shard_map/ppermute | solution.py:27
  13.9 0.0 copy-done.1
  13.9 0.0 copy-done.2
  13.9 0.0 copy-done.4
  13.9 0.0 copy-start.7
  13.9 1.5 %attend.1 = (f32[32,512]{1,0:T(8,128)S(1)}, bf16[512,128]{1,0:T(8,128)(2,1)S(1)}, f32[512,128]{1,0:T(8,128)S(1)}, f32[512,128]{1,0:T(8,128)S(1)}, f32[512,128]{1,0:T(8,128)S(1)}) custom-call(bf16[32,2048]{1,0:T(8,128)(2,1)S(1)} %bitcast.9, bf16[8,512,256]{2,1,0:T(8,128)(2,1)S(1)} %copy-done.1, bf16[8,512,256]{2,1,0:T(8,128)(2,1)S(1)} %copy-done.2, ...), custom_call_target="tpu_custom_call" | custom-call | flops 134217728 | bytes 4194304 | tf_op jit(solution)/shard_map/attend/pallas_call | solution.py:272
  15.5 0.0 collective-permute-done.7.refs_13_
  15.5 0.0 collective-permute-done.8.refs_14_
  15.5 0.0 collective-permute-done.3.refs_8_
  15.5 0.4 %collective-permute-done.4.refs_9_ = bf16[96,128]{1,0:T(8,128)(2,1)S(1)} collective-permute-done((bf16[96,128]{1,0:T(8,128)(2,1)S(1)}, bf16[96,128]{1,0:T(8,128)(2,1)S(1)}, u32[]{:S(2)}, u32[]{:S(2)}) %collective-permute-start.4) | collective-permute-done | bytes 24608 | tf_op jit(solution)/shard_map/ppermute | solution.py:27
  16.0 0.0 collective-permute-done.5.refs_10_
  16.0 0.0 copy-done.7
  16.0 1.4 %finish.1 = (bf16[32,2048]{1,0:T(8,128)(2,1)}, bf16[32,256]{1,0:T(8,128)(2,1)}, bf16[32,256]{1,0:T(8,128)(2,1)}) custom-call(f32[1,128]{1,0:T(1,128)S(1)} %bitcast.11, f32[32,512]{1,0:T(8,128)S(1)} %get-tuple-element.27.refs_1_, bf16[512,128]{1,0:T(8,128)(2,1)S(1)} %get-tuple-element.28.refs_2_, f32[512,128]{1,0:T(8,128)S(1)} %get-tuple-element.29.refs_3_, ...), custom_call_target="tpu_custom_call" | custom-call | bytes 1000000 | tf_op jit(solution)/shard_map/finish/pallas_call | solution.py:459
  (1 shorter events, 0.0 us)
Async XLA Ops:
  0.6 0.8 %copy-start.5 = (bf16[64,512]{1,0:T(8,128)(2,1)S(1)}, bf16[64,512]{1,0:T(8,128)(2,1)}, u32[]{:S(2)}) copy-start(bf16[64,512]{1,0:T(8,128)(2,1)} %up_all_ref.1) | copy-start | bytes 196612
  0.6 0.8 %copy-start.6 = (bf16[320,64]{0,1:T(8,128)(2,1)S(1)}, bf16[320,64]{0,1:T(8,128)(2,1)}, u32[]{:S(2)}) copy-start(bf16[320,64]{0,1:T(8,128)(2,1)} %param.12) | copy-start | bytes 122884
  0.7 6.5 %copy-start.3 = (bf16[4,8,1280]{2,1,0:T(8,128)(2,1)S(1)}, bf16[4,8,1280]{2,1,0:T(8,128)(2,1)}, u32[]{:S(2)}) copy-start(bf16[4,8,1280]{2,1,0:T(8,128)(2,1)} %param.10) | copy-start | bytes 245764
  0.7 6.5 %copy-start = (bf16[1280,2048]{1,0:T(8,128)(2,1)S(1)}, bf16[1280,2048]{1,0:T(8,128)(2,1)}, u32[]{:S(2)}) copy-start(bf16[1280,2048]{1,0:T(8,128)(2,1)} %weight_ref.1) | copy-start | bytes 15728644
  1.6 8.4 %collective-permute-start.2 = (bf16[224,128]{1,0:T(8,128)(2,1)S(1)}, bf16[224,128]{1,0:T(8,128)(2,1)S(1)}, u32[]{:S(2)}, u32[]{:S(2)}) collective-permute-start(bf16[224,128]{1,0:T(8,128)(2,1)S(1)} %pack.1.refs_5_.refs_2_), channel_id=1, source_target_pairs={{0,8},{4,12},{8,0},{12,4},{1,9},{5,13},{9,1},{13,5},{2,10},{6,14},... | collective-permute-start | bytes 172040 | tf_op jit(solution)/shard_map/ppermute | solution.py:27
  5.6 6.1 %collective-permute-start.1 = (bf16[224,128]{1,0:T(8,128)(2,1)S(1)}, bf16[224,128]{1,0:T(8,128)(2,1)S(1)}, u32[]{:S(2)}, u32[]{:S(2)}) collective-permute-start(bf16[224,128]{1,0:T(8,128)(2,1)S(1)} %pack.1.refs_5_.refs_2_), channel_id=1, source_target_pairs={{0,12},{4,8},{8,4},{12,0},{1,13},{5,9},{9,5},{13,1},{2,14},{6,10},... | collective-permute-start | bytes 172040 | tf_op jit(solution)/shard_map/ppermute | solution.py:27
  6.9 4.8 %collective-permute-start = (bf16[224,128]{1,0:T(8,128)(2,1)S(1)}, bf16[224,128]{1,0:T(8,128)(2,1)S(1)}, u32[]{:S(2)}, u32[]{:S(2)}) collective-permute-start(bf16[224,128]{1,0:T(8,128)(2,1)S(1)} %pack.1.refs_5_.refs_2_), channel_id=1, source_target_pairs={{0,4},{4,0},{8,12},{12,8},{1,5},{5,1},{9,13},{13,9},{2,6},{6,2},{1... | collective-permute-start | bytes 172040 | tf_op jit(solution)/shard_map/ppermute | solution.py:27
  7.2 6.7 %copy-start.1 = (bf16[8,512,256]{2,1,0:T(8,128)(2,1)S(1)}, bf16[8,512,256]{2,1,0:T(8,128)(2,1)}, u32[]{:S(2)}) copy-start(bf16[8,512,256]{2,1,0:T(8,128)(2,1)} %keys_ref.1) | copy-start | bytes 6291460
  7.2 6.7 %copy-start.2 = (bf16[8,512,256]{2,1,0:T(8,128)(2,1)S(1)}, bf16[8,512,256]{2,1,0:T(8,128)(2,1)}, u32[]{:S(2)}) copy-start(bf16[8,512,256]{2,1,0:T(8,128)(2,1)} %values_ref.1) | copy-start | bytes 6291460
  7.2 6.7 %copy-start.4 = (bf16[4,8,2048]{2,1,0:T(8,128)(2,1)S(1)}, bf16[4,8,2048]{2,1,0:T(8,128)(2,1)}, u32[]{:S(2)}) copy-start(bf16[4,8,2048]{2,1,0:T(8,128)(2,1)} %param.15) | copy-start | bytes 393220
  8.3 5.3 %collective-permute-start.6 = (bf16[32,512]{1,0:T(8,128)(2,1)S(1)}, bf16[32,512]{1,0:T(8,128)(2,1)S(1)}, u32[]{:S(2)}, u32[]{:S(2)}) collective-permute-start(bf16[32,512]{1,0:T(8,128)(2,1)S(1)} %get-tuple-element.37), channel_id=1, source_target_pairs={{0,3},{1,2},{2,1},{3,0},{4,7},{5,6},{6,5},{7,4},{8,11},{9,10},{10,... | collective-permute-start | bytes 98312 | tf_op jit(solution)/shard_map/ppermute | solution.py:27
  8.8 6.7 %collective-permute-start.7 = (bf16[32,512]{1,0:T(8,128)(2,1)S(1)}, bf16[32,512]{1,0:T(8,128)(2,1)S(1)}, u32[]{:S(2)}, u32[]{:S(2)}) collective-permute-start(bf16[32,512]{1,0:T(8,128)(2,1)S(1)} %get-tuple-element.38), channel_id=1, source_target_pairs={{0,2},{1,3},{2,0},{3,1},{4,6},{5,7},{6,4},{7,5},{8,10},{9,11},{10,... | collective-permute-start | bytes 98312 | tf_op jit(solution)/shard_map/ppermute | solution.py:27
  10.0 5.5 %collective-permute-start.8 = (bf16[32,512]{1,0:T(8,128)(2,1)S(1)}, bf16[32,512]{1,0:T(8,128)(2,1)S(1)}, u32[]{:S(2)}, u32[]{:S(2)}) collective-permute-start(bf16[32,512]{1,0:T(8,128)(2,1)S(1)} %get-tuple-element.39), channel_id=1, source_target_pairs={{0,1},{1,0},{2,3},{3,2},{4,5},{5,4},{6,7},{7,6},{8,9},{9,8},{10,11... | collective-permute-start | bytes 98312 | tf_op jit(solution)/shard_map/ppermute | solution.py:27
  12.0 3.5 %collective-permute-start.3 = (bf16[96,128]{1,0:T(8,128)(2,1)S(1)}, bf16[96,128]{1,0:T(8,128)(2,1)S(1)}, u32[]{:S(2)}, u32[]{:S(2)}) collective-permute-start(bf16[96,128]{1,0:T(8,128)(2,1)S(1)} %get-tuple-element.34), channel_id=1, source_target_pairs={{0,3},{1,2},{2,1},{3,0},{4,7},{5,6},{6,5},{7,4},{8,11},{9,10},{10,... | collective-permute-start | bytes 73736 | tf_op jit(solution)/shard_map/ppermute | solution.py:27
  12.1 3.9 %collective-permute-start.4 = (bf16[96,128]{1,0:T(8,128)(2,1)S(1)}, bf16[96,128]{1,0:T(8,128)(2,1)S(1)}, u32[]{:S(2)}, u32[]{:S(2)}) collective-permute-start(bf16[96,128]{1,0:T(8,128)(2,1)S(1)} %get-tuple-element.35), channel_id=1, source_target_pairs={{0,2},{1,3},{2,0},{3,1},{4,6},{5,7},{6,4},{7,5},{8,10},{9,11},{10,... | collective-permute-start | bytes 73736 | tf_op jit(solution)/shard_map/ppermute | solution.py:27
  13.6 2.3 %collective-permute-start.5 = (bf16[96,128]{1,0:T(8,128)(2,1)S(1)}, bf16[96,128]{1,0:T(8,128)(2,1)S(1)}, u32[]{:S(2)}, u32[]{:S(2)}) collective-permute-start(bf16[96,128]{1,0:T(8,128)(2,1)S(1)} %get-tuple-element.36), channel_id=1, source_target_pairs={{0,1},{1,0},{2,3},{3,2},{4,5},{5,4},{6,7},{7,6},{8,9},{9,8},{10,11... | collective-permute-start | bytes 73736 | tf_op jit(solution)/shard_map/ppermute | solution.py:27
  13.9 2.0 %copy-start.7 = (f32[128]{0:T(128)S(1)}, f32[128]{0:T(128)}, u32[]{:S(2)}) copy-start(f32[128]{0:T(128)} %param.14) | copy-start | bytes 1540

commit v23 on v22

--- a/solution.py
+++ b/solution.py
@@ -97,10 +97,10 @@
 
 
 def project_kernel(step_count, row_count, shards, replicas, *refs):
-    owners_hbm, lengths_hbm, tokens_ref, weight_ref, turns_ref, _ = refs[:6]
-    block_refs = refs[6 : 5 + shards]
-    left_ref, pick_ref, cosine_ref, sine_ref, bias_ref = refs[5 + shards : 10 + shards]
-    owners_ref, lengths_ref, token_buf, sems = refs[10 + shards :]
+    owners_hbm, lengths_hbm, tokens_ref, weight_ref, turns_ref, _, _, _ = refs[:8]
+    block_refs = refs[8 : 7 + shards]
+    left_ref, pick_ref, cosine_ref, sine_ref, bias_ref = refs[7 + shards : 12 + shards]
+    owners_ref, lengths_ref, token_buf, sems = refs[12 + shards :]
     owners_copy = pltpu.make_async_copy(owners_hbm, owners_ref, sems.at[0])
     lengths_copy = pltpu.make_async_copy(lengths_hbm, lengths_ref, sems.at[1])
     owners_copy.start()
@@ -150,7 +150,7 @@
 
 
 def project(
-    owners, lengths, tokens, weight, turns, after, step_count, slots, shards, replicas
+    owners, lengths, tokens, weight, turns, after, keys, values, step_count, shards, replicas
 ):
     rows, depth = tokens.shape
     row_count = rows // step_count
@@ -165,9 +165,9 @@
             jax.ShapeDtypeStruct((shards * replicas, lanes), f32),
             table,
             table,
-            jax.ShapeDtypeStruct((row_count, slots), f32),
+            jax.ShapeDtypeStruct((row_count, keys.shape[1]), f32),
         ],
-        in_specs=[stays_in_hbm] * 2 + [whole_in_vmem] * 4,
+        in_specs=[stays_in_hbm] * 2 + [whole_in_vmem] * 6,
         out_specs=[whole_in_vmem] * (shards + 4),
         scratch_shapes=[
             pltpu.SMEM(owners.shape, jnp.int32),
@@ -177,10 +177,8 @@
         ],
         compiler_params=pltpu.CompilerParams(vmem_limit_bytes=6 * 2**20),
         name="project",
-        cost_estimate=pl.CostEstimate(
-            flops=2 * rows * weight.size, bytes_accessed=2 * weight.size, transcendentals=0
-        ),
-    )(*in_hbm(owners, lengths), tokens, weight, turns, after)
+        cost_estimate=pl.CostEstimate(flops=0, bytes_accessed=200000, transcendentals=0),
+    )(*in_hbm(owners, lengths), tokens, weight, turns, after, keys, values)
     return outs[: shards - 1], *outs[shards - 1 :]
 
 
@@ -517,8 +515,9 @@
         key_value_weight,
         turns,
         packed if fits else adapter_up,
+        cache_keys,
+        stored_values,
         step_count,
-        cache_keys.shape[1],
         shards,
         replicas if fits else 1,
     )

time: 17.6 us -> 17.6 us (level)
  transfers between devices with their start and end apart: 9 -> 9, of which waited for: 3 -> 4; matrix products, arithmetic and copies ran while one was open for 0% -> 0% of each run, Pallas kernels for 17% -> 16%
where the time goes in v23:
time: 17.6 us; the launch traced here: 17.4 us
  starting transfers between devices  9.42 us (54%)
  Pallas kernels  4.31 us (24%)
  waiting for transfers between devices  2.13 us (12%)
  local copies, waits for them, and re-layouts  0.8 us (5%)
  between operations  0.75 us (4%)
    ppermute x9, starting transfers between devices, swap(): return lax.ppermute(block, axis, [(s, s ^ offset) for s in range(count)])  9.42 us
    ppermute x9, waiting for transfers between devices, swap(): return lax.ppermute(block, axis, [(s, s ^ offset) for s in range(count)])  2.13 us
    pallas_call x1, Pallas kernels, attend(): pl.pallas_call(functools.partial(attend_kernel, step_count, width // lane...  1.45 us
    pallas_call x1, Pallas kernels, finish(): pl.pallas_call(functools.partial(finish_kernel, step_count, row_count, he...  1.44 us
    pallas_call x1, Pallas kernels, project(): pl.pallas_call(functools.partial(project_kernel, step_count, row_count, s...  1.04 us
    unnamed x16, local copies, waits for them, and re-layouts  0.8 us
  transfers between devices with their start and end apart: 9, of which 4 were waited for; matrix products, arithmetic and copies ran while one was open for 0% of the time, Pallas kernels for 16%

profile of v23, /device:TPU:0, one launch (start us, length us, event | category | flops | bytes accessed | tf_op | source)
XLA Modules:
  0.0 17.4 jit_solution(4135435500859090260)
XLA Ops:
  0.6 0.0 copy-start.5
  0.6 0.0 copy-start.6
  0.7 0.0 copy-start.2
  0.7 0.0 copy-start.1
  0.7 0.0 copy-start.3
  0.7 0.0 copy-start
  0.7 0.8 %copy-done.5 = bf16[64,512]{1,0:T(8,128)(2,1)S(1)} copy-done((bf16[64,512]{1,0:T(8,128)(2,1)S(1)}, bf16[64,512]{1,0:T(8,128)(2,1)}, u32[]{:S(2)}) %copy-start.5) | copy-done | bytes 65560
  1.5 0.0 copy-done.6
  1.5 0.1 pack.1.refs_5_.refs_2_
  1.6 4.0 %collective-permute-start.2 = (bf16[224,128]{1,0:T(8,128)(2,1)S(1)}, bf16[224,128]{1,0:T(8,128)(2,1)S(1)}, u32[]{:S(2)}, u32[]{:S(2)}) collective-permute-start(bf16[224,128]{1,0:T(8,128)(2,1)S(1)} %pack.1.refs_5_.refs_2_), channel_id=1, source_target_pairs={{0,8},{4,12},{8,0},{12,4},{1,9},{5,13},{9,1},{13,5},{2,10},{6,14},... | collective-permute-start | bytes 172040 | tf_op jit(solution)/shard_map/ppermute | solution.py:27
  5.6 1.3 %collective-permute-start.1 = (bf16[224,128]{1,0:T(8,128)(2,1)S(1)}, bf16[224,128]{1,0:T(8,128)(2,1)S(1)}, u32[]{:S(2)}, u32[]{:S(2)}) collective-permute-start(bf16[224,128]{1,0:T(8,128)(2,1)S(1)} %pack.1.refs_5_.refs_2_), channel_id=1, source_target_pairs={{0,12},{4,8},{8,4},{12,0},{1,13},{5,9},{9,5},{13,1},{2,14},{6,10},... | collective-permute-start | bytes 172040 | tf_op jit(solution)/shard_map/ppermute | solution.py:27
  7.0 0.2 %collective-permute-start = (bf16[224,128]{1,0:T(8,128)(2,1)S(1)}, bf16[224,128]{1,0:T(8,128)(2,1)S(1)}, u32[]{:S(2)}, u32[]{:S(2)}) collective-permute-start(bf16[224,128]{1,0:T(8,128)(2,1)S(1)} %pack.1.refs_5_.refs_2_), channel_id=1, source_target_pairs={{0,4},{4,0},{8,12},{12,8},{1,5},{5,1},{9,13},{13,9},{2,6},{6,2},{1... | collective-permute-start | bytes 172040 | tf_op jit(solution)/shard_map/ppermute | solution.py:27
  7.2 0.0 copy-done.2
  7.2 0.0 copy-done.1
  7.2 0.0 copy-done.3
  7.2 0.0 copy-done
  7.2 0.0 copy-start.4
  7.2 1.0 %project.1 = (bf16[32,512]{1,0:T(8,128)(2,1)S(1)}, bf16[32,512]{1,0:T(8,128)(2,1)S(1)}, bf16[32,512]{1,0:T(8,128)(2,1)S(1)}, bf16[32,1536]{1,0:T(8,128)(2,1)S(1)...) custom-call(s32[4]{0:T(128)} %refs_0_.1, s32[8]{0:T(128)} %refs_1_.1, ...), custom_call_target="tpu_custom_call" | custom-call | bytes 200000 | tf_op jit(solution)/shard_map/project/pallas_call | solution.py:160
  8.3 0.4 %collective-permute-start.6 = (bf16[32,512]{1,0:T(8,128)(2,1)S(1)}, bf16[32,512]{1,0:T(8,128)(2,1)S(1)}, u32[]{:S(2)}, u32[]{:S(2)}) collective-permute-start(bf16[32,512]{1,0:T(8,128)(2,1)S(1)} %get-tuple-element.37), channel_id=1, source_target_pairs={{0,3},{1,2},{2,1},{3,0},{4,7},{5,6},{6,5},{7,4},{8,11},{9,10},{10,... | collective-permute-start | bytes 98312 | tf_op jit(solution)/shard_map/ppermute | solution.py:27
  8.7 1.2 %collective-permute-start.7 = (bf16[32,512]{1,0:T(8,128)(2,1)S(1)}, bf16[32,512]{1,0:T(8,128)(2,1)S(1)}, u32[]{:S(2)}, u32[]{:S(2)}) collective-permute-start(bf16[32,512]{1,0:T(8,128)(2,1)S(1)} %get-tuple-element.38), channel_id=1, source_target_pairs={{0,2},{1,3},{2,0},{3,1},{4,6},{5,7},{6,4},{7,5},{8,10},{9,11},{10,... | collective-permute-start | bytes 98312 | tf_op jit(solution)/shard_map/ppermute | solution.py:27
  9.9 0.0 collective-permute-done.2.refs_5_
  9.9 0.3 %collective-permute-start.8 = (bf16[32,512]{1,0:T(8,128)(2,1)S(1)}, bf16[32,512]{1,0:T(8,128)(2,1)S(1)}, u32[]{:S(2)}, u32[]{:S(2)}) collective-permute-start(bf16[32,512]{1,0:T(8,128)(2,1)S(1)} %get-tuple-element.39), channel_id=1, source_target_pairs={{0,1},{1,0},{2,3},{3,2},{4,5},{5,4},{6,7},{7,6},{8,9},{9,8},{10,11... | collective-permute-start | bytes 98312 | tf_op jit(solution)/shard_map/ppermute | solution.py:27
  10.2 1.5 %collective-permute-done.1.refs_4_ = bf16[224,128]{1,0:T(8,128)(2,1)S(1)} collective-permute-done((bf16[224,128]{1,0:T(8,128)(2,1)S(1)}, bf16[224,128]{1,0:T(8,128)(2,1)S(1)}, u32[]{:S(2)}, u32[]{:S(2)}) %collective-permute-start.1) | collective-permute-done | bytes 57376 | tf_op jit(solution)/shard_map/ppermute | solution.py:27
  11.7 0.1 collective-permute-done.refs_3_
  11.7 0.3 %route.1 = (bf16[96,128]{1,0:T(8,128)(2,1)S(1)}, bf16[96,128]{1,0:T(8,128)(2,1)S(1)}, bf16[96,128]{1,0:T(8,128)(2,1)S(1)}, bf16[96,128]{1,0:T(8,128)(2,1)S(1)}) custom-call(bf16[32,1536]{1,0:T(8,128)(2,1)S(1)} %get-tuple-element.24.refs_0_, f32[16,128]{1,0:T(8,128)S(1)} %get-tuple-element.25.refs_1_, bf16[224,128]{1,0:T(8,128)(2,1)S(1)} %pack.1.refs_5_.refs_2_, ...), custom_call_target="tpu_custom_call" | custom-call | bytes 800000 | tf_op jit(solution)/shard_map/route/pallas_call | solution.py:340
  12.0 0.0 collective-permute-start.3
  12.1 1.6 %collective-permute-start.4 = (bf16[96,128]{1,0:T(8,128)(2,1)S(1)}, bf16[96,128]{1,0:T(8,128)(2,1)S(1)}, u32[]{:S(2)}, u32[]{:S(2)}) collective-permute-start(bf16[96,128]{1,0:T(8,128)(2,1)S(1)} %get-tuple-element.35), channel_id=1, source_target_pairs={{0,2},{1,3},{2,0},{3,1},{4,6},{5,7},{6,4},{7,5},{8,10},{9,11},{10,... | collective-permute-start | bytes 73736 | tf_op jit(solution)/shard_map/ppermute | solution.py:27
  13.6 0.0 collective-permute-done.6.refs_12_
  13.6 0.3 %collective-permute-start.5 = (bf16[96,128]{1,0:T(8,128)(2,1)S(1)}, bf16[96,128]{1,0:T(8,128)(2,1)S(1)}, u32[]{:S(2)}, u32[]{:S(2)}) collective-permute-start(bf16[96,128]{1,0:T(8,128)(2,1)S(1)} %get-tuple-element.36), channel_id=1, source_target_pairs={{0,1},{1,0},{2,3},{3,2},{4,5},{5,4},{6,7},{7,6},{8,9},{9,8},{10,11... | collective-permute-start | bytes 73736 | tf_op jit(solution)/shard_map/ppermute | solution.py:27
  13.9 0.0 copy-done.4
  13.9 0.0 copy-start.7
  13.9 1.4 %attend.1 = (f32[32,512]{1,0:T(8,128)S(1)}, bf16[512,128]{1,0:T(8,128)(2,1)S(1)}, f32[512,128]{1,0:T(8,128)S(1)}, f32[512,128]{1,0:T(8,128)S(1)}, f32[512,128]{1,0:T(8,128)S(1)}) custom-call(bf16[32,2048]{1,0:T(8,128)(2,1)S(1)} %bitcast.9, bf16[8,512,256]{2,1,0:T(8,128)(2,1)S(1)} %copy-done.1, bf16[8,512,256]{2,1,0:T(8,128)(2,1)S(1)} %copy-done.2, ...), custom_call_target="tpu_custom_call" | custom-call | flops 134217728 | bytes 4194304 | tf_op jit(solution)/shard_map/attend/pallas_call | solution.py:270
  15.4 0.0 collective-permute-done.7.refs_13_
  15.4 0.0 collective-permute-done.8.refs_14_
  15.4 0.1 collective-permute-done.3.refs_8_
  15.5 0.4 %collective-permute-done.4.refs_9_ = bf16[96,128]{1,0:T(8,128)(2,1)S(1)} collective-permute-done((bf16[96,128]{1,0:T(8,128)(2,1)S(1)}, bf16[96,128]{1,0:T(8,128)(2,1)S(1)}, u32[]{:S(2)}, u32[]{:S(2)}) %collective-permute-start.4) | collective-permute-done | bytes 24608 | tf_op jit(solution)/shard_map/ppermute | solution.py:27
  16.0 0.0 collective-permute-done.5.refs_10_
  16.0 0.0 copy-done.7
  16.0 1.4 %finish.1 = (bf16[32,2048]{1,0:T(8,128)(2,1)}, bf16[32,256]{1,0:T(8,128)(2,1)}, bf16[32,256]{1,0:T(8,128)(2,1)}) custom-call(f32[1,128]{1,0:T(1,128)S(1)} %bitcast.11, f32[32,512]{1,0:T(8,128)S(1)} %get-tuple-element.27.refs_1_, bf16[512,128]{1,0:T(8,128)(2,1)S(1)} %get-tuple-element.28.refs_2_, f32[512,128]{1,0:T(8,128)S(1)} %get-tuple-element.29.refs_3_, ...), custom_call_target="tpu_custom_call" | custom-call | bytes 1000000 | tf_op jit(solution)/shard_map/finish/pallas_call | solution.py:457
  (1 shorter events, 0.0 us)
Async XLA Ops:
  0.6 0.8 %copy-start.5 = (bf16[64,512]{1,0:T(8,128)(2,1)S(1)}, bf16[64,512]{1,0:T(8,128)(2,1)}, u32[]{:S(2)}) copy-start(bf16[64,512]{1,0:T(8,128)(2,1)} %up_all_ref.1) | copy-start | bytes 196612
  0.6 0.8 %copy-start.6 = (bf16[320,64]{0,1:T(8,128)(2,1)S(1)}, bf16[320,64]{0,1:T(8,128)(2,1)}, u32[]{:S(2)}) copy-start(bf16[320,64]{0,1:T(8,128)(2,1)} %param.12) | copy-start | bytes 122884
  0.7 6.5 %copy-start.2 = (bf16[8,512,256]{2,1,0:T(8,128)(2,1)S(1)}, bf16[8,512,256]{2,1,0:T(8,128)(2,1)}, u32[]{:S(2)}) copy-start(bf16[8,512,256]{2,1,0:T(8,128)(2,1)} %values_ref.1) | copy-start | bytes 6291460
  0.7 6.5 %copy-start.1 = (bf16[8,512,256]{2,1,0:T(8,128)(2,1)S(1)}, bf16[8,512,256]{2,1,0:T(8,128)(2,1)}, u32[]{:S(2)}) copy-start(bf16[8,512,256]{2,1,0:T(8,128)(2,1)} %keys_ref.1) | copy-start | bytes 6291460
  0.7 6.5 %copy-start.3 = (bf16[4,8,1280]{2,1,0:T(8,128)(2,1)S(1)}, bf16[4,8,1280]{2,1,0:T(8,128)(2,1)}, u32[]{:S(2)}) copy-start(bf16[4,8,1280]{2,1,0:T(8,128)(2,1)} %param.10) | copy-start | bytes 245764
  0.7 6.5 %copy-start = (bf16[1280,2048]{1,0:T(8,128)(2,1)S(1)}, bf16[1280,2048]{1,0:T(8,128)(2,1)}, u32[]{:S(2)}) copy-start(bf16[1280,2048]{1,0:T(8,128)(2,1)} %weight_ref.1) | copy-start | bytes 15728644
  1.6 8.3 %collective-permute-start.2 = (bf16[224,128]{1,0:T(8,128)(2,1)S(1)}, bf16[224,128]{1,0:T(8,128)(2,1)S(1)}, u32[]{:S(2)}, u32[]{:S(2)}) collective-permute-start(bf16[224,128]{1,0:T(8,128)(2,1)S(1)} %pack.1.refs_5_.refs_2_), channel_id=1, source_target_pairs={{0,8},{4,12},{8,0},{12,4},{1,9},{5,13},{9,1},{13,5},{2,10},{6,14},... | collective-permute-start | bytes 172040 | tf_op jit(solution)/shard_map/ppermute | solution.py:27
  5.6 6.1 %collective-permute-start.1 = (bf16[224,128]{1,0:T(8,128)(2,1)S(1)}, bf16[224,128]{1,0:T(8,128)(2,1)S(1)}, u32[]{:S(2)}, u32[]{:S(2)}) collective-permute-start(bf16[224,128]{1,0:T(8,128)(2,1)S(1)} %pack.1.refs_5_.refs_2_), channel_id=1, source_target_pairs={{0,12},{4,8},{8,4},{12,0},{1,13},{5,9},{9,5},{13,1},{2,14},{6,10},... | collective-permute-start | bytes 172040 | tf_op jit(solution)/shard_map/ppermute | solution.py:27
  7.0 4.8 %collective-permute-start = (bf16[224,128]{1,0:T(8,128)(2,1)S(1)}, bf16[224,128]{1,0:T(8,128)(2,1)S(1)}, u32[]{:S(2)}, u32[]{:S(2)}) collective-permute-start(bf16[224,128]{1,0:T(8,128)(2,1)S(1)} %pack.1.refs_5_.refs_2_), channel_id=1, source_target_pairs={{0,4},{4,0},{8,12},{12,8},{1,5},{5,1},{9,13},{13,9},{2,6},{6,2},{1... | collective-permute-start | bytes 172040 | tf_op jit(solution)/shard_map/ppermute | solution.py:27
  7.2 6.7 %copy-start.4 = (bf16[4,8,2048]{2,1,0:T(8,128)(2,1)S(1)}, bf16[4,8,2048]{2,1,0:T(8,128)(2,1)}, u32[]{:S(2)}) copy-start(bf16[4,8,2048]{2,1,0:T(8,128)(2,1)} %param.15) | copy-start | bytes 393220
  8.3 5.4 %collective-permute-start.6 = (bf16[32,512]{1,0:T(8,128)(2,1)S(1)}, bf16[32,512]{1,0:T(8,128)(2,1)S(1)}, u32[]{:S(2)}, u32[]{:S(2)}) collective-permute-start(bf16[32,512]{1,0:T(8,128)(2,1)S(1)} %get-tuple-element.37), channel_id=1, source_target_pairs={{0,3},{1,2},{2,1},{3,0},{4,7},{5,6},{6,5},{7,4},{8,11},{9,10},{10,... | collective-permute-start | bytes 98312 | tf_op jit(solution)/shard_map/ppermute | solution.py:27
  8.7 6.7 %collective-permute-start.7 = (bf16[32,512]{1,0:T(8,128)(2,1)S(1)}, bf16[32,512]{1,0:T(8,128)(2,1)S(1)}, u32[]{:S(2)}, u32[]{:S(2)}) collective-permute-start(bf16[32,512]{1,0:T(8,128)(2,1)S(1)} %get-tuple-element.38), channel_id=1, source_target_pairs={{0,2},{1,3},{2,0},{3,1},{4,6},{5,7},{6,4},{7,5},{8,10},{9,11},{10,... | collective-permute-start | bytes 98312 | tf_op jit(solution)/shard_map/ppermute | solution.py:27
  9.9 5.5 %collective-permute-start.8 = (bf16[32,512]{1,0:T(8,128)(2,1)S(1)}, bf16[32,512]{1,0:T(8,128)(2,1)S(1)}, u32[]{:S(2)}, u32[]{:S(2)}) collective-permute-start(bf16[32,512]{1,0:T(8,128)(2,1)S(1)} %get-tuple-element.39), channel_id=1, source_target_pairs={{0,1},{1,0},{2,3},{3,2},{4,5},{5,4},{6,7},{7,6},{8,9},{9,8},{10,11... | collective-permute-start | bytes 98312 | tf_op jit(solution)/shard_map/ppermute | solution.py:27
  12.0 3.5 %collective-permute-start.3 = (bf16[96,128]{1,0:T(8,128)(2,1)S(1)}, bf16[96,128]{1,0:T(8,128)(2,1)S(1)}, u32[]{:S(2)}, u32[]{:S(2)}) collective-permute-start(bf16[96,128]{1,0:T(8,128)(2,1)S(1)} %get-tuple-element.34), channel_id=1, source_target_pairs={{0,3},{1,2},{2,1},{3,0},{4,7},{5,6},{6,5},{7,4},{8,11},{9,10},{10,... | collective-permute-start | bytes 73736 | tf_op jit(solution)/shard_map/ppermute | solution.py:27
  12.1 3.9 %collective-permute-start.4 = (bf16[96,128]{1,0:T(8,128)(2,1)S(1)}, bf16[96,128]{1,0:T(8,128)(2,1)S(1)}, u32[]{:S(2)}, u32[]{:S(2)}) collective-permute-start(bf16[96,128]{1,0:T(8,128)(2,1)S(1)} %get-tuple-element.35), channel_id=1, source_target_pairs={{0,2},{1,3},{2,0},{3,1},{4,6},{5,7},{6,4},{7,5},{8,10},{9,11},{10,... | collective-permute-start | bytes 73736 | tf_op jit(solution)/shard_map/ppermute | solution.py:27
  13.6 2.3 %collective-permute-start.5 = (bf16[96,128]{1,0:T(8,128)(2,1)S(1)}, bf16[96,128]{1,0:T(8,128)(2,1)S(1)}, u32[]{:S(2)}, u32[]{:S(2)}) collective-permute-start(bf16[96,128]{1,0:T(8,128)(2,1)S(1)} %get-tuple-element.36), channel_id=1, source_target_pairs={{0,1},{1,0},{2,3},{3,2},{4,5},{5,4},{6,7},{7,6},{8,9},{9,8},{10,11... | collective-permute-start | bytes 73736 | tf_op jit(solution)/shard_map/ppermute | solution.py:27
  13.9 2.0 %copy-start.7 = (f32[128]{0:T(128)S(1)}, f32[128]{0:T(128)}, u32[]{:S(2)}) copy-start(f32[128]{0:T(128)} %param.14) | copy-start | bytes 1540

commit v24 on v23

--- a/solution.py
+++ b/solution.py
@@ -294,8 +294,7 @@
 
 
 def piece_places(replicas):
-    order = [0, 1] + list(range(replicas - 1, 1, -1))
-    return [order.index(i) for i in range(replicas)]
+    return [0] + list(range(replicas - 1, 0, -1))
 
 
 def route_kernel(replicas, shards, *refs):

time: 17.6 us -> 19 us (1.080)
  waiting for transfers between devices: 2.13 us -> 3.53 us
    ppermute x9, waiting for transfers between devices: 2.13 us -> 3.53 us  [swap(): return lax.ppermute(block, axis, [(s, s ^ offset) for s in range(count)])]
  transfers between devices with their start and end apart: 9 -> 9, of which waited for: 4 -> 4; matrix products, arithmetic and copies ran while one was open for 0% -> 0% of each run, Pallas kernels for 16% -> 15%
where the time goes in v24:
time: 19 us; the launch traced here: 18.8 us
  starting transfers between devices  9.42 us (50%)
  Pallas kernels  4.31 us (23%)
  waiting for transfers between devices  3.53 us (19%)
  local copies, waits for them, and re-layouts  0.8 us (4%)
  between operations  0.76 us (4%)
    ppermute x9, starting transfers between devices, swap(): return lax.ppermute(block, axis, [(s, s ^ offset) for s in range(count)])  9.42 us
    ppermute x9, waiting for transfers between devices, swap(): return lax.ppermute(block, axis, [(s, s ^ offset) for s in range(count)])  3.53 us
    pallas_call x1, Pallas kernels, attend(): pl.pallas_call(functools.partial(attend_kernel, step_count, width // lane...  1.45 us
    pallas_call x1, Pallas kernels, finish(): pl.pallas_call(functools.partial(finish_kernel, step_count, row_count, he...  1.43 us
    pallas_call x1, Pallas kernels, project(): pl.pallas_call(functools.partial(project_kernel, step_count, row_count, s...  1.04 us
    unnamed x16, local copies, waits for them, and re-layouts  0.8 us
  transfers between devices with their start and end apart: 9, of which 4 were waited for; matrix products, arithmetic and copies ran while one was open for 0% of the time, Pallas kernels for 15%

profile of v24, /device:TPU:0, one launch (start us, length us, event | category | flops | bytes accessed | tf_op | source)
XLA Modules:
  0.0 18.8 jit_solution(5892239146617253361)
XLA Ops:
  0.6 0.0 copy-start.5
  0.6 0.0 copy-start.6
  0.7 0.0 copy-start.2
  0.7 0.0 copy-start.1
  0.7 0.0 copy-start.3
  0.7 0.0 copy-start
  0.7 0.8 %copy-done.5 = bf16[64,512]{1,0:T(8,128)(2,1)S(1)} copy-done((bf16[64,512]{1,0:T(8,128)(2,1)S(1)}, bf16[64,512]{1,0:T(8,128)(2,1)}, u32[]{:S(2)}) %copy-start.5) | copy-done | bytes 65560
  1.5 0.0 copy-done.6
  1.5 0.1 pack.1.refs_5_.refs_2_
  1.6 3.0 %collective-permute-start.2 = (bf16[224,128]{1,0:T(8,128)(2,1)S(1)}, bf16[224,128]{1,0:T(8,128)(2,1)S(1)}, u32[]{:S(2)}, u32[]{:S(2)}) collective-permute-start(bf16[224,128]{1,0:T(8,128)(2,1)S(1)} %pack.1.refs_5_.refs_2_), channel_id=1, source_target_pairs={{0,4},{4,0},{8,12},{12,8},{1,5},{5,1},{9,13},{13,9},{2,6},{6,2},{1... | collective-permute-start | bytes 172040 | tf_op jit(solution)/shard_map/ppermute | solution.py:27
  4.6 2.6 %collective-permute-start.1 = (bf16[224,128]{1,0:T(8,128)(2,1)S(1)}, bf16[224,128]{1,0:T(8,128)(2,1)S(1)}, u32[]{:S(2)}, u32[]{:S(2)}) collective-permute-start(bf16[224,128]{1,0:T(8,128)(2,1)S(1)} %pack.1.refs_5_.refs_2_), channel_id=1, source_target_pairs={{0,8},{4,12},{8,0},{12,4},{1,9},{5,13},{9,1},{13,5},{2,10},{6,14},... | collective-permute-start | bytes 172040 | tf_op jit(solution)/shard_map/ppermute | solution.py:27
  7.2 0.0 collective-permute-start
  7.2 0.0 copy-done.2
  7.2 0.0 copy-done.1
  7.2 0.0 copy-done.3
  7.2 0.0 copy-done
  7.2 0.0 copy-start.4
  7.2 1.0 %project.1 = (bf16[32,512]{1,0:T(8,128)(2,1)S(1)}, bf16[32,512]{1,0:T(8,128)(2,1)S(1)}, bf16[32,512]{1,0:T(8,128)(2,1)S(1)}, bf16[32,1536]{1,0:T(8,128)(2,1)S(1)...) custom-call(s32[4]{0:T(128)} %refs_0_.1, s32[8]{0:T(128)} %refs_1_.1, ...), custom_call_target="tpu_custom_call" | custom-call | bytes 200000 | tf_op jit(solution)/shard_map/project/pallas_call | solution.py:160
  8.3 0.4 %collective-permute-start.6 = (bf16[32,512]{1,0:T(8,128)(2,1)S(1)}, bf16[32,512]{1,0:T(8,128)(2,1)S(1)}, u32[]{:S(2)}, u32[]{:S(2)}) collective-permute-start(bf16[32,512]{1,0:T(8,128)(2,1)S(1)} %get-tuple-element.37), channel_id=1, source_target_pairs={{0,3},{1,2},{2,1},{3,0},{4,7},{5,6},{6,5},{7,4},{8,11},{9,10},{10,... | collective-permute-start | bytes 98312 | tf_op jit(solution)/shard_map/ppermute | solution.py:27
  8.7 1.4 %collective-permute-start.7 = (bf16[32,512]{1,0:T(8,128)(2,1)S(1)}, bf16[32,512]{1,0:T(8,128)(2,1)S(1)}, u32[]{:S(2)}, u32[]{:S(2)}) collective-permute-start(bf16[32,512]{1,0:T(8,128)(2,1)S(1)} %get-tuple-element.38), channel_id=1, source_target_pairs={{0,2},{1,3},{2,0},{3,1},{4,6},{5,7},{6,4},{7,5},{8,10},{9,11},{10,... | collective-permute-start | bytes 98312 | tf_op jit(solution)/shard_map/ppermute | solution.py:27
  10.1 0.0 collective-permute-done.2.refs_5_
  10.1 0.1 collective-permute-start.8
  10.2 0.6 %collective-permute-done.1.refs_4_ = bf16[224,128]{1,0:T(8,128)(2,1)S(1)} collective-permute-done((bf16[224,128]{1,0:T(8,128)(2,1)S(1)}, bf16[224,128]{1,0:T(8,128)(2,1)S(1)}, u32[]{:S(2)}, u32[]{:S(2)}) %collective-permute-start.1) | collective-permute-done | bytes 57376 | tf_op jit(solution)/shard_map/ppermute | solution.py:27
  10.8 2.4 %collective-permute-done.refs_3_ = bf16[224,128]{1,0:T(8,128)(2,1)S(1)} collective-permute-done((bf16[224,128]{1,0:T(8,128)(2,1)S(1)}, bf16[224,128]{1,0:T(8,128)(2,1)S(1)}, u32[]{:S(2)}, u32[]{:S(2)}) %collective-permute-start) | collective-permute-done | bytes 57376 | tf_op jit(solution)/shard_map/ppermute | solution.py:27
  13.2 0.3 %route.1 = (bf16[96,128]{1,0:T(8,128)(2,1)S(1)}, bf16[96,128]{1,0:T(8,128)(2,1)S(1)}, bf16[96,128]{1,0:T(8,128)(2,1)S(1)}, bf16[96,128]{1,0:T(8,128)(2,1)S(1)}) custom-call(bf16[32,1536]{1,0:T(8,128)(2,1)S(1)} %get-tuple-element.24.refs_0_, f32[16,128]{1,0:T(8,128)S(1)} %get-tuple-element.25.refs_1_, bf16[224,128]{1,0:T(8,128)(2,1)S(1)} %pack.1.refs_5_.refs_2_, ...), custom_call_target="tpu_custom_call" | custom-call | bytes 800000 | tf_op jit(solution)/shard_map/route/pallas_call | solution.py:339
  13.5 0.0 collective-permute-start.3
  13.5 1.6 %collective-permute-start.4 = (bf16[96,128]{1,0:T(8,128)(2,1)S(1)}, bf16[96,128]{1,0:T(8,128)(2,1)S(1)}, u32[]{:S(2)}, u32[]{:S(2)}) collective-permute-start(bf16[96,128]{1,0:T(8,128)(2,1)S(1)} %get-tuple-element.35), channel_id=1, source_target_pairs={{0,2},{1,3},{2,0},{3,1},{4,6},{5,7},{6,4},{7,5},{8,10},{9,11},{10,... | collective-permute-start | bytes 73736 | tf_op jit(solution)/shard_map/ppermute | solution.py:27
  15.0 0.0 collective-permute-done.6.refs_12_
  15.0 0.3 %collective-permute-start.5 = (bf16[96,128]{1,0:T(8,128)(2,1)S(1)}, bf16[96,128]{1,0:T(8,128)(2,1)S(1)}, u32[]{:S(2)}, u32[]{:S(2)}) collective-permute-start(bf16[96,128]{1,0:T(8,128)(2,1)S(1)} %get-tuple-element.36), channel_id=1, source_target_pairs={{0,1},{1,0},{2,3},{3,2},{4,5},{5,4},{6,7},{7,6},{8,9},{9,8},{10,11... | collective-permute-start | bytes 73736 | tf_op jit(solution)/shard_map/ppermute | solution.py:27
  15.3 0.0 copy-done.4
  15.3 0.0 copy-start.7
  15.3 1.4 %attend.1 = (f32[32,512]{1,0:T(8,128)S(1)}, bf16[512,128]{1,0:T(8,128)(2,1)S(1)}, f32[512,128]{1,0:T(8,128)S(1)}, f32[512,128]{1,0:T(8,128)S(1)}, f32[512,128]{1,0:T(8,128)S(1)}) custom-call(bf16[32,2048]{1,0:T(8,128)(2,1)S(1)} %bitcast.9, bf16[8,512,256]{2,1,0:T(8,128)(2,1)S(1)} %copy-done.1, bf16[8,512,256]{2,1,0:T(8,128)(2,1)S(1)} %copy-done.2, ...), custom_call_target="tpu_custom_call" | custom-call | flops 134217728 | bytes 4194304 | tf_op jit(solution)/shard_map/attend/pallas_call | solution.py:270
  16.8 0.0 collective-permute-done.7.refs_13_
  16.8 0.0 collective-permute-done.8.refs_14_
  16.8 0.1 collective-permute-done.3.refs_8_
  16.9 0.4 %collective-permute-done.4.refs_9_ = bf16[96,128]{1,0:T(8,128)(2,1)S(1)} collective-permute-done((bf16[96,128]{1,0:T(8,128)(2,1)S(1)}, bf16[96,128]{1,0:T(8,128)(2,1)S(1)}, u32[]{:S(2)}, u32[]{:S(2)}) %collective-permute-start.4) | collective-permute-done | bytes 24608 | tf_op jit(solution)/shard_map/ppermute | solution.py:27
  17.4 0.0 collective-permute-done.5.refs_10_
  17.4 0.0 copy-done.7
  17.4 1.4 %finish.1 = (bf16[32,2048]{1,0:T(8,128)(2,1)}, bf16[32,256]{1,0:T(8,128)(2,1)}, bf16[32,256]{1,0:T(8,128)(2,1)}) custom-call(f32[1,128]{1,0:T(1,128)S(1)} %bitcast.11, f32[32,512]{1,0:T(8,128)S(1)} %get-tuple-element.27.refs_1_, bf16[512,128]{1,0:T(8,128)(2,1)S(1)} %get-tuple-element.28.refs_2_, f32[512,128]{1,0:T(8,128)S(1)} %get-tuple-element.29.refs_3_, ...), custom_call_target="tpu_custom_call" | custom-call | bytes 1000000 | tf_op jit(solution)/shard_map/finish/pallas_call | solution.py:456
  (1 shorter events, 0.0 us)
Async XLA Ops:
  0.6 0.8 %copy-start.5 = (bf16[64,512]{1,0:T(8,128)(2,1)S(1)}, bf16[64,512]{1,0:T(8,128)(2,1)}, u32[]{:S(2)}) copy-start(bf16[64,512]{1,0:T(8,128)(2,1)} %up_all_ref.1) | copy-start | bytes 196612
  0.6 0.8 %copy-start.6 = (bf16[320,64]{0,1:T(8,128)(2,1)S(1)}, bf16[320,64]{0,1:T(8,128)(2,1)}, u32[]{:S(2)}) copy-start(bf16[320,64]{0,1:T(8,128)(2,1)} %param.12) | copy-start | bytes 122884
  0.7 6.5 %copy-start.2 = (bf16[8,512,256]{2,1,0:T(8,128)(2,1)S(1)}, bf16[8,512,256]{2,1,0:T(8,128)(2,1)}, u32[]{:S(2)}) copy-start(bf16[8,512,256]{2,1,0:T(8,128)(2,1)} %values_ref.1) | copy-start | bytes 6291460
  0.7 6.5 %copy-start.1 = (bf16[8,512,256]{2,1,0:T(8,128)(2,1)S(1)}, bf16[8,512,256]{2,1,0:T(8,128)(2,1)}, u32[]{:S(2)}) copy-start(bf16[8,512,256]{2,1,0:T(8,128)(2,1)} %keys_ref.1) | copy-start | bytes 6291460
  0.7 6.5 %copy-start.3 = (bf16[4,8,1280]{2,1,0:T(8,128)(2,1)S(1)}, bf16[4,8,1280]{2,1,0:T(8,128)(2,1)}, u32[]{:S(2)}) copy-start(bf16[4,8,1280]{2,1,0:T(8,128)(2,1)} %param.10) | copy-start | bytes 245764
  0.7 6.5 %copy-start = (bf16[1280,2048]{1,0:T(8,128)(2,1)S(1)}, bf16[1280,2048]{1,0:T(8,128)(2,1)}, u32[]{:S(2)}) copy-start(bf16[1280,2048]{1,0:T(8,128)(2,1)} %weight_ref.1) | copy-start | bytes 15728644
  1.6 8.6 %collective-permute-start.2 = (bf16[224,128]{1,0:T(8,128)(2,1)S(1)}, bf16[224,128]{1,0:T(8,128)(2,1)S(1)}, u32[]{:S(2)}, u32[]{:S(2)}) collective-permute-start(bf16[224,128]{1,0:T(8,128)(2,1)S(1)} %pack.1.refs_5_.refs_2_), channel_id=1, source_target_pairs={{0,4},{4,0},{8,12},{12,8},{1,5},{5,1},{9,13},{13,9},{2,6},{6,2},{1... | collective-permute-start | bytes 172040 | tf_op jit(solution)/shard_map/ppermute | solution.py:27
  4.6 6.2 %collective-permute-start.1 = (bf16[224,128]{1,0:T(8,128)(2,1)S(1)}, bf16[224,128]{1,0:T(8,128)(2,1)S(1)}, u32[]{:S(2)}, u32[]{:S(2)}) collective-permute-start(bf16[224,128]{1,0:T(8,128)(2,1)S(1)} %pack.1.refs_5_.refs_2_), channel_id=1, source_target_pairs={{0,8},{4,12},{8,0},{12,4},{1,9},{5,13},{9,1},{13,5},{2,10},{6,14},... | collective-permute-start | bytes 172040 | tf_op jit(solution)/shard_map/ppermute | solution.py:27
  7.2 6.0 %collective-permute-start = (bf16[224,128]{1,0:T(8,128)(2,1)S(1)}, bf16[224,128]{1,0:T(8,128)(2,1)S(1)}, u32[]{:S(2)}, u32[]{:S(2)}) collective-permute-start(bf16[224,128]{1,0:T(8,128)(2,1)S(1)} %pack.1.refs_5_.refs_2_), channel_id=1, source_target_pairs={{0,12},{4,8},{8,4},{12,0},{1,13},{5,9},{9,5},{13,1},{2,14},{6,10},... | collective-permute-start | bytes 172040 | tf_op jit(solution)/shard_map/ppermute | solution.py:27
  7.2 8.1 %copy-start.4 = (bf16[4,8,2048]{2,1,0:T(8,128)(2,1)S(1)}, bf16[4,8,2048]{2,1,0:T(8,128)(2,1)}, u32[]{:S(2)}) copy-start(bf16[4,8,2048]{2,1,0:T(8,128)(2,1)} %param.15) | copy-start | bytes 393220
  8.3 6.8 %collective-permute-start.6 = (bf16[32,512]{1,0:T(8,128)(2,1)S(1)}, bf16[32,512]{1,0:T(8,128)(2,1)S(1)}, u32[]{:S(2)}, u32[]{:S(2)}) collective-permute-start(bf16[32,512]{1,0:T(8,128)(2,1)S(1)} %get-tuple-element.37), channel_id=1, source_target_pairs={{0,3},{1,2},{2,1},{3,0},{4,7},{5,6},{6,5},{7,4},{8,11},{9,10},{10,... | collective-permute-start | bytes 98312 | tf_op jit(solution)/shard_map/ppermute | solution.py:27
  8.7 8.1 %collective-permute-start.7 = (bf16[32,512]{1,0:T(8,128)(2,1)S(1)}, bf16[32,512]{1,0:T(8,128)(2,1)S(1)}, u32[]{:S(2)}, u32[]{:S(2)}) collective-permute-start(bf16[32,512]{1,0:T(8,128)(2,1)S(1)} %get-tuple-element.38), channel_id=1, source_target_pairs={{0,2},{1,3},{2,0},{3,1},{4,6},{5,7},{6,4},{7,5},{8,10},{9,11},{10,... | collective-permute-start | bytes 98312 | tf_op jit(solution)/shard_map/ppermute | solution.py:27
  10.1 6.7 %collective-permute-start.8 = (bf16[32,512]{1,0:T(8,128)(2,1)S(1)}, bf16[32,512]{1,0:T(8,128)(2,1)S(1)}, u32[]{:S(2)}, u32[]{:S(2)}) collective-permute-start(bf16[32,512]{1,0:T(8,128)(2,1)S(1)} %get-tuple-element.39), channel_id=1, source_target_pairs={{0,1},{1,0},{2,3},{3,2},{4,5},{5,4},{6,7},{7,6},{8,9},{9,8},{10,11... | collective-permute-start | bytes 98312 | tf_op jit(solution)/shard_map/ppermute | solution.py:27
  13.5 3.5 %collective-permute-start.3 = (bf16[96,128]{1,0:T(8,128)(2,1)S(1)}, bf16[96,128]{1,0:T(8,128)(2,1)S(1)}, u32[]{:S(2)}, u32[]{:S(2)}) collective-permute-start(bf16[96,128]{1,0:T(8,128)(2,1)S(1)} %get-tuple-element.34), channel_id=1, source_target_pairs={{0,3},{1,2},{2,1},{3,0},{4,7},{5,6},{6,5},{7,4},{8,11},{9,10},{10,... | collective-permute-start | bytes 73736 | tf_op jit(solution)/shard_map/ppermute | solution.py:27
  13.5 3.9 %collective-permute-start.4 = (bf16[96,128]{1,0:T(8,128)(2,1)S(1)}, bf16[96,128]{1,0:T(8,128)(2,1)S(1)}, u32[]{:S(2)}, u32[]{:S(2)}) collective-permute-start(bf16[96,128]{1,0:T(8,128)(2,1)S(1)} %get-tuple-element.35), channel_id=1, source_target_pairs={{0,2},{1,3},{2,0},{3,1},{4,6},{5,7},{6,4},{7,5},{8,10},{9,11},{10,... | collective-permute-start | bytes 73736 | tf_op jit(solution)/shard_map/ppermute | solution.py:27
  15.0 2.3 %collective-permute-start.5 = (bf16[96,128]{1,0:T(8,128)(2,1)S(1)}, bf16[96,128]{1,0:T(8,128)(2,1)S(1)}, u32[]{:S(2)}, u32[]{:S(2)}) collective-permute-start(bf16[96,128]{1,0:T(8,128)(2,1)S(1)} %get-tuple-element.36), channel_id=1, source_target_pairs={{0,1},{1,0},{2,3},{3,2},{4,5},{5,4},{6,7},{7,6},{8,9},{9,8},{10,11... | collective-permute-start | bytes 73736 | tf_op jit(solution)/shard_map/ppermute | solution.py:27
  15.3 2.0 %copy-start.7 = (f32[128]{0:T(128)S(1)}, f32[128]{0:T(128)}, u32[]{:S(2)}) copy-start(f32[128]{0:T(128)} %param.14) | copy-start | bytes 1540

commit v25 on v23

--- a/solution.py
+++ b/solution.py
@@ -78,7 +78,7 @@
         first += rank_part
 
 
-def pack(down, up, rank_part, after):
+def pack(down, up, rank_part, after, beside):
     rows = (down.size + rank_part * up.shape[1]) // lanes
     return pl.pallas_call(
         pack_kernel,
@@ -87,7 +87,7 @@
         out_specs=whole_in_vmem,
         compiler_params=pltpu.CompilerParams(vmem_limit_bytes=2 * 2**20),
         name="pack",
-        cost_estimate=pl.CostEstimate(flops=0, bytes_accessed=200000, transcendentals=0),
+        cost_estimate=beside,
     )(down, up, after)
 
 
@@ -501,12 +501,14 @@
         and rank == lanes // 2
         and rank_part % 16 == 0
     )
+    pieces_size = 2 * (adapter_down.size + adapter_up.size)
     fetched = 2 * (key_value_weight.size + cache_keys.size + stored_values.size)
     turns = frequencies(
-        pl.CostEstimate(flops=1000 * fetched, bytes_accessed=fetched, transcendentals=0)
-    )
+        pl.CostEstimate(flops=10000 * pieces_size, bytes_accessed=10 * pieces_size, transcendentals=0)
+    )
+    beside = pl.CostEstimate(flops=1000 * fetched, bytes_accessed=fetched, transcendentals=0)
     if fits:
-        packed = pack(adapter_down.T, adapter_up, rank_part, turns)
+        packed = pack(adapter_down.T, adapter_up, rank_part, turns, beside)
         pieces = [packed] + [swap(packed, "rollout", i) for i in range(1, replicas)]
     blocks, left, pick, cosine, sine, bias = project(
         owners,

time: 17.6 us -> 17.6 us (level)
    unnamed x16 -> x18, local copies, waits for them, and re-layouts: 0.8 us -> 0.83 us
where the time goes in v25:
time: 17.6 us; the launch traced here: 17.4 us
  starting transfers between devices  9.42 us (54%)
  Pallas kernels  4.31 us (24%)
  waiting for transfers between devices  2.11 us (12%)
  local copies, waits for them, and re-layouts  0.83 us (5%)
  between operations  0.75 us (4%)
    ppermute x9, starting transfers between devices, swap(): return lax.ppermute(block, axis, [(s, s ^ offset) for s in range(count)])  9.42 us
    ppermute x9, waiting for transfers between devices, swap(): return lax.ppermute(block, axis, [(s, s ^ offset) for s in range(count)])  2.11 us
    pallas_call x1, Pallas kernels, attend(): pl.pallas_call(functools.partial(attend_kernel, step_count, width // lane...  1.45 us
    pallas_call x1, Pallas kernels, finish(): pl.pallas_call(functools.partial(finish_kernel, step_count, row_count, he...  1.44 us
    pallas_call x1, Pallas kernels, project(): pl.pallas_call(functools.partial(project_kernel, step_count, row_count, s...  1.04 us
    unnamed x18, local copies, waits for them, and re-layouts  0.83 us
  transfers between devices with their start and end apart: 9, of which 4 were waited for; matrix products, arithmetic and copies ran while one was open for 0% of the time, Pallas kernels for 16%

profile of v25, /device:TPU:0, one launch (start us, length us, event | category | flops | bytes accessed | tf_op | source)
XLA Modules:
  0.0 17.4 jit_solution(682719522623129427)
XLA Ops:
  0.6 0.0 copy-start.5
  0.6 0.0 copy-start.6
  0.7 0.0 slice-start
  0.7 0.8 %copy-done.5 = bf16[64,512]{1,0:T(8,128)(2,1)S(1)} copy-done((bf16[64,512]{1,0:T(8,128)(2,1)S(1)}, bf16[64,512]{1,0:T(8,128)(2,1)}, u32[]{:S(2)}) %copy-start.5) | copy-done | bytes 65560
  1.5 0.0 copy-done.6
  1.5 0.0 slice-start.1
  1.5 0.0 copy-start
  1.5 0.0 copy-start.1
  1.5 0.0 copy-start.2
  1.5 0.1 pack.1.refs_5_.refs_2_
  1.6 4.1 %collective-permute-start.2 = (bf16[224,128]{1,0:T(8,128)(2,1)S(1)}, bf16[224,128]{1,0:T(8,128)(2,1)S(1)}, u32[]{:S(2)}, u32[]{:S(2)}) collective-permute-start(bf16[224,128]{1,0:T(8,128)(2,1)S(1)} %pack.1.refs_5_.refs_2_), channel_id=1, source_target_pairs={{0,8},{4,12},{8,0},{12,4},{1,9},{5,13},{9,1},{13,5},{2,10},{6,14},... | collective-permute-start | bytes 172040 | tf_op jit(solution)/shard_map/ppermute | solution.py:27
  5.6 1.3 %collective-permute-start.1 = (bf16[224,128]{1,0:T(8,128)(2,1)S(1)}, bf16[224,128]{1,0:T(8,128)(2,1)S(1)}, u32[]{:S(2)}, u32[]{:S(2)}) collective-permute-start(bf16[224,128]{1,0:T(8,128)(2,1)S(1)} %pack.1.refs_5_.refs_2_), channel_id=1, source_target_pairs={{0,12},{4,8},{8,4},{12,0},{1,13},{5,9},{9,5},{13,1},{2,14},{6,10},... | collective-permute-start | bytes 172040 | tf_op jit(solution)/shard_map/ppermute | solution.py:27
  7.0 0.2 %collective-permute-start = (bf16[224,128]{1,0:T(8,128)(2,1)S(1)}, bf16[224,128]{1,0:T(8,128)(2,1)S(1)}, u32[]{:S(2)}, u32[]{:S(2)}) collective-permute-start(bf16[224,128]{1,0:T(8,128)(2,1)S(1)} %pack.1.refs_5_.refs_2_), channel_id=1, source_target_pairs={{0,4},{4,0},{8,12},{12,8},{1,5},{5,1},{9,13},{13,9},{2,6},{6,2},{1... | collective-permute-start | bytes 172040 | tf_op jit(solution)/shard_map/ppermute | solution.py:27
  7.2 0.0 slice-done
  7.2 0.0 slice-done.1
  7.2 0.0 copy-done
  7.2 0.0 copy-done.1
  7.2 0.0 copy-done.2
  7.2 0.0 copy-start.3
  7.2 1.0 %project.1 = (bf16[32,512]{1,0:T(8,128)(2,1)S(1)}, bf16[32,512]{1,0:T(8,128)(2,1)S(1)}, bf16[32,512]{1,0:T(8,128)(2,1)S(1)}, bf16[32,1536]{1,0:T(8,128)(2,1)S(1)...) custom-call(s32[4]{0:T(128)} %refs_0_.1, s32[8]{0:T(128)} %refs_1_.1, ...), custom_call_target="tpu_custom_call" | custom-call | bytes 200000 | tf_op jit(solution)/shard_map/project/pallas_call | solution.py:160
  8.3 0.4 %collective-permute-start.6 = (bf16[32,512]{1,0:T(8,128)(2,1)S(1)}, bf16[32,512]{1,0:T(8,128)(2,1)S(1)}, u32[]{:S(2)}, u32[]{:S(2)}) collective-permute-start(bf16[32,512]{1,0:T(8,128)(2,1)S(1)} %get-tuple-element.37), channel_id=1, source_target_pairs={{0,3},{1,2},{2,1},{3,0},{4,7},{5,6},{6,5},{7,4},{8,11},{9,10},{10,... | collective-permute-start | bytes 98312 | tf_op jit(solution)/shard_map/ppermute | solution.py:27
  8.7 1.2 %collective-permute-start.7 = (bf16[32,512]{1,0:T(8,128)(2,1)S(1)}, bf16[32,512]{1,0:T(8,128)(2,1)S(1)}, u32[]{:S(2)}, u32[]{:S(2)}) collective-permute-start(bf16[32,512]{1,0:T(8,128)(2,1)S(1)} %get-tuple-element.38), channel_id=1, source_target_pairs={{0,2},{1,3},{2,0},{3,1},{4,6},{5,7},{6,4},{7,5},{8,10},{9,11},{10,... | collective-permute-start | bytes 98312 | tf_op jit(solution)/shard_map/ppermute | solution.py:27
  9.9 0.0 collective-permute-done.2.refs_5_
  9.9 0.3 %collective-permute-start.8 = (bf16[32,512]{1,0:T(8,128)(2,1)S(1)}, bf16[32,512]{1,0:T(8,128)(2,1)S(1)}, u32[]{:S(2)}, u32[]{:S(2)}) collective-permute-start(bf16[32,512]{1,0:T(8,128)(2,1)S(1)} %get-tuple-element.39), channel_id=1, source_target_pairs={{0,1},{1,0},{2,3},{3,2},{4,5},{5,4},{6,7},{7,6},{8,9},{9,8},{10,11... | collective-permute-start | bytes 98312 | tf_op jit(solution)/shard_map/ppermute | solution.py:27
  10.2 1.5 %collective-permute-done.1.refs_4_ = bf16[224,128]{1,0:T(8,128)(2,1)S(1)} collective-permute-done((bf16[224,128]{1,0:T(8,128)(2,1)S(1)}, bf16[224,128]{1,0:T(8,128)(2,1)S(1)}, u32[]{:S(2)}, u32[]{:S(2)}) %collective-permute-start.1) | collective-permute-done | bytes 57376 | tf_op jit(solution)/shard_map/ppermute | solution.py:27
  11.7 0.1 collective-permute-done.refs_3_
  11.8 0.3 %route.1 = (bf16[96,128]{1,0:T(8,128)(2,1)S(1)}, bf16[96,128]{1,0:T(8,128)(2,1)S(1)}, bf16[96,128]{1,0:T(8,128)(2,1)S(1)}, bf16[96,128]{1,0:T(8,128)(2,1)S(1)}) custom-call(bf16[32,1536]{1,0:T(8,128)(2,1)S(1)} %get-tuple-element.24.refs_0_, f32[16,128]{1,0:T(8,128)S(1)} %get-tuple-element.25.refs_1_, bf16[224,128]{1,0:T(8,128)(2,1)S(1)} %pack.1.refs_5_.refs_2_, ...), custom_call_target="tpu_custom_call" | custom-call | bytes 800000 | tf_op jit(solution)/shard_map/route/pallas_call | solution.py:340
  12.1 0.0 collective-permute-start.3
  12.1 1.6 %collective-permute-start.4 = (bf16[96,128]{1,0:T(8,128)(2,1)S(1)}, bf16[96,128]{1,0:T(8,128)(2,1)S(1)}, u32[]{:S(2)}, u32[]{:S(2)}) collective-permute-start(bf16[96,128]{1,0:T(8,128)(2,1)S(1)} %get-tuple-element.35), channel_id=1, source_target_pairs={{0,2},{1,3},{2,0},{3,1},{4,6},{5,7},{6,4},{7,5},{8,10},{9,11},{10,... | collective-permute-start | bytes 73736 | tf_op jit(solution)/shard_map/ppermute | solution.py:27
  13.7 0.0 collective-permute-done.6.refs_12_
  13.7 0.3 %collective-permute-start.5 = (bf16[96,128]{1,0:T(8,128)(2,1)S(1)}, bf16[96,128]{1,0:T(8,128)(2,1)S(1)}, u32[]{:S(2)}, u32[]{:S(2)}) collective-permute-start(bf16[96,128]{1,0:T(8,128)(2,1)S(1)} %get-tuple-element.36), channel_id=1, source_target_pairs={{0,1},{1,0},{2,3},{3,2},{4,5},{5,4},{6,7},{7,6},{8,9},{9,8},{10,11... | collective-permute-start | bytes 73736 | tf_op jit(solution)/shard_map/ppermute | solution.py:27
  13.9 0.0 copy-done.3
  13.9 0.0 copy-start.4
  14.0 1.4 %attend.1 = (f32[32,512]{1,0:T(8,128)S(1)}, bf16[512,128]{1,0:T(8,128)(2,1)S(1)}, f32[512,128]{1,0:T(8,128)S(1)}, f32[512,128]{1,0:T(8,128)S(1)}, f32[512,128]{1,0:T(8,128)S(1)}) custom-call(bf16[32,2048]{1,0:T(8,128)(2,1)S(1)} %bitcast.11, bf16[8,512,256]{2,1,0:T(8,128)(2,1)S(1)} %copy-done, bf16[8,512,256]{2,1,0:T(8,128)(2,1)S(1)} %copy-done.1, ...), custom_call_target="tpu_custom_call" | custom-call | flops 134217728 | bytes 4194304 | tf_op jit(solution)/shard_map/attend/pallas_call | solution.py:270
  15.4 0.0 collective-permute-done.7.refs_13_
  15.4 0.0 collective-permute-done.8.refs_14_
  15.4 0.1 collective-permute-done.3.refs_8_
  15.5 0.4 %collective-permute-done.4.refs_9_ = bf16[96,128]{1,0:T(8,128)(2,1)S(1)} collective-permute-done((bf16[96,128]{1,0:T(8,128)(2,1)S(1)}, bf16[96,128]{1,0:T(8,128)(2,1)S(1)}, u32[]{:S(2)}, u32[]{:S(2)}) %collective-permute-start.4) | collective-permute-done | bytes 24608 | tf_op jit(solution)/shard_map/ppermute | solution.py:27
  16.0 0.0 collective-permute-done.5.refs_10_
  16.0 0.0 copy-done.4
  16.0 1.4 %finish.1 = (bf16[32,2048]{1,0:T(8,128)(2,1)}, bf16[32,256]{1,0:T(8,128)(2,1)}, bf16[32,256]{1,0:T(8,128)(2,1)}) custom-call(f32[1,128]{1,0:T(1,128)S(1)} %bitcast.12, f32[32,512]{1,0:T(8,128)S(1)} %get-tuple-element.27.refs_1_, bf16[512,128]{1,0:T(8,128)(2,1)S(1)} %get-tuple-element.28.refs_2_, f32[512,128]{1,0:T(8,128)S(1)} %get-tuple-element.29.refs_3_, ...), custom_call_target="tpu_custom_call" | custom-call | bytes 1000000 | tf_op jit(solution)/shard_map/finish/pallas_call | solution.py:457
  (2 shorter events, 0.0 us)
Async XLA Ops:
  0.6 0.8 %copy-start.5 = (bf16[64,512]{1,0:T(8,128)(2,1)S(1)}, bf16[64,512]{1,0:T(8,128)(2,1)}, u32[]{:S(2)}) copy-start(bf16[64,512]{1,0:T(8,128)(2,1)} %up_all_ref.1) | copy-start | bytes 196612
  0.6 0.8 %copy-start.6 = (bf16[320,64]{0,1:T(8,128)(2,1)S(1)}, bf16[320,64]{0,1:T(8,128)(2,1)}, u32[]{:S(2)}) copy-start(bf16[320,64]{0,1:T(8,128)(2,1)} %param.12) | copy-start | bytes 122884
  0.7 6.5 %slice-start = ((s8[5242880]{0:T(1024)(128)(4,1)}), s8[4194304]{0:T(1024)(128)(4,1)S(1)}, s32[]{:S(2)}) async-start(s8[5242880]{0:T(1024)(128)(4,1)} %bitcast.7), calls=%async_computation | async-start | bytes 8388608
  1.5 5.7 %slice-start.1 = ((s8[5242880]{0:T(1024)(128)(4,1)}), s8[1048576]{0:T(1024)(128)(4,1)S(1)}, s32[]{:S(2)}) async-start(s8[5242880]{0:T(1024)(128)(4,1)} %bitcast.7), calls=%async_computation.1 | async-start | bytes 2097152
  1.5 5.7 %copy-start = (bf16[8,512,256]{2,1,0:T(8,128)(2,1)S(1)}, bf16[8,512,256]{2,1,0:T(8,128)(2,1)}, u32[]{:S(2)}) copy-start(bf16[8,512,256]{2,1,0:T(8,128)(2,1)} %keys_ref.1) | copy-start | bytes 6291460
  1.5 5.7 %copy-start.1 = (bf16[8,512,256]{2,1,0:T(8,128)(2,1)S(1)}, bf16[8,512,256]{2,1,0:T(8,128)(2,1)}, u32[]{:S(2)}) copy-start(bf16[8,512,256]{2,1,0:T(8,128)(2,1)} %values_ref.1) | copy-start | bytes 6291460
  1.5 5.7 %copy-start.2 = (bf16[4,8,1280]{2,1,0:T(8,128)(2,1)S(1)}, bf16[4,8,1280]{2,1,0:T(8,128)(2,1)}, u32[]{:S(2)}) copy-start(bf16[4,8,1280]{2,1,0:T(8,128)(2,1)} %param.10) | copy-start | bytes 245764
  1.6 8.4 %collective-permute-start.2 = (bf16[224,128]{1,0:T(8,128)(2,1)S(1)}, bf16[224,128]{1,0:T(8,128)(2,1)S(1)}, u32[]{:S(2)}, u32[]{:S(2)}) collective-permute-start(bf16[224,128]{1,0:T(8,128)(2,1)S(1)} %pack.1.refs_5_.refs_2_), channel_id=1, source_target_pairs={{0,8},{4,12},{8,0},{12,4},{1,9},{5,13},{9,1},{13,5},{2,10},{6,14},... | collective-permute-start | bytes 172040 | tf_op jit(solution)/shard_map/ppermute | solution.py:27
  5.6 6.1 %collective-permute-start.1 = (bf16[224,128]{1,0:T(8,128)(2,1)S(1)}, bf16[224,128]{1,0:T(8,128)(2,1)S(1)}, u32[]{:S(2)}, u32[]{:S(2)}) collective-permute-start(bf16[224,128]{1,0:T(8,128)(2,1)S(1)} %pack.1.refs_5_.refs_2_), channel_id=1, source_target_pairs={{0,12},{4,8},{8,4},{12,0},{1,13},{5,9},{9,5},{13,1},{2,14},{6,10},... | collective-permute-start | bytes 172040 | tf_op jit(solution)/shard_map/ppermute | solution.py:27
  7.0 4.8 %collective-permute-start = (bf16[224,128]{1,0:T(8,128)(2,1)S(1)}, bf16[224,128]{1,0:T(8,128)(2,1)S(1)}, u32[]{:S(2)}, u32[]{:S(2)}) collective-permute-start(bf16[224,128]{1,0:T(8,128)(2,1)S(1)} %pack.1.refs_5_.refs_2_), channel_id=1, source_target_pairs={{0,4},{4,0},{8,12},{12,8},{1,5},{5,1},{9,13},{13,9},{2,6},{6,2},{1... | collective-permute-start | bytes 172040 | tf_op jit(solution)/shard_map/ppermute | solution.py:27
  7.2 6.7 %copy-start.3 = (bf16[4,8,2048]{2,1,0:T(8,128)(2,1)S(1)}, bf16[4,8,2048]{2,1,0:T(8,128)(2,1)}, u32[]{:S(2)}) copy-start(bf16[4,8,2048]{2,1,0:T(8,128)(2,1)} %param.15) | copy-start | bytes 393220
  8.3 5.4 %collective-permute-start.6 = (bf16[32,512]{1,0:T(8,128)(2,1)S(1)}, bf16[32,512]{1,0:T(8,128)(2,1)S(1)}, u32[]{:S(2)}, u32[]{:S(2)}) collective-permute-start(bf16[32,512]{1,0:T(8,128)(2,1)S(1)} %get-tuple-element.37), channel_id=1, source_target_pairs={{0,3},{1,2},{2,1},{3,0},{4,7},{5,6},{6,5},{7,4},{8,11},{9,10},{10,... | collective-permute-start | bytes 98312 | tf_op jit(solution)/shard_map/ppermute | solution.py:27
  8.7 6.7 %collective-permute-start.7 = (bf16[32,512]{1,0:T(8,128)(2,1)S(1)}, bf16[32,512]{1,0:T(8,128)(2,1)S(1)}, u32[]{:S(2)}, u32[]{:S(2)}) collective-permute-start(bf16[32,512]{1,0:T(8,128)(2,1)S(1)} %get-tuple-element.38), channel_id=1, source_target_pairs={{0,2},{1,3},{2,0},{3,1},{4,6},{5,7},{6,4},{7,5},{8,10},{9,11},{10,... | collective-permute-start | bytes 98312 | tf_op jit(solution)/shard_map/ppermute | solution.py:27
  9.9 5.5 %collective-permute-start.8 = (bf16[32,512]{1,0:T(8,128)(2,1)S(1)}, bf16[32,512]{1,0:T(8,128)(2,1)S(1)}, u32[]{:S(2)}, u32[]{:S(2)}) collective-permute-start(bf16[32,512]{1,0:T(8,128)(2,1)S(1)} %get-tuple-element.39), channel_id=1, source_target_pairs={{0,1},{1,0},{2,3},{3,2},{4,5},{5,4},{6,7},{7,6},{8,9},{9,8},{10,11... | collective-permute-start | bytes 98312 | tf_op jit(solution)/shard_map/ppermute | solution.py:27
  12.1 3.5 %collective-permute-start.3 = (bf16[96,128]{1,0:T(8,128)(2,1)S(1)}, bf16[96,128]{1,0:T(8,128)(2,1)S(1)}, u32[]{:S(2)}, u32[]{:S(2)}) collective-permute-start(bf16[96,128]{1,0:T(8,128)(2,1)S(1)} %get-tuple-element.34), channel_id=1, source_target_pairs={{0,3},{1,2},{2,1},{3,0},{4,7},{5,6},{6,5},{7,4},{8,11},{9,10},{10,... | collective-permute-start | bytes 73736 | tf_op jit(solution)/shard_map/ppermute | solution.py:27
  12.1 3.9 %collective-permute-start.4 = (bf16[96,128]{1,0:T(8,128)(2,1)S(1)}, bf16[96,128]{1,0:T(8,128)(2,1)S(1)}, u32[]{:S(2)}, u32[]{:S(2)}) collective-permute-start(bf16[96,128]{1,0:T(8,128)(2,1)S(1)} %get-tuple-element.35), channel_id=1, source_target_pairs={{0,2},{1,3},{2,0},{3,1},{4,6},{5,7},{6,4},{7,5},{8,10},{9,11},{10,... | collective-permute-start | bytes 73736 | tf_op jit(solution)/shard_map/ppermute | solution.py:27
  13.7 2.3 %collective-permute-start.5 = (bf16[96,128]{1,0:T(8,128)(2,1)S(1)}, bf16[96,128]{1,0:T(8,128)(2,1)S(1)}, u32[]{:S(2)}, u32[]{:S(2)}) collective-permute-start(bf16[96,128]{1,0:T(8,128)(2,1)S(1)} %get-tuple-element.36), channel_id=1, source_target_pairs={{0,1},{1,0},{2,3},{3,2},{4,5},{5,4},{6,7},{7,6},{8,9},{9,8},{10,11... | collective-permute-start | bytes 73736 | tf_op jit(solution)/shard_map/ppermute | solution.py:27
  13.9 2.0 %copy-start.4 = (f32[128]{0:T(128)S(1)}, f32[128]{0:T(128)}, u32[]{:S(2)}) copy-start(f32[128]{0:T(128)} %param.14) | copy-start | bytes 1540

commit v26 on v23

--- a/solution.py
+++ b/solution.py
@@ -469,7 +469,7 @@
         compiler_params=pltpu.CompilerParams(vmem_limit_bytes=6 * 2**20),
         name="finish",
         cost_estimate=pl.CostEstimate(flops=0, bytes_accessed=1000000, transcendentals=0),
-    )(gain, mine, *partials, *packets[::-1], *others[::-1])
+    )(gain, mine, *partials, *packets[::-1], *others[1:], *others[:1])
 
 
 def per_device(

time: 17.6 us -> 17.6 us (level)
  waiting for transfers between devices: 2.13 us -> 1.85 us
  starting transfers between devices: 9.42 us -> 9.7 us
    ppermute x9, starting transfers between devices: 9.42 us -> 9.7 us  [swap(): return lax.ppermute(block, axis, [(s, s ^ offset) for s in range(count)])]
    ppermute x9, waiting for transfers between devices: 2.13 us -> 1.85 us  [swap(): return lax.ppermute(block, axis, [(s, s ^ offset) for s in range(count)])]
where the time goes in v26:
time: 17.6 us; the launch traced here: 17.4 us
  starting transfers between devices  9.7 us (55%)
  Pallas kernels  4.3 us (24%)
  waiting for transfers between devices  1.85 us (11%)
  local copies, waits for them, and re-layouts  0.8 us (5%)
  between operations  0.75 us (4%)
    ppermute x9, starting transfers between devices, swap(): return lax.ppermute(block, axis, [(s, s ^ offset) for s in range(count)])  9.7 us
    ppermute x9, waiting for transfers between devices, swap(): return lax.ppermute(block, axis, [(s, s ^ offset) for s in range(count)])  1.85 us
    pallas_call x1, Pallas kernels, attend(): pl.pallas_call(functools.partial(attend_kernel, step_count, width // lane...  1.45 us
    pallas_call x1, Pallas kernels, finish(): pl.pallas_call(functools.partial(finish_kernel, step_count, row_count, he...  1.44 us
    pallas_call x1, Pallas kernels, project(): pl.pallas_call(functools.partial(project_kernel, step_count, row_count, s...  1.04 us
    unnamed x16, local copies, waits for them, and re-layouts  0.8 us
  transfers between devices with their start and end apart: 9, of which 4 were waited for; matrix products, arithmetic and copies ran while one was open for 0% of the time, Pallas kernels for 16%

profile of v26, /device:TPU:0, one launch (start us, length us, event | category | flops | bytes accessed | tf_op | source)
XLA Modules:
  0.0 17.4 jit_solution(3299600626935308267)
XLA Ops:
  0.6 0.0 copy-start.5
  0.6 0.0 copy-start.6
  0.7 0.0 copy-start.2
  0.7 0.0 copy-start.1
  0.7 0.0 copy-start.3
  0.7 0.0 copy-start
  0.7 0.8 %copy-done.5 = bf16[64,512]{1,0:T(8,128)(2,1)S(1)} copy-done((bf16[64,512]{1,0:T(8,128)(2,1)S(1)}, bf16[64,512]{1,0:T(8,128)(2,1)}, u32[]{:S(2)}) %copy-start.5) | copy-done | bytes 65560
  1.5 0.0 copy-done.6
  1.5 0.1 pack.1.refs_5_.refs_2_
  1.6 4.0 %collective-permute-start.2 = (bf16[224,128]{1,0:T(8,128)(2,1)S(1)}, bf16[224,128]{1,0:T(8,128)(2,1)S(1)}, u32[]{:S(2)}, u32[]{:S(2)}) collective-permute-start(bf16[224,128]{1,0:T(8,128)(2,1)S(1)} %pack.1.refs_5_.refs_2_), channel_id=1, source_target_pairs={{0,8},{4,12},{8,0},{12,4},{1,9},{5,13},{9,1},{13,5},{2,10},{6,14},... | collective-permute-start | bytes 172040 | tf_op jit(solution)/shard_map/ppermute | solution.py:27
  5.6 1.3 %collective-permute-start.1 = (bf16[224,128]{1,0:T(8,128)(2,1)S(1)}, bf16[224,128]{1,0:T(8,128)(2,1)S(1)}, u32[]{:S(2)}, u32[]{:S(2)}) collective-permute-start(bf16[224,128]{1,0:T(8,128)(2,1)S(1)} %pack.1.refs_5_.refs_2_), channel_id=1, source_target_pairs={{0,12},{4,8},{8,4},{12,0},{1,13},{5,9},{9,5},{13,1},{2,14},{6,10},... | collective-permute-start | bytes 172040 | tf_op jit(solution)/shard_map/ppermute | solution.py:27
  7.0 0.2 %collective-permute-start = (bf16[224,128]{1,0:T(8,128)(2,1)S(1)}, bf16[224,128]{1,0:T(8,128)(2,1)S(1)}, u32[]{:S(2)}, u32[]{:S(2)}) collective-permute-start(bf16[224,128]{1,0:T(8,128)(2,1)S(1)} %pack.1.refs_5_.refs_2_), channel_id=1, source_target_pairs={{0,4},{4,0},{8,12},{12,8},{1,5},{5,1},{9,13},{13,9},{2,6},{6,2},{1... | collective-permute-start | bytes 172040 | tf_op jit(solution)/shard_map/ppermute | solution.py:27
  7.2 0.0 copy-done.2
  7.2 0.0 copy-done.1
  7.2 0.0 copy-done.3
  7.2 0.0 copy-done
  7.2 0.0 copy-start.4
  7.2 1.0 %project.1 = (bf16[32,512]{1,0:T(8,128)(2,1)S(1)}, bf16[32,512]{1,0:T(8,128)(2,1)S(1)}, bf16[32,512]{1,0:T(8,128)(2,1)S(1)}, bf16[32,1536]{1,0:T(8,128)(2,1)S(1)...) custom-call(s32[4]{0:T(128)} %refs_0_.1, s32[8]{0:T(128)} %refs_1_.1, ...), custom_call_target="tpu_custom_call" | custom-call | bytes 200000 | tf_op jit(solution)/shard_map/project/pallas_call | solution.py:160
  8.3 1.6 %collective-permute-start.6 = (bf16[32,512]{1,0:T(8,128)(2,1)S(1)}, bf16[32,512]{1,0:T(8,128)(2,1)S(1)}, u32[]{:S(2)}, u32[]{:S(2)}) collective-permute-start(bf16[32,512]{1,0:T(8,128)(2,1)S(1)} %get-tuple-element.37), channel_id=1, source_target_pairs={{0,2},{1,3},{2,0},{3,1},{4,6},{5,7},{6,4},{7,5},{8,10},{9,11},{10,... | collective-permute-start | bytes 98312 | tf_op jit(solution)/shard_map/ppermute | solution.py:27
  9.8 0.0 collective-permute-start.7
  9.8 0.0 collective-permute-done.2.refs_5_
  9.8 0.6 %collective-permute-start.8 = (bf16[32,512]{1,0:T(8,128)(2,1)S(1)}, bf16[32,512]{1,0:T(8,128)(2,1)S(1)}, u32[]{:S(2)}, u32[]{:S(2)}) collective-permute-start(bf16[32,512]{1,0:T(8,128)(2,1)S(1)} %get-tuple-element.39), channel_id=1, source_target_pairs={{0,1},{1,0},{2,3},{3,2},{4,5},{5,4},{6,7},{7,6},{8,9},{9,8},{10,11... | collective-permute-start | bytes 98312 | tf_op jit(solution)/shard_map/ppermute | solution.py:27
  10.5 1.2 %collective-permute-done.1.refs_4_ = bf16[224,128]{1,0:T(8,128)(2,1)S(1)} collective-permute-done((bf16[224,128]{1,0:T(8,128)(2,1)S(1)}, bf16[224,128]{1,0:T(8,128)(2,1)S(1)}, u32[]{:S(2)}, u32[]{:S(2)}) %collective-permute-start.1) | collective-permute-done | bytes 57376 | tf_op jit(solution)/shard_map/ppermute | solution.py:27
  11.7 0.1 collective-permute-done.refs_3_
  11.7 0.3 %route.1 = (bf16[96,128]{1,0:T(8,128)(2,1)S(1)}, bf16[96,128]{1,0:T(8,128)(2,1)S(1)}, bf16[96,128]{1,0:T(8,128)(2,1)S(1)}, bf16[96,128]{1,0:T(8,128)(2,1)S(1)}) custom-call(bf16[32,1536]{1,0:T(8,128)(2,1)S(1)} %get-tuple-element.24.refs_0_, f32[16,128]{1,0:T(8,128)S(1)} %get-tuple-element.25.refs_1_, bf16[224,128]{1,0:T(8,128)(2,1)S(1)} %pack.1.refs_5_.refs_2_, ...), custom_call_target="tpu_custom_call" | custom-call | bytes 800000 | tf_op jit(solution)/shard_map/route/pallas_call | solution.py:340
  12.0 0.0 collective-permute-start.3
  12.1 1.6 %collective-permute-start.4 = (bf16[96,128]{1,0:T(8,128)(2,1)S(1)}, bf16[96,128]{1,0:T(8,128)(2,1)S(1)}, u32[]{:S(2)}, u32[]{:S(2)}) collective-permute-start(bf16[96,128]{1,0:T(8,128)(2,1)S(1)} %get-tuple-element.35), channel_id=1, source_target_pairs={{0,2},{1,3},{2,0},{3,1},{4,6},{5,7},{6,4},{7,5},{8,10},{9,11},{10,... | collective-permute-start | bytes 73736 | tf_op jit(solution)/shard_map/ppermute | solution.py:27
  13.6 0.0 collective-permute-done.6.refs_12_
  13.6 0.3 %collective-permute-start.5 = (bf16[96,128]{1,0:T(8,128)(2,1)S(1)}, bf16[96,128]{1,0:T(8,128)(2,1)S(1)}, u32[]{:S(2)}, u32[]{:S(2)}) collective-permute-start(bf16[96,128]{1,0:T(8,128)(2,1)S(1)} %get-tuple-element.36), channel_id=1, source_target_pairs={{0,1},{1,0},{2,3},{3,2},{4,5},{5,4},{6,7},{7,6},{8,9},{9,8},{10,11... | collective-permute-start | bytes 73736 | tf_op jit(solution)/shard_map/ppermute | solution.py:27
  13.9 0.0 copy-done.4
  13.9 0.0 copy-start.7
  13.9 1.4 %attend.1 = (f32[32,512]{1,0:T(8,128)S(1)}, bf16[512,128]{1,0:T(8,128)(2,1)S(1)}, f32[512,128]{1,0:T(8,128)S(1)}, f32[512,128]{1,0:T(8,128)S(1)}, f32[512,128]{1,0:T(8,128)S(1)}) custom-call(bf16[32,2048]{1,0:T(8,128)(2,1)S(1)} %bitcast.9, bf16[8,512,256]{2,1,0:T(8,128)(2,1)S(1)} %copy-done.1, bf16[8,512,256]{2,1,0:T(8,128)(2,1)S(1)} %copy-done.2, ...), custom_call_target="tpu_custom_call" | custom-call | flops 134217728 | bytes 4194304 | tf_op jit(solution)/shard_map/attend/pallas_call | solution.py:270
  15.4 0.0 collective-permute-done.7.refs_13_
  15.4 0.0 collective-permute-done.8.refs_14_
  15.4 0.1 collective-permute-done.3.refs_8_
  15.5 0.4 %collective-permute-done.4.refs_9_ = bf16[96,128]{1,0:T(8,128)(2,1)S(1)} collective-permute-done((bf16[96,128]{1,0:T(8,128)(2,1)S(1)}, bf16[96,128]{1,0:T(8,128)(2,1)S(1)}, u32[]{:S(2)}, u32[]{:S(2)}) %collective-permute-start.4) | collective-permute-done | bytes 24608 | tf_op jit(solution)/shard_map/ppermute | solution.py:27
  16.0 0.0 collective-permute-done.5.refs_10_
  16.0 0.0 copy-done.7
  16.0 1.4 %finish.1 = (bf16[32,2048]{1,0:T(8,128)(2,1)}, bf16[32,256]{1,0:T(8,128)(2,1)}, bf16[32,256]{1,0:T(8,128)(2,1)}) custom-call(f32[1,128]{1,0:T(1,128)S(1)} %bitcast.11, f32[32,512]{1,0:T(8,128)S(1)} %get-tuple-element.27.refs_1_, bf16[512,128]{1,0:T(8,128)(2,1)S(1)} %get-tuple-element.28.refs_2_, f32[512,128]{1,0:T(8,128)S(1)} %get-tuple-element.29.refs_3_, ...), custom_call_target="tpu_custom_call" | custom-call | bytes 1000000 | tf_op jit(solution)/shard_map/finish/pallas_call | solution.py:457
  (1 shorter events, 0.0 us)
Async XLA Ops:
  0.6 0.8 %copy-start.5 = (bf16[64,512]{1,0:T(8,128)(2,1)S(1)}, bf16[64,512]{1,0:T(8,128)(2,1)}, u32[]{:S(2)}) copy-start(bf16[64,512]{1,0:T(8,128)(2,1)} %up_all_ref.1) | copy-start | bytes 196612
  0.6 0.8 %copy-start.6 = (bf16[320,64]{0,1:T(8,128)(2,1)S(1)}, bf16[320,64]{0,1:T(8,128)(2,1)}, u32[]{:S(2)}) copy-start(bf16[320,64]{0,1:T(8,128)(2,1)} %param.12) | copy-start | bytes 122884
  0.7 6.5 %copy-start.2 = (bf16[8,512,256]{2,1,0:T(8,128)(2,1)S(1)}, bf16[8,512,256]{2,1,0:T(8,128)(2,1)}, u32[]{:S(2)}) copy-start(bf16[8,512,256]{2,1,0:T(8,128)(2,1)} %values_ref.1) | copy-start | bytes 6291460
  0.7 6.5 %copy-start.1 = (bf16[8,512,256]{2,1,0:T(8,128)(2,1)S(1)}, bf16[8,512,256]{2,1,0:T(8,128)(2,1)}, u32[]{:S(2)}) copy-start(bf16[8,512,256]{2,1,0:T(8,128)(2,1)} %keys_ref.1) | copy-start | bytes 6291460
  0.7 6.5 %copy-start.3 = (bf16[4,8,1280]{2,1,0:T(8,128)(2,1)S(1)}, bf16[4,8,1280]{2,1,0:T(8,128)(2,1)}, u32[]{:S(2)}) copy-start(bf16[4,8,1280]{2,1,0:T(8,128)(2,1)} %param.10) | copy-start | bytes 245764
  0.7 6.5 %copy-start = (bf16[1280,2048]{1,0:T(8,128)(2,1)S(1)}, bf16[1280,2048]{1,0:T(8,128)(2,1)}, u32[]{:S(2)}) copy-start(bf16[1280,2048]{1,0:T(8,128)(2,1)} %weight_ref.1) | copy-start | bytes 15728644
  1.6 8.3 %collective-permute-start.2 = (bf16[224,128]{1,0:T(8,128)(2,1)S(1)}, bf16[224,128]{1,0:T(8,128)(2,1)S(1)}, u32[]{:S(2)}, u32[]{:S(2)}) collective-permute-start(bf16[224,128]{1,0:T(8,128)(2,1)S(1)} %pack.1.refs_5_.refs_2_), channel_id=1, source_target_pairs={{0,8},{4,12},{8,0},{12,4},{1,9},{5,13},{9,1},{13,5},{2,10},{6,14},... | collective-permute-start | bytes 172040 | tf_op jit(solution)/shard_map/ppermute | solution.py:27
  5.6 6.1 %collective-permute-start.1 = (bf16[224,128]{1,0:T(8,128)(2,1)S(1)}, bf16[224,128]{1,0:T(8,128)(2,1)S(1)}, u32[]{:S(2)}, u32[]{:S(2)}) collective-permute-start(bf16[224,128]{1,0:T(8,128)(2,1)S(1)} %pack.1.refs_5_.refs_2_), channel_id=1, source_target_pairs={{0,12},{4,8},{8,4},{12,0},{1,13},{5,9},{9,5},{13,1},{2,14},{6,10},... | collective-permute-start | bytes 172040 | tf_op jit(solution)/shard_map/ppermute | solution.py:27
  7.0 4.8 %collective-permute-start = (bf16[224,128]{1,0:T(8,128)(2,1)S(1)}, bf16[224,128]{1,0:T(8,128)(2,1)S(1)}, u32[]{:S(2)}, u32[]{:S(2)}) collective-permute-start(bf16[224,128]{1,0:T(8,128)(2,1)S(1)} %pack.1.refs_5_.refs_2_), channel_id=1, source_target_pairs={{0,4},{4,0},{8,12},{12,8},{1,5},{5,1},{9,13},{13,9},{2,6},{6,2},{1... | collective-permute-start | bytes 172040 | tf_op jit(solution)/shard_map/ppermute | solution.py:27
  7.2 6.7 %copy-start.4 = (bf16[4,8,2048]{2,1,0:T(8,128)(2,1)S(1)}, bf16[4,8,2048]{2,1,0:T(8,128)(2,1)}, u32[]{:S(2)}) copy-start(bf16[4,8,2048]{2,1,0:T(8,128)(2,1)} %param.15) | copy-start | bytes 393220
  8.3 5.4 %collective-permute-start.6 = (bf16[32,512]{1,0:T(8,128)(2,1)S(1)}, bf16[32,512]{1,0:T(8,128)(2,1)S(1)}, u32[]{:S(2)}, u32[]{:S(2)}) collective-permute-start(bf16[32,512]{1,0:T(8,128)(2,1)S(1)} %get-tuple-element.37), channel_id=1, source_target_pairs={{0,2},{1,3},{2,0},{3,1},{4,6},{5,7},{6,4},{7,5},{8,10},{9,11},{10,... | collective-permute-start | bytes 98312 | tf_op jit(solution)/shard_map/ppermute | solution.py:27
  9.8 5.6 %collective-permute-start.7 = (bf16[32,512]{1,0:T(8,128)(2,1)S(1)}, bf16[32,512]{1,0:T(8,128)(2,1)S(1)}, u32[]{:S(2)}, u32[]{:S(2)}) collective-permute-start(bf16[32,512]{1,0:T(8,128)(2,1)S(1)} %get-tuple-element.38), channel_id=1, source_target_pairs={{0,3},{1,2},{2,1},{3,0},{4,7},{5,6},{6,5},{7,4},{8,11},{9,10},{10,... | collective-permute-start | bytes 98312 | tf_op jit(solution)/shard_map/ppermute | solution.py:27
  9.8 5.6 %collective-permute-start.8 = (bf16[32,512]{1,0:T(8,128)(2,1)S(1)}, bf16[32,512]{1,0:T(8,128)(2,1)S(1)}, u32[]{:S(2)}, u32[]{:S(2)}) collective-permute-start(bf16[32,512]{1,0:T(8,128)(2,1)S(1)} %get-tuple-element.39), channel_id=1, source_target_pairs={{0,1},{1,0},{2,3},{3,2},{4,5},{5,4},{6,7},{7,6},{8,9},{9,8},{10,11... | collective-permute-start | bytes 98312 | tf_op jit(solution)/shard_map/ppermute | solution.py:27
  12.0 3.5 %collective-permute-start.3 = (bf16[96,128]{1,0:T(8,128)(2,1)S(1)}, bf16[96,128]{1,0:T(8,128)(2,1)S(1)}, u32[]{:S(2)}, u32[]{:S(2)}) collective-permute-start(bf16[96,128]{1,0:T(8,128)(2,1)S(1)} %get-tuple-element.34), channel_id=1, source_target_pairs={{0,3},{1,2},{2,1},{3,0},{4,7},{5,6},{6,5},{7,4},{8,11},{9,10},{10,... | collective-permute-start | bytes 73736 | tf_op jit(solution)/shard_map/ppermute | solution.py:27
  12.1 3.9 %collective-permute-start.4 = (bf16[96,128]{1,0:T(8,128)(2,1)S(1)}, bf16[96,128]{1,0:T(8,128)(2,1)S(1)}, u32[]{:S(2)}, u32[]{:S(2)}) collective-permute-start(bf16[96,128]{1,0:T(8,128)(2,1)S(1)} %get-tuple-element.35), channel_id=1, source_target_pairs={{0,2},{1,3},{2,0},{3,1},{4,6},{5,7},{6,4},{7,5},{8,10},{9,11},{10,... | collective-permute-start | bytes 73736 | tf_op jit(solution)/shard_map/ppermute | solution.py:27
  13.6 2.3 %collective-permute-start.5 = (bf16[96,128]{1,0:T(8,128)(2,1)S(1)}, bf16[96,128]{1,0:T(8,128)(2,1)S(1)}, u32[]{:S(2)}, u32[]{:S(2)}) collective-permute-start(bf16[96,128]{1,0:T(8,128)(2,1)S(1)} %get-tuple-element.36), channel_id=1, source_target_pairs={{0,1},{1,0},{2,3},{3,2},{4,5},{5,4},{6,7},{7,6},{8,9},{9,8},{10,11... | collective-permute-start | bytes 73736 | tf_op jit(solution)/shard_map/ppermute | solution.py:27
  13.9 2.0 %copy-start.7 = (f32[128]{0:T(128)S(1)}, f32[128]{0:T(128)}, u32[]{:S(2)}) copy-start(f32[128]{0:T(128)} %param.14) | copy-start | bytes 1540
